TPU v7x, 128 devices: a whole 4x4x4 slice. The times are simulated.
128 devices in a mesh: dp: 16 (over y_lo, z, core), fsdp: 8 (over y_hi, x).
Axes of the slice: x: 4, y: 4 (y_hi: 2, y_lo: 2; y = y_hi * 2 + y_lo), z: 4, core: 2. Of those that a mesh axis runs over, the one named last changes fastest.
Arguments:
- context: bfloat16 [65536, 1024], P(('dp', 'fsdp')), may hold values from -6 to 6
- residual: bfloat16 [65536, 2048], P(('dp', 'fsdp')), may hold values from -6 to 6
- out_weight: bfloat16 [1024, 2048], P('fsdp'), may hold values from -0.1875 to 0.1875
- norm_gain: float32 [2048], replicated, may hold values from 0.5 to 1.5
- user_vectors: bfloat16 [1024, 2048], P(('dp', 'fsdp')), may hold values from -12 to 12
- positive: int32 [1024], P(('dp', 'fsdp')), may hold values from 0 to 255
- item_ids: int32 [256], P(('dp', 'fsdp')), may hold values from 0 to 127
- item_counts: int32 [256], P(('dp', 'fsdp')), may hold values from 1 to 5000
- lengths: int32 [256], P(('dp', 'fsdp')), may hold values from 64 to 256
Outputs:
- mean_loss: float32 [], replicated
- residual_grad: bfloat16 [65536, 2048], P(('dp', 'fsdp'))
- context_grad: bfloat16 [65536, 1024], P(('dp', 'fsdp'))
- weight_grad: bfloat16 [1024, 2048], P('fsdp')
- norm_gain_grad: float32 [2048], replicated
- user_grad: bfloat16 [1024, 2048], P(('dp', 'fsdp'))
All inputs are finite; a program needn't handle non-finite values.
Results may differ from a plain program's by a relative error of at most 0.015.
Values may be sent and summed in bfloat16 or wider, within the bound.
No kernel may reach another device: no remote copies, remote signals or barrier semaphores. Data moves between devices by JAX's collectives and lax.ppermute only.
A program may use at most 128 MiB of HBM per device.

v0:
```python
import jax
import jax.numpy as jnp
from jax import lax
from jax.sharding import PartitionSpec as P

EPSILON = 1e-06
MASKED_FILL = -1e30


def contract_rows(left, right):
    return lax.dot_general(
        left, right, (((0,), (0,)), ((), ())), preferred_element_type=jnp.float32
    )


def contract_last(left, right):
    return lax.dot_general(
        left, right, (((1,), (1,)), ((), ())), preferred_element_type=jnp.float32
    )


def on_device(
    context, residual, out_weight, norm_gain, user_vectors, positive, item_ids, item_counts, lengths
):
    tok_rows, head_width = context.shape
    model_width = residual.shape[1]
    items_here = lengths.shape[0]
    item_length = tok_rows // items_here
    users_here = user_vectors.shape[0]
    devices_all = lax.axis_size("dp") * lax.axis_size("fsdp")
    columns = context
    attended = jnp.dot(
        columns,
        lax.all_gather(out_weight, "fsdp", axis=0, tiled=True),
        preferred_element_type=jnp.float32,
    )
    stream = residual.astype(jnp.float32) + attended
    inverse_root_mean = lax.rsqrt(jnp.mean(stream * stream, axis=-1, keepdims=True) + EPSILON)
    normed = stream * inverse_root_mean * norm_gain
    positions = jnp.arange(item_length, dtype=jnp.int32)
    inside = (positions[None, :] < lengths[:, None])[:, :, None]
    length_float = lengths.astype(jnp.float32)[:, None]
    normed_items = normed.reshape(items_here, item_length, model_width)
    pooled = jnp.sum(jnp.where(inside, normed_items, 0.0), axis=1) / length_float
    emb_scale = lax.rsqrt(jnp.mean(pooled * pooled, axis=-1, keepdims=True) + EPSILON)
    embedding = (pooled * emb_scale).astype(jnp.bfloat16)
    keys = jnp.stack([item_ids, item_counts], axis=1)
    keys_all = lax.all_gather(keys, ("dp", "fsdp"), axis=0, tiled=True)
    emb_all = lax.all_gather(embedding, ("dp", "fsdp"), axis=0, tiled=True)
    items_all = jnp.arange(keys_all.shape[0], dtype=jnp.int32)
    onehot = items_all[None, :] == positive[:, None]
    positive_id = jnp.sum(jnp.where(onehot, keys_all[None, :, 0], 0), axis=1)
    excluded = (keys_all[None, :, 0] == positive_id[:, None]) & jnp.logical_not(onehot)
    scores = contract_last(user_vectors, emb_all)
    log_counts = jnp.log(keys_all[:, 1].astype(jnp.float32))
    logits = jnp.where(excluded, MASKED_FILL, scores - log_counts[None, :])
    row_max = jnp.max(logits, axis=1, keepdims=True)
    weights = jnp.where(excluded, 0.0, jnp.exp(logits - row_max))
    row_total = jnp.sum(weights, axis=1, keepdims=True)
    log_total = row_max[:, 0] + jnp.log(row_total[:, 0])
    loss_part = jnp.sum(log_total - jnp.sum(jnp.where(onehot, logits, 0.0), axis=1))
    logit_grad = (weights / row_total - onehot.astype(jnp.float32)).astype(jnp.bfloat16)
    user_grad = jnp.dot(logit_grad, emb_all, preferred_element_type=jnp.float32).astype(
        jnp.bfloat16
    )
    emb_grad = lax.psum_scatter(
        contract_rows(logit_grad, user_vectors), ("dp", "fsdp"), scatter_dimension=0, tiled=True
    )
    pooled_grad = emb_scale * emb_grad - pooled * emb_scale**3 * jnp.mean(
        pooled * emb_grad, axis=-1, keepdims=True
    )
    normed_grad = jnp.where(inside, pooled_grad[:, None, :] / length_float[:, :, None], 0.0)
    normed_grad = normed_grad.reshape(tok_rows, model_width)
    gain_part = jnp.sum(normed_grad * stream * inverse_root_mean, axis=0)
    scaled = norm_gain * normed_grad
    stream_grad = inverse_root_mean * scaled - stream * inverse_root_mean**3 * jnp.mean(
        scaled * stream, axis=-1, keepdims=True
    )
    residual_grad = stream_grad.astype(jnp.bfloat16)
    context_grad = contract_last(
        residual_grad, lax.all_gather(out_weight, "fsdp", axis=0, tiled=True)
    )
    context_grad = context_grad.astype(jnp.bfloat16)
    dp_count = lax.axis_size("dp")
    fsdp_count = lax.axis_size("fsdp")
    piece_rows = head_width // (dp_count * fsdp_count)
    reordered = context.reshape(tok_rows, fsdp_count, dp_count, piece_rows)
    reordered = jnp.transpose(reordered, (0, 2, 1, 3)).reshape(tok_rows, head_width)
    columns = reordered
    own_piece = lax.psum_scatter(
        contract_rows(columns, residual_grad), ("dp", "fsdp"), scatter_dimension=0, tiled=True
    )
    weight_grad = lax.all_gather(own_piece.astype(jnp.bfloat16), "dp", axis=0, tiled=True)
    loss_sum, gain_grad = lax.psum((loss_part, gain_part), ("dp", "fsdp"))
    mean_loss = loss_sum / (users_here * devices_all)
    return (mean_loss, residual_grad, context_grad, weight_grad, gain_grad, user_grad)


def solution(mesh):
    placed = (
        P(("dp", "fsdp"), None),
        P(("dp", "fsdp"), None),
        P("fsdp", None),
        P(),
        P(("dp", "fsdp"), None),
        P(("dp", "fsdp")),
        P(("dp", "fsdp")),
        P(("dp", "fsdp")),
        P(("dp", "fsdp")),
    )
    return jax.shard_map(
        on_device,
        mesh=mesh,
        in_specs=placed,
        out_specs=(
            P(),
            P(("dp", "fsdp"), None),
            P(("dp", "fsdp"), None),
            P("fsdp", None),
            P(),
            P(("dp", "fsdp"), None),
        ),
        check_vma=False,
    )
```

profile of v0, /device:TPU:1, one launch (start us, length us, event | category | flops | bytes accessed | tf_op | source)
XLA Modules:
  0.0 1256.7 jit_solution(12810117053481718820)
XLA Ops:
  7.2 0.0 copy-start
  7.2 0.0 all-gather.5.cloned.1.call-start
  7.2 0.7 all-gather.5.cloned.1.call-update
  7.9 0.0 all-gather.7.cloned.1.call-start
  8.0 0.7 convert_element_type.36
  8.6 0.7 iota_compare_fusion.1
  9.3 0.0 copy-start.6
  9.4 75.3 %all-gather.5.cloned.1.call-done = bf16[1024,2048]{1,0:T(8,128)(2,1)} async-done(((bf16[128,2048]{1,0:T(8,128)(2,1)}), bf16[1024,2048]{1,0:T(8,128)(2,1)}) %all-gather.5.cloned.1.call-update) | async-done | bytes 4194320 | tf_op jit(solution)/shard_map/all_gather | solution.py:34
  84.7 5.7 multiply_reduce_fusion
  90.4 0.0 copy-start.1
  90.4 0.0 copy-start.8
  90.4 0.0 copy-start.9
  90.4 0.0 copy-start.7
  90.4 1.9 copy-done.1
  92.3 0.0 copy-done.6
  92.3 0.7 select_reduce_fusion
  93.0 0.0 copy-start.4
  93.0 0.2 multiply_reduce_fusion.2
  93.2 0.7 fusion.12
  93.9 0.0 all-gather.7.cloned.1.call-update
  93.9 0.0 all-reduce.4.cloned.1.call-start
  94.0 0.0 copy-done.8
  94.0 0.0 copy-done.9
  94.0 0.1 copy.29
  94.1 298.8 %all-gather = s32[128,2,2]{2,1,0:T(2,128)S(1)} all-gather(s32[1,2,2]{2,1,0:T(2,128)S(1)} %bitcast.62), channel_id=1, replica_groups=mesh['dp'=16,'fsdp'=8] {'dp','fsdp'}, dimensions={0}, use_global_device_ids=true | all-gather | bytes 2064 | tf_op jit(solution)/shard_map/all_gather | solution.py:48
  392.9 0.1 copy.37
  393.0 0.1 convert_log_fusion
  393.1 0.1 copy.39
  393.2 0.0 copy-done.7
  393.2 0.2 select_reduce_fusion.2
  393.4 0.0 all-gather.7.cloned.1.call-done
  393.4 1.5 reshape.111
  394.9 0.0 copy-done
  394.9 0.5 fusion.16
  395.4 0.2 fusion.14
  395.6 1.9 fusion.15
  397.5 0.0 all-reduce.4.cloned.1.call-update
  397.5 0.0 reduce-scatter.4.cloned.1.call-start
  397.6 0.0 copy-done.4
  397.6 0.5 copy.32
  398.1 1.1 copy.33
  399.2 156.7 %all-reduce.4.cloned.1.call-done = f32[256,2048]{1,0:T(8,128)} async-done(((f32[256,2048]{1,0:T(8,128)}), f32[256,2048]{1,0:T(8,128)}) %all-reduce.4.cloned.1.call-update) | async-done | bytes 2097168
  555.9 0.0 copy-start.2
  556.0 1.1 multiply_reduce_fusion.1
  557.1 1.1 subtract_divide_fusion
  558.2 3.3 fusion.8
  561.5 0.0 copy-start.5
  561.5 0.0 copy-done.2
  561.5 1.3 fusion.5
  562.8 0.0 copy-start.3
  562.8 0.0 copy-done.5
  562.8 5.6 convolution_bitcast_fusion
  568.5 9.1 copy.35
  577.6 0.0 reduce-scatter.4.cloned.1.call-update
  577.6 0.6 subtract_reduce_fusion
  578.2 0.9 convolution_convert_fusion
  579.1 65.5 %all-reduce.1 = (f32[]{:T(128)}, f32[2048]{0:T(1024)}) all-reduce(f32[]{:T(128)} %subtract_reduce_fusion, f32[2048]{0:T(1024)S(1)} %get-tuple-element.18), channel_id=1, replica_groups=mesh['dp'=16,'fsdp'=8] {'dp','fsdp'}, use_global_device_ids=true, to_apply=%region_8.9 | all-reduce | flops 2049 | bytes 16392 | tf_op jit(solution)/shard_map/psum | solution.py:94
  645.3 0.0 copy-done.3
  645.4 5.5 convolution_convert_fusion.1
  650.9 563.8 %reduce-scatter.4.cloned.1.call-done = f32[8,2048]{1,0:T(8,128)} async-done(((f32[1024,2048]{1,0:T(8,128)}), f32[8,2048]{1,0:T(8,128)}) %reduce-scatter.4.cloned.1.call-update) | async-done | bytes 65552 | tf_op jit(solution)/shard_map/reduce_scatter | solution.py:90
  1214.7 0.8 convert_element_type.43
  1215.5 32.7 %all_gather.16 = bf16[128,2048]{1,0:T(8,128)(2,1)S(1)} all-gather(bf16[8,2048]{1,0:T(8,128)(2,1)S(1)} %convert_element_type.43), channel_id=1, replica_groups=mesh['dp'=16,'fsdp'=8] {'dp'}, dimensions={0}, use_global_device_ids=true | all-gather | bytes 557056 | tf_op jit(solution)/shard_map/all_gather | solution.py:93
  1248.2 0.8 copy.42
  (6 shorter events, 0.1 us)
Async XLA Ops:
  7.2 387.7 %copy-start = (bf16[8,2048]{1,0:T(8,128)(2,1)S(1)}, bf16[8,2048]{1,0:T(8,128)(2,1)}, u32[]{:S(2)}) copy-start(bf16[8,2048]{1,0:T(8,128)(2,1)} %param.13) | copy-start | bytes 98308
  7.2 77.5 %all-gather.5.cloned.1.call-start = ((), (), s32[]{:S(2)}) async-start(), calls=%async_computation.1 | async-start | bytes 4718592 | tf_op jit(solution)/shard_map/all_gather | solution.py:34
  7.9 385.5 %all-gather.7.cloned.1.call-start = ((), (), s32[]{:S(2)}) async-start(), calls=%async_computation.2 | async-start | bytes 1056768 | tf_op jit(solution)/shard_map/all_gather | solution.py:49
  9.3 82.9 %copy-start.6 = (f32[2048]{0:T(1024)S(1)}, f32[2048]{0:T(1024)}, u32[]{:S(2)}) copy-start(f32[2048]{0:T(1024)} %param.12) | copy-start | bytes 24580
  90.4 1.9 copy-start.1
  90.4 3.6 copy-start.8
  90.4 3.6 copy-start.9
  90.4 302.8 %copy-start.7 = (s32[8]{0:T(128)S(1)}, s32[8]{0:T(128)}, u32[]{:S(2)}) copy-start(s32[8]{0:T(128)} %param.14) | copy-start | bytes 100
  93.0 304.6 %copy-start.4 = (bf16[512,1024]{1,0:T(8,128)(2,1)S(1)}, bf16[512,1024]{1,0:T(8,128)(2,1)}, u32[]{:S(2)}) copy-start(bf16[512,1024]{1,0:T(8,128)(2,1)} %param.9) | copy-start | bytes 3145732
  93.9 462.0 %all-reduce.4.cloned.1.call-start = ((), (), s32[]{:S(2)}) async-start(), calls=%async_computation.4 | async-start | bytes 4194304
  397.5 817.2 %reduce-scatter.4.cloned.1.call-start = ((), (), s32[]{:S(2)}) async-start(), calls=%async_computation.3 | async-start | bytes 8454144 | tf_op jit(solution)/shard_map/reduce_scatter | solution.py:90
  555.9 5.6 copy-start.2
  561.5 1.3 copy-start.5
  562.8 82.5 %copy-start.3 = (bf16[512,2048]{1,0:T(8,128)(2,1)}, bf16[512,2048]{1,0:T(8,128)(2,1)S(1)}, u32[]{:S(2)}) copy-start(bf16[512,2048]{1,0:T(8,128)(2,1)S(1)} %fusion.5) | copy-start | bytes 6291460
Sparse Core Ops, SparseCore 0:
  10.4 74.2 all-gather.4
  94.0 293.4 all-gather.6
  397.6 158.2 all-reduce.3
  577.7 636.8 reduce-scatter.3
where the time goes:
time: 1260 us
  waiting for transfers between devices  797 us (63%)
  blocking collectives  397 us (32%)
  matrix products  20.1 us (2%)
  between operations  15.8 us (1%)
  local copies, waits for them, and re-layouts  15.2 us (1%)
    reduce_scatter x1, waiting for transfers between devices, on_device(): lax.psum_scatter(contract_rows(columns, residual_grad), ('dp', 'fsdp'), s...  564 us
    all_gather x1, blocking collectives, on_device(): keys_all = lax.all_gather(keys, ('dp', 'fsdp'), axis=0, tiled=True)  299 us
    unnamed x5, waiting for transfers between devices  157 us
    all_gather x1, waiting for transfers between devices, on_device(): lax.all_gather(out_weight, 'fsdp', axis=0, tiled=True)  75.3 us
    psum x1, blocking collectives, on_device(): loss_sum, gain_grad = lax.psum((loss_part, gain_part), ('dp', 'fsdp'))  65.5 us
    all_gather x1, blocking collectives, on_device(): lax.all_gather(own_piece.astype(jnp.bfloat16), 'dp', axis=0, tiled=True)  32.7 us
  transfers between devices with their start and end apart: 4, of which 3 were waited for; matrix products, arithmetic and copies ran while one was open for 1% of the time, Pallas kernels for 0%

commit v1 on v0

v1 whole, which is shorter than its diff:
```python
import functools

import jax
import jax.numpy as jnp
from jax import lax
from jax.experimental import pallas as pl
from jax.experimental.pallas import tpu as pltpu
from jax.sharding import PartitionSpec as P

EPSILON = 1e-06
MASKED_FILL = -1e30
AXES = ("dp", "fsdp")
F32 = jnp.float32
BF16 = jnp.bfloat16
VMEM = pl.BlockSpec(memory_space=pltpu.VMEM)
SMEM = pl.BlockSpec(memory_space=pltpu.SMEM)
ANY = pl.BlockSpec(memory_space=pl.ANY)


def params(mebibytes):
    return pltpu.CompilerParams(vmem_limit_bytes=mebibytes * 1024 * 1024)


def after(value, other):
    return lax.optimization_barrier((value, other))[0]

LABELS = 128


def linear(x, y, z, c):
    return ((((y % 2) * 4 + z) * 2 + c) * 2 + y // 2) * 4 + x


def move(value, where):
    perm = []
    for x in range(4):
        for y in range(4):
            for z in range(4):
                for c in range(2):
                    perm.append((linear(x, y, z, c), linear(*where(x, y, z, c))))
    return lax.ppermute(value, AXES, perm)


def swap_core(value):
    return move(value, lambda x, y, z, c: (x, y, z, 1 - c))


def swap_x(value, bits):
    return move(value, lambda x, y, z, c: (x ^ bits, y, z, c))


def swap_y(value, bits):
    return move(value, lambda x, y, z, c: (x, y ^ bits, z, c))


def swap_z(value, bits):
    return move(value, lambda x, y, z, c: (x, y, z ^ bits, c))


def doubled(value, swap, bits):
    return jnp.concatenate([value, swap(value, bits)], axis=0)


def dot(left, right):
    return jnp.dot(left, right, preferred_element_type=F32)


def contract_rows(left, right):
    return lax.dot_general(left, right, (((0,), (0,)), ((), ())), preferred_element_type=F32)


def contract_last(left, right):
    return lax.dot_general(left, right, (((1,), (1,)), ((), ())), preferred_element_type=F32)


def column_offsets(core, width):
    half, part = width // 2, width // 4
    mine = pl.multiple_of(core * half, half)
    other = pl.multiple_of((1 - core) * half, half)
    return (
        (mine, pl.multiple_of(mine + part, part)),
        (other, pl.multiple_of(other + part, part)),
    )


def second_order(half):
    return [r3 * 4 + r1 * 2 + half for r3 in range(2) for r1 in range(2)]


def block_home(x, y_hi, r3, r1, ry):
    return (y_hi ^ ry) * 4 + (x ^ (r1 ^ (3 * r3)))


def forward_kernel(where, lengths, context, residual, gain, labels, *refs):
    firsts, seconds = (refs[0:2], refs[4:6]), (refs[2:4], refs[6:8])
    stream, inverse, pooled, embedding = refs[8:]
    tokens, width = residual.shape
    part = width // 4
    block = context.shape[1] // 8
    items = lengths.shape[0]
    length = tokens // items
    ordered = [
        jnp.concatenate(
            [context[:, b * block : (b + 1) * block] for b in second_order(half)], axis=1
        )
        for half in range(2)
    ]
    for side, (first_at, second_at) in enumerate(column_offsets(where[3], width)):
        acc = residual[:, pl.ds(first_at, part)].astype(F32)
        for half in range(2):
            span = context[:, half * 4 * block : (half + 1) * 4 * block]
            acc = acc + dot(span, firsts[side][half][...])
        stream[:, pl.ds(first_at, part)] = acc
        acc = residual[:, pl.ds(second_at, part)].astype(F32)
        for half in range(2):
            acc = acc + dot(ordered[half], seconds[side][half][...])
        stream[:, pl.ds(second_at, part)] = acc
    for i in range(items):
        rows = stream[i * length : (i + 1) * length, :]
        inv = lax.rsqrt(jnp.mean(rows * rows, axis=-1, keepdims=True) + EPSILON)
        inverse[i * length : (i + 1) * length, :] = inv
        position = lax.broadcasted_iota(jnp.int32, (length, 1), 0)
        kept = jnp.where(position < lengths[i], inv, 0.0)
        total = jnp.sum(rows * kept, axis=0, keepdims=True)
        pooled[i : i + 1, :] = total * gain[...] / lengths[i].astype(F32)
    pool = pooled[...]
    scale = lax.rsqrt(jnp.mean(pool * pool, axis=-1, keepdims=True) + EPSILON)
    embedding[:, :width] = (pool * scale).astype(BF16)
    embedding[:, width:] = labels[...]


def bit(value, k):
    return (value >> k) & 1


def one_hot_turn(rows, home):
    to = lax.broadcasted_iota(jnp.int32, (rows, rows), 0)
    of = lax.broadcasted_iota(jnp.int32, (rows, rows), 1)
    return jnp.where(to == home(of), 1.0, 0.0).astype(BF16)


def loss_kernel(users_here, items_here, where, gain, *refs):
    user_refs, emb_refs = refs[:2], refs[2:6]
    sums, user_grad, grads, emb_grads = refs[6:]
    x, y, z, core = where[0], where[1], where[2], where[3]
    group, full = emb_refs[0].shape
    width = full - LABELS
    items = 4 * group
    people = 2 * user_refs[0].shape[0]

    def item_home(s):
        one = s // items_here
        ax = x ^ bit(one, 0) ^ (3 * bit(one, 1))
        ay = y ^ bit(one, 2) ^ (3 * bit(one, 3))
        az = z ^ bit(one, 4) ^ (3 * bit(one, 5))
        ac = core ^ bit(one, 6)
        return (((ac * 4 + az) * 4 + ay) * 4 + ax) * items_here + s % items_here

    def user_home(s):
        one = s // users_here
        ay = y ^ (3 * bit(one, 0)) ^ bit(one, 1)
        az = z ^ bit(one, 2) ^ (3 * bit(one, 3))
        ac = core ^ bit(one, 4)
        return ((ac * 4 + az) * 4 + ay) * users_here + s % users_here

    placed = jnp.concatenate([ref[...] for ref in emb_refs], axis=0)
    turned = dot(one_hot_turn(items, item_home), placed).astype(BF16)
    emb, labels = turned[:, :width], turned[:, width:]
    placed = jnp.concatenate([ref[...] for ref in user_refs], axis=0)
    turned = dot(one_hot_turn(people, user_home), placed).astype(BF16)
    users = turned[:, :width]
    positive = turned[:, width : width + 1].astype(F32)
    item_labels = contract_rows(labels, one_hot_turn(items, lambda s: s))
    ids = item_labels[0:1, :]
    log_counts = jnp.log(item_labels[1:2, :] * 128.0 + item_labels[2:3, :])
    item = lax.broadcasted_iota(jnp.int32, (1, items), 1)
    chip = item // items_here
    index = linear(chip % 4, (chip // 4) % 4, (chip // 16) % 4, chip // 64) * items_here
    index = (index + item % items_here).astype(F32)
    onehot = index == positive
    positive_id = jnp.sum(jnp.where(onehot, ids, 0.0), axis=1, keepdims=True)
    excluded = (ids == positive_id) & jnp.logical_not(onehot)
    scores = contract_last(users, emb)
    logits = jnp.where(excluded, MASKED_FILL, scores - log_counts)
    row_max = jnp.max(logits, axis=1, keepdims=True)
    weights = jnp.where(excluded, 0.0, jnp.exp(logits - row_max))
    row_total = jnp.sum(weights, axis=1, keepdims=True)
    picked = jnp.sum(jnp.where(onehot, logits, 0.0), axis=1, keepdims=True)
    losses = row_max + jnp.log(row_total) - picked
    grad = (weights / row_total - jnp.where(onehot, 1.0, 0.0)).astype(BF16)
    grads[...] = grad.astype(F32)
    all_grads = contract_rows(grad, users)
    emb_grads[...] = all_grads
    emb_float = emb.astype(F32)
    product = emb_float * all_grads
    mean = jnp.mean(product, axis=-1, keepdims=True)
    gain_sum = jnp.sum(product - emb_float * emb_float * mean, axis=0, keepdims=True)
    place = (core * 4 + z) * 4 + y
    near = 4 * items_here
    sums[:, :width] = emb_grads[pl.ds(pl.multiple_of(place * near, near), near), :]
    piece = width // near
    for j in range(near):
        sums[j : j + 1, width : width + piece] = gain_sum[:, j * piece : (j + 1) * piece]
    loss = jnp.sum(losses, axis=0, keepdims=True)
    sums[:, width + piece :] = jnp.broadcast_to(loss, (near, LABELS))
    own = grads[pl.ds(pl.multiple_of(place * users_here, users_here), users_here), :]
    user_grad[...] = dot(own.astype(BF16), emb).astype(BF16)


def residual_kernel(people, where, lengths, stream, inverse, pooled, gain, sums, *refs):
    residual_grad, send, gain_grad, loss = refs
    tokens, width = stream.shape
    half = width // 2
    items = lengths.shape[0]
    length = tokens // items
    near = sums.shape[0]
    piece = width // near
    line = lax.broadcasted_iota(jnp.int32, (near, 1), 0)
    for i in range(items):
        mine = jnp.sum(
            jnp.where(line == where[0] * items + i, sums[:, :width], 0.0), axis=0, keepdims=True
        )
        pool = pooled[i : i + 1, :]
        scale = lax.rsqrt(jnp.mean(pool * pool, axis=-1, keepdims=True) + EPSILON)
        pool_grad = scale * mine - pool * scale * scale * scale * jnp.mean(
            pool * mine, axis=-1, keepdims=True
        )
        row = gain[...] * pool_grad / lengths[i].astype(F32)
        span = slice(i * length, (i + 1) * length)
        rows = stream[span, :]
        inv = inverse[span, :]
        position = lax.broadcasted_iota(jnp.int32, (length, 1), 0)
        kept = jnp.where(position < lengths[i], inv, 0.0)
        mean = jnp.mean(rows * row, axis=-1, keepdims=True)
        residual_grad[span, :] = (kept * row - rows * (kept * inv * inv * mean)).astype(BF16)
    send[...] = residual_grad[:, pl.ds(pl.multiple_of((1 - where[3]) * half, half), half)]
    for j in range(near):
        at = slice(j * piece, (j + 1) * piece)
        gain_grad[:, at] = sums[j : j + 1, width : width + piece] / gain[:, at]
    loss[...] = sums[0:1, width + piece : width + piece + 1] / people


def context_kernel(where, residual_grad, *refs):
    firsts, seconds = (refs[0:2], refs[4:6]), (refs[2:4], refs[6:8])
    context_grad = refs[8]
    width = residual_grad.shape[1]
    part = width // 4
    block = context_grad.shape[1] // 8
    offsets = column_offsets(where[3], width)
    near = [residual_grad[:, pl.ds(first, part)] for first, _ in offsets]
    far = [residual_grad[:, pl.ds(second, part)] for _, second in offsets]
    from_first = [sum(contract_last(near[s], firsts[s][h][...]) for s in range(2)) for h in range(2)]
    from_second = [sum(contract_last(far[s], seconds[s][h][...]) for s in range(2)) for h in range(2)]
    for r3 in range(2):
        for r1 in range(2):
            for ry in range(2):
                a, b = (r1 * 2 + ry) * block, (r3 * 2 + r1) * block
                value = from_first[r3][:, a : a + block] + from_second[ry][:, b : b + block]
                home = block_home(where[0], where[1] // 2, r3, r1, ry)
                context_grad[:, pl.ds(pl.multiple_of(home * block, block), block)] = value.astype(BF16)


def blocks_kernel(half, where, own_context, peer_context, residual_grad, peer_grad, first, second):
    width = residual_grad.shape[1]
    part = width // 4
    block = own_context.shape[0] // 8
    first_at, second_at = column_offsets(where[3], width)[0]
    span = slice(half * 4 * block, (half + 1) * 4 * block)
    value = dot(own_context[span, :], residual_grad[:, pl.ds(first_at, part)])
    value = value + dot(peer_context[span, :], peer_grad[:, :part])
    first[...] = value.astype(first.dtype)

    def ordered(ref):
        return jnp.concatenate(
            [ref[b * block : (b + 1) * block, :] for b in second_order(half)], axis=0
        )

    value = dot(ordered(own_context), residual_grad[:, pl.ds(second_at, part)])
    value = value + dot(ordered(peer_context), peer_grad[:, part:])
    second[...] = value.astype(second.dtype)


def shaped(shape, dtype=F32):
    return jax.ShapeDtypeStruct(shape, dtype)


def added(kept, sent, swap, bits):
    return kept + swap(sent.astype(BF16), bits).astype(F32)


def folded(value, swap, bits):
    rows = value.shape[0] // 2
    return added(value[:rows], value[rows:], swap, bits)


def all_added(value, swap, bits):
    value = lax.reduce_precision(value, 8, 7)
    return added(value, value, swap, bits)


def on_device(
    context, residual, out_weight, norm_gain, user_vectors, positive, item_ids, item_counts, lengths
):
    tokens, head = context.shape
    width = residual.shape[1]
    items_here = lengths.shape[0]
    users_here = user_vectors.shape[0]
    dp, fsdp = lax.axis_index("dp"), lax.axis_index("fsdp")
    y_lo, z, core = dp // 8, (dp // 2) % 4, dp % 2
    y_hi, x = fsdp // 4, fsdp % 4
    y = y_hi * 2 + y_lo
    where = jnp.stack([x, y, z, core]).astype(jnp.int32)
    half, part = width // 2, width // 4
    rows = out_weight.shape[0]
    gain = norm_gain[None, :]

    mine = lax.dynamic_slice(out_weight, (0, core * half), (rows, half))
    first = doubled(mine[:, :part], swap_y, 3)
    second = doubled(mine[:, part:], swap_x, 1)
    step_one = first
    first = doubled(first, swap_x, 1)
    second = doubled(second, swap_x, 3)
    step_two = first
    firsts = [first, swap_x(first, 3)]
    seconds = [second, swap_y(second, 3)]
    pieces = firsts + seconds
    pieces = pieces + [swap_core(p) for p in pieces]

    order = [
        block_home(x, y_hi, r3, r1, ry) for r3 in range(2) for r1 in range(2) for ry in range(2)
    ]
    later = after(context, step_one)
    turned = jnp.concatenate(
        [lax.dynamic_slice(later, (0, at * rows), (tokens, rows)) for at in order], axis=1
    )

    labels = jnp.pad(positive[:, None], ((0, 0), (0, LABELS - 1))).astype(BF16)
    users = after(jnp.concatenate([user_vectors, labels], axis=1), step_one)
    users = doubled(users, swap_y, 3)
    users = doubled(users, swap_y, 1)
    users = after(users, step_two)
    users = doubled(users, swap_z, 1)
    users = doubled(users, swap_z, 3)
    labels = jnp.stack([item_ids, item_counts // 128, item_counts % 128], axis=1)
    labels = jnp.pad(labels, ((0, 0), (0, LABELS - 3))).astype(BF16)

    stream, inverse, pooled, emb = pl.pallas_call(
        forward_kernel,
        out_shape=(
            shaped((tokens, width)),
            shaped((tokens, 1)),
            shaped((items_here, width)),
            shaped((items_here, width + LABELS), BF16),
        ),
        in_specs=[SMEM, SMEM] + [VMEM] * 12,
        out_specs=(VMEM,) * 4,
        compiler_params=params(20),
        name="forward",
    )(where, lengths, turned, residual, gain, labels, *pieces)

    users, turned = lax.optimization_barrier((users, turned, emb))[:2]
    user_pieces = [users, swap_core(users)]
    own_context = turned.T
    peer_context = swap_core(own_context)
    for swap, bits in ((swap_x, 1), (swap_x, 3), (swap_y, 1), (swap_y, 3), (swap_z, 1)):
        emb = doubled(emb, swap, bits)
    emb_pieces = [emb, swap_z(emb, 3)]
    emb_pieces = emb_pieces + [swap_core(p) for p in emb_pieces]

    near = 4 * items_here
    items, people = 128 * items_here, 32 * users_here
    sums, user_grad = pl.pallas_call(
        functools.partial(loss_kernel, users_here, items_here),
        out_shape=(
            shaped((near, width + width // near + LABELS)),
            shaped((users_here, width), BF16),
        ),
        in_specs=[SMEM] + [VMEM] * 7,
        out_specs=(VMEM,) * 2,
        scratch_shapes=[pltpu.VMEM((people, items), F32), pltpu.VMEM((items, width), F32)],
        compiler_params=params(24),
        name="loss",
    )(where, gain, *user_pieces, *emb_pieces)
    sums = sums + swap_x(sums, 3)
    sums = sums + swap_x(sums, 1)

    residual_grad, send, gain_grad, loss = pl.pallas_call(
        functools.partial(residual_kernel, 4 * people),
        out_shape=(
            shaped((tokens, width), BF16),
            shaped((tokens, half), BF16),
            shaped((1, width)),
            shaped((1, 1)),
        ),
        in_specs=[SMEM, SMEM] + [VMEM] * 5,
        out_specs=(VMEM,) * 4,
        compiler_params=params(16),
        name="residual",
    )(where, lengths, stream, inverse, pooled, gain, sums)
    peer_grad = swap_core(send)
    context_grad = pl.pallas_call(
        context_kernel,
        out_shape=shaped((tokens, head), BF16),
        in_specs=[SMEM] + [VMEM] * 9,
        out_specs=VMEM,
        compiler_params=params(14),
        name="context",
    )(where, residual_grad, *pieces)

    operands = (where, own_context, peer_context, residual_grad, peer_grad)

    def blocks(which, dtype, name):
        return pl.pallas_call(
            functools.partial(blocks_kernel, which),
            out_shape=(shaped((4 * rows, part), dtype),) * 2,
            in_specs=[SMEM] + [VMEM] * 4,
            out_specs=(VMEM,) * 2,
            compiler_params=params(14),
            name=name,
        )(*operands)

    first_sent, second_sent = blocks(1, BF16, "blocks_sent")
    first, second = blocks(0, F32, "blocks_kept")
    first = added(first, first_sent, swap_x, 3)
    second = added(second, second_sent, swap_y, 3)
    first = folded(first, swap_x, 1)
    second = folded(second, swap_x, 3)
    first = folded(first, swap_y, 3)
    second = folded(second, swap_x, 1)
    first, second, context_grad = lax.optimization_barrier((first, second, context_grad))
    first = all_added(first, swap_y, 1)
    second = all_added(second, swap_z, 1)
    first = all_added(first, swap_z, 1)
    second = all_added(second, swap_z, 3)
    first = all_added(first, swap_z, 3)
    second = all_added(second, swap_y, 1)
    own = jnp.concatenate([first, second], axis=1).astype(BF16)
    other = swap_core(own)
    weight_grad = jnp.where(
        core == 0, jnp.concatenate([own, other], axis=1), jnp.concatenate([other, own], axis=1)
    )
    return (loss[0, 0], residual_grad, context_grad, weight_grad, gain_grad[0], user_grad)


def solution(mesh):
    placed = (
        P(AXES, None),
        P(AXES, None),
        P("fsdp", None),
        P(),
        P(AXES, None),
        P(AXES),
        P(AXES),
        P(AXES),
        P(AXES),
    )
    return jax.shard_map(
        on_device,
        mesh=mesh,
        in_specs=placed,
        out_specs=(P(), P(AXES, None), P(AXES, None), P("fsdp", None), P(), P(AXES, None)),
        check_vma=False,
    )
```

time: 1260 us -> 161 us (0.13)
  waiting for transfers between devices: 797 us -> 47 us
  blocking collectives: 397 us -> 0 us
  starting transfers between devices: 0.16 us -> 71.8 us
  Pallas kernels: 0 us -> 21.3 us
  matrix products: 20.1 us -> 0 us
  between operations: 15.8 us -> 1.09 us
    reduce_scatter x1 -> x0, waiting for transfers between devices: 564 us -> none  [on_device(): lax.psum_scatter(contract_rows(columns, residual_grad), ('dp', 'fsdp'), s...]
    all_gather x2 -> x0, blocking collectives: 331 us -> none  [the longest x1 299 us: on_device(): keys_all = lax.all_gather(keys, ('dp', 'fsdp'), axis=0, tiled=True)]
    unnamed x5 -> x0, waiting for transfers between devices: 157 us -> none
    all_gather x2 -> x0, waiting for transfers between devices: 75.4 us -> none  [the longest x1 75.3 us: on_device(): lax.all_gather(out_weight, 'fsdp', axis=0, tiled=True)]
    ppermute x0 -> x40, starting transfers between devices: none -> 71.8 us  [move(): return lax.ppermute(value, AXES, perm)]
    psum x1 -> x0, blocking collectives: 65.5 us -> none  [on_device(): loss_sum, gain_grad = lax.psum((loss_part, gain_part), ('dp', 'fsdp'))]
    ppermute x0 -> x40, waiting for transfers between devices: none -> 47 us  [move(): return lax.ppermute(value, AXES, perm)]
    pallas_call x0 -> x6, Pallas kernels: none -> 21.3 us  [the longest x1 5.39 us: on_device(): pl.pallas_call(context_kernel, out_shape=shaped((tokens, head), BF16), in...]
  transfers between devices with their start and end apart: 4 -> 40, of which waited for: 3 -> 24; matrix products, arithmetic and copies ran while one was open for 1% -> 6% of each run, Pallas kernels for 0% -> 9%
where the time goes in v1:
time: 161 us
  starting transfers between devices  71.8 us (45%)
  waiting for transfers between devices  47 us (29%)
  Pallas kernels  21.3 us (13%)
  local copies, waits for them, and re-layouts  14 us (9%)
  other arithmetic  5.37 us (3%)
    ppermute x40, starting transfers between devices, move(): return lax.ppermute(value, AXES, perm)  71.8 us
    ppermute x40, waiting for transfers between devices, move(): return lax.ppermute(value, AXES, perm)  47 us
    unnamed x23, local copies, waits for them, and re-layouts  7.48 us
    pallas_call x1, Pallas kernels, on_device(): pl.pallas_call(context_kernel, out_shape=shaped((tokens, head), BF16), in...  5.39 us
    pallas_call x1, Pallas kernels, on_device(): pl.pallas_call(forward_kernel, out_shape=(shaped((tokens, width)), shaped...  4.94 us
    pallas_call x1, Pallas kernels, on_device(): pl.pallas_call(functools.partial(loss_kernel, users_here, items_here), ou...  4.44 us
    pallas_call x2, Pallas kernels, blocks(): pl.pallas_call(functools.partial(blocks_kernel, which), out_shape=(shaped...  3.6 us
  transfers between devices with their start and end apart: 40, of which 24 were waited for; matrix products, arithmetic and copies ran while one was open for 6% of the time, Pallas kernels for 9%

profile of v1, /device:TPU:1, one launch (start us, length us, event | category | flops | bytes accessed | tf_op | source)
XLA Modules:
  0.0 160.6 jit_solution(8875396074671823068)
XLA Ops:
  0.7 1.0 constant_dynamic-slice_fusion.1
  1.7 2.1 %collective-permute-start.3 = (bf16[128,512]{1,0:T(8,128)(2,1)S(1)}, bf16[128,512]{1,0:T(8,128)(2,1)S(1)}, u32[]{:S(2)}, u32[]{:S(2)}) collective-permute-start(bf16[128,512]{1,0:T(8,128)(2,1)S(1)} %get-tuple-element.50), channel_id=1, source_target_pairs={{0,1},{8,9},{16,17},{24,25},{32,33},{40,41},{48,49},{56,57},{64,65... | collective-permute-start | bytes 393224 | tf_op jit(solution)/shard_map/ppermute | solution.py:41
  3.8 2.7 %collective-permute-start = (bf16[128,512]{1,0:T(8,128)(2,1)S(1)}, bf16[128,512]{1,0:T(8,128)(2,1)S(1)}, u32[]{:S(2)}, u32[]{:S(2)}) collective-permute-start(bf16[128,512]{1,0:T(8,128)(2,1)S(1)} %get-tuple-element.51), channel_id=1, source_target_pairs={{0,68},{8,76},{16,84},{24,92},{32,100},{40,108},{48,116},{56,124},... | collective-permute-start | bytes 393224 | tf_op jit(solution)/shard_map/ppermute | solution.py:41
  6.5 0.7 convert_bitcast_fusion
  7.3 0.8 fusion.5
  8.9 0.7 collective-permute-start.1
  9.6 2.2 %collective-permute-start.4 = (bf16[256,512]{1,0:T(8,128)(2,1)S(1)}, bf16[256,512]{1,0:T(8,128)(2,1)S(1)}, u32[]{:S(2)}, u32[]{:S(2)}) collective-permute-start(bf16[256,512]{1,0:T(8,128)(2,1)S(1)} %pad_maximum_fusion.5), channel_id=1, source_target_pairs={{0,3},{8,11},{16,19},{24,27},{32,35},{40,43},{48,51},{56,59},{64,6... | collective-permute-start | bytes 786440 | tf_op jit(solution)/shard_map/ppermute | solution.py:41
  12.0 2.6 %collective-permute-done.1 = bf16[256,512]{1,0:T(8,128)(2,1)S(1)} collective-permute-done((bf16[256,512]{1,0:T(8,128)(2,1)S(1)}, bf16[256,512]{1,0:T(8,128)(2,1)S(1)}, u32[]{:S(2)}, u32[]{:S(2)}) %collective-permute-start.1) | collective-permute-done | bytes 262176 | tf_op jit(solution)/shard_map/ppermute | solution.py:41
  14.7 1.9 %collective-permute-start.2 = (bf16[512,512]{1,0:T(8,128)(2,1)S(1)}, bf16[512,512]{1,0:T(8,128)(2,1)}, u32[]{:S(2)}, u32[]{:S(2)}) collective-permute-start(bf16[512,512]{1,0:T(8,128)(2,1)S(1)} %pad_maximum_fusion.1.refs_0_), channel_id=1, source_target_pairs={{0,3},{8,11},{16,19},{24,27},{32,35},{40,43},{48,51},{56,59},{64,6... | collective-permute-start | bytes 1572872 | tf_op jit(solution)/shard_map/ppermute | solution.py:41
  16.8 2.6 %collective-permute-start.5 = (bf16[512,512]{1,0:T(8,128)(2,1)S(1)}, bf16[512,512]{1,0:T(8,128)(2,1)}, u32[]{:S(2)}, u32[]{:S(2)}) collective-permute-start(bf16[512,512]{1,0:T(8,128)(2,1)S(1)} %pad_maximum_fusion.2.refs_2_), channel_id=1, source_target_pairs={{0,68},{8,76},{16,84},{24,92},{32,100},{40,108},{48,116},{56,124},... | collective-permute-start | bytes 1572872 | tf_op jit(solution)/shard_map/ppermute | solution.py:41
  19.7 1.5 copy.15
  21.3 4.0 %collective-permute-start.6 = (bf16[512,512]{1,0:T(8,128)(2,1)S(1)}, bf16[512,512]{1,0:T(8,128)(2,1)}, u32[]{:S(2)}, u32[]{:S(2)}) collective-permute-start(bf16[512,512]{1,0:T(8,128)(2,1)S(1)} %pad_maximum_fusion.1.refs_0_), channel_id=1, source_target_pairs={{0,8},{8,0},{16,24},{24,16},{32,40},{40,32},{48,56},{56,48},{64,72... | collective-permute-start | bytes 1572872 | tf_op jit(solution)/shard_map/ppermute | solution.py:41
  25.4 2.2 %collective-permute-done.2.refs_1_ = bf16[512,512]{1,0:T(8,128)(2,1)} collective-permute-done((bf16[512,512]{1,0:T(8,128)(2,1)S(1)}, bf16[512,512]{1,0:T(8,128)(2,1)}, u32[]{:S(2)}, u32[]{:S(2)}) %collective-permute-start.2) | collective-permute-done | bytes 524320 | tf_op jit(solution)/shard_map/ppermute | solution.py:41
  27.6 3.4 %collective-permute-start.7 = (bf16[512,512]{1,0:T(8,128)(2,1)}, bf16[512,512]{1,0:T(8,128)(2,1)}, u32[]{:S(2)}, u32[]{:S(2)}) collective-permute-start(bf16[512,512]{1,0:T(8,128)(2,1)} %collective-permute-done.2.refs_1_), channel_id=1, source_target_pairs={{0,8},{8,0},{16,24},{24,16},{32,40},{40,32},{48,56},{56,48},{64,72... | collective-permute-start | bytes 1572872 | tf_op jit(solution)/shard_map/ppermute | solution.py:41
  31.0 1.9 %collective-permute-start.9 = (bf16[512,512]{1,0:T(8,128)(2,1)}, bf16[512,512]{1,0:T(8,128)(2,1)}, u32[]{:S(2)}, u32[]{:S(2)}) collective-permute-start(bf16[512,512]{1,0:T(8,128)(2,1)} %collective-permute-done.5.refs_3_), channel_id=1, source_target_pairs={{0,8},{8,0},{16,24},{24,16},{32,40},{40,32},{48,56},{56,48},{64,72... | collective-permute-start | bytes 1572872 | tf_op jit(solution)/shard_map/ppermute | solution.py:41
  33.6 1.2 collective-permute-done.9.refs_7_
  34.8 1.6 copy-done.4
  36.4 4.9 %forward.1 = (f32[512,2048]{1,0:T(8,128)S(1)}, f32[512,1]{1,0:T(8,128)S(1)}, f32[2,2048]{1,0:T(2,128)S(1)}, bf16[2,2176]{1,0:T(2,128)(2,1)S(1)}) custom-call(s32[4]{0:T(128)S(1)} %pad_add_fusion.where, s32[2]{0:T(128)S(1)} %copy-done.6, bf16[512,1024]{1,0:T(8,128)(2,1)S(1)} %copy.26.context, bf16[512,2048]{1,0:T(8,128)(2,1)S(1)} %copy-done.4, ...), custom_call_target="tpu_custom_call" | custom-call | tf_op jit(solution)/shard_map/forward/pallas_call | solution.py:347
  41.3 2.0 %copy-done.2 = f32[512,2048]{1,0:T(8,128)} copy-done((f32[512,2048]{1,0:T(8,128)}, f32[512,2048]{1,0:T(8,128)S(1)}, u32[]{:S(2)}) %copy-start.2) | copy-done | bytes 4194328
  43.6 2.2 %collective-permute-done.15 = bf16[2,2176]{1,0:T(2,128)(2,1)S(1)} collective-permute-done((bf16[2,2176]{1,0:T(2,128)(2,1)S(1)}, bf16[2,2176]{1,0:T(2,128)(2,1)S(1)}, u32[]{:S(2)}, u32[]{:S(2)}) %collective-permute-start.15) | collective-permute-done | bytes 8736 | tf_op jit(solution)/shard_map/ppermute | solution.py:41
  45.8 1.6 collective-permute-start.16
  47.4 1.7 %collective-permute-start.12 = (bf16[32,2176]{1,0:T(8,128)(2,1)S(1)}, bf16[32,2176]{1,0:T(8,128)(2,1)S(1)}, u32[]{:S(2)}, u32[]{:S(2)}) collective-permute-start(bf16[32,2176]{1,0:T(8,128)(2,1)S(1)} %pad_maximum_fusion.7), channel_id=1, source_target_pairs={{0,16},{8,24},{16,0},{24,8},{32,48},{40,56},{48,32},{56,40},{64,80... | collective-permute-start | bytes 417800 | tf_op jit(solution)/shard_map/ppermute | solution.py:41
  49.9 2.0 %collective-permute-done.12 = bf16[32,2176]{1,0:T(8,128)(2,1)S(1)} collective-permute-done((bf16[32,2176]{1,0:T(8,128)(2,1)S(1)}, bf16[32,2176]{1,0:T(8,128)(2,1)S(1)}, u32[]{:S(2)}, u32[]{:S(2)}) %collective-permute-start.12) | collective-permute-done | bytes 139296 | tf_op jit(solution)/shard_map/ppermute | solution.py:41
  51.9 3.7 %collective-permute-start.13 = (bf16[64,2176]{1,0:T(8,128)(2,1)S(1)}, bf16[64,2176]{1,0:T(8,128)(2,1)}, u32[]{:S(2)}, u32[]{:S(2)}) collective-permute-start(bf16[64,2176]{1,0:T(8,128)(2,1)S(1)} %pad_maximum_fusion.3), channel_id=1, source_target_pairs={{0,48},{8,56},{16,32},{24,40},{32,16},{40,24},{48,0},{56,8},{64,11... | collective-permute-start | bytes 835592 | tf_op jit(solution)/shard_map/ppermute | solution.py:41
  55.6 2.7 %collective-permute-start.18 = (bf16[16,2176]{1,0:T(8,128)(2,1)S(1)}, bf16[16,2176]{1,0:T(8,128)(2,1)S(1)}, u32[]{:S(2)}, u32[]{:S(2)}) collective-permute-start(bf16[16,2176]{1,0:T(8,128)(2,1)S(1)} %pad_maximum_fusion.9), channel_id=1, source_target_pairs={{0,68},{8,76},{16,84},{24,92},{32,100},{40,108},{48,116},{56,124},... | collective-permute-start | bytes 208904 | tf_op jit(solution)/shard_map/ppermute | solution.py:41
  58.4 2.1 %collective-permute-done.18 = bf16[16,2176]{1,0:T(8,128)(2,1)S(1)} collective-permute-done((bf16[16,2176]{1,0:T(8,128)(2,1)S(1)}, bf16[16,2176]{1,0:T(8,128)(2,1)S(1)}, u32[]{:S(2)}, u32[]{:S(2)}) %collective-permute-start.18) | collective-permute-done | bytes 69664 | tf_op jit(solution)/shard_map/ppermute | solution.py:41
  60.5 1.9 %concatenate.78 = bf16[32,2176]{1,0:T(8,128)(2,1)} concatenate(bf16[2,2176]{1,0:T(2,128)(2,1)S(1)} %get-tuple-element.34, bf16[2,2176]{1,0:T(2,128)(2,1)S(1)} %collective-permute-done.15, bf16[4,2176]{1,0:T(4,128)(2,1)S(1)} %collective-permute-done.16, bf16[8,2176]{1,0:T(8,128)(2,1)S(1)} %collective-permute-done.17, bf16[16,2176]{1,0:T(8,128)(2,1)S(1)} %collective-permute-done.18), dimensions={0} | concatenate | bytes 278528 | tf_op jit(solution)/shard_map/concatenate | solution.py:61
  62.4 1.0 pad_maximum_fusion.refs_0_
  63.4 3.8 %collective-permute-start.14 = (bf16[128,2176]{1,0:T(8,128)(2,1)S(1)}, bf16[128,2176]{1,0:T(8,128)(2,1)}, u32[]{:S(2)}, u32[]{:S(2)}) collective-permute-start(bf16[128,2176]{1,0:T(8,128)(2,1)S(1)} %pad_maximum_fusion.refs_0_), channel_id=1, source_target_pairs={{0,8},{8,0},{16,24},{24,16},{32,40},{40,32},{48,56},{56,48},{64,72... | collective-permute-start | bytes 1671176 | tf_op jit(solution)/shard_map/ppermute | solution.py:41
  67.2 1.0 concatenate.79.refs_2_
  68.2 2.0 %collective-permute-start.20 = (bf16[64,2176]{1,0:T(8,128)(2,1)S(1)}, bf16[64,2176]{1,0:T(8,128)(2,1)S(1)}, u32[]{:S(2)}, u32[]{:S(2)}) collective-permute-start(bf16[64,2176]{1,0:T(8,128)(2,1)S(1)} %concatenate.79.refs_2_), channel_id=1, source_target_pairs={{0,48},{8,56},{16,32},{24,40},{32,16},{40,24},{48,0},{56,8},{64,11... | collective-permute-start | bytes 835592 | tf_op jit(solution)/shard_map/ppermute | solution.py:41
  70.3 4.2 %collective-permute-start.21 = (bf16[64,2176]{1,0:T(8,128)(2,1)S(1)}, bf16[64,2176]{1,0:T(8,128)(2,1)S(1)}, u32[]{:S(2)}, u32[]{:S(2)}) collective-permute-start(bf16[64,2176]{1,0:T(8,128)(2,1)S(1)} %concatenate.79.refs_2_), channel_id=1, source_target_pairs={{0,8},{8,0},{16,24},{24,16},{32,40},{40,32},{48,56},{56,48},{64,72... | collective-permute-start | bytes 835592 | tf_op jit(solution)/shard_map/ppermute | solution.py:41
  74.9 5.4 %collective-permute-start.22 = (bf16[64,2176]{1,0:T(8,128)(2,1)S(1)}, bf16[64,2176]{1,0:T(8,128)(2,1)S(1)}, u32[]{:S(2)}, u32[]{:S(2)}) collective-permute-start(bf16[64,2176]{1,0:T(8,128)(2,1)S(1)} %collective-permute-done.20.refs_3_), channel_id=1, source_target_pairs={{0,8},{8,0},{16,24},{24,16},{32,40},{40,32},{48,56},{56,48},{64,72... | collective-permute-start | bytes 835592 | tf_op jit(solution)/shard_map/ppermute | solution.py:41
  80.3 1.2 collective-permute-done.22.refs_5_
  81.5 4.4 %loss.1 = (f32[8,2432]{1,0:T(8,128)S(1)}, bf16[8,2048]{1,0:T(8,128)(2,1)}) custom-call(s32[4]{0:T(128)S(1)} %pad_add_fusion.where, f32[1,2048]{1,0:T(1,128)S(1)} %bitcast.20, bf16[128,2176]{1,0:T(8,128)(2,1)S(1)} %pad_maximum_fusion.refs_0_, bf16[128,2176]{1,0:T(8,128)(2,1)} %collective-permute-done.14.refs_1_, bf16[64,2176]{1,0:T(8,128)(2,1)S(1)} %concatenate.79.refs_2_, ...), custom_call_target="tpu_custom_call" | custom-call | tf_op jit(solution)/shard_map/loss/pallas_call | solution.py:372
  86.0 1.0 collective-permute-start.23
  87.0 3.4 %collective-permute-done.23 = f32[8,2432]{1,0:T(8,128)S(1)} collective-permute-done((f32[8,2432]{1,0:T(8,128)S(1)}, f32[8,2432]{1,0:T(8,128)S(1)}, u32[]{:S(2)}, u32[]{:S(2)}) %collective-permute-start.23) | collective-permute-done | bytes 77856 | tf_op jit(solution)/shard_map/ppermute | solution.py:41
  90.5 1.6 collective-permute-start.25
  92.1 1.6 %collective-permute-done.24 = f32[8,2432]{1,0:T(8,128)S(1)} collective-permute-done((f32[8,2432]{1,0:T(8,128)S(1)}, f32[8,2432]{1,0:T(8,128)S(1)}, u32[]{:S(2)}, u32[]{:S(2)}) %collective-permute-start.24) | collective-permute-done | bytes 77856 | tf_op jit(solution)/shard_map/ppermute | solution.py:41
  93.8 2.2 %copy-done.3 = f32[512,2048]{1,0:T(8,128)S(1)} copy-done((f32[512,2048]{1,0:T(8,128)S(1)}, f32[512,2048]{1,0:T(8,128)}, u32[]{:S(2)}) %copy-start.3) | copy-done | bytes 4194328
  96.0 3.0 %residual.3 = (bf16[512,2048]{1,0:T(8,128)(2,1)}, bf16[512,1024]{1,0:T(8,128)(2,1)S(1)}, f32[1,2048]{1,0:T(1,128)}, f32[1,1]{1,0:T(1,128)}) custom-call(s32[4]{0:T(128)S(1)} %pad_add_fusion.where, s32[2]{0:T(128)S(1)} %copy-done.6, f32[512,2048]{1,0:T(8,128)S(1)} %copy-done.3, f32[512,1]{1,0:T(8,128)S(1)} %get-tuple-element.30.inverse, ...), custom_call_target="tpu_custom_call" | custom-call | tf_op jit(solution)/shard_map/residual/pallas_call | solution.py:387
  98.9 2.7 %collective-permute-start.26 = (bf16[512,1024]{1,0:T(8,128)(2,1)S(1)}, bf16[512,1024]{1,0:T(8,128)(2,1)S(1)}, u32[]{:S(2)}, u32[]{:S(2)}) collective-permute-start(bf16[512,1024]{1,0:T(8,128)(2,1)S(1)} %get-tuple-element.40), channel_id=1, source_target_pairs={{0,8},{8,0},{16,24},{24,16},{32,40},{40,32},{48,56},{56,48},{64,72... | collective-permute-start | bytes 3145736 | tf_op jit(solution)/shard_map/ppermute | solution.py:41
  101.6 2.3 %collective-permute-done.26.peer_grad = bf16[512,1024]{1,0:T(8,128)(2,1)S(1)} collective-permute-done((bf16[512,1024]{1,0:T(8,128)(2,1)S(1)}, bf16[512,1024]{1,0:T(8,128)(2,1)S(1)}, u32[]{:S(2)}, u32[]{:S(2)}) %collective-permute-start.26) | collective-permute-done | bytes 1048608 | tf_op jit(solution)/shard_map/ppermute | solution.py:41
  103.9 1.6 copy-done
  105.5 1.8 %blocks_sent.1 = (bf16[512,512]{1,0:T(8,128)(2,1)S(1)}, bf16[512,512]{1,0:T(8,128)(2,1)S(1)}) custom-call(s32[4]{0:T(128)S(1)} %pad_add_fusion.where, bf16[1024,512]{1,0:T(8,128)(2,1)S(1)} %bitcast.17, bf16[1024,512]{1,0:T(8,128)(2,1)S(1)} %collective-permute-done.25.peer_context, bf16[512,2048]{1,0:T(8,128)(2,1)S(1)} %copy-done, ...), custom_call_target="tpu_custom_call" | custom-call | tf_op jit(solution)/shard_map/blocks_sent/pallas_call | solution.py:413
  107.3 1.1 collective-permute-start.27
  108.4 2.7 %collective-permute-start.30 = (bf16[512,512]{1,0:T(8,128)(2,1)S(1)}, bf16[512,512]{1,0:T(8,128)(2,1)S(1)}, u32[]{:S(2)}, u32[]{:S(2)}) collective-permute-start(bf16[512,512]{1,0:T(8,128)(2,1)S(1)} %get-tuple-element.44), channel_id=1, source_target_pairs={{0,68},{8,76},{16,84},{24,92},{32,100},{40,108},{48,116},{56,124},... | collective-permute-start | bytes 1572872 | tf_op jit(solution)/shard_map/ppermute | solution.py:41
  111.1 1.8 %blocks_kept.1 = (f32[512,512]{1,0:T(8,128)S(1)}, f32[512,512]{1,0:T(8,128)S(1)}) custom-call(s32[4]{0:T(128)S(1)} %pad_add_fusion.where, bf16[1024,512]{1,0:T(8,128)(2,1)S(1)} %bitcast.18, bf16[1024,512]{1,0:T(8,128)(2,1)S(1)} %collective-permute-done.25.peer_context, bf16[512,2048]{1,0:T(8,128)(2,1)S(1)} %copy-done, ...), custom_call_target="tpu_custom_call" | custom-call | tf_op jit(solution)/shard_map/blocks_kept/pallas_call | solution.py:413
  112.9 8.8 %collective-permute-done.27 = bf16[512,512]{1,0:T(8,128)(2,1)S(1)} collective-permute-done((bf16[512,512]{1,0:T(8,128)(2,1)S(1)}, bf16[512,512]{1,0:T(8,128)(2,1)S(1)}, u32[]{:S(2)}, u32[]{:S(2)}) %collective-permute-start.27) | collective-permute-done | bytes 524320 | tf_op jit(solution)/shard_map/ppermute | solution.py:41
  122.6 1.7 %collective-permute-start.31 = (bf16[256,512]{1,0:T(8,128)(2,1)S(1)}, bf16[256,512]{1,0:T(8,128)(2,1)S(1)}, u32[]{:S(2)}, u32[]{:S(2)}) collective-permute-start(bf16[256,512]{1,0:T(8,128)(2,1)S(1)} %slice.60), channel_id=1, source_target_pairs={{0,3},{8,11},{16,19},{24,27},{32,35},{40,43},{48,51},{56,59},{64,6... | collective-permute-start | bytes 786440 | tf_op jit(solution)/shard_map/ppermute | solution.py:41
  124.4 5.4 %context.1 = bf16[512,1024]{1,0:T(8,128)(2,1)} custom-call(s32[4]{0:T(128)S(1)} %pad_add_fusion.where, bf16[512,2048]{1,0:T(8,128)(2,1)S(1)} %copy-done.1, bf16[512,512]{1,0:T(8,128)(2,1)S(1)} %pad_maximum_fusion.1.refs_0_, bf16[512,512]{1,0:T(8,128)(2,1)} %collective-permute-done.2.refs_1_, bf16[512,512]{1,0:T(8,128)(2,1)S(1)} %pad_maximum_fusion.2.refs_2_, ...), custom_call_target="tpu_custom_call" | custom-call | tf_op jit(solution)/shard_map/context/pallas_call | solution.py:401
  129.9 2.7 %collective-permute-start.29 = (bf16[128,512]{1,0:T(8,128)(2,1)S(1)}, bf16[128,512]{1,0:T(8,128)(2,1)S(1)}, u32[]{:S(2)}, u32[]{:S(2)}) collective-permute-start(bf16[128,512]{1,0:T(8,128)(2,1)S(1)} %slice.63), channel_id=1, source_target_pairs={{0,68},{8,76},{16,84},{24,92},{32,100},{40,108},{48,116},{56,124},... | collective-permute-start | bytes 393224 | tf_op jit(solution)/shard_map/ppermute | solution.py:41
  132.7 0.8 collective-permute-start.32
  133.5 1.5 collective-permute-done.29
  135.0 1.9 %collective-permute-done.32 = bf16[128,512]{1,0:T(8,128)(2,1)S(1)} collective-permute-done((bf16[128,512]{1,0:T(8,128)(2,1)S(1)}, bf16[128,512]{1,0:T(8,128)(2,1)S(1)}, u32[]{:S(2)}, u32[]{:S(2)}) %collective-permute-start.32) | collective-permute-done | bytes 131104 | tf_op jit(solution)/shard_map/ppermute | solution.py:41
  137.2 3.7 %collective-permute-done.36 = bf16[128,512]{1,0:T(8,128)(2,1)S(1)} collective-permute-done((bf16[128,512]{1,0:T(8,128)(2,1)S(1)}, bf16[128,512]{1,0:T(8,128)(2,1)S(1)}, u32[]{:S(2)}, u32[]{:S(2)}) %collective-permute-start.36) | collective-permute-done | bytes 131104 | tf_op jit(solution)/shard_map/ppermute | solution.py:41
  140.9 1.9 %collective-permute-start.37 = (bf16[128,512]{1,0:T(8,128)(2,1)S(1)}, bf16[128,512]{1,0:T(8,128)(2,1)S(1)}, u32[]{:S(2)}, u32[]{:S(2)}) collective-permute-start(bf16[128,512]{1,0:T(8,128)(2,1)S(1)} %fusion.4), channel_id=1, source_target_pairs={{0,48},{8,56},{16,32},{24,40},{32,16},{40,24},{48,0},{56,8},{64,11... | collective-permute-start | bytes 393224 | tf_op jit(solution)/shard_map/ppermute | solution.py:41
  143.0 3.1 %collective-permute-done.37 = bf16[128,512]{1,0:T(8,128)(2,1)S(1)} collective-permute-done((bf16[128,512]{1,0:T(8,128)(2,1)S(1)}, bf16[128,512]{1,0:T(8,128)(2,1)S(1)}, u32[]{:S(2)}, u32[]{:S(2)}) %collective-permute-start.37) | collective-permute-done | bytes 131104 | tf_op jit(solution)/shard_map/ppermute | solution.py:41
  146.8 1.3 collective-permute-start.35
  148.2 2.1 %collective-permute-done.38 = bf16[128,512]{1,0:T(8,128)(2,1)S(1)} collective-permute-done((bf16[128,512]{1,0:T(8,128)(2,1)S(1)}, bf16[128,512]{1,0:T(8,128)(2,1)S(1)}, u32[]{:S(2)}, u32[]{:S(2)}) %collective-permute-start.38) | collective-permute-done | bytes 131104 | tf_op jit(solution)/shard_map/ppermute | solution.py:41
  150.4 1.6 %collective-permute-done.35 = bf16[128,512]{1,0:T(8,128)(2,1)S(1)} collective-permute-done((bf16[128,512]{1,0:T(8,128)(2,1)S(1)}, bf16[128,512]{1,0:T(8,128)(2,1)S(1)}, u32[]{:S(2)}, u32[]{:S(2)}) %collective-permute-start.35) | collective-permute-done | bytes 131104 | tf_op jit(solution)/shard_map/ppermute | solution.py:41
  152.1 6.4 %collective-permute-start.39 = (bf16[128,1024]{1,0:T(8,128)(2,1)S(1)}, bf16[128,1024]{1,0:T(8,128)(2,1)S(1)}, u32[]{:S(2)}, u32[]{:S(2)}) collective-permute-start(bf16[128,1024]{1,0:T(8,128)(2,1)S(1)} %pad_maximum_fusion.6), channel_id=1, source_target_pairs={{0,8},{8,0},{16,24},{24,16},{32,40},{40,32},{48,56},{56,48},{64,72... | collective-permute-start | bytes 786440 | tf_op jit(solution)/shard_map/ppermute | solution.py:41
  158.5 1.2 collective-permute-done.39
  159.7 0.9 maximum_select_fusion
  (94 shorter events, 6.7 us)
Async XLA Ops:
  0.6 11.2 %copy-start.7 = (s32[2]{0:T(128)S(1)}, s32[2]{0:T(128)}, u32[]{:S(2)}) copy-start(s32[2]{0:T(128)} %param.16) | copy-start | bytes 28
  1.7 8.0 %collective-permute-start.3 = (bf16[128,512]{1,0:T(8,128)(2,1)S(1)}, bf16[128,512]{1,0:T(8,128)(2,1)S(1)}, u32[]{:S(2)}, u32[]{:S(2)}) collective-permute-start(bf16[128,512]{1,0:T(8,128)(2,1)S(1)} %get-tuple-element.50), channel_id=1, source_target_pairs={{0,1},{8,9},{16,17},{24,25},{32,33},{40,41},{48,49},{56,57},{64,65... | collective-permute-start | bytes 393224 | tf_op jit(solution)/shard_map/ppermute | solution.py:41
  3.8 5.1 %collective-permute-start = (bf16[128,512]{1,0:T(8,128)(2,1)S(1)}, bf16[128,512]{1,0:T(8,128)(2,1)S(1)}, u32[]{:S(2)}, u32[]{:S(2)}) collective-permute-start(bf16[128,512]{1,0:T(8,128)(2,1)S(1)} %get-tuple-element.51), channel_id=1, source_target_pairs={{0,68},{8,76},{16,84},{24,92},{32,100},{40,108},{48,116},{56,124},... | collective-permute-start | bytes 393224 | tf_op jit(solution)/shard_map/ppermute | solution.py:41
  8.9 5.8 %collective-permute-start.1 = (bf16[256,512]{1,0:T(8,128)(2,1)S(1)}, bf16[256,512]{1,0:T(8,128)(2,1)S(1)}, u32[]{:S(2)}, u32[]{:S(2)}) collective-permute-start(bf16[256,512]{1,0:T(8,128)(2,1)S(1)} %pad_maximum_fusion.4), channel_id=1, source_target_pairs={{0,1},{8,9},{16,17},{24,25},{32,33},{40,41},{48,49},{56,57},{64,65... | collective-permute-start | bytes 786440 | tf_op jit(solution)/shard_map/ppermute | solution.py:41
  9.6 7.1 %collective-permute-start.4 = (bf16[256,512]{1,0:T(8,128)(2,1)S(1)}, bf16[256,512]{1,0:T(8,128)(2,1)S(1)}, u32[]{:S(2)}, u32[]{:S(2)}) collective-permute-start(bf16[256,512]{1,0:T(8,128)(2,1)S(1)} %pad_maximum_fusion.5), channel_id=1, source_target_pairs={{0,3},{8,11},{16,19},{24,27},{32,35},{40,43},{48,51},{56,59},{64,6... | collective-permute-start | bytes 786440 | tf_op jit(solution)/shard_map/ppermute | solution.py:41
  14.7 12.9 %collective-permute-start.2 = (bf16[512,512]{1,0:T(8,128)(2,1)S(1)}, bf16[512,512]{1,0:T(8,128)(2,1)}, u32[]{:S(2)}, u32[]{:S(2)}) collective-permute-start(bf16[512,512]{1,0:T(8,128)(2,1)S(1)} %pad_maximum_fusion.1.refs_0_), channel_id=1, source_target_pairs={{0,3},{8,11},{16,19},{24,27},{32,35},{40,43},{48,51},{56,59},{64,6... | collective-permute-start | bytes 1572872 | tf_op jit(solution)/shard_map/ppermute | solution.py:41
  16.8 14.2 %collective-permute-start.5 = (bf16[512,512]{1,0:T(8,128)(2,1)S(1)}, bf16[512,512]{1,0:T(8,128)(2,1)}, u32[]{:S(2)}, u32[]{:S(2)}) collective-permute-start(bf16[512,512]{1,0:T(8,128)(2,1)S(1)} %pad_maximum_fusion.2.refs_2_), channel_id=1, source_target_pairs={{0,68},{8,76},{16,84},{24,92},{32,100},{40,108},{48,116},{56,124},... | collective-permute-start | bytes 1572872 | tf_op jit(solution)/shard_map/ppermute | solution.py:41
  19.5 23.9 %collective-permute-start.10 = (bf16[8,2176]{1,0:T(8,128)(2,1)S(1)}, bf16[8,2176]{1,0:T(8,128)(2,1)S(1)}, u32[]{:S(2)}, u32[]{:S(2)}) collective-permute-start(bf16[8,2176]{1,0:T(8,128)(2,1)S(1)} %fusion.5), channel_id=1, source_target_pairs={{0,68},{8,76},{16,84},{24,92},{32,100},{40,108},{48,116},{56,124},... | collective-permute-start | bytes 104456 | tf_op jit(solution)/shard_map/ppermute | solution.py:41
  21.3 12.3 %collective-permute-start.6 = (bf16[512,512]{1,0:T(8,128)(2,1)S(1)}, bf16[512,512]{1,0:T(8,128)(2,1)}, u32[]{:S(2)}, u32[]{:S(2)}) collective-permute-start(bf16[512,512]{1,0:T(8,128)(2,1)S(1)} %pad_maximum_fusion.1.refs_0_), channel_id=1, source_target_pairs={{0,8},{8,0},{16,24},{24,16},{32,40},{40,32},{48,56},{56,48},{64,72... | collective-permute-start | bytes 1572872 | tf_op jit(solution)/shard_map/ppermute | solution.py:41
  25.3 8.3 %collective-permute-start.8 = (bf16[512,512]{1,0:T(8,128)(2,1)S(1)}, bf16[512,512]{1,0:T(8,128)(2,1)}, u32[]{:S(2)}, u32[]{:S(2)}) collective-permute-start(bf16[512,512]{1,0:T(8,128)(2,1)S(1)} %pad_maximum_fusion.2.refs_2_), channel_id=1, source_target_pairs={{0,8},{8,0},{16,24},{24,16},{32,40},{40,32},{48,56},{56,48},{64,72... | collective-permute-start | bytes 1572872 | tf_op jit(solution)/shard_map/ppermute | solution.py:41
  27.6 6.0 %collective-permute-start.7 = (bf16[512,512]{1,0:T(8,128)(2,1)}, bf16[512,512]{1,0:T(8,128)(2,1)}, u32[]{:S(2)}, u32[]{:S(2)}) collective-permute-start(bf16[512,512]{1,0:T(8,128)(2,1)} %collective-permute-done.2.refs_1_), channel_id=1, source_target_pairs={{0,8},{8,0},{16,24},{24,16},{32,40},{40,32},{48,56},{56,48},{64,72... | collective-permute-start | bytes 1572872 | tf_op jit(solution)/shard_map/ppermute | solution.py:41
  31.0 3.8 %collective-permute-start.9 = (bf16[512,512]{1,0:T(8,128)(2,1)}, bf16[512,512]{1,0:T(8,128)(2,1)}, u32[]{:S(2)}, u32[]{:S(2)}) collective-permute-start(bf16[512,512]{1,0:T(8,128)(2,1)} %collective-permute-done.5.refs_3_), channel_id=1, source_target_pairs={{0,8},{8,0},{16,24},{24,16},{32,40},{40,32},{48,56},{56,48},{64,72... | collective-permute-start | bytes 1572872 | tf_op jit(solution)/shard_map/ppermute | solution.py:41
  33.0 1.8 %copy-start.5 = (f32[2048]{0:T(1024)S(1)}, f32[2048]{0:T(1024)}, u32[]{:S(2)}) copy-start(f32[2048]{0:T(1024)} %param.12) | copy-start | bytes 24580
  33.0 1.8 %copy-start.6 = (s32[2]{0:T(128)S(1)}, s32[2]{0:T(128)}, u32[]{:S(2)}) copy-start(s32[2]{0:T(128)} %lengths.3) | copy-start | bytes 28
  34.8 1.6 copy-start.4
  41.3 2.0 %copy-start.2 = (f32[512,2048]{1,0:T(8,128)}, f32[512,2048]{1,0:T(8,128)S(1)}, u32[]{:S(2)}) copy-start(f32[512,2048]{1,0:T(8,128)S(1)} %get-tuple-element.29.stream) | copy-start | bytes 12582916
  43.3 2.5 %collective-permute-start.15 = (bf16[2,2176]{1,0:T(2,128)(2,1)S(1)}, bf16[2,2176]{1,0:T(2,128)(2,1)S(1)}, u32[]{:S(2)}, u32[]{:S(2)}) collective-permute-start(bf16[2,2176]{1,0:T(2,128)(2,1)S(1)} %get-tuple-element.34), channel_id=1, source_target_pairs={{0,1},{8,9},{16,17},{24,25},{32,33},{40,41},{48,49},{56,57},{64,65... | collective-permute-start | bytes 26120 | tf_op jit(solution)/shard_map/ppermute | solution.py:41
  43.5 3.9 %collective-permute-start.11 = (bf16[16,2176]{1,0:T(8,128)(2,1)S(1)}, bf16[16,2176]{1,0:T(8,128)(2,1)S(1)}, u32[]{:S(2)}, u32[]{:S(2)}) collective-permute-start(bf16[16,2176]{1,0:T(8,128)(2,1)S(1)} %pad_maximum_fusion.8), channel_id=1, source_target_pairs={{0,64},{8,72},{16,80},{24,88},{32,96},{40,104},{48,112},{56,120},{... | collective-permute-start | bytes 208904 | tf_op jit(solution)/shard_map/ppermute | solution.py:41
  45.8 3.9 %collective-permute-start.16 = (bf16[4,2176]{1,0:T(4,128)(2,1)S(1)}, bf16[4,2176]{1,0:T(4,128)(2,1)S(1)}, u32[]{:S(2)}, u32[]{:S(2)}) collective-permute-start(bf16[4,2176]{1,0:T(4,128)(2,1)S(1)} %pad_maximum_fusion.11), channel_id=1, source_target_pairs={{0,3},{8,11},{16,19},{24,27},{32,35},{40,43},{48,51},{56,59},{64,6... | collective-permute-start | bytes 52232 | tf_op jit(solution)/shard_map/ppermute | solution.py:41
  47.4 4.5 %collective-permute-start.12 = (bf16[32,2176]{1,0:T(8,128)(2,1)S(1)}, bf16[32,2176]{1,0:T(8,128)(2,1)S(1)}, u32[]{:S(2)}, u32[]{:S(2)}) collective-permute-start(bf16[32,2176]{1,0:T(8,128)(2,1)S(1)} %pad_maximum_fusion.7), channel_id=1, source_target_pairs={{0,16},{8,24},{16,0},{24,8},{32,48},{40,56},{48,32},{56,40},{64,80... | collective-permute-start | bytes 417800 | tf_op jit(solution)/shard_map/ppermute | solution.py:41
  49.8 5.8 %collective-permute-start.17 = (bf16[8,2176]{1,0:T(8,128)(2,1)S(1)}, bf16[8,2176]{1,0:T(8,128)(2,1)S(1)}, u32[]{:S(2)}, u32[]{:S(2)}) collective-permute-start(bf16[8,2176]{1,0:T(8,128)(2,1)S(1)} %pad_maximum_fusion.10), channel_id=1, source_target_pairs={{0,64},{8,72},{16,80},{24,88},{32,96},{40,104},{48,112},{56,120},{... | collective-permute-start | bytes 104456 | tf_op jit(solution)/shard_map/ppermute | solution.py:41
  51.9 10.5 %collective-permute-start.13 = (bf16[64,2176]{1,0:T(8,128)(2,1)S(1)}, bf16[64,2176]{1,0:T(8,128)(2,1)}, u32[]{:S(2)}, u32[]{:S(2)}) collective-permute-start(bf16[64,2176]{1,0:T(8,128)(2,1)S(1)} %pad_maximum_fusion.3), channel_id=1, source_target_pairs={{0,48},{8,56},{16,32},{24,40},{32,16},{40,24},{48,0},{56,8},{64,11... | collective-permute-start | bytes 835592 | tf_op jit(solution)/shard_map/ppermute | solution.py:41
  55.6 4.8 %collective-permute-start.18 = (bf16[16,2176]{1,0:T(8,128)(2,1)S(1)}, bf16[16,2176]{1,0:T(8,128)(2,1)S(1)}, u32[]{:S(2)}, u32[]{:S(2)}) collective-permute-start(bf16[16,2176]{1,0:T(8,128)(2,1)S(1)} %pad_maximum_fusion.9), channel_id=1, source_target_pairs={{0,68},{8,76},{16,84},{24,92},{32,100},{40,108},{48,116},{56,124},... | collective-permute-start | bytes 208904 | tf_op jit(solution)/shard_map/ppermute | solution.py:41
  62.4 4.8 %collective-permute-start.19 = (bf16[32,2176]{1,0:T(8,128)(2,1)}, bf16[32,2176]{1,0:T(8,128)(2,1)}, u32[]{:S(2)}, u32[]{:S(2)}) collective-permute-start(bf16[32,2176]{1,0:T(8,128)(2,1)} %concatenate.78), channel_id=1, source_target_pairs={{0,16},{8,24},{16,0},{24,8},{32,48},{40,56},{48,32},{56,40},{64,80... | collective-permute-start | bytes 417800 | tf_op jit(solution)/shard_map/ppermute | solution.py:41
  63.4 16.9 %collective-permute-start.14 = (bf16[128,2176]{1,0:T(8,128)(2,1)S(1)}, bf16[128,2176]{1,0:T(8,128)(2,1)}, u32[]{:S(2)}, u32[]{:S(2)}) collective-permute-start(bf16[128,2176]{1,0:T(8,128)(2,1)S(1)} %pad_maximum_fusion.refs_0_), channel_id=1, source_target_pairs={{0,8},{8,0},{16,24},{24,16},{32,40},{40,32},{48,56},{56,48},{64,72... | collective-permute-start | bytes 1671176 | tf_op jit(solution)/shard_map/ppermute | solution.py:41
  68.2 6.7 %collective-permute-start.20 = (bf16[64,2176]{1,0:T(8,128)(2,1)S(1)}, bf16[64,2176]{1,0:T(8,128)(2,1)S(1)}, u32[]{:S(2)}, u32[]{:S(2)}) collective-permute-start(bf16[64,2176]{1,0:T(8,128)(2,1)S(1)} %concatenate.79.refs_2_), channel_id=1, source_target_pairs={{0,48},{8,56},{16,32},{24,40},{32,16},{40,24},{48,0},{56,8},{64,11... | collective-permute-start | bytes 835592 | tf_op jit(solution)/shard_map/ppermute | solution.py:41
  70.3 10.1 %collective-permute-start.21 = (bf16[64,2176]{1,0:T(8,128)(2,1)S(1)}, bf16[64,2176]{1,0:T(8,128)(2,1)S(1)}, u32[]{:S(2)}, u32[]{:S(2)}) collective-permute-start(bf16[64,2176]{1,0:T(8,128)(2,1)S(1)} %concatenate.79.refs_2_), channel_id=1, source_target_pairs={{0,8},{8,0},{16,24},{24,16},{32,40},{40,32},{48,56},{56,48},{64,72... | collective-permute-start | bytes 835592 | tf_op jit(solution)/shard_map/ppermute | solution.py:41
  74.9 6.6 %collective-permute-start.22 = (bf16[64,2176]{1,0:T(8,128)(2,1)S(1)}, bf16[64,2176]{1,0:T(8,128)(2,1)S(1)}, u32[]{:S(2)}, u32[]{:S(2)}) collective-permute-start(bf16[64,2176]{1,0:T(8,128)(2,1)S(1)} %collective-permute-done.20.refs_3_), channel_id=1, source_target_pairs={{0,8},{8,0},{16,24},{24,16},{32,40},{40,32},{48,56},{56,48},{64,72... | collective-permute-start | bytes 835592 | tf_op jit(solution)/shard_map/ppermute | solution.py:41
  86.0 4.5 %collective-permute-start.23 = (f32[8,2432]{1,0:T(8,128)S(1)}, f32[8,2432]{1,0:T(8,128)S(1)}, u32[]{:S(2)}, u32[]{:S(2)}) collective-permute-start(f32[8,2432]{1,0:T(8,128)S(1)} %get-tuple-element.36), channel_id=1, source_target_pairs={{0,3},{8,11},{16,19},{24,27},{32,35},{40,43},{48,51},{56,59},{64,6... | collective-permute-start | bytes 233480 | tf_op jit(solution)/shard_map/ppermute | solution.py:41
  90.4 3.3 %collective-permute-start.24 = (f32[8,2432]{1,0:T(8,128)S(1)}, f32[8,2432]{1,0:T(8,128)S(1)}, u32[]{:S(2)}, u32[]{:S(2)}) collective-permute-start(f32[8,2432]{1,0:T(8,128)S(1)} %add.142), channel_id=1, source_target_pairs={{0,1},{8,9},{16,17},{24,25},{32,33},{40,41},{48,49},{56,57},{64,65... | collective-permute-start | bytes 233480 | tf_op jit(solution)/shard_map/ppermute | solution.py:41
  90.5 11.1 %collective-permute-start.25 = (bf16[1024,512]{1,0:T(8,128)(2,1)S(1)}, bf16[1024,512]{1,0:T(8,128)(2,1)S(1)}, u32[]{:S(2)}, u32[]{:S(2)}) collective-permute-start(bf16[1024,512]{1,0:T(8,128)(2,1)S(1)} %bitcast.16), channel_id=1, source_target_pairs={{0,8},{8,0},{16,24},{24,16},{32,40},{40,32},{48,56},{56,48},{64,72... | collective-permute-start | bytes 3145736 | tf_op jit(solution)/shard_map/ppermute | solution.py:41
  93.8 2.2 %copy-start.3 = (f32[512,2048]{1,0:T(8,128)S(1)}, f32[512,2048]{1,0:T(8,128)}, u32[]{:S(2)}) copy-start(f32[512,2048]{1,0:T(8,128)} %copy-done.2) | copy-start | bytes 12582916
  98.9 5.0 %collective-permute-start.26 = (bf16[512,1024]{1,0:T(8,128)(2,1)S(1)}, bf16[512,1024]{1,0:T(8,128)(2,1)S(1)}, u32[]{:S(2)}, u32[]{:S(2)}) collective-permute-start(bf16[512,1024]{1,0:T(8,128)(2,1)S(1)} %get-tuple-element.40), channel_id=1, source_target_pairs={{0,8},{8,0},{16,24},{24,16},{32,40},{40,32},{48,56},{56,48},{64,72... | collective-permute-start | bytes 3145736 | tf_op jit(solution)/shard_map/ppermute | solution.py:41
  103.9 1.6 copy-start
  107.3 14.4 %collective-permute-start.27 = (bf16[512,512]{1,0:T(8,128)(2,1)S(1)}, bf16[512,512]{1,0:T(8,128)(2,1)S(1)}, u32[]{:S(2)}, u32[]{:S(2)}) collective-permute-start(bf16[512,512]{1,0:T(8,128)(2,1)S(1)} %get-tuple-element.42), channel_id=1, source_target_pairs={{0,3},{8,11},{16,19},{24,27},{32,35},{40,43},{48,51},{56,59},{64,6... | collective-permute-start | bytes 1572872 | tf_op jit(solution)/shard_map/ppermute | solution.py:41
  108.4 14.0 %collective-permute-start.30 = (bf16[512,512]{1,0:T(8,128)(2,1)S(1)}, bf16[512,512]{1,0:T(8,128)(2,1)S(1)}, u32[]{:S(2)}, u32[]{:S(2)}) collective-permute-start(bf16[512,512]{1,0:T(8,128)(2,1)S(1)} %get-tuple-element.44), channel_id=1, source_target_pairs={{0,68},{8,76},{16,84},{24,92},{32,100},{40,108},{48,116},{56,124},... | collective-permute-start | bytes 1572872 | tf_op jit(solution)/shard_map/ppermute | solution.py:41
  121.9 7.8 %collective-permute-start.28 = (bf16[256,512]{1,0:T(8,128)(2,1)S(1)}, bf16[256,512]{1,0:T(8,128)(2,1)S(1)}, u32[]{:S(2)}, u32[]{:S(2)}) collective-permute-start(bf16[256,512]{1,0:T(8,128)(2,1)S(1)} %slice.61), channel_id=1, source_target_pairs={{0,1},{8,9},{16,17},{24,25},{32,33},{40,41},{48,49},{56,57},{64,65... | collective-permute-start | bytes 786440 | tf_op jit(solution)/shard_map/ppermute | solution.py:41
  122.4 1.9 %copy-start.1 = (bf16[512,2048]{1,0:T(8,128)(2,1)S(1)}, bf16[512,2048]{1,0:T(8,128)(2,1)}, u32[]{:S(2)}) copy-start(bf16[512,2048]{1,0:T(8,128)(2,1)} %get-tuple-element.23.residual_grad) | copy-start | bytes 6291460
  122.6 10.0 %collective-permute-start.31 = (bf16[256,512]{1,0:T(8,128)(2,1)S(1)}, bf16[256,512]{1,0:T(8,128)(2,1)S(1)}, u32[]{:S(2)}, u32[]{:S(2)}) collective-permute-start(bf16[256,512]{1,0:T(8,128)(2,1)S(1)} %slice.60), channel_id=1, source_target_pairs={{0,3},{8,11},{16,19},{24,27},{32,35},{40,43},{48,51},{56,59},{64,6... | collective-permute-start | bytes 786440 | tf_op jit(solution)/shard_map/ppermute | solution.py:41
  129.9 5.1 %collective-permute-start.29 = (bf16[128,512]{1,0:T(8,128)(2,1)S(1)}, bf16[128,512]{1,0:T(8,128)(2,1)S(1)}, u32[]{:S(2)}, u32[]{:S(2)}) collective-permute-start(bf16[128,512]{1,0:T(8,128)(2,1)S(1)} %slice.63), channel_id=1, source_target_pairs={{0,68},{8,76},{16,84},{24,92},{32,100},{40,108},{48,116},{56,124},... | collective-permute-start | bytes 393224 | tf_op jit(solution)/shard_map/ppermute | solution.py:41
  132.7 4.2 %collective-permute-start.32 = (bf16[128,512]{1,0:T(8,128)(2,1)S(1)}, bf16[128,512]{1,0:T(8,128)(2,1)S(1)}, u32[]{:S(2)}, u32[]{:S(2)}) collective-permute-start(bf16[128,512]{1,0:T(8,128)(2,1)S(1)} %slice.62), channel_id=1, source_target_pairs={{0,1},{8,9},{16,17},{24,25},{32,33},{40,41},{48,49},{56,57},{64,65... | collective-permute-start | bytes 393224 | tf_op jit(solution)/shard_map/ppermute | solution.py:41
  137.0 3.9 %collective-permute-start.36 = (bf16[128,512]{1,0:T(8,128)(2,1)S(1)}, bf16[128,512]{1,0:T(8,128)(2,1)S(1)}, u32[]{:S(2)}, u32[]{:S(2)}) collective-permute-start(bf16[128,512]{1,0:T(8,128)(2,1)S(1)} %reduce-precision_convert_fusion), channel_id=1, source_target_pairs={{0,16},{8,24},{16,0},{24,8},{32,48},{40,56},{48,32},{56,40},{64,80... | collective-permute-start | bytes 393224 | tf_op jit(solution)/shard_map/ppermute | solution.py:41
  137.1 5.7 %collective-permute-start.33 = (bf16[128,512]{1,0:T(8,128)(2,1)S(1)}, bf16[128,512]{1,0:T(8,128)(2,1)S(1)}, u32[]{:S(2)}, u32[]{:S(2)}) collective-permute-start(bf16[128,512]{1,0:T(8,128)(2,1)S(1)} %reduce-precision_convert_fusion.1), channel_id=1, source_target_pairs={{0,64},{8,72},{16,80},{24,88},{32,96},{40,104},{48,112},{56,120},{... | collective-permute-start | bytes 393224 | tf_op jit(solution)/shard_map/ppermute | solution.py:41
  140.9 5.1 %collective-permute-start.37 = (bf16[128,512]{1,0:T(8,128)(2,1)S(1)}, bf16[128,512]{1,0:T(8,128)(2,1)S(1)}, u32[]{:S(2)}, u32[]{:S(2)}) collective-permute-start(bf16[128,512]{1,0:T(8,128)(2,1)S(1)} %fusion.4), channel_id=1, source_target_pairs={{0,48},{8,56},{16,32},{24,40},{32,16},{40,24},{48,0},{56,8},{64,11... | collective-permute-start | bytes 393224 | tf_op jit(solution)/shard_map/ppermute | solution.py:41
  142.9 3.9 %collective-permute-start.34 = (bf16[128,512]{1,0:T(8,128)(2,1)S(1)}, bf16[128,512]{1,0:T(8,128)(2,1)S(1)}, u32[]{:S(2)}, u32[]{:S(2)}) collective-permute-start(bf16[128,512]{1,0:T(8,128)(2,1)S(1)} %fusion.3), channel_id=1, source_target_pairs={{0,16},{8,24},{16,0},{24,8},{32,48},{40,56},{48,32},{56,40},{64,80... | collective-permute-start | bytes 393224 | tf_op jit(solution)/shard_map/ppermute | solution.py:41
  146.1 4.2 %collective-permute-start.38 = (bf16[128,512]{1,0:T(8,128)(2,1)S(1)}, bf16[128,512]{1,0:T(8,128)(2,1)S(1)}, u32[]{:S(2)}, u32[]{:S(2)}) collective-permute-start(bf16[128,512]{1,0:T(8,128)(2,1)S(1)} %fusion.1), channel_id=1, source_target_pairs={{0,64},{8,72},{16,80},{24,88},{32,96},{40,104},{48,112},{56,120},{... | collective-permute-start | bytes 393224 | tf_op jit(solution)/shard_map/ppermute | solution.py:41
  146.8 5.2 %collective-permute-start.35 = (bf16[128,512]{1,0:T(8,128)(2,1)S(1)}, bf16[128,512]{1,0:T(8,128)(2,1)S(1)}, u32[]{:S(2)}, u32[]{:S(2)}) collective-permute-start(bf16[128,512]{1,0:T(8,128)(2,1)S(1)} %fusion), channel_id=1, source_target_pairs={{0,48},{8,56},{16,32},{24,40},{32,16},{40,24},{48,0},{56,8},{64,11... | collective-permute-start | bytes 393224 | tf_op jit(solution)/shard_map/ppermute | solution.py:41
  152.1 7.6 %collective-permute-start.39 = (bf16[128,1024]{1,0:T(8,128)(2,1)S(1)}, bf16[128,1024]{1,0:T(8,128)(2,1)S(1)}, u32[]{:S(2)}, u32[]{:S(2)}) collective-permute-start(bf16[128,1024]{1,0:T(8,128)(2,1)S(1)} %pad_maximum_fusion.6), channel_id=1, source_target_pairs={{0,8},{8,0},{16,24},{24,16},{32,40},{40,32},{48,56},{56,48},{64,72... | collective-permute-start | bytes 786440 | tf_op jit(solution)/shard_map/ppermute | solution.py:41

commit v2 on v1

--- a/solution.py
+++ b/solution.py
@@ -14,7 +14,7 @@
 BF16 = jnp.bfloat16
 VMEM = pl.BlockSpec(memory_space=pltpu.VMEM)
 SMEM = pl.BlockSpec(memory_space=pltpu.SMEM)
-ANY = pl.BlockSpec(memory_space=pl.ANY)
+HBM = pl.BlockSpec(memory_space=pltpu.HBM)
 
 
 def params(mebibytes):
@@ -58,7 +58,7 @@
 
 
 def doubled(value, swap, bits):
-    return jnp.concatenate([value, swap(value, bits)], axis=0)
+    return lax.optimization_barrier(jnp.concatenate([value, swap(value, bits)], axis=0))
 
 
 def dot(left, right):
@@ -93,12 +93,14 @@
 
 def forward_kernel(where, lengths, context, residual, gain, labels, *refs):
     firsts, seconds = (refs[0:2], refs[4:6]), (refs[2:4], refs[6:8])
-    stream, inverse, pooled, embedding = refs[8:]
+    stream, inverse, pooled, embedding, added_rows, sem = refs[8:]
     tokens, width = residual.shape
     part = width // 4
     block = context.shape[1] // 8
     items = lengths.shape[0]
     length = tokens // items
+    copy = pltpu.make_async_copy(residual, added_rows, sem)
+    copy.start()
     ordered = [
         jnp.concatenate(
             [context[:, b * block : (b + 1) * block] for b in second_order(half)], axis=1
@@ -106,17 +108,18 @@
         for half in range(2)
     ]
     for side, (first_at, second_at) in enumerate(column_offsets(where[3], width)):
-        acc = residual[:, pl.ds(first_at, part)].astype(F32)
-        for half in range(2):
-            span = context[:, half * 4 * block : (half + 1) * 4 * block]
-            acc = acc + dot(span, firsts[side][half][...])
-        stream[:, pl.ds(first_at, part)] = acc
-        acc = residual[:, pl.ds(second_at, part)].astype(F32)
-        for half in range(2):
-            acc = acc + dot(ordered[half], seconds[side][half][...])
-        stream[:, pl.ds(second_at, part)] = acc
+        spans = [context[:, half * 4 * block : (half + 1) * 4 * block] for half in range(2)]
+        stream[:, pl.ds(first_at, part)] = dot(spans[0], firsts[side][0][...]) + dot(
+            spans[1], firsts[side][1][...]
+        )
+        stream[:, pl.ds(second_at, part)] = dot(ordered[0], seconds[side][0][...]) + dot(
+            ordered[1], seconds[side][1][...]
+        )
+    copy.wait()
     for i in range(items):
-        rows = stream[i * length : (i + 1) * length, :]
+        span = slice(i * length, (i + 1) * length)
+        rows = stream[span, :] + added_rows[span, :].astype(F32)
+        stream[span, :] = rows
         inv = lax.rsqrt(jnp.mean(rows * rows, axis=-1, keepdims=True) + EPSILON)
         inverse[i * length : (i + 1) * length, :] = inv
         position = lax.broadcasted_iota(jnp.int32, (length, 1), 0)
@@ -158,8 +161,8 @@
 
     def user_home(s):
         one = s // users_here
-        ay = y ^ (3 * bit(one, 0)) ^ bit(one, 1)
-        az = z ^ bit(one, 2) ^ (3 * bit(one, 3))
+        az = z ^ bit(one, 0) ^ (3 * bit(one, 1))
+        ay = y ^ bit(one, 2) ^ (3 * bit(one, 3))
         ac = core ^ bit(one, 4)
         return ((ac * 4 + az) * 4 + ay) * users_here + s % users_here
 
@@ -208,7 +211,7 @@
 
 
 def residual_kernel(people, where, lengths, stream, inverse, pooled, gain, sums, *refs):
-    residual_grad, send, gain_grad, loss = refs
+    residual_grad, keep, send, gain_grad, loss = refs
     tokens, width = stream.shape
     half = width // 2
     items = lengths.shape[0]
@@ -233,6 +236,7 @@
         kept = jnp.where(position < lengths[i], inv, 0.0)
         mean = jnp.mean(rows * row, axis=-1, keepdims=True)
         residual_grad[span, :] = (kept * row - rows * (kept * inv * inv * mean)).astype(BF16)
+    keep[...] = residual_grad[:, pl.ds(pl.multiple_of(where[3] * half, half), half)]
     send[...] = residual_grad[:, pl.ds(pl.multiple_of((1 - where[3]) * half, half), half)]
     for j in range(near):
         at = slice(j * piece, (j + 1) * piece)
@@ -240,15 +244,13 @@
     loss[...] = sums[0:1, width + piece : width + piece + 1] / people
 
 
-def context_kernel(where, residual_grad, *refs):
+def context_kernel(where, keep, send, *refs):
     firsts, seconds = (refs[0:2], refs[4:6]), (refs[2:4], refs[6:8])
     context_grad = refs[8]
-    width = residual_grad.shape[1]
-    part = width // 4
+    part = keep.shape[1] // 2
     block = context_grad.shape[1] // 8
-    offsets = column_offsets(where[3], width)
-    near = [residual_grad[:, pl.ds(first, part)] for first, _ in offsets]
-    far = [residual_grad[:, pl.ds(second, part)] for _, second in offsets]
+    near = [ref[:, :part] for ref in (keep, send)]
+    far = [ref[:, part:] for ref in (keep, send)]
     from_first = [sum(contract_last(near[s], firsts[s][h][...]) for s in range(2)) for h in range(2)]
     from_second = [sum(contract_last(far[s], seconds[s][h][...]) for s in range(2)) for h in range(2)]
     for r3 in range(2):
@@ -260,13 +262,11 @@
                 context_grad[:, pl.ds(pl.multiple_of(home * block, block), block)] = value.astype(BF16)
 
 
-def blocks_kernel(half, where, own_context, peer_context, residual_grad, peer_grad, first, second):
-    width = residual_grad.shape[1]
-    part = width // 4
+def blocks_kernel(half, own_context, peer_context, own_grad, peer_grad, first, second):
+    part = own_grad.shape[1] // 2
     block = own_context.shape[0] // 8
-    first_at, second_at = column_offsets(where[3], width)[0]
     span = slice(half * 4 * block, (half + 1) * 4 * block)
-    value = dot(own_context[span, :], residual_grad[:, pl.ds(first_at, part)])
+    value = dot(own_context[span, :], own_grad[:, :part])
     value = value + dot(peer_context[span, :], peer_grad[:, :part])
     first[...] = value.astype(first.dtype)
 
@@ -275,7 +275,7 @@
             [ref[b * block : (b + 1) * block, :] for b in second_order(half)], axis=0
         )
 
-    value = dot(ordered(own_context), residual_grad[:, pl.ds(second_at, part)])
+    value = dot(ordered(own_context), own_grad[:, part:])
     value = value + dot(ordered(peer_context), peer_grad[:, part:])
     second[...] = value.astype(second.dtype)
 
@@ -320,7 +320,6 @@
     step_one = first
     first = doubled(first, swap_x, 1)
     second = doubled(second, swap_x, 3)
-    step_two = first
     firsts = [first, swap_x(first, 3)]
     seconds = [second, swap_y(second, 3)]
     pieces = firsts + seconds
@@ -335,14 +334,13 @@
     )
 
     labels = jnp.pad(positive[:, None], ((0, 0), (0, LABELS - 1))).astype(BF16)
-    users = after(jnp.concatenate([user_vectors, labels], axis=1), step_one)
-    users = doubled(users, swap_y, 3)
-    users = doubled(users, swap_y, 1)
-    users = after(users, step_two)
+    users = jnp.concatenate([user_vectors, labels], axis=1)
     users = doubled(users, swap_z, 1)
     users = doubled(users, swap_z, 3)
+    users = doubled(users, swap_y, 1)
     labels = jnp.stack([item_ids, item_counts // 128, item_counts % 128], axis=1)
     labels = jnp.pad(labels, ((0, 0), (0, LABELS - 3))).astype(BF16)
+    users, labels = lax.optimization_barrier((users, labels))
 
     stream, inverse, pooled, emb = pl.pallas_call(
         forward_kernel,
@@ -352,15 +350,16 @@
             shaped((items_here, width)),
             shaped((items_here, width + LABELS), BF16),
         ),
-        in_specs=[SMEM, SMEM] + [VMEM] * 12,
+        in_specs=[SMEM, SMEM, VMEM, HBM] + [VMEM] * 10,
         out_specs=(VMEM,) * 4,
+        scratch_shapes=[pltpu.VMEM((tokens, width), BF16), pltpu.SemaphoreType.DMA],
         compiler_params=params(20),
         name="forward",
     )(where, lengths, turned, residual, gain, labels, *pieces)
 
-    users, turned = lax.optimization_barrier((users, turned, emb))[:2]
+    users = doubled(after(users, emb), swap_y, 3)
     user_pieces = [users, swap_core(users)]
-    own_context = turned.T
+    own_context = after(turned, emb).T
     peer_context = swap_core(own_context)
     for swap, bits in ((swap_x, 1), (swap_x, 3), (swap_y, 1), (swap_y, 3), (swap_z, 1)):
         emb = doubled(emb, swap, bits)
@@ -384,16 +383,17 @@
     sums = sums + swap_x(sums, 3)
     sums = sums + swap_x(sums, 1)
 
-    residual_grad, send, gain_grad, loss = pl.pallas_call(
+    residual_grad, keep, send, gain_grad, loss = pl.pallas_call(
         functools.partial(residual_kernel, 4 * people),
         out_shape=(
             shaped((tokens, width), BF16),
+            shaped((tokens, half), BF16),
             shaped((tokens, half), BF16),
             shaped((1, width)),
             shaped((1, 1)),
         ),
         in_specs=[SMEM, SMEM] + [VMEM] * 5,
-        out_specs=(VMEM,) * 4,
+        out_specs=(VMEM,) * 5,
         compiler_params=params(16),
         name="residual",
     )(where, lengths, stream, inverse, pooled, gain, sums)
@@ -401,19 +401,19 @@
     context_grad = pl.pallas_call(
         context_kernel,
         out_shape=shaped((tokens, head), BF16),
-        in_specs=[SMEM] + [VMEM] * 9,
+        in_specs=[SMEM] + [VMEM] * 10,
         out_specs=VMEM,
         compiler_params=params(14),
         name="context",
-    )(where, residual_grad, *pieces)
-
-    operands = (where, own_context, peer_context, residual_grad, peer_grad)
+    )(where, keep, send, *pieces)
+
+    operands = (own_context, peer_context, keep, peer_grad)
 
     def blocks(which, dtype, name):
         return pl.pallas_call(
             functools.partial(blocks_kernel, which),
             out_shape=(shaped((4 * rows, part), dtype),) * 2,
-            in_specs=[SMEM] + [VMEM] * 4,
+            in_specs=[VMEM] * 4,
             out_specs=(VMEM,) * 2,
             compiler_params=params(14),
             name=name,
@@ -421,13 +421,13 @@
 
     first_sent, second_sent = blocks(1, BF16, "blocks_sent")
     first, second = blocks(0, F32, "blocks_kept")
+    first, second, context_grad = lax.optimization_barrier((first, second, context_grad))
     first = added(first, first_sent, swap_x, 3)
     second = added(second, second_sent, swap_y, 3)
     first = folded(first, swap_x, 1)
     second = folded(second, swap_x, 3)
     first = folded(first, swap_y, 3)
     second = folded(second, swap_x, 1)
-    first, second, context_grad = lax.optimization_barrier((first, second, context_grad))
     first = all_added(first, swap_y, 1)
     second = all_added(second, swap_z, 1)
     first = all_added(first, swap_z, 1)

time: 161 us -> 154 us (0.957)
  local copies, waits for them, and re-layouts: 14 us -> 4.33 us
  waiting for transfers between devices: 47 us -> 53.8 us
  starting transfers between devices: 71.8 us -> 65.1 us
  other arithmetic: 5.37 us -> 8.55 us
    ppermute x40, waiting for transfers between devices: 47 us -> 53.8 us  [move(): return lax.ppermute(value, AXES, perm)]
    ppermute x40, starting transfers between devices: 71.8 us -> 65.1 us  [move(): return lax.ppermute(value, AXES, perm)]
    unnamed x23 -> x15, local copies, waits for them, and re-layouts: 7.48 us -> 1.72 us
    concatenate x2 -> x0, local copies, waits for them, and re-layouts: 2.94 us -> none  [doubled(): return jnp.concatenate([value, swap(value, bits)], axis=0)]
    concatenate x12 -> x14, other arithmetic: 2.02 us -> 4.39 us  [the longest x13 3.63 us: doubled(): jnp.concatenate([value, swap(value, bits)], axis=0)]
  transfers between devices with their start and end apart: 40 -> 40, of which waited for: 24 -> 28; matrix products, arithmetic and copies ran while one was open for 6% -> 6% of each run, Pallas kernels for 9% -> 6%
where the time goes in v2:
time: 154 us; the launch traced here: 153 us
  starting transfers between devices  65.1 us (42%)
  waiting for transfers between devices  53.8 us (35%)
  Pallas kernels  20.5 us (13%)
  other arithmetic  8.55 us (6%)
  local copies, waits for them, and re-layouts  4.33 us (3%)
    ppermute x40, starting transfers between devices, move(): return lax.ppermute(value, AXES, perm)  65.1 us
    ppermute x40, waiting for transfers between devices, move(): return lax.ppermute(value, AXES, perm)  53.8 us
    pallas_call x1, Pallas kernels, on_device(): pl.pallas_call(forward_kernel, out_shape=(shaped((tokens, width)), shaped...  5.64 us
    pallas_call x1, Pallas kernels, on_device(): pl.pallas_call(context_kernel, out_shape=shaped((tokens, head), BF16), in...  5.4 us
    pallas_call x1, Pallas kernels, on_device(): pl.pallas_call(functools.partial(loss_kernel, users_here, items_here), ou...  3.91 us
    concatenate x13, other arithmetic, doubled(): jnp.concatenate([value, swap(value, bits)], axis=0)  3.63 us
  transfers between devices with their start and end apart: 40, of which 28 were waited for; matrix products, arithmetic and copies ran while one was open for 6% of the time, Pallas kernels for 6%

profile of v2, /device:TPU:1, one launch (start us, length us, event | category | flops | bytes accessed | tf_op | source)
XLA Modules:
  0.0 153.3 jit_solution(5740043817653201235)
XLA Ops:
  1.5 0.8 pad_maximum_fusion.12
  2.3 2.5 %collective-permute-start.1 = (bf16[8,2176]{1,0:T(8,128)(2,1)S(1)}, bf16[8,2176]{1,0:T(8,128)(2,1)S(1)}, u32[]{:S(2)}, u32[]{:S(2)}) collective-permute-start(bf16[8,2176]{1,0:T(8,128)(2,1)S(1)} %pad_maximum_fusion.12), channel_id=1, source_target_pairs={{0,16},{8,24},{16,0},{24,8},{32,48},{40,56},{48,32},{56,40},{64,80... | collective-permute-start | bytes 104456 | tf_op jit(solution)/shard_map/ppermute | solution.py:41
  4.7 1.0 constant_dynamic-slice_fusion.1
  5.7 1.3 collective-permute-start.6
  7.0 2.7 %collective-permute-start = (bf16[128,512]{1,0:T(8,128)(2,1)S(1)}, bf16[128,512]{1,0:T(8,128)(2,1)S(1)}, u32[]{:S(2)}, u32[]{:S(2)}) collective-permute-start(bf16[128,512]{1,0:T(8,128)(2,1)S(1)} %get-tuple-element.53), channel_id=1, source_target_pairs={{0,68},{8,76},{16,84},{24,92},{32,100},{40,108},{48,116},{56,124},... | collective-permute-start | bytes 393224 | tf_op jit(solution)/shard_map/ppermute | solution.py:41
  11.5 0.8 pad_maximum_fusion.10
  12.3 2.2 %collective-permute-start.2 = (bf16[16,2176]{1,0:T(8,128)(2,1)S(1)}, bf16[16,2176]{1,0:T(8,128)(2,1)S(1)}, u32[]{:S(2)}, u32[]{:S(2)}) collective-permute-start(bf16[16,2176]{1,0:T(8,128)(2,1)S(1)} %pad_maximum_fusion.10), channel_id=1, source_target_pairs={{0,48},{8,56},{16,32},{24,40},{32,16},{40,24},{48,0},{56,8},{64,11... | collective-permute-start | bytes 208904 | tf_op jit(solution)/shard_map/ppermute | solution.py:41
  15.0 2.5 %collective-permute-start.7 = (bf16[256,512]{1,0:T(8,128)(2,1)S(1)}, bf16[256,512]{1,0:T(8,128)(2,1)}, u32[]{:S(2)}, u32[]{:S(2)}) collective-permute-start(bf16[256,512]{1,0:T(8,128)(2,1)S(1)} %pad_maximum_fusion.6), channel_id=1, source_target_pairs={{0,3},{8,11},{16,19},{24,27},{32,35},{40,43},{48,51},{56,59},{64,6... | collective-permute-start | bytes 786440 | tf_op jit(solution)/shard_map/ppermute | solution.py:41
  18.7 2.0 %collective-permute-done.4 = bf16[256,512]{1,0:T(8,128)(2,1)S(1)} collective-permute-done((bf16[256,512]{1,0:T(8,128)(2,1)S(1)}, bf16[256,512]{1,0:T(8,128)(2,1)S(1)}, u32[]{:S(2)}, u32[]{:S(2)}) %collective-permute-start.4) | collective-permute-done | bytes 262176 | tf_op jit(solution)/shard_map/ppermute | solution.py:41
  20.7 1.3 collective-permute-done.7
  22.0 1.0 pad_maximum_fusion.2.refs_2_
  23.1 2.6 %collective-permute-start.5 = (bf16[512,512]{1,0:T(8,128)(2,1)S(1)}, bf16[512,512]{1,0:T(8,128)(2,1)}, u32[]{:S(2)}, u32[]{:S(2)}) collective-permute-start(bf16[512,512]{1,0:T(8,128)(2,1)S(1)} %pad_maximum_fusion.1.refs_0_), channel_id=1, source_target_pairs={{0,3},{8,11},{16,19},{24,27},{32,35},{40,43},{48,51},{56,59},{64,6... | collective-permute-start | bytes 1572872 | tf_op jit(solution)/shard_map/ppermute | solution.py:41
  25.8 4.0 %collective-permute-start.11 = (bf16[512,512]{1,0:T(8,128)(2,1)S(1)}, bf16[512,512]{1,0:T(8,128)(2,1)}, u32[]{:S(2)}, u32[]{:S(2)}) collective-permute-start(bf16[512,512]{1,0:T(8,128)(2,1)S(1)} %pad_maximum_fusion.2.refs_2_), channel_id=1, source_target_pairs={{0,8},{8,0},{16,24},{24,16},{32,40},{40,32},{48,56},{56,48},{64,72... | collective-permute-start | bytes 1572872 | tf_op jit(solution)/shard_map/ppermute | solution.py:41
  29.9 4.9 %collective-permute-done.8.refs_3_ = bf16[512,512]{1,0:T(8,128)(2,1)} collective-permute-done((bf16[512,512]{1,0:T(8,128)(2,1)S(1)}, bf16[512,512]{1,0:T(8,128)(2,1)}, u32[]{:S(2)}, u32[]{:S(2)}) %collective-permute-start.8) | collective-permute-done | bytes 524320 | tf_op jit(solution)/shard_map/ppermute | solution.py:41
  34.8 3.9 %collective-permute-start.12 = (bf16[512,512]{1,0:T(8,128)(2,1)}, bf16[512,512]{1,0:T(8,128)(2,1)}, u32[]{:S(2)}, u32[]{:S(2)}) collective-permute-start(bf16[512,512]{1,0:T(8,128)(2,1)} %collective-permute-done.8.refs_3_), channel_id=1, source_target_pairs={{0,8},{8,0},{16,24},{24,16},{32,40},{40,32},{48,56},{56,48},{64,72... | collective-permute-start | bytes 1572872 | tf_op jit(solution)/shard_map/ppermute | solution.py:41
  39.4 1.0 pad_maximum_fusion.3
  40.6 0.7 collective-permute-done.10.refs_5_
  41.4 1.6 %copy-done = bf16[512,2048]{1,0:T(8,128)(2,1)S(1)} copy-done((bf16[512,2048]{1,0:T(8,128)(2,1)S(1)}, bf16[512,2048]{1,0:T(8,128)(2,1)}, u32[]{:S(2)}) %copy-start) | copy-done | bytes 2097176
  42.9 5.6 %forward.1 = (f32[512,2048]{1,0:T(8,128)S(1)}, f32[512,1]{1,0:T(8,128)S(1)}, f32[2,2048]{1,0:T(2,128)S(1)}, bf16[2,2176]{1,0:T(2,128)(2,1)S(1)}) custom-call(s32[4]{0:T(128)S(1)} %pad_add_fusion.where, s32[2]{0:T(128)S(1)} %copy-done.2, bf16[512,1024]{1,0:T(8,128)(2,1)S(1)} %copy.27.context, bf16[512,2048]{1,0:T(8,128)(2,1)S(1)} %copy-done, ...), custom_call_target="tpu_custom_call" | custom-call | tf_op jit(solution)/shard_map/forward/pallas_call | solution.py:345
  48.7 2.5 %collective-permute-done.15 = bf16[2,2176]{1,0:T(2,128)(2,1)S(1)} collective-permute-done((bf16[2,2176]{1,0:T(2,128)(2,1)S(1)}, bf16[2,2176]{1,0:T(2,128)(2,1)S(1)}, u32[]{:S(2)}, u32[]{:S(2)}) %collective-permute-start.15) | collective-permute-done | bytes 8736 | tf_op jit(solution)/shard_map/ppermute | solution.py:41
  51.2 2.6 %collective-permute-start.16 = (bf16[4,2176]{1,0:T(4,128)(2,1)S(1)}, bf16[4,2176]{1,0:T(4,128)(2,1)S(1)}, u32[]{:S(2)}, u32[]{:S(2)}) collective-permute-start(bf16[4,2176]{1,0:T(4,128)(2,1)S(1)} %pad_maximum_fusion.14), channel_id=1, source_target_pairs={{0,3},{8,11},{16,19},{24,27},{32,35},{40,43},{48,51},{56,59},{64,6... | collective-permute-start | bytes 52232 | tf_op jit(solution)/shard_map/ppermute | solution.py:41
  53.8 1.3 collective-permute-done.16
  55.2 2.8 %collective-permute-done.17 = bf16[8,2176]{1,0:T(8,128)(2,1)S(1)} collective-permute-done((bf16[8,2176]{1,0:T(8,128)(2,1)S(1)}, bf16[8,2176]{1,0:T(8,128)(2,1)S(1)}, u32[]{:S(2)}, u32[]{:S(2)}) %collective-permute-start.17) | collective-permute-done | bytes 34848 | tf_op jit(solution)/shard_map/ppermute | solution.py:41
  58.0 1.9 %collective-permute-start.18 = (bf16[16,2176]{1,0:T(8,128)(2,1)S(1)}, bf16[16,2176]{1,0:T(8,128)(2,1)S(1)}, u32[]{:S(2)}, u32[]{:S(2)}) collective-permute-start(bf16[16,2176]{1,0:T(8,128)(2,1)S(1)} %pad_maximum_fusion.11), channel_id=1, source_target_pairs={{0,68},{8,76},{16,84},{24,92},{32,100},{40,108},{48,116},{56,124},... | collective-permute-start | bytes 208904 | tf_op jit(solution)/shard_map/ppermute | solution.py:41
  59.9 2.4 %collective-permute-done.18 = bf16[16,2176]{1,0:T(8,128)(2,1)S(1)} collective-permute-done((bf16[16,2176]{1,0:T(8,128)(2,1)S(1)}, bf16[16,2176]{1,0:T(8,128)(2,1)S(1)}, u32[]{:S(2)}, u32[]{:S(2)}) %collective-permute-start.18) | collective-permute-done | bytes 69664 | tf_op jit(solution)/shard_map/ppermute | solution.py:41
  62.4 0.8 collective-permute-start.19
  63.2 1.9 %collective-permute-start.13 = (bf16[64,2176]{1,0:T(8,128)(2,1)S(1)}, bf16[64,2176]{1,0:T(8,128)(2,1)S(1)}, u32[]{:S(2)}, u32[]{:S(2)}) collective-permute-start(bf16[64,2176]{1,0:T(8,128)(2,1)S(1)} %pad_maximum_fusion.3), channel_id=1, source_target_pairs={{0,68},{8,76},{16,84},{24,92},{32,100},{40,108},{48,116},{56,124},... | collective-permute-start | bytes 835592 | tf_op jit(solution)/shard_map/ppermute | solution.py:41
  65.1 1.5 %collective-permute-done.19 = bf16[32,2176]{1,0:T(8,128)(2,1)S(1)} collective-permute-done((bf16[32,2176]{1,0:T(8,128)(2,1)S(1)}, bf16[32,2176]{1,0:T(8,128)(2,1)S(1)}, u32[]{:S(2)}, u32[]{:S(2)}) %collective-permute-start.19) | collective-permute-done | bytes 139296 | tf_op jit(solution)/shard_map/ppermute | solution.py:41
  66.7 1.2 collective-permute-start.20
  67.9 1.9 %collective-permute-done.13 = bf16[64,2176]{1,0:T(8,128)(2,1)S(1)} collective-permute-done((bf16[64,2176]{1,0:T(8,128)(2,1)S(1)}, bf16[64,2176]{1,0:T(8,128)(2,1)S(1)}, u32[]{:S(2)}, u32[]{:S(2)}) %collective-permute-start.13) | collective-permute-done | bytes 278560 | tf_op jit(solution)/shard_map/ppermute | solution.py:41
  69.9 6.5 %collective-permute-start.14 = (bf16[128,2176]{1,0:T(8,128)(2,1)S(1)}, bf16[128,2176]{1,0:T(8,128)(2,1)S(1)}, u32[]{:S(2)}, u32[]{:S(2)}) collective-permute-start(bf16[128,2176]{1,0:T(8,128)(2,1)S(1)} %pad_maximum_fusion.refs_0_), channel_id=1, source_target_pairs={{0,8},{8,0},{16,24},{24,16},{32,40},{40,32},{48,56},{56,48},{64,72... | collective-permute-start | bytes 1671176 | tf_op jit(solution)/shard_map/ppermute | solution.py:41
  76.4 3.9 %collective-permute-start.22 = (bf16[64,2176]{1,0:T(8,128)(2,1)S(1)}, bf16[64,2176]{1,0:T(8,128)(2,1)S(1)}, u32[]{:S(2)}, u32[]{:S(2)}) collective-permute-start(bf16[64,2176]{1,0:T(8,128)(2,1)S(1)} %collective-permute-done.20.refs_3_), channel_id=1, source_target_pairs={{0,8},{8,0},{16,24},{24,16},{32,40},{40,32},{48,56},{56,48},{64,72... | collective-permute-start | bytes 835592 | tf_op jit(solution)/shard_map/ppermute | solution.py:41
  80.4 1.2 collective-permute-done.22.refs_5_
  81.5 3.9 %loss.1 = (f32[8,2432]{1,0:T(8,128)S(1)}, bf16[8,2048]{1,0:T(8,128)(2,1)}) custom-call(s32[4]{0:T(128)S(1)} %pad_add_fusion.where, f32[1,2048]{1,0:T(1,128)S(1)} %bitcast.20, bf16[128,2176]{1,0:T(8,128)(2,1)S(1)} %pad_maximum_fusion.refs_0_, bf16[128,2176]{1,0:T(8,128)(2,1)S(1)} %collective-permute-done.14.refs_1_, ...), custom_call_target="tpu_custom_call" | custom-call | tf_op jit(solution)/shard_map/loss/pallas_call | solution.py:371
  85.5 2.5 %collective-permute-start.23 = (f32[8,2432]{1,0:T(8,128)S(1)}, f32[8,2432]{1,0:T(8,128)S(1)}, u32[]{:S(2)}, u32[]{:S(2)}) collective-permute-start(f32[8,2432]{1,0:T(8,128)S(1)} %get-tuple-element.37), channel_id=1, source_target_pairs={{0,3},{8,11},{16,19},{24,27},{32,35},{40,43},{48,51},{56,59},{64,6... | collective-permute-start | bytes 233480 | tf_op jit(solution)/shard_map/ppermute | solution.py:41
  87.9 2.0 %collective-permute-done.23 = f32[8,2432]{1,0:T(8,128)S(1)} collective-permute-done((f32[8,2432]{1,0:T(8,128)S(1)}, f32[8,2432]{1,0:T(8,128)S(1)}, u32[]{:S(2)}, u32[]{:S(2)}) %collective-permute-start.23) | collective-permute-done | bytes 77856 | tf_op jit(solution)/shard_map/ppermute | solution.py:41
  90.0 1.6 %collective-permute-start.25 = (bf16[1024,512]{1,0:T(8,128)(2,1)S(1)}, bf16[1024,512]{1,0:T(8,128)(2,1)S(1)}, u32[]{:S(2)}, u32[]{:S(2)}) collective-permute-start(bf16[1024,512]{1,0:T(8,128)(2,1)S(1)} %bitcast.16), channel_id=1, source_target_pairs={{0,8},{8,0},{16,24},{24,16},{32,40},{40,32},{48,56},{56,48},{64,72... | collective-permute-start | bytes 3145736 | tf_op jit(solution)/shard_map/ppermute | solution.py:41
  91.6 1.6 %collective-permute-done.24 = f32[8,2432]{1,0:T(8,128)S(1)} collective-permute-done((f32[8,2432]{1,0:T(8,128)S(1)}, f32[8,2432]{1,0:T(8,128)S(1)}, u32[]{:S(2)}, u32[]{:S(2)}) %collective-permute-start.24) | collective-permute-done | bytes 77856 | tf_op jit(solution)/shard_map/ppermute | solution.py:41
  93.3 3.1 %residual.3 = (bf16[512,2048]{1,0:T(8,128)(2,1)}, bf16[512,1024]{1,0:T(8,128)(2,1)S(1)}, bf16[512,1024]{1,0:T(8,128)(2,1)S(1)}, f32[1,2048]{1,0:T(1,128)}, f32[1,1]{1,0:T(1,128)}) custom-call(s32[4]{0:T(128)S(1)} %pad_add_fusion.where, s32[2]{0:T(128)S(1)} %copy-done.2, f32[512,2048]{1,0:T(8,128)S(1)} %get-tuple-element.31.stream, ...), custom_call_target="tpu_custom_call" | custom-call | tf_op jit(solution)/shard_map/residual/pallas_call | solution.py:386
  96.3 2.7 %collective-permute-start.26 = (bf16[512,1024]{1,0:T(8,128)(2,1)S(1)}, bf16[512,1024]{1,0:T(8,128)(2,1)S(1)}, u32[]{:S(2)}, u32[]{:S(2)}) collective-permute-start(bf16[512,1024]{1,0:T(8,128)(2,1)S(1)} %get-tuple-element.42.send), channel_id=1, source_target_pairs={{0,8},{8,0},{16,24},{24,16},{32,40},{40,32},{48,56},{56,48},{64,72... | collective-permute-start | bytes 3145736 | tf_op jit(solution)/shard_map/ppermute | solution.py:41
  99.0 2.3 %collective-permute-done.26.peer_grad = bf16[512,1024]{1,0:T(8,128)(2,1)S(1)} collective-permute-done((bf16[512,1024]{1,0:T(8,128)(2,1)S(1)}, bf16[512,1024]{1,0:T(8,128)(2,1)S(1)}, u32[]{:S(2)}, u32[]{:S(2)}) %collective-permute-start.26) | collective-permute-done | bytes 1048608 | tf_op jit(solution)/shard_map/ppermute | solution.py:41
  101.3 1.3 blocks_sent.1
  102.6 2.6 %collective-permute-start.27 = (bf16[512,512]{1,0:T(8,128)(2,1)S(1)}, bf16[512,512]{1,0:T(8,128)(2,1)S(1)}, u32[]{:S(2)}, u32[]{:S(2)}) collective-permute-start(bf16[512,512]{1,0:T(8,128)(2,1)S(1)} %get-tuple-element.47), channel_id=1, source_target_pairs={{0,3},{8,11},{16,19},{24,27},{32,35},{40,43},{48,51},{56,59},{64,6... | collective-permute-start | bytes 1572872 | tf_op jit(solution)/shard_map/ppermute | solution.py:41
  105.1 1.9 %collective-permute-start.33 = (bf16[512,512]{1,0:T(8,128)(2,1)S(1)}, bf16[512,512]{1,0:T(8,128)(2,1)S(1)}, u32[]{:S(2)}, u32[]{:S(2)}) collective-permute-start(bf16[512,512]{1,0:T(8,128)(2,1)S(1)} %get-tuple-element.49), channel_id=1, source_target_pairs={{0,68},{8,76},{16,84},{24,92},{32,100},{40,108},{48,116},{56,124},... | collective-permute-start | bytes 1572872 | tf_op jit(solution)/shard_map/ppermute | solution.py:41
  107.0 5.4 %context.1 = bf16[512,1024]{1,0:T(8,128)(2,1)} custom-call(s32[4]{0:T(128)S(1)} %pad_add_fusion.where, bf16[512,1024]{1,0:T(8,128)(2,1)S(1)} %get-tuple-element.41.own_grad.keep, bf16[512,1024]{1,0:T(8,128)(2,1)S(1)} %get-tuple-element.42.send, bf16[512,512]{1,0:T(8,128)(2,1)S(1)} %pad_maximum_fusion.1.refs_0_, ...), custom_call_target="tpu_custom_call" | custom-call | tf_op jit(solution)/shard_map/context/pallas_call | solution.py:401
  112.4 1.3 blocks_kept.1
  113.7 3.3 %collective-permute-done.27 = bf16[512,512]{1,0:T(8,128)(2,1)S(1)} collective-permute-done((bf16[512,512]{1,0:T(8,128)(2,1)S(1)}, bf16[512,512]{1,0:T(8,128)(2,1)S(1)}, u32[]{:S(2)}, u32[]{:S(2)}) %collective-permute-start.27) | collective-permute-done | bytes 524320 | tf_op jit(solution)/shard_map/ppermute | solution.py:41
  117.3 1.9 %collective-permute-done.33 = bf16[512,512]{1,0:T(8,128)(2,1)S(1)} collective-permute-done((bf16[512,512]{1,0:T(8,128)(2,1)S(1)}, bf16[512,512]{1,0:T(8,128)(2,1)S(1)}, u32[]{:S(2)}, u32[]{:S(2)}) %collective-permute-start.33) | collective-permute-done | bytes 524320 | tf_op jit(solution)/shard_map/ppermute | solution.py:41
  120.1 3.8 %collective-permute-done.28 = bf16[256,512]{1,0:T(8,128)(2,1)S(1)} collective-permute-done((bf16[256,512]{1,0:T(8,128)(2,1)S(1)}, bf16[256,512]{1,0:T(8,128)(2,1)S(1)}, u32[]{:S(2)}, u32[]{:S(2)}) %collective-permute-start.28) | collective-permute-done | bytes 262176 | tf_op jit(solution)/shard_map/ppermute | solution.py:41
  124.0 2.0 %collective-permute-start.29 = (bf16[128,512]{1,0:T(8,128)(2,1)S(1)}, bf16[128,512]{1,0:T(8,128)(2,1)S(1)}, u32[]{:S(2)}, u32[]{:S(2)}) collective-permute-start(bf16[128,512]{1,0:T(8,128)(2,1)S(1)} %slice.83), channel_id=1, source_target_pairs={{0,68},{8,76},{16,84},{24,92},{32,100},{40,108},{48,116},{56,124},... | collective-permute-start | bytes 393224 | tf_op jit(solution)/shard_map/ppermute | solution.py:41
  126.0 0.9 collective-permute-done.34
  127.1 2.0 %collective-permute-done.29 = bf16[128,512]{1,0:T(8,128)(2,1)S(1)} collective-permute-done((bf16[128,512]{1,0:T(8,128)(2,1)S(1)}, bf16[128,512]{1,0:T(8,128)(2,1)S(1)}, u32[]{:S(2)}, u32[]{:S(2)}) %collective-permute-start.29) | collective-permute-done | bytes 131104 | tf_op jit(solution)/shard_map/ppermute | solution.py:41
  129.2 2.0 %collective-permute-done.35 = bf16[128,512]{1,0:T(8,128)(2,1)S(1)} collective-permute-done((bf16[128,512]{1,0:T(8,128)(2,1)S(1)}, bf16[128,512]{1,0:T(8,128)(2,1)S(1)}, u32[]{:S(2)}, u32[]{:S(2)}) %collective-permute-start.35) | collective-permute-done | bytes 131104 | tf_op jit(solution)/shard_map/ppermute | solution.py:41
  131.3 2.0 %collective-permute-done.30 = bf16[128,512]{1,0:T(8,128)(2,1)S(1)} collective-permute-done((bf16[128,512]{1,0:T(8,128)(2,1)S(1)}, bf16[128,512]{1,0:T(8,128)(2,1)S(1)}, u32[]{:S(2)}, u32[]{:S(2)}) %collective-permute-start.30) | collective-permute-done | bytes 131104 | tf_op jit(solution)/shard_map/ppermute | solution.py:41
  133.5 1.7 %collective-permute-done.36 = bf16[128,512]{1,0:T(8,128)(2,1)S(1)} collective-permute-done((bf16[128,512]{1,0:T(8,128)(2,1)S(1)}, bf16[128,512]{1,0:T(8,128)(2,1)S(1)}, u32[]{:S(2)}, u32[]{:S(2)}) %collective-permute-start.36) | collective-permute-done | bytes 131104 | tf_op jit(solution)/shard_map/ppermute | solution.py:41
  135.2 1.3 collective-permute-start.37
  136.5 0.8 collective-permute-done.31
  137.3 1.3 collective-permute-start.32
  138.6 1.7 %collective-permute-done.37 = bf16[128,512]{1,0:T(8,128)(2,1)S(1)} collective-permute-done((bf16[128,512]{1,0:T(8,128)(2,1)S(1)}, bf16[128,512]{1,0:T(8,128)(2,1)S(1)}, u32[]{:S(2)}, u32[]{:S(2)}) %collective-permute-start.37) | collective-permute-done | bytes 131104 | tf_op jit(solution)/shard_map/ppermute | solution.py:41
  140.5 2.0 %collective-permute-done.32 = bf16[128,512]{1,0:T(8,128)(2,1)S(1)} collective-permute-done((bf16[128,512]{1,0:T(8,128)(2,1)S(1)}, bf16[128,512]{1,0:T(8,128)(2,1)S(1)}, u32[]{:S(2)}, u32[]{:S(2)}) %collective-permute-start.32) | collective-permute-done | bytes 131104 | tf_op jit(solution)/shard_map/ppermute | solution.py:41
  142.6 2.0 %collective-permute-done.38 = bf16[128,512]{1,0:T(8,128)(2,1)S(1)} collective-permute-done((bf16[128,512]{1,0:T(8,128)(2,1)S(1)}, bf16[128,512]{1,0:T(8,128)(2,1)S(1)}, u32[]{:S(2)}, u32[]{:S(2)}) %collective-permute-start.38) | collective-permute-done | bytes 131104 | tf_op jit(solution)/shard_map/ppermute | solution.py:41
  144.7 6.5 %collective-permute-start.39 = (bf16[128,1024]{1,0:T(8,128)(2,1)S(1)}, bf16[128,1024]{1,0:T(8,128)(2,1)S(1)}, u32[]{:S(2)}, u32[]{:S(2)}) collective-permute-start(bf16[128,1024]{1,0:T(8,128)(2,1)S(1)} %pad_maximum_fusion.7), channel_id=1, source_target_pairs={{0,8},{8,0},{16,24},{24,16},{32,40},{40,32},{48,56},{56,48},{64,72... | collective-permute-start | bytes 786440 | tf_op jit(solution)/shard_map/ppermute | solution.py:41
  151.2 1.2 collective-permute-done.39
  152.4 0.9 maximum_select_fusion
  (85 shorter events, 8.3 us)
Async XLA Ops:
  0.6 17.5 %copy-start.3 = (bf16[512,1024]{1,0:T(8,128)(2,1)S(1)}, bf16[512,1024]{1,0:T(8,128)(2,1)}, u32[]{:S(2)}) copy-start(bf16[512,1024]{1,0:T(8,128)(2,1)} %param.9) | copy-start | bytes 3145732
  2.3 9.3 %collective-permute-start.1 = (bf16[8,2176]{1,0:T(8,128)(2,1)S(1)}, bf16[8,2176]{1,0:T(8,128)(2,1)S(1)}, u32[]{:S(2)}, u32[]{:S(2)}) collective-permute-start(bf16[8,2176]{1,0:T(8,128)(2,1)S(1)} %pad_maximum_fusion.12), channel_id=1, source_target_pairs={{0,16},{8,24},{16,0},{24,8},{32,48},{40,56},{48,32},{56,40},{64,80... | collective-permute-start | bytes 104456 | tf_op jit(solution)/shard_map/ppermute | solution.py:41
  5.7 8.9 %collective-permute-start.6 = (bf16[128,512]{1,0:T(8,128)(2,1)S(1)}, bf16[128,512]{1,0:T(8,128)(2,1)S(1)}, u32[]{:S(2)}, u32[]{:S(2)}) collective-permute-start(bf16[128,512]{1,0:T(8,128)(2,1)S(1)} %get-tuple-element.52), channel_id=1, source_target_pairs={{0,1},{8,9},{16,17},{24,25},{32,33},{40,41},{48,49},{56,57},{64,65... | collective-permute-start | bytes 393224 | tf_op jit(solution)/shard_map/ppermute | solution.py:41
  7.0 7.6 %collective-permute-start = (bf16[128,512]{1,0:T(8,128)(2,1)S(1)}, bf16[128,512]{1,0:T(8,128)(2,1)S(1)}, u32[]{:S(2)}, u32[]{:S(2)}) collective-permute-start(bf16[128,512]{1,0:T(8,128)(2,1)S(1)} %get-tuple-element.53), channel_id=1, source_target_pairs={{0,68},{8,76},{16,84},{24,92},{32,100},{40,108},{48,116},{56,124},... | collective-permute-start | bytes 393224 | tf_op jit(solution)/shard_map/ppermute | solution.py:41
  12.3 5.1 %collective-permute-start.2 = (bf16[16,2176]{1,0:T(8,128)(2,1)S(1)}, bf16[16,2176]{1,0:T(8,128)(2,1)S(1)}, u32[]{:S(2)}, u32[]{:S(2)}) collective-permute-start(bf16[16,2176]{1,0:T(8,128)(2,1)S(1)} %pad_maximum_fusion.10), channel_id=1, source_target_pairs={{0,48},{8,56},{16,32},{24,40},{32,16},{40,24},{48,0},{56,8},{64,11... | collective-permute-start | bytes 208904 | tf_op jit(solution)/shard_map/ppermute | solution.py:41
  14.6 6.1 %collective-permute-start.4 = (bf16[256,512]{1,0:T(8,128)(2,1)S(1)}, bf16[256,512]{1,0:T(8,128)(2,1)S(1)}, u32[]{:S(2)}, u32[]{:S(2)}) collective-permute-start(bf16[256,512]{1,0:T(8,128)(2,1)S(1)} %pad_maximum_fusion.5), channel_id=1, source_target_pairs={{0,1},{8,9},{16,17},{24,25},{32,33},{40,41},{48,49},{56,57},{64,65... | collective-permute-start | bytes 786440 | tf_op jit(solution)/shard_map/ppermute | solution.py:41
  15.0 7.0 %collective-permute-start.7 = (bf16[256,512]{1,0:T(8,128)(2,1)S(1)}, bf16[256,512]{1,0:T(8,128)(2,1)}, u32[]{:S(2)}, u32[]{:S(2)}) collective-permute-start(bf16[256,512]{1,0:T(8,128)(2,1)S(1)} %pad_maximum_fusion.6), channel_id=1, source_target_pairs={{0,3},{8,11},{16,19},{24,27},{32,35},{40,43},{48,51},{56,59},{64,6... | collective-permute-start | bytes 786440 | tf_op jit(solution)/shard_map/ppermute | solution.py:41
  18.1 21.3 %collective-permute-start.3 = (bf16[32,2176]{1,0:T(8,128)(2,1)}, bf16[32,2176]{1,0:T(8,128)(2,1)}, u32[]{:S(2)}, u32[]{:S(2)}) collective-permute-start(bf16[32,2176]{1,0:T(8,128)(2,1)} %pad_maximum_fusion.8), channel_id=1, source_target_pairs={{0,64},{8,72},{16,80},{24,88},{32,96},{40,104},{48,112},{56,120},{... | collective-permute-start | bytes 417800 | tf_op jit(solution)/shard_map/ppermute | solution.py:41
  23.0 11.8 %collective-permute-start.8 = (bf16[512,512]{1,0:T(8,128)(2,1)S(1)}, bf16[512,512]{1,0:T(8,128)(2,1)}, u32[]{:S(2)}, u32[]{:S(2)}) collective-permute-start(bf16[512,512]{1,0:T(8,128)(2,1)S(1)} %pad_maximum_fusion.2.refs_2_), channel_id=1, source_target_pairs={{0,68},{8,76},{16,84},{24,92},{32,100},{40,108},{48,116},{56,124},... | collective-permute-start | bytes 1572872 | tf_op jit(solution)/shard_map/ppermute | solution.py:41
  23.1 15.6 %collective-permute-start.5 = (bf16[512,512]{1,0:T(8,128)(2,1)S(1)}, bf16[512,512]{1,0:T(8,128)(2,1)}, u32[]{:S(2)}, u32[]{:S(2)}) collective-permute-start(bf16[512,512]{1,0:T(8,128)(2,1)S(1)} %pad_maximum_fusion.1.refs_0_), channel_id=1, source_target_pairs={{0,3},{8,11},{16,19},{24,27},{32,35},{40,43},{48,51},{56,59},{64,6... | collective-permute-start | bytes 1572872 | tf_op jit(solution)/shard_map/ppermute | solution.py:41
  25.6 15.7 %copy-start.1 = (f32[2048]{0:T(1024)S(1)}, f32[2048]{0:T(1024)}, u32[]{:S(2)}) copy-start(f32[2048]{0:T(1024)} %param.12) | copy-start | bytes 24580
  25.7 15.7 %copy-start.2 = (s32[2]{0:T(128)S(1)}, s32[2]{0:T(128)}, u32[]{:S(2)}) copy-start(s32[2]{0:T(128)} %lengths.3) | copy-start | bytes 28
  25.8 14.6 %collective-permute-start.11 = (bf16[512,512]{1,0:T(8,128)(2,1)S(1)}, bf16[512,512]{1,0:T(8,128)(2,1)}, u32[]{:S(2)}, u32[]{:S(2)}) collective-permute-start(bf16[512,512]{1,0:T(8,128)(2,1)S(1)} %pad_maximum_fusion.2.refs_2_), channel_id=1, source_target_pairs={{0,8},{8,0},{16,24},{24,16},{32,40},{40,32},{48,56},{56,48},{64,72... | collective-permute-start | bytes 1572872 | tf_op jit(solution)/shard_map/ppermute | solution.py:41
  29.8 10.6 %collective-permute-start.9 = (bf16[512,512]{1,0:T(8,128)(2,1)S(1)}, bf16[512,512]{1,0:T(8,128)(2,1)}, u32[]{:S(2)}, u32[]{:S(2)}) collective-permute-start(bf16[512,512]{1,0:T(8,128)(2,1)S(1)} %pad_maximum_fusion.1.refs_0_), channel_id=1, source_target_pairs={{0,8},{8,0},{16,24},{24,16},{32,40},{40,32},{48,56},{56,48},{64,72... | collective-permute-start | bytes 1572872 | tf_op jit(solution)/shard_map/ppermute | solution.py:41
  34.8 5.8 %collective-permute-start.12 = (bf16[512,512]{1,0:T(8,128)(2,1)}, bf16[512,512]{1,0:T(8,128)(2,1)}, u32[]{:S(2)}, u32[]{:S(2)}) collective-permute-start(bf16[512,512]{1,0:T(8,128)(2,1)} %collective-permute-done.8.refs_3_), channel_id=1, source_target_pairs={{0,8},{8,0},{16,24},{24,16},{32,40},{40,32},{48,56},{56,48},{64,72... | collective-permute-start | bytes 1572872 | tf_op jit(solution)/shard_map/ppermute | solution.py:41
  38.7 2.6 %collective-permute-start.10 = (bf16[512,512]{1,0:T(8,128)(2,1)}, bf16[512,512]{1,0:T(8,128)(2,1)}, u32[]{:S(2)}, u32[]{:S(2)}) collective-permute-start(bf16[512,512]{1,0:T(8,128)(2,1)} %collective-permute-done.5.refs_1_), channel_id=1, source_target_pairs={{0,8},{8,0},{16,24},{24,16},{32,40},{40,32},{48,56},{56,48},{64,72... | collective-permute-start | bytes 1572872 | tf_op jit(solution)/shard_map/ppermute | solution.py:41
  41.4 1.6 %copy-start = (bf16[512,2048]{1,0:T(8,128)(2,1)S(1)}, bf16[512,2048]{1,0:T(8,128)(2,1)}, u32[]{:S(2)}) copy-start(bf16[512,2048]{1,0:T(8,128)(2,1)} %residual.2) | copy-start | bytes 6291460
  48.6 2.6 %collective-permute-start.15 = (bf16[2,2176]{1,0:T(2,128)(2,1)S(1)}, bf16[2,2176]{1,0:T(2,128)(2,1)S(1)}, u32[]{:S(2)}, u32[]{:S(2)}) collective-permute-start(bf16[2,2176]{1,0:T(2,128)(2,1)S(1)} %get-tuple-element.35), channel_id=1, source_target_pairs={{0,1},{8,9},{16,17},{24,25},{32,33},{40,41},{48,49},{56,57},{64,65... | collective-permute-start | bytes 26120 | tf_op jit(solution)/shard_map/ppermute | solution.py:41
  51.2 3.9 %collective-permute-start.16 = (bf16[4,2176]{1,0:T(4,128)(2,1)S(1)}, bf16[4,2176]{1,0:T(4,128)(2,1)S(1)}, u32[]{:S(2)}, u32[]{:S(2)}) collective-permute-start(bf16[4,2176]{1,0:T(4,128)(2,1)S(1)} %pad_maximum_fusion.14), channel_id=1, source_target_pairs={{0,3},{8,11},{16,19},{24,27},{32,35},{40,43},{48,51},{56,59},{64,6... | collective-permute-start | bytes 52232 | tf_op jit(solution)/shard_map/ppermute | solution.py:41
  55.1 2.9 %collective-permute-start.17 = (bf16[8,2176]{1,0:T(8,128)(2,1)S(1)}, bf16[8,2176]{1,0:T(8,128)(2,1)S(1)}, u32[]{:S(2)}, u32[]{:S(2)}) collective-permute-start(bf16[8,2176]{1,0:T(8,128)(2,1)S(1)} %pad_maximum_fusion.13), channel_id=1, source_target_pairs={{0,64},{8,72},{16,80},{24,88},{32,96},{40,104},{48,112},{56,120},{... | collective-permute-start | bytes 104456 | tf_op jit(solution)/shard_map/ppermute | solution.py:41
  58.0 4.4 %collective-permute-start.18 = (bf16[16,2176]{1,0:T(8,128)(2,1)S(1)}, bf16[16,2176]{1,0:T(8,128)(2,1)S(1)}, u32[]{:S(2)}, u32[]{:S(2)}) collective-permute-start(bf16[16,2176]{1,0:T(8,128)(2,1)S(1)} %pad_maximum_fusion.11), channel_id=1, source_target_pairs={{0,68},{8,76},{16,84},{24,92},{32,100},{40,108},{48,116},{56,124},... | collective-permute-start | bytes 208904 | tf_op jit(solution)/shard_map/ppermute | solution.py:41
  62.4 4.3 %collective-permute-start.19 = (bf16[32,2176]{1,0:T(8,128)(2,1)S(1)}, bf16[32,2176]{1,0:T(8,128)(2,1)S(1)}, u32[]{:S(2)}, u32[]{:S(2)}) collective-permute-start(bf16[32,2176]{1,0:T(8,128)(2,1)S(1)} %pad_maximum_fusion.9), channel_id=1, source_target_pairs={{0,16},{8,24},{16,0},{24,8},{32,48},{40,56},{48,32},{56,40},{64,80... | collective-permute-start | bytes 417800 | tf_op jit(solution)/shard_map/ppermute | solution.py:41
  63.2 6.6 %collective-permute-start.13 = (bf16[64,2176]{1,0:T(8,128)(2,1)S(1)}, bf16[64,2176]{1,0:T(8,128)(2,1)S(1)}, u32[]{:S(2)}, u32[]{:S(2)}) collective-permute-start(bf16[64,2176]{1,0:T(8,128)(2,1)S(1)} %pad_maximum_fusion.3), channel_id=1, source_target_pairs={{0,68},{8,76},{16,84},{24,92},{32,100},{40,108},{48,116},{56,124},... | collective-permute-start | bytes 835592 | tf_op jit(solution)/shard_map/ppermute | solution.py:41
  66.7 9.7 %collective-permute-start.20 = (bf16[64,2176]{1,0:T(8,128)(2,1)S(1)}, bf16[64,2176]{1,0:T(8,128)(2,1)S(1)}, u32[]{:S(2)}, u32[]{:S(2)}) collective-permute-start(bf16[64,2176]{1,0:T(8,128)(2,1)S(1)} %pad_maximum_fusion.4.refs_2_), channel_id=1, source_target_pairs={{0,48},{8,56},{16,32},{24,40},{32,16},{40,24},{48,0},{56,8},{64,11... | collective-permute-start | bytes 835592 | tf_op jit(solution)/shard_map/ppermute | solution.py:41
  69.9 11.7 %collective-permute-start.14 = (bf16[128,2176]{1,0:T(8,128)(2,1)S(1)}, bf16[128,2176]{1,0:T(8,128)(2,1)S(1)}, u32[]{:S(2)}, u32[]{:S(2)}) collective-permute-start(bf16[128,2176]{1,0:T(8,128)(2,1)S(1)} %pad_maximum_fusion.refs_0_), channel_id=1, source_target_pairs={{0,8},{8,0},{16,24},{24,16},{32,40},{40,32},{48,56},{56,48},{64,72... | collective-permute-start | bytes 1671176 | tf_op jit(solution)/shard_map/ppermute | solution.py:41
  76.3 4.0 %collective-permute-start.21 = (bf16[64,2176]{1,0:T(8,128)(2,1)S(1)}, bf16[64,2176]{1,0:T(8,128)(2,1)S(1)}, u32[]{:S(2)}, u32[]{:S(2)}) collective-permute-start(bf16[64,2176]{1,0:T(8,128)(2,1)S(1)} %pad_maximum_fusion.4.refs_2_), channel_id=1, source_target_pairs={{0,8},{8,0},{16,24},{24,16},{32,40},{40,32},{48,56},{56,48},{64,72... | collective-permute-start | bytes 835592 | tf_op jit(solution)/shard_map/ppermute | solution.py:41
  76.4 5.1 %collective-permute-start.22 = (bf16[64,2176]{1,0:T(8,128)(2,1)S(1)}, bf16[64,2176]{1,0:T(8,128)(2,1)S(1)}, u32[]{:S(2)}, u32[]{:S(2)}) collective-permute-start(bf16[64,2176]{1,0:T(8,128)(2,1)S(1)} %collective-permute-done.20.refs_3_), channel_id=1, source_target_pairs={{0,8},{8,0},{16,24},{24,16},{32,40},{40,32},{48,56},{56,48},{64,72... | collective-permute-start | bytes 835592 | tf_op jit(solution)/shard_map/ppermute | solution.py:41
  85.5 4.5 %collective-permute-start.23 = (f32[8,2432]{1,0:T(8,128)S(1)}, f32[8,2432]{1,0:T(8,128)S(1)}, u32[]{:S(2)}, u32[]{:S(2)}) collective-permute-start(f32[8,2432]{1,0:T(8,128)S(1)} %get-tuple-element.37), channel_id=1, source_target_pairs={{0,3},{8,11},{16,19},{24,27},{32,35},{40,43},{48,51},{56,59},{64,6... | collective-permute-start | bytes 233480 | tf_op jit(solution)/shard_map/ppermute | solution.py:41
  89.9 3.3 %collective-permute-start.24 = (f32[8,2432]{1,0:T(8,128)S(1)}, f32[8,2432]{1,0:T(8,128)S(1)}, u32[]{:S(2)}, u32[]{:S(2)}) collective-permute-start(f32[8,2432]{1,0:T(8,128)S(1)} %add.142), channel_id=1, source_target_pairs={{0,1},{8,9},{16,17},{24,25},{32,33},{40,41},{48,49},{56,57},{64,65... | collective-permute-start | bytes 233480 | tf_op jit(solution)/shard_map/ppermute | solution.py:41
  90.0 9.0 %collective-permute-start.25 = (bf16[1024,512]{1,0:T(8,128)(2,1)S(1)}, bf16[1024,512]{1,0:T(8,128)(2,1)S(1)}, u32[]{:S(2)}, u32[]{:S(2)}) collective-permute-start(bf16[1024,512]{1,0:T(8,128)(2,1)S(1)} %bitcast.16), channel_id=1, source_target_pairs={{0,8},{8,0},{16,24},{24,16},{32,40},{40,32},{48,56},{56,48},{64,72... | collective-permute-start | bytes 3145736 | tf_op jit(solution)/shard_map/ppermute | solution.py:41
  96.3 5.0 %collective-permute-start.26 = (bf16[512,1024]{1,0:T(8,128)(2,1)S(1)}, bf16[512,1024]{1,0:T(8,128)(2,1)S(1)}, u32[]{:S(2)}, u32[]{:S(2)}) collective-permute-start(bf16[512,1024]{1,0:T(8,128)(2,1)S(1)} %get-tuple-element.42.send), channel_id=1, source_target_pairs={{0,8},{8,0},{16,24},{24,16},{32,40},{40,32},{48,56},{56,48},{64,72... | collective-permute-start | bytes 3145736 | tf_op jit(solution)/shard_map/ppermute | solution.py:41
  102.6 14.4 %collective-permute-start.27 = (bf16[512,512]{1,0:T(8,128)(2,1)S(1)}, bf16[512,512]{1,0:T(8,128)(2,1)S(1)}, u32[]{:S(2)}, u32[]{:S(2)}) collective-permute-start(bf16[512,512]{1,0:T(8,128)(2,1)S(1)} %get-tuple-element.47), channel_id=1, source_target_pairs={{0,3},{8,11},{16,19},{24,27},{32,35},{40,43},{48,51},{56,59},{64,6... | collective-permute-start | bytes 1572872 | tf_op jit(solution)/shard_map/ppermute | solution.py:41
  105.1 14.0 %collective-permute-start.33 = (bf16[512,512]{1,0:T(8,128)(2,1)S(1)}, bf16[512,512]{1,0:T(8,128)(2,1)S(1)}, u32[]{:S(2)}, u32[]{:S(2)}) collective-permute-start(bf16[512,512]{1,0:T(8,128)(2,1)S(1)} %get-tuple-element.49), channel_id=1, source_target_pairs={{0,68},{8,76},{16,84},{24,92},{32,100},{40,108},{48,116},{56,124},... | collective-permute-start | bytes 1572872 | tf_op jit(solution)/shard_map/ppermute | solution.py:41
  117.2 6.7 %collective-permute-start.28 = (bf16[256,512]{1,0:T(8,128)(2,1)S(1)}, bf16[256,512]{1,0:T(8,128)(2,1)S(1)}, u32[]{:S(2)}, u32[]{:S(2)}) collective-permute-start(bf16[256,512]{1,0:T(8,128)(2,1)S(1)} %slice.81), channel_id=1, source_target_pairs={{0,1},{8,9},{16,17},{24,25},{32,33},{40,41},{48,49},{56,57},{64,65... | collective-permute-start | bytes 786440 | tf_op jit(solution)/shard_map/ppermute | solution.py:41
  119.3 7.6 %collective-permute-start.34 = (bf16[256,512]{1,0:T(8,128)(2,1)S(1)}, bf16[256,512]{1,0:T(8,128)(2,1)S(1)}, u32[]{:S(2)}, u32[]{:S(2)}) collective-permute-start(bf16[256,512]{1,0:T(8,128)(2,1)S(1)} %slice.80), channel_id=1, source_target_pairs={{0,3},{8,11},{16,19},{24,27},{32,35},{40,43},{48,51},{56,59},{64,6... | collective-permute-start | bytes 786440 | tf_op jit(solution)/shard_map/ppermute | solution.py:41
  124.0 5.1 %collective-permute-start.29 = (bf16[128,512]{1,0:T(8,128)(2,1)S(1)}, bf16[128,512]{1,0:T(8,128)(2,1)S(1)}, u32[]{:S(2)}, u32[]{:S(2)}) collective-permute-start(bf16[128,512]{1,0:T(8,128)(2,1)S(1)} %slice.83), channel_id=1, source_target_pairs={{0,68},{8,76},{16,84},{24,92},{32,100},{40,108},{48,116},{56,124},... | collective-permute-start | bytes 393224 | tf_op jit(solution)/shard_map/ppermute | solution.py:41
  127.0 4.2 %collective-permute-start.35 = (bf16[128,512]{1,0:T(8,128)(2,1)S(1)}, bf16[128,512]{1,0:T(8,128)(2,1)S(1)}, u32[]{:S(2)}, u32[]{:S(2)}) collective-permute-start(bf16[128,512]{1,0:T(8,128)(2,1)S(1)} %slice.82), channel_id=1, source_target_pairs={{0,1},{8,9},{16,17},{24,25},{32,33},{40,41},{48,49},{56,57},{64,65... | collective-permute-start | bytes 393224 | tf_op jit(solution)/shard_map/ppermute | solution.py:41
  129.1 4.2 %collective-permute-start.30 = (bf16[128,512]{1,0:T(8,128)(2,1)S(1)}, bf16[128,512]{1,0:T(8,128)(2,1)S(1)}, u32[]{:S(2)}, u32[]{:S(2)}) collective-permute-start(bf16[128,512]{1,0:T(8,128)(2,1)S(1)} %fusion.13), channel_id=1, source_target_pairs={{0,64},{8,72},{16,80},{24,88},{32,96},{40,104},{48,112},{56,120},{... | collective-permute-start | bytes 393224 | tf_op jit(solution)/shard_map/ppermute | solution.py:41
  131.2 3.9 %collective-permute-start.36 = (bf16[128,512]{1,0:T(8,128)(2,1)S(1)}, bf16[128,512]{1,0:T(8,128)(2,1)S(1)}, u32[]{:S(2)}, u32[]{:S(2)}) collective-permute-start(bf16[128,512]{1,0:T(8,128)(2,1)S(1)} %fusion.14), channel_id=1, source_target_pairs={{0,16},{8,24},{16,0},{24,8},{32,48},{40,56},{48,32},{56,40},{64,80... | collective-permute-start | bytes 393224 | tf_op jit(solution)/shard_map/ppermute | solution.py:41
  133.4 3.9 %collective-permute-start.31 = (bf16[128,512]{1,0:T(8,128)(2,1)S(1)}, bf16[128,512]{1,0:T(8,128)(2,1)S(1)}, u32[]{:S(2)}, u32[]{:S(2)}) collective-permute-start(bf16[128,512]{1,0:T(8,128)(2,1)S(1)} %fusion.2), channel_id=1, source_target_pairs={{0,16},{8,24},{16,0},{24,8},{32,48},{40,56},{48,32},{56,40},{64,80... | collective-permute-start | bytes 393224 | tf_op jit(solution)/shard_map/ppermute | solution.py:41
  135.2 5.1 %collective-permute-start.37 = (bf16[128,512]{1,0:T(8,128)(2,1)S(1)}, bf16[128,512]{1,0:T(8,128)(2,1)S(1)}, u32[]{:S(2)}, u32[]{:S(2)}) collective-permute-start(bf16[128,512]{1,0:T(8,128)(2,1)S(1)} %fusion.3), channel_id=1, source_target_pairs={{0,48},{8,56},{16,32},{24,40},{32,16},{40,24},{48,0},{56,8},{64,11... | collective-permute-start | bytes 393224 | tf_op jit(solution)/shard_map/ppermute | solution.py:41
  137.3 5.1 %collective-permute-start.32 = (bf16[128,512]{1,0:T(8,128)(2,1)S(1)}, bf16[128,512]{1,0:T(8,128)(2,1)S(1)}, u32[]{:S(2)}, u32[]{:S(2)}) collective-permute-start(bf16[128,512]{1,0:T(8,128)(2,1)S(1)} %fusion.4), channel_id=1, source_target_pairs={{0,48},{8,56},{16,32},{24,40},{32,16},{40,24},{48,0},{56,8},{64,11... | collective-permute-start | bytes 393224 | tf_op jit(solution)/shard_map/ppermute | solution.py:41
  140.4 4.2 %collective-permute-start.38 = (bf16[128,512]{1,0:T(8,128)(2,1)S(1)}, bf16[128,512]{1,0:T(8,128)(2,1)S(1)}, u32[]{:S(2)}, u32[]{:S(2)}) collective-permute-start(bf16[128,512]{1,0:T(8,128)(2,1)S(1)} %fusion.5), channel_id=1, source_target_pairs={{0,64},{8,72},{16,80},{24,88},{32,96},{40,104},{48,112},{56,120},{... | collective-permute-start | bytes 393224 | tf_op jit(solution)/shard_map/ppermute | solution.py:41
  144.7 7.7 %collective-permute-start.39 = (bf16[128,1024]{1,0:T(8,128)(2,1)S(1)}, bf16[128,1024]{1,0:T(8,128)(2,1)S(1)}, u32[]{:S(2)}, u32[]{:S(2)}) collective-permute-start(bf16[128,1024]{1,0:T(8,128)(2,1)S(1)} %pad_maximum_fusion.7), channel_id=1, source_target_pairs={{0,8},{8,0},{16,24},{24,16},{32,40},{40,32},{48,56},{56,48},{64,72... | collective-permute-start | bytes 786440 | tf_op jit(solution)/shard_map/ppermute | solution.py:41

commit v3 on v2

--- a/solution.py
+++ b/solution.py
@@ -25,6 +25,7 @@
     return lax.optimization_barrier((value, other))[0]
 
 LABELS = 128
+OFFSETS = (0, 1, 3, 2)
 
 
 def linear(x, y, z, c):
@@ -57,6 +58,10 @@
     return move(value, lambda x, y, z, c: (x, y, z ^ bits, c))
 
 
+def four(value, swap):
+    return [value] + [swap(value, bits) for bits in OFFSETS[1:]]
+
+
 def doubled(value, swap, bits):
     return lax.optimization_barrier(jnp.concatenate([value, swap(value, bits)], axis=0))
 
@@ -83,17 +88,17 @@
     )
 
 
-def second_order(half):
-    return [r3 * 4 + r1 * 2 + half for r3 in range(2) for r1 in range(2)]
-
-
-def block_home(x, y_hi, r3, r1, ry):
-    return (y_hi ^ ry) * 4 + (x ^ (r1 ^ (3 * r3)))
+def with_ry(ry):
+    return [q * 2 + ry for q in range(4)]
+
+
+def block_home(x, y_hi, q, ry):
+    return (y_hi ^ ry) * 4 + (x ^ OFFSETS[q])
 
 
 def forward_kernel(where, lengths, context, residual, gain, labels, *refs):
-    firsts, seconds = (refs[0:2], refs[4:6]), (refs[2:4], refs[6:8])
-    stream, inverse, pooled, embedding, added_rows, sem = refs[8:]
+    firsts, seconds = (refs[0:2], refs[6:8]), (refs[2:6], refs[8:12])
+    stream, inverse, pooled, embedding, added_rows, sem = refs[12:]
     tokens, width = residual.shape
     part = width // 4
     block = context.shape[1] // 8
@@ -102,18 +107,16 @@
     copy = pltpu.make_async_copy(residual, added_rows, sem)
     copy.start()
     ordered = [
-        jnp.concatenate(
-            [context[:, b * block : (b + 1) * block] for b in second_order(half)], axis=1
-        )
-        for half in range(2)
+        jnp.concatenate([context[:, b * block : (b + 1) * block] for b in with_ry(ry)], axis=1)
+        for ry in range(2)
     ]
     for side, (first_at, second_at) in enumerate(column_offsets(where[3], width)):
-        spans = [context[:, half * 4 * block : (half + 1) * 4 * block] for half in range(2)]
-        stream[:, pl.ds(first_at, part)] = dot(spans[0], firsts[side][0][...]) + dot(
-            spans[1], firsts[side][1][...]
+        stream[:, pl.ds(first_at, part)] = dot(ordered[0], firsts[side][0][...]) + dot(
+            ordered[1], firsts[side][1][...]
         )
-        stream[:, pl.ds(second_at, part)] = dot(ordered[0], seconds[side][0][...]) + dot(
-            ordered[1], seconds[side][1][...]
+        stream[:, pl.ds(second_at, part)] = sum(
+            dot(context[:, q * 2 * block : (q + 1) * 2 * block], seconds[side][q][...])
+            for q in range(4)
         )
     copy.wait()
     for i in range(items):
@@ -143,12 +146,12 @@
 
 
 def loss_kernel(users_here, items_here, where, gain, *refs):
-    user_refs, emb_refs = refs[:2], refs[2:6]
-    sums, user_grad, grads, emb_grads = refs[6:]
+    user_refs, emb_refs = refs[:2], refs[2:10]
+    sums, user_grad, grads, emb_grads = refs[10:14], refs[14], refs[15], refs[16]
     x, y, z, core = where[0], where[1], where[2], where[3]
     group, full = emb_refs[0].shape
     width = full - LABELS
-    items = 4 * group
+    items = 8 * group
     people = 2 * user_refs[0].shape[0]
 
     def item_home(s):
@@ -200,29 +203,28 @@
     gain_sum = jnp.sum(product - emb_float * emb_float * mean, axis=0, keepdims=True)
     place = (core * 4 + z) * 4 + y
     near = 4 * items_here
-    sums[:, :width] = emb_grads[pl.ds(pl.multiple_of(place * near, near), near), :]
-    piece = width // near
-    for j in range(near):
-        sums[j : j + 1, width : width + piece] = gain_sum[:, j * piece : (j + 1) * piece]
-    loss = jnp.sum(losses, axis=0, keepdims=True)
-    sums[:, width + piece :] = jnp.broadcast_to(loss, (near, LABELS))
+    rows = emb_grads[pl.ds(pl.multiple_of(place * near, near), near), :]
+    line = lax.broadcasted_iota(jnp.int32, (near, 1), 0)
+    loss = jnp.broadcast_to(jnp.sum(losses, axis=0, keepdims=True), (1, width))
+    for q in range(4):
+        for i in range(items_here):
+            chosen = line == (x ^ OFFSETS[q]) * items_here + i
+            sums[q][i : i + 1, :] = jnp.sum(jnp.where(chosen, rows, 0.0), axis=0, keepdims=True)
+        sums[q][items_here : items_here + 1, :] = gain_sum
+        sums[q][items_here + 1 :, :] = loss
     own = grads[pl.ds(pl.multiple_of(place * users_here, users_here), users_here), :]
     user_grad[...] = dot(own.astype(BF16), emb).astype(BF16)
 
 
-def residual_kernel(people, where, lengths, stream, inverse, pooled, gain, sums, *refs):
-    residual_grad, keep, send, gain_grad, loss = refs
+def residual_kernel(people, where, lengths, stream, inverse, pooled, gain, *refs):
+    residual_grad, keep, send, gain_grad, loss = refs[4:]
+    sums = (refs[0][...] + refs[1][...]) + (refs[2][...] + refs[3][...])
     tokens, width = stream.shape
     half = width // 2
     items = lengths.shape[0]
     length = tokens // items
-    near = sums.shape[0]
-    piece = width // near
-    line = lax.broadcasted_iota(jnp.int32, (near, 1), 0)
     for i in range(items):
-        mine = jnp.sum(
-            jnp.where(line == where[0] * items + i, sums[:, :width], 0.0), axis=0, keepdims=True
-        )
+        mine = sums[i : i + 1, :]
         pool = pooled[i : i + 1, :]
         scale = lax.rsqrt(jnp.mean(pool * pool, axis=-1, keepdims=True) + EPSILON)
         pool_grad = scale * mine - pool * scale * scale * scale * jnp.mean(
@@ -238,28 +240,29 @@
         residual_grad[span, :] = (kept * row - rows * (kept * inv * inv * mean)).astype(BF16)
     keep[...] = residual_grad[:, pl.ds(pl.multiple_of(where[3] * half, half), half)]
     send[...] = residual_grad[:, pl.ds(pl.multiple_of((1 - where[3]) * half, half), half)]
-    for j in range(near):
-        at = slice(j * piece, (j + 1) * piece)
-        gain_grad[:, at] = sums[j : j + 1, width : width + piece] / gain[:, at]
-    loss[...] = sums[0:1, width + piece : width + piece + 1] / people
+    gain_grad[...] = sums[items : items + 1, :] / gain[...]
+    loss[...] = sums[items + 1 :, 0:1] / people
 
 
 def context_kernel(where, keep, send, *refs):
-    firsts, seconds = (refs[0:2], refs[4:6]), (refs[2:4], refs[6:8])
-    context_grad = refs[8]
+    firsts, seconds = (refs[0:2], refs[6:8]), (refs[2:6], refs[8:12])
+    context_grad = refs[12]
     part = keep.shape[1] // 2
     block = context_grad.shape[1] // 8
     near = [ref[:, :part] for ref in (keep, send)]
     far = [ref[:, part:] for ref in (keep, send)]
-    from_first = [sum(contract_last(near[s], firsts[s][h][...]) for s in range(2)) for h in range(2)]
-    from_second = [sum(contract_last(far[s], seconds[s][h][...]) for s in range(2)) for h in range(2)]
-    for r3 in range(2):
-        for r1 in range(2):
-            for ry in range(2):
-                a, b = (r1 * 2 + ry) * block, (r3 * 2 + r1) * block
-                value = from_first[r3][:, a : a + block] + from_second[ry][:, b : b + block]
-                home = block_home(where[0], where[1] // 2, r3, r1, ry)
-                context_grad[:, pl.ds(pl.multiple_of(home * block, block), block)] = value.astype(BF16)
+    from_first = [
+        sum(contract_last(near[s], firsts[s][ry][...]) for s in range(2)) for ry in range(2)
+    ]
+    for q in range(4):
+        from_second = sum(contract_last(far[s], seconds[s][q][...]) for s in range(2))
+        for ry in range(2):
+            value = (
+                from_first[ry][:, q * block : (q + 1) * block]
+                + from_second[:, ry * block : (ry + 1) * block]
+            )
+            home = block_home(where[0], where[1] // 2, q, ry)
+            context_grad[:, pl.ds(pl.multiple_of(home * block, block), block)] = value.astype(BF16)
 
 
 def blocks_kernel(half, own_context, peer_context, own_grad, peer_grad, first, second):
@@ -272,7 +275,7 @@
 
     def ordered(ref):
         return jnp.concatenate(
-            [ref[b * block : (b + 1) * block, :] for b in second_order(half)], axis=0
+            [ref[b * block : (b + 1) * block, :] for b in with_ry(half)], axis=0
         )
 
     value = dot(ordered(own_context), own_grad[:, part:])
@@ -315,20 +318,13 @@
     gain = norm_gain[None, :]
 
     mine = lax.dynamic_slice(out_weight, (0, core * half), (rows, half))
-    first = doubled(mine[:, :part], swap_y, 3)
-    second = doubled(mine[:, part:], swap_x, 1)
-    step_one = first
-    first = doubled(first, swap_x, 1)
-    second = doubled(second, swap_x, 3)
-    firsts = [first, swap_x(first, 3)]
-    seconds = [second, swap_y(second, 3)]
-    pieces = firsts + seconds
+    second = doubled(mine[:, part:], swap_y, 3)
+    first = lax.optimization_barrier(jnp.concatenate(four(mine[:, :part], swap_x), axis=0))
+    pieces = [first, swap_y(first, 3)] + four(second, swap_x)
     pieces = pieces + [swap_core(p) for p in pieces]
 
-    order = [
-        block_home(x, y_hi, r3, r1, ry) for r3 in range(2) for r1 in range(2) for ry in range(2)
-    ]
-    later = after(context, step_one)
+    order = [block_home(x, y_hi, q, ry) for q in range(4) for ry in range(2)]
+    later = after(context, second)
     turned = jnp.concatenate(
         [lax.dynamic_slice(later, (0, at * rows), (tokens, rows)) for at in order], axis=1
     )
@@ -337,7 +333,6 @@
     users = jnp.concatenate([user_vectors, labels], axis=1)
     users = doubled(users, swap_z, 1)
     users = doubled(users, swap_z, 3)
-    users = doubled(users, swap_y, 1)
     labels = jnp.stack([item_ids, item_counts // 128, item_counts % 128], axis=1)
     labels = jnp.pad(labels, ((0, 0), (0, LABELS - 3))).astype(BF16)
     users, labels = lax.optimization_barrier((users, labels))
@@ -350,38 +345,33 @@
             shaped((items_here, width)),
             shaped((items_here, width + LABELS), BF16),
         ),
-        in_specs=[SMEM, SMEM, VMEM, HBM] + [VMEM] * 10,
+        in_specs=[SMEM, SMEM, VMEM, HBM] + [VMEM] * 14,
         out_specs=(VMEM,) * 4,
         scratch_shapes=[pltpu.VMEM((tokens, width), BF16), pltpu.SemaphoreType.DMA],
         compiler_params=params(20),
         name="forward",
     )(where, lengths, turned, residual, gain, labels, *pieces)
 
-    users = doubled(after(users, emb), swap_y, 3)
-    user_pieces = [users, swap_core(users)]
     own_context = after(turned, emb).T
     peer_context = swap_core(own_context)
-    for swap, bits in ((swap_x, 1), (swap_x, 3), (swap_y, 1), (swap_y, 3), (swap_z, 1)):
-        emb = doubled(emb, swap, bits)
-    emb_pieces = [emb, swap_z(emb, 3)]
+    emb = lax.optimization_barrier(jnp.concatenate(four(emb, swap_x), axis=0))
+    users = doubled(doubled(after(users, emb), swap_y, 1), swap_y, 3)
+    user_pieces = [users, swap_core(users)]
+    emb = lax.optimization_barrier(jnp.concatenate(four(emb, swap_y), axis=0))
+    emb_pieces = four(emb, swap_z)
     emb_pieces = emb_pieces + [swap_core(p) for p in emb_pieces]
 
-    near = 4 * items_here
     items, people = 128 * items_here, 32 * users_here
-    sums, user_grad = pl.pallas_call(
+    *sums, user_grad = pl.pallas_call(
         functools.partial(loss_kernel, users_here, items_here),
-        out_shape=(
-            shaped((near, width + width // near + LABELS)),
-            shaped((users_here, width), BF16),
-        ),
-        in_specs=[SMEM] + [VMEM] * 7,
-        out_specs=(VMEM,) * 2,
+        out_shape=(shaped((items_here + 2, width)),) * 4 + (shaped((users_here, width), BF16),),
+        in_specs=[SMEM] + [VMEM] * 11,
+        out_specs=(VMEM,) * 5,
         scratch_shapes=[pltpu.VMEM((people, items), F32), pltpu.VMEM((items, width), F32)],
         compiler_params=params(24),
         name="loss",
     )(where, gain, *user_pieces, *emb_pieces)
-    sums = sums + swap_x(sums, 3)
-    sums = sums + swap_x(sums, 1)
+    sums = [sums[0]] + [swap_x(sums[q], OFFSETS[q]) for q in (1, 2, 3)]
 
     residual_grad, keep, send, gain_grad, loss = pl.pallas_call(
         functools.partial(residual_kernel, 4 * people),
@@ -392,16 +382,16 @@
             shaped((1, width)),
             shaped((1, 1)),
         ),
-        in_specs=[SMEM, SMEM] + [VMEM] * 5,
+        in_specs=[SMEM, SMEM] + [VMEM] * 8,
         out_specs=(VMEM,) * 5,
         compiler_params=params(16),
         name="residual",
-    )(where, lengths, stream, inverse, pooled, gain, sums)
+    )(where, lengths, stream, inverse, pooled, gain, *sums)
     peer_grad = swap_core(send)
     context_grad = pl.pallas_call(
         context_kernel,
         out_shape=shaped((tokens, head), BF16),
-        in_specs=[SMEM] + [VMEM] * 10,
+        in_specs=[SMEM] + [VMEM] * 14,
         out_specs=VMEM,
         compiler_params=params(14),
         name="context",

time: 154 us -> 154 us (level)
  local copies, waits for them, and re-layouts: 4.33 us -> 13.4 us
  waiting for transfers between devices: 53.8 us -> 50.2 us
  starting transfers between devices: 65.1 us -> 61.7 us
  other arithmetic: 8.55 us -> 6.43 us
    unnamed x15 -> x23, local copies, waits for them, and re-layouts: 1.72 us -> 9.01 us
    ppermute x40 -> x50, waiting for transfers between devices: 53.8 us -> 50.2 us  [move(): return lax.ppermute(value, AXES, perm)]
    ppermute x40 -> x50, starting transfers between devices: 65.1 us -> 61.7 us  [move(): return lax.ppermute(value, AXES, perm)]
    concatenate x13 -> x5, other arithmetic: 3.63 us -> 1.52 us  [doubled(): jnp.concatenate([value, swap(value, bits)], axis=0)]
  transfers between devices with their start and end apart: 40 -> 50, of which waited for: 28 -> 25; matrix products, arithmetic and copies ran while one was open for 6% -> 10% of each run, Pallas kernels for 6% -> 6%
where the time goes in v3:
time: 154 us; the launch traced here: 153 us
  starting transfers between devices  61.7 us (40%)
  waiting for transfers between devices  50.2 us (33%)
  Pallas kernels  20.2 us (13%)
  local copies, waits for them, and re-layouts  13.4 us (9%)
  other arithmetic  6.43 us (4%)
    ppermute x50, starting transfers between devices, move(): return lax.ppermute(value, AXES, perm)  61.7 us
    ppermute x50, waiting for transfers between devices, move(): return lax.ppermute(value, AXES, perm)  50.2 us
    unnamed x23, local copies, waits for them, and re-layouts  9.01 us
    pallas_call x1, Pallas kernels, on_device(): pl.pallas_call(forward_kernel, out_shape=(shaped((tokens, width)), shaped...  5.48 us
    pallas_call x1, Pallas kernels, on_device(): pl.pallas_call(context_kernel, out_shape=shaped((tokens, head), BF16), in...  5.21 us
    pallas_call x1, Pallas kernels, on_device(): pl.pallas_call(functools.partial(loss_kernel, users_here, items_here), ou...  4.09 us
  transfers between devices with their start and end apart: 50, of which 25 were waited for; matrix products, arithmetic and copies ran while one was open for 10% of the time, Pallas kernels for 6%

profile of v3, /device:TPU:1, one launch (start us, length us, event | category | flops | bytes accessed | tf_op | source)
XLA Modules:
  0.0 153.0 jit_solution(13260135182390279046)
XLA Ops:
  0.7 1.1 constant_dynamic-slice_fusion.1
  1.7 3.7 %collective-permute-start.5 = (bf16[128,512]{1,0:T(8,128)(2,1)S(1)}, bf16[128,512]{1,0:T(8,128)(2,1)S(1)}, u32[]{:S(2)}, u32[]{:S(2)}) collective-permute-start(bf16[128,512]{1,0:T(8,128)(2,1)S(1)} %get-tuple-element.58), channel_id=1, source_target_pairs={{0,2},{8,10},{16,18},{24,26},{32,34},{40,42},{48,50},{56,58},{64,6... | collective-permute-start | bytes 393224 | tf_op jit(solution)/shard_map/ppermute | solution.py:42
  7.8 1.6 %collective-permute-start.1 = (bf16[8,2176]{1,0:T(8,128)(2,1)S(1)}, bf16[8,2176]{1,0:T(8,128)(2,1)S(1)}, u32[]{:S(2)}, u32[]{:S(2)}) collective-permute-start(bf16[8,2176]{1,0:T(8,128)(2,1)S(1)} %pad_maximum_fusion.8), channel_id=1, source_target_pairs={{0,16},{8,24},{16,0},{24,8},{32,48},{40,56},{48,32},{56,40},{64,80... | collective-permute-start | bytes 104456 | tf_op jit(solution)/shard_map/ppermute | solution.py:42
  9.4 2.7 %collective-permute-start = (bf16[128,512]{1,0:T(8,128)(2,1)S(1)}, bf16[128,512]{1,0:T(8,128)(2,1)S(1)}, u32[]{:S(2)}, u32[]{:S(2)}) collective-permute-start(bf16[128,512]{1,0:T(8,128)(2,1)S(1)} %get-tuple-element.59), channel_id=1, source_target_pairs={{0,68},{8,76},{16,84},{24,92},{32,100},{40,108},{48,116},{56,124},... | collective-permute-start | bytes 393224 | tf_op jit(solution)/shard_map/ppermute | solution.py:42
  14.7 2.2 %collective-permute-start.2 = (bf16[16,2176]{1,0:T(8,128)(2,1)S(1)}, bf16[16,2176]{1,0:T(8,128)(2,1)S(1)}, u32[]{:S(2)}, u32[]{:S(2)}) collective-permute-start(bf16[16,2176]{1,0:T(8,128)(2,1)S(1)} %pad_maximum_fusion.7), channel_id=1, source_target_pairs={{0,48},{8,56},{16,32},{24,40},{32,16},{40,24},{48,0},{56,8},{64,11... | collective-permute-start | bytes 208904 | tf_op jit(solution)/shard_map/ppermute | solution.py:42
  17.0 1.2 collective-permute-start.6
  19.8 3.0 %collective-permute-start.12 = (bf16[256,512]{1,0:T(8,128)(2,1)S(1)}, bf16[256,512]{1,0:T(8,128)(2,1)S(1)}, u32[]{:S(2)}, u32[]{:S(2)}) collective-permute-start(bf16[256,512]{1,0:T(8,128)(2,1)S(1)} %pad_maximum_fusion.3.refs_2_), channel_id=1, source_target_pairs={{0,8},{8,0},{16,24},{24,16},{32,40},{40,32},{48,56},{56,48},{64,72... | collective-permute-start | bytes 786440 | tf_op jit(solution)/shard_map/ppermute | solution.py:42
  22.8 3.3 %collective-permute-start.9 = (bf16[256,512]{1,0:T(8,128)(2,1)S(1)}, bf16[256,512]{1,0:T(8,128)(2,1)}, u32[]{:S(2)}, u32[]{:S(2)}) collective-permute-start(bf16[256,512]{1,0:T(8,128)(2,1)S(1)} %pad_maximum_fusion.3.refs_2_), channel_id=1, source_target_pairs={{0,2},{8,10},{16,18},{24,26},{32,34},{40,42},{48,50},{56,58},{64,6... | collective-permute-start | bytes 786440 | tf_op jit(solution)/shard_map/ppermute | solution.py:42
  27.0 1.3 copy.15
  28.3 0.9 dynamic-slice_dynamic-update-slice_fusion.7
  29.2 0.9 dynamic-slice_dynamic-update-slice_fusion.6
  30.2 0.9 dynamic-slice_dynamic-update-slice_fusion.5
  32.7 0.9 dynamic-slice_dynamic-update-slice_fusion.4
  33.6 0.9 dynamic-slice_dynamic-update-slice_fusion.3
  34.6 4.0 %collective-permute-done.8.refs_4_ = bf16[256,512]{1,0:T(8,128)(2,1)} collective-permute-done((bf16[256,512]{1,0:T(8,128)(2,1)S(1)}, bf16[256,512]{1,0:T(8,128)(2,1)}, u32[]{:S(2)}, u32[]{:S(2)}) %collective-permute-start.8) | collective-permute-done | bytes 262176 | tf_op jit(solution)/shard_map/ppermute | solution.py:42
  39.1 0.9 dynamic-slice_dynamic-update-slice_fusion.2
  40.0 0.9 dynamic-slice_dynamic-update-slice_fusion.1
  41.0 0.9 dynamic-slice_dynamic-update-slice_fusion
  42.5 1.6 %copy-done = bf16[512,2048]{1,0:T(8,128)(2,1)S(1)} copy-done((bf16[512,2048]{1,0:T(8,128)(2,1)S(1)}, bf16[512,2048]{1,0:T(8,128)(2,1)}, u32[]{:S(2)}) %copy-start) | copy-done | bytes 2097176
  44.1 0.9 copy-done.2
  45.1 5.5 %forward.1 = (f32[512,2048]{1,0:T(8,128)S(1)}, f32[512,1]{1,0:T(8,128)S(1)}, f32[2,2048]{1,0:T(2,128)S(1)}, bf16[2,2176]{1,0:T(2,128)(2,1)S(1)}) custom-call(s32[4]{0:T(128)S(1)} %pad_add_fusion.where, s32[2]{0:T(128)S(1)} %copy-done.5, bf16[512,1024]{1,0:T(8,128)(2,1)S(1)} %copy.27.context, bf16[512,2048]{1,0:T(8,128)(2,1)S(1)} %copy-done, ...), custom_call_target="tpu_custom_call" | custom-call | tf_op jit(solution)/shard_map/forward/pallas_call | solution.py:340
  50.5 2.1 %collective-permute-start.18 = (bf16[2,2176]{1,0:T(2,128)(2,1)S(1)}, bf16[2,2176]{1,0:T(2,128)(2,1)S(1)}, u32[]{:S(2)}, u32[]{:S(2)}) collective-permute-start(bf16[2,2176]{1,0:T(2,128)(2,1)S(1)} %get-tuple-element.38), channel_id=1, source_target_pairs={{0,2},{8,10},{16,18},{24,26},{32,34},{40,42},{48,50},{56,58},{64,6... | collective-permute-start | bytes 26120 | tf_op jit(solution)/shard_map/ppermute | solution.py:42
  52.7 1.8 %collective-permute-start.17 = (bf16[2,2176]{1,0:T(2,128)(2,1)S(1)}, bf16[2,2176]{1,0:T(2,128)(2,1)S(1)}, u32[]{:S(2)}, u32[]{:S(2)}) collective-permute-start(bf16[2,2176]{1,0:T(2,128)(2,1)S(1)} %get-tuple-element.38), channel_id=1, source_target_pairs={{0,3},{8,11},{16,19},{24,27},{32,35},{40,43},{48,51},{56,59},{64,6... | collective-permute-start | bytes 26120 | tf_op jit(solution)/shard_map/ppermute | solution.py:42
  54.6 1.8 %collective-permute-done.17 = bf16[2,2176]{1,0:T(2,128)(2,1)S(1)} collective-permute-done((bf16[2,2176]{1,0:T(2,128)(2,1)S(1)}, bf16[2,2176]{1,0:T(2,128)(2,1)S(1)}, u32[]{:S(2)}, u32[]{:S(2)}) %collective-permute-start.17) | collective-permute-done | bytes 8736 | tf_op jit(solution)/shard_map/ppermute | solution.py:42
  56.4 0.9 collective-permute-done.16
  57.5 3.9 %collective-permute-done.19 = bf16[32,2176]{1,0:T(8,128)(2,1)S(1)} collective-permute-done((bf16[32,2176]{1,0:T(8,128)(2,1)S(1)}, bf16[32,2176]{1,0:T(8,128)(2,1)S(1)}, u32[]{:S(2)}, u32[]{:S(2)}) %collective-permute-start.19) | collective-permute-done | bytes 139296 | tf_op jit(solution)/shard_map/ppermute | solution.py:42
  62.2 1.1 collective-permute-start.24
  63.2 1.2 collective-permute-start.23
  64.8 4.2 %collective-permute-done.20 = bf16[64,2176]{1,0:T(8,128)(2,1)S(1)} collective-permute-done((bf16[64,2176]{1,0:T(8,128)(2,1)S(1)}, bf16[64,2176]{1,0:T(8,128)(2,1)S(1)}, u32[]{:S(2)}, u32[]{:S(2)}) %collective-permute-start.20) | collective-permute-done | bytes 278560 | tf_op jit(solution)/shard_map/ppermute | solution.py:42
  69.0 3.9 %collective-permute-start.21 = (bf16[128,2176]{1,0:T(8,128)(2,1)S(1)}, bf16[128,2176]{1,0:T(8,128)(2,1)S(1)}, u32[]{:S(2)}, u32[]{:S(2)}) collective-permute-start(bf16[128,2176]{1,0:T(8,128)(2,1)S(1)} %pad_maximum_fusion.refs_0_), channel_id=1, source_target_pairs={{0,8},{8,0},{16,24},{24,16},{32,40},{40,32},{48,56},{56,48},{64,72... | collective-permute-start | bytes 1671176 | tf_op jit(solution)/shard_map/ppermute | solution.py:42
  73.0 2.2 %collective-permute-start.27 = (bf16[32,2176]{1,0:T(8,128)(2,1)S(1)}, bf16[32,2176]{1,0:T(8,128)(2,1)S(1)}, u32[]{:S(2)}, u32[]{:S(2)}) collective-permute-start(bf16[32,2176]{1,0:T(8,128)(2,1)S(1)} %pad_maximum_fusion.6.refs_2_), channel_id=1, source_target_pairs={{0,32},{8,40},{16,48},{24,56},{32,0},{40,8},{48,16},{56,24},{64,96... | collective-permute-start | bytes 417800 | tf_op jit(solution)/shard_map/ppermute | solution.py:42
  76.8 2.8 %collective-permute-done.27.refs_5_ = bf16[32,2176]{1,0:T(8,128)(2,1)S(1)} collective-permute-done((bf16[32,2176]{1,0:T(8,128)(2,1)S(1)}, bf16[32,2176]{1,0:T(8,128)(2,1)S(1)}, u32[]{:S(2)}, u32[]{:S(2)}) %collective-permute-start.27) | collective-permute-done | bytes 139296 | tf_op jit(solution)/shard_map/ppermute | solution.py:42
  79.6 1.2 collective-permute-start.31
  80.8 2.4 %collective-permute-done.26.refs_4_ = bf16[32,2176]{1,0:T(8,128)(2,1)S(1)} collective-permute-done((bf16[32,2176]{1,0:T(8,128)(2,1)S(1)}, bf16[32,2176]{1,0:T(8,128)(2,1)S(1)}, u32[]{:S(2)}, u32[]{:S(2)}) %collective-permute-start.26) | collective-permute-done | bytes 139296 | tf_op jit(solution)/shard_map/ppermute | solution.py:42
  83.7 1.0 collective-permute-done.30.refs_8_
  85.0 4.1 %loss.1 = (f32[4,2048]{1,0:T(4,128)S(1)}, f32[4,2048]{1,0:T(4,128)S(1)}, f32[4,2048]{1,0:T(4,128)S(1)}, f32[4,2048]{1,0:T(4,128)S(1)}, bf16[8,2048]{1,0:T(8,128)(2,1)}) custom-call(s32[4]{0:T(128)S(1)} %pad_add_fusion.where, f32[1,2048]{1,0:T(1,128)S(1)} %bitcast.20, bf16[128,2176]{1,0:T(8,128)(2,1)S(1)} %pad_maximum_fusion.refs_0_, ...), custom_call_target="tpu_custom_call" | custom-call | tf_op jit(solution)/shard_map/loss/pallas_call | solution.py:365
  89.1 0.9 collective-permute-start.33
  90.0 2.3 %collective-permute-start.34 = (f32[4,2048]{1,0:T(4,128)S(1)}, f32[4,2048]{1,0:T(4,128)S(1)}, u32[]{:S(2)}, u32[]{:S(2)}) collective-permute-start(f32[4,2048]{1,0:T(4,128)S(1)} %get-tuple-element.43), channel_id=1, source_target_pairs={{0,2},{8,10},{16,18},{24,26},{32,34},{40,42},{48,50},{56,58},{64,6... | collective-permute-start | bytes 98312 | tf_op jit(solution)/shard_map/ppermute | solution.py:42
  92.4 1.0 collective-permute-start.35
  94.3 3.0 %residual.3 = (bf16[512,2048]{1,0:T(8,128)(2,1)}, bf16[512,1024]{1,0:T(8,128)(2,1)S(1)}, bf16[512,1024]{1,0:T(8,128)(2,1)S(1)}, f32[1,2048]{1,0:T(1,128)}, f32[1,1]{1,0:T(1,128)}) custom-call(s32[4]{0:T(128)S(1)} %pad_add_fusion.where, s32[2]{0:T(128)S(1)} %copy-done.5, f32[512,2048]{1,0:T(8,128)S(1)} %get-tuple-element.34.stream, ...), custom_call_target="tpu_custom_call" | custom-call | tf_op jit(solution)/shard_map/residual/pallas_call | solution.py:376
  97.3 1.6 %collective-permute-start.36 = (bf16[512,1024]{1,0:T(8,128)(2,1)S(1)}, bf16[512,1024]{1,0:T(8,128)(2,1)S(1)}, u32[]{:S(2)}, u32[]{:S(2)}) collective-permute-start(bf16[512,1024]{1,0:T(8,128)(2,1)S(1)} %get-tuple-element.48.send), channel_id=1, source_target_pairs={{0,8},{8,0},{16,24},{24,16},{32,40},{40,32},{48,56},{56,48},{64,72... | collective-permute-start | bytes 3145736 | tf_op jit(solution)/shard_map/ppermute | solution.py:42
  98.9 2.3 %collective-permute-done.36.peer_grad = bf16[512,1024]{1,0:T(8,128)(2,1)S(1)} collective-permute-done((bf16[512,1024]{1,0:T(8,128)(2,1)S(1)}, bf16[512,1024]{1,0:T(8,128)(2,1)S(1)}, u32[]{:S(2)}, u32[]{:S(2)}) %collective-permute-start.36) | collective-permute-done | bytes 1048608 | tf_op jit(solution)/shard_map/ppermute | solution.py:42
  101.2 1.2 blocks_sent.1
  102.5 1.8 %collective-permute-start.37 = (bf16[512,512]{1,0:T(8,128)(2,1)S(1)}, bf16[512,512]{1,0:T(8,128)(2,1)S(1)}, u32[]{:S(2)}, u32[]{:S(2)}) collective-permute-start(bf16[512,512]{1,0:T(8,128)(2,1)S(1)} %get-tuple-element.53), channel_id=1, source_target_pairs={{0,3},{8,11},{16,19},{24,27},{32,35},{40,43},{48,51},{56,59},{64,6... | collective-permute-start | bytes 1572872 | tf_op jit(solution)/shard_map/ppermute | solution.py:42
  104.3 1.1 collective-permute-start.43
  105.4 5.2 %context.1 = bf16[512,1024]{1,0:T(8,128)(2,1)} custom-call(s32[4]{0:T(128)S(1)} %pad_add_fusion.where, bf16[512,1024]{1,0:T(8,128)(2,1)S(1)} %get-tuple-element.47.own_grad.keep, bf16[512,1024]{1,0:T(8,128)(2,1)S(1)} %get-tuple-element.48.send, bf16[512,512]{1,0:T(8,128)(2,1)S(1)} %pad_maximum_fusion.1.refs_0_, ...), custom_call_target="tpu_custom_call" | custom-call | tf_op jit(solution)/shard_map/context/pallas_call | solution.py:391
  110.6 1.2 blocks_kept.1
  111.9 5.0 %collective-permute-done.37 = bf16[512,512]{1,0:T(8,128)(2,1)S(1)} collective-permute-done((bf16[512,512]{1,0:T(8,128)(2,1)S(1)}, bf16[512,512]{1,0:T(8,128)(2,1)S(1)}, u32[]{:S(2)}, u32[]{:S(2)}) %collective-permute-start.37) | collective-permute-done | bytes 524320 | tf_op jit(solution)/shard_map/ppermute | solution.py:42
  117.2 1.1 collective-permute-done.43
  118.5 1.0 collective-permute-start.44
  119.5 4.2 %collective-permute-done.38 = bf16[256,512]{1,0:T(8,128)(2,1)S(1)} collective-permute-done((bf16[256,512]{1,0:T(8,128)(2,1)S(1)}, bf16[256,512]{1,0:T(8,128)(2,1)S(1)}, u32[]{:S(2)}, u32[]{:S(2)}) %collective-permute-start.38) | collective-permute-done | bytes 262176 | tf_op jit(solution)/shard_map/ppermute | solution.py:42
  123.9 1.2 collective-permute-start.39
  125.1 1.0 collective-permute-done.44
  126.3 2.7 %collective-permute-done.39 = bf16[128,512]{1,0:T(8,128)(2,1)S(1)} collective-permute-done((bf16[128,512]{1,0:T(8,128)(2,1)S(1)}, bf16[128,512]{1,0:T(8,128)(2,1)S(1)}, u32[]{:S(2)}, u32[]{:S(2)}) %collective-permute-start.39) | collective-permute-done | bytes 131104 | tf_op jit(solution)/shard_map/ppermute | solution.py:42
  129.1 1.0 collective-permute-done.45
  130.6 2.6 %collective-permute-done.40 = bf16[128,512]{1,0:T(8,128)(2,1)S(1)} collective-permute-done((bf16[128,512]{1,0:T(8,128)(2,1)S(1)}, bf16[128,512]{1,0:T(8,128)(2,1)S(1)}, u32[]{:S(2)}, u32[]{:S(2)}) %collective-permute-start.40) | collective-permute-done | bytes 131104 | tf_op jit(solution)/shard_map/ppermute | solution.py:42
  134.1 2.2 %collective-permute-start.47 = (bf16[128,512]{1,0:T(8,128)(2,1)S(1)}, bf16[128,512]{1,0:T(8,128)(2,1)S(1)}, u32[]{:S(2)}, u32[]{:S(2)}) collective-permute-start(bf16[128,512]{1,0:T(8,128)(2,1)S(1)} %fusion.3), channel_id=1, source_target_pairs={{0,48},{8,56},{16,32},{24,40},{32,16},{40,24},{48,0},{56,8},{64,11... | collective-permute-start | bytes 393224 | tf_op jit(solution)/shard_map/ppermute | solution.py:42
  136.3 1.7 %collective-permute-done.41 = bf16[128,512]{1,0:T(8,128)(2,1)S(1)} collective-permute-done((bf16[128,512]{1,0:T(8,128)(2,1)S(1)}, bf16[128,512]{1,0:T(8,128)(2,1)S(1)}, u32[]{:S(2)}, u32[]{:S(2)}) %collective-permute-start.41) | collective-permute-done | bytes 131104 | tf_op jit(solution)/shard_map/ppermute | solution.py:42
  138.0 2.2 %collective-permute-start.42 = (bf16[128,512]{1,0:T(8,128)(2,1)S(1)}, bf16[128,512]{1,0:T(8,128)(2,1)S(1)}, u32[]{:S(2)}, u32[]{:S(2)}) collective-permute-start(bf16[128,512]{1,0:T(8,128)(2,1)S(1)} %fusion.4), channel_id=1, source_target_pairs={{0,48},{8,56},{16,32},{24,40},{32,16},{40,24},{48,0},{56,8},{64,11... | collective-permute-start | bytes 393224 | tf_op jit(solution)/shard_map/ppermute | solution.py:42
  140.4 2.7 %collective-permute-done.42 = bf16[128,512]{1,0:T(8,128)(2,1)S(1)} collective-permute-done((bf16[128,512]{1,0:T(8,128)(2,1)S(1)}, bf16[128,512]{1,0:T(8,128)(2,1)S(1)}, u32[]{:S(2)}, u32[]{:S(2)}) %collective-permute-start.42) | collective-permute-done | bytes 131104 | tf_op jit(solution)/shard_map/ppermute | solution.py:42
  143.2 1.2 collective-permute-done.48
  144.6 6.3 %collective-permute-start.49 = (bf16[128,1024]{1,0:T(8,128)(2,1)S(1)}, bf16[128,1024]{1,0:T(8,128)(2,1)S(1)}, u32[]{:S(2)}, u32[]{:S(2)}) collective-permute-start(bf16[128,1024]{1,0:T(8,128)(2,1)S(1)} %pad_maximum_fusion.4), channel_id=1, source_target_pairs={{0,8},{8,0},{16,24},{24,16},{32,40},{40,32},{48,56},{56,48},{64,72... | collective-permute-start | bytes 786440 | tf_op jit(solution)/shard_map/ppermute | solution.py:42
  150.9 1.2 collective-permute-done.49
  152.1 0.9 maximum_select_fusion
  (106 shorter events, 17.8 us)
Async XLA Ops:
  0.6 26.3 %copy-start.6 = (bf16[512,1024]{1,0:T(8,128)(2,1)S(1)}, bf16[512,1024]{1,0:T(8,128)(2,1)}, u32[]{:S(2)}) copy-start(bf16[512,1024]{1,0:T(8,128)(2,1)} %param.9) | copy-start | bytes 3145732
  1.7 15.2 %collective-permute-start.5 = (bf16[128,512]{1,0:T(8,128)(2,1)S(1)}, bf16[128,512]{1,0:T(8,128)(2,1)S(1)}, u32[]{:S(2)}, u32[]{:S(2)}) collective-permute-start(bf16[128,512]{1,0:T(8,128)(2,1)S(1)} %get-tuple-element.58), channel_id=1, source_target_pairs={{0,2},{8,10},{16,18},{24,26},{32,34},{40,42},{48,50},{56,58},{64,6... | collective-permute-start | bytes 393224 | tf_op jit(solution)/shard_map/ppermute | solution.py:42
  5.4 11.6 %collective-permute-start.4 = (bf16[128,512]{1,0:T(8,128)(2,1)S(1)}, bf16[128,512]{1,0:T(8,128)(2,1)S(1)}, u32[]{:S(2)}, u32[]{:S(2)}) collective-permute-start(bf16[128,512]{1,0:T(8,128)(2,1)S(1)} %get-tuple-element.58), channel_id=1, source_target_pairs={{0,3},{8,11},{16,19},{24,27},{32,35},{40,43},{48,51},{56,59},{64,6... | collective-permute-start | bytes 393224 | tf_op jit(solution)/shard_map/ppermute | solution.py:42
  6.3 10.7 %collective-permute-start.3 = (bf16[128,512]{1,0:T(8,128)(2,1)S(1)}, bf16[128,512]{1,0:T(8,128)(2,1)S(1)}, u32[]{:S(2)}, u32[]{:S(2)}) collective-permute-start(bf16[128,512]{1,0:T(8,128)(2,1)S(1)} %get-tuple-element.58), channel_id=1, source_target_pairs={{0,1},{8,9},{16,17},{24,25},{32,33},{40,41},{48,49},{56,57},{64,65... | collective-permute-start | bytes 393224 | tf_op jit(solution)/shard_map/ppermute | solution.py:42
  7.8 6.2 %collective-permute-start.1 = (bf16[8,2176]{1,0:T(8,128)(2,1)S(1)}, bf16[8,2176]{1,0:T(8,128)(2,1)S(1)}, u32[]{:S(2)}, u32[]{:S(2)}) collective-permute-start(bf16[8,2176]{1,0:T(8,128)(2,1)S(1)} %pad_maximum_fusion.8), channel_id=1, source_target_pairs={{0,16},{8,24},{16,0},{24,8},{32,48},{40,56},{48,32},{56,40},{64,80... | collective-permute-start | bytes 104456 | tf_op jit(solution)/shard_map/ppermute | solution.py:42
  9.4 10.4 %collective-permute-start = (bf16[128,512]{1,0:T(8,128)(2,1)S(1)}, bf16[128,512]{1,0:T(8,128)(2,1)S(1)}, u32[]{:S(2)}, u32[]{:S(2)}) collective-permute-start(bf16[128,512]{1,0:T(8,128)(2,1)S(1)} %get-tuple-element.59), channel_id=1, source_target_pairs={{0,68},{8,76},{16,84},{24,92},{32,100},{40,108},{48,116},{56,124},... | collective-permute-start | bytes 393224 | tf_op jit(solution)/shard_map/ppermute | solution.py:42
  14.7 4.4 %collective-permute-start.2 = (bf16[16,2176]{1,0:T(8,128)(2,1)S(1)}, bf16[16,2176]{1,0:T(8,128)(2,1)S(1)}, u32[]{:S(2)}, u32[]{:S(2)}) collective-permute-start(bf16[16,2176]{1,0:T(8,128)(2,1)S(1)} %pad_maximum_fusion.7), channel_id=1, source_target_pairs={{0,48},{8,56},{16,32},{24,40},{32,16},{40,24},{48,0},{56,8},{64,11... | collective-permute-start | bytes 208904 | tf_op jit(solution)/shard_map/ppermute | solution.py:42
  17.0 14.8 %collective-permute-start.6 = (bf16[512,512]{1,0:T(8,128)(2,1)S(1)}, bf16[512,512]{1,0:T(8,128)(2,1)S(1)}, u32[]{:S(2)}, u32[]{:S(2)}) collective-permute-start(bf16[512,512]{1,0:T(8,128)(2,1)S(1)} %pad_maximum_fusion.1.refs_0_), channel_id=1, source_target_pairs={{0,68},{8,76},{16,84},{24,92},{32,100},{40,108},{48,116},{56,124},... | collective-permute-start | bytes 1572872 | tf_op jit(solution)/shard_map/ppermute | solution.py:42
  19.8 11.3 %collective-permute-start.12 = (bf16[256,512]{1,0:T(8,128)(2,1)S(1)}, bf16[256,512]{1,0:T(8,128)(2,1)S(1)}, u32[]{:S(2)}, u32[]{:S(2)}) collective-permute-start(bf16[256,512]{1,0:T(8,128)(2,1)S(1)} %pad_maximum_fusion.3.refs_2_), channel_id=1, source_target_pairs={{0,8},{8,0},{16,24},{24,16},{32,40},{40,32},{48,56},{56,48},{64,72... | collective-permute-start | bytes 786440 | tf_op jit(solution)/shard_map/ppermute | solution.py:42
  22.8 11.7 %collective-permute-start.9 = (bf16[256,512]{1,0:T(8,128)(2,1)S(1)}, bf16[256,512]{1,0:T(8,128)(2,1)}, u32[]{:S(2)}, u32[]{:S(2)}) collective-permute-start(bf16[256,512]{1,0:T(8,128)(2,1)S(1)} %pad_maximum_fusion.3.refs_2_), channel_id=1, source_target_pairs={{0,2},{8,10},{16,18},{24,26},{32,34},{40,42},{48,50},{56,58},{64,6... | collective-permute-start | bytes 786440 | tf_op jit(solution)/shard_map/ppermute | solution.py:42
  26.1 12.5 %collective-permute-start.8 = (bf16[256,512]{1,0:T(8,128)(2,1)S(1)}, bf16[256,512]{1,0:T(8,128)(2,1)}, u32[]{:S(2)}, u32[]{:S(2)}) collective-permute-start(bf16[256,512]{1,0:T(8,128)(2,1)S(1)} %pad_maximum_fusion.3.refs_2_), channel_id=1, source_target_pairs={{0,3},{8,11},{16,19},{24,27},{32,35},{40,43},{48,51},{56,59},{64,6... | collective-permute-start | bytes 786440 | tf_op jit(solution)/shard_map/ppermute | solution.py:42
  27.0 12.1 %collective-permute-start.7 = (bf16[256,512]{1,0:T(8,128)(2,1)S(1)}, bf16[256,512]{1,0:T(8,128)(2,1)}, u32[]{:S(2)}, u32[]{:S(2)}) collective-permute-start(bf16[256,512]{1,0:T(8,128)(2,1)S(1)} %pad_maximum_fusion.3.refs_2_), channel_id=1, source_target_pairs={{0,1},{8,9},{16,17},{24,25},{32,33},{40,41},{48,49},{56,57},{64,65... | collective-permute-start | bytes 786440 | tf_op jit(solution)/shard_map/ppermute | solution.py:42
  28.3 14.2 %copy-start.4 = (f32[2048]{0:T(1024)S(1)}, f32[2048]{0:T(1024)}, u32[]{:S(2)}) copy-start(f32[2048]{0:T(1024)} %param.12) | copy-start | bytes 24580
  28.3 14.2 %copy-start.5 = (s32[2]{0:T(128)S(1)}, s32[2]{0:T(128)}, u32[]{:S(2)}) copy-start(s32[2]{0:T(128)} %lengths.3) | copy-start | bytes 28
  31.1 9.9 %copy-start.1 = (bf16[256,512]{1,0:T(8,128)(2,1)}, bf16[256,512]{1,0:T(8,128)(2,1)S(1)}, u32[]{:S(2)}) copy-start(bf16[256,512]{1,0:T(8,128)(2,1)S(1)} %collective-permute-done.12.refs_8_) | copy-start | bytes 786436
  31.1 11.4 %collective-permute-start.10 = (bf16[512,512]{1,0:T(8,128)(2,1)S(1)}, bf16[512,512]{1,0:T(8,128)(2,1)}, u32[]{:S(2)}, u32[]{:S(2)}) collective-permute-start(bf16[512,512]{1,0:T(8,128)(2,1)S(1)} %pad_maximum_fusion.1.refs_0_), channel_id=1, source_target_pairs={{0,8},{8,0},{16,24},{24,16},{32,40},{40,32},{48,56},{56,48},{64,72... | collective-permute-start | bytes 1572872 | tf_op jit(solution)/shard_map/ppermute | solution.py:42
  31.8 10.6 %collective-permute-start.11 = (bf16[512,512]{1,0:T(8,128)(2,1)S(1)}, bf16[512,512]{1,0:T(8,128)(2,1)}, u32[]{:S(2)}, u32[]{:S(2)}) collective-permute-start(bf16[512,512]{1,0:T(8,128)(2,1)S(1)} %collective-permute-done.6.refs_1_), channel_id=1, source_target_pairs={{0,8},{8,0},{16,24},{24,16},{32,40},{40,32},{48,56},{56,48},{64,72... | collective-permute-start | bytes 1572872 | tf_op jit(solution)/shard_map/ppermute | solution.py:42
  34.5 7.9 %collective-permute-start.15 = (bf16[256,512]{1,0:T(8,128)(2,1)}, bf16[256,512]{1,0:T(8,128)(2,1)}, u32[]{:S(2)}, u32[]{:S(2)}) collective-permute-start(bf16[256,512]{1,0:T(8,128)(2,1)} %collective-permute-done.9.refs_5_), channel_id=1, source_target_pairs={{0,8},{8,0},{16,24},{24,16},{32,40},{40,32},{48,56},{56,48},{64,72... | collective-permute-start | bytes 786440 | tf_op jit(solution)/shard_map/ppermute | solution.py:42
  38.6 3.8 %collective-permute-start.14 = (bf16[256,512]{1,0:T(8,128)(2,1)}, bf16[256,512]{1,0:T(8,128)(2,1)}, u32[]{:S(2)}, u32[]{:S(2)}) collective-permute-start(bf16[256,512]{1,0:T(8,128)(2,1)} %collective-permute-done.8.refs_4_), channel_id=1, source_target_pairs={{0,8},{8,0},{16,24},{24,16},{32,40},{40,32},{48,56},{56,48},{64,72... | collective-permute-start | bytes 786440 | tf_op jit(solution)/shard_map/ppermute | solution.py:42
  39.1 3.4 %collective-permute-start.13 = (bf16[256,512]{1,0:T(8,128)(2,1)}, bf16[256,512]{1,0:T(8,128)(2,1)}, u32[]{:S(2)}, u32[]{:S(2)}) collective-permute-start(bf16[256,512]{1,0:T(8,128)(2,1)} %collective-permute-done.7.refs_3_), channel_id=1, source_target_pairs={{0,8},{8,0},{16,24},{24,16},{32,40},{40,32},{48,56},{56,48},{64,72... | collective-permute-start | bytes 786440 | tf_op jit(solution)/shard_map/ppermute | solution.py:42
  42.5 1.6 %copy-start = (bf16[512,2048]{1,0:T(8,128)(2,1)S(1)}, bf16[512,2048]{1,0:T(8,128)(2,1)}, u32[]{:S(2)}) copy-start(bf16[512,2048]{1,0:T(8,128)(2,1)} %residual.2) | copy-start | bytes 6291460
  44.1 0.9 copy-start.2
  45.1 12.3 %copy-start.7 = (bf16[32,2176]{1,0:T(8,128)(2,1)S(1)}, bf16[32,2176]{1,0:T(8,128)(2,1)}, u32[]{:S(2)}) copy-start(bf16[32,2176]{1,0:T(8,128)(2,1)} %pad_maximum_fusion.5) | copy-start | bytes 417796
  50.5 4.1 %collective-permute-start.18 = (bf16[2,2176]{1,0:T(2,128)(2,1)S(1)}, bf16[2,2176]{1,0:T(2,128)(2,1)S(1)}, u32[]{:S(2)}, u32[]{:S(2)}) collective-permute-start(bf16[2,2176]{1,0:T(2,128)(2,1)S(1)} %get-tuple-element.38), channel_id=1, source_target_pairs={{0,2},{8,10},{16,18},{24,26},{32,34},{40,42},{48,50},{56,58},{64,6... | collective-permute-start | bytes 26120 | tf_op jit(solution)/shard_map/ppermute | solution.py:42
  52.7 3.7 %collective-permute-start.17 = (bf16[2,2176]{1,0:T(2,128)(2,1)S(1)}, bf16[2,2176]{1,0:T(2,128)(2,1)S(1)}, u32[]{:S(2)}, u32[]{:S(2)}) collective-permute-start(bf16[2,2176]{1,0:T(2,128)(2,1)S(1)} %get-tuple-element.38), channel_id=1, source_target_pairs={{0,3},{8,11},{16,19},{24,27},{32,35},{40,43},{48,51},{56,59},{64,6... | collective-permute-start | bytes 26120 | tf_op jit(solution)/shard_map/ppermute | solution.py:42
  54.5 2.8 %collective-permute-start.16 = (bf16[2,2176]{1,0:T(2,128)(2,1)S(1)}, bf16[2,2176]{1,0:T(2,128)(2,1)S(1)}, u32[]{:S(2)}, u32[]{:S(2)}) collective-permute-start(bf16[2,2176]{1,0:T(2,128)(2,1)S(1)} %get-tuple-element.38), channel_id=1, source_target_pairs={{0,1},{8,9},{16,17},{24,25},{32,33},{40,41},{48,49},{56,57},{64,65... | collective-permute-start | bytes 26120 | tf_op jit(solution)/shard_map/ppermute | solution.py:42
  57.4 4.0 %collective-permute-start.19 = (bf16[32,2176]{1,0:T(8,128)(2,1)S(1)}, bf16[32,2176]{1,0:T(8,128)(2,1)S(1)}, u32[]{:S(2)}, u32[]{:S(2)}) collective-permute-start(bf16[32,2176]{1,0:T(8,128)(2,1)S(1)} %copy-done.7), channel_id=1, source_target_pairs={{0,64},{8,72},{16,80},{24,88},{32,96},{40,104},{48,112},{56,120},{... | collective-permute-start | bytes 417800 | tf_op jit(solution)/shard_map/ppermute | solution.py:42
  61.4 7.6 %collective-permute-start.20 = (bf16[64,2176]{1,0:T(8,128)(2,1)S(1)}, bf16[64,2176]{1,0:T(8,128)(2,1)S(1)}, u32[]{:S(2)}, u32[]{:S(2)}) collective-permute-start(bf16[64,2176]{1,0:T(8,128)(2,1)S(1)} %pad_maximum_fusion.2), channel_id=1, source_target_pairs={{0,68},{8,76},{16,84},{24,92},{32,100},{40,108},{48,116},{56,124},... | collective-permute-start | bytes 835592 | tf_op jit(solution)/shard_map/ppermute | solution.py:42
  62.2 10.8 %collective-permute-start.24 = (bf16[8,2176]{1,0:T(8,128)(2,1)S(1)}, bf16[8,2176]{1,0:T(8,128)(2,1)S(1)}, u32[]{:S(2)}, u32[]{:S(2)}) collective-permute-start(bf16[8,2176]{1,0:T(8,128)(2,1)S(1)} %pad_maximum_fusion.9), channel_id=1, source_target_pairs={{0,4},{8,12},{16,20},{24,28},{32,36},{40,44},{48,52},{56,60},{64,6... | collective-permute-start | bytes 104456 | tf_op jit(solution)/shard_map/ppermute | solution.py:42
  63.2 9.7 %collective-permute-start.23 = (bf16[8,2176]{1,0:T(8,128)(2,1)S(1)}, bf16[8,2176]{1,0:T(8,128)(2,1)S(1)}, u32[]{:S(2)}, u32[]{:S(2)}) collective-permute-start(bf16[8,2176]{1,0:T(8,128)(2,1)S(1)} %pad_maximum_fusion.9), channel_id=1, source_target_pairs={{0,68},{8,76},{16,84},{24,92},{32,100},{40,108},{48,116},{56,124},... | collective-permute-start | bytes 104456 | tf_op jit(solution)/shard_map/ppermute | solution.py:42
  64.4 8.6 %collective-permute-start.22 = (bf16[8,2176]{1,0:T(8,128)(2,1)S(1)}, bf16[8,2176]{1,0:T(8,128)(2,1)S(1)}, u32[]{:S(2)}, u32[]{:S(2)}) collective-permute-start(bf16[8,2176]{1,0:T(8,128)(2,1)S(1)} %pad_maximum_fusion.9), channel_id=1, source_target_pairs={{0,64},{8,72},{16,80},{24,88},{32,96},{40,104},{48,112},{56,120},{... | collective-permute-start | bytes 104456 | tf_op jit(solution)/shard_map/ppermute | solution.py:42
  69.0 16.0 %collective-permute-start.21 = (bf16[128,2176]{1,0:T(8,128)(2,1)S(1)}, bf16[128,2176]{1,0:T(8,128)(2,1)S(1)}, u32[]{:S(2)}, u32[]{:S(2)}) collective-permute-start(bf16[128,2176]{1,0:T(8,128)(2,1)S(1)} %pad_maximum_fusion.refs_0_), channel_id=1, source_target_pairs={{0,8},{8,0},{16,24},{24,16},{32,40},{40,32},{48,56},{56,48},{64,72... | collective-permute-start | bytes 1671176 | tf_op jit(solution)/shard_map/ppermute | solution.py:42
  73.0 6.6 %collective-permute-start.27 = (bf16[32,2176]{1,0:T(8,128)(2,1)S(1)}, bf16[32,2176]{1,0:T(8,128)(2,1)S(1)}, u32[]{:S(2)}, u32[]{:S(2)}) collective-permute-start(bf16[32,2176]{1,0:T(8,128)(2,1)S(1)} %pad_maximum_fusion.6.refs_2_), channel_id=1, source_target_pairs={{0,32},{8,40},{16,48},{24,56},{32,0},{40,8},{48,16},{56,24},{64,96... | collective-permute-start | bytes 417800 | tf_op jit(solution)/shard_map/ppermute | solution.py:42
  75.2 8.0 %collective-permute-start.26 = (bf16[32,2176]{1,0:T(8,128)(2,1)S(1)}, bf16[32,2176]{1,0:T(8,128)(2,1)S(1)}, u32[]{:S(2)}, u32[]{:S(2)}) collective-permute-start(bf16[32,2176]{1,0:T(8,128)(2,1)S(1)} %pad_maximum_fusion.6.refs_2_), channel_id=1, source_target_pairs={{0,48},{8,56},{16,32},{24,40},{32,16},{40,24},{48,0},{56,8},{64,11... | collective-permute-start | bytes 417800 | tf_op jit(solution)/shard_map/ppermute | solution.py:42
  75.5 8.2 %collective-permute-start.25 = (bf16[32,2176]{1,0:T(8,128)(2,1)S(1)}, bf16[32,2176]{1,0:T(8,128)(2,1)S(1)}, u32[]{:S(2)}, u32[]{:S(2)}) collective-permute-start(bf16[32,2176]{1,0:T(8,128)(2,1)S(1)} %pad_maximum_fusion.6.refs_2_), channel_id=1, source_target_pairs={{0,16},{8,24},{16,0},{24,8},{32,48},{40,56},{48,32},{56,40},{64,80... | collective-permute-start | bytes 417800 | tf_op jit(solution)/shard_map/ppermute | solution.py:42
  75.9 7.8 %collective-permute-start.28 = (bf16[32,2176]{1,0:T(8,128)(2,1)S(1)}, bf16[32,2176]{1,0:T(8,128)(2,1)S(1)}, u32[]{:S(2)}, u32[]{:S(2)}) collective-permute-start(bf16[32,2176]{1,0:T(8,128)(2,1)S(1)} %pad_maximum_fusion.6.refs_2_), channel_id=1, source_target_pairs={{0,8},{8,0},{16,24},{24,16},{32,40},{40,32},{48,56},{56,48},{64,72... | collective-permute-start | bytes 417800 | tf_op jit(solution)/shard_map/ppermute | solution.py:42
  79.6 4.1 %collective-permute-start.31 = (bf16[32,2176]{1,0:T(8,128)(2,1)S(1)}, bf16[32,2176]{1,0:T(8,128)(2,1)S(1)}, u32[]{:S(2)}, u32[]{:S(2)}) collective-permute-start(bf16[32,2176]{1,0:T(8,128)(2,1)S(1)} %collective-permute-done.27.refs_5_), channel_id=1, source_target_pairs={{0,8},{8,0},{16,24},{24,16},{32,40},{40,32},{48,56},{56,48},{64,72... | collective-permute-start | bytes 417800 | tf_op jit(solution)/shard_map/ppermute | solution.py:42
  83.2 1.5 collective-permute-start.30
  83.7 1.4 collective-permute-start.29
  89.1 4.3 %collective-permute-start.32 = (f32[4,2048]{1,0:T(4,128)S(1)}, f32[4,2048]{1,0:T(4,128)S(1)}, u32[]{:S(2)}, u32[]{:S(2)}) collective-permute-start(f32[4,2048]{1,0:T(4,128)S(1)} %get-tuple-element.41), channel_id=1, source_target_pairs={{0,1},{8,9},{16,17},{24,25},{32,33},{40,41},{48,49},{56,57},{64,65... | collective-permute-start | bytes 98312 | tf_op jit(solution)/shard_map/ppermute | solution.py:42
  89.1 4.3 %collective-permute-start.33 = (f32[4,2048]{1,0:T(4,128)S(1)}, f32[4,2048]{1,0:T(4,128)S(1)}, u32[]{:S(2)}, u32[]{:S(2)}) collective-permute-start(f32[4,2048]{1,0:T(4,128)S(1)} %get-tuple-element.42), channel_id=1, source_target_pairs={{0,3},{8,11},{16,19},{24,27},{32,35},{40,43},{48,51},{56,59},{64,6... | collective-permute-start | bytes 98312 | tf_op jit(solution)/shard_map/ppermute | solution.py:42
  90.0 4.3 %collective-permute-start.34 = (f32[4,2048]{1,0:T(4,128)S(1)}, f32[4,2048]{1,0:T(4,128)S(1)}, u32[]{:S(2)}, u32[]{:S(2)}) collective-permute-start(f32[4,2048]{1,0:T(4,128)S(1)} %get-tuple-element.43), channel_id=1, source_target_pairs={{0,2},{8,10},{16,18},{24,26},{32,34},{40,42},{48,50},{56,58},{64,6... | collective-permute-start | bytes 98312 | tf_op jit(solution)/shard_map/ppermute | solution.py:42
  92.4 6.5 %collective-permute-start.35 = (bf16[1024,512]{1,0:T(8,128)(2,1)S(1)}, bf16[1024,512]{1,0:T(8,128)(2,1)S(1)}, u32[]{:S(2)}, u32[]{:S(2)}) collective-permute-start(bf16[1024,512]{1,0:T(8,128)(2,1)S(1)} %bitcast.16), channel_id=1, source_target_pairs={{0,8},{8,0},{16,24},{24,16},{32,40},{40,32},{48,56},{56,48},{64,72... | collective-permute-start | bytes 3145736 | tf_op jit(solution)/shard_map/ppermute | solution.py:42
  97.3 3.9 %collective-permute-start.36 = (bf16[512,1024]{1,0:T(8,128)(2,1)S(1)}, bf16[512,1024]{1,0:T(8,128)(2,1)S(1)}, u32[]{:S(2)}, u32[]{:S(2)}) collective-permute-start(bf16[512,1024]{1,0:T(8,128)(2,1)S(1)} %get-tuple-element.48.send), channel_id=1, source_target_pairs={{0,8},{8,0},{16,24},{24,16},{32,40},{40,32},{48,56},{56,48},{64,72... | collective-permute-start | bytes 3145736 | tf_op jit(solution)/shard_map/ppermute | solution.py:42
  101.2 4.2 %copy-start.3 = (bf16[256,512]{1,0:T(8,128)(2,1)S(1)}, bf16[256,512]{1,0:T(8,128)(2,1)}, u32[]{:S(2)}) copy-start(bf16[256,512]{1,0:T(8,128)(2,1)} %copy-done.1) | copy-start | bytes 786436
  102.5 14.4 %collective-permute-start.37 = (bf16[512,512]{1,0:T(8,128)(2,1)S(1)}, bf16[512,512]{1,0:T(8,128)(2,1)S(1)}, u32[]{:S(2)}, u32[]{:S(2)}) collective-permute-start(bf16[512,512]{1,0:T(8,128)(2,1)S(1)} %get-tuple-element.53), channel_id=1, source_target_pairs={{0,3},{8,11},{16,19},{24,27},{32,35},{40,43},{48,51},{56,59},{64,6... | collective-permute-start | bytes 1572872 | tf_op jit(solution)/shard_map/ppermute | solution.py:42
  104.3 14.0 %collective-permute-start.43 = (bf16[512,512]{1,0:T(8,128)(2,1)S(1)}, bf16[512,512]{1,0:T(8,128)(2,1)S(1)}, u32[]{:S(2)}, u32[]{:S(2)}) collective-permute-start(bf16[512,512]{1,0:T(8,128)(2,1)S(1)} %get-tuple-element.55), channel_id=1, source_target_pairs={{0,68},{8,76},{16,84},{24,92},{32,100},{40,108},{48,116},{56,124},... | collective-permute-start | bytes 1572872 | tf_op jit(solution)/shard_map/ppermute | solution.py:42
  117.1 6.7 %collective-permute-start.38 = (bf16[256,512]{1,0:T(8,128)(2,1)S(1)}, bf16[256,512]{1,0:T(8,128)(2,1)S(1)}, u32[]{:S(2)}, u32[]{:S(2)}) collective-permute-start(bf16[256,512]{1,0:T(8,128)(2,1)S(1)} %slice.81), channel_id=1, source_target_pairs={{0,1},{8,9},{16,17},{24,25},{32,33},{40,41},{48,49},{56,57},{64,65... | collective-permute-start | bytes 786440 | tf_op jit(solution)/shard_map/ppermute | solution.py:42
  118.5 7.6 %collective-permute-start.44 = (bf16[256,512]{1,0:T(8,128)(2,1)S(1)}, bf16[256,512]{1,0:T(8,128)(2,1)S(1)}, u32[]{:S(2)}, u32[]{:S(2)}) collective-permute-start(bf16[256,512]{1,0:T(8,128)(2,1)S(1)} %slice.80), channel_id=1, source_target_pairs={{0,3},{8,11},{16,19},{24,27},{32,35},{40,43},{48,51},{56,59},{64,6... | collective-permute-start | bytes 786440 | tf_op jit(solution)/shard_map/ppermute | solution.py:42
  123.9 5.1 %collective-permute-start.39 = (bf16[128,512]{1,0:T(8,128)(2,1)S(1)}, bf16[128,512]{1,0:T(8,128)(2,1)S(1)}, u32[]{:S(2)}, u32[]{:S(2)}) collective-permute-start(bf16[128,512]{1,0:T(8,128)(2,1)S(1)} %slice.83), channel_id=1, source_target_pairs={{0,68},{8,76},{16,84},{24,92},{32,100},{40,108},{48,116},{56,124},... | collective-permute-start | bytes 393224 | tf_op jit(solution)/shard_map/ppermute | solution.py:42
  126.2 3.9 %collective-permute-start.45 = (bf16[128,512]{1,0:T(8,128)(2,1)S(1)}, bf16[128,512]{1,0:T(8,128)(2,1)S(1)}, u32[]{:S(2)}, u32[]{:S(2)}) collective-permute-start(bf16[128,512]{1,0:T(8,128)(2,1)S(1)} %slice.82), channel_id=1, source_target_pairs={{0,1},{8,9},{16,17},{24,25},{32,33},{40,41},{48,49},{56,57},{64,65... | collective-permute-start | bytes 393224 | tf_op jit(solution)/shard_map/ppermute | solution.py:42
  129.0 4.2 %collective-permute-start.40 = (bf16[128,512]{1,0:T(8,128)(2,1)S(1)}, bf16[128,512]{1,0:T(8,128)(2,1)S(1)}, u32[]{:S(2)}, u32[]{:S(2)}) collective-permute-start(bf16[128,512]{1,0:T(8,128)(2,1)S(1)} %fusion.13), channel_id=1, source_target_pairs={{0,64},{8,72},{16,80},{24,88},{32,96},{40,104},{48,112},{56,120},{... | collective-permute-start | bytes 393224 | tf_op jit(solution)/shard_map/ppermute | solution.py:42
  130.1 3.9 %collective-permute-start.46 = (bf16[128,512]{1,0:T(8,128)(2,1)S(1)}, bf16[128,512]{1,0:T(8,128)(2,1)S(1)}, u32[]{:S(2)}, u32[]{:S(2)}) collective-permute-start(bf16[128,512]{1,0:T(8,128)(2,1)S(1)} %fusion.14), channel_id=1, source_target_pairs={{0,16},{8,24},{16,0},{24,8},{32,48},{40,56},{48,32},{56,40},{64,80... | collective-permute-start | bytes 393224 | tf_op jit(solution)/shard_map/ppermute | solution.py:42
  133.3 4.7 %collective-permute-start.41 = (bf16[128,512]{1,0:T(8,128)(2,1)S(1)}, bf16[128,512]{1,0:T(8,128)(2,1)S(1)}, u32[]{:S(2)}, u32[]{:S(2)}) collective-permute-start(bf16[128,512]{1,0:T(8,128)(2,1)S(1)} %fusion.2), channel_id=1, source_target_pairs={{0,16},{8,24},{16,0},{24,8},{32,48},{40,56},{48,32},{56,40},{64,80... | collective-permute-start | bytes 393224 | tf_op jit(solution)/shard_map/ppermute | solution.py:42
  134.1 6.1 %collective-permute-start.47 = (bf16[128,512]{1,0:T(8,128)(2,1)S(1)}, bf16[128,512]{1,0:T(8,128)(2,1)S(1)}, u32[]{:S(2)}, u32[]{:S(2)}) collective-permute-start(bf16[128,512]{1,0:T(8,128)(2,1)S(1)} %fusion.3), channel_id=1, source_target_pairs={{0,48},{8,56},{16,32},{24,40},{32,16},{40,24},{48,0},{56,8},{64,11... | collective-permute-start | bytes 393224 | tf_op jit(solution)/shard_map/ppermute | solution.py:42
  138.0 5.1 %collective-permute-start.42 = (bf16[128,512]{1,0:T(8,128)(2,1)S(1)}, bf16[128,512]{1,0:T(8,128)(2,1)S(1)}, u32[]{:S(2)}, u32[]{:S(2)}) collective-permute-start(bf16[128,512]{1,0:T(8,128)(2,1)S(1)} %fusion.4), channel_id=1, source_target_pairs={{0,48},{8,56},{16,32},{24,40},{32,16},{40,24},{48,0},{56,8},{64,11... | collective-permute-start | bytes 393224 | tf_op jit(solution)/shard_map/ppermute | solution.py:42
  140.3 4.2 %collective-permute-start.48 = (bf16[128,512]{1,0:T(8,128)(2,1)S(1)}, bf16[128,512]{1,0:T(8,128)(2,1)S(1)}, u32[]{:S(2)}, u32[]{:S(2)}) collective-permute-start(bf16[128,512]{1,0:T(8,128)(2,1)S(1)} %fusion.5), channel_id=1, source_target_pairs={{0,64},{8,72},{16,80},{24,88},{32,96},{40,104},{48,112},{56,120},{... | collective-permute-start | bytes 393224 | tf_op jit(solution)/shard_map/ppermute | solution.py:42
  144.6 7.4 %collective-permute-start.49 = (bf16[128,1024]{1,0:T(8,128)(2,1)S(1)}, bf16[128,1024]{1,0:T(8,128)(2,1)S(1)}, u32[]{:S(2)}, u32[]{:S(2)}) collective-permute-start(bf16[128,1024]{1,0:T(8,128)(2,1)S(1)} %pad_maximum_fusion.4), channel_id=1, source_target_pairs={{0,8},{8,0},{16,24},{24,16},{32,40},{40,32},{48,56},{56,48},{64,72... | collective-permute-start | bytes 786440 | tf_op jit(solution)/shard_map/ppermute | solution.py:42

commit v4 on v3

--- a/solution.py
+++ b/solution.py
@@ -15,6 +15,7 @@
 VMEM = pl.BlockSpec(memory_space=pltpu.VMEM)
 SMEM = pl.BlockSpec(memory_space=pltpu.SMEM)
 HBM = pl.BlockSpec(memory_space=pltpu.HBM)
+ANY = pl.BlockSpec(memory_space=pl.ANY)
 
 
 def params(mebibytes):
@@ -25,6 +26,7 @@
     return lax.optimization_barrier((value, other))[0]
 
 LABELS = 128
+POSITIVE = 8
 OFFSETS = (0, 1, 3, 2)
 
 
@@ -88,15 +90,24 @@
     )
 
 
-def with_ry(ry):
-    return [q * 2 + ry for q in range(4)]
-
-
 def block_home(x, y_hi, q, ry):
     return (y_hi ^ ry) * 4 + (x ^ OFFSETS[q])
 
 
-def forward_kernel(where, lengths, context, residual, gain, labels, *refs):
+def blocks_of(ref, where, pairs, block):
+    picked = []
+    for q, ry in pairs:
+        home = block_home(where[0], where[1] // 2, q, ry)
+        picked.append(ref[:, pl.ds(pl.multiple_of(home * block, block), block)])
+    return jnp.concatenate(picked, axis=1)
+
+
+def weight_rows(ref, block):
+    rows = ref.shape[0] // 2
+    return jnp.concatenate([ref[:block, :], ref[rows : rows + block, :]], axis=0)
+
+
+def forward_kernel(where, lengths, ids, counts, positive, context, residual, gain, *refs):
     firsts, seconds = (refs[0:2], refs[6:8]), (refs[2:6], refs[8:12])
     stream, inverse, pooled, embedding, added_rows, sem = refs[12:]
     tokens, width = residual.shape
@@ -106,17 +117,14 @@
     length = tokens // items
     copy = pltpu.make_async_copy(residual, added_rows, sem)
     copy.start()
-    ordered = [
-        jnp.concatenate([context[:, b * block : (b + 1) * block] for b in with_ry(ry)], axis=1)
-        for ry in range(2)
-    ]
+    by_ry = [blocks_of(context, where, [(q, ry) for q in range(4)], block) for ry in range(2)]
+    by_q = [blocks_of(context, where, [(q, 0), (q, 1)], block) for q in range(4)]
     for side, (first_at, second_at) in enumerate(column_offsets(where[3], width)):
-        stream[:, pl.ds(first_at, part)] = dot(ordered[0], firsts[side][0][...]) + dot(
-            ordered[1], firsts[side][1][...]
+        stream[:, pl.ds(first_at, part)] = sum(
+            dot(by_ry[ry], firsts[side][ry][...]) for ry in range(2)
         )
         stream[:, pl.ds(second_at, part)] = sum(
-            dot(context[:, q * 2 * block : (q + 1) * 2 * block], seconds[side][q][...])
-            for q in range(4)
+            dot(by_q[q], weight_rows(seconds[side][q], block)) for q in range(4)
         )
     copy.wait()
     for i in range(items):
@@ -132,7 +140,15 @@
     pool = pooled[...]
     scale = lax.rsqrt(jnp.mean(pool * pool, axis=-1, keepdims=True) + EPSILON)
     embedding[:, :width] = (pool * scale).astype(BF16)
-    embedding[:, width:] = labels[...]
+    row = lax.broadcasted_iota(jnp.int32, (items, LABELS), 0)
+    lane = lax.broadcasted_iota(jnp.int32, (items, LABELS), 1)
+    labels = jnp.zeros((items, LABELS), jnp.int32)
+    for i in range(items):
+        for at, value in enumerate((ids[i], counts[i] // 128, counts[i] % 128)):
+            labels = jnp.where((row == i) & (lane == at), value, labels)
+    for u in range(positive.shape[0]):
+        labels = jnp.where((row == 0) & (lane == POSITIVE + u), positive[u], labels)
+    embedding[:, width:] = labels.astype(F32).astype(BF16)
 
 
 def bit(value, k):
@@ -145,14 +161,29 @@
     return jnp.where(to == home(of), 1.0, 0.0).astype(BF16)
 
 
-def loss_kernel(users_here, items_here, where, gain, *refs):
-    user_refs, emb_refs = refs[:2], refs[2:10]
-    sums, user_grad, grads, emb_grads = refs[10:14], refs[14], refs[15], refs[16]
+def loss_kernel(users_here, items_here, block, where, gain, *refs):
+    piece_refs, emb_refs = refs[:8], refs[8:16]
+    sums, user_grad, grads, emb_grads, riders, sems = refs[16:20], *refs[20:]
     x, y, z, core = where[0], where[1], where[2], where[3]
     group, full = emb_refs[0].shape
     width = full - LABELS
     items = 8 * group
-    people = 2 * user_refs[0].shape[0]
+    people = 16 * users_here
+    half_rows, part = piece_refs[0].shape[0] // 2, piece_refs[0].shape[1]
+    parts = width // part
+    rode = parts * users_here
+    copies = []
+    for n in range(8):
+        for ry in range(2):
+            copies.append(
+                pltpu.make_async_copy(
+                    piece_refs[n].at[pl.ds(ry * half_rows + block, rode)],
+                    riders.at[pl.ds((n * 2 + ry) * rode, rode)],
+                    sems.at[n * 2 + ry],
+                )
+            )
+    for copy in copies:
+        copy.start()
 
     def item_home(s):
         one = s // items_here
@@ -162,20 +193,37 @@
         ac = core ^ bit(one, 6)
         return (((ac * 4 + az) * 4 + ay) * 4 + ax) * items_here + s % items_here
 
-    def user_home(s):
-        one = s // users_here
-        az = z ^ bit(one, 0) ^ (3 * bit(one, 1))
-        ay = y ^ bit(one, 2) ^ (3 * bit(one, 3))
-        ac = core ^ bit(one, 4)
-        return ((ac * 4 + az) * 4 + ay) * users_here + s % users_here
-
     placed = jnp.concatenate([ref[...] for ref in emb_refs], axis=0)
     turned = dot(one_hot_turn(items, item_home), placed).astype(BF16)
     emb, labels = turned[:, :width], turned[:, width:]
-    placed = jnp.concatenate([ref[...] for ref in user_refs], axis=0)
-    turned = dot(one_hot_turn(people, user_home), placed).astype(BF16)
-    users = turned[:, :width]
-    positive = turned[:, width : width + 1].astype(F32)
+    for copy in copies:
+        copy.wait()
+    to = lax.broadcasted_iota(jnp.int32, (people, 16 * rode), 0)
+    of = lax.broadcasted_iota(jnp.int32, (people, 16 * rode), 1)
+    one = of // rode
+    holder = ((core ^ bit(one, 3)) * 2 + ((y // 2) ^ bit(one, 0))) * 4 + (
+        x ^ bit(one, 1) ^ (3 * bit(one, 2))
+    )
+    home = holder * users_here + of % users_here
+    column = (of % rode) // users_here
+    users = jnp.concatenate(
+        [
+            dot(
+                jnp.where((to == home) & (column == j), 1.0, 0.0).astype(BF16), riders[...]
+            ).astype(BF16)
+            for j in range(parts)
+        ],
+        axis=1,
+    )
+    person = lax.broadcasted_iota(jnp.int32, (people, items), 0)
+    at = lax.broadcasted_iota(jnp.int32, (people, items), 1)
+    g = person // users_here
+    g_y = jnp.where((g // 4) % 2 == y // 2, y, 3 - y)
+    g_row = (((g // 8 * 4 + z) * 4 + g_y) * 4 + g % 4) * items_here
+    positives = dot(jnp.where(at == g_row, 1.0, 0.0).astype(BF16), labels)
+    lane = lax.broadcasted_iota(jnp.int32, (people, LABELS), 1)
+    slot = lax.broadcasted_iota(jnp.int32, (people, LABELS), 0) % users_here
+    positive = jnp.sum(jnp.where(lane == POSITIVE + slot, positives, 0.0), axis=1, keepdims=True)
     item_labels = contract_rows(labels, one_hot_turn(items, lambda s: s))
     ids = item_labels[0:1, :]
     log_counts = jnp.log(item_labels[1:2, :] * 128.0 + item_labels[2:3, :])
@@ -201,30 +249,34 @@
     product = emb_float * all_grads
     mean = jnp.mean(product, axis=-1, keepdims=True)
     gain_sum = jnp.sum(product - emb_float * emb_float * mean, axis=0, keepdims=True)
-    place = (core * 4 + z) * 4 + y
-    near = 4 * items_here
-    rows = emb_grads[pl.ds(pl.multiple_of(place * near, near), near), :]
-    line = lax.broadcasted_iota(jnp.int32, (near, 1), 0)
+    line = lax.broadcasted_iota(jnp.int32, (8 * items_here, 1), 0)
     loss = jnp.broadcast_to(jnp.sum(losses, axis=0, keepdims=True), (1, width))
     for q in range(4):
-        for i in range(items_here):
-            chosen = line == (x ^ OFFSETS[q]) * items_here + i
-            sums[q][i : i + 1, :] = jnp.sum(jnp.where(chosen, rows, 0.0), axis=0, keepdims=True)
-        sums[q][items_here : items_here + 1, :] = gain_sum
-        sums[q][items_here + 1 :, :] = loss
-    own = grads[pl.ds(pl.multiple_of(place * users_here, users_here), users_here), :]
+        az = z ^ OFFSETS[q]
+        start = ((core * 4 + az) * 4 + (y // 2) * 2) * 4 * items_here
+        rows = emb_grads[pl.ds(pl.multiple_of(start, 8 * items_here), 8 * items_here), :]
+        for other in range(2):
+            for i in range(items_here):
+                chosen = line == (((y % 2) ^ other) * 4 + x) * items_here + i
+                n = other * items_here + i
+                sums[q][n : n + 1, :] = jnp.sum(
+                    jnp.where(chosen, rows, 0.0), axis=0, keepdims=True
+                )
+        sums[q][2 * items_here : 2 * items_here + 1, :] = gain_sum
+        sums[q][2 * items_here + 1 :, :] = jnp.broadcast_to(loss, (6 - 2 * items_here + 1, width))
+    place = ((core * 2 + y // 2) * 4 + x) * users_here
+    own = grads[pl.ds(pl.multiple_of(place, users_here), users_here), :]
     user_grad[...] = dot(own.astype(BF16), emb).astype(BF16)
 
 
 def residual_kernel(people, where, lengths, stream, inverse, pooled, gain, *refs):
-    residual_grad, keep, send, gain_grad, loss = refs[4:]
-    sums = (refs[0][...] + refs[1][...]) + (refs[2][...] + refs[3][...])
+    own_sums, other_sums, residual_grad, keep, send, gain_grad, loss = refs
     tokens, width = stream.shape
     half = width // 2
     items = lengths.shape[0]
     length = tokens // items
     for i in range(items):
-        mine = sums[i : i + 1, :]
+        mine = own_sums[i : i + 1, :] + other_sums[items + i : items + i + 1, :]
         pool = pooled[i : i + 1, :]
         scale = lax.rsqrt(jnp.mean(pool * pool, axis=-1, keepdims=True) + EPSILON)
         pool_grad = scale * mine - pool * scale * scale * scale * jnp.mean(
@@ -240,8 +292,10 @@
         residual_grad[span, :] = (kept * row - rows * (kept * inv * inv * mean)).astype(BF16)
     keep[...] = residual_grad[:, pl.ds(pl.multiple_of(where[3] * half, half), half)]
     send[...] = residual_grad[:, pl.ds(pl.multiple_of((1 - where[3]) * half, half), half)]
-    gain_grad[...] = sums[items : items + 1, :] / gain[...]
-    loss[...] = sums[items + 1 :, 0:1] / people
+    at = 2 * items
+    gain_grad[...] = (own_sums[at : at + 1, :] + other_sums[at : at + 1, :]) / gain[...]
+    at = at + 1
+    loss[...] = (own_sums[at : at + 1, 0:1] + other_sums[at : at + 1, 0:1]) / people
 
 
 def context_kernel(where, keep, send, *refs):
@@ -255,7 +309,7 @@
         sum(contract_last(near[s], firsts[s][ry][...]) for s in range(2)) for ry in range(2)
     ]
     for q in range(4):
-        from_second = sum(contract_last(far[s], seconds[s][q][...]) for s in range(2))
+        from_second = sum(contract_last(far[s], weight_rows(seconds[s][q], block)) for s in range(2))
         for ry in range(2):
             value = (
                 from_first[ry][:, q * block : (q + 1) * block]
@@ -265,22 +319,18 @@
             context_grad[:, pl.ds(pl.multiple_of(home * block, block), block)] = value.astype(BF16)
 
 
-def blocks_kernel(half, own_context, peer_context, own_grad, peer_grad, first, second):
+def blocks_kernel(half, where, own_context, peer_context, own_grad, peer_grad, first, second):
     part = own_grad.shape[1] // 2
-    block = own_context.shape[0] // 8
-    span = slice(half * 4 * block, (half + 1) * 4 * block)
-    value = dot(own_context[span, :], own_grad[:, :part])
-    value = value + dot(peer_context[span, :], peer_grad[:, :part])
-    first[...] = value.astype(first.dtype)
-
-    def ordered(ref):
-        return jnp.concatenate(
-            [ref[b * block : (b + 1) * block, :] for b in with_ry(half)], axis=0
-        )
-
-    value = dot(ordered(own_context), own_grad[:, part:])
-    value = value + dot(ordered(peer_context), peer_grad[:, part:])
-    second[...] = value.astype(second.dtype)
+    block = own_context.shape[1] // 8
+
+    def product(pairs, at):
+        return contract_rows(
+            blocks_of(own_context, where, pairs, block), own_grad[:, at : at + part]
+        ) + contract_rows(blocks_of(peer_context, where, pairs, block), peer_grad[:, at : at + part])
+
+    pairs = [(q, ry) for q in (2 * half, 2 * half + 1) for ry in range(2)]
+    first[...] = product(pairs, 0).astype(first.dtype)
+    second[...] = product([(q, half) for q in range(4)], part).astype(second.dtype)
 
 
 def shaped(shape, dtype=F32):
@@ -318,24 +368,11 @@
     gain = norm_gain[None, :]
 
     mine = lax.dynamic_slice(out_weight, (0, core * half), (rows, half))
-    second = doubled(mine[:, part:], swap_y, 3)
+    riders = [user_vectors[:, j * part : (j + 1) * part] for j in range(width // part)]
+    second = doubled(jnp.concatenate([mine[:, part:]] + riders, axis=0), swap_y, 3)
     first = lax.optimization_barrier(jnp.concatenate(four(mine[:, :part], swap_x), axis=0))
     pieces = [first, swap_y(first, 3)] + four(second, swap_x)
     pieces = pieces + [swap_core(p) for p in pieces]
-
-    order = [block_home(x, y_hi, q, ry) for q in range(4) for ry in range(2)]
-    later = after(context, second)
-    turned = jnp.concatenate(
-        [lax.dynamic_slice(later, (0, at * rows), (tokens, rows)) for at in order], axis=1
-    )
-
-    labels = jnp.pad(positive[:, None], ((0, 0), (0, LABELS - 1))).astype(BF16)
-    users = jnp.concatenate([user_vectors, labels], axis=1)
-    users = doubled(users, swap_z, 1)
-    users = doubled(users, swap_z, 3)
-    labels = jnp.stack([item_ids, item_counts // 128, item_counts % 128], axis=1)
-    labels = jnp.pad(labels, ((0, 0), (0, LABELS - 3))).astype(BF16)
-    users, labels = lax.optimization_barrier((users, labels))
 
     stream, inverse, pooled, emb = pl.pallas_call(
         forward_kernel,
@@ -345,36 +382,40 @@
             shaped((items_here, width)),
             shaped((items_here, width + LABELS), BF16),
         ),
-        in_specs=[SMEM, SMEM, VMEM, HBM] + [VMEM] * 14,
+        in_specs=[SMEM] * 5 + [VMEM, HBM] + [VMEM] * 13,
         out_specs=(VMEM,) * 4,
         scratch_shapes=[pltpu.VMEM((tokens, width), BF16), pltpu.SemaphoreType.DMA],
         compiler_params=params(20),
         name="forward",
-    )(where, lengths, turned, residual, gain, labels, *pieces)
-
-    own_context = after(turned, emb).T
-    peer_context = swap_core(own_context)
+    )(where, lengths, item_ids, item_counts, positive, context, residual, gain, *pieces)
+
     emb = lax.optimization_barrier(jnp.concatenate(four(emb, swap_x), axis=0))
-    users = doubled(doubled(after(users, emb), swap_y, 1), swap_y, 3)
-    user_pieces = [users, swap_core(users)]
+    peer_context = swap_core(after(context, emb))
     emb = lax.optimization_barrier(jnp.concatenate(four(emb, swap_y), axis=0))
     emb_pieces = four(emb, swap_z)
     emb_pieces = emb_pieces + [swap_core(p) for p in emb_pieces]
 
-    items, people = 128 * items_here, 32 * users_here
+    items, people = 128 * items_here, 16 * users_here
+    riding = pieces[2:6] + pieces[8:12]
     *sums, user_grad = pl.pallas_call(
-        functools.partial(loss_kernel, users_here, items_here),
-        out_shape=(shaped((items_here + 2, width)),) * 4 + (shaped((users_here, width), BF16),),
-        in_specs=[SMEM] + [VMEM] * 11,
+        functools.partial(loss_kernel, users_here, items_here, rows),
+        out_shape=(shaped((8, width)),) * 4 + (shaped((users_here, width), BF16),),
+        in_specs=[SMEM, VMEM] + [ANY] * 8 + [VMEM] * 8,
         out_specs=(VMEM,) * 5,
-        scratch_shapes=[pltpu.VMEM((people, items), F32), pltpu.VMEM((items, width), F32)],
+        scratch_shapes=[
+            pltpu.VMEM((people, items), F32),
+            pltpu.VMEM((items, width), F32),
+            pltpu.VMEM((people * (width // part), part), BF16),
+            pltpu.SemaphoreType.DMA((16,)),
+        ],
         compiler_params=params(24),
         name="loss",
-    )(where, gain, *user_pieces, *emb_pieces)
-    sums = [sums[0]] + [swap_x(sums[q], OFFSETS[q]) for q in (1, 2, 3)]
+    )(where, gain, *riding, *emb_pieces)
+    sums = [sums[0]] + [swap_z(sums[q], OFFSETS[q]) for q in (1, 2, 3)]
+    sums = (sums[0] + sums[1]) + (sums[2] + sums[3])
 
     residual_grad, keep, send, gain_grad, loss = pl.pallas_call(
-        functools.partial(residual_kernel, 4 * people),
+        functools.partial(residual_kernel, 8 * people),
         out_shape=(
             shaped((tokens, width), BF16),
             shaped((tokens, half), BF16),
@@ -382,11 +423,11 @@
             shaped((1, width)),
             shaped((1, 1)),
         ),
-        in_specs=[SMEM, SMEM] + [VMEM] * 8,
+        in_specs=[SMEM, SMEM] + [VMEM] * 6,
         out_specs=(VMEM,) * 5,
         compiler_params=params(16),
         name="residual",
-    )(where, lengths, stream, inverse, pooled, gain, *sums)
+    )(where, lengths, stream, inverse, pooled, gain, sums, swap_y(sums, 1))
     peer_grad = swap_core(send)
     context_grad = pl.pallas_call(
         context_kernel,
@@ -397,13 +438,13 @@
         name="context",
     )(where, keep, send, *pieces)
 
-    operands = (own_context, peer_context, keep, peer_grad)
+    operands = (where, context, peer_context, keep, peer_grad)
 
     def blocks(which, dtype, name):
         return pl.pallas_call(
             functools.partial(blocks_kernel, which),
             out_shape=(shaped((4 * rows, part), dtype),) * 2,
-            in_specs=[VMEM] * 4,
+            in_specs=[SMEM] + [VMEM] * 4,
             out_specs=(VMEM,) * 2,
             compiler_params=params(14),
             name=name,

time: 154 us -> 151 us (0.981)
  starting transfers between devices: 61.7 us -> 67.7 us
  local copies, waits for them, and re-layouts: 13.4 us -> 9.01 us
  other arithmetic: 6.43 us -> 2.11 us
  Pallas kernels: 20.2 us -> 22.6 us
  waiting for transfers between devices: 50.2 us -> 48.2 us
    ppermute x50 -> x46, starting transfers between devices: 61.7 us -> 67.7 us  [move(): return lax.ppermute(value, AXES, perm)]
    concatenate x6 -> x0, other arithmetic: 2.28 us -> none  [the longest x5 1.52 us: doubled(): jnp.concatenate([value, swap(value, bits)], axis=0)]
    ppermute x50 -> x46, waiting for transfers between devices: 50.2 us -> 48.2 us  [move(): return lax.ppermute(value, AXES, perm)]
    unnamed x23 -> x21, local copies, waits for them, and re-layouts: 9.01 us -> 8.17 us
  transfers between devices with their start and end apart: 50 -> 46, of which waited for: 25 -> 27; matrix products, arithmetic and copies ran while one was open for 10% -> 4% of each run, Pallas kernels for 6% -> 7%
where the time goes in v4:
time: 151 us
  starting transfers between devices  67.7 us (45%)
  waiting for transfers between devices  48.2 us (32%)
  Pallas kernels  22.6 us (15%)
  local copies, waits for them, and re-layouts  9.01 us (6%)
  other arithmetic  2.11 us (1%)
    ppermute x46, starting transfers between devices, move(): return lax.ppermute(value, AXES, perm)  67.7 us
    ppermute x46, waiting for transfers between devices, move(): return lax.ppermute(value, AXES, perm)  48.2 us
    unnamed x21, local copies, waits for them, and re-layouts  8.17 us
    pallas_call x1, Pallas kernels, on_device(): pl.pallas_call(forward_kernel, out_shape=(shaped((tokens, width)), shaped...  5.38 us
    pallas_call x1, Pallas kernels, on_device(): pl.pallas_call(functools.partial(loss_kernel, users_here, items_here, row...  5.34 us
    pallas_call x1, Pallas kernels, on_device(): pl.pallas_call(context_kernel, out_shape=shaped((tokens, head), BF16), in...  5.1 us
    pallas_call x2, Pallas kernels, blocks(): pl.pallas_call(functools.partial(blocks_kernel, which), out_shape=(shaped...  3.71 us
    pallas_call x1, Pallas kernels, on_device(): pl.pallas_call(functools.partial(residual_kernel, 8 * people), out_shape=...  3.04 us
  transfers between devices with their start and end apart: 46, of which 27 were waited for; matrix products, arithmetic and copies ran while one was open for 4% of the time, Pallas kernels for 7%

profile of v4, /device:TPU:1, one launch (start us, length us, event | category | flops | bytes accessed | tf_op | source)
XLA Modules:
  0.0 150.5 jit_solution(1379917835012534692)
XLA Ops:
  0.7 1.1 dynamic-slice_dynamic-update-slice_fusion.1
  1.8 3.7 %collective-permute-start.2 = (bf16[128,512]{1,0:T(8,128)(2,1)S(1)}, bf16[128,512]{1,0:T(8,128)(2,1)S(1)}, u32[]{:S(2)}, u32[]{:S(2)}) collective-permute-start(bf16[128,512]{1,0:T(8,128)(2,1)S(1)} %get-tuple-element.52), channel_id=1, source_target_pairs={{0,2},{8,10},{16,18},{24,26},{32,34},{40,42},{48,50},{56,58},{64,6... | collective-permute-start | bytes 393224 | tf_op jit(solution)/shard_map/ppermute | solution.py:44
  5.4 0.9 collective-permute-start.1
  6.3 0.7 constant_dynamic-update-slice_fusion.3
  7.0 0.7 constant_dynamic-update-slice_fusion.2
  7.7 0.7 constant_dynamic-update-slice_fusion.1
  8.4 0.7 constant_dynamic-update-slice_fusion
  9.1 2.7 %collective-permute-start.4 = (bf16[160,512]{1,0:T(8,128)(2,1)S(1)}, bf16[160,512]{1,0:T(8,128)(2,1)S(1)}, u32[]{:S(2)}, u32[]{:S(2)}) collective-permute-start(bf16[160,512]{1,0:T(8,128)(2,1)S(1)} %get-tuple-element.53), channel_id=1, source_target_pairs={{0,68},{8,76},{16,84},{24,92},{32,100},{40,108},{48,116},{56,124},... | collective-permute-start | bytes 491528 | tf_op jit(solution)/shard_map/ppermute | solution.py:44
  11.8 0.7 constant_dynamic-update-slice_fusion.7
  12.5 0.7 constant_dynamic-update-slice_fusion.6
  13.3 1.2 collective-permute-start.3
  14.5 0.7 constant_dynamic-update-slice_fusion.5
  15.2 2.0 %collective-permute-start.10 = (bf16[320,512]{1,0:T(8,128)(2,1)S(1)}, bf16[320,512]{1,0:T(8,128)(2,1)S(1)}, u32[]{:S(2)}, u32[]{:S(2)}) collective-permute-start(bf16[320,512]{1,0:T(8,128)(2,1)S(1)} %constant_dynamic-update-slice_fusion.4.refs_2_.refs_0_), channel_id=1, source_target_pairs={{0,8},{8,0},{16,24},{24,16},{32,40},{40,32},{48,56},{56,48},{64,72... | collective-permute-start | bytes 983048 | tf_op jit(solution)/shard_map/ppermute | solution.py:44
  17.2 4.2 %collective-permute-start.7 = (bf16[320,512]{1,0:T(8,128)(2,1)S(1)}, bf16[320,512]{1,0:T(8,128)(2,1)S(1)}, u32[]{:S(2)}, u32[]{:S(2)}) collective-permute-start(bf16[320,512]{1,0:T(8,128)(2,1)S(1)} %constant_dynamic-update-slice_fusion.4.refs_2_.refs_0_), channel_id=1, source_target_pairs={{0,2},{8,10},{16,18},{24,26},{32,34},{40,42},{48,50},{56,58},{64,6... | collective-permute-start | bytes 983048 | tf_op jit(solution)/shard_map/ppermute | solution.py:44
  21.8 4.7 %collective-permute-done.3.refs_1_ = bf16[512,512]{1,0:T(8,128)(2,1)} collective-permute-done((bf16[512,512]{1,0:T(8,128)(2,1)S(1)}, bf16[512,512]{1,0:T(8,128)(2,1)}, u32[]{:S(2)}, u32[]{:S(2)}) %collective-permute-start.3) | collective-permute-done | bytes 524320 | tf_op jit(solution)/shard_map/ppermute | solution.py:44
  26.6 2.4 %collective-permute-start.9 = (bf16[512,512]{1,0:T(8,128)(2,1)}, bf16[512,512]{1,0:T(8,128)(2,1)}, u32[]{:S(2)}, u32[]{:S(2)}) collective-permute-start(bf16[512,512]{1,0:T(8,128)(2,1)} %collective-permute-done.3.refs_1_), channel_id=1, source_target_pairs={{0,8},{8,0},{16,24},{24,16},{32,40},{40,32},{48,56},{56,48},{64,72... | collective-permute-start | bytes 1572872 | tf_op jit(solution)/shard_map/ppermute | solution.py:44
  29.4 0.9 collective-permute-start.13
  30.4 6.2 %collective-permute-done.6.refs_4_.refs_2_ = bf16[320,512]{1,0:T(8,128)(2,1)S(1)} collective-permute-done((bf16[320,512]{1,0:T(8,128)(2,1)S(1)}, bf16[320,512]{1,0:T(8,128)(2,1)S(1)}, u32[]{:S(2)}, u32[]{:S(2)}) %collective-permute-start.6) | collective-permute-done | bytes 327712 | tf_op jit(solution)/shard_map/ppermute | solution.py:44
  37.2 1.3 collective-permute-done.12.refs_10_.refs_6_
  39.0 1.6 %copy-done.1 = bf16[512,2048]{1,0:T(8,128)(2,1)S(1)} copy-done((bf16[512,2048]{1,0:T(8,128)(2,1)S(1)}, bf16[512,2048]{1,0:T(8,128)(2,1)}, u32[]{:S(2)}) %copy-start.1) | copy-done | bytes 2097176
  40.5 0.7 copy-done.5
  41.9 5.4 %forward.1 = (f32[512,2048]{1,0:T(8,128)S(1)}, f32[512,1]{1,0:T(8,128)S(1)}, f32[2,2048]{1,0:T(2,128)S(1)}, bf16[2,2176]{1,0:T(2,128)(2,1)S(1)}) custom-call(s32[4]{0:T(128)S(1)} %pad_add_fusion.where, s32[2]{0:T(128)S(1)} %copy-done.3, s32[2]{0:T(128)S(1)} %copy-done.4, s32[2]{0:T(128)S(1)} %copy-done.5, s32[8]{0:T(128)S(1)} %copy-done.6, ...), custom_call_target="tpu_custom_call" | custom-call | tf_op jit(solution)/shard_map/forward/pallas_call | solution.py:377
  47.2 1.5 %collective-permute-start.16 = (bf16[2,2176]{1,0:T(2,128)(2,1)S(1)}, bf16[2,2176]{1,0:T(2,128)(2,1)S(1)}, u32[]{:S(2)}, u32[]{:S(2)}) collective-permute-start(bf16[2,2176]{1,0:T(2,128)(2,1)S(1)} %get-tuple-element.31), channel_id=1, source_target_pairs={{0,2},{8,10},{16,18},{24,26},{32,34},{40,42},{48,50},{56,58},{64,6... | collective-permute-start | bytes 26120 | tf_op jit(solution)/shard_map/ppermute | solution.py:44
  48.8 2.0 %collective-permute-start.15 = (bf16[2,2176]{1,0:T(2,128)(2,1)S(1)}, bf16[2,2176]{1,0:T(2,128)(2,1)S(1)}, u32[]{:S(2)}, u32[]{:S(2)}) collective-permute-start(bf16[2,2176]{1,0:T(2,128)(2,1)S(1)} %get-tuple-element.31), channel_id=1, source_target_pairs={{0,3},{8,11},{16,19},{24,27},{32,35},{40,43},{48,51},{56,59},{64,6... | collective-permute-start | bytes 26120 | tf_op jit(solution)/shard_map/ppermute | solution.py:44
  51.3 1.2 collective-permute-done.15
  52.5 1.1 collective-permute-done.14
  53.6 2.5 %collective-permute-start.19 = (bf16[8,2176]{1,0:T(8,128)(2,1)S(1)}, bf16[8,2176]{1,0:T(8,128)(2,1)S(1)}, u32[]{:S(2)}, u32[]{:S(2)}) collective-permute-start(bf16[8,2176]{1,0:T(8,128)(2,1)S(1)} %pad_maximum_fusion.3), channel_id=1, source_target_pairs={{0,4},{8,12},{16,20},{24,28},{32,36},{40,44},{48,52},{56,60},{64,6... | collective-permute-start | bytes 104456 | tf_op jit(solution)/shard_map/ppermute | solution.py:44
  56.1 1.1 collective-permute-start.18
  58.0 2.5 %collective-permute-done.18 = bf16[8,2176]{1,0:T(8,128)(2,1)S(1)} collective-permute-done((bf16[8,2176]{1,0:T(8,128)(2,1)S(1)}, bf16[8,2176]{1,0:T(8,128)(2,1)S(1)}, u32[]{:S(2)}, u32[]{:S(2)}) %collective-permute-start.18) | collective-permute-done | bytes 34848 | tf_op jit(solution)/shard_map/ppermute | solution.py:44
  60.6 3.7 %collective-permute-start.22 = (bf16[32,2176]{1,0:T(8,128)(2,1)S(1)}, bf16[32,2176]{1,0:T(8,128)(2,1)S(1)}, u32[]{:S(2)}, u32[]{:S(2)}) collective-permute-start(bf16[32,2176]{1,0:T(8,128)(2,1)S(1)} %pad_maximum_fusion.2.refs_8_), channel_id=1, source_target_pairs={{0,32},{8,40},{16,48},{24,56},{32,0},{40,8},{48,16},{56,24},{64,96... | collective-permute-start | bytes 417800 | tf_op jit(solution)/shard_map/ppermute | solution.py:44
  65.0 3.3 %collective-permute-start.23 = (bf16[32,2176]{1,0:T(8,128)(2,1)S(1)}, bf16[32,2176]{1,0:T(8,128)(2,1)S(1)}, u32[]{:S(2)}, u32[]{:S(2)}) collective-permute-start(bf16[32,2176]{1,0:T(8,128)(2,1)S(1)} %pad_maximum_fusion.2.refs_8_), channel_id=1, source_target_pairs={{0,8},{8,0},{16,24},{24,16},{32,40},{40,32},{48,56},{56,48},{64,72... | collective-permute-start | bytes 417800 | tf_op jit(solution)/shard_map/ppermute | solution.py:44
  68.3 2.6 %collective-permute-start.26 = (bf16[32,2176]{1,0:T(8,128)(2,1)S(1)}, bf16[32,2176]{1,0:T(8,128)(2,1)S(1)}, u32[]{:S(2)}, u32[]{:S(2)}) collective-permute-start(bf16[32,2176]{1,0:T(8,128)(2,1)S(1)} %collective-permute-done.22.refs_11_), channel_id=1, source_target_pairs={{0,8},{8,0},{16,24},{24,16},{32,40},{40,32},{48,56},{56,48},{64,72... | collective-permute-start | bytes 417800 | tf_op jit(solution)/shard_map/ppermute | solution.py:44
  70.9 2.6 %collective-permute-start.25 = (bf16[32,2176]{1,0:T(8,128)(2,1)S(1)}, bf16[32,2176]{1,0:T(8,128)(2,1)S(1)}, u32[]{:S(2)}, u32[]{:S(2)}) collective-permute-start(bf16[32,2176]{1,0:T(8,128)(2,1)S(1)} %collective-permute-done.21.refs_10_), channel_id=1, source_target_pairs={{0,8},{8,0},{16,24},{24,16},{32,40},{40,32},{48,56},{56,48},{64,72... | collective-permute-start | bytes 417800 | tf_op jit(solution)/shard_map/ppermute | solution.py:44
  73.6 1.0 collective-permute-done.25.refs_14_
  74.9 5.3 %loss.1 = (f32[8,2048]{1,0:T(8,128)S(1)}, f32[8,2048]{1,0:T(8,128)S(1)}, f32[8,2048]{1,0:T(8,128)S(1)}, f32[8,2048]{1,0:T(8,128)S(1)}, bf16[8,2048]{1,0:T(8,128)(2,1)}) custom-call(s32[4]{0:T(128)S(1)} %pad_add_fusion.where, f32[1,2048]{1,0:T(1,128)S(1)} %bitcast.8, bf16[320,512]{1,0:T(8,128)(2,1)S(1)} %constant_dynamic-update-slice_fusion.4.refs_2_.refs_0_, ...), custom_call_target="tpu_custom_call" | custom-call | tf_op jit(solution)/shard_map/loss/pallas_call | solution.py:400
  80.5 1.6 %collective-permute-start.28 = (f32[8,2048]{1,0:T(8,128)S(1)}, f32[8,2048]{1,0:T(8,128)S(1)}, u32[]{:S(2)}, u32[]{:S(2)}) collective-permute-start(f32[8,2048]{1,0:T(8,128)S(1)} %get-tuple-element.34), channel_id=1, source_target_pairs={{0,48},{8,56},{16,32},{24,40},{32,16},{40,24},{48,0},{56,8},{64,11... | collective-permute-start | bytes 196616 | tf_op jit(solution)/shard_map/ppermute | solution.py:44
  82.1 1.5 %collective-permute-start.29 = (f32[8,2048]{1,0:T(8,128)S(1)}, f32[8,2048]{1,0:T(8,128)S(1)}, u32[]{:S(2)}, u32[]{:S(2)}) collective-permute-start(f32[8,2048]{1,0:T(8,128)S(1)} %get-tuple-element.35), channel_id=1, source_target_pairs={{0,32},{8,40},{16,48},{24,56},{32,0},{40,8},{48,16},{56,24},{64,96... | collective-permute-start | bytes 196616 | tf_op jit(solution)/shard_map/ppermute | solution.py:44
  83.9 1.0 collective-permute-done.28
  84.9 1.9 %collective-permute-done.29 = f32[8,2048]{1,0:T(8,128)S(1)} collective-permute-done((f32[8,2048]{1,0:T(8,128)S(1)}, f32[8,2048]{1,0:T(8,128)S(1)}, u32[]{:S(2)}, u32[]{:S(2)}) %collective-permute-start.29) | collective-permute-done | bytes 65568 | tf_op jit(solution)/shard_map/ppermute | solution.py:44
  87.2 2.1 %collective-permute-start.31 = (bf16[512,1024]{1,0:T(8,128)(2,1)S(1)}, bf16[512,1024]{1,0:T(8,128)(2,1)S(1)}, u32[]{:S(2)}, u32[]{:S(2)}) collective-permute-start(bf16[512,1024]{1,0:T(8,128)(2,1)S(1)} %copy-done), channel_id=1, source_target_pairs={{0,8},{8,0},{16,24},{24,16},{32,40},{40,32},{48,56},{56,48},{64,72... | collective-permute-start | bytes 3145736 | tf_op jit(solution)/shard_map/ppermute | solution.py:44
  89.9 3.0 %residual.3 = (bf16[512,2048]{1,0:T(8,128)(2,1)}, bf16[512,1024]{1,0:T(8,128)(2,1)S(1)}, bf16[512,1024]{1,0:T(8,128)(2,1)S(1)}, f32[1,2048]{1,0:T(1,128)}, f32[1,1]{1,0:T(1,128)}) custom-call(s32[4]{0:T(128)S(1)} %pad_add_fusion.where, s32[2]{0:T(128)S(1)} %copy-done.3, f32[512,2048]{1,0:T(8,128)S(1)} %get-tuple-element.28.stream, ...), custom_call_target="tpu_custom_call" | custom-call | tf_op jit(solution)/shard_map/residual/pallas_call | solution.py:417
  93.0 3.0 %collective-permute-start.32 = (bf16[512,1024]{1,0:T(8,128)(2,1)S(1)}, bf16[512,1024]{1,0:T(8,128)(2,1)S(1)}, u32[]{:S(2)}, u32[]{:S(2)}) collective-permute-start(bf16[512,1024]{1,0:T(8,128)(2,1)S(1)} %get-tuple-element.40.send), channel_id=1, source_target_pairs={{0,8},{8,0},{16,24},{24,16},{32,40},{40,32},{48,56},{56,48},{64,72... | collective-permute-start | bytes 3145736 | tf_op jit(solution)/shard_map/ppermute | solution.py:44
  96.0 2.3 %collective-permute-done.32.peer_grad = bf16[512,1024]{1,0:T(8,128)(2,1)S(1)} collective-permute-done((bf16[512,1024]{1,0:T(8,128)(2,1)S(1)}, bf16[512,1024]{1,0:T(8,128)(2,1)S(1)}, u32[]{:S(2)}, u32[]{:S(2)}) %collective-permute-start.32) | collective-permute-done | bytes 1048608 | tf_op jit(solution)/shard_map/ppermute | solution.py:44
  98.2 1.9 %blocks_sent.1 = (bf16[512,512]{1,0:T(8,128)(2,1)S(1)}, bf16[512,512]{1,0:T(8,128)(2,1)S(1)}) custom-call(s32[4]{0:T(128)S(1)} %pad_add_fusion.where, bf16[512,1024]{1,0:T(8,128)(2,1)S(1)} %copy-done, bf16[512,1024]{1,0:T(8,128)(2,1)S(1)} %collective-permute-done.31.peer_context, bf16[512,1024]{1,0:T(8,128)(2,1)S(1)} %get-tuple-element.39.own_grad.keep, ...), custom_call_target="tpu_custom_call" | custom-call | tf_op jit(solution)/shard_map/blocks_sent/pallas_call | solution.py:444
  100.1 1.0 collective-permute-start.33
  101.1 1.7 %collective-permute-start.39 = (bf16[512,512]{1,0:T(8,128)(2,1)S(1)}, bf16[512,512]{1,0:T(8,128)(2,1)S(1)}, u32[]{:S(2)}, u32[]{:S(2)}) collective-permute-start(bf16[512,512]{1,0:T(8,128)(2,1)S(1)} %get-tuple-element.47), channel_id=1, source_target_pairs={{0,68},{8,76},{16,84},{24,92},{32,100},{40,108},{48,116},{56,124},... | collective-permute-start | bytes 1572872 | tf_op jit(solution)/shard_map/ppermute | solution.py:44
  102.8 5.1 %context.3 = bf16[512,1024]{1,0:T(8,128)(2,1)} custom-call(s32[4]{0:T(128)S(1)} %pad_add_fusion.where, bf16[512,1024]{1,0:T(8,128)(2,1)S(1)} %get-tuple-element.39.own_grad.keep, bf16[512,1024]{1,0:T(8,128)(2,1)S(1)} %get-tuple-element.40.send, bf16[512,512]{1,0:T(8,128)(2,1)S(1)} %pad_maximum_fusion.refs_0_, ...), custom_call_target="tpu_custom_call" | custom-call | tf_op jit(solution)/shard_map/context/pallas_call | solution.py:432
  108.0 1.8 %blocks_kept.1 = (f32[512,512]{1,0:T(8,128)S(1)}, f32[512,512]{1,0:T(8,128)S(1)}) custom-call(s32[4]{0:T(128)S(1)} %pad_add_fusion.where, bf16[512,1024]{1,0:T(8,128)(2,1)S(1)} %copy-done, bf16[512,1024]{1,0:T(8,128)(2,1)S(1)} %collective-permute-done.31.peer_context, bf16[512,1024]{1,0:T(8,128)(2,1)S(1)} %get-tuple-element.39.own_grad.keep, ...), custom_call_target="tpu_custom_call" | custom-call | tf_op jit(solution)/shard_map/blocks_kept/pallas_call | solution.py:444
  109.8 4.7 %collective-permute-done.33 = bf16[512,512]{1,0:T(8,128)(2,1)S(1)} collective-permute-done((bf16[512,512]{1,0:T(8,128)(2,1)S(1)}, bf16[512,512]{1,0:T(8,128)(2,1)S(1)}, u32[]{:S(2)}, u32[]{:S(2)}) %collective-permute-start.33) | collective-permute-done | bytes 524320 | tf_op jit(solution)/shard_map/ppermute | solution.py:44
  115.4 1.8 %collective-permute-start.40 = (bf16[256,512]{1,0:T(8,128)(2,1)S(1)}, bf16[256,512]{1,0:T(8,128)(2,1)S(1)}, u32[]{:S(2)}, u32[]{:S(2)}) collective-permute-start(bf16[256,512]{1,0:T(8,128)(2,1)S(1)} %slice.104), channel_id=1, source_target_pairs={{0,3},{8,11},{16,19},{24,27},{32,35},{40,43},{48,51},{56,59},{64,6... | collective-permute-start | bytes 786440 | tf_op jit(solution)/shard_map/ppermute | solution.py:44
  117.2 4.2 %collective-permute-done.34 = bf16[256,512]{1,0:T(8,128)(2,1)S(1)} collective-permute-done((bf16[256,512]{1,0:T(8,128)(2,1)S(1)}, bf16[256,512]{1,0:T(8,128)(2,1)S(1)}, u32[]{:S(2)}, u32[]{:S(2)}) %collective-permute-start.34) | collective-permute-done | bytes 262176 | tf_op jit(solution)/shard_map/ppermute | solution.py:44
  121.5 1.8 %collective-permute-start.35 = (bf16[128,512]{1,0:T(8,128)(2,1)S(1)}, bf16[128,512]{1,0:T(8,128)(2,1)S(1)}, u32[]{:S(2)}, u32[]{:S(2)}) collective-permute-start(bf16[128,512]{1,0:T(8,128)(2,1)S(1)} %slice.107), channel_id=1, source_target_pairs={{0,68},{8,76},{16,84},{24,92},{32,100},{40,108},{48,116},{56,124},... | collective-permute-start | bytes 393224 | tf_op jit(solution)/shard_map/ppermute | solution.py:44
  124.1 2.6 %collective-permute-done.35 = bf16[128,512]{1,0:T(8,128)(2,1)S(1)} collective-permute-done((bf16[128,512]{1,0:T(8,128)(2,1)S(1)}, bf16[128,512]{1,0:T(8,128)(2,1)S(1)}, u32[]{:S(2)}, u32[]{:S(2)}) %collective-permute-start.35) | collective-permute-done | bytes 131104 | tf_op jit(solution)/shard_map/ppermute | solution.py:44
  126.8 0.8 collective-permute-done.41
  127.6 0.9 collective-permute-start.42
  128.5 2.2 %collective-permute-done.36 = bf16[128,512]{1,0:T(8,128)(2,1)S(1)} collective-permute-done((bf16[128,512]{1,0:T(8,128)(2,1)S(1)}, bf16[128,512]{1,0:T(8,128)(2,1)S(1)}, u32[]{:S(2)}, u32[]{:S(2)}) %collective-permute-start.36) | collective-permute-done | bytes 131104 | tf_op jit(solution)/shard_map/ppermute | solution.py:44
  130.8 0.9 collective-permute-start.37
  131.8 1.1 collective-permute-start.43
  132.9 2.7 %collective-permute-done.37 = bf16[128,512]{1,0:T(8,128)(2,1)S(1)} collective-permute-done((bf16[128,512]{1,0:T(8,128)(2,1)S(1)}, bf16[128,512]{1,0:T(8,128)(2,1)S(1)}, u32[]{:S(2)}, u32[]{:S(2)}) %collective-permute-start.37) | collective-permute-done | bytes 131104 | tf_op jit(solution)/shard_map/ppermute | solution.py:44
  135.7 1.3 collective-permute-start.38
  137.5 3.2 %collective-permute-done.38 = bf16[128,512]{1,0:T(8,128)(2,1)S(1)} collective-permute-done((bf16[128,512]{1,0:T(8,128)(2,1)S(1)}, bf16[128,512]{1,0:T(8,128)(2,1)S(1)}, u32[]{:S(2)}, u32[]{:S(2)}) %collective-permute-start.38) | collective-permute-done | bytes 131104 | tf_op jit(solution)/shard_map/ppermute | solution.py:44
  141.1 7.4 %collective-permute-start.45 = (bf16[128,1024]{1,0:T(8,128)(2,1)S(1)}, bf16[128,1024]{1,0:T(8,128)(2,1)S(1)}, u32[]{:S(2)}, u32[]{:S(2)}) collective-permute-start(bf16[128,1024]{1,0:T(8,128)(2,1)S(1)} %pad_maximum_fusion.1), channel_id=1, source_target_pairs={{0,8},{8,0},{16,24},{24,16},{32,40},{40,32},{48,56},{56,48},{64,72... | collective-permute-start | bytes 786440 | tf_op jit(solution)/shard_map/ppermute | solution.py:44
  148.4 1.2 collective-permute-done.45
  149.6 0.9 maximum_select_fusion
  (80 shorter events, 9.6 us)
Async XLA Ops:
  0.6 38.3 %copy-start = (bf16[512,1024]{1,0:T(8,128)(2,1)S(1)}, bf16[512,1024]{1,0:T(8,128)(2,1)}, u32[]{:S(2)}) copy-start(bf16[512,1024]{1,0:T(8,128)(2,1)} %own_context.3) | copy-start | bytes 3145732
  0.6 38.3 %copy-start.3 = (s32[2]{0:T(128)S(1)}, s32[2]{0:T(128)}, u32[]{:S(2)}) copy-start(s32[2]{0:T(128)} %lengths.3) | copy-start | bytes 28
  0.7 38.3 %copy-start.4 = (s32[2]{0:T(128)S(1)}, s32[2]{0:T(128)}, u32[]{:S(2)}) copy-start(s32[2]{0:T(128)} %ids.1) | copy-start | bytes 28
  0.7 38.3 %copy-start.2 = (f32[2048]{0:T(1024)S(1)}, f32[2048]{0:T(1024)}, u32[]{:S(2)}) copy-start(f32[2048]{0:T(1024)} %param.12) | copy-start | bytes 24580
  1.8 11.5 %collective-permute-start.2 = (bf16[128,512]{1,0:T(8,128)(2,1)S(1)}, bf16[128,512]{1,0:T(8,128)(2,1)S(1)}, u32[]{:S(2)}, u32[]{:S(2)}) collective-permute-start(bf16[128,512]{1,0:T(8,128)(2,1)S(1)} %get-tuple-element.52), channel_id=1, source_target_pairs={{0,2},{8,10},{16,18},{24,26},{32,34},{40,42},{48,50},{56,58},{64,6... | collective-permute-start | bytes 393224 | tf_op jit(solution)/shard_map/ppermute | solution.py:44
  5.4 7.8 %collective-permute-start.1 = (bf16[128,512]{1,0:T(8,128)(2,1)S(1)}, bf16[128,512]{1,0:T(8,128)(2,1)S(1)}, u32[]{:S(2)}, u32[]{:S(2)}) collective-permute-start(bf16[128,512]{1,0:T(8,128)(2,1)S(1)} %get-tuple-element.52), channel_id=1, source_target_pairs={{0,3},{8,11},{16,19},{24,27},{32,35},{40,43},{48,51},{56,59},{64,6... | collective-permute-start | bytes 393224 | tf_op jit(solution)/shard_map/ppermute | solution.py:44
  6.3 7.0 %collective-permute-start = (bf16[128,512]{1,0:T(8,128)(2,1)S(1)}, bf16[128,512]{1,0:T(8,128)(2,1)S(1)}, u32[]{:S(2)}, u32[]{:S(2)}) collective-permute-start(bf16[128,512]{1,0:T(8,128)(2,1)S(1)} %get-tuple-element.52), channel_id=1, source_target_pairs={{0,1},{8,9},{16,17},{24,25},{32,33},{40,41},{48,49},{56,57},{64,65... | collective-permute-start | bytes 393224 | tf_op jit(solution)/shard_map/ppermute | solution.py:44
  9.1 6.1 %collective-permute-start.4 = (bf16[160,512]{1,0:T(8,128)(2,1)S(1)}, bf16[160,512]{1,0:T(8,128)(2,1)S(1)}, u32[]{:S(2)}, u32[]{:S(2)}) collective-permute-start(bf16[160,512]{1,0:T(8,128)(2,1)S(1)} %get-tuple-element.53), channel_id=1, source_target_pairs={{0,68},{8,76},{16,84},{24,92},{32,100},{40,108},{48,116},{56,124},... | collective-permute-start | bytes 491528 | tf_op jit(solution)/shard_map/ppermute | solution.py:44
  13.3 13.3 %collective-permute-start.3 = (bf16[512,512]{1,0:T(8,128)(2,1)S(1)}, bf16[512,512]{1,0:T(8,128)(2,1)}, u32[]{:S(2)}, u32[]{:S(2)}) collective-permute-start(bf16[512,512]{1,0:T(8,128)(2,1)S(1)} %pad_maximum_fusion.refs_0_), channel_id=1, source_target_pairs={{0,68},{8,76},{16,84},{24,92},{32,100},{40,108},{48,116},{56,124},... | collective-permute-start | bytes 1572872 | tf_op jit(solution)/shard_map/ppermute | solution.py:44
  15.2 6.2 %collective-permute-start.10 = (bf16[320,512]{1,0:T(8,128)(2,1)S(1)}, bf16[320,512]{1,0:T(8,128)(2,1)S(1)}, u32[]{:S(2)}, u32[]{:S(2)}) collective-permute-start(bf16[320,512]{1,0:T(8,128)(2,1)S(1)} %constant_dynamic-update-slice_fusion.4.refs_2_.refs_0_), channel_id=1, source_target_pairs={{0,8},{8,0},{16,24},{24,16},{32,40},{40,32},{48,56},{56,48},{64,72... | collective-permute-start | bytes 983048 | tf_op jit(solution)/shard_map/ppermute | solution.py:44
  17.2 12.2 %collective-permute-start.7 = (bf16[320,512]{1,0:T(8,128)(2,1)S(1)}, bf16[320,512]{1,0:T(8,128)(2,1)S(1)}, u32[]{:S(2)}, u32[]{:S(2)}) collective-permute-start(bf16[320,512]{1,0:T(8,128)(2,1)S(1)} %constant_dynamic-update-slice_fusion.4.refs_2_.refs_0_), channel_id=1, source_target_pairs={{0,2},{8,10},{16,18},{24,26},{32,34},{40,42},{48,50},{56,58},{64,6... | collective-permute-start | bytes 983048 | tf_op jit(solution)/shard_map/ppermute | solution.py:44
  21.4 15.2 %collective-permute-start.6 = (bf16[320,512]{1,0:T(8,128)(2,1)S(1)}, bf16[320,512]{1,0:T(8,128)(2,1)S(1)}, u32[]{:S(2)}, u32[]{:S(2)}) collective-permute-start(bf16[320,512]{1,0:T(8,128)(2,1)S(1)} %constant_dynamic-update-slice_fusion.4.refs_2_.refs_0_), channel_id=1, source_target_pairs={{0,3},{8,11},{16,19},{24,27},{32,35},{40,43},{48,51},{56,59},{64,6... | collective-permute-start | bytes 983048 | tf_op jit(solution)/shard_map/ppermute | solution.py:44
  21.4 15.7 %collective-permute-start.5 = (bf16[320,512]{1,0:T(8,128)(2,1)S(1)}, bf16[320,512]{1,0:T(8,128)(2,1)S(1)}, u32[]{:S(2)}, u32[]{:S(2)}) collective-permute-start(bf16[320,512]{1,0:T(8,128)(2,1)S(1)} %constant_dynamic-update-slice_fusion.4.refs_2_.refs_0_), channel_id=1, source_target_pairs={{0,1},{8,9},{16,17},{24,25},{32,33},{40,41},{48,49},{56,57},{64,65... | collective-permute-start | bytes 983048 | tf_op jit(solution)/shard_map/ppermute | solution.py:44
  21.4 15.8 %collective-permute-start.8 = (bf16[512,512]{1,0:T(8,128)(2,1)S(1)}, bf16[512,512]{1,0:T(8,128)(2,1)}, u32[]{:S(2)}, u32[]{:S(2)}) collective-permute-start(bf16[512,512]{1,0:T(8,128)(2,1)S(1)} %pad_maximum_fusion.refs_0_), channel_id=1, source_target_pairs={{0,8},{8,0},{16,24},{24,16},{32,40},{40,32},{48,56},{56,48},{64,72... | collective-permute-start | bytes 1572872 | tf_op jit(solution)/shard_map/ppermute | solution.py:44
  26.6 12.3 %collective-permute-start.9 = (bf16[512,512]{1,0:T(8,128)(2,1)}, bf16[512,512]{1,0:T(8,128)(2,1)}, u32[]{:S(2)}, u32[]{:S(2)}) collective-permute-start(bf16[512,512]{1,0:T(8,128)(2,1)} %collective-permute-done.3.refs_1_), channel_id=1, source_target_pairs={{0,8},{8,0},{16,24},{24,16},{32,40},{40,32},{48,56},{56,48},{64,72... | collective-permute-start | bytes 1572872 | tf_op jit(solution)/shard_map/ppermute | solution.py:44
  29.4 7.8 %collective-permute-start.13 = (bf16[320,512]{1,0:T(8,128)(2,1)S(1)}, bf16[320,512]{1,0:T(8,128)(2,1)S(1)}, u32[]{:S(2)}, u32[]{:S(2)}) collective-permute-start(bf16[320,512]{1,0:T(8,128)(2,1)S(1)} %collective-permute-done.7.refs_5_.refs_3_), channel_id=1, source_target_pairs={{0,8},{8,0},{16,24},{24,16},{32,40},{40,32},{48,56},{56,48},{64,72... | collective-permute-start | bytes 983048 | tf_op jit(solution)/shard_map/ppermute | solution.py:44
  36.6 1.9 %collective-permute-start.12 = (bf16[320,512]{1,0:T(8,128)(2,1)S(1)}, bf16[320,512]{1,0:T(8,128)(2,1)}, u32[]{:S(2)}, u32[]{:S(2)}) collective-permute-start(bf16[320,512]{1,0:T(8,128)(2,1)S(1)} %collective-permute-done.6.refs_4_.refs_2_), channel_id=1, source_target_pairs={{0,8},{8,0},{16,24},{24,16},{32,40},{40,32},{48,56},{56,48},{64,72... | collective-permute-start | bytes 983048 | tf_op jit(solution)/shard_map/ppermute | solution.py:44
  37.1 1.9 %collective-permute-start.11 = (bf16[320,512]{1,0:T(8,128)(2,1)S(1)}, bf16[320,512]{1,0:T(8,128)(2,1)}, u32[]{:S(2)}, u32[]{:S(2)}) collective-permute-start(bf16[320,512]{1,0:T(8,128)(2,1)S(1)} %collective-permute-done.5.refs_3_.refs_1_), channel_id=1, source_target_pairs={{0,8},{8,0},{16,24},{24,16},{32,40},{40,32},{48,56},{56,48},{64,72... | collective-permute-start | bytes 983048 | tf_op jit(solution)/shard_map/ppermute | solution.py:44
  38.9 1.6 %copy-start.1 = (bf16[512,2048]{1,0:T(8,128)(2,1)S(1)}, bf16[512,2048]{1,0:T(8,128)(2,1)}, u32[]{:S(2)}) copy-start(bf16[512,2048]{1,0:T(8,128)(2,1)} %residual.2) | copy-start | bytes 6291460
  40.5 0.7 copy-start.5
  41.2 0.7 copy-start.6
  47.2 4.1 %collective-permute-start.16 = (bf16[2,2176]{1,0:T(2,128)(2,1)S(1)}, bf16[2,2176]{1,0:T(2,128)(2,1)S(1)}, u32[]{:S(2)}, u32[]{:S(2)}) collective-permute-start(bf16[2,2176]{1,0:T(2,128)(2,1)S(1)} %get-tuple-element.31), channel_id=1, source_target_pairs={{0,2},{8,10},{16,18},{24,26},{32,34},{40,42},{48,50},{56,58},{64,6... | collective-permute-start | bytes 26120 | tf_op jit(solution)/shard_map/ppermute | solution.py:44
  48.8 3.7 %collective-permute-start.15 = (bf16[2,2176]{1,0:T(2,128)(2,1)S(1)}, bf16[2,2176]{1,0:T(2,128)(2,1)S(1)}, u32[]{:S(2)}, u32[]{:S(2)}) collective-permute-start(bf16[2,2176]{1,0:T(2,128)(2,1)S(1)} %get-tuple-element.31), channel_id=1, source_target_pairs={{0,3},{8,11},{16,19},{24,27},{32,35},{40,43},{48,51},{56,59},{64,6... | collective-permute-start | bytes 26120 | tf_op jit(solution)/shard_map/ppermute | solution.py:44
  50.8 2.8 %collective-permute-start.14 = (bf16[2,2176]{1,0:T(2,128)(2,1)S(1)}, bf16[2,2176]{1,0:T(2,128)(2,1)S(1)}, u32[]{:S(2)}, u32[]{:S(2)}) collective-permute-start(bf16[2,2176]{1,0:T(2,128)(2,1)S(1)} %get-tuple-element.31), channel_id=1, source_target_pairs={{0,1},{8,9},{16,17},{24,25},{32,33},{40,41},{48,49},{56,57},{64,65... | collective-permute-start | bytes 26120 | tf_op jit(solution)/shard_map/ppermute | solution.py:44
  53.6 4.4 %collective-permute-start.19 = (bf16[8,2176]{1,0:T(8,128)(2,1)S(1)}, bf16[8,2176]{1,0:T(8,128)(2,1)S(1)}, u32[]{:S(2)}, u32[]{:S(2)}) collective-permute-start(bf16[8,2176]{1,0:T(8,128)(2,1)S(1)} %pad_maximum_fusion.3), channel_id=1, source_target_pairs={{0,4},{8,12},{16,20},{24,28},{32,36},{40,44},{48,52},{56,60},{64,6... | collective-permute-start | bytes 104456 | tf_op jit(solution)/shard_map/ppermute | solution.py:44
  56.1 4.5 %collective-permute-start.18 = (bf16[8,2176]{1,0:T(8,128)(2,1)S(1)}, bf16[8,2176]{1,0:T(8,128)(2,1)S(1)}, u32[]{:S(2)}, u32[]{:S(2)}) collective-permute-start(bf16[8,2176]{1,0:T(8,128)(2,1)S(1)} %pad_maximum_fusion.3), channel_id=1, source_target_pairs={{0,68},{8,76},{16,84},{24,92},{32,100},{40,108},{48,116},{56,124},... | collective-permute-start | bytes 104456 | tf_op jit(solution)/shard_map/ppermute | solution.py:44
  57.2 3.3 %collective-permute-start.17 = (bf16[8,2176]{1,0:T(8,128)(2,1)S(1)}, bf16[8,2176]{1,0:T(8,128)(2,1)S(1)}, u32[]{:S(2)}, u32[]{:S(2)}) collective-permute-start(bf16[8,2176]{1,0:T(8,128)(2,1)S(1)} %pad_maximum_fusion.3), channel_id=1, source_target_pairs={{0,64},{8,72},{16,80},{24,88},{32,96},{40,104},{48,112},{56,120},{... | collective-permute-start | bytes 104456 | tf_op jit(solution)/shard_map/ppermute | solution.py:44
  60.6 7.7 %collective-permute-start.22 = (bf16[32,2176]{1,0:T(8,128)(2,1)S(1)}, bf16[32,2176]{1,0:T(8,128)(2,1)S(1)}, u32[]{:S(2)}, u32[]{:S(2)}) collective-permute-start(bf16[32,2176]{1,0:T(8,128)(2,1)S(1)} %pad_maximum_fusion.2.refs_8_), channel_id=1, source_target_pairs={{0,32},{8,40},{16,48},{24,56},{32,0},{40,8},{48,16},{56,24},{64,96... | collective-permute-start | bytes 417800 | tf_op jit(solution)/shard_map/ppermute | solution.py:44
  64.2 6.7 %collective-permute-start.21 = (bf16[32,2176]{1,0:T(8,128)(2,1)S(1)}, bf16[32,2176]{1,0:T(8,128)(2,1)S(1)}, u32[]{:S(2)}, u32[]{:S(2)}) collective-permute-start(bf16[32,2176]{1,0:T(8,128)(2,1)S(1)} %pad_maximum_fusion.2.refs_8_), channel_id=1, source_target_pairs={{0,48},{8,56},{16,32},{24,40},{32,16},{40,24},{48,0},{56,8},{64,11... | collective-permute-start | bytes 417800 | tf_op jit(solution)/shard_map/ppermute | solution.py:44
  64.7 8.9 %collective-permute-start.20 = (bf16[32,2176]{1,0:T(8,128)(2,1)S(1)}, bf16[32,2176]{1,0:T(8,128)(2,1)S(1)}, u32[]{:S(2)}, u32[]{:S(2)}) collective-permute-start(bf16[32,2176]{1,0:T(8,128)(2,1)S(1)} %pad_maximum_fusion.2.refs_8_), channel_id=1, source_target_pairs={{0,16},{8,24},{16,0},{24,8},{32,48},{40,56},{48,32},{56,40},{64,80... | collective-permute-start | bytes 417800 | tf_op jit(solution)/shard_map/ppermute | solution.py:44
  65.0 8.6 %collective-permute-start.23 = (bf16[32,2176]{1,0:T(8,128)(2,1)S(1)}, bf16[32,2176]{1,0:T(8,128)(2,1)S(1)}, u32[]{:S(2)}, u32[]{:S(2)}) collective-permute-start(bf16[32,2176]{1,0:T(8,128)(2,1)S(1)} %pad_maximum_fusion.2.refs_8_), channel_id=1, source_target_pairs={{0,8},{8,0},{16,24},{24,16},{32,40},{40,32},{48,56},{56,48},{64,72... | collective-permute-start | bytes 417800 | tf_op jit(solution)/shard_map/ppermute | solution.py:44
  68.3 5.3 %collective-permute-start.26 = (bf16[32,2176]{1,0:T(8,128)(2,1)S(1)}, bf16[32,2176]{1,0:T(8,128)(2,1)S(1)}, u32[]{:S(2)}, u32[]{:S(2)}) collective-permute-start(bf16[32,2176]{1,0:T(8,128)(2,1)S(1)} %collective-permute-done.22.refs_11_), channel_id=1, source_target_pairs={{0,8},{8,0},{16,24},{24,16},{32,40},{40,32},{48,56},{56,48},{64,72... | collective-permute-start | bytes 417800 | tf_op jit(solution)/shard_map/ppermute | solution.py:44
  70.9 3.6 %collective-permute-start.25 = (bf16[32,2176]{1,0:T(8,128)(2,1)S(1)}, bf16[32,2176]{1,0:T(8,128)(2,1)S(1)}, u32[]{:S(2)}, u32[]{:S(2)}) collective-permute-start(bf16[32,2176]{1,0:T(8,128)(2,1)S(1)} %collective-permute-done.21.refs_10_), channel_id=1, source_target_pairs={{0,8},{8,0},{16,24},{24,16},{32,40},{40,32},{48,56},{56,48},{64,72... | collective-permute-start | bytes 417800 | tf_op jit(solution)/shard_map/ppermute | solution.py:44
  73.6 1.4 collective-permute-start.24
  80.3 3.6 %collective-permute-start.27 = (f32[8,2048]{1,0:T(8,128)S(1)}, f32[8,2048]{1,0:T(8,128)S(1)}, u32[]{:S(2)}, u32[]{:S(2)}) collective-permute-start(f32[8,2048]{1,0:T(8,128)S(1)} %get-tuple-element.33), channel_id=1, source_target_pairs={{0,16},{8,24},{16,0},{24,8},{32,48},{40,56},{48,32},{56,40},{64,80... | collective-permute-start | bytes 196616 | tf_op jit(solution)/shard_map/ppermute | solution.py:44
  80.5 4.3 %collective-permute-start.28 = (f32[8,2048]{1,0:T(8,128)S(1)}, f32[8,2048]{1,0:T(8,128)S(1)}, u32[]{:S(2)}, u32[]{:S(2)}) collective-permute-start(f32[8,2048]{1,0:T(8,128)S(1)} %get-tuple-element.34), channel_id=1, source_target_pairs={{0,48},{8,56},{16,32},{24,40},{32,16},{40,24},{48,0},{56,8},{64,11... | collective-permute-start | bytes 196616 | tf_op jit(solution)/shard_map/ppermute | solution.py:44
  82.1 4.6 %collective-permute-start.29 = (f32[8,2048]{1,0:T(8,128)S(1)}, f32[8,2048]{1,0:T(8,128)S(1)}, u32[]{:S(2)}, u32[]{:S(2)}) collective-permute-start(f32[8,2048]{1,0:T(8,128)S(1)} %get-tuple-element.35), channel_id=1, source_target_pairs={{0,32},{8,40},{16,48},{24,56},{32,0},{40,8},{48,16},{56,24},{64,96... | collective-permute-start | bytes 196616 | tf_op jit(solution)/shard_map/ppermute | solution.py:44
  86.7 3.2 %collective-permute-start.30 = (f32[8,2048]{1,0:T(8,128)S(1)}, f32[8,2048]{1,0:T(8,128)S(1)}, u32[]{:S(2)}, u32[]{:S(2)}) collective-permute-start(f32[8,2048]{1,0:T(8,128)S(1)} %add_add_fusion.refs_0_), channel_id=1, source_target_pairs={{0,64},{8,72},{16,80},{24,88},{32,96},{40,104},{48,112},{56,120},{... | collective-permute-start | bytes 196616 | tf_op jit(solution)/shard_map/ppermute | solution.py:44
  87.2 8.7 %collective-permute-start.31 = (bf16[512,1024]{1,0:T(8,128)(2,1)S(1)}, bf16[512,1024]{1,0:T(8,128)(2,1)S(1)}, u32[]{:S(2)}, u32[]{:S(2)}) collective-permute-start(bf16[512,1024]{1,0:T(8,128)(2,1)S(1)} %copy-done), channel_id=1, source_target_pairs={{0,8},{8,0},{16,24},{24,16},{32,40},{40,32},{48,56},{56,48},{64,72... | collective-permute-start | bytes 3145736 | tf_op jit(solution)/shard_map/ppermute | solution.py:44
  93.0 5.3 %collective-permute-start.32 = (bf16[512,1024]{1,0:T(8,128)(2,1)S(1)}, bf16[512,1024]{1,0:T(8,128)(2,1)S(1)}, u32[]{:S(2)}, u32[]{:S(2)}) collective-permute-start(bf16[512,1024]{1,0:T(8,128)(2,1)S(1)} %get-tuple-element.40.send), channel_id=1, source_target_pairs={{0,8},{8,0},{16,24},{24,16},{32,40},{40,32},{48,56},{56,48},{64,72... | collective-permute-start | bytes 3145736 | tf_op jit(solution)/shard_map/ppermute | solution.py:44
  100.1 14.4 %collective-permute-start.33 = (bf16[512,512]{1,0:T(8,128)(2,1)S(1)}, bf16[512,512]{1,0:T(8,128)(2,1)S(1)}, u32[]{:S(2)}, u32[]{:S(2)}) collective-permute-start(bf16[512,512]{1,0:T(8,128)(2,1)S(1)} %get-tuple-element.45), channel_id=1, source_target_pairs={{0,3},{8,11},{16,19},{24,27},{32,35},{40,43},{48,51},{56,59},{64,6... | collective-permute-start | bytes 1572872 | tf_op jit(solution)/shard_map/ppermute | solution.py:44
  101.1 14.0 %collective-permute-start.39 = (bf16[512,512]{1,0:T(8,128)(2,1)S(1)}, bf16[512,512]{1,0:T(8,128)(2,1)S(1)}, u32[]{:S(2)}, u32[]{:S(2)}) collective-permute-start(bf16[512,512]{1,0:T(8,128)(2,1)S(1)} %get-tuple-element.47), channel_id=1, source_target_pairs={{0,68},{8,76},{16,84},{24,92},{32,100},{40,108},{48,116},{56,124},... | collective-permute-start | bytes 1572872 | tf_op jit(solution)/shard_map/ppermute | solution.py:44
  114.7 6.7 %collective-permute-start.34 = (bf16[256,512]{1,0:T(8,128)(2,1)S(1)}, bf16[256,512]{1,0:T(8,128)(2,1)S(1)}, u32[]{:S(2)}, u32[]{:S(2)}) collective-permute-start(bf16[256,512]{1,0:T(8,128)(2,1)S(1)} %slice.105), channel_id=1, source_target_pairs={{0,1},{8,9},{16,17},{24,25},{32,33},{40,41},{48,49},{56,57},{64,65... | collective-permute-start | bytes 786440 | tf_op jit(solution)/shard_map/ppermute | solution.py:44
  115.4 8.0 %collective-permute-start.40 = (bf16[256,512]{1,0:T(8,128)(2,1)S(1)}, bf16[256,512]{1,0:T(8,128)(2,1)S(1)}, u32[]{:S(2)}, u32[]{:S(2)}) collective-permute-start(bf16[256,512]{1,0:T(8,128)(2,1)S(1)} %slice.104), channel_id=1, source_target_pairs={{0,3},{8,11},{16,19},{24,27},{32,35},{40,43},{48,51},{56,59},{64,6... | collective-permute-start | bytes 786440 | tf_op jit(solution)/shard_map/ppermute | solution.py:44
  121.5 5.1 %collective-permute-start.35 = (bf16[128,512]{1,0:T(8,128)(2,1)S(1)}, bf16[128,512]{1,0:T(8,128)(2,1)S(1)}, u32[]{:S(2)}, u32[]{:S(2)}) collective-permute-start(bf16[128,512]{1,0:T(8,128)(2,1)S(1)} %slice.107), channel_id=1, source_target_pairs={{0,68},{8,76},{16,84},{24,92},{32,100},{40,108},{48,116},{56,124},... | collective-permute-start | bytes 393224 | tf_op jit(solution)/shard_map/ppermute | solution.py:44
  123.5 4.1 %collective-permute-start.41 = (bf16[128,512]{1,0:T(8,128)(2,1)S(1)}, bf16[128,512]{1,0:T(8,128)(2,1)S(1)}, u32[]{:S(2)}, u32[]{:S(2)}) collective-permute-start(bf16[128,512]{1,0:T(8,128)(2,1)S(1)} %slice.106), channel_id=1, source_target_pairs={{0,1},{8,9},{16,17},{24,25},{32,33},{40,41},{48,49},{56,57},{64,65... | collective-permute-start | bytes 393224 | tf_op jit(solution)/shard_map/ppermute | solution.py:44
  126.7 4.1 %collective-permute-start.36 = (bf16[128,512]{1,0:T(8,128)(2,1)S(1)}, bf16[128,512]{1,0:T(8,128)(2,1)S(1)}, u32[]{:S(2)}, u32[]{:S(2)}) collective-permute-start(bf16[128,512]{1,0:T(8,128)(2,1)S(1)} %fusion.6), channel_id=1, source_target_pairs={{0,64},{8,72},{16,80},{24,88},{32,96},{40,104},{48,112},{56,120},{... | collective-permute-start | bytes 393224 | tf_op jit(solution)/shard_map/ppermute | solution.py:44
  127.6 4.1 %collective-permute-start.42 = (bf16[128,512]{1,0:T(8,128)(2,1)S(1)}, bf16[128,512]{1,0:T(8,128)(2,1)S(1)}, u32[]{:S(2)}, u32[]{:S(2)}) collective-permute-start(bf16[128,512]{1,0:T(8,128)(2,1)S(1)} %fusion.7), channel_id=1, source_target_pairs={{0,16},{8,24},{16,0},{24,8},{32,48},{40,56},{48,32},{56,40},{64,80... | collective-permute-start | bytes 393224 | tf_op jit(solution)/shard_map/ppermute | solution.py:44
  130.8 4.8 %collective-permute-start.37 = (bf16[128,512]{1,0:T(8,128)(2,1)S(1)}, bf16[128,512]{1,0:T(8,128)(2,1)S(1)}, u32[]{:S(2)}, u32[]{:S(2)}) collective-permute-start(bf16[128,512]{1,0:T(8,128)(2,1)S(1)} %fusion.2), channel_id=1, source_target_pairs={{0,16},{8,24},{16,0},{24,8},{32,48},{40,56},{48,32},{56,40},{64,80... | collective-permute-start | bytes 393224 | tf_op jit(solution)/shard_map/ppermute | solution.py:44
  131.8 5.2 %collective-permute-start.43 = (bf16[128,512]{1,0:T(8,128)(2,1)S(1)}, bf16[128,512]{1,0:T(8,128)(2,1)S(1)}, u32[]{:S(2)}, u32[]{:S(2)}) collective-permute-start(bf16[128,512]{1,0:T(8,128)(2,1)S(1)} %fusion.3), channel_id=1, source_target_pairs={{0,48},{8,56},{16,32},{24,40},{32,16},{40,24},{48,0},{56,8},{64,11... | collective-permute-start | bytes 393224 | tf_op jit(solution)/shard_map/ppermute | solution.py:44
  135.7 5.1 %collective-permute-start.38 = (bf16[128,512]{1,0:T(8,128)(2,1)S(1)}, bf16[128,512]{1,0:T(8,128)(2,1)S(1)}, u32[]{:S(2)}, u32[]{:S(2)}) collective-permute-start(bf16[128,512]{1,0:T(8,128)(2,1)S(1)} %fusion.4), channel_id=1, source_target_pairs={{0,48},{8,56},{16,32},{24,40},{32,16},{40,24},{48,0},{56,8},{64,11... | collective-permute-start | bytes 393224 | tf_op jit(solution)/shard_map/ppermute | solution.py:44
  137.0 3.9 %collective-permute-start.44 = (bf16[128,512]{1,0:T(8,128)(2,1)S(1)}, bf16[128,512]{1,0:T(8,128)(2,1)S(1)}, u32[]{:S(2)}, u32[]{:S(2)}) collective-permute-start(bf16[128,512]{1,0:T(8,128)(2,1)S(1)} %fusion.5), channel_id=1, source_target_pairs={{0,64},{8,72},{16,80},{24,88},{32,96},{40,104},{48,112},{56,120},{... | collective-permute-start | bytes 393224 | tf_op jit(solution)/shard_map/ppermute | solution.py:44
  141.1 8.5 %collective-permute-start.45 = (bf16[128,1024]{1,0:T(8,128)(2,1)S(1)}, bf16[128,1024]{1,0:T(8,128)(2,1)S(1)}, u32[]{:S(2)}, u32[]{:S(2)}) collective-permute-start(bf16[128,1024]{1,0:T(8,128)(2,1)S(1)} %pad_maximum_fusion.1), channel_id=1, source_target_pairs={{0,8},{8,0},{16,24},{24,16},{32,40},{40,32},{48,56},{56,48},{64,72... | collective-permute-start | bytes 786440 | tf_op jit(solution)/shard_map/ppermute | solution.py:44

commit v5 on v4

--- a/solution.py
+++ b/solution.py
@@ -103,8 +103,19 @@
 
 
 def weight_rows(ref, block):
-    rows = ref.shape[0] // 2
-    return jnp.concatenate([ref[:block, :], ref[rows : rows + block, :]], axis=0)
+    rows = ref.shape[0] // 4
+    return jnp.concatenate([ref[q * rows : q * rows + block, :] for q in range(4)], axis=0)
+
+
+def pack_kernel(weight, users, first, second):
+    rows, width = weight.shape
+    part = width // 4
+    first_at, second_at = column_offsets(lax.axis_index("dp") % 2, width)[0]
+    first[:rows, :] = weight[:, pl.ds(first_at, part)]
+    second[...] = weight[:, pl.ds(second_at, part)]
+    wide = users[...].astype(F32)
+    riding = jnp.concatenate([wide[:, j * part : (j + 1) * part] for j in range(4)], axis=0)
+    first[rows:, :] = riding.astype(BF16)
 
 
 def forward_kernel(where, lengths, ids, counts, positive, context, residual, gain, *refs):
@@ -121,10 +132,10 @@
     by_q = [blocks_of(context, where, [(q, 0), (q, 1)], block) for q in range(4)]
     for side, (first_at, second_at) in enumerate(column_offsets(where[3], width)):
         stream[:, pl.ds(first_at, part)] = sum(
-            dot(by_ry[ry], firsts[side][ry][...]) for ry in range(2)
+            dot(by_ry[ry], weight_rows(firsts[side][ry], block)) for ry in range(2)
         )
         stream[:, pl.ds(second_at, part)] = sum(
-            dot(by_q[q], weight_rows(seconds[side][q], block)) for q in range(4)
+            dot(by_q[q], seconds[side][q][...]) for q in range(4)
         )
     copy.wait()
     for i in range(items):
@@ -162,24 +173,24 @@
 
 
 def loss_kernel(users_here, items_here, block, where, gain, *refs):
-    piece_refs, emb_refs = refs[:8], refs[8:16]
-    sums, user_grad, grads, emb_grads, riders, sems = refs[16:20], *refs[20:]
+    piece_refs, emb_refs = refs[:4], refs[4:12]
+    sums, user_grad, grads, emb_grads, riders, sems = refs[12:16], *refs[16:]
     x, y, z, core = where[0], where[1], where[2], where[3]
     group, full = emb_refs[0].shape
     width = full - LABELS
     items = 8 * group
     people = 16 * users_here
-    half_rows, part = piece_refs[0].shape[0] // 2, piece_refs[0].shape[1]
+    stride, part = piece_refs[0].shape[0] // 4, piece_refs[0].shape[1]
     parts = width // part
     rode = parts * users_here
     copies = []
-    for n in range(8):
-        for ry in range(2):
+    for n in range(4):
+        for q in range(4):
             copies.append(
                 pltpu.make_async_copy(
-                    piece_refs[n].at[pl.ds(ry * half_rows + block, rode)],
-                    riders.at[pl.ds((n * 2 + ry) * rode, rode)],
-                    sems.at[n * 2 + ry],
+                    piece_refs[n].at[pl.ds(q * stride + block, rode)],
+                    riders.at[pl.ds((n * 4 + q) * rode, rode)],
+                    sems.at[n * 4 + q],
                 )
             )
     for copy in copies:
@@ -201,8 +212,8 @@
     to = lax.broadcasted_iota(jnp.int32, (people, 16 * rode), 0)
     of = lax.broadcasted_iota(jnp.int32, (people, 16 * rode), 1)
     one = of // rode
-    holder = ((core ^ bit(one, 3)) * 2 + ((y // 2) ^ bit(one, 0))) * 4 + (
-        x ^ bit(one, 1) ^ (3 * bit(one, 2))
+    holder = ((core ^ bit(one, 3)) * 2 + ((y // 2) ^ bit(one, 2))) * 4 + (
+        x ^ bit(one, 0) ^ (3 * bit(one, 1))
     )
     home = holder * users_here + of % users_here
     column = (of % rode) // users_here
@@ -306,10 +317,11 @@
     near = [ref[:, :part] for ref in (keep, send)]
     far = [ref[:, part:] for ref in (keep, send)]
     from_first = [
-        sum(contract_last(near[s], firsts[s][ry][...]) for s in range(2)) for ry in range(2)
+        sum(contract_last(near[s], weight_rows(firsts[s][ry], block)) for s in range(2))
+        for ry in range(2)
     ]
     for q in range(4):
-        from_second = sum(contract_last(far[s], weight_rows(seconds[s][q], block)) for s in range(2))
+        from_second = sum(contract_last(far[s], seconds[s][q][...]) for s in range(2))
         for ry in range(2):
             value = (
                 from_first[ry][:, q * block : (q + 1) * block]
@@ -319,7 +331,7 @@
             context_grad[:, pl.ds(pl.multiple_of(home * block, block), block)] = value.astype(BF16)
 
 
-def blocks_kernel(half, where, own_context, peer_context, own_grad, peer_grad, first, second):
+def blocks_kernel(kept, where, own_context, peer_context, own_grad, peer_grad, first, *seconds):
     part = own_grad.shape[1] // 2
     block = own_context.shape[1] // 8
 
@@ -328,9 +340,12 @@
             blocks_of(own_context, where, pairs, block), own_grad[:, at : at + part]
         ) + contract_rows(blocks_of(peer_context, where, pairs, block), peer_grad[:, at : at + part])
 
-    pairs = [(q, ry) for q in (2 * half, 2 * half + 1) for ry in range(2)]
-    first[...] = product(pairs, 0).astype(first.dtype)
-    second[...] = product([(q, half) for q in range(4)], part).astype(second.dtype)
+    ry = 0 if kept else 1
+    first[...] = product([(q, ry) for q in range(4)], 0).astype(first.dtype)
+    places = (0,) if kept else (1, 2, 3)
+    value = product([(q, ry) for q in places for ry in range(2)], part)
+    for n, second in enumerate(seconds):
+        second[...] = value[n * 2 * block : (n + 1) * 2 * block].astype(second.dtype)
 
 
 def shaped(shape, dtype=F32):
@@ -367,10 +382,18 @@
     rows = out_weight.shape[0]
     gain = norm_gain[None, :]
 
-    mine = lax.dynamic_slice(out_weight, (0, core * half), (rows, half))
-    riders = [user_vectors[:, j * part : (j + 1) * part] for j in range(width // part)]
-    second = doubled(jnp.concatenate([mine[:, part:]] + riders, axis=0), swap_y, 3)
-    first = lax.optimization_barrier(jnp.concatenate(four(mine[:, :part], swap_x), axis=0))
+    rode = users_here * (width // part)
+    first, second = pl.pallas_call(
+        pack_kernel,
+        out_shape=(shaped((rows + rode, part), BF16), shaped((rows, part), BF16)),
+        in_specs=[VMEM] * 2,
+        out_specs=(VMEM,) * 2,
+        compiler_params=params(6),
+        name="pack",
+    )(out_weight, user_vectors)
+    second = doubled(second, swap_y, 3)
+    first = jnp.concatenate(four(first, swap_x), axis=0)
+    first, second = lax.optimization_barrier((first, second))
     pieces = [first, swap_y(first, 3)] + four(second, swap_x)
     pieces = pieces + [swap_core(p) for p in pieces]
 
@@ -396,11 +419,11 @@
     emb_pieces = emb_pieces + [swap_core(p) for p in emb_pieces]
 
     items, people = 128 * items_here, 16 * users_here
-    riding = pieces[2:6] + pieces[8:12]
+    riding = pieces[0:2] + pieces[6:8]
     *sums, user_grad = pl.pallas_call(
         functools.partial(loss_kernel, users_here, items_here, rows),
         out_shape=(shaped((8, width)),) * 4 + (shaped((users_here, width), BF16),),
-        in_specs=[SMEM, VMEM] + [ANY] * 8 + [VMEM] * 8,
+        in_specs=[SMEM, VMEM] + [ANY] * 4 + [VMEM] * 8,
         out_specs=(VMEM,) * 5,
         scratch_shapes=[
             pltpu.VMEM((people, items), F32),
@@ -440,25 +463,28 @@
 
     operands = (where, context, peer_context, keep, peer_grad)
 
-    def blocks(which, dtype, name):
+    def blocks(kept, dtype, name):
+        counts = 1 if kept else 3
         return pl.pallas_call(
-            functools.partial(blocks_kernel, which),
-            out_shape=(shaped((4 * rows, part), dtype),) * 2,
+            functools.partial(blocks_kernel, kept),
+            out_shape=(shaped((4 * rows, part), dtype),) + (shaped((2 * rows, part), dtype),) * counts,
             in_specs=[SMEM] + [VMEM] * 4,
-            out_specs=(VMEM,) * 2,
-            compiler_params=params(14),
+            out_specs=(VMEM,) * (1 + counts),
+            compiler_params=params(16),
             name=name,
         )(*operands)
 
-    first_sent, second_sent = blocks(1, BF16, "blocks_sent")
-    first, second = blocks(0, F32, "blocks_kept")
+    first_sent, *second_sent = blocks(False, BF16, "blocks_sent")
+    first, second = blocks(True, F32, "blocks_kept")
     first, second, context_grad = lax.optimization_barrier((first, second, context_grad))
-    first = added(first, first_sent, swap_x, 3)
-    second = added(second, second_sent, swap_y, 3)
-    first = folded(first, swap_x, 1)
-    second = folded(second, swap_x, 3)
-    first = folded(first, swap_y, 3)
-    second = folded(second, swap_x, 1)
+    first = added(first, first_sent, swap_y, 3)
+    arrived = [swap_x(first[q * rows : (q + 1) * rows].astype(BF16), OFFSETS[q]) for q in (1, 2, 3)]
+    for q in (1, 2, 3):
+        second = second + swap_x(second_sent[q - 1], OFFSETS[q]).astype(F32)
+    second = folded(second, swap_y, 3)
+    first = first[:rows]
+    for piece in arrived:
+        first = first + piece.astype(F32)
     first = all_added(first, swap_y, 1)
     second = all_added(second, swap_z, 1)
     first = all_added(first, swap_z, 1)

time: 151 us -> 161 us (1.066)
  waiting for transfers between devices: 48.2 us -> 60.5 us
  local copies, waits for them, and re-layouts: 9.01 us -> 4.84 us
    ppermute x46 -> x48, waiting for transfers between devices: 48.2 us -> 60.5 us  [move(): return lax.ppermute(value, AXES, perm)]
    unnamed x21 -> x18, local copies, waits for them, and re-layouts: 8.17 us -> 4.79 us
    ppermute x46 -> x48, starting transfers between devices: 67.7 us -> 69.1 us  [move(): return lax.ppermute(value, AXES, perm)]
    pallas_call x2 -> x3, Pallas kernels: 3.71 us -> 3.75 us  [the longest x2 3.72 us: blocks(): pl.pallas_call(functools.partial(blocks_kernel, kept), out_shape=(shaped(...]
  transfers between devices with their start and end apart: 46 -> 48, of which waited for: 27 -> 28; matrix products, arithmetic and copies ran while one was open for 4% -> 1% of each run, Pallas kernels for 7% -> 6%
where the time goes in v5:
time: 161 us; the launch traced here: 160 us
  starting transfers between devices  69.1 us (43%)
  waiting for transfers between devices  60.5 us (38%)
  Pallas kernels  22.9 us (14%)
  local copies, waits for them, and re-layouts  4.84 us (3%)
  other arithmetic  1.98 us (1%)
    ppermute x48, starting transfers between devices, move(): return lax.ppermute(value, AXES, perm)  69.1 us
    ppermute x48, waiting for transfers between devices, move(): return lax.ppermute(value, AXES, perm)  60.5 us
    pallas_call x1, Pallas kernels, on_device(): pl.pallas_call(functools.partial(loss_kernel, users_here, items_here, row...  5.62 us
    pallas_call x1, Pallas kernels, on_device(): pl.pallas_call(forward_kernel, out_shape=(shaped((tokens, width)), shaped...  5.38 us
    pallas_call x1, Pallas kernels, on_device(): pl.pallas_call(context_kernel, out_shape=shaped((tokens, head), BF16), in...  5.1 us
    unnamed x18, local copies, waits for them, and re-layouts  4.79 us
    pallas_call x2, Pallas kernels, blocks(): pl.pallas_call(functools.partial(blocks_kernel, kept), out_shape=(shaped(...  3.72 us
  transfers between devices with their start and end apart: 48, of which 28 were waited for; matrix products, arithmetic and copies ran while one was open for 1% of the time, Pallas kernels for 6%

profile of v5, /device:TPU:1, one launch (start us, length us, event | category | flops | bytes accessed | tf_op | source)
XLA Modules:
  0.0 160.2 jit_solution(7268387369146821468)
XLA Ops:
  0.7 1.1 copy-done.2
  1.8 0.8 copy-done.4
  2.6 3.6 %collective-permute-start.3 = (bf16[128,512]{1,0:T(8,128)(2,1)S(1)}, bf16[128,512]{1,0:T(8,128)(2,1)S(1)}, u32[]{:S(2)}, u32[]{:S(2)}) collective-permute-start(bf16[128,512]{1,0:T(8,128)(2,1)S(1)} %get-tuple-element.35), channel_id=1, source_target_pairs={{0,68},{8,76},{16,84},{24,92},{32,100},{40,108},{48,116},{56,124},... | collective-permute-start | bytes 393224 | tf_op jit(solution)/shard_map/ppermute | solution.py:44
  6.2 2.7 %collective-permute-start.2 = (bf16[160,512]{1,0:T(8,128)(2,1)S(1)}, bf16[160,512]{1,0:T(8,128)(2,1)S(1)}, u32[]{:S(2)}, u32[]{:S(2)}) collective-permute-start(bf16[160,512]{1,0:T(8,128)(2,1)S(1)} %get-tuple-element.34), channel_id=1, source_target_pairs={{0,2},{8,10},{16,18},{24,26},{32,34},{40,42},{48,50},{56,58},{64,6... | collective-permute-start | bytes 491528 | tf_op jit(solution)/shard_map/ppermute | solution.py:44
  9.0 0.9 collective-permute-start.1
  9.9 2.6 %collective-permute-done.2 = bf16[160,512]{1,0:T(8,128)(2,1)S(1)} collective-permute-done((bf16[160,512]{1,0:T(8,128)(2,1)S(1)}, bf16[160,512]{1,0:T(8,128)(2,1)S(1)}, u32[]{:S(2)}, u32[]{:S(2)}) %collective-permute-start.2) | collective-permute-done | bytes 163872 | tf_op jit(solution)/shard_map/ppermute | solution.py:44
  12.5 4.3 %collective-permute-done.1 = bf16[160,512]{1,0:T(8,128)(2,1)S(1)} collective-permute-done((bf16[160,512]{1,0:T(8,128)(2,1)S(1)}, bf16[160,512]{1,0:T(8,128)(2,1)S(1)}, u32[]{:S(2)}, u32[]{:S(2)}) %collective-permute-start.1) | collective-permute-done | bytes 163872 | tf_op jit(solution)/shard_map/ppermute | solution.py:44
  17.1 1.3 collective-permute-start.10
  18.4 14.7 %collective-permute-done.4.refs_1_ = bf16[640,512]{1,0:T(8,128)(2,1)S(1)} collective-permute-done((bf16[640,512]{1,0:T(8,128)(2,1)S(1)}, bf16[640,512]{1,0:T(8,128)(2,1)S(1)}, u32[]{:S(2)}, u32[]{:S(2)}) %collective-permute-start.4) | collective-permute-done | bytes 655392 | tf_op jit(solution)/shard_map/ppermute | solution.py:44
  33.1 2.1 %collective-permute-start.9 = (bf16[640,512]{1,0:T(8,128)(2,1)S(1)}, bf16[640,512]{1,0:T(8,128)(2,1)}, u32[]{:S(2)}, u32[]{:S(2)}) collective-permute-start(bf16[640,512]{1,0:T(8,128)(2,1)S(1)} %collective-permute-done.4.refs_1_), channel_id=1, source_target_pairs={{0,8},{8,0},{16,24},{24,16},{32,40},{40,32},{48,56},{56,48},{64,72... | collective-permute-start | bytes 1966088 | tf_op jit(solution)/shard_map/ppermute | solution.py:44
  35.2 1.6 collective-permute-start.7
  36.8 2.7 %collective-permute-start.6 = (bf16[256,512]{1,0:T(8,128)(2,1)S(1)}, bf16[256,512]{1,0:T(8,128)(2,1)}, u32[]{:S(2)}, u32[]{:S(2)}) collective-permute-start(bf16[256,512]{1,0:T(8,128)(2,1)S(1)} %pad_maximum_fusion.1.refs_2_), channel_id=1, source_target_pairs={{0,3},{8,11},{16,19},{24,27},{32,35},{40,43},{48,51},{56,59},{64,6... | collective-permute-start | bytes 786440 | tf_op jit(solution)/shard_map/ppermute | solution.py:44
  39.5 5.4 %collective-permute-done.7.refs_5_ = bf16[256,512]{1,0:T(8,128)(2,1)} collective-permute-done((bf16[256,512]{1,0:T(8,128)(2,1)S(1)}, bf16[256,512]{1,0:T(8,128)(2,1)}, u32[]{:S(2)}, u32[]{:S(2)}) %collective-permute-start.7) | collective-permute-done | bytes 262176 | tf_op jit(solution)/shard_map/ppermute | solution.py:44
  44.8 1.2 collective-permute-start.13
  46.0 4.7 %collective-permute-done.6.refs_4_ = bf16[256,512]{1,0:T(8,128)(2,1)} collective-permute-done((bf16[256,512]{1,0:T(8,128)(2,1)S(1)}, bf16[256,512]{1,0:T(8,128)(2,1)}, u32[]{:S(2)}, u32[]{:S(2)}) %collective-permute-start.6) | collective-permute-done | bytes 262176 | tf_op jit(solution)/shard_map/ppermute | solution.py:44
  51.9 0.8 collective-permute-done.12.refs_10_
  53.3 1.6 copy-done.1
  56.2 5.4 %forward.1 = (f32[512,2048]{1,0:T(8,128)S(1)}, f32[512,1]{1,0:T(8,128)S(1)}, f32[2,2048]{1,0:T(2,128)S(1)}, bf16[2,2176]{1,0:T(2,128)(2,1)S(1)}) custom-call(s32[4]{0:T(128)S(1)} %pad_add_fusion.where, s32[2]{0:T(128)S(1)} %copy-done.5, s32[2]{0:T(128)S(1)} %copy-done.6, s32[2]{0:T(128)S(1)} %copy-done.7, s32[8]{0:T(128)S(1)} %copy-done.8, ...), custom_call_target="tpu_custom_call" | custom-call | tf_op jit(solution)/shard_map/forward/pallas_call | solution.py:400
  61.6 2.0 %collective-permute-start.16 = (bf16[2,2176]{1,0:T(2,128)(2,1)S(1)}, bf16[2,2176]{1,0:T(2,128)(2,1)S(1)}, u32[]{:S(2)}, u32[]{:S(2)}) collective-permute-start(bf16[2,2176]{1,0:T(2,128)(2,1)S(1)} %get-tuple-element.41), channel_id=1, source_target_pairs={{0,2},{8,10},{16,18},{24,26},{32,34},{40,42},{48,50},{56,58},{64,6... | collective-permute-start | bytes 26120 | tf_op jit(solution)/shard_map/ppermute | solution.py:44
  63.6 2.1 %collective-permute-start.15 = (bf16[2,2176]{1,0:T(2,128)(2,1)S(1)}, bf16[2,2176]{1,0:T(2,128)(2,1)S(1)}, u32[]{:S(2)}, u32[]{:S(2)}) collective-permute-start(bf16[2,2176]{1,0:T(2,128)(2,1)S(1)} %get-tuple-element.41), channel_id=1, source_target_pairs={{0,3},{8,11},{16,19},{24,27},{32,35},{40,43},{48,51},{56,59},{64,6... | collective-permute-start | bytes 26120 | tf_op jit(solution)/shard_map/ppermute | solution.py:44
  65.7 1.6 collective-permute-done.15
  67.3 1.2 collective-permute-done.14
  68.6 1.0 collective-permute-start.18
  69.7 1.6 %collective-permute-start.17 = (bf16[8,2176]{1,0:T(8,128)(2,1)S(1)}, bf16[8,2176]{1,0:T(8,128)(2,1)S(1)}, u32[]{:S(2)}, u32[]{:S(2)}) collective-permute-start(bf16[8,2176]{1,0:T(8,128)(2,1)S(1)} %pad_maximum_fusion.4), channel_id=1, source_target_pairs={{0,64},{8,72},{16,80},{24,88},{32,96},{40,104},{48,112},{56,120},{... | collective-permute-start | bytes 104456 | tf_op jit(solution)/shard_map/ppermute | solution.py:44
  71.3 1.7 %collective-permute-done.19 = bf16[8,2176]{1,0:T(8,128)(2,1)S(1)} collective-permute-done((bf16[8,2176]{1,0:T(8,128)(2,1)S(1)}, bf16[8,2176]{1,0:T(8,128)(2,1)S(1)}, u32[]{:S(2)}, u32[]{:S(2)}) %collective-permute-start.19) | collective-permute-done | bytes 34848 | tf_op jit(solution)/shard_map/ppermute | solution.py:44
  73.1 3.7 %collective-permute-start.22 = (bf16[32,2176]{1,0:T(8,128)(2,1)S(1)}, bf16[32,2176]{1,0:T(8,128)(2,1)S(1)}, u32[]{:S(2)}, u32[]{:S(2)}) collective-permute-start(bf16[32,2176]{1,0:T(8,128)(2,1)S(1)} %pad_maximum_fusion.3.refs_4_), channel_id=1, source_target_pairs={{0,32},{8,40},{16,48},{24,56},{32,0},{40,8},{48,16},{56,24},{64,96... | collective-permute-start | bytes 417800 | tf_op jit(solution)/shard_map/ppermute | solution.py:44
  77.5 3.5 %collective-permute-start.23 = (bf16[32,2176]{1,0:T(8,128)(2,1)S(1)}, bf16[32,2176]{1,0:T(8,128)(2,1)S(1)}, u32[]{:S(2)}, u32[]{:S(2)}) collective-permute-start(bf16[32,2176]{1,0:T(8,128)(2,1)S(1)} %pad_maximum_fusion.3.refs_4_), channel_id=1, source_target_pairs={{0,8},{8,0},{16,24},{24,16},{32,40},{40,32},{48,56},{56,48},{64,72... | collective-permute-start | bytes 417800 | tf_op jit(solution)/shard_map/ppermute | solution.py:44
  81.0 2.8 %collective-permute-start.26 = (bf16[32,2176]{1,0:T(8,128)(2,1)S(1)}, bf16[32,2176]{1,0:T(8,128)(2,1)S(1)}, u32[]{:S(2)}, u32[]{:S(2)}) collective-permute-start(bf16[32,2176]{1,0:T(8,128)(2,1)S(1)} %collective-permute-done.22.refs_7_), channel_id=1, source_target_pairs={{0,8},{8,0},{16,24},{24,16},{32,40},{40,32},{48,56},{56,48},{64,72... | collective-permute-start | bytes 417800 | tf_op jit(solution)/shard_map/ppermute | solution.py:44
  83.8 2.4 %collective-permute-start.25 = (bf16[32,2176]{1,0:T(8,128)(2,1)S(1)}, bf16[32,2176]{1,0:T(8,128)(2,1)S(1)}, u32[]{:S(2)}, u32[]{:S(2)}) collective-permute-start(bf16[32,2176]{1,0:T(8,128)(2,1)S(1)} %collective-permute-done.21.refs_6_), channel_id=1, source_target_pairs={{0,8},{8,0},{16,24},{24,16},{32,40},{40,32},{48,56},{56,48},{64,72... | collective-permute-start | bytes 417800 | tf_op jit(solution)/shard_map/ppermute | solution.py:44
  86.3 1.0 collective-permute-done.25.refs_10_
  87.6 5.6 %loss.1 = (f32[8,2048]{1,0:T(8,128)S(1)}, f32[8,2048]{1,0:T(8,128)S(1)}, f32[8,2048]{1,0:T(8,128)S(1)}, f32[8,2048]{1,0:T(8,128)S(1)}, bf16[8,2048]{1,0:T(8,128)(2,1)}) custom-call(s32[4]{0:T(128)S(1)} %pad_add_fusion.where, f32[1,2048]{1,0:T(1,128)S(1)} %bitcast.8, bf16[640,512]{1,0:T(8,128)(2,1)S(1)} %pad_maximum_fusion.refs_0_, ...), custom_call_target="tpu_custom_call" | custom-call | tf_op jit(solution)/shard_map/loss/pallas_call | solution.py:423
  93.4 1.7 %collective-permute-start.28 = (f32[8,2048]{1,0:T(8,128)S(1)}, f32[8,2048]{1,0:T(8,128)S(1)}, u32[]{:S(2)}, u32[]{:S(2)}) collective-permute-start(f32[8,2048]{1,0:T(8,128)S(1)} %get-tuple-element.44), channel_id=1, source_target_pairs={{0,48},{8,56},{16,32},{24,40},{32,16},{40,24},{48,0},{56,8},{64,11... | collective-permute-start | bytes 196616 | tf_op jit(solution)/shard_map/ppermute | solution.py:44
  95.1 1.5 collective-permute-start.29
  96.8 0.9 collective-permute-done.28
  97.8 2.0 %collective-permute-done.29 = f32[8,2048]{1,0:T(8,128)S(1)} collective-permute-done((f32[8,2048]{1,0:T(8,128)S(1)}, f32[8,2048]{1,0:T(8,128)S(1)}, u32[]{:S(2)}, u32[]{:S(2)}) %collective-permute-start.29) | collective-permute-done | bytes 65568 | tf_op jit(solution)/shard_map/ppermute | solution.py:44
  99.7 1.6 %collective-permute-start.30 = (f32[8,2048]{1,0:T(8,128)S(1)}, f32[8,2048]{1,0:T(8,128)S(1)}, u32[]{:S(2)}, u32[]{:S(2)}) collective-permute-start(f32[8,2048]{1,0:T(8,128)S(1)} %add_add_fusion.refs_0_), channel_id=1, source_target_pairs={{0,64},{8,72},{16,80},{24,88},{32,96},{40,104},{48,112},{56,120},{... | collective-permute-start | bytes 196616 | tf_op jit(solution)/shard_map/ppermute | solution.py:44
  101.3 2.1 %collective-permute-start.31 = (bf16[512,1024]{1,0:T(8,128)(2,1)S(1)}, bf16[512,1024]{1,0:T(8,128)(2,1)S(1)}, u32[]{:S(2)}, u32[]{:S(2)}) collective-permute-start(bf16[512,1024]{1,0:T(8,128)(2,1)S(1)} %copy-done), channel_id=1, source_target_pairs={{0,8},{8,0},{16,24},{24,16},{32,40},{40,32},{48,56},{56,48},{64,72... | collective-permute-start | bytes 3145736 | tf_op jit(solution)/shard_map/ppermute | solution.py:44
  103.5 3.0 %residual.3 = (bf16[512,2048]{1,0:T(8,128)(2,1)}, bf16[512,1024]{1,0:T(8,128)(2,1)S(1)}, bf16[512,1024]{1,0:T(8,128)(2,1)S(1)}, f32[1,2048]{1,0:T(1,128)}, f32[1,1]{1,0:T(1,128)}) custom-call(s32[4]{0:T(128)S(1)} %pad_add_fusion.where, s32[2]{0:T(128)S(1)} %copy-done.5, f32[512,2048]{1,0:T(8,128)S(1)} %get-tuple-element.38.stream, ...), custom_call_target="tpu_custom_call" | custom-call | tf_op jit(solution)/shard_map/residual/pallas_call | solution.py:440
  106.5 2.5 %collective-permute-start.32 = (bf16[512,1024]{1,0:T(8,128)(2,1)S(1)}, bf16[512,1024]{1,0:T(8,128)(2,1)S(1)}, u32[]{:S(2)}, u32[]{:S(2)}) collective-permute-start(bf16[512,1024]{1,0:T(8,128)(2,1)S(1)} %get-tuple-element.50.send), channel_id=1, source_target_pairs={{0,8},{8,0},{16,24},{24,16},{32,40},{40,32},{48,56},{56,48},{64,72... | collective-permute-start | bytes 3145736 | tf_op jit(solution)/shard_map/ppermute | solution.py:44
  109.0 2.3 %collective-permute-done.32.peer_grad = bf16[512,1024]{1,0:T(8,128)(2,1)S(1)} collective-permute-done((bf16[512,1024]{1,0:T(8,128)(2,1)S(1)}, bf16[512,1024]{1,0:T(8,128)(2,1)S(1)}, u32[]{:S(2)}, u32[]{:S(2)}) %collective-permute-start.32) | collective-permute-done | bytes 1048608 | tf_op jit(solution)/shard_map/ppermute | solution.py:44
  111.2 2.1 %blocks_sent.1 = (bf16[512,512]{1,0:T(8,128)(2,1)S(1)}, bf16[256,512]{1,0:T(8,128)(2,1)S(1)}, bf16[256,512]{1,0:T(8,128)(2,1)S(1)}, bf16[256,512]{1,0:T(8,128)(2,1)S(1)}) custom-call(s32[4]{0:T(128)S(1)} %pad_add_fusion.where, bf16[512,1024]{1,0:T(8,128)(2,1)S(1)} %copy-done, bf16[512,1024]{1,0:T(8,128)(2,1)S(1)} %collective-permute-done.31.peer_context, ...), custom_call_target="tpu_custom_call" | custom-call | tf_op jit(solution)/shard_map/blocks_sent/pallas_call | solution.py:468
  113.5 1.4 collective-permute-start.41
  114.8 1.9 %collective-permute-start.42 = (bf16[256,512]{1,0:T(8,128)(2,1)S(1)}, bf16[256,512]{1,0:T(8,128)(2,1)S(1)}, u32[]{:S(2)}, u32[]{:S(2)}) collective-permute-start(bf16[256,512]{1,0:T(8,128)(2,1)S(1)} %get-tuple-element.59), channel_id=1, source_target_pairs={{0,2},{8,10},{16,18},{24,26},{32,34},{40,42},{48,50},{56,58},{64,6... | collective-permute-start | bytes 786440 | tf_op jit(solution)/shard_map/ppermute | solution.py:44
  116.7 1.4 collective-permute-start.33
  118.1 5.1 %context.3 = bf16[512,1024]{1,0:T(8,128)(2,1)} custom-call(s32[4]{0:T(128)S(1)} %pad_add_fusion.where, bf16[512,1024]{1,0:T(8,128)(2,1)S(1)} %get-tuple-element.49.own_grad.keep, bf16[512,1024]{1,0:T(8,128)(2,1)S(1)} %get-tuple-element.50.send, bf16[640,512]{1,0:T(8,128)(2,1)S(1)} %pad_maximum_fusion.refs_0_, ...), custom_call_target="tpu_custom_call" | custom-call | tf_op jit(solution)/shard_map/context/pallas_call | solution.py:455
  123.2 1.6 blocks_kept.1
  124.8 2.5 %collective-permute-done.42 = bf16[256,512]{1,0:T(8,128)(2,1)S(1)} collective-permute-done((bf16[256,512]{1,0:T(8,128)(2,1)S(1)}, bf16[256,512]{1,0:T(8,128)(2,1)S(1)}, u32[]{:S(2)}, u32[]{:S(2)}) %collective-permute-start.42) | collective-permute-done | bytes 262176 | tf_op jit(solution)/shard_map/ppermute | solution.py:44
  127.4 1.5 collective-permute-start.43
  128.9 1.2 collective-permute-done.33
  130.8 1.7 %collective-permute-start.36 = (bf16[128,512]{1,0:T(8,128)(2,1)S(1)}, bf16[128,512]{1,0:T(8,128)(2,1)S(1)}, u32[]{:S(2)}, u32[]{:S(2)}) collective-permute-start(bf16[128,512]{1,0:T(8,128)(2,1)S(1)} %get-tuple-element.67), channel_id=1, source_target_pairs={{0,2},{8,10},{16,18},{24,26},{32,34},{40,42},{48,50},{56,58},{64,6... | collective-permute-start | bytes 393224 | tf_op jit(solution)/shard_map/ppermute | solution.py:44
  132.6 1.8 %collective-permute-start.35 = (bf16[128,512]{1,0:T(8,128)(2,1)S(1)}, bf16[128,512]{1,0:T(8,128)(2,1)S(1)}, u32[]{:S(2)}, u32[]{:S(2)}) collective-permute-start(bf16[128,512]{1,0:T(8,128)(2,1)S(1)} %get-tuple-element.68), channel_id=1, source_target_pairs={{0,3},{8,11},{16,19},{24,27},{32,35},{40,43},{48,51},{56,59},{64,6... | collective-permute-start | bytes 393224 | tf_op jit(solution)/shard_map/ppermute | solution.py:44
  134.3 0.9 collective-permute-start.44
  135.3 1.2 collective-permute-done.36
  136.5 1.3 collective-permute-done.35
  138.6 1.1 collective-permute-start.45
  139.7 2.3 %collective-permute-done.37 = bf16[128,512]{1,0:T(8,128)(2,1)S(1)} collective-permute-done((bf16[128,512]{1,0:T(8,128)(2,1)S(1)}, bf16[128,512]{1,0:T(8,128)(2,1)S(1)}, u32[]{:S(2)}, u32[]{:S(2)}) %collective-permute-start.37) | collective-permute-done | bytes 131104 | tf_op jit(solution)/shard_map/ppermute | solution.py:44
  142.0 0.9 collective-permute-start.38
  143.8 0.9 collective-permute-start.46
  144.7 1.5 collective-permute-done.38
  146.2 1.2 collective-permute-start.39
  148.1 3.2 %collective-permute-done.39 = bf16[128,512]{1,0:T(8,128)(2,1)S(1)} collective-permute-done((bf16[128,512]{1,0:T(8,128)(2,1)S(1)}, bf16[128,512]{1,0:T(8,128)(2,1)S(1)}, u32[]{:S(2)}, u32[]{:S(2)}) %collective-permute-start.39) | collective-permute-done | bytes 131104 | tf_op jit(solution)/shard_map/ppermute | solution.py:44
  151.4 6.7 %collective-permute-start.47 = (bf16[128,1024]{1,0:T(8,128)(2,1)S(1)}, bf16[128,1024]{1,0:T(8,128)(2,1)S(1)}, u32[]{:S(2)}, u32[]{:S(2)}) collective-permute-start(bf16[128,1024]{1,0:T(8,128)(2,1)S(1)} %pad_maximum_fusion.2), channel_id=1, source_target_pairs={{0,8},{8,0},{16,24},{24,16},{32,40},{40,32},{48,56},{56,48},{64,72... | collective-permute-start | bytes 786440 | tf_op jit(solution)/shard_map/ppermute | solution.py:44
  158.1 1.2 collective-permute-done.47
  159.3 0.9 maximum_select_fusion
  (77 shorter events, 8.7 us)
Async XLA Ops:
  0.6 52.7 %copy-start = (bf16[512,1024]{1,0:T(8,128)(2,1)S(1)}, bf16[512,1024]{1,0:T(8,128)(2,1)}, u32[]{:S(2)}) copy-start(bf16[512,1024]{1,0:T(8,128)(2,1)} %own_context.3) | copy-start | bytes 3145732
  0.6 1.1 copy-start.2
  1.8 0.8 copy-start.4
  2.5 50.8 %copy-start.3 = (f32[2048]{0:T(1024)S(1)}, f32[2048]{0:T(1024)}, u32[]{:S(2)}) copy-start(f32[2048]{0:T(1024)} %param.12) | copy-start | bytes 24580
  2.5 50.8 %copy-start.5 = (s32[2]{0:T(128)S(1)}, s32[2]{0:T(128)}, u32[]{:S(2)}) copy-start(s32[2]{0:T(128)} %lengths.3) | copy-start | bytes 28
  2.5 50.8 %copy-start.6 = (s32[2]{0:T(128)S(1)}, s32[2]{0:T(128)}, u32[]{:S(2)}) copy-start(s32[2]{0:T(128)} %ids.1) | copy-start | bytes 28
  2.6 7.3 %collective-permute-start.3 = (bf16[128,512]{1,0:T(8,128)(2,1)S(1)}, bf16[128,512]{1,0:T(8,128)(2,1)S(1)}, u32[]{:S(2)}, u32[]{:S(2)}) collective-permute-start(bf16[128,512]{1,0:T(8,128)(2,1)S(1)} %get-tuple-element.35), channel_id=1, source_target_pairs={{0,68},{8,76},{16,84},{24,92},{32,100},{40,108},{48,116},{56,124},... | collective-permute-start | bytes 393224 | tf_op jit(solution)/shard_map/ppermute | solution.py:44
  6.2 6.3 %collective-permute-start.2 = (bf16[160,512]{1,0:T(8,128)(2,1)S(1)}, bf16[160,512]{1,0:T(8,128)(2,1)S(1)}, u32[]{:S(2)}, u32[]{:S(2)}) collective-permute-start(bf16[160,512]{1,0:T(8,128)(2,1)S(1)} %get-tuple-element.34), channel_id=1, source_target_pairs={{0,2},{8,10},{16,18},{24,26},{32,34},{40,42},{48,50},{56,58},{64,6... | collective-permute-start | bytes 491528 | tf_op jit(solution)/shard_map/ppermute | solution.py:44
  9.0 7.8 %collective-permute-start.1 = (bf16[160,512]{1,0:T(8,128)(2,1)S(1)}, bf16[160,512]{1,0:T(8,128)(2,1)S(1)}, u32[]{:S(2)}, u32[]{:S(2)}) collective-permute-start(bf16[160,512]{1,0:T(8,128)(2,1)S(1)} %get-tuple-element.34), channel_id=1, source_target_pairs={{0,3},{8,11},{16,19},{24,27},{32,35},{40,43},{48,51},{56,59},{64,6... | collective-permute-start | bytes 491528 | tf_op jit(solution)/shard_map/ppermute | solution.py:44
  9.8 6.9 %collective-permute-start = (bf16[160,512]{1,0:T(8,128)(2,1)S(1)}, bf16[160,512]{1,0:T(8,128)(2,1)S(1)}, u32[]{:S(2)}, u32[]{:S(2)}) collective-permute-start(bf16[160,512]{1,0:T(8,128)(2,1)S(1)} %get-tuple-element.34), channel_id=1, source_target_pairs={{0,1},{8,9},{16,17},{24,25},{32,33},{40,41},{48,49},{56,57},{64,65... | collective-permute-start | bytes 491528 | tf_op jit(solution)/shard_map/ppermute | solution.py:44
  16.8 16.3 %collective-permute-start.4 = (bf16[640,512]{1,0:T(8,128)(2,1)S(1)}, bf16[640,512]{1,0:T(8,128)(2,1)S(1)}, u32[]{:S(2)}, u32[]{:S(2)}) collective-permute-start(bf16[640,512]{1,0:T(8,128)(2,1)S(1)} %pad_maximum_fusion.refs_0_), channel_id=1, source_target_pairs={{0,68},{8,76},{16,84},{24,92},{32,100},{40,108},{48,116},{56,124},... | collective-permute-start | bytes 1966088 | tf_op jit(solution)/shard_map/ppermute | solution.py:44
  17.1 22.3 %collective-permute-start.10 = (bf16[256,512]{1,0:T(8,128)(2,1)S(1)}, bf16[256,512]{1,0:T(8,128)(2,1)S(1)}, u32[]{:S(2)}, u32[]{:S(2)}) collective-permute-start(bf16[256,512]{1,0:T(8,128)(2,1)S(1)} %pad_maximum_fusion.1.refs_2_), channel_id=1, source_target_pairs={{0,8},{8,0},{16,24},{24,16},{32,40},{40,32},{48,56},{56,48},{64,72... | collective-permute-start | bytes 786440 | tf_op jit(solution)/shard_map/ppermute | solution.py:44
  18.4 34.9 %collective-permute-start.8 = (bf16[640,512]{1,0:T(8,128)(2,1)S(1)}, bf16[640,512]{1,0:T(8,128)(2,1)S(1)}, u32[]{:S(2)}, u32[]{:S(2)}) collective-permute-start(bf16[640,512]{1,0:T(8,128)(2,1)S(1)} %pad_maximum_fusion.refs_0_), channel_id=1, source_target_pairs={{0,8},{8,0},{16,24},{24,16},{32,40},{40,32},{48,56},{56,48},{64,72... | collective-permute-start | bytes 1966088 | tf_op jit(solution)/shard_map/ppermute | solution.py:44
  33.1 20.2 %collective-permute-start.9 = (bf16[640,512]{1,0:T(8,128)(2,1)S(1)}, bf16[640,512]{1,0:T(8,128)(2,1)}, u32[]{:S(2)}, u32[]{:S(2)}) collective-permute-start(bf16[640,512]{1,0:T(8,128)(2,1)S(1)} %collective-permute-done.4.refs_1_), channel_id=1, source_target_pairs={{0,8},{8,0},{16,24},{24,16},{32,40},{40,32},{48,56},{56,48},{64,72... | collective-permute-start | bytes 1966088 | tf_op jit(solution)/shard_map/ppermute | solution.py:44
  35.2 9.6 %collective-permute-start.7 = (bf16[256,512]{1,0:T(8,128)(2,1)S(1)}, bf16[256,512]{1,0:T(8,128)(2,1)}, u32[]{:S(2)}, u32[]{:S(2)}) collective-permute-start(bf16[256,512]{1,0:T(8,128)(2,1)S(1)} %pad_maximum_fusion.1.refs_2_), channel_id=1, source_target_pairs={{0,2},{8,10},{16,18},{24,26},{32,34},{40,42},{48,50},{56,58},{64,6... | collective-permute-start | bytes 786440 | tf_op jit(solution)/shard_map/ppermute | solution.py:44
  36.8 13.9 %collective-permute-start.6 = (bf16[256,512]{1,0:T(8,128)(2,1)S(1)}, bf16[256,512]{1,0:T(8,128)(2,1)}, u32[]{:S(2)}, u32[]{:S(2)}) collective-permute-start(bf16[256,512]{1,0:T(8,128)(2,1)S(1)} %pad_maximum_fusion.1.refs_2_), channel_id=1, source_target_pairs={{0,3},{8,11},{16,19},{24,27},{32,35},{40,43},{48,51},{56,59},{64,6... | collective-permute-start | bytes 786440 | tf_op jit(solution)/shard_map/ppermute | solution.py:44
  39.5 11.7 %collective-permute-start.5 = (bf16[256,512]{1,0:T(8,128)(2,1)S(1)}, bf16[256,512]{1,0:T(8,128)(2,1)}, u32[]{:S(2)}, u32[]{:S(2)}) collective-permute-start(bf16[256,512]{1,0:T(8,128)(2,1)S(1)} %pad_maximum_fusion.1.refs_2_), channel_id=1, source_target_pairs={{0,1},{8,9},{16,17},{24,25},{32,33},{40,41},{48,49},{56,57},{64,65... | collective-permute-start | bytes 786440 | tf_op jit(solution)/shard_map/ppermute | solution.py:44
  44.8 7.0 %collective-permute-start.13 = (bf16[256,512]{1,0:T(8,128)(2,1)}, bf16[256,512]{1,0:T(8,128)(2,1)}, u32[]{:S(2)}, u32[]{:S(2)}) collective-permute-start(bf16[256,512]{1,0:T(8,128)(2,1)} %collective-permute-done.7.refs_5_), channel_id=1, source_target_pairs={{0,8},{8,0},{16,24},{24,16},{32,40},{40,32},{48,56},{56,48},{64,72... | collective-permute-start | bytes 786440 | tf_op jit(solution)/shard_map/ppermute | solution.py:44
  50.7 2.0 %collective-permute-start.12 = (bf16[256,512]{1,0:T(8,128)(2,1)}, bf16[256,512]{1,0:T(8,128)(2,1)}, u32[]{:S(2)}, u32[]{:S(2)}) collective-permute-start(bf16[256,512]{1,0:T(8,128)(2,1)} %collective-permute-done.6.refs_4_), channel_id=1, source_target_pairs={{0,8},{8,0},{16,24},{24,16},{32,40},{40,32},{48,56},{56,48},{64,72... | collective-permute-start | bytes 786440 | tf_op jit(solution)/shard_map/ppermute | solution.py:44
  51.2 2.1 %collective-permute-start.11 = (bf16[256,512]{1,0:T(8,128)(2,1)}, bf16[256,512]{1,0:T(8,128)(2,1)}, u32[]{:S(2)}, u32[]{:S(2)}) collective-permute-start(bf16[256,512]{1,0:T(8,128)(2,1)} %collective-permute-done.5.refs_3_), channel_id=1, source_target_pairs={{0,8},{8,0},{16,24},{24,16},{32,40},{40,32},{48,56},{56,48},{64,72... | collective-permute-start | bytes 786440 | tf_op jit(solution)/shard_map/ppermute | solution.py:44
  53.3 1.6 copy-start.1
  54.9 0.7 copy-start.7
  55.6 0.7 copy-start.8
  61.6 4.1 %collective-permute-start.16 = (bf16[2,2176]{1,0:T(2,128)(2,1)S(1)}, bf16[2,2176]{1,0:T(2,128)(2,1)S(1)}, u32[]{:S(2)}, u32[]{:S(2)}) collective-permute-start(bf16[2,2176]{1,0:T(2,128)(2,1)S(1)} %get-tuple-element.41), channel_id=1, source_target_pairs={{0,2},{8,10},{16,18},{24,26},{32,34},{40,42},{48,50},{56,58},{64,6... | collective-permute-start | bytes 26120 | tf_op jit(solution)/shard_map/ppermute | solution.py:44
  63.6 3.7 %collective-permute-start.15 = (bf16[2,2176]{1,0:T(2,128)(2,1)S(1)}, bf16[2,2176]{1,0:T(2,128)(2,1)S(1)}, u32[]{:S(2)}, u32[]{:S(2)}) collective-permute-start(bf16[2,2176]{1,0:T(2,128)(2,1)S(1)} %get-tuple-element.41), channel_id=1, source_target_pairs={{0,3},{8,11},{16,19},{24,27},{32,35},{40,43},{48,51},{56,59},{64,6... | collective-permute-start | bytes 26120 | tf_op jit(solution)/shard_map/ppermute | solution.py:44
  65.7 2.8 %collective-permute-start.14 = (bf16[2,2176]{1,0:T(2,128)(2,1)S(1)}, bf16[2,2176]{1,0:T(2,128)(2,1)S(1)}, u32[]{:S(2)}, u32[]{:S(2)}) collective-permute-start(bf16[2,2176]{1,0:T(2,128)(2,1)S(1)} %get-tuple-element.41), channel_id=1, source_target_pairs={{0,1},{8,9},{16,17},{24,25},{32,33},{40,41},{48,49},{56,57},{64,65... | collective-permute-start | bytes 26120 | tf_op jit(solution)/shard_map/ppermute | solution.py:44
  68.5 4.5 %collective-permute-start.19 = (bf16[8,2176]{1,0:T(8,128)(2,1)S(1)}, bf16[8,2176]{1,0:T(8,128)(2,1)S(1)}, u32[]{:S(2)}, u32[]{:S(2)}) collective-permute-start(bf16[8,2176]{1,0:T(8,128)(2,1)S(1)} %pad_maximum_fusion.4), channel_id=1, source_target_pairs={{0,4},{8,12},{16,20},{24,28},{32,36},{40,44},{48,52},{56,60},{64,6... | collective-permute-start | bytes 104456 | tf_op jit(solution)/shard_map/ppermute | solution.py:44
  68.6 4.5 %collective-permute-start.18 = (bf16[8,2176]{1,0:T(8,128)(2,1)S(1)}, bf16[8,2176]{1,0:T(8,128)(2,1)S(1)}, u32[]{:S(2)}, u32[]{:S(2)}) collective-permute-start(bf16[8,2176]{1,0:T(8,128)(2,1)S(1)} %pad_maximum_fusion.4), channel_id=1, source_target_pairs={{0,68},{8,76},{16,84},{24,92},{32,100},{40,108},{48,116},{56,124},... | collective-permute-start | bytes 104456 | tf_op jit(solution)/shard_map/ppermute | solution.py:44
  69.7 3.4 %collective-permute-start.17 = (bf16[8,2176]{1,0:T(8,128)(2,1)S(1)}, bf16[8,2176]{1,0:T(8,128)(2,1)S(1)}, u32[]{:S(2)}, u32[]{:S(2)}) collective-permute-start(bf16[8,2176]{1,0:T(8,128)(2,1)S(1)} %pad_maximum_fusion.4), channel_id=1, source_target_pairs={{0,64},{8,72},{16,80},{24,88},{32,96},{40,104},{48,112},{56,120},{... | collective-permute-start | bytes 104456 | tf_op jit(solution)/shard_map/ppermute | solution.py:44
  73.1 7.9 %collective-permute-start.22 = (bf16[32,2176]{1,0:T(8,128)(2,1)S(1)}, bf16[32,2176]{1,0:T(8,128)(2,1)S(1)}, u32[]{:S(2)}, u32[]{:S(2)}) collective-permute-start(bf16[32,2176]{1,0:T(8,128)(2,1)S(1)} %pad_maximum_fusion.3.refs_4_), channel_id=1, source_target_pairs={{0,32},{8,40},{16,48},{24,56},{32,0},{40,8},{48,16},{56,24},{64,96... | collective-permute-start | bytes 417800 | tf_op jit(solution)/shard_map/ppermute | solution.py:44
  76.8 7.0 %collective-permute-start.21 = (bf16[32,2176]{1,0:T(8,128)(2,1)S(1)}, bf16[32,2176]{1,0:T(8,128)(2,1)S(1)}, u32[]{:S(2)}, u32[]{:S(2)}) collective-permute-start(bf16[32,2176]{1,0:T(8,128)(2,1)S(1)} %pad_maximum_fusion.3.refs_4_), channel_id=1, source_target_pairs={{0,48},{8,56},{16,32},{24,40},{32,16},{40,24},{48,0},{56,8},{64,11... | collective-permute-start | bytes 417800 | tf_op jit(solution)/shard_map/ppermute | solution.py:44
  77.2 9.1 %collective-permute-start.20 = (bf16[32,2176]{1,0:T(8,128)(2,1)S(1)}, bf16[32,2176]{1,0:T(8,128)(2,1)S(1)}, u32[]{:S(2)}, u32[]{:S(2)}) collective-permute-start(bf16[32,2176]{1,0:T(8,128)(2,1)S(1)} %pad_maximum_fusion.3.refs_4_), channel_id=1, source_target_pairs={{0,16},{8,24},{16,0},{24,8},{32,48},{40,56},{48,32},{56,40},{64,80... | collective-permute-start | bytes 417800 | tf_op jit(solution)/shard_map/ppermute | solution.py:44
  77.5 8.8 %collective-permute-start.23 = (bf16[32,2176]{1,0:T(8,128)(2,1)S(1)}, bf16[32,2176]{1,0:T(8,128)(2,1)S(1)}, u32[]{:S(2)}, u32[]{:S(2)}) collective-permute-start(bf16[32,2176]{1,0:T(8,128)(2,1)S(1)} %pad_maximum_fusion.3.refs_4_), channel_id=1, source_target_pairs={{0,8},{8,0},{16,24},{24,16},{32,40},{40,32},{48,56},{56,48},{64,72... | collective-permute-start | bytes 417800 | tf_op jit(solution)/shard_map/ppermute | solution.py:44
  81.0 5.3 %collective-permute-start.26 = (bf16[32,2176]{1,0:T(8,128)(2,1)S(1)}, bf16[32,2176]{1,0:T(8,128)(2,1)S(1)}, u32[]{:S(2)}, u32[]{:S(2)}) collective-permute-start(bf16[32,2176]{1,0:T(8,128)(2,1)S(1)} %collective-permute-done.22.refs_7_), channel_id=1, source_target_pairs={{0,8},{8,0},{16,24},{24,16},{32,40},{40,32},{48,56},{56,48},{64,72... | collective-permute-start | bytes 417800 | tf_op jit(solution)/shard_map/ppermute | solution.py:44
  83.8 3.4 %collective-permute-start.25 = (bf16[32,2176]{1,0:T(8,128)(2,1)S(1)}, bf16[32,2176]{1,0:T(8,128)(2,1)S(1)}, u32[]{:S(2)}, u32[]{:S(2)}) collective-permute-start(bf16[32,2176]{1,0:T(8,128)(2,1)S(1)} %collective-permute-done.21.refs_6_), channel_id=1, source_target_pairs={{0,8},{8,0},{16,24},{24,16},{32,40},{40,32},{48,56},{56,48},{64,72... | collective-permute-start | bytes 417800 | tf_op jit(solution)/shard_map/ppermute | solution.py:44
  86.3 1.4 collective-permute-start.24
  93.3 3.6 %collective-permute-start.27 = (f32[8,2048]{1,0:T(8,128)S(1)}, f32[8,2048]{1,0:T(8,128)S(1)}, u32[]{:S(2)}, u32[]{:S(2)}) collective-permute-start(f32[8,2048]{1,0:T(8,128)S(1)} %get-tuple-element.43), channel_id=1, source_target_pairs={{0,16},{8,24},{16,0},{24,8},{32,48},{40,56},{48,32},{56,40},{64,80... | collective-permute-start | bytes 196616 | tf_op jit(solution)/shard_map/ppermute | solution.py:44
  93.4 4.4 %collective-permute-start.28 = (f32[8,2048]{1,0:T(8,128)S(1)}, f32[8,2048]{1,0:T(8,128)S(1)}, u32[]{:S(2)}, u32[]{:S(2)}) collective-permute-start(f32[8,2048]{1,0:T(8,128)S(1)} %get-tuple-element.44), channel_id=1, source_target_pairs={{0,48},{8,56},{16,32},{24,40},{32,16},{40,24},{48,0},{56,8},{64,11... | collective-permute-start | bytes 196616 | tf_op jit(solution)/shard_map/ppermute | solution.py:44
  95.1 4.6 %collective-permute-start.29 = (f32[8,2048]{1,0:T(8,128)S(1)}, f32[8,2048]{1,0:T(8,128)S(1)}, u32[]{:S(2)}, u32[]{:S(2)}) collective-permute-start(f32[8,2048]{1,0:T(8,128)S(1)} %get-tuple-element.45), channel_id=1, source_target_pairs={{0,32},{8,40},{16,48},{24,56},{32,0},{40,8},{48,16},{56,24},{64,96... | collective-permute-start | bytes 196616 | tf_op jit(solution)/shard_map/ppermute | solution.py:44
  99.7 3.7 %collective-permute-start.30 = (f32[8,2048]{1,0:T(8,128)S(1)}, f32[8,2048]{1,0:T(8,128)S(1)}, u32[]{:S(2)}, u32[]{:S(2)}) collective-permute-start(f32[8,2048]{1,0:T(8,128)S(1)} %add_add_fusion.refs_0_), channel_id=1, source_target_pairs={{0,64},{8,72},{16,80},{24,88},{32,96},{40,104},{48,112},{56,120},{... | collective-permute-start | bytes 196616 | tf_op jit(solution)/shard_map/ppermute | solution.py:44
  101.3 7.6 %collective-permute-start.31 = (bf16[512,1024]{1,0:T(8,128)(2,1)S(1)}, bf16[512,1024]{1,0:T(8,128)(2,1)S(1)}, u32[]{:S(2)}, u32[]{:S(2)}) collective-permute-start(bf16[512,1024]{1,0:T(8,128)(2,1)S(1)} %copy-done), channel_id=1, source_target_pairs={{0,8},{8,0},{16,24},{24,16},{32,40},{40,32},{48,56},{56,48},{64,72... | collective-permute-start | bytes 3145736 | tf_op jit(solution)/shard_map/ppermute | solution.py:44
  106.5 4.7 %collective-permute-start.32 = (bf16[512,1024]{1,0:T(8,128)(2,1)S(1)}, bf16[512,1024]{1,0:T(8,128)(2,1)S(1)}, u32[]{:S(2)}, u32[]{:S(2)}) collective-permute-start(bf16[512,1024]{1,0:T(8,128)(2,1)S(1)} %get-tuple-element.50.send), channel_id=1, source_target_pairs={{0,8},{8,0},{16,24},{24,16},{32,40},{40,32},{48,56},{56,48},{64,72... | collective-permute-start | bytes 3145736 | tf_op jit(solution)/shard_map/ppermute | solution.py:44
  113.4 11.4 %collective-permute-start.40 = (bf16[256,512]{1,0:T(8,128)(2,1)S(1)}, bf16[256,512]{1,0:T(8,128)(2,1)S(1)}, u32[]{:S(2)}, u32[]{:S(2)}) collective-permute-start(bf16[256,512]{1,0:T(8,128)(2,1)S(1)} %get-tuple-element.57), channel_id=1, source_target_pairs={{0,1},{8,9},{16,17},{24,25},{32,33},{40,41},{48,49},{56,57},{64,65... | collective-permute-start | bytes 786440 | tf_op jit(solution)/shard_map/ppermute | solution.py:44
  113.5 11.3 %collective-permute-start.41 = (bf16[256,512]{1,0:T(8,128)(2,1)S(1)}, bf16[256,512]{1,0:T(8,128)(2,1)S(1)}, u32[]{:S(2)}, u32[]{:S(2)}) collective-permute-start(bf16[256,512]{1,0:T(8,128)(2,1)S(1)} %get-tuple-element.58), channel_id=1, source_target_pairs={{0,3},{8,11},{16,19},{24,27},{32,35},{40,43},{48,51},{56,59},{64,6... | collective-permute-start | bytes 786440 | tf_op jit(solution)/shard_map/ppermute | solution.py:44
  114.8 12.4 %collective-permute-start.42 = (bf16[256,512]{1,0:T(8,128)(2,1)S(1)}, bf16[256,512]{1,0:T(8,128)(2,1)S(1)}, u32[]{:S(2)}, u32[]{:S(2)}) collective-permute-start(bf16[256,512]{1,0:T(8,128)(2,1)S(1)} %get-tuple-element.59), channel_id=1, source_target_pairs={{0,2},{8,10},{16,18},{24,26},{32,34},{40,42},{48,50},{56,58},{64,6... | collective-permute-start | bytes 786440 | tf_op jit(solution)/shard_map/ppermute | solution.py:44
  116.7 13.4 %collective-permute-start.33 = (bf16[512,512]{1,0:T(8,128)(2,1)S(1)}, bf16[512,512]{1,0:T(8,128)(2,1)S(1)}, u32[]{:S(2)}, u32[]{:S(2)}) collective-permute-start(bf16[512,512]{1,0:T(8,128)(2,1)S(1)} %get-tuple-element.55), channel_id=1, source_target_pairs={{0,68},{8,76},{16,84},{24,92},{32,100},{40,108},{48,116},{56,124},... | collective-permute-start | bytes 1572872 | tf_op jit(solution)/shard_map/ppermute | solution.py:44
  127.4 6.9 %collective-permute-start.43 = (bf16[128,512]{1,0:T(8,128)(2,1)S(1)}, bf16[128,512]{1,0:T(8,128)(2,1)S(1)}, u32[]{:S(2)}, u32[]{:S(2)}) collective-permute-start(bf16[128,512]{1,0:T(8,128)(2,1)S(1)} %slice.53), channel_id=1, source_target_pairs={{0,68},{8,76},{16,84},{24,92},{32,100},{40,108},{48,116},{56,124},... | collective-permute-start | bytes 393224 | tf_op jit(solution)/shard_map/ppermute | solution.py:44
  130.4 4.9 %collective-permute-start.34 = (bf16[128,512]{1,0:T(8,128)(2,1)S(1)}, bf16[128,512]{1,0:T(8,128)(2,1)S(1)}, u32[]{:S(2)}, u32[]{:S(2)}) collective-permute-start(bf16[128,512]{1,0:T(8,128)(2,1)S(1)} %get-tuple-element.66), channel_id=1, source_target_pairs={{0,1},{8,9},{16,17},{24,25},{32,33},{40,41},{48,49},{56,57},{64,65... | collective-permute-start | bytes 393224 | tf_op jit(solution)/shard_map/ppermute | solution.py:44
  130.8 5.6 %collective-permute-start.36 = (bf16[128,512]{1,0:T(8,128)(2,1)S(1)}, bf16[128,512]{1,0:T(8,128)(2,1)S(1)}, u32[]{:S(2)}, u32[]{:S(2)}) collective-permute-start(bf16[128,512]{1,0:T(8,128)(2,1)S(1)} %get-tuple-element.67), channel_id=1, source_target_pairs={{0,2},{8,10},{16,18},{24,26},{32,34},{40,42},{48,50},{56,58},{64,6... | collective-permute-start | bytes 393224 | tf_op jit(solution)/shard_map/ppermute | solution.py:44
  132.6 5.2 %collective-permute-start.35 = (bf16[128,512]{1,0:T(8,128)(2,1)S(1)}, bf16[128,512]{1,0:T(8,128)(2,1)S(1)}, u32[]{:S(2)}, u32[]{:S(2)}) collective-permute-start(bf16[128,512]{1,0:T(8,128)(2,1)S(1)} %get-tuple-element.68), channel_id=1, source_target_pairs={{0,3},{8,11},{16,19},{24,27},{32,35},{40,43},{48,51},{56,59},{64,6... | collective-permute-start | bytes 393224 | tf_op jit(solution)/shard_map/ppermute | solution.py:44
  134.3 4.2 %collective-permute-start.44 = (bf16[128,512]{1,0:T(8,128)(2,1)S(1)}, bf16[128,512]{1,0:T(8,128)(2,1)S(1)}, u32[]{:S(2)}, u32[]{:S(2)}) collective-permute-start(bf16[128,512]{1,0:T(8,128)(2,1)S(1)} %fusion.8), channel_id=1, source_target_pairs={{0,16},{8,24},{16,0},{24,8},{32,48},{40,56},{48,32},{56,40},{64,80... | collective-permute-start | bytes 393224 | tf_op jit(solution)/shard_map/ppermute | solution.py:44
  137.8 4.2 %collective-permute-start.37 = (bf16[128,512]{1,0:T(8,128)(2,1)S(1)}, bf16[128,512]{1,0:T(8,128)(2,1)S(1)}, u32[]{:S(2)}, u32[]{:S(2)}) collective-permute-start(bf16[128,512]{1,0:T(8,128)(2,1)S(1)} %get-tuple-element.62), channel_id=1, source_target_pairs={{0,64},{8,72},{16,80},{24,88},{32,96},{40,104},{48,112},{56,120},{... | collective-permute-start | bytes 393224 | tf_op jit(solution)/shard_map/ppermute | solution.py:44
  138.6 5.1 %collective-permute-start.45 = (bf16[128,512]{1,0:T(8,128)(2,1)S(1)}, bf16[128,512]{1,0:T(8,128)(2,1)S(1)}, u32[]{:S(2)}, u32[]{:S(2)}) collective-permute-start(bf16[128,512]{1,0:T(8,128)(2,1)S(1)} %fusion.5), channel_id=1, source_target_pairs={{0,48},{8,56},{16,32},{24,40},{32,16},{40,24},{48,0},{56,8},{64,11... | collective-permute-start | bytes 393224 | tf_op jit(solution)/shard_map/ppermute | solution.py:44
  142.0 4.1 %collective-permute-start.38 = (bf16[128,512]{1,0:T(8,128)(2,1)S(1)}, bf16[128,512]{1,0:T(8,128)(2,1)S(1)}, u32[]{:S(2)}, u32[]{:S(2)}) collective-permute-start(bf16[128,512]{1,0:T(8,128)(2,1)S(1)} %fusion.4), channel_id=1, source_target_pairs={{0,16},{8,24},{16,0},{24,8},{32,48},{40,56},{48,32},{56,40},{64,80... | collective-permute-start | bytes 393224 | tf_op jit(solution)/shard_map/ppermute | solution.py:44
  143.8 4.2 %collective-permute-start.46 = (bf16[128,512]{1,0:T(8,128)(2,1)S(1)}, bf16[128,512]{1,0:T(8,128)(2,1)S(1)}, u32[]{:S(2)}, u32[]{:S(2)}) collective-permute-start(bf16[128,512]{1,0:T(8,128)(2,1)S(1)} %fusion.7), channel_id=1, source_target_pairs={{0,64},{8,72},{16,80},{24,88},{32,96},{40,104},{48,112},{56,120},{... | collective-permute-start | bytes 393224 | tf_op jit(solution)/shard_map/ppermute | solution.py:44
  146.2 5.1 %collective-permute-start.39 = (bf16[128,512]{1,0:T(8,128)(2,1)S(1)}, bf16[128,512]{1,0:T(8,128)(2,1)S(1)}, u32[]{:S(2)}, u32[]{:S(2)}) collective-permute-start(bf16[128,512]{1,0:T(8,128)(2,1)S(1)} %fusion.6), channel_id=1, source_target_pairs={{0,48},{8,56},{16,32},{24,40},{32,16},{40,24},{48,0},{56,8},{64,11... | collective-permute-start | bytes 393224 | tf_op jit(solution)/shard_map/ppermute | solution.py:44
  151.4 7.9 %collective-permute-start.47 = (bf16[128,1024]{1,0:T(8,128)(2,1)S(1)}, bf16[128,1024]{1,0:T(8,128)(2,1)S(1)}, u32[]{:S(2)}, u32[]{:S(2)}) collective-permute-start(bf16[128,1024]{1,0:T(8,128)(2,1)S(1)} %pad_maximum_fusion.2), channel_id=1, source_target_pairs={{0,8},{8,0},{16,24},{24,16},{32,40},{40,32},{48,56},{56,48},{64,72... | collective-permute-start | bytes 786440 | tf_op jit(solution)/shard_map/ppermute | solution.py:44

commit v6 on v5

--- a/solution.py
+++ b/solution.py
@@ -90,6 +90,14 @@
     )
 
 
+def with_r3(r3):
+    return [(q, ry) for q in (2 * r3, 2 * r3 + 1) for ry in range(2)]
+
+
+def with_ry(ry):
+    return [(q, ry) for q in range(4)]
+
+
 def block_home(x, y_hi, q, ry):
     return (y_hi ^ ry) * 4 + (x ^ OFFSETS[q])
 
@@ -118,24 +126,26 @@
     first[rows:, :] = riding.astype(BF16)
 
 
-def forward_kernel(where, lengths, ids, counts, positive, context, residual, gain, *refs):
-    firsts, seconds = (refs[0:2], refs[6:8]), (refs[2:6], refs[8:12])
-    stream, inverse, pooled, embedding, added_rows, sem = refs[12:]
+def forward_kernel(items, ints, context, residual, gain, *refs):
+    firsts, seconds = (refs[0:2], refs[4:6]), (refs[2:4], refs[6:8])
+    stream, inverse, pooled, embedding, added_rows, sem = refs[8:]
+    where = [ints[i] for i in range(4)]
+    lengths, ids, counts = ([ints[4 + j * items + i] for i in range(items)] for j in range(3))
+    positive = [ints[i] for i in range(4 + 3 * items, ints.shape[0])]
     tokens, width = residual.shape
     part = width // 4
     block = context.shape[1] // 8
-    items = lengths.shape[0]
     length = tokens // items
     copy = pltpu.make_async_copy(residual, added_rows, sem)
     copy.start()
-    by_ry = [blocks_of(context, where, [(q, ry) for q in range(4)], block) for ry in range(2)]
-    by_q = [blocks_of(context, where, [(q, 0), (q, 1)], block) for q in range(4)]
+    by_r3 = [blocks_of(context, where, with_r3(r3), block) for r3 in range(2)]
+    by_ry = [blocks_of(context, where, with_ry(ry), block) for ry in range(2)]
     for side, (first_at, second_at) in enumerate(column_offsets(where[3], width)):
         stream[:, pl.ds(first_at, part)] = sum(
-            dot(by_ry[ry], weight_rows(firsts[side][ry], block)) for ry in range(2)
+            dot(by_r3[r3], weight_rows(firsts[side][r3], block)) for r3 in range(2)
         )
         stream[:, pl.ds(second_at, part)] = sum(
-            dot(by_q[q], seconds[side][q][...]) for q in range(4)
+            dot(by_ry[ry], seconds[side][ry][...]) for ry in range(2)
         )
     copy.wait()
     for i in range(items):
@@ -157,7 +167,7 @@
     for i in range(items):
         for at, value in enumerate((ids[i], counts[i] // 128, counts[i] % 128)):
             labels = jnp.where((row == i) & (lane == at), value, labels)
-    for u in range(positive.shape[0]):
+    for u in range(len(positive)):
         labels = jnp.where((row == 0) & (lane == POSITIVE + u), positive[u], labels)
     embedding[:, width:] = labels.astype(F32).astype(BF16)
 
@@ -185,12 +195,12 @@
     rode = parts * users_here
     copies = []
     for n in range(4):
-        for q in range(4):
+        for b in range(4):
             copies.append(
                 pltpu.make_async_copy(
-                    piece_refs[n].at[pl.ds(q * stride + block, rode)],
-                    riders.at[pl.ds((n * 4 + q) * rode, rode)],
-                    sems.at[n * 4 + q],
+                    piece_refs[n].at[pl.ds(b * stride + block, rode)],
+                    riders.at[pl.ds((n * 4 + b) * rode, rode)],
+                    sems.at[n * 4 + b],
                 )
             )
     for copy in copies:
@@ -212,8 +222,8 @@
     to = lax.broadcasted_iota(jnp.int32, (people, 16 * rode), 0)
     of = lax.broadcasted_iota(jnp.int32, (people, 16 * rode), 1)
     one = of // rode
-    holder = ((core ^ bit(one, 3)) * 2 + ((y // 2) ^ bit(one, 2))) * 4 + (
-        x ^ bit(one, 0) ^ (3 * bit(one, 1))
+    holder = ((core ^ bit(one, 3)) * 2 + ((y // 2) ^ bit(one, 0))) * 4 + (
+        x ^ bit(one, 1) ^ (3 * bit(one, 2))
     )
     home = holder * users_here + of % users_here
     column = (of % rode) // users_here
@@ -310,23 +320,21 @@
 
 
 def context_kernel(where, keep, send, *refs):
-    firsts, seconds = (refs[0:2], refs[6:8]), (refs[2:6], refs[8:12])
-    context_grad = refs[12]
+    firsts, seconds = (refs[0:2], refs[4:6]), (refs[2:4], refs[6:8])
+    context_grad = refs[8]
     part = keep.shape[1] // 2
     block = context_grad.shape[1] // 8
     near = [ref[:, :part] for ref in (keep, send)]
     far = [ref[:, part:] for ref in (keep, send)]
     from_first = [
-        sum(contract_last(near[s], weight_rows(firsts[s][ry], block)) for s in range(2))
-        for ry in range(2)
+        sum(contract_last(near[s], weight_rows(firsts[s][r3], block)) for s in range(2))
+        for r3 in range(2)
     ]
-    for q in range(4):
-        from_second = sum(contract_last(far[s], seconds[s][q][...]) for s in range(2))
-        for ry in range(2):
-            value = (
-                from_first[ry][:, q * block : (q + 1) * block]
-                + from_second[:, ry * block : (ry + 1) * block]
-            )
+    for ry in range(2):
+        from_second = sum(contract_last(far[s], seconds[s][ry][...]) for s in range(2))
+        for q in range(4):
+            b = ((q % 2) * 2 + ry) * block
+            value = from_first[q // 2][:, b : b + block] + from_second[:, q * block : (q + 1) * block]
             home = block_home(where[0], where[1] // 2, q, ry)
             context_grad[:, pl.ds(pl.multiple_of(home * block, block), block)] = value.astype(BF16)
 
@@ -391,26 +399,32 @@
         compiler_params=params(6),
         name="pack",
     )(out_weight, user_vectors)
-    second = doubled(second, swap_y, 3)
-    first = jnp.concatenate(four(first, swap_x), axis=0)
-    first, second = lax.optimization_barrier((first, second))
-    pieces = [first, swap_y(first, 3)] + four(second, swap_x)
+    for (first_swap, n), (second_swap, m) in (
+        ((swap_y, 3), (swap_x, 1)),
+        ((swap_x, 1), (swap_x, 3)),
+    ):
+        first = jnp.concatenate([first, first_swap(first, n)], axis=0)
+        second = jnp.concatenate([second, second_swap(second, m)], axis=0)
+        first, second = lax.optimization_barrier((first, second))
+    first_far, second_far = lax.optimization_barrier((swap_x(first, 3), swap_y(second, 3)))
+    pieces = [first, first_far, second, second_far]
     pieces = pieces + [swap_core(p) for p in pieces]
+    ints = jnp.concatenate([where, lengths, item_ids, item_counts, positive])
 
     stream, inverse, pooled, emb = pl.pallas_call(
-        forward_kernel,
+        functools.partial(forward_kernel, items_here),
         out_shape=(
             shaped((tokens, width)),
             shaped((tokens, 1)),
             shaped((items_here, width)),
             shaped((items_here, width + LABELS), BF16),
         ),
-        in_specs=[SMEM] * 5 + [VMEM, HBM] + [VMEM] * 13,
+        in_specs=[SMEM, VMEM, HBM] + [VMEM] * 9,
         out_specs=(VMEM,) * 4,
         scratch_shapes=[pltpu.VMEM((tokens, width), BF16), pltpu.SemaphoreType.DMA],
         compiler_params=params(20),
         name="forward",
-    )(where, lengths, item_ids, item_counts, positive, context, residual, gain, *pieces)
+    )(ints, context, residual, gain, *pieces)
 
     emb = lax.optimization_barrier(jnp.concatenate(four(emb, swap_x), axis=0))
     peer_context = swap_core(after(context, emb))
@@ -419,7 +433,7 @@
     emb_pieces = emb_pieces + [swap_core(p) for p in emb_pieces]
 
     items, people = 128 * items_here, 16 * users_here
-    riding = pieces[0:2] + pieces[6:8]
+    riding = pieces[0:2] + pieces[4:6]
     *sums, user_grad = pl.pallas_call(
         functools.partial(loss_kernel, users_here, items_here, rows),
         out_shape=(shaped((8, width)),) * 4 + (shaped((users_here, width), BF16),),
@@ -455,7 +469,7 @@
     context_grad = pl.pallas_call(
         context_kernel,
         out_shape=shaped((tokens, head), BF16),
-        in_specs=[SMEM] + [VMEM] * 14,
+        in_specs=[SMEM] + [VMEM] * 10,
         out_specs=VMEM,
         compiler_params=params(14),
         name="context",

time: 161 us -> 149 us (0.925)
  waiting for transfers between devices: 60.5 us -> 47.3 us
  starting transfers between devices: 69.1 us -> 71.2 us
    ppermute x48 -> x44, waiting for transfers between devices: 60.5 us -> 47.3 us  [move(): return lax.ppermute(value, AXES, perm)]
    ppermute x48 -> x44, starting transfers between devices: 69.1 us -> 71.2 us  [move(): return lax.ppermute(value, AXES, perm)]
    unnamed x18 -> x12, local copies, waits for them, and re-layouts: 4.79 us -> 3.48 us
  transfers between devices with their start and end apart: 48 -> 44, of which waited for: 28 -> 28; matrix products, arithmetic and copies ran while one was open for 1% -> 1% of each run, Pallas kernels for 6% -> 7%
where the time goes in v6:
time: 149 us
  starting transfers between devices  71.2 us (48%)
  waiting for transfers between devices  47.3 us (32%)
  Pallas kernels  22.9 us (15%)
  local copies, waits for them, and re-layouts  4.29 us (3%)
  other arithmetic  2.05 us (1%)
    ppermute x44, starting transfers between devices, move(): return lax.ppermute(value, AXES, perm)  71.2 us
    ppermute x44, waiting for transfers between devices, move(): return lax.ppermute(value, AXES, perm)  47.3 us
    pallas_call x1, Pallas kernels, on_device(): pl.pallas_call(functools.partial(loss_kernel, users_here, items_here, row...  5.62 us
    pallas_call x1, Pallas kernels, on_device(): pl.pallas_call(functools.partial(forward_kernel, items_here), out_shape=(...  5.4 us
    pallas_call x1, Pallas kernels, on_device(): pl.pallas_call(context_kernel, out_shape=shaped((tokens, head), BF16), in...  5.11 us
    pallas_call x2, Pallas kernels, blocks(): pl.pallas_call(functools.partial(blocks_kernel, kept), out_shape=(shaped(...  3.73 us
    unnamed x12, local copies, waits for them, and re-layouts  3.48 us
    pallas_call x1, Pallas kernels, on_device(): pl.pallas_call(functools.partial(residual_kernel, 8 * people), out_shape=...  3.02 us
  transfers between devices with their start and end apart: 44, of which 28 were waited for; matrix products, arithmetic and copies ran while one was open for 1% of the time, Pallas kernels for 7%

profile of v6, /device:TPU:1, one launch (start us, length us, event | category | flops | bytes accessed | tf_op | source)
XLA Modules:
  0.0 148.6 jit_solution(5670751157772543797)
XLA Ops:
  0.7 1.1 copy-done.2
  1.8 0.8 copy-done.4
  2.6 2.1 %collective-permute-start.1 = (bf16[128,512]{1,0:T(8,128)(2,1)S(1)}, bf16[128,512]{1,0:T(8,128)(2,1)S(1)}, u32[]{:S(2)}, u32[]{:S(2)}) collective-permute-start(bf16[128,512]{1,0:T(8,128)(2,1)S(1)} %get-tuple-element.39), channel_id=1, source_target_pairs={{0,1},{8,9},{16,17},{24,25},{32,33},{40,41},{48,49},{56,57},{64,65... | collective-permute-start | bytes 393224 | tf_op jit(solution)/shard_map/ppermute | solution.py:44
  4.7 2.7 %collective-permute-start = (bf16[160,512]{1,0:T(8,128)(2,1)S(1)}, bf16[160,512]{1,0:T(8,128)(2,1)S(1)}, u32[]{:S(2)}, u32[]{:S(2)}) collective-permute-start(bf16[160,512]{1,0:T(8,128)(2,1)S(1)} %get-tuple-element.38), channel_id=1, source_target_pairs={{0,68},{8,76},{16,84},{24,92},{32,100},{40,108},{48,116},{56,124},... | collective-permute-start | bytes 491528 | tf_op jit(solution)/shard_map/ppermute | solution.py:44
  7.4 3.3 %collective-permute-done = bf16[160,512]{1,0:T(8,128)(2,1)S(1)} collective-permute-done((bf16[160,512]{1,0:T(8,128)(2,1)S(1)}, bf16[160,512]{1,0:T(8,128)(2,1)S(1)}, u32[]{:S(2)}, u32[]{:S(2)}) %collective-permute-start) | collective-permute-done | bytes 163872 | tf_op jit(solution)/shard_map/ppermute | solution.py:44
  10.8 1.9 %collective-permute-start.3 = (bf16[256,512]{1,0:T(8,128)(2,1)S(1)}, bf16[256,512]{1,0:T(8,128)(2,1)S(1)}, u32[]{:S(2)}, u32[]{:S(2)}) collective-permute-start(bf16[256,512]{1,0:T(8,128)(2,1)S(1)} %pad_maximum_fusion.3), channel_id=1, source_target_pairs={{0,3},{8,11},{16,19},{24,27},{32,35},{40,43},{48,51},{56,59},{64,6... | collective-permute-start | bytes 786440 | tf_op jit(solution)/shard_map/ppermute | solution.py:44
  13.0 5.1 %collective-permute-done.3 = bf16[256,512]{1,0:T(8,128)(2,1)S(1)} collective-permute-done((bf16[256,512]{1,0:T(8,128)(2,1)S(1)}, bf16[256,512]{1,0:T(8,128)(2,1)S(1)}, u32[]{:S(2)}, u32[]{:S(2)}) %collective-permute-start.3) | collective-permute-done | bytes 262176 | tf_op jit(solution)/shard_map/ppermute | solution.py:44
  18.1 1.7 %collective-permute-done.2 = bf16[320,512]{1,0:T(8,128)(2,1)S(1)} collective-permute-done((bf16[320,512]{1,0:T(8,128)(2,1)S(1)}, bf16[320,512]{1,0:T(8,128)(2,1)S(1)}, u32[]{:S(2)}, u32[]{:S(2)}) %collective-permute-start.2) | collective-permute-done | bytes 327712 | tf_op jit(solution)/shard_map/ppermute | solution.py:44
  19.9 0.9 collective-permute-start.4
  20.8 2.5 %collective-permute-start.5 = (bf16[512,512]{1,0:T(8,128)(2,1)S(1)}, bf16[512,512]{1,0:T(8,128)(2,1)}, u32[]{:S(2)}, u32[]{:S(2)}) collective-permute-start(bf16[512,512]{1,0:T(8,128)(2,1)S(1)} %pad_maximum_fusion.1.refs_2_), channel_id=1, source_target_pairs={{0,68},{8,76},{16,84},{24,92},{32,100},{40,108},{48,116},{56,124},... | collective-permute-start | bytes 1572872 | tf_op jit(solution)/shard_map/ppermute | solution.py:44
  23.3 3.6 %collective-permute-start.6 = (bf16[640,512]{1,0:T(8,128)(2,1)S(1)}, bf16[640,512]{1,0:T(8,128)(2,1)S(1)}, u32[]{:S(2)}, u32[]{:S(2)}) collective-permute-start(bf16[640,512]{1,0:T(8,128)(2,1)S(1)} %pad_maximum_fusion.refs_0_), channel_id=1, source_target_pairs={{0,8},{8,0},{16,24},{24,16},{32,40},{40,32},{48,56},{56,48},{64,72... | collective-permute-start | bytes 1966088 | tf_op jit(solution)/shard_map/ppermute | solution.py:44
  27.0 5.3 %collective-permute-done.5.refs_3_ = bf16[512,512]{1,0:T(8,128)(2,1)} collective-permute-done((bf16[512,512]{1,0:T(8,128)(2,1)S(1)}, bf16[512,512]{1,0:T(8,128)(2,1)}, u32[]{:S(2)}, u32[]{:S(2)}) %collective-permute-start.5) | collective-permute-done | bytes 524320 | tf_op jit(solution)/shard_map/ppermute | solution.py:44
  32.3 2.2 %collective-permute-done.4.refs_1_ = bf16[640,512]{1,0:T(8,128)(2,1)S(1)} collective-permute-done((bf16[640,512]{1,0:T(8,128)(2,1)S(1)}, bf16[640,512]{1,0:T(8,128)(2,1)S(1)}, u32[]{:S(2)}, u32[]{:S(2)}) %collective-permute-start.4) | collective-permute-done | bytes 655392 | tf_op jit(solution)/shard_map/ppermute | solution.py:44
  34.5 3.8 %collective-permute-start.7 = (bf16[640,512]{1,0:T(8,128)(2,1)S(1)}, bf16[640,512]{1,0:T(8,128)(2,1)}, u32[]{:S(2)}, u32[]{:S(2)}) collective-permute-start(bf16[640,512]{1,0:T(8,128)(2,1)S(1)} %collective-permute-done.4.refs_1_), channel_id=1, source_target_pairs={{0,8},{8,0},{16,24},{24,16},{32,40},{40,32},{48,56},{56,48},{64,72... | collective-permute-start | bytes 1966088 | tf_op jit(solution)/shard_map/ppermute | solution.py:44
  38.8 0.8 concatenate.34.ints
  39.6 2.1 %collective-permute-done.8.refs_6_ = bf16[512,512]{1,0:T(8,128)(2,1)} collective-permute-done((bf16[512,512]{1,0:T(8,128)(2,1)S(1)}, bf16[512,512]{1,0:T(8,128)(2,1)}, u32[]{:S(2)}, u32[]{:S(2)}) %collective-permute-start.8) | collective-permute-done | bytes 524320 | tf_op jit(solution)/shard_map/ppermute | solution.py:44
  41.9 1.6 %copy-done.1 = bf16[512,2048]{1,0:T(8,128)(2,1)S(1)} copy-done((bf16[512,2048]{1,0:T(8,128)(2,1)S(1)}, bf16[512,2048]{1,0:T(8,128)(2,1)}, u32[]{:S(2)}) %copy-start.1) | copy-done | bytes 2097176
  43.5 5.4 %forward.1 = (f32[512,2048]{1,0:T(8,128)S(1)}, f32[512,1]{1,0:T(8,128)S(1)}, f32[2,2048]{1,0:T(2,128)S(1)}, bf16[2,2176]{1,0:T(2,128)(2,1)S(1)}) custom-call(s32[18]{0:T(128)S(1)} %concatenate.34.ints, bf16[512,1024]{1,0:T(8,128)(2,1)S(1)} %copy-done, bf16[512,2048]{1,0:T(8,128)(2,1)S(1)} %copy-done.1, f32[1,2048]{1,0:T(1,128)S(1)} %bitcast.7, ...), custom_call_target="tpu_custom_call" | custom-call | tf_op jit(solution)/shard_map/forward/pallas_call | solution.py:414
  49.0 1.5 %collective-permute-start.11 = (bf16[2,2176]{1,0:T(2,128)(2,1)S(1)}, bf16[2,2176]{1,0:T(2,128)(2,1)S(1)}, u32[]{:S(2)}, u32[]{:S(2)}) collective-permute-start(bf16[2,2176]{1,0:T(2,128)(2,1)S(1)} %get-tuple-element.49), channel_id=1, source_target_pairs={{0,3},{8,11},{16,19},{24,27},{32,35},{40,43},{48,51},{56,59},{64,6... | collective-permute-start | bytes 26120 | tf_op jit(solution)/shard_map/ppermute | solution.py:44
  50.5 1.1 collective-permute-start.10
  51.6 1.4 collective-permute-done.12
  53.3 1.6 %collective-permute-start.15 = (bf16[8,2176]{1,0:T(8,128)(2,1)S(1)}, bf16[8,2176]{1,0:T(8,128)(2,1)S(1)}, u32[]{:S(2)}, u32[]{:S(2)}) collective-permute-start(bf16[8,2176]{1,0:T(8,128)(2,1)S(1)} %pad_maximum_fusion.6), channel_id=1, source_target_pairs={{0,4},{8,12},{16,20},{24,28},{32,36},{40,44},{48,52},{56,60},{64,6... | collective-permute-start | bytes 104456 | tf_op jit(solution)/shard_map/ppermute | solution.py:44
  54.9 1.1 collective-permute-start.14
  56.5 1.2 collective-permute-done.15
  57.7 1.2 collective-permute-done.14
  58.9 3.7 %collective-permute-start.18 = (bf16[32,2176]{1,0:T(8,128)(2,1)S(1)}, bf16[32,2176]{1,0:T(8,128)(2,1)S(1)}, u32[]{:S(2)}, u32[]{:S(2)}) collective-permute-start(bf16[32,2176]{1,0:T(8,128)(2,1)S(1)} %pad_maximum_fusion.5.refs_4_), channel_id=1, source_target_pairs={{0,32},{8,40},{16,48},{24,56},{32,0},{40,8},{48,16},{56,24},{64,96... | collective-permute-start | bytes 417800 | tf_op jit(solution)/shard_map/ppermute | solution.py:44
  63.3 3.8 %collective-permute-start.19 = (bf16[32,2176]{1,0:T(8,128)(2,1)S(1)}, bf16[32,2176]{1,0:T(8,128)(2,1)S(1)}, u32[]{:S(2)}, u32[]{:S(2)}) collective-permute-start(bf16[32,2176]{1,0:T(8,128)(2,1)S(1)} %pad_maximum_fusion.5.refs_4_), channel_id=1, source_target_pairs={{0,8},{8,0},{16,24},{24,16},{32,40},{40,32},{48,56},{56,48},{64,72... | collective-permute-start | bytes 417800 | tf_op jit(solution)/shard_map/ppermute | solution.py:44
  67.1 3.1 %collective-permute-start.22 = (bf16[32,2176]{1,0:T(8,128)(2,1)S(1)}, bf16[32,2176]{1,0:T(8,128)(2,1)S(1)}, u32[]{:S(2)}, u32[]{:S(2)}) collective-permute-start(bf16[32,2176]{1,0:T(8,128)(2,1)S(1)} %collective-permute-done.18.refs_7_), channel_id=1, source_target_pairs={{0,8},{8,0},{16,24},{24,16},{32,40},{40,32},{48,56},{56,48},{64,72... | collective-permute-start | bytes 417800 | tf_op jit(solution)/shard_map/ppermute | solution.py:44
  70.3 2.1 %collective-permute-start.21 = (bf16[32,2176]{1,0:T(8,128)(2,1)S(1)}, bf16[32,2176]{1,0:T(8,128)(2,1)S(1)}, u32[]{:S(2)}, u32[]{:S(2)}) collective-permute-start(bf16[32,2176]{1,0:T(8,128)(2,1)S(1)} %collective-permute-done.17.refs_6_), channel_id=1, source_target_pairs={{0,8},{8,0},{16,24},{24,16},{32,40},{40,32},{48,56},{56,48},{64,72... | collective-permute-start | bytes 417800 | tf_op jit(solution)/shard_map/ppermute | solution.py:44
  72.5 0.9 collective-permute-done.21.refs_10_
  73.7 5.6 %loss.1 = (f32[8,2048]{1,0:T(8,128)S(1)}, f32[8,2048]{1,0:T(8,128)S(1)}, f32[8,2048]{1,0:T(8,128)S(1)}, f32[8,2048]{1,0:T(8,128)S(1)}, bf16[8,2048]{1,0:T(8,128)(2,1)}) custom-call(s32[4]{0:T(128)S(1)} %pad_add_fusion.where, f32[1,2048]{1,0:T(1,128)S(1)} %bitcast.8, bf16[640,512]{1,0:T(8,128)(2,1)S(1)} %pad_maximum_fusion.refs_0_, ...), custom_call_target="tpu_custom_call" | custom-call | tf_op jit(solution)/shard_map/loss/pallas_call | solution.py:437
  79.5 1.7 %collective-permute-start.24 = (f32[8,2048]{1,0:T(8,128)S(1)}, f32[8,2048]{1,0:T(8,128)S(1)}, u32[]{:S(2)}, u32[]{:S(2)}) collective-permute-start(f32[8,2048]{1,0:T(8,128)S(1)} %get-tuple-element.52), channel_id=1, source_target_pairs={{0,48},{8,56},{16,32},{24,40},{32,16},{40,24},{48,0},{56,8},{64,11... | collective-permute-start | bytes 196616 | tf_op jit(solution)/shard_map/ppermute | solution.py:44
  81.2 1.5 %collective-permute-start.25 = (f32[8,2048]{1,0:T(8,128)S(1)}, f32[8,2048]{1,0:T(8,128)S(1)}, u32[]{:S(2)}, u32[]{:S(2)}) collective-permute-start(f32[8,2048]{1,0:T(8,128)S(1)} %get-tuple-element.53), channel_id=1, source_target_pairs={{0,32},{8,40},{16,48},{24,56},{32,0},{40,8},{48,16},{56,24},{64,96... | collective-permute-start | bytes 196616 | tf_op jit(solution)/shard_map/ppermute | solution.py:44
  82.9 1.3 collective-permute-done.24
  84.2 1.6 %collective-permute-done.25 = f32[8,2048]{1,0:T(8,128)S(1)} collective-permute-done((f32[8,2048]{1,0:T(8,128)S(1)}, f32[8,2048]{1,0:T(8,128)S(1)}, u32[]{:S(2)}, u32[]{:S(2)}) %collective-permute-start.25) | collective-permute-done | bytes 65568 | tf_op jit(solution)/shard_map/ppermute | solution.py:44
  86.3 2.1 %collective-permute-start.27 = (bf16[512,1024]{1,0:T(8,128)(2,1)S(1)}, bf16[512,1024]{1,0:T(8,128)(2,1)S(1)}, u32[]{:S(2)}, u32[]{:S(2)}) collective-permute-start(bf16[512,1024]{1,0:T(8,128)(2,1)S(1)} %copy-done), channel_id=1, source_target_pairs={{0,8},{8,0},{16,24},{24,16},{32,40},{40,32},{48,56},{56,48},{64,72... | collective-permute-start | bytes 3145736 | tf_op jit(solution)/shard_map/ppermute | solution.py:44
  89.0 3.0 %residual.3 = (bf16[512,2048]{1,0:T(8,128)(2,1)}, bf16[512,1024]{1,0:T(8,128)(2,1)S(1)}, bf16[512,1024]{1,0:T(8,128)(2,1)S(1)}, f32[1,2048]{1,0:T(1,128)}, f32[1,1]{1,0:T(1,128)}) custom-call(s32[4]{0:T(128)S(1)} %pad_add_fusion.where, s32[2]{0:T(128)S(1)} %copy-done.5, f32[512,2048]{1,0:T(8,128)S(1)} %get-tuple-element.46.stream, ...), custom_call_target="tpu_custom_call" | custom-call | tf_op jit(solution)/shard_map/residual/pallas_call | solution.py:454
  92.0 3.0 %collective-permute-start.28 = (bf16[512,1024]{1,0:T(8,128)(2,1)S(1)}, bf16[512,1024]{1,0:T(8,128)(2,1)S(1)}, u32[]{:S(2)}, u32[]{:S(2)}) collective-permute-start(bf16[512,1024]{1,0:T(8,128)(2,1)S(1)} %get-tuple-element.58.send), channel_id=1, source_target_pairs={{0,8},{8,0},{16,24},{24,16},{32,40},{40,32},{48,56},{56,48},{64,72... | collective-permute-start | bytes 3145736 | tf_op jit(solution)/shard_map/ppermute | solution.py:44
  95.0 2.3 %collective-permute-done.28.peer_grad = bf16[512,1024]{1,0:T(8,128)(2,1)S(1)} collective-permute-done((bf16[512,1024]{1,0:T(8,128)(2,1)S(1)}, bf16[512,1024]{1,0:T(8,128)(2,1)S(1)}, u32[]{:S(2)}, u32[]{:S(2)}) %collective-permute-start.28) | collective-permute-done | bytes 1048608 | tf_op jit(solution)/shard_map/ppermute | solution.py:44
  97.3 2.1 %blocks_sent.1 = (bf16[512,512]{1,0:T(8,128)(2,1)S(1)}, bf16[256,512]{1,0:T(8,128)(2,1)S(1)}, bf16[256,512]{1,0:T(8,128)(2,1)S(1)}, bf16[256,512]{1,0:T(8,128)(2,1)S(1)}) custom-call(s32[4]{0:T(128)S(1)} %pad_add_fusion.where, bf16[512,1024]{1,0:T(8,128)(2,1)S(1)} %copy-done, bf16[512,1024]{1,0:T(8,128)(2,1)S(1)} %collective-permute-done.27.peer_context, ...), custom_call_target="tpu_custom_call" | custom-call | tf_op jit(solution)/shard_map/blocks_sent/pallas_call | solution.py:482
  99.4 1.2 collective-permute-start.36
  100.7 0.8 collective-permute-start.37
  101.5 1.3 collective-permute-start.38
  102.8 1.8 %collective-permute-start.29 = (bf16[512,512]{1,0:T(8,128)(2,1)S(1)}, bf16[512,512]{1,0:T(8,128)(2,1)S(1)}, u32[]{:S(2)}, u32[]{:S(2)}) collective-permute-start(bf16[512,512]{1,0:T(8,128)(2,1)S(1)} %get-tuple-element.63), channel_id=1, source_target_pairs={{0,68},{8,76},{16,84},{24,92},{32,100},{40,108},{48,116},{56,124},... | collective-permute-start | bytes 1572872 | tf_op jit(solution)/shard_map/ppermute | solution.py:44
  104.5 5.1 %context.3 = bf16[512,1024]{1,0:T(8,128)(2,1)} custom-call(s32[4]{0:T(128)S(1)} %pad_add_fusion.where, bf16[512,1024]{1,0:T(8,128)(2,1)S(1)} %get-tuple-element.57.own_grad.keep, bf16[512,1024]{1,0:T(8,128)(2,1)S(1)} %get-tuple-element.58.send, bf16[640,512]{1,0:T(8,128)(2,1)S(1)} %pad_maximum_fusion.refs_0_, ...), custom_call_target="tpu_custom_call" | custom-call | tf_op jit(solution)/shard_map/context/pallas_call | solution.py:469
  109.7 1.6 %blocks_kept.1 = (f32[512,512]{1,0:T(8,128)S(1)}, f32[256,512]{1,0:T(8,128)S(1)}) custom-call(s32[4]{0:T(128)S(1)} %pad_add_fusion.where, bf16[512,1024]{1,0:T(8,128)(2,1)S(1)} %copy-done, bf16[512,1024]{1,0:T(8,128)(2,1)S(1)} %collective-permute-done.27.peer_context, bf16[512,1024]{1,0:T(8,128)(2,1)S(1)} %get-tuple-element.57.own_grad.keep, ...), custom_call_target="tpu_custom_call" | custom-call | tf_op jit(solution)/shard_map/blocks_kept/pallas_call | solution.py:482
  111.3 3.4 %collective-permute-done.37 = bf16[256,512]{1,0:T(8,128)(2,1)S(1)} collective-permute-done((bf16[256,512]{1,0:T(8,128)(2,1)S(1)}, bf16[256,512]{1,0:T(8,128)(2,1)S(1)}, u32[]{:S(2)}, u32[]{:S(2)}) %collective-permute-start.37) | collective-permute-done | bytes 262176 | tf_op jit(solution)/shard_map/ppermute | solution.py:44
  114.9 1.9 %collective-permute-start.39 = (bf16[128,512]{1,0:T(8,128)(2,1)S(1)}, bf16[128,512]{1,0:T(8,128)(2,1)S(1)}, u32[]{:S(2)}, u32[]{:S(2)}) collective-permute-start(bf16[128,512]{1,0:T(8,128)(2,1)S(1)} %slice.53), channel_id=1, source_target_pairs={{0,68},{8,76},{16,84},{24,92},{32,100},{40,108},{48,116},{56,124},... | collective-permute-start | bytes 393224 | tf_op jit(solution)/shard_map/ppermute | solution.py:44
  117.7 1.0 collective-permute-start.32
  118.7 2.3 %collective-permute-start.31 = (bf16[128,512]{1,0:T(8,128)(2,1)S(1)}, bf16[128,512]{1,0:T(8,128)(2,1)S(1)}, u32[]{:S(2)}, u32[]{:S(2)}) collective-permute-start(bf16[128,512]{1,0:T(8,128)(2,1)S(1)} %get-tuple-element.76), channel_id=1, source_target_pairs={{0,3},{8,11},{16,19},{24,27},{32,35},{40,43},{48,51},{56,59},{64,6... | collective-permute-start | bytes 393224 | tf_op jit(solution)/shard_map/ppermute | solution.py:44
  121.0 0.9 collective-permute-start.40
  121.9 1.8 %collective-permute-done.32 = bf16[128,512]{1,0:T(8,128)(2,1)S(1)} collective-permute-done((bf16[128,512]{1,0:T(8,128)(2,1)S(1)}, bf16[128,512]{1,0:T(8,128)(2,1)S(1)}, u32[]{:S(2)}, u32[]{:S(2)}) %collective-permute-start.32) | collective-permute-done | bytes 131104 | tf_op jit(solution)/shard_map/ppermute | solution.py:44
  123.7 0.7 collective-permute-done.31
  124.9 0.9 collective-permute-start.41
  125.8 2.8 %collective-permute-done.33 = bf16[128,512]{1,0:T(8,128)(2,1)S(1)} collective-permute-done((bf16[128,512]{1,0:T(8,128)(2,1)S(1)}, bf16[128,512]{1,0:T(8,128)(2,1)S(1)}, u32[]{:S(2)}, u32[]{:S(2)}) %collective-permute-start.33) | collective-permute-done | bytes 131104 | tf_op jit(solution)/shard_map/ppermute | solution.py:44
  128.7 1.0 collective-permute-start.34
  130.1 1.2 collective-permute-start.42
  131.3 1.5 %collective-permute-done.34 = bf16[128,512]{1,0:T(8,128)(2,1)S(1)} collective-permute-done((bf16[128,512]{1,0:T(8,128)(2,1)S(1)}, bf16[128,512]{1,0:T(8,128)(2,1)S(1)}, u32[]{:S(2)}, u32[]{:S(2)}) %collective-permute-start.34) | collective-permute-done | bytes 131104 | tf_op jit(solution)/shard_map/ppermute | solution.py:44
  132.9 1.0 collective-permute-start.35
  133.9 1.2 collective-permute-done.42
  135.2 2.9 %collective-permute-done.35 = bf16[128,512]{1,0:T(8,128)(2,1)S(1)} collective-permute-done((bf16[128,512]{1,0:T(8,128)(2,1)S(1)}, bf16[128,512]{1,0:T(8,128)(2,1)S(1)}, u32[]{:S(2)}, u32[]{:S(2)}) %collective-permute-start.35) | collective-permute-done | bytes 131104 | tf_op jit(solution)/shard_map/ppermute | solution.py:44
  138.2 8.3 %collective-permute-start.43 = (bf16[128,1024]{1,0:T(8,128)(2,1)S(1)}, bf16[128,1024]{1,0:T(8,128)(2,1)S(1)}, u32[]{:S(2)}, u32[]{:S(2)}) collective-permute-start(bf16[128,1024]{1,0:T(8,128)(2,1)S(1)} %pad_maximum_fusion.4), channel_id=1, source_target_pairs={{0,8},{8,0},{16,24},{24,16},{32,40},{40,32},{48,56},{56,48},{64,72... | collective-permute-start | bytes 786440 | tf_op jit(solution)/shard_map/ppermute | solution.py:44
  146.5 1.2 collective-permute-done.43
  147.7 0.9 maximum_select_fusion
  (66 shorter events, 7.1 us)
Async XLA Ops:
  0.6 41.2 %copy-start = (bf16[512,1024]{1,0:T(8,128)(2,1)S(1)}, bf16[512,1024]{1,0:T(8,128)(2,1)}, u32[]{:S(2)}) copy-start(bf16[512,1024]{1,0:T(8,128)(2,1)} %own_context.3) | copy-start | bytes 3145732
  0.6 1.1 copy-start.2
  1.8 0.8 copy-start.4
  2.5 36.3 %copy-start.5 = (s32[2]{0:T(128)S(1)}, s32[2]{0:T(128)}, u32[]{:S(2)}) copy-start(s32[2]{0:T(128)} %lengths.1) | copy-start | bytes 28
  2.5 39.3 %copy-start.3 = (f32[2048]{0:T(1024)S(1)}, f32[2048]{0:T(1024)}, u32[]{:S(2)}) copy-start(f32[2048]{0:T(1024)} %param.12) | copy-start | bytes 24580
  2.6 4.9 %collective-permute-start.1 = (bf16[128,512]{1,0:T(8,128)(2,1)S(1)}, bf16[128,512]{1,0:T(8,128)(2,1)S(1)}, u32[]{:S(2)}, u32[]{:S(2)}) collective-permute-start(bf16[128,512]{1,0:T(8,128)(2,1)S(1)} %get-tuple-element.39), channel_id=1, source_target_pairs={{0,1},{8,9},{16,17},{24,25},{32,33},{40,41},{48,49},{56,57},{64,65... | collective-permute-start | bytes 393224 | tf_op jit(solution)/shard_map/ppermute | solution.py:44
  4.7 6.1 %collective-permute-start = (bf16[160,512]{1,0:T(8,128)(2,1)S(1)}, bf16[160,512]{1,0:T(8,128)(2,1)S(1)}, u32[]{:S(2)}, u32[]{:S(2)}) collective-permute-start(bf16[160,512]{1,0:T(8,128)(2,1)S(1)} %get-tuple-element.38), channel_id=1, source_target_pairs={{0,68},{8,76},{16,84},{24,92},{32,100},{40,108},{48,116},{56,124},... | collective-permute-start | bytes 491528 | tf_op jit(solution)/shard_map/ppermute | solution.py:44
  10.8 7.3 %collective-permute-start.3 = (bf16[256,512]{1,0:T(8,128)(2,1)S(1)}, bf16[256,512]{1,0:T(8,128)(2,1)S(1)}, u32[]{:S(2)}, u32[]{:S(2)}) collective-permute-start(bf16[256,512]{1,0:T(8,128)(2,1)S(1)} %pad_maximum_fusion.3), channel_id=1, source_target_pairs={{0,3},{8,11},{16,19},{24,27},{32,35},{40,43},{48,51},{56,59},{64,6... | collective-permute-start | bytes 786440 | tf_op jit(solution)/shard_map/ppermute | solution.py:44
  12.7 7.1 %collective-permute-start.2 = (bf16[320,512]{1,0:T(8,128)(2,1)S(1)}, bf16[320,512]{1,0:T(8,128)(2,1)S(1)}, u32[]{:S(2)}, u32[]{:S(2)}) collective-permute-start(bf16[320,512]{1,0:T(8,128)(2,1)S(1)} %pad_maximum_fusion.2), channel_id=1, source_target_pairs={{0,1},{8,9},{16,17},{24,25},{32,33},{40,41},{48,49},{56,57},{64,65... | collective-permute-start | bytes 983048 | tf_op jit(solution)/shard_map/ppermute | solution.py:44
  19.9 14.6 %collective-permute-start.4 = (bf16[640,512]{1,0:T(8,128)(2,1)S(1)}, bf16[640,512]{1,0:T(8,128)(2,1)S(1)}, u32[]{:S(2)}, u32[]{:S(2)}) collective-permute-start(bf16[640,512]{1,0:T(8,128)(2,1)S(1)} %pad_maximum_fusion.refs_0_), channel_id=1, source_target_pairs={{0,3},{8,11},{16,19},{24,27},{32,35},{40,43},{48,51},{56,59},{64,6... | collective-permute-start | bytes 1966088 | tf_op jit(solution)/shard_map/ppermute | solution.py:44
  20.8 11.5 %collective-permute-start.5 = (bf16[512,512]{1,0:T(8,128)(2,1)S(1)}, bf16[512,512]{1,0:T(8,128)(2,1)}, u32[]{:S(2)}, u32[]{:S(2)}) collective-permute-start(bf16[512,512]{1,0:T(8,128)(2,1)S(1)} %pad_maximum_fusion.1.refs_2_), channel_id=1, source_target_pairs={{0,68},{8,76},{16,84},{24,92},{32,100},{40,108},{48,116},{56,124},... | collective-permute-start | bytes 1572872 | tf_op jit(solution)/shard_map/ppermute | solution.py:44
  23.3 18.3 %collective-permute-start.6 = (bf16[640,512]{1,0:T(8,128)(2,1)S(1)}, bf16[640,512]{1,0:T(8,128)(2,1)S(1)}, u32[]{:S(2)}, u32[]{:S(2)}) collective-permute-start(bf16[640,512]{1,0:T(8,128)(2,1)S(1)} %pad_maximum_fusion.refs_0_), channel_id=1, source_target_pairs={{0,8},{8,0},{16,24},{24,16},{32,40},{40,32},{48,56},{56,48},{64,72... | collective-permute-start | bytes 1966088 | tf_op jit(solution)/shard_map/ppermute | solution.py:44
  34.5 7.4 %collective-permute-start.7 = (bf16[640,512]{1,0:T(8,128)(2,1)S(1)}, bf16[640,512]{1,0:T(8,128)(2,1)}, u32[]{:S(2)}, u32[]{:S(2)}) collective-permute-start(bf16[640,512]{1,0:T(8,128)(2,1)S(1)} %collective-permute-done.4.refs_1_), channel_id=1, source_target_pairs={{0,8},{8,0},{16,24},{24,16},{32,40},{40,32},{48,56},{56,48},{64,72... | collective-permute-start | bytes 1966088 | tf_op jit(solution)/shard_map/ppermute | solution.py:44
  38.3 3.4 %collective-permute-start.8 = (bf16[512,512]{1,0:T(8,128)(2,1)S(1)}, bf16[512,512]{1,0:T(8,128)(2,1)}, u32[]{:S(2)}, u32[]{:S(2)}) collective-permute-start(bf16[512,512]{1,0:T(8,128)(2,1)S(1)} %pad_maximum_fusion.1.refs_2_), channel_id=1, source_target_pairs={{0,8},{8,0},{16,24},{24,16},{32,40},{40,32},{48,56},{56,48},{64,72... | collective-permute-start | bytes 1572872 | tf_op jit(solution)/shard_map/ppermute | solution.py:44
  38.3 3.6 %collective-permute-start.9 = (bf16[512,512]{1,0:T(8,128)(2,1)}, bf16[512,512]{1,0:T(8,128)(2,1)}, u32[]{:S(2)}, u32[]{:S(2)}) collective-permute-start(bf16[512,512]{1,0:T(8,128)(2,1)} %collective-permute-done.5.refs_3_), channel_id=1, source_target_pairs={{0,8},{8,0},{16,24},{24,16},{32,40},{40,32},{48,56},{56,48},{64,72... | collective-permute-start | bytes 1572872 | tf_op jit(solution)/shard_map/ppermute | solution.py:44
  41.9 1.6 %copy-start.1 = (bf16[512,2048]{1,0:T(8,128)(2,1)S(1)}, bf16[512,2048]{1,0:T(8,128)(2,1)}, u32[]{:S(2)}) copy-start(bf16[512,2048]{1,0:T(8,128)(2,1)} %residual.2) | copy-start | bytes 6291460
  48.9 4.1 %collective-permute-start.12 = (bf16[2,2176]{1,0:T(2,128)(2,1)S(1)}, bf16[2,2176]{1,0:T(2,128)(2,1)S(1)}, u32[]{:S(2)}, u32[]{:S(2)}) collective-permute-start(bf16[2,2176]{1,0:T(2,128)(2,1)S(1)} %get-tuple-element.49), channel_id=1, source_target_pairs={{0,2},{8,10},{16,18},{24,26},{32,34},{40,42},{48,50},{56,58},{64,6... | collective-permute-start | bytes 26120 | tf_op jit(solution)/shard_map/ppermute | solution.py:44
  49.0 4.0 %collective-permute-start.11 = (bf16[2,2176]{1,0:T(2,128)(2,1)S(1)}, bf16[2,2176]{1,0:T(2,128)(2,1)S(1)}, u32[]{:S(2)}, u32[]{:S(2)}) collective-permute-start(bf16[2,2176]{1,0:T(2,128)(2,1)S(1)} %get-tuple-element.49), channel_id=1, source_target_pairs={{0,3},{8,11},{16,19},{24,27},{32,35},{40,43},{48,51},{56,59},{64,6... | collective-permute-start | bytes 26120 | tf_op jit(solution)/shard_map/ppermute | solution.py:44
  50.5 2.8 %collective-permute-start.10 = (bf16[2,2176]{1,0:T(2,128)(2,1)S(1)}, bf16[2,2176]{1,0:T(2,128)(2,1)S(1)}, u32[]{:S(2)}, u32[]{:S(2)}) collective-permute-start(bf16[2,2176]{1,0:T(2,128)(2,1)S(1)} %get-tuple-element.49), channel_id=1, source_target_pairs={{0,1},{8,9},{16,17},{24,25},{32,33},{40,41},{48,49},{56,57},{64,65... | collective-permute-start | bytes 26120 | tf_op jit(solution)/shard_map/ppermute | solution.py:44
  53.3 4.4 %collective-permute-start.15 = (bf16[8,2176]{1,0:T(8,128)(2,1)S(1)}, bf16[8,2176]{1,0:T(8,128)(2,1)S(1)}, u32[]{:S(2)}, u32[]{:S(2)}) collective-permute-start(bf16[8,2176]{1,0:T(8,128)(2,1)S(1)} %pad_maximum_fusion.6), channel_id=1, source_target_pairs={{0,4},{8,12},{16,20},{24,28},{32,36},{40,44},{48,52},{56,60},{64,6... | collective-permute-start | bytes 104456 | tf_op jit(solution)/shard_map/ppermute | solution.py:44
  54.9 4.0 %collective-permute-start.14 = (bf16[8,2176]{1,0:T(8,128)(2,1)S(1)}, bf16[8,2176]{1,0:T(8,128)(2,1)S(1)}, u32[]{:S(2)}, u32[]{:S(2)}) collective-permute-start(bf16[8,2176]{1,0:T(8,128)(2,1)S(1)} %pad_maximum_fusion.6), channel_id=1, source_target_pairs={{0,68},{8,76},{16,84},{24,92},{32,100},{40,108},{48,116},{56,124},... | collective-permute-start | bytes 104456 | tf_op jit(solution)/shard_map/ppermute | solution.py:44
  56.0 2.9 %collective-permute-start.13 = (bf16[8,2176]{1,0:T(8,128)(2,1)S(1)}, bf16[8,2176]{1,0:T(8,128)(2,1)S(1)}, u32[]{:S(2)}, u32[]{:S(2)}) collective-permute-start(bf16[8,2176]{1,0:T(8,128)(2,1)S(1)} %pad_maximum_fusion.6), channel_id=1, source_target_pairs={{0,64},{8,72},{16,80},{24,88},{32,96},{40,104},{48,112},{56,120},{... | collective-permute-start | bytes 104456 | tf_op jit(solution)/shard_map/ppermute | solution.py:44
  58.9 8.2 %collective-permute-start.18 = (bf16[32,2176]{1,0:T(8,128)(2,1)S(1)}, bf16[32,2176]{1,0:T(8,128)(2,1)S(1)}, u32[]{:S(2)}, u32[]{:S(2)}) collective-permute-start(bf16[32,2176]{1,0:T(8,128)(2,1)S(1)} %pad_maximum_fusion.5.refs_4_), channel_id=1, source_target_pairs={{0,32},{8,40},{16,48},{24,56},{32,0},{40,8},{48,16},{56,24},{64,96... | collective-permute-start | bytes 417800 | tf_op jit(solution)/shard_map/ppermute | solution.py:44
  62.6 7.7 %collective-permute-start.17 = (bf16[32,2176]{1,0:T(8,128)(2,1)S(1)}, bf16[32,2176]{1,0:T(8,128)(2,1)S(1)}, u32[]{:S(2)}, u32[]{:S(2)}) collective-permute-start(bf16[32,2176]{1,0:T(8,128)(2,1)S(1)} %pad_maximum_fusion.5.refs_4_), channel_id=1, source_target_pairs={{0,48},{8,56},{16,32},{24,40},{32,16},{40,24},{48,0},{56,8},{64,11... | collective-permute-start | bytes 417800 | tf_op jit(solution)/shard_map/ppermute | solution.py:44
  63.0 9.3 %collective-permute-start.16 = (bf16[32,2176]{1,0:T(8,128)(2,1)S(1)}, bf16[32,2176]{1,0:T(8,128)(2,1)S(1)}, u32[]{:S(2)}, u32[]{:S(2)}) collective-permute-start(bf16[32,2176]{1,0:T(8,128)(2,1)S(1)} %pad_maximum_fusion.5.refs_4_), channel_id=1, source_target_pairs={{0,16},{8,24},{16,0},{24,8},{32,48},{40,56},{48,32},{56,40},{64,80... | collective-permute-start | bytes 417800 | tf_op jit(solution)/shard_map/ppermute | solution.py:44
  63.3 9.1 %collective-permute-start.19 = (bf16[32,2176]{1,0:T(8,128)(2,1)S(1)}, bf16[32,2176]{1,0:T(8,128)(2,1)S(1)}, u32[]{:S(2)}, u32[]{:S(2)}) collective-permute-start(bf16[32,2176]{1,0:T(8,128)(2,1)S(1)} %pad_maximum_fusion.5.refs_4_), channel_id=1, source_target_pairs={{0,8},{8,0},{16,24},{24,16},{32,40},{40,32},{48,56},{56,48},{64,72... | collective-permute-start | bytes 417800 | tf_op jit(solution)/shard_map/ppermute | solution.py:44
  67.1 5.3 %collective-permute-start.22 = (bf16[32,2176]{1,0:T(8,128)(2,1)S(1)}, bf16[32,2176]{1,0:T(8,128)(2,1)S(1)}, u32[]{:S(2)}, u32[]{:S(2)}) collective-permute-start(bf16[32,2176]{1,0:T(8,128)(2,1)S(1)} %collective-permute-done.18.refs_7_), channel_id=1, source_target_pairs={{0,8},{8,0},{16,24},{24,16},{32,40},{40,32},{48,56},{56,48},{64,72... | collective-permute-start | bytes 417800 | tf_op jit(solution)/shard_map/ppermute | solution.py:44
  70.3 3.1 %collective-permute-start.21 = (bf16[32,2176]{1,0:T(8,128)(2,1)S(1)}, bf16[32,2176]{1,0:T(8,128)(2,1)S(1)}, u32[]{:S(2)}, u32[]{:S(2)}) collective-permute-start(bf16[32,2176]{1,0:T(8,128)(2,1)S(1)} %collective-permute-done.17.refs_6_), channel_id=1, source_target_pairs={{0,8},{8,0},{16,24},{24,16},{32,40},{40,32},{48,56},{56,48},{64,72... | collective-permute-start | bytes 417800 | tf_op jit(solution)/shard_map/ppermute | solution.py:44
  72.4 1.4 collective-permute-start.20
  79.4 3.6 %collective-permute-start.23 = (f32[8,2048]{1,0:T(8,128)S(1)}, f32[8,2048]{1,0:T(8,128)S(1)}, u32[]{:S(2)}, u32[]{:S(2)}) collective-permute-start(f32[8,2048]{1,0:T(8,128)S(1)} %get-tuple-element.51), channel_id=1, source_target_pairs={{0,16},{8,24},{16,0},{24,8},{32,48},{40,56},{48,32},{56,40},{64,80... | collective-permute-start | bytes 196616 | tf_op jit(solution)/shard_map/ppermute | solution.py:44
  79.5 4.8 %collective-permute-start.24 = (f32[8,2048]{1,0:T(8,128)S(1)}, f32[8,2048]{1,0:T(8,128)S(1)}, u32[]{:S(2)}, u32[]{:S(2)}) collective-permute-start(f32[8,2048]{1,0:T(8,128)S(1)} %get-tuple-element.52), channel_id=1, source_target_pairs={{0,48},{8,56},{16,32},{24,40},{32,16},{40,24},{48,0},{56,8},{64,11... | collective-permute-start | bytes 196616 | tf_op jit(solution)/shard_map/ppermute | solution.py:44
  81.2 4.6 %collective-permute-start.25 = (f32[8,2048]{1,0:T(8,128)S(1)}, f32[8,2048]{1,0:T(8,128)S(1)}, u32[]{:S(2)}, u32[]{:S(2)}) collective-permute-start(f32[8,2048]{1,0:T(8,128)S(1)} %get-tuple-element.53), channel_id=1, source_target_pairs={{0,32},{8,40},{16,48},{24,56},{32,0},{40,8},{48,16},{56,24},{64,96... | collective-permute-start | bytes 196616 | tf_op jit(solution)/shard_map/ppermute | solution.py:44
  85.8 3.2 %collective-permute-start.26 = (f32[8,2048]{1,0:T(8,128)S(1)}, f32[8,2048]{1,0:T(8,128)S(1)}, u32[]{:S(2)}, u32[]{:S(2)}) collective-permute-start(f32[8,2048]{1,0:T(8,128)S(1)} %add_add_fusion.refs_0_), channel_id=1, source_target_pairs={{0,64},{8,72},{16,80},{24,88},{32,96},{40,104},{48,112},{56,120},{... | collective-permute-start | bytes 196616 | tf_op jit(solution)/shard_map/ppermute | solution.py:44
  86.3 8.7 %collective-permute-start.27 = (bf16[512,1024]{1,0:T(8,128)(2,1)S(1)}, bf16[512,1024]{1,0:T(8,128)(2,1)S(1)}, u32[]{:S(2)}, u32[]{:S(2)}) collective-permute-start(bf16[512,1024]{1,0:T(8,128)(2,1)S(1)} %copy-done), channel_id=1, source_target_pairs={{0,8},{8,0},{16,24},{24,16},{32,40},{40,32},{48,56},{56,48},{64,72... | collective-permute-start | bytes 3145736 | tf_op jit(solution)/shard_map/ppermute | solution.py:44
  92.0 5.3 %collective-permute-start.28 = (bf16[512,1024]{1,0:T(8,128)(2,1)S(1)}, bf16[512,1024]{1,0:T(8,128)(2,1)S(1)}, u32[]{:S(2)}, u32[]{:S(2)}) collective-permute-start(bf16[512,1024]{1,0:T(8,128)(2,1)S(1)} %get-tuple-element.58.send), channel_id=1, source_target_pairs={{0,8},{8,0},{16,24},{24,16},{32,40},{40,32},{48,56},{56,48},{64,72... | collective-permute-start | bytes 3145736 | tf_op jit(solution)/shard_map/ppermute | solution.py:44
  99.4 11.8 %collective-permute-start.36 = (bf16[256,512]{1,0:T(8,128)(2,1)S(1)}, bf16[256,512]{1,0:T(8,128)(2,1)S(1)}, u32[]{:S(2)}, u32[]{:S(2)}) collective-permute-start(bf16[256,512]{1,0:T(8,128)(2,1)S(1)} %get-tuple-element.65), channel_id=1, source_target_pairs={{0,1},{8,9},{16,17},{24,25},{32,33},{40,41},{48,49},{56,57},{64,65... | collective-permute-start | bytes 786440 | tf_op jit(solution)/shard_map/ppermute | solution.py:44
  100.7 14.0 %collective-permute-start.37 = (bf16[256,512]{1,0:T(8,128)(2,1)S(1)}, bf16[256,512]{1,0:T(8,128)(2,1)S(1)}, u32[]{:S(2)}, u32[]{:S(2)}) collective-permute-start(bf16[256,512]{1,0:T(8,128)(2,1)S(1)} %get-tuple-element.66), channel_id=1, source_target_pairs={{0,3},{8,11},{16,19},{24,27},{32,35},{40,43},{48,51},{56,59},{64,6... | collective-permute-start | bytes 786440 | tf_op jit(solution)/shard_map/ppermute | solution.py:44
  101.5 13.2 %collective-permute-start.38 = (bf16[256,512]{1,0:T(8,128)(2,1)S(1)}, bf16[256,512]{1,0:T(8,128)(2,1)S(1)}, u32[]{:S(2)}, u32[]{:S(2)}) collective-permute-start(bf16[256,512]{1,0:T(8,128)(2,1)S(1)} %get-tuple-element.67), channel_id=1, source_target_pairs={{0,2},{8,10},{16,18},{24,26},{32,34},{40,42},{48,50},{56,58},{64,6... | collective-permute-start | bytes 786440 | tf_op jit(solution)/shard_map/ppermute | solution.py:44
  102.8 14.0 %collective-permute-start.29 = (bf16[512,512]{1,0:T(8,128)(2,1)S(1)}, bf16[512,512]{1,0:T(8,128)(2,1)S(1)}, u32[]{:S(2)}, u32[]{:S(2)}) collective-permute-start(bf16[512,512]{1,0:T(8,128)(2,1)S(1)} %get-tuple-element.63), channel_id=1, source_target_pairs={{0,68},{8,76},{16,84},{24,92},{32,100},{40,108},{48,116},{56,124},... | collective-permute-start | bytes 1572872 | tf_op jit(solution)/shard_map/ppermute | solution.py:44
  114.9 6.0 %collective-permute-start.39 = (bf16[128,512]{1,0:T(8,128)(2,1)S(1)}, bf16[128,512]{1,0:T(8,128)(2,1)S(1)}, u32[]{:S(2)}, u32[]{:S(2)}) collective-permute-start(bf16[128,512]{1,0:T(8,128)(2,1)S(1)} %slice.53), channel_id=1, source_target_pairs={{0,68},{8,76},{16,84},{24,92},{32,100},{40,108},{48,116},{56,124},... | collective-permute-start | bytes 393224 | tf_op jit(solution)/shard_map/ppermute | solution.py:44
  117.0 4.9 %collective-permute-start.30 = (bf16[128,512]{1,0:T(8,128)(2,1)S(1)}, bf16[128,512]{1,0:T(8,128)(2,1)S(1)}, u32[]{:S(2)}, u32[]{:S(2)}) collective-permute-start(bf16[128,512]{1,0:T(8,128)(2,1)S(1)} %get-tuple-element.74), channel_id=1, source_target_pairs={{0,1},{8,9},{16,17},{24,25},{32,33},{40,41},{48,49},{56,57},{64,65... | collective-permute-start | bytes 393224 | tf_op jit(solution)/shard_map/ppermute | solution.py:44
  117.7 6.1 %collective-permute-start.32 = (bf16[128,512]{1,0:T(8,128)(2,1)S(1)}, bf16[128,512]{1,0:T(8,128)(2,1)S(1)}, u32[]{:S(2)}, u32[]{:S(2)}) collective-permute-start(bf16[128,512]{1,0:T(8,128)(2,1)S(1)} %get-tuple-element.75), channel_id=1, source_target_pairs={{0,2},{8,10},{16,18},{24,26},{32,34},{40,42},{48,50},{56,58},{64,6... | collective-permute-start | bytes 393224 | tf_op jit(solution)/shard_map/ppermute | solution.py:44
  118.7 5.7 %collective-permute-start.31 = (bf16[128,512]{1,0:T(8,128)(2,1)S(1)}, bf16[128,512]{1,0:T(8,128)(2,1)S(1)}, u32[]{:S(2)}, u32[]{:S(2)}) collective-permute-start(bf16[128,512]{1,0:T(8,128)(2,1)S(1)} %get-tuple-element.76), channel_id=1, source_target_pairs={{0,3},{8,11},{16,19},{24,27},{32,35},{40,43},{48,51},{56,59},{64,6... | collective-permute-start | bytes 393224 | tf_op jit(solution)/shard_map/ppermute | solution.py:44
  121.0 3.9 %collective-permute-start.40 = (bf16[128,512]{1,0:T(8,128)(2,1)S(1)}, bf16[128,512]{1,0:T(8,128)(2,1)S(1)}, u32[]{:S(2)}, u32[]{:S(2)}) collective-permute-start(bf16[128,512]{1,0:T(8,128)(2,1)S(1)} %fusion.8), channel_id=1, source_target_pairs={{0,16},{8,24},{16,0},{24,8},{32,48},{40,56},{48,32},{56,40},{64,80... | collective-permute-start | bytes 393224 | tf_op jit(solution)/shard_map/ppermute | solution.py:44
  124.5 4.2 %collective-permute-start.33 = (bf16[128,512]{1,0:T(8,128)(2,1)S(1)}, bf16[128,512]{1,0:T(8,128)(2,1)S(1)}, u32[]{:S(2)}, u32[]{:S(2)}) collective-permute-start(bf16[128,512]{1,0:T(8,128)(2,1)S(1)} %get-tuple-element.70), channel_id=1, source_target_pairs={{0,64},{8,72},{16,80},{24,88},{32,96},{40,104},{48,112},{56,120},{... | collective-permute-start | bytes 393224 | tf_op jit(solution)/shard_map/ppermute | solution.py:44
  124.9 5.1 %collective-permute-start.41 = (bf16[128,512]{1,0:T(8,128)(2,1)S(1)}, bf16[128,512]{1,0:T(8,128)(2,1)S(1)}, u32[]{:S(2)}, u32[]{:S(2)}) collective-permute-start(bf16[128,512]{1,0:T(8,128)(2,1)S(1)} %fusion.5), channel_id=1, source_target_pairs={{0,48},{8,56},{16,32},{24,40},{32,16},{40,24},{48,0},{56,8},{64,11... | collective-permute-start | bytes 393224 | tf_op jit(solution)/shard_map/ppermute | solution.py:44
  128.7 4.2 %collective-permute-start.34 = (bf16[128,512]{1,0:T(8,128)(2,1)S(1)}, bf16[128,512]{1,0:T(8,128)(2,1)S(1)}, u32[]{:S(2)}, u32[]{:S(2)}) collective-permute-start(bf16[128,512]{1,0:T(8,128)(2,1)S(1)} %fusion.4), channel_id=1, source_target_pairs={{0,16},{8,24},{16,0},{24,8},{32,48},{40,56},{48,32},{56,40},{64,80... | collective-permute-start | bytes 393224 | tf_op jit(solution)/shard_map/ppermute | solution.py:44
  130.1 5.0 %collective-permute-start.42 = (bf16[128,512]{1,0:T(8,128)(2,1)S(1)}, bf16[128,512]{1,0:T(8,128)(2,1)S(1)}, u32[]{:S(2)}, u32[]{:S(2)}) collective-permute-start(bf16[128,512]{1,0:T(8,128)(2,1)S(1)} %fusion.7), channel_id=1, source_target_pairs={{0,64},{8,72},{16,80},{24,88},{32,96},{40,104},{48,112},{56,120},{... | collective-permute-start | bytes 393224 | tf_op jit(solution)/shard_map/ppermute | solution.py:44
  132.9 5.1 %collective-permute-start.35 = (bf16[128,512]{1,0:T(8,128)(2,1)S(1)}, bf16[128,512]{1,0:T(8,128)(2,1)S(1)}, u32[]{:S(2)}, u32[]{:S(2)}) collective-permute-start(bf16[128,512]{1,0:T(8,128)(2,1)S(1)} %fusion.6), channel_id=1, source_target_pairs={{0,48},{8,56},{16,32},{24,40},{32,16},{40,24},{48,0},{56,8},{64,11... | collective-permute-start | bytes 393224 | tf_op jit(solution)/shard_map/ppermute | solution.py:44
  138.2 9.5 %collective-permute-start.43 = (bf16[128,1024]{1,0:T(8,128)(2,1)S(1)}, bf16[128,1024]{1,0:T(8,128)(2,1)S(1)}, u32[]{:S(2)}, u32[]{:S(2)}) collective-permute-start(bf16[128,1024]{1,0:T(8,128)(2,1)S(1)} %pad_maximum_fusion.4), channel_id=1, source_target_pairs={{0,8},{8,0},{16,24},{24,16},{32,40},{40,32},{48,56},{56,48},{64,72... | collective-permute-start | bytes 786440 | tf_op jit(solution)/shard_map/ppermute | solution.py:44

commit v7 on v6

--- a/solution.py
+++ b/solution.py
@@ -80,22 +80,18 @@
     return lax.dot_general(left, right, (((1,), (1,)), ((), ())), preferred_element_type=F32)
 
 
-def column_offsets(core, width):
-    half, part = width // 2, width // 4
-    mine = pl.multiple_of(core * half, half)
-    other = pl.multiple_of((1 - core) * half, half)
+def parts_of(half):
+    wide = half * 3 // 8
+    pair = range(2)
     return (
-        (mine, pl.multiple_of(mine + part, part)),
-        (other, pl.multiple_of(other + part, part)),
+        (0, wide, [[(r3 * 2 + r1, ry) for r1 in pair for ry in pair] for r3 in pair]),
+        (wide, wide, [[(q, ry) for q in range(4)] for ry in pair]),
+        (
+            2 * wide,
+            half - 2 * wide,
+            [[(r3 * 2 + r1, ry) for ry in pair for r3 in pair] for r1 in pair],
+        ),
     )
-
-
-def with_r3(r3):
-    return [(q, ry) for q in (2 * r3, 2 * r3 + 1) for ry in range(2)]
-
-
-def with_ry(ry):
-    return [(q, ry) for q in range(4)]
 
 
 def block_home(x, y_hi, q, ry):
@@ -112,41 +108,51 @@
 
 def weight_rows(ref, block):
     rows = ref.shape[0] // 4
+    if rows == block:
+        return ref[...]
     return jnp.concatenate([ref[q * rows : q * rows + block, :] for q in range(4)], axis=0)
 
 
-def pack_kernel(weight, users, first, second):
+def pack_kernel(weight, users, first, second, third, held, sems):
     rows, width = weight.shape
-    part = width // 4
-    first_at, second_at = column_offsets(lax.axis_index("dp") % 2, width)[0]
-    first[:rows, :] = weight[:, pl.ds(first_at, part)]
-    second[...] = weight[:, pl.ds(second_at, part)]
-    wide = users[...].astype(F32)
-    riding = jnp.concatenate([wide[:, j * part : (j + 1) * part] for j in range(4)], axis=0)
-    first[rows:, :] = riding.astype(BF16)
+    half = width // 2
+    mine = (lax.axis_index("dp") % 2) * half
+    copies = [pltpu.make_async_copy(users, held, sems.at[3])]
+    for n, ((start, columns, _), out) in enumerate(zip(parts_of(half), (first, second, third))):
+        at = pl.multiple_of(mine + start, 128)
+        copies.append(
+            pltpu.make_async_copy(
+                weight.at[:, pl.ds(at, columns)], out.at[pl.ds(0, rows)], sems.at[n]
+            )
+        )
+    for copy in copies:
+        copy.start()
+    for copy in copies:
+        copy.wait()
+    part = third.shape[1]
+    wide = held[...].astype(F32)
+    riding = [wide[:, j * part : (j + 1) * part] for j in range(width // part)]
+    third[rows:, :] = jnp.concatenate(riding, axis=0).astype(BF16)
 
 
 def forward_kernel(items, ints, context, residual, gain, *refs):
-    firsts, seconds = (refs[0:2], refs[4:6]), (refs[2:4], refs[6:8])
-    stream, inverse, pooled, embedding, added_rows, sem = refs[8:]
+    stream, inverse, pooled, embedding, added_rows, sem = refs[12:]
     where = [ints[i] for i in range(4)]
     lengths, ids, counts = ([ints[4 + j * items + i] for i in range(items)] for j in range(3))
     positive = [ints[i] for i in range(4 + 3 * items, ints.shape[0])]
     tokens, width = residual.shape
-    part = width // 4
+    half = width // 2
     block = context.shape[1] // 8
     length = tokens // items
     copy = pltpu.make_async_copy(residual, added_rows, sem)
     copy.start()
-    by_r3 = [blocks_of(context, where, with_r3(r3), block) for r3 in range(2)]
-    by_ry = [blocks_of(context, where, with_ry(ry), block) for ry in range(2)]
-    for side, (first_at, second_at) in enumerate(column_offsets(where[3], width)):
-        stream[:, pl.ds(first_at, part)] = sum(
-            dot(by_r3[r3], weight_rows(firsts[side][r3], block)) for r3 in range(2)
-        )
-        stream[:, pl.ds(second_at, part)] = sum(
-            dot(by_ry[ry], seconds[side][ry][...]) for ry in range(2)
-        )
+    for p, (start, columns, orders) in enumerate(parts_of(half)):
+        lanes = [blocks_of(context, where, order, block) for order in orders]
+        for side in range(2):
+            base = where[3] * half if side == 0 else (1 - where[3]) * half
+            stream[:, pl.ds(pl.multiple_of(base + start, 128), columns)] = sum(
+                dot(lanes[k], weight_rows(refs[side * 6 + p * 2 + k], block)) for k in range(2)
+            )
     copy.wait()
     for i in range(items):
         span = slice(i * length, (i + 1) * length)
@@ -219,23 +225,27 @@
     emb, labels = turned[:, :width], turned[:, width:]
     for copy in copies:
         copy.wait()
-    to = lax.broadcasted_iota(jnp.int32, (people, 16 * rode), 0)
-    of = lax.broadcasted_iota(jnp.int32, (people, 16 * rode), 1)
-    one = of // rode
-    holder = ((core ^ bit(one, 3)) * 2 + ((y // 2) ^ bit(one, 0))) * 4 + (
-        x ^ bit(one, 1) ^ (3 * bit(one, 2))
-    )
-    home = holder * users_here + of % users_here
-    column = (of % rode) // users_here
-    users = jnp.concatenate(
+    def user_home(s):
+        one = s // users_here
+        ac, ay = core ^ bit(one, 3), (y // 2) ^ bit(one, 1)
+        ax = x ^ bit(one, 2) ^ (3 * bit(one, 0))
+        return ((ac * 2 + ay) * 4 + ax) * users_here + s % users_here
+
+    wide = riders[...].astype(F32)
+    placed = jnp.concatenate(
         [
-            dot(
-                jnp.where((to == home) & (column == j), 1.0, 0.0).astype(BF16), riders[...]
-            ).astype(BF16)
+            jnp.concatenate(
+                [
+                    wide[n * rode + j * users_here : n * rode + (j + 1) * users_here, :]
+                    for n in range(16)
+                ],
+                axis=0,
+            )
             for j in range(parts)
         ],
         axis=1,
-    )
+    ).astype(BF16)
+    users = dot(one_hot_turn(people, user_home), placed).astype(BF16)
     person = lax.broadcasted_iota(jnp.int32, (people, items), 0)
     at = lax.broadcasted_iota(jnp.int32, (people, items), 1)
     g = person // users_here
@@ -320,23 +330,24 @@
 
 
 def context_kernel(where, keep, send, *refs):
-    firsts, seconds = (refs[0:2], refs[4:6]), (refs[2:4], refs[6:8])
-    context_grad = refs[8]
-    part = keep.shape[1] // 2
+    context_grad = refs[12]
+    half = keep.shape[1]
     block = context_grad.shape[1] // 8
-    near = [ref[:, :part] for ref in (keep, send)]
-    far = [ref[:, part:] for ref in (keep, send)]
-    from_first = [
-        sum(contract_last(near[s], weight_rows(firsts[s][r3], block)) for s in range(2))
-        for r3 in range(2)
-    ]
-    for ry in range(2):
-        from_second = sum(contract_last(far[s], seconds[s][ry][...]) for s in range(2))
-        for q in range(4):
-            b = ((q % 2) * 2 + ry) * block
-            value = from_first[q // 2][:, b : b + block] + from_second[:, q * block : (q + 1) * block]
-            home = block_home(where[0], where[1] // 2, q, ry)
-            context_grad[:, pl.ds(pl.multiple_of(home * block, block), block)] = value.astype(BF16)
+    values = {}
+    for p, (start, columns, orders) in enumerate(parts_of(half)):
+        for k, order in enumerate(orders):
+            product = sum(
+                contract_last(
+                    grad[:, start : start + columns], weight_rows(refs[side * 6 + p * 2 + k], block)
+                )
+                for side, grad in enumerate((keep, send))
+            )
+            for b, place in enumerate(order):
+                piece = product[:, b * block : (b + 1) * block]
+                values[place] = values[place] + piece if place in values else piece
+    for (q, ry), value in values.items():
+        home = block_home(where[0], where[1] // 2, q, ry)
+        context_grad[:, pl.ds(pl.multiple_of(home * block, block), block)] = value.astype(BF16)
 
 
 def blocks_kernel(kept, where, own_context, peer_context, own_grad, peer_grad, first, *seconds):
@@ -390,26 +401,39 @@
     rows = out_weight.shape[0]
     gain = norm_gain[None, :]
 
-    rode = users_here * (width // part)
-    first, second = pl.pallas_call(
+    columns = [part_columns for _, part_columns, _ in parts_of(half)]
+    rode = users_here * (width // columns[2])
+    travel = pl.pallas_call(
         pack_kernel,
-        out_shape=(shaped((rows + rode, part), BF16), shaped((rows, part), BF16)),
-        in_specs=[VMEM] * 2,
-        out_specs=(VMEM,) * 2,
+        out_shape=(
+            shaped((rows, columns[0]), BF16),
+            shaped((rows, columns[1]), BF16),
+            shaped((rows + rode, columns[2]), BF16),
+        ),
+        in_specs=[ANY] * 2,
+        out_specs=(VMEM,) * 3,
+        scratch_shapes=[
+            pltpu.VMEM((users_here, width), BF16),
+            pltpu.SemaphoreType.DMA((4,)),
+        ],
         compiler_params=params(6),
         name="pack",
     )(out_weight, user_vectors)
-    for (first_swap, n), (second_swap, m) in (
-        ((swap_y, 3), (swap_x, 1)),
-        ((swap_x, 1), (swap_x, 3)),
-    ):
-        first = jnp.concatenate([first, first_swap(first, n)], axis=0)
-        second = jnp.concatenate([second, second_swap(second, m)], axis=0)
-        first, second = lax.optimization_barrier((first, second))
-    first_far, second_far = lax.optimization_barrier((swap_x(first, 3), swap_y(second, 3)))
-    pieces = [first, first_far, second, second_far]
+    steps = ((swap_y, 3), (swap_x, 1), (swap_x, 3))
+    for step in range(2):
+        turns = [steps[step], steps[step + 1], steps[(step + 2) % 3]]
+        travel = [jnp.concatenate([v, swap(v, n)], axis=0) for v, (swap, n) in zip(travel, turns)]
+        travel = lax.optimization_barrier(travel)
+    arrived = [swap_x(travel[0], 3), swap_y(travel[1], 3), swap_x(travel[2], 1)]
+    arrived = lax.optimization_barrier(arrived)
+    pieces = [piece for both in zip(travel, arrived) for piece in both]
     pieces = pieces + [swap_core(p) for p in pieces]
-    ints = jnp.concatenate([where, lengths, item_ids, item_counts, positive])
+    ints, filled = 0, 0
+    numbers = (where, lengths, item_ids, item_counts, positive)
+    count = sum(v.shape[0] for v in numbers)
+    for v in numbers:
+        ints = ints + jnp.pad(v, (filled, count - filled - v.shape[0]))
+        filled += v.shape[0]
 
     stream, inverse, pooled, emb = pl.pallas_call(
         functools.partial(forward_kernel, items_here),
@@ -419,7 +443,7 @@
             shaped((items_here, width)),
             shaped((items_here, width + LABELS), BF16),
         ),
-        in_specs=[SMEM, VMEM, HBM] + [VMEM] * 9,
+        in_specs=[SMEM, VMEM, HBM] + [VMEM] * 13,
         out_specs=(VMEM,) * 4,
         scratch_shapes=[pltpu.VMEM((tokens, width), BF16), pltpu.SemaphoreType.DMA],
         compiler_params=params(20),
@@ -433,7 +457,7 @@
     emb_pieces = emb_pieces + [swap_core(p) for p in emb_pieces]
 
     items, people = 128 * items_here, 16 * users_here
-    riding = pieces[0:2] + pieces[4:6]
+    riding = pieces[4:6] + pieces[10:12]
     *sums, user_grad = pl.pallas_call(
         functools.partial(loss_kernel, users_here, items_here, rows),
         out_shape=(shaped((8, width)),) * 4 + (shaped((users_here, width), BF16),),
@@ -442,7 +466,7 @@
         scratch_shapes=[
             pltpu.VMEM((people, items), F32),
             pltpu.VMEM((items, width), F32),
-            pltpu.VMEM((people * (width // part), part), BF16),
+            pltpu.VMEM((16 * rode, columns[2]), BF16),
             pltpu.SemaphoreType.DMA((16,)),
         ],
         compiler_params=params(24),
@@ -469,7 +493,7 @@
     context_grad = pl.pallas_call(
         context_kernel,
         out_shape=shaped((tokens, head), BF16),
-        in_specs=[SMEM] + [VMEM] * 10,
+        in_specs=[SMEM] + [VMEM] * 14,
         out_specs=VMEM,
         compiler_params=params(14),
         name="context",

time: 149 us -> 145 us (0.973)
  waiting for transfers between devices: 47.3 us -> 40.1 us
    ppermute x44 -> x49, waiting for transfers between devices: 47.3 us -> 40.1 us  [move(): return lax.ppermute(value, AXES, perm)]
    unnamed x12 -> x24, local copies, waits for them, and re-layouts: 3.48 us -> 5.24 us
    ppermute x44 -> x49, starting transfers between devices: 71.2 us -> 72.6 us  [move(): return lax.ppermute(value, AXES, perm)]
  transfers between devices with their start and end apart: 44 -> 49, of which waited for: 28 -> 30; matrix products, arithmetic and copies ran while one was open for 1% -> 1% of each run, Pallas kernels for 7% -> 7%
where the time goes in v7:
time: 145 us; the launch traced here: 144 us
  starting transfers between devices  72.6 us (50%)
  waiting for transfers between devices  40.1 us (28%)
  Pallas kernels  23.4 us (16%)
  local copies, waits for them, and re-layouts  5.28 us (4%)
  other arithmetic  2.17 us (1%)
    ppermute x49, starting transfers between devices, move(): return lax.ppermute(value, AXES, perm)  72.6 us
    ppermute x49, waiting for transfers between devices, move(): return lax.ppermute(value, AXES, perm)  40.1 us
    pallas_call x1, Pallas kernels, on_device(): pl.pallas_call(functools.partial(forward_kernel, items_here), out_shape=(...  5.88 us
    pallas_call x1, Pallas kernels, on_device(): pl.pallas_call(context_kernel, out_shape=shaped((tokens, head), BF16), in...  5.57 us
    unnamed x24, local copies, waits for them, and re-layouts  5.24 us
    pallas_call x1, Pallas kernels, on_device(): pl.pallas_call(functools.partial(loss_kernel, users_here, items_here, row...  5.07 us
    pallas_call x2, Pallas kernels, blocks(): pl.pallas_call(functools.partial(blocks_kernel, kept), out_shape=(shaped(...  3.72 us
    pallas_call x1, Pallas kernels, on_device(): pl.pallas_call(functools.partial(residual_kernel, 8 * people), out_shape=...  3.03 us
  transfers between devices with their start and end apart: 49, of which 30 were waited for; matrix products, arithmetic and copies ran while one was open for 1% of the time, Pallas kernels for 7%

profile of v7, /device:TPU:1, one launch (start us, length us, event | category | flops | bytes accessed | tf_op | source)
XLA Modules:
  0.0 144.5 jit_solution(396352770007759848)
XLA Ops:
  0.7 1.1 copy-done.5
  1.8 0.8 copy-done.7
  2.7 3.6 %collective-permute-start = (bf16[128,384]{1,0:T(8,128)(2,1)S(1)}, bf16[128,384]{1,0:T(8,128)(2,1)S(1)}, u32[]{:S(2)}, u32[]{:S(2)}) collective-permute-start(bf16[128,384]{1,0:T(8,128)(2,1)S(1)} %get-tuple-element.42), channel_id=1, source_target_pairs={{0,68},{8,76},{16,84},{24,92},{32,100},{40,108},{48,116},{56,124},... | collective-permute-start | bytes 294920 | tf_op jit(solution)/shard_map/ppermute | solution.py:44
  6.3 1.2 collective-permute-start.1
  7.6 1.8 %collective-permute-start.2 = (bf16[192,256]{1,0:T(8,128)(2,1)S(1)}, bf16[192,256]{1,0:T(8,128)(2,1)S(1)}, u32[]{:S(2)}, u32[]{:S(2)}) collective-permute-start(bf16[192,256]{1,0:T(8,128)(2,1)S(1)} %get-tuple-element.44), channel_id=1, source_target_pairs={{0,3},{8,11},{16,19},{24,27},{32,35},{40,43},{48,51},{56,59},{64,6... | collective-permute-start | bytes 294920 | tf_op jit(solution)/shard_map/ppermute | solution.py:44
  9.8 2.4 %collective-permute-done.2 = bf16[192,256]{1,0:T(8,128)(2,1)S(1)} collective-permute-done((bf16[192,256]{1,0:T(8,128)(2,1)S(1)}, bf16[192,256]{1,0:T(8,128)(2,1)S(1)}, u32[]{:S(2)}, u32[]{:S(2)}) %collective-permute-start.2) | collective-permute-done | bytes 98336 | tf_op jit(solution)/shard_map/ppermute | solution.py:44
  12.3 1.9 %collective-permute-start.4 = (bf16[256,384]{1,0:T(8,128)(2,1)S(1)}, bf16[256,384]{1,0:T(8,128)(2,1)S(1)}, u32[]{:S(2)}, u32[]{:S(2)}) collective-permute-start(bf16[256,384]{1,0:T(8,128)(2,1)S(1)} %pad_maximum_fusion.5), channel_id=1, source_target_pairs={{0,3},{8,11},{16,19},{24,27},{32,35},{40,43},{48,51},{56,59},{64,6... | collective-permute-start | bytes 589832 | tf_op jit(solution)/shard_map/ppermute | solution.py:44
  14.6 2.2 %collective-permute-done.3 = bf16[256,384]{1,0:T(8,128)(2,1)S(1)} collective-permute-done((bf16[256,384]{1,0:T(8,128)(2,1)S(1)}, bf16[256,384]{1,0:T(8,128)(2,1)S(1)}, u32[]{:S(2)}, u32[]{:S(2)}) %collective-permute-start.3) | collective-permute-done | bytes 196640 | tf_op jit(solution)/shard_map/ppermute | solution.py:44
  16.9 1.3 collective-permute-done.4
  18.2 2.1 %collective-permute-done.5 = bf16[384,256]{1,0:T(8,128)(2,1)S(1)} collective-permute-done((bf16[384,256]{1,0:T(8,128)(2,1)S(1)}, bf16[384,256]{1,0:T(8,128)(2,1)S(1)}, u32[]{:S(2)}, u32[]{:S(2)}) %collective-permute-start.5) | collective-permute-done | bytes 196640 | tf_op jit(solution)/shard_map/ppermute | solution.py:44
  20.3 0.9 collective-permute-start.6
  21.5 4.5 %collective-permute-start.9 = (bf16[512,384]{1,0:T(8,128)(2,1)S(1)}, bf16[512,384]{1,0:T(8,128)(2,1)S(1)}, u32[]{:S(2)}, u32[]{:S(2)}) collective-permute-start(bf16[512,384]{1,0:T(8,128)(2,1)S(1)} %pad_maximum_fusion.refs_0_), channel_id=1, source_target_pairs={{0,8},{8,0},{16,24},{24,16},{32,40},{40,32},{48,56},{56,48},{64,72... | collective-permute-start | bytes 1179656 | tf_op jit(solution)/shard_map/ppermute | solution.py:44
  26.0 2.8 %collective-permute-done.6.refs_1_ = bf16[512,384]{1,0:T(8,128)(2,1)} collective-permute-done((bf16[512,384]{1,0:T(8,128)(2,1)S(1)}, bf16[512,384]{1,0:T(8,128)(2,1)}, u32[]{:S(2)}, u32[]{:S(2)}) %collective-permute-start.6) | collective-permute-done | bytes 393248 | tf_op jit(solution)/shard_map/ppermute | solution.py:44
  28.8 4.4 %collective-permute-start.13 = (bf16[768,256]{1,0:T(8,128)(2,1)S(1)}, bf16[768,256]{1,0:T(8,128)(2,1)S(1)}, u32[]{:S(2)}, u32[]{:S(2)}) collective-permute-start(bf16[768,256]{1,0:T(8,128)(2,1)S(1)} %pad_maximum_fusion.2.refs_4_.refs_0_), channel_id=1, source_target_pairs={{0,8},{8,0},{16,24},{24,16},{32,40},{40,32},{48,56},{56,48},{64,72... | collective-permute-start | bytes 1179656 | tf_op jit(solution)/shard_map/ppermute | solution.py:44
  33.2 0.9 collective-permute-start.10
  36.8 1.6 %copy-done.1 = bf16[512,2048]{1,0:T(8,128)(2,1)S(1)} copy-done((bf16[512,2048]{1,0:T(8,128)(2,1)S(1)}, bf16[512,2048]{1,0:T(8,128)(2,1)}, u32[]{:S(2)}) %copy-start.1) | copy-done | bytes 2097176
  38.4 1.0 copy-done.3
  39.3 5.9 %forward.1 = (f32[512,2048]{1,0:T(8,128)S(1)}, f32[512,1]{1,0:T(8,128)S(1)}, f32[2,2048]{1,0:T(2,128)S(1)}, bf16[2,2176]{1,0:T(2,128)(2,1)S(1)}) custom-call(s32[18]{0:T(128)S(1)} %pad_add_fusion.1.ints, bf16[512,1024]{1,0:T(8,128)(2,1)S(1)} %copy-done, bf16[512,2048]{1,0:T(8,128)(2,1)S(1)} %copy-done.1, f32[1,2048]{1,0:T(1,128)S(1)} %bitcast.7, ...), custom_call_target="tpu_custom_call" | custom-call | tf_op jit(solution)/shard_map/forward/pallas_call | solution.py:438
  45.2 2.1 %collective-permute-start.17 = (bf16[2,2176]{1,0:T(2,128)(2,1)S(1)}, bf16[2,2176]{1,0:T(2,128)(2,1)S(1)}, u32[]{:S(2)}, u32[]{:S(2)}) collective-permute-start(bf16[2,2176]{1,0:T(2,128)(2,1)S(1)} %get-tuple-element.57), channel_id=1, source_target_pairs={{0,2},{8,10},{16,18},{24,26},{32,34},{40,42},{48,50},{56,58},{64,6... | collective-permute-start | bytes 26120 | tf_op jit(solution)/shard_map/ppermute | solution.py:44
  47.3 0.9 collective-permute-start.16
  48.2 1.2 collective-permute-done.17
  49.3 1.7 %collective-permute-done.16 = bf16[2,2176]{1,0:T(2,128)(2,1)S(1)} collective-permute-done((bf16[2,2176]{1,0:T(2,128)(2,1)S(1)}, bf16[2,2176]{1,0:T(2,128)(2,1)S(1)}, u32[]{:S(2)}, u32[]{:S(2)}) %collective-permute-start.16) | collective-permute-done | bytes 8736 | tf_op jit(solution)/shard_map/ppermute | solution.py:44
  51.2 1.7 %collective-permute-start.19 = (bf16[8,2176]{1,0:T(8,128)(2,1)S(1)}, bf16[8,2176]{1,0:T(8,128)(2,1)S(1)}, u32[]{:S(2)}, u32[]{:S(2)}) collective-permute-start(bf16[8,2176]{1,0:T(8,128)(2,1)S(1)} %pad_maximum_fusion.8), channel_id=1, source_target_pairs={{0,68},{8,76},{16,84},{24,92},{32,100},{40,108},{48,116},{56,124},... | collective-permute-start | bytes 104456 | tf_op jit(solution)/shard_map/ppermute | solution.py:44
  52.9 0.9 collective-permute-start.18
  53.8 1.7 %collective-permute-done.20 = bf16[8,2176]{1,0:T(8,128)(2,1)S(1)} collective-permute-done((bf16[8,2176]{1,0:T(8,128)(2,1)S(1)}, bf16[8,2176]{1,0:T(8,128)(2,1)S(1)}, u32[]{:S(2)}, u32[]{:S(2)}) %collective-permute-start.20) | collective-permute-done | bytes 34848 | tf_op jit(solution)/shard_map/ppermute | solution.py:44
  55.7 3.7 %collective-permute-start.23 = (bf16[32,2176]{1,0:T(8,128)(2,1)S(1)}, bf16[32,2176]{1,0:T(8,128)(2,1)S(1)}, u32[]{:S(2)}, u32[]{:S(2)}) collective-permute-start(bf16[32,2176]{1,0:T(8,128)(2,1)S(1)} %pad_maximum_fusion.7.refs_4_), channel_id=1, source_target_pairs={{0,32},{8,40},{16,48},{24,56},{32,0},{40,8},{48,16},{56,24},{64,96... | collective-permute-start | bytes 417800 | tf_op jit(solution)/shard_map/ppermute | solution.py:44
  60.1 3.8 %collective-permute-start.24 = (bf16[32,2176]{1,0:T(8,128)(2,1)S(1)}, bf16[32,2176]{1,0:T(8,128)(2,1)S(1)}, u32[]{:S(2)}, u32[]{:S(2)}) collective-permute-start(bf16[32,2176]{1,0:T(8,128)(2,1)S(1)} %pad_maximum_fusion.7.refs_4_), channel_id=1, source_target_pairs={{0,8},{8,0},{16,24},{24,16},{32,40},{40,32},{48,56},{56,48},{64,72... | collective-permute-start | bytes 417800 | tf_op jit(solution)/shard_map/ppermute | solution.py:44
  63.9 3.1 %collective-permute-start.27 = (bf16[32,2176]{1,0:T(8,128)(2,1)S(1)}, bf16[32,2176]{1,0:T(8,128)(2,1)S(1)}, u32[]{:S(2)}, u32[]{:S(2)}) collective-permute-start(bf16[32,2176]{1,0:T(8,128)(2,1)S(1)} %collective-permute-done.23.refs_7_), channel_id=1, source_target_pairs={{0,8},{8,0},{16,24},{24,16},{32,40},{40,32},{48,56},{56,48},{64,72... | collective-permute-start | bytes 417800 | tf_op jit(solution)/shard_map/ppermute | solution.py:44
  67.0 2.1 %collective-permute-start.26 = (bf16[32,2176]{1,0:T(8,128)(2,1)S(1)}, bf16[32,2176]{1,0:T(8,128)(2,1)S(1)}, u32[]{:S(2)}, u32[]{:S(2)}) collective-permute-start(bf16[32,2176]{1,0:T(8,128)(2,1)S(1)} %collective-permute-done.22.refs_6_), channel_id=1, source_target_pairs={{0,8},{8,0},{16,24},{24,16},{32,40},{40,32},{48,56},{56,48},{64,72... | collective-permute-start | bytes 417800 | tf_op jit(solution)/shard_map/ppermute | solution.py:44
  69.2 1.0 collective-permute-done.26.refs_10_
  70.5 5.1 %loss.1 = (f32[8,2048]{1,0:T(8,128)S(1)}, f32[8,2048]{1,0:T(8,128)S(1)}, f32[8,2048]{1,0:T(8,128)S(1)}, f32[8,2048]{1,0:T(8,128)S(1)}, bf16[8,2048]{1,0:T(8,128)(2,1)}) custom-call(s32[4]{0:T(128)S(1)} %pad_add_fusion.where, f32[1,2048]{1,0:T(1,128)S(1)} %bitcast.8, bf16[768,256]{1,0:T(8,128)(2,1)S(1)} %pad_maximum_fusion.2.refs_4_.refs_0_, ...), custom_call_target="tpu_custom_call" | custom-call | tf_op jit(solution)/shard_map/loss/pallas_call | solution.py:461
  75.7 1.7 %collective-permute-start.29 = (f32[8,2048]{1,0:T(8,128)S(1)}, f32[8,2048]{1,0:T(8,128)S(1)}, u32[]{:S(2)}, u32[]{:S(2)}) collective-permute-start(f32[8,2048]{1,0:T(8,128)S(1)} %get-tuple-element.60), channel_id=1, source_target_pairs={{0,48},{8,56},{16,32},{24,40},{32,16},{40,24},{48,0},{56,8},{64,11... | collective-permute-start | bytes 196616 | tf_op jit(solution)/shard_map/ppermute | solution.py:44
  77.4 1.5 %collective-permute-start.30 = (f32[8,2048]{1,0:T(8,128)S(1)}, f32[8,2048]{1,0:T(8,128)S(1)}, u32[]{:S(2)}, u32[]{:S(2)}) collective-permute-start(f32[8,2048]{1,0:T(8,128)S(1)} %get-tuple-element.61), channel_id=1, source_target_pairs={{0,32},{8,40},{16,48},{24,56},{32,0},{40,8},{48,16},{56,24},{64,96... | collective-permute-start | bytes 196616 | tf_op jit(solution)/shard_map/ppermute | solution.py:44
  79.2 1.3 collective-permute-done.29
  80.4 1.6 %collective-permute-done.30 = f32[8,2048]{1,0:T(8,128)S(1)} collective-permute-done((f32[8,2048]{1,0:T(8,128)S(1)}, f32[8,2048]{1,0:T(8,128)S(1)}, u32[]{:S(2)}, u32[]{:S(2)}) %collective-permute-start.30) | collective-permute-done | bytes 65568 | tf_op jit(solution)/shard_map/ppermute | solution.py:44
  82.0 1.3 collective-permute-start.31
  83.3 2.1 %collective-permute-start.32 = (bf16[512,1024]{1,0:T(8,128)(2,1)S(1)}, bf16[512,1024]{1,0:T(8,128)(2,1)S(1)}, u32[]{:S(2)}, u32[]{:S(2)}) collective-permute-start(bf16[512,1024]{1,0:T(8,128)(2,1)S(1)} %copy-done), channel_id=1, source_target_pairs={{0,8},{8,0},{16,24},{24,16},{32,40},{40,32},{48,56},{56,48},{64,72... | collective-permute-start | bytes 3145736 | tf_op jit(solution)/shard_map/ppermute | solution.py:44
  85.4 3.0 %residual.3 = (bf16[512,2048]{1,0:T(8,128)(2,1)}, bf16[512,1024]{1,0:T(8,128)(2,1)S(1)}, bf16[512,1024]{1,0:T(8,128)(2,1)S(1)}, f32[1,2048]{1,0:T(1,128)}, f32[1,1]{1,0:T(1,128)}) custom-call(s32[4]{0:T(128)S(1)} %pad_add_fusion.where, s32[2]{0:T(128)S(1)} %copy-done.8, f32[512,2048]{1,0:T(8,128)S(1)} %get-tuple-element.54.stream, ...), custom_call_target="tpu_custom_call" | custom-call | tf_op jit(solution)/shard_map/residual/pallas_call | solution.py:478
  88.5 2.8 %collective-permute-start.33 = (bf16[512,1024]{1,0:T(8,128)(2,1)S(1)}, bf16[512,1024]{1,0:T(8,128)(2,1)S(1)}, u32[]{:S(2)}, u32[]{:S(2)}) collective-permute-start(bf16[512,1024]{1,0:T(8,128)(2,1)S(1)} %get-tuple-element.66.send), channel_id=1, source_target_pairs={{0,8},{8,0},{16,24},{24,16},{32,40},{40,32},{48,56},{56,48},{64,72... | collective-permute-start | bytes 3145736 | tf_op jit(solution)/shard_map/ppermute | solution.py:44
  91.3 2.3 %collective-permute-done.33.peer_grad = bf16[512,1024]{1,0:T(8,128)(2,1)S(1)} collective-permute-done((bf16[512,1024]{1,0:T(8,128)(2,1)S(1)}, bf16[512,1024]{1,0:T(8,128)(2,1)S(1)}, u32[]{:S(2)}, u32[]{:S(2)}) %collective-permute-start.33) | collective-permute-done | bytes 1048608 | tf_op jit(solution)/shard_map/ppermute | solution.py:44
  93.5 2.1 %blocks_sent.1 = (bf16[512,512]{1,0:T(8,128)(2,1)S(1)}, bf16[256,512]{1,0:T(8,128)(2,1)S(1)}, bf16[256,512]{1,0:T(8,128)(2,1)S(1)}, bf16[256,512]{1,0:T(8,128)(2,1)S(1)}) custom-call(s32[4]{0:T(128)S(1)} %pad_add_fusion.where, bf16[512,1024]{1,0:T(8,128)(2,1)S(1)} %copy-done, bf16[512,1024]{1,0:T(8,128)(2,1)S(1)} %collective-permute-done.32.peer_context, ...), custom_call_target="tpu_custom_call" | custom-call | tf_op jit(solution)/shard_map/blocks_sent/pallas_call | solution.py:506
  95.8 1.8 %collective-permute-start.42 = (bf16[256,512]{1,0:T(8,128)(2,1)S(1)}, bf16[256,512]{1,0:T(8,128)(2,1)S(1)}, u32[]{:S(2)}, u32[]{:S(2)}) collective-permute-start(bf16[256,512]{1,0:T(8,128)(2,1)S(1)} %get-tuple-element.74), channel_id=1, source_target_pairs={{0,3},{8,11},{16,19},{24,27},{32,35},{40,43},{48,51},{56,59},{64,6... | collective-permute-start | bytes 786440 | tf_op jit(solution)/shard_map/ppermute | solution.py:44
  97.6 1.4 collective-permute-start.43
  99.0 1.3 collective-permute-start.34
  100.3 5.6 %context.3 = bf16[512,1024]{1,0:T(8,128)(2,1)} custom-call(s32[4]{0:T(128)S(1)} %pad_add_fusion.where, bf16[512,1024]{1,0:T(8,128)(2,1)S(1)} %get-tuple-element.65.own_grad.keep, bf16[512,1024]{1,0:T(8,128)(2,1)S(1)} %get-tuple-element.66.send, bf16[512,384]{1,0:T(8,128)(2,1)S(1)} %pad_maximum_fusion.refs_0_, ...), custom_call_target="tpu_custom_call" | custom-call | tf_op jit(solution)/shard_map/context/pallas_call | solution.py:493
  105.9 1.6 %blocks_kept.1 = (f32[512,512]{1,0:T(8,128)S(1)}, f32[256,512]{1,0:T(8,128)S(1)}) custom-call(s32[4]{0:T(128)S(1)} %pad_add_fusion.where, bf16[512,1024]{1,0:T(8,128)(2,1)S(1)} %copy-done, bf16[512,1024]{1,0:T(8,128)(2,1)S(1)} %collective-permute-done.32.peer_context, bf16[512,1024]{1,0:T(8,128)(2,1)S(1)} %get-tuple-element.65.own_grad.keep, ...), custom_call_target="tpu_custom_call" | custom-call | tf_op jit(solution)/shard_map/blocks_kept/pallas_call | solution.py:506
  107.5 2.8 %collective-permute-done.43 = bf16[256,512]{1,0:T(8,128)(2,1)S(1)} collective-permute-done((bf16[256,512]{1,0:T(8,128)(2,1)S(1)}, bf16[256,512]{1,0:T(8,128)(2,1)S(1)}, u32[]{:S(2)}, u32[]{:S(2)}) %collective-permute-start.43) | collective-permute-done | bytes 262176 | tf_op jit(solution)/shard_map/ppermute | solution.py:44
  110.5 1.4 collective-permute-start.44
  113.4 2.5 %collective-permute-start.37 = (bf16[128,512]{1,0:T(8,128)(2,1)S(1)}, bf16[128,512]{1,0:T(8,128)(2,1)S(1)}, u32[]{:S(2)}, u32[]{:S(2)}) collective-permute-start(bf16[128,512]{1,0:T(8,128)(2,1)S(1)} %get-tuple-element.83), channel_id=1, source_target_pairs={{0,2},{8,10},{16,18},{24,26},{32,34},{40,42},{48,50},{56,58},{64,6... | collective-permute-start | bytes 393224 | tf_op jit(solution)/shard_map/ppermute | solution.py:44
  115.9 0.9 collective-permute-start.36
  116.9 0.9 collective-permute-start.45
  117.8 1.9 %collective-permute-done.37 = bf16[128,512]{1,0:T(8,128)(2,1)S(1)} collective-permute-done((bf16[128,512]{1,0:T(8,128)(2,1)S(1)}, bf16[128,512]{1,0:T(8,128)(2,1)S(1)}, u32[]{:S(2)}, u32[]{:S(2)}) %collective-permute-start.37) | collective-permute-done | bytes 131104 | tf_op jit(solution)/shard_map/ppermute | solution.py:44
  119.7 1.4 collective-permute-done.36
  121.3 0.9 collective-permute-start.46
  122.2 2.8 %collective-permute-done.38 = bf16[128,512]{1,0:T(8,128)(2,1)S(1)} collective-permute-done((bf16[128,512]{1,0:T(8,128)(2,1)S(1)}, bf16[128,512]{1,0:T(8,128)(2,1)S(1)}, u32[]{:S(2)}, u32[]{:S(2)}) %collective-permute-start.38) | collective-permute-done | bytes 131104 | tf_op jit(solution)/shard_map/ppermute | solution.py:44
  125.1 0.9 collective-permute-start.39
  126.5 1.5 %collective-permute-start.47 = (bf16[128,512]{1,0:T(8,128)(2,1)S(1)}, bf16[128,512]{1,0:T(8,128)(2,1)S(1)}, u32[]{:S(2)}, u32[]{:S(2)}) collective-permute-start(bf16[128,512]{1,0:T(8,128)(2,1)S(1)} %fusion.7), channel_id=1, source_target_pairs={{0,64},{8,72},{16,80},{24,88},{32,96},{40,104},{48,112},{56,120},{... | collective-permute-start | bytes 393224 | tf_op jit(solution)/shard_map/ppermute | solution.py:44
  128.0 1.2 collective-permute-done.39
  129.3 0.9 collective-permute-start.40
  130.2 1.0 collective-permute-done.47
  131.4 3.1 %collective-permute-done.40 = bf16[128,512]{1,0:T(8,128)(2,1)S(1)} collective-permute-done((bf16[128,512]{1,0:T(8,128)(2,1)S(1)}, bf16[128,512]{1,0:T(8,128)(2,1)S(1)}, u32[]{:S(2)}, u32[]{:S(2)}) %collective-permute-start.40) | collective-permute-done | bytes 131104 | tf_op jit(solution)/shard_map/ppermute | solution.py:44
  134.5 7.9 %collective-permute-start.48 = (bf16[128,1024]{1,0:T(8,128)(2,1)S(1)}, bf16[128,1024]{1,0:T(8,128)(2,1)S(1)}, u32[]{:S(2)}, u32[]{:S(2)}) collective-permute-start(bf16[128,1024]{1,0:T(8,128)(2,1)S(1)} %pad_maximum_fusion.3), channel_id=1, source_target_pairs={{0,8},{8,0},{16,24},{24,16},{32,40},{40,32},{48,56},{56,48},{64,72... | collective-permute-start | bytes 786440 | tf_op jit(solution)/shard_map/ppermute | solution.py:44
  142.4 1.2 collective-permute-done.48
  143.6 0.9 maximum_select_fusion
  (90 shorter events, 8.5 us)
Async XLA Ops:
  0.6 36.1 %copy-start = (bf16[512,1024]{1,0:T(8,128)(2,1)S(1)}, bf16[512,1024]{1,0:T(8,128)(2,1)}, u32[]{:S(2)}) copy-start(bf16[512,1024]{1,0:T(8,128)(2,1)} %own_context.3) | copy-start | bytes 3145732
  0.6 1.1 copy-start.5
  1.8 0.8 copy-start.7
  2.5 32.9 %copy-start.8 = (s32[2]{0:T(128)S(1)}, s32[2]{0:T(128)}, u32[]{:S(2)}) copy-start(s32[2]{0:T(128)} %lengths.1) | copy-start | bytes 28
  2.5 32.9 %copy-start.9 = (s32[8]{0:T(128)S(1)}, s32[8]{0:T(128)}, u32[]{:S(2)}) copy-start(s32[8]{0:T(128)} %param.14) | copy-start | bytes 100
  2.5 32.9 %copy-start.10 = (s32[2]{0:T(128)S(1)}, s32[2]{0:T(128)}, u32[]{:S(2)}) copy-start(s32[2]{0:T(128)} %param.16) | copy-start | bytes 28
  2.5 33.0 %copy-start.11 = (s32[2]{0:T(128)S(1)}, s32[2]{0:T(128)}, u32[]{:S(2)}) copy-start(s32[2]{0:T(128)} %param.15) | copy-start | bytes 28
  2.5 34.2 %copy-start.6 = (f32[2048]{0:T(1024)S(1)}, f32[2048]{0:T(1024)}, u32[]{:S(2)}) copy-start(f32[2048]{0:T(1024)} %param.12) | copy-start | bytes 24580
  2.7 6.7 %collective-permute-start = (bf16[128,384]{1,0:T(8,128)(2,1)S(1)}, bf16[128,384]{1,0:T(8,128)(2,1)S(1)}, u32[]{:S(2)}, u32[]{:S(2)}) collective-permute-start(bf16[128,384]{1,0:T(8,128)(2,1)S(1)} %get-tuple-element.42), channel_id=1, source_target_pairs={{0,68},{8,76},{16,84},{24,92},{32,100},{40,108},{48,116},{56,124},... | collective-permute-start | bytes 294920 | tf_op jit(solution)/shard_map/ppermute | solution.py:44
  6.3 3.5 %collective-permute-start.1 = (bf16[128,384]{1,0:T(8,128)(2,1)S(1)}, bf16[128,384]{1,0:T(8,128)(2,1)S(1)}, u32[]{:S(2)}, u32[]{:S(2)}) collective-permute-start(bf16[128,384]{1,0:T(8,128)(2,1)S(1)} %get-tuple-element.43), channel_id=1, source_target_pairs={{0,1},{8,9},{16,17},{24,25},{32,33},{40,41},{48,49},{56,57},{64,65... | collective-permute-start | bytes 294920 | tf_op jit(solution)/shard_map/ppermute | solution.py:44
  7.6 4.7 %collective-permute-start.2 = (bf16[192,256]{1,0:T(8,128)(2,1)S(1)}, bf16[192,256]{1,0:T(8,128)(2,1)S(1)}, u32[]{:S(2)}, u32[]{:S(2)}) collective-permute-start(bf16[192,256]{1,0:T(8,128)(2,1)S(1)} %get-tuple-element.44), channel_id=1, source_target_pairs={{0,3},{8,11},{16,19},{24,27},{32,35},{40,43},{48,51},{56,59},{64,6... | collective-permute-start | bytes 294920 | tf_op jit(solution)/shard_map/ppermute | solution.py:44
  12.3 4.6 %collective-permute-start.3 = (bf16[256,384]{1,0:T(8,128)(2,1)S(1)}, bf16[256,384]{1,0:T(8,128)(2,1)S(1)}, u32[]{:S(2)}, u32[]{:S(2)}) collective-permute-start(bf16[256,384]{1,0:T(8,128)(2,1)S(1)} %pad_maximum_fusion.4), channel_id=1, source_target_pairs={{0,1},{8,9},{16,17},{24,25},{32,33},{40,41},{48,49},{56,57},{64,65... | collective-permute-start | bytes 589832 | tf_op jit(solution)/shard_map/ppermute | solution.py:44
  12.3 5.8 %collective-permute-start.4 = (bf16[256,384]{1,0:T(8,128)(2,1)S(1)}, bf16[256,384]{1,0:T(8,128)(2,1)S(1)}, u32[]{:S(2)}, u32[]{:S(2)}) collective-permute-start(bf16[256,384]{1,0:T(8,128)(2,1)S(1)} %pad_maximum_fusion.5), channel_id=1, source_target_pairs={{0,3},{8,11},{16,19},{24,27},{32,35},{40,43},{48,51},{56,59},{64,6... | collective-permute-start | bytes 589832 | tf_op jit(solution)/shard_map/ppermute | solution.py:44
  14.2 6.0 %collective-permute-start.5 = (bf16[384,256]{1,0:T(8,128)(2,1)S(1)}, bf16[384,256]{1,0:T(8,128)(2,1)S(1)}, u32[]{:S(2)}, u32[]{:S(2)}) collective-permute-start(bf16[384,256]{1,0:T(8,128)(2,1)S(1)} %pad_maximum_fusion.6), channel_id=1, source_target_pairs={{0,68},{8,76},{16,84},{24,92},{32,100},{40,108},{48,116},{56,124},... | collective-permute-start | bytes 589832 | tf_op jit(solution)/shard_map/ppermute | solution.py:44
  20.3 8.5 %collective-permute-start.6 = (bf16[512,384]{1,0:T(8,128)(2,1)S(1)}, bf16[512,384]{1,0:T(8,128)(2,1)}, u32[]{:S(2)}, u32[]{:S(2)}) collective-permute-start(bf16[512,384]{1,0:T(8,128)(2,1)S(1)} %pad_maximum_fusion.refs_0_), channel_id=1, source_target_pairs={{0,3},{8,11},{16,19},{24,27},{32,35},{40,43},{48,51},{56,59},{64,6... | collective-permute-start | bytes 1179656 | tf_op jit(solution)/shard_map/ppermute | solution.py:44
  21.2 12.0 %collective-permute-start.7 = (bf16[512,384]{1,0:T(8,128)(2,1)S(1)}, bf16[512,384]{1,0:T(8,128)(2,1)}, u32[]{:S(2)}, u32[]{:S(2)}) collective-permute-start(bf16[512,384]{1,0:T(8,128)(2,1)S(1)} %pad_maximum_fusion.1.refs_2_), channel_id=1, source_target_pairs={{0,68},{8,76},{16,84},{24,92},{32,100},{40,108},{48,116},{56,124},... | collective-permute-start | bytes 1179656 | tf_op jit(solution)/shard_map/ppermute | solution.py:44
  21.5 11.8 %collective-permute-start.8 = (bf16[768,256]{1,0:T(8,128)(2,1)S(1)}, bf16[768,256]{1,0:T(8,128)(2,1)S(1)}, u32[]{:S(2)}, u32[]{:S(2)}) collective-permute-start(bf16[768,256]{1,0:T(8,128)(2,1)S(1)} %pad_maximum_fusion.2.refs_4_.refs_0_), channel_id=1, source_target_pairs={{0,1},{8,9},{16,17},{24,25},{32,33},{40,41},{48,49},{56,57},{64,65... | collective-permute-start | bytes 1179656 | tf_op jit(solution)/shard_map/ppermute | solution.py:44
  21.5 12.7 %collective-permute-start.9 = (bf16[512,384]{1,0:T(8,128)(2,1)S(1)}, bf16[512,384]{1,0:T(8,128)(2,1)S(1)}, u32[]{:S(2)}, u32[]{:S(2)}) collective-permute-start(bf16[512,384]{1,0:T(8,128)(2,1)S(1)} %pad_maximum_fusion.refs_0_), channel_id=1, source_target_pairs={{0,8},{8,0},{16,24},{24,16},{32,40},{40,32},{48,56},{56,48},{64,72... | collective-permute-start | bytes 1179656 | tf_op jit(solution)/shard_map/ppermute | solution.py:44
  26.0 9.6 %collective-permute-start.11 = (bf16[512,384]{1,0:T(8,128)(2,1)S(1)}, bf16[512,384]{1,0:T(8,128)(2,1)}, u32[]{:S(2)}, u32[]{:S(2)}) collective-permute-start(bf16[512,384]{1,0:T(8,128)(2,1)S(1)} %pad_maximum_fusion.1.refs_2_), channel_id=1, source_target_pairs={{0,8},{8,0},{16,24},{24,16},{32,40},{40,32},{48,56},{56,48},{64,72... | collective-permute-start | bytes 1179656 | tf_op jit(solution)/shard_map/ppermute | solution.py:44
  28.8 6.8 %collective-permute-start.13 = (bf16[768,256]{1,0:T(8,128)(2,1)S(1)}, bf16[768,256]{1,0:T(8,128)(2,1)S(1)}, u32[]{:S(2)}, u32[]{:S(2)}) collective-permute-start(bf16[768,256]{1,0:T(8,128)(2,1)S(1)} %pad_maximum_fusion.2.refs_4_.refs_0_), channel_id=1, source_target_pairs={{0,8},{8,0},{16,24},{24,16},{32,40},{40,32},{48,56},{56,48},{64,72... | collective-permute-start | bytes 1179656 | tf_op jit(solution)/shard_map/ppermute | solution.py:44
  33.2 2.6 %collective-permute-start.10 = (bf16[512,384]{1,0:T(8,128)(2,1)}, bf16[512,384]{1,0:T(8,128)(2,1)}, u32[]{:S(2)}, u32[]{:S(2)}) collective-permute-start(bf16[512,384]{1,0:T(8,128)(2,1)} %collective-permute-done.6.refs_1_), channel_id=1, source_target_pairs={{0,8},{8,0},{16,24},{24,16},{32,40},{40,32},{48,56},{56,48},{64,72... | collective-permute-start | bytes 1179656 | tf_op jit(solution)/shard_map/ppermute | solution.py:44
  34.1 2.3 %collective-permute-start.12 = (bf16[512,384]{1,0:T(8,128)(2,1)}, bf16[512,384]{1,0:T(8,128)(2,1)}, u32[]{:S(2)}, u32[]{:S(2)}) collective-permute-start(bf16[512,384]{1,0:T(8,128)(2,1)} %collective-permute-done.7.refs_3_), channel_id=1, source_target_pairs={{0,8},{8,0},{16,24},{24,16},{32,40},{40,32},{48,56},{56,48},{64,72... | collective-permute-start | bytes 1179656 | tf_op jit(solution)/shard_map/ppermute | solution.py:44
  34.1 0.7 copy-start.2
  34.9 1.9 %collective-permute-start.14 = (bf16[768,256]{1,0:T(8,128)(2,1)S(1)}, bf16[768,256]{1,0:T(8,128)(2,1)S(1)}, u32[]{:S(2)}, u32[]{:S(2)}) collective-permute-start(bf16[768,256]{1,0:T(8,128)(2,1)S(1)} %collective-permute-done.8.refs_5_.refs_1_), channel_id=1, source_target_pairs={{0,8},{8,0},{16,24},{24,16},{32,40},{40,32},{48,56},{56,48},{64,72... | collective-permute-start | bytes 1179656 | tf_op jit(solution)/shard_map/ppermute | solution.py:44
  36.8 1.6 %copy-start.1 = (bf16[512,2048]{1,0:T(8,128)(2,1)S(1)}, bf16[512,2048]{1,0:T(8,128)(2,1)}, u32[]{:S(2)}) copy-start(bf16[512,2048]{1,0:T(8,128)(2,1)} %residual.2) | copy-start | bytes 6291460
  38.3 1.0 copy-start.3
  45.2 4.1 %collective-permute-start.17 = (bf16[2,2176]{1,0:T(2,128)(2,1)S(1)}, bf16[2,2176]{1,0:T(2,128)(2,1)S(1)}, u32[]{:S(2)}, u32[]{:S(2)}) collective-permute-start(bf16[2,2176]{1,0:T(2,128)(2,1)S(1)} %get-tuple-element.57), channel_id=1, source_target_pairs={{0,2},{8,10},{16,18},{24,26},{32,34},{40,42},{48,50},{56,58},{64,6... | collective-permute-start | bytes 26120 | tf_op jit(solution)/shard_map/ppermute | solution.py:44
  47.3 3.7 %collective-permute-start.16 = (bf16[2,2176]{1,0:T(2,128)(2,1)S(1)}, bf16[2,2176]{1,0:T(2,128)(2,1)S(1)}, u32[]{:S(2)}, u32[]{:S(2)}) collective-permute-start(bf16[2,2176]{1,0:T(2,128)(2,1)S(1)} %get-tuple-element.57), channel_id=1, source_target_pairs={{0,3},{8,11},{16,19},{24,27},{32,35},{40,43},{48,51},{56,59},{64,6... | collective-permute-start | bytes 26120 | tf_op jit(solution)/shard_map/ppermute | solution.py:44
  48.1 2.9 %collective-permute-start.15 = (bf16[2,2176]{1,0:T(2,128)(2,1)S(1)}, bf16[2,2176]{1,0:T(2,128)(2,1)S(1)}, u32[]{:S(2)}, u32[]{:S(2)}) collective-permute-start(bf16[2,2176]{1,0:T(2,128)(2,1)S(1)} %get-tuple-element.57), channel_id=1, source_target_pairs={{0,1},{8,9},{16,17},{24,25},{32,33},{40,41},{48,49},{56,57},{64,65... | collective-permute-start | bytes 26120 | tf_op jit(solution)/shard_map/ppermute | solution.py:44
  51.1 4.5 %collective-permute-start.20 = (bf16[8,2176]{1,0:T(8,128)(2,1)S(1)}, bf16[8,2176]{1,0:T(8,128)(2,1)S(1)}, u32[]{:S(2)}, u32[]{:S(2)}) collective-permute-start(bf16[8,2176]{1,0:T(8,128)(2,1)S(1)} %pad_maximum_fusion.8), channel_id=1, source_target_pairs={{0,4},{8,12},{16,20},{24,28},{32,36},{40,44},{48,52},{56,60},{64,6... | collective-permute-start | bytes 104456 | tf_op jit(solution)/shard_map/ppermute | solution.py:44
  51.2 4.5 %collective-permute-start.19 = (bf16[8,2176]{1,0:T(8,128)(2,1)S(1)}, bf16[8,2176]{1,0:T(8,128)(2,1)S(1)}, u32[]{:S(2)}, u32[]{:S(2)}) collective-permute-start(bf16[8,2176]{1,0:T(8,128)(2,1)S(1)} %pad_maximum_fusion.8), channel_id=1, source_target_pairs={{0,68},{8,76},{16,84},{24,92},{32,100},{40,108},{48,116},{56,124},... | collective-permute-start | bytes 104456 | tf_op jit(solution)/shard_map/ppermute | solution.py:44
  52.9 2.8 %collective-permute-start.18 = (bf16[8,2176]{1,0:T(8,128)(2,1)S(1)}, bf16[8,2176]{1,0:T(8,128)(2,1)S(1)}, u32[]{:S(2)}, u32[]{:S(2)}) collective-permute-start(bf16[8,2176]{1,0:T(8,128)(2,1)S(1)} %pad_maximum_fusion.8), channel_id=1, source_target_pairs={{0,64},{8,72},{16,80},{24,88},{32,96},{40,104},{48,112},{56,120},{... | collective-permute-start | bytes 104456 | tf_op jit(solution)/shard_map/ppermute | solution.py:44
  55.7 8.2 %collective-permute-start.23 = (bf16[32,2176]{1,0:T(8,128)(2,1)S(1)}, bf16[32,2176]{1,0:T(8,128)(2,1)S(1)}, u32[]{:S(2)}, u32[]{:S(2)}) collective-permute-start(bf16[32,2176]{1,0:T(8,128)(2,1)S(1)} %pad_maximum_fusion.7.refs_4_), channel_id=1, source_target_pairs={{0,32},{8,40},{16,48},{24,56},{32,0},{40,8},{48,16},{56,24},{64,96... | collective-permute-start | bytes 417800 | tf_op jit(solution)/shard_map/ppermute | solution.py:44
  59.4 7.7 %collective-permute-start.22 = (bf16[32,2176]{1,0:T(8,128)(2,1)S(1)}, bf16[32,2176]{1,0:T(8,128)(2,1)S(1)}, u32[]{:S(2)}, u32[]{:S(2)}) collective-permute-start(bf16[32,2176]{1,0:T(8,128)(2,1)S(1)} %pad_maximum_fusion.7.refs_4_), channel_id=1, source_target_pairs={{0,48},{8,56},{16,32},{24,40},{32,16},{40,24},{48,0},{56,8},{64,11... | collective-permute-start | bytes 417800 | tf_op jit(solution)/shard_map/ppermute | solution.py:44
  59.8 9.4 %collective-permute-start.21 = (bf16[32,2176]{1,0:T(8,128)(2,1)S(1)}, bf16[32,2176]{1,0:T(8,128)(2,1)S(1)}, u32[]{:S(2)}, u32[]{:S(2)}) collective-permute-start(bf16[32,2176]{1,0:T(8,128)(2,1)S(1)} %pad_maximum_fusion.7.refs_4_), channel_id=1, source_target_pairs={{0,16},{8,24},{16,0},{24,8},{32,48},{40,56},{48,32},{56,40},{64,80... | collective-permute-start | bytes 417800 | tf_op jit(solution)/shard_map/ppermute | solution.py:44
  60.1 9.1 %collective-permute-start.24 = (bf16[32,2176]{1,0:T(8,128)(2,1)S(1)}, bf16[32,2176]{1,0:T(8,128)(2,1)S(1)}, u32[]{:S(2)}, u32[]{:S(2)}) collective-permute-start(bf16[32,2176]{1,0:T(8,128)(2,1)S(1)} %pad_maximum_fusion.7.refs_4_), channel_id=1, source_target_pairs={{0,8},{8,0},{16,24},{24,16},{32,40},{40,32},{48,56},{56,48},{64,72... | collective-permute-start | bytes 417800 | tf_op jit(solution)/shard_map/ppermute | solution.py:44
  63.9 5.3 %collective-permute-start.27 = (bf16[32,2176]{1,0:T(8,128)(2,1)S(1)}, bf16[32,2176]{1,0:T(8,128)(2,1)S(1)}, u32[]{:S(2)}, u32[]{:S(2)}) collective-permute-start(bf16[32,2176]{1,0:T(8,128)(2,1)S(1)} %collective-permute-done.23.refs_7_), channel_id=1, source_target_pairs={{0,8},{8,0},{16,24},{24,16},{32,40},{40,32},{48,56},{56,48},{64,72... | collective-permute-start | bytes 417800 | tf_op jit(solution)/shard_map/ppermute | solution.py:44
  67.0 3.1 %collective-permute-start.26 = (bf16[32,2176]{1,0:T(8,128)(2,1)S(1)}, bf16[32,2176]{1,0:T(8,128)(2,1)S(1)}, u32[]{:S(2)}, u32[]{:S(2)}) collective-permute-start(bf16[32,2176]{1,0:T(8,128)(2,1)S(1)} %collective-permute-done.22.refs_6_), channel_id=1, source_target_pairs={{0,8},{8,0},{16,24},{24,16},{32,40},{40,32},{48,56},{56,48},{64,72... | collective-permute-start | bytes 417800 | tf_op jit(solution)/shard_map/ppermute | solution.py:44
  69.1 1.4 collective-permute-start.25
  75.6 3.6 %collective-permute-start.28 = (f32[8,2048]{1,0:T(8,128)S(1)}, f32[8,2048]{1,0:T(8,128)S(1)}, u32[]{:S(2)}, u32[]{:S(2)}) collective-permute-start(f32[8,2048]{1,0:T(8,128)S(1)} %get-tuple-element.59), channel_id=1, source_target_pairs={{0,16},{8,24},{16,0},{24,8},{32,48},{40,56},{48,32},{56,40},{64,80... | collective-permute-start | bytes 196616 | tf_op jit(solution)/shard_map/ppermute | solution.py:44
  75.7 4.8 %collective-permute-start.29 = (f32[8,2048]{1,0:T(8,128)S(1)}, f32[8,2048]{1,0:T(8,128)S(1)}, u32[]{:S(2)}, u32[]{:S(2)}) collective-permute-start(f32[8,2048]{1,0:T(8,128)S(1)} %get-tuple-element.60), channel_id=1, source_target_pairs={{0,48},{8,56},{16,32},{24,40},{32,16},{40,24},{48,0},{56,8},{64,11... | collective-permute-start | bytes 196616 | tf_op jit(solution)/shard_map/ppermute | solution.py:44
  77.4 4.6 %collective-permute-start.30 = (f32[8,2048]{1,0:T(8,128)S(1)}, f32[8,2048]{1,0:T(8,128)S(1)}, u32[]{:S(2)}, u32[]{:S(2)}) collective-permute-start(f32[8,2048]{1,0:T(8,128)S(1)} %get-tuple-element.61), channel_id=1, source_target_pairs={{0,32},{8,40},{16,48},{24,56},{32,0},{40,8},{48,16},{56,24},{64,96... | collective-permute-start | bytes 196616 | tf_op jit(solution)/shard_map/ppermute | solution.py:44
  82.0 3.4 %collective-permute-start.31 = (f32[8,2048]{1,0:T(8,128)S(1)}, f32[8,2048]{1,0:T(8,128)S(1)}, u32[]{:S(2)}, u32[]{:S(2)}) collective-permute-start(f32[8,2048]{1,0:T(8,128)S(1)} %add_add_fusion.refs_0_), channel_id=1, source_target_pairs={{0,64},{8,72},{16,80},{24,88},{32,96},{40,104},{48,112},{56,120},{... | collective-permute-start | bytes 196616 | tf_op jit(solution)/shard_map/ppermute | solution.py:44
  83.3 7.9 %collective-permute-start.32 = (bf16[512,1024]{1,0:T(8,128)(2,1)S(1)}, bf16[512,1024]{1,0:T(8,128)(2,1)S(1)}, u32[]{:S(2)}, u32[]{:S(2)}) collective-permute-start(bf16[512,1024]{1,0:T(8,128)(2,1)S(1)} %copy-done), channel_id=1, source_target_pairs={{0,8},{8,0},{16,24},{24,16},{32,40},{40,32},{48,56},{56,48},{64,72... | collective-permute-start | bytes 3145736 | tf_op jit(solution)/shard_map/ppermute | solution.py:44
  88.5 5.1 %collective-permute-start.33 = (bf16[512,1024]{1,0:T(8,128)(2,1)S(1)}, bf16[512,1024]{1,0:T(8,128)(2,1)S(1)}, u32[]{:S(2)}, u32[]{:S(2)}) collective-permute-start(bf16[512,1024]{1,0:T(8,128)(2,1)S(1)} %get-tuple-element.66.send), channel_id=1, source_target_pairs={{0,8},{8,0},{16,24},{24,16},{32,40},{40,32},{48,56},{56,48},{64,72... | collective-permute-start | bytes 3145736 | tf_op jit(solution)/shard_map/ppermute | solution.py:44
  93.5 6.8 %copy-start.4 = (bf16[512,384]{1,0:T(8,128)(2,1)S(1)}, bf16[512,384]{1,0:T(8,128)(2,1)}, u32[]{:S(2)}) copy-start(bf16[512,384]{1,0:T(8,128)(2,1)} %copy-done.2) | copy-start | bytes 1179652
  95.7 11.8 %collective-permute-start.41 = (bf16[256,512]{1,0:T(8,128)(2,1)S(1)}, bf16[256,512]{1,0:T(8,128)(2,1)S(1)}, u32[]{:S(2)}, u32[]{:S(2)}) collective-permute-start(bf16[256,512]{1,0:T(8,128)(2,1)S(1)} %get-tuple-element.73), channel_id=1, source_target_pairs={{0,1},{8,9},{16,17},{24,25},{32,33},{40,41},{48,49},{56,57},{64,65... | collective-permute-start | bytes 786440 | tf_op jit(solution)/shard_map/ppermute | solution.py:44
  95.8 11.7 %collective-permute-start.42 = (bf16[256,512]{1,0:T(8,128)(2,1)S(1)}, bf16[256,512]{1,0:T(8,128)(2,1)S(1)}, u32[]{:S(2)}, u32[]{:S(2)}) collective-permute-start(bf16[256,512]{1,0:T(8,128)(2,1)S(1)} %get-tuple-element.74), channel_id=1, source_target_pairs={{0,3},{8,11},{16,19},{24,27},{32,35},{40,43},{48,51},{56,59},{64,6... | collective-permute-start | bytes 786440 | tf_op jit(solution)/shard_map/ppermute | solution.py:44
  97.6 12.8 %collective-permute-start.43 = (bf16[256,512]{1,0:T(8,128)(2,1)S(1)}, bf16[256,512]{1,0:T(8,128)(2,1)S(1)}, u32[]{:S(2)}, u32[]{:S(2)}) collective-permute-start(bf16[256,512]{1,0:T(8,128)(2,1)S(1)} %get-tuple-element.75), channel_id=1, source_target_pairs={{0,2},{8,10},{16,18},{24,26},{32,34},{40,42},{48,50},{56,58},{64,6... | collective-permute-start | bytes 786440 | tf_op jit(solution)/shard_map/ppermute | solution.py:44
  99.0 13.4 %collective-permute-start.34 = (bf16[512,512]{1,0:T(8,128)(2,1)S(1)}, bf16[512,512]{1,0:T(8,128)(2,1)S(1)}, u32[]{:S(2)}, u32[]{:S(2)}) collective-permute-start(bf16[512,512]{1,0:T(8,128)(2,1)S(1)} %get-tuple-element.71), channel_id=1, source_target_pairs={{0,68},{8,76},{16,84},{24,92},{32,100},{40,108},{48,116},{56,124},... | collective-permute-start | bytes 1572872 | tf_op jit(solution)/shard_map/ppermute | solution.py:44
  110.5 6.3 %collective-permute-start.44 = (bf16[128,512]{1,0:T(8,128)(2,1)S(1)}, bf16[128,512]{1,0:T(8,128)(2,1)S(1)}, u32[]{:S(2)}, u32[]{:S(2)}) collective-permute-start(bf16[128,512]{1,0:T(8,128)(2,1)S(1)} %slice.53), channel_id=1, source_target_pairs={{0,68},{8,76},{16,84},{24,92},{32,100},{40,108},{48,116},{56,124},... | collective-permute-start | bytes 393224 | tf_op jit(solution)/shard_map/ppermute | solution.py:44
  112.7 5.1 %collective-permute-start.35 = (bf16[128,512]{1,0:T(8,128)(2,1)S(1)}, bf16[128,512]{1,0:T(8,128)(2,1)S(1)}, u32[]{:S(2)}, u32[]{:S(2)}) collective-permute-start(bf16[128,512]{1,0:T(8,128)(2,1)S(1)} %get-tuple-element.82), channel_id=1, source_target_pairs={{0,1},{8,9},{16,17},{24,25},{32,33},{40,41},{48,49},{56,57},{64,65... | collective-permute-start | bytes 393224 | tf_op jit(solution)/shard_map/ppermute | solution.py:44
  113.4 6.3 %collective-permute-start.37 = (bf16[128,512]{1,0:T(8,128)(2,1)S(1)}, bf16[128,512]{1,0:T(8,128)(2,1)S(1)}, u32[]{:S(2)}, u32[]{:S(2)}) collective-permute-start(bf16[128,512]{1,0:T(8,128)(2,1)S(1)} %get-tuple-element.83), channel_id=1, source_target_pairs={{0,2},{8,10},{16,18},{24,26},{32,34},{40,42},{48,50},{56,58},{64,6... | collective-permute-start | bytes 393224 | tf_op jit(solution)/shard_map/ppermute | solution.py:44
  115.9 5.2 %collective-permute-start.36 = (bf16[128,512]{1,0:T(8,128)(2,1)S(1)}, bf16[128,512]{1,0:T(8,128)(2,1)S(1)}, u32[]{:S(2)}, u32[]{:S(2)}) collective-permute-start(bf16[128,512]{1,0:T(8,128)(2,1)S(1)} %get-tuple-element.84), channel_id=1, source_target_pairs={{0,3},{8,11},{16,19},{24,27},{32,35},{40,43},{48,51},{56,59},{64,6... | collective-permute-start | bytes 393224 | tf_op jit(solution)/shard_map/ppermute | solution.py:44
  116.9 4.4 %collective-permute-start.45 = (bf16[128,512]{1,0:T(8,128)(2,1)S(1)}, bf16[128,512]{1,0:T(8,128)(2,1)S(1)}, u32[]{:S(2)}, u32[]{:S(2)}) collective-permute-start(bf16[128,512]{1,0:T(8,128)(2,1)S(1)} %fusion.8), channel_id=1, source_target_pairs={{0,16},{8,24},{16,0},{24,8},{32,48},{40,56},{48,32},{56,40},{64,80... | collective-permute-start | bytes 393224 | tf_op jit(solution)/shard_map/ppermute | solution.py:44
  121.1 3.9 %collective-permute-start.38 = (bf16[128,512]{1,0:T(8,128)(2,1)S(1)}, bf16[128,512]{1,0:T(8,128)(2,1)S(1)}, u32[]{:S(2)}, u32[]{:S(2)}) collective-permute-start(bf16[128,512]{1,0:T(8,128)(2,1)S(1)} %get-tuple-element.78), channel_id=1, source_target_pairs={{0,64},{8,72},{16,80},{24,88},{32,96},{40,104},{48,112},{56,120},{... | collective-permute-start | bytes 393224 | tf_op jit(solution)/shard_map/ppermute | solution.py:44
  121.3 5.1 %collective-permute-start.46 = (bf16[128,512]{1,0:T(8,128)(2,1)S(1)}, bf16[128,512]{1,0:T(8,128)(2,1)S(1)}, u32[]{:S(2)}, u32[]{:S(2)}) collective-permute-start(bf16[128,512]{1,0:T(8,128)(2,1)S(1)} %fusion.5), channel_id=1, source_target_pairs={{0,48},{8,56},{16,32},{24,40},{32,16},{40,24},{48,0},{56,8},{64,11... | collective-permute-start | bytes 393224 | tf_op jit(solution)/shard_map/ppermute | solution.py:44
  125.1 4.2 %collective-permute-start.39 = (bf16[128,512]{1,0:T(8,128)(2,1)S(1)}, bf16[128,512]{1,0:T(8,128)(2,1)S(1)}, u32[]{:S(2)}, u32[]{:S(2)}) collective-permute-start(bf16[128,512]{1,0:T(8,128)(2,1)S(1)} %fusion.4), channel_id=1, source_target_pairs={{0,16},{8,24},{16,0},{24,8},{32,48},{40,56},{48,32},{56,40},{64,80... | collective-permute-start | bytes 393224 | tf_op jit(solution)/shard_map/ppermute | solution.py:44
  126.5 4.8 %collective-permute-start.47 = (bf16[128,512]{1,0:T(8,128)(2,1)S(1)}, bf16[128,512]{1,0:T(8,128)(2,1)S(1)}, u32[]{:S(2)}, u32[]{:S(2)}) collective-permute-start(bf16[128,512]{1,0:T(8,128)(2,1)S(1)} %fusion.7), channel_id=1, source_target_pairs={{0,64},{8,72},{16,80},{24,88},{32,96},{40,104},{48,112},{56,120},{... | collective-permute-start | bytes 393224 | tf_op jit(solution)/shard_map/ppermute | solution.py:44
  129.3 5.1 %collective-permute-start.40 = (bf16[128,512]{1,0:T(8,128)(2,1)S(1)}, bf16[128,512]{1,0:T(8,128)(2,1)S(1)}, u32[]{:S(2)}, u32[]{:S(2)}) collective-permute-start(bf16[128,512]{1,0:T(8,128)(2,1)S(1)} %fusion.6), channel_id=1, source_target_pairs={{0,48},{8,56},{16,32},{24,40},{32,16},{40,24},{48,0},{56,8},{64,11... | collective-permute-start | bytes 393224 | tf_op jit(solution)/shard_map/ppermute | solution.py:44
  134.5 9.0 %collective-permute-start.48 = (bf16[128,1024]{1,0:T(8,128)(2,1)S(1)}, bf16[128,1024]{1,0:T(8,128)(2,1)S(1)}, u32[]{:S(2)}, u32[]{:S(2)}) collective-permute-start(bf16[128,1024]{1,0:T(8,128)(2,1)S(1)} %pad_maximum_fusion.3), channel_id=1, source_target_pairs={{0,8},{8,0},{16,24},{24,16},{32,40},{40,32},{48,56},{56,48},{64,72... | collective-permute-start | bytes 786440 | tf_op jit(solution)/shard_map/ppermute | solution.py:44

commit v8 on v7

--- a/solution.py
+++ b/solution.py
@@ -350,21 +350,21 @@
         context_grad[:, pl.ds(pl.multiple_of(home * block, block), block)] = value.astype(BF16)
 
 
-def blocks_kernel(kept, where, own_context, peer_context, own_grad, peer_grad, first, *seconds):
+def blocks_kernel(first_blocks, second_blocks, where, own_context, peer_context, own_grad, peer_grad, *outs):
     part = own_grad.shape[1] // 2
     block = own_context.shape[1] // 8
-
-    def product(pairs, at):
-        return contract_rows(
-            blocks_of(own_context, where, pairs, block), own_grad[:, at : at + part]
-        ) + contract_rows(blocks_of(peer_context, where, pairs, block), peer_grad[:, at : at + part])
-
-    ry = 0 if kept else 1
-    first[...] = product([(q, ry) for q in range(4)], 0).astype(first.dtype)
-    places = (0,) if kept else (1, 2, 3)
-    value = product([(q, ry) for q in places for ry in range(2)], part)
-    for n, second in enumerate(seconds):
-        second[...] = value[n * 2 * block : (n + 1) * 2 * block].astype(second.dtype)
+    outs = list(outs)
+    for at, blocks in ((0, first_blocks), (part, second_blocks)):
+        if not blocks:
+            continue
+        value = contract_rows(
+            blocks_of(own_context, where, blocks, block), own_grad[:, at : at + part]
+        ) + contract_rows(blocks_of(peer_context, where, blocks, block), peer_grad[:, at : at + part])
+        done = 0
+        while done < value.shape[0]:
+            out = outs.pop(0)
+            out[...] = value[done : done + out.shape[0]].astype(out.dtype)
+            done += out.shape[0]
 
 
 def shaped(shape, dtype=F32):
@@ -446,7 +446,7 @@
         in_specs=[SMEM, VMEM, HBM] + [VMEM] * 13,
         out_specs=(VMEM,) * 4,
         scratch_shapes=[pltpu.VMEM((tokens, width), BF16), pltpu.SemaphoreType.DMA],
-        compiler_params=params(20),
+        compiler_params=params(16),
         name="forward",
     )(ints, context, residual, gain, *pieces)
 
@@ -469,7 +469,7 @@
             pltpu.VMEM((16 * rode, columns[2]), BF16),
             pltpu.SemaphoreType.DMA((16,)),
         ],
-        compiler_params=params(24),
+        compiler_params=params(18),
         name="loss",
     )(where, gain, *riding, *emb_pieces)
     sums = [sums[0]] + [swap_z(sums[q], OFFSETS[q]) for q in (1, 2, 3)]
@@ -499,26 +499,36 @@
         name="context",
     )(where, keep, send, *pieces)
 
-    operands = (where, context, peer_context, keep, peer_grad)
-
-    def blocks(kept, dtype, name):
-        counts = 1 if kept else 3
+    def blocks(first_blocks, second_blocks, heights, dtype, operands, name):
         return pl.pallas_call(
-            functools.partial(blocks_kernel, kept),
-            out_shape=(shaped((4 * rows, part), dtype),) + (shaped((2 * rows, part), dtype),) * counts,
+            functools.partial(blocks_kernel, first_blocks, second_blocks),
+            out_shape=tuple(shaped((height * rows, half // 2), dtype) for height in heights),
             in_specs=[SMEM] + [VMEM] * 4,
-            out_specs=(VMEM,) * (1 + counts),
-            compiler_params=params(16),
+            out_specs=(VMEM,) * len(heights),
+            compiler_params=params(14),
             name=name,
-        )(*operands)
-
-    first_sent, *second_sent = blocks(False, BF16, "blocks_sent")
-    first, second = blocks(True, F32, "blocks_kept")
-    first, second, context_grad = lax.optimization_barrier((first, second, context_grad))
-    first = added(first, first_sent, swap_y, 3)
+        )(where, *operands)
+
+    def with_ry(ry):
+        return [(q, ry) for q in range(4)]
+
+    def with_q(*places):
+        return [(q, ry) for q in places for ry in range(2)]
+
+    operands = (context, peer_context, keep, peer_grad)
+    (first_sent,) = blocks(with_ry(1), [], (4,), BF16, operands, "first_sent")
+    first_sent, peer_grad = lax.optimization_barrier((first_sent, peer_grad))
+    operands = (context, peer_context, keep, peer_grad)
+    second_sent = blocks([], with_q(1, 2, 3), (2, 2, 2), BF16, operands, "second_sent")
+    first, second = blocks(with_ry(0), with_q(0), (4, 2), F32, operands, "kept")
+    arrived = [swap_y(first_sent, 3)] + [swap_x(second_sent[q - 1], OFFSETS[q]) for q in (1, 2, 3)]
+    arrived, first, second, context_grad = lax.optimization_barrier(
+        (arrived, first, second, context_grad)
+    )
+    first = first + arrived[0].astype(F32)
+    for piece in arrived[1:]:
+        second = second + piece.astype(F32)
     arrived = [swap_x(first[q * rows : (q + 1) * rows].astype(BF16), OFFSETS[q]) for q in (1, 2, 3)]
-    for q in (1, 2, 3):
-        second = second + swap_x(second_sent[q - 1], OFFSETS[q]).astype(F32)
     second = folded(second, swap_y, 3)
     first = first[:rows]
     for piece in arrived:

time: 145 us -> 145 us (level)
    pallas_call x2 -> x3, Pallas kernels: 3.72 us -> 4.46 us  [blocks(): pl.pallas_call(functools.partial(blocks_kernel, first_blocks, second_bloc...]
    unnamed x24 -> x22, local copies, waits for them, and re-layouts: 5.24 us -> 5.23 us
  transfers between devices with their start and end apart: 49 -> 49, of which waited for: 30 -> 30; matrix products, arithmetic and copies ran while one was open for 1% -> 1% of each run, Pallas kernels for 7% -> 8%
where the time goes in v8:
time: 145 us
  starting transfers between devices  71.6 us (49%)
  waiting for transfers between devices  40.5 us (28%)
  Pallas kernels  24.1 us (17%)
  local copies, waits for them, and re-layouts  5.28 us (4%)
  other arithmetic  2.19 us (2%)
    ppermute x49, starting transfers between devices, move(): return lax.ppermute(value, AXES, perm)  71.6 us
    ppermute x49, waiting for transfers between devices, move(): return lax.ppermute(value, AXES, perm)  40.5 us
    pallas_call x1, Pallas kernels, on_device(): pl.pallas_call(functools.partial(forward_kernel, items_here), out_shape=(...  5.88 us
    pallas_call x1, Pallas kernels, on_device(): pl.pallas_call(context_kernel, out_shape=shaped((tokens, head), BF16), in...  5.55 us
    unnamed x22, local copies, waits for them, and re-layouts  5.23 us
    pallas_call x1, Pallas kernels, on_device(): pl.pallas_call(functools.partial(loss_kernel, users_here, items_here, row...  5.06 us
    pallas_call x3, Pallas kernels, blocks(): pl.pallas_call(functools.partial(blocks_kernel, first_blocks, second_bloc...  4.46 us
    pallas_call x1, Pallas kernels, on_device(): pl.pallas_call(functools.partial(residual_kernel, 8 * people), out_shape=...  3.04 us
  transfers between devices with their start and end apart: 49, of which 30 were waited for; matrix products, arithmetic and copies ran while one was open for 1% of the time, Pallas kernels for 8%

profile of v8, /device:TPU:1, one launch (start us, length us, event | category | flops | bytes accessed | tf_op | source)
XLA Modules:
  0.0 144.7 jit_solution(6101593293797198776)
XLA Ops:
  0.7 1.1 copy-done.4
  2.7 3.6 %collective-permute-start = (bf16[128,384]{1,0:T(8,128)(2,1)S(1)}, bf16[128,384]{1,0:T(8,128)(2,1)S(1)}, u32[]{:S(2)}, u32[]{:S(2)}) collective-permute-start(bf16[128,384]{1,0:T(8,128)(2,1)S(1)} %get-tuple-element.47), channel_id=1, source_target_pairs={{0,68},{8,76},{16,84},{24,92},{32,100},{40,108},{48,116},{56,124},... | collective-permute-start | bytes 294920 | tf_op jit(solution)/shard_map/ppermute | solution.py:44
  6.3 1.2 collective-permute-start.1
  7.6 1.8 %collective-permute-start.2 = (bf16[192,256]{1,0:T(8,128)(2,1)S(1)}, bf16[192,256]{1,0:T(8,128)(2,1)S(1)}, u32[]{:S(2)}, u32[]{:S(2)}) collective-permute-start(bf16[192,256]{1,0:T(8,128)(2,1)S(1)} %get-tuple-element.49), channel_id=1, source_target_pairs={{0,3},{8,11},{16,19},{24,27},{32,35},{40,43},{48,51},{56,59},{64,6... | collective-permute-start | bytes 294920 | tf_op jit(solution)/shard_map/ppermute | solution.py:44
  9.8 2.4 %collective-permute-done.2 = bf16[192,256]{1,0:T(8,128)(2,1)S(1)} collective-permute-done((bf16[192,256]{1,0:T(8,128)(2,1)S(1)}, bf16[192,256]{1,0:T(8,128)(2,1)S(1)}, u32[]{:S(2)}, u32[]{:S(2)}) %collective-permute-start.2) | collective-permute-done | bytes 98336 | tf_op jit(solution)/shard_map/ppermute | solution.py:44
  12.3 1.9 %collective-permute-start.4 = (bf16[256,384]{1,0:T(8,128)(2,1)S(1)}, bf16[256,384]{1,0:T(8,128)(2,1)S(1)}, u32[]{:S(2)}, u32[]{:S(2)}) collective-permute-start(bf16[256,384]{1,0:T(8,128)(2,1)S(1)} %pad_maximum_fusion.5), channel_id=1, source_target_pairs={{0,3},{8,11},{16,19},{24,27},{32,35},{40,43},{48,51},{56,59},{64,6... | collective-permute-start | bytes 589832 | tf_op jit(solution)/shard_map/ppermute | solution.py:44
  14.6 2.2 %collective-permute-done.3 = bf16[256,384]{1,0:T(8,128)(2,1)S(1)} collective-permute-done((bf16[256,384]{1,0:T(8,128)(2,1)S(1)}, bf16[256,384]{1,0:T(8,128)(2,1)S(1)}, u32[]{:S(2)}, u32[]{:S(2)}) %collective-permute-start.3) | collective-permute-done | bytes 196640 | tf_op jit(solution)/shard_map/ppermute | solution.py:44
  16.9 1.3 collective-permute-done.4
  18.2 2.1 %collective-permute-done.5 = bf16[384,256]{1,0:T(8,128)(2,1)S(1)} collective-permute-done((bf16[384,256]{1,0:T(8,128)(2,1)S(1)}, bf16[384,256]{1,0:T(8,128)(2,1)S(1)}, u32[]{:S(2)}, u32[]{:S(2)}) %collective-permute-start.5) | collective-permute-done | bytes 196640 | tf_op jit(solution)/shard_map/ppermute | solution.py:44
  20.3 0.9 collective-permute-start.6
  21.5 4.5 %collective-permute-start.9 = (bf16[512,384]{1,0:T(8,128)(2,1)S(1)}, bf16[512,384]{1,0:T(8,128)(2,1)S(1)}, u32[]{:S(2)}, u32[]{:S(2)}) collective-permute-start(bf16[512,384]{1,0:T(8,128)(2,1)S(1)} %pad_maximum_fusion.refs_0_), channel_id=1, source_target_pairs={{0,8},{8,0},{16,24},{24,16},{32,40},{40,32},{48,56},{56,48},{64,72... | collective-permute-start | bytes 1179656 | tf_op jit(solution)/shard_map/ppermute | solution.py:44
  26.0 2.8 %collective-permute-done.6.refs_1_ = bf16[512,384]{1,0:T(8,128)(2,1)} collective-permute-done((bf16[512,384]{1,0:T(8,128)(2,1)S(1)}, bf16[512,384]{1,0:T(8,128)(2,1)}, u32[]{:S(2)}, u32[]{:S(2)}) %collective-permute-start.6) | collective-permute-done | bytes 393248 | tf_op jit(solution)/shard_map/ppermute | solution.py:44
  28.8 4.4 %collective-permute-start.13 = (bf16[768,256]{1,0:T(8,128)(2,1)S(1)}, bf16[768,256]{1,0:T(8,128)(2,1)S(1)}, u32[]{:S(2)}, u32[]{:S(2)}) collective-permute-start(bf16[768,256]{1,0:T(8,128)(2,1)S(1)} %pad_maximum_fusion.2.refs_4_.refs_0_), channel_id=1, source_target_pairs={{0,8},{8,0},{16,24},{24,16},{32,40},{40,32},{48,56},{56,48},{64,72... | collective-permute-start | bytes 1179656 | tf_op jit(solution)/shard_map/ppermute | solution.py:44
  33.2 0.9 collective-permute-start.10
  36.8 1.6 %copy-done.1 = bf16[512,2048]{1,0:T(8,128)(2,1)S(1)} copy-done((bf16[512,2048]{1,0:T(8,128)(2,1)S(1)}, bf16[512,2048]{1,0:T(8,128)(2,1)}, u32[]{:S(2)}) %copy-start.1) | copy-done | bytes 2097176
  38.4 1.0 copy-done.3
  39.3 5.9 %forward.1 = (f32[512,2048]{1,0:T(8,128)S(1)}, f32[512,1]{1,0:T(8,128)S(1)}, f32[2,2048]{1,0:T(2,128)S(1)}, bf16[2,2176]{1,0:T(2,128)(2,1)S(1)}) custom-call(s32[18]{0:T(128)S(1)} %pad_add_fusion.1.ints, bf16[512,1024]{1,0:T(8,128)(2,1)S(1)} %copy-done, bf16[512,2048]{1,0:T(8,128)(2,1)S(1)} %copy-done.1, f32[1,2048]{1,0:T(1,128)S(1)} %bitcast.7, ...), custom_call_target="tpu_custom_call" | custom-call | tf_op jit(solution)/shard_map/forward/pallas_call | solution.py:438
  45.2 2.1 %collective-permute-start.17 = (bf16[2,2176]{1,0:T(2,128)(2,1)S(1)}, bf16[2,2176]{1,0:T(2,128)(2,1)S(1)}, u32[]{:S(2)}, u32[]{:S(2)}) collective-permute-start(bf16[2,2176]{1,0:T(2,128)(2,1)S(1)} %get-tuple-element.62), channel_id=1, source_target_pairs={{0,2},{8,10},{16,18},{24,26},{32,34},{40,42},{48,50},{56,58},{64,6... | collective-permute-start | bytes 26120 | tf_op jit(solution)/shard_map/ppermute | solution.py:44
  48.2 1.2 collective-permute-done.17
  49.3 1.7 %collective-permute-done.16 = bf16[2,2176]{1,0:T(2,128)(2,1)S(1)} collective-permute-done((bf16[2,2176]{1,0:T(2,128)(2,1)S(1)}, bf16[2,2176]{1,0:T(2,128)(2,1)S(1)}, u32[]{:S(2)}, u32[]{:S(2)}) %collective-permute-start.16) | collective-permute-done | bytes 8736 | tf_op jit(solution)/shard_map/ppermute | solution.py:44
  51.2 1.7 %collective-permute-start.19 = (bf16[8,2176]{1,0:T(8,128)(2,1)S(1)}, bf16[8,2176]{1,0:T(8,128)(2,1)S(1)}, u32[]{:S(2)}, u32[]{:S(2)}) collective-permute-start(bf16[8,2176]{1,0:T(8,128)(2,1)S(1)} %pad_maximum_fusion.8), channel_id=1, source_target_pairs={{0,68},{8,76},{16,84},{24,92},{32,100},{40,108},{48,116},{56,124},... | collective-permute-start | bytes 104456 | tf_op jit(solution)/shard_map/ppermute | solution.py:44
  52.9 0.9 collective-permute-start.18
  53.8 1.7 %collective-permute-done.20 = bf16[8,2176]{1,0:T(8,128)(2,1)S(1)} collective-permute-done((bf16[8,2176]{1,0:T(8,128)(2,1)S(1)}, bf16[8,2176]{1,0:T(8,128)(2,1)S(1)}, u32[]{:S(2)}, u32[]{:S(2)}) %collective-permute-start.20) | collective-permute-done | bytes 34848 | tf_op jit(solution)/shard_map/ppermute | solution.py:44
  55.7 3.7 %collective-permute-start.23 = (bf16[32,2176]{1,0:T(8,128)(2,1)S(1)}, bf16[32,2176]{1,0:T(8,128)(2,1)S(1)}, u32[]{:S(2)}, u32[]{:S(2)}) collective-permute-start(bf16[32,2176]{1,0:T(8,128)(2,1)S(1)} %pad_maximum_fusion.7.refs_4_), channel_id=1, source_target_pairs={{0,32},{8,40},{16,48},{24,56},{32,0},{40,8},{48,16},{56,24},{64,96... | collective-permute-start | bytes 417800 | tf_op jit(solution)/shard_map/ppermute | solution.py:44
  60.1 3.8 %collective-permute-start.24 = (bf16[32,2176]{1,0:T(8,128)(2,1)S(1)}, bf16[32,2176]{1,0:T(8,128)(2,1)S(1)}, u32[]{:S(2)}, u32[]{:S(2)}) collective-permute-start(bf16[32,2176]{1,0:T(8,128)(2,1)S(1)} %pad_maximum_fusion.7.refs_4_), channel_id=1, source_target_pairs={{0,8},{8,0},{16,24},{24,16},{32,40},{40,32},{48,56},{56,48},{64,72... | collective-permute-start | bytes 417800 | tf_op jit(solution)/shard_map/ppermute | solution.py:44
  63.9 3.1 %collective-permute-start.27 = (bf16[32,2176]{1,0:T(8,128)(2,1)S(1)}, bf16[32,2176]{1,0:T(8,128)(2,1)S(1)}, u32[]{:S(2)}, u32[]{:S(2)}) collective-permute-start(bf16[32,2176]{1,0:T(8,128)(2,1)S(1)} %collective-permute-done.23.refs_7_), channel_id=1, source_target_pairs={{0,8},{8,0},{16,24},{24,16},{32,40},{40,32},{48,56},{56,48},{64,72... | collective-permute-start | bytes 417800 | tf_op jit(solution)/shard_map/ppermute | solution.py:44
  67.0 2.1 %collective-permute-start.26 = (bf16[32,2176]{1,0:T(8,128)(2,1)S(1)}, bf16[32,2176]{1,0:T(8,128)(2,1)S(1)}, u32[]{:S(2)}, u32[]{:S(2)}) collective-permute-start(bf16[32,2176]{1,0:T(8,128)(2,1)S(1)} %collective-permute-done.22.refs_6_), channel_id=1, source_target_pairs={{0,8},{8,0},{16,24},{24,16},{32,40},{40,32},{48,56},{56,48},{64,72... | collective-permute-start | bytes 417800 | tf_op jit(solution)/shard_map/ppermute | solution.py:44
  69.2 1.0 collective-permute-done.26.refs_10_
  70.5 5.1 %loss.1 = (f32[8,2048]{1,0:T(8,128)S(1)}, f32[8,2048]{1,0:T(8,128)S(1)}, f32[8,2048]{1,0:T(8,128)S(1)}, f32[8,2048]{1,0:T(8,128)S(1)}, bf16[8,2048]{1,0:T(8,128)(2,1)}) custom-call(s32[4]{0:T(128)S(1)} %pad_add_fusion.where, f32[1,2048]{1,0:T(1,128)S(1)} %bitcast.8, bf16[768,256]{1,0:T(8,128)(2,1)S(1)} %pad_maximum_fusion.2.refs_4_.refs_0_, ...), custom_call_target="tpu_custom_call" | custom-call | tf_op jit(solution)/shard_map/loss/pallas_call | solution.py:461
  75.7 1.7 %collective-permute-start.29 = (f32[8,2048]{1,0:T(8,128)S(1)}, f32[8,2048]{1,0:T(8,128)S(1)}, u32[]{:S(2)}, u32[]{:S(2)}) collective-permute-start(f32[8,2048]{1,0:T(8,128)S(1)} %get-tuple-element.65), channel_id=1, source_target_pairs={{0,48},{8,56},{16,32},{24,40},{32,16},{40,24},{48,0},{56,8},{64,11... | collective-permute-start | bytes 196616 | tf_op jit(solution)/shard_map/ppermute | solution.py:44
  77.4 1.5 %collective-permute-start.30 = (f32[8,2048]{1,0:T(8,128)S(1)}, f32[8,2048]{1,0:T(8,128)S(1)}, u32[]{:S(2)}, u32[]{:S(2)}) collective-permute-start(f32[8,2048]{1,0:T(8,128)S(1)} %get-tuple-element.66), channel_id=1, source_target_pairs={{0,32},{8,40},{16,48},{24,56},{32,0},{40,8},{48,16},{56,24},{64,96... | collective-permute-start | bytes 196616 | tf_op jit(solution)/shard_map/ppermute | solution.py:44
  79.2 1.3 collective-permute-done.29
  80.4 1.6 %collective-permute-done.30 = f32[8,2048]{1,0:T(8,128)S(1)} collective-permute-done((f32[8,2048]{1,0:T(8,128)S(1)}, f32[8,2048]{1,0:T(8,128)S(1)}, u32[]{:S(2)}, u32[]{:S(2)}) %collective-permute-start.30) | collective-permute-done | bytes 65568 | tf_op jit(solution)/shard_map/ppermute | solution.py:44
  82.1 1.3 collective-permute-start.31
  83.3 2.1 %collective-permute-start.32 = (bf16[512,1024]{1,0:T(8,128)(2,1)S(1)}, bf16[512,1024]{1,0:T(8,128)(2,1)S(1)}, u32[]{:S(2)}, u32[]{:S(2)}) collective-permute-start(bf16[512,1024]{1,0:T(8,128)(2,1)S(1)} %copy-done), channel_id=1, source_target_pairs={{0,8},{8,0},{16,24},{24,16},{32,40},{40,32},{48,56},{56,48},{64,72... | collective-permute-start | bytes 3145736 | tf_op jit(solution)/shard_map/ppermute | solution.py:44
  85.4 3.0 %residual.3 = (bf16[512,2048]{1,0:T(8,128)(2,1)}, bf16[512,1024]{1,0:T(8,128)(2,1)S(1)}, bf16[512,1024]{1,0:T(8,128)(2,1)S(1)}, f32[1,2048]{1,0:T(1,128)}, f32[1,1]{1,0:T(1,128)}) custom-call(s32[4]{0:T(128)S(1)} %pad_add_fusion.where, s32[2]{0:T(128)S(1)} %copy-done.7, f32[512,2048]{1,0:T(8,128)S(1)} %get-tuple-element.59.stream, ...), custom_call_target="tpu_custom_call" | custom-call | tf_op jit(solution)/shard_map/residual/pallas_call | solution.py:478
  88.5 2.8 %collective-permute-start.33 = (bf16[512,1024]{1,0:T(8,128)(2,1)S(1)}, bf16[512,1024]{1,0:T(8,128)(2,1)S(1)}, u32[]{:S(2)}, u32[]{:S(2)}) collective-permute-start(bf16[512,1024]{1,0:T(8,128)(2,1)S(1)} %get-tuple-element.71.send), channel_id=1, source_target_pairs={{0,8},{8,0},{16,24},{24,16},{32,40},{40,32},{48,56},{56,48},{64,72... | collective-permute-start | bytes 3145736 | tf_op jit(solution)/shard_map/ppermute | solution.py:44
  91.3 2.3 %collective-permute-done.33.peer_grad = bf16[512,1024]{1,0:T(8,128)(2,1)S(1)} collective-permute-done((bf16[512,1024]{1,0:T(8,128)(2,1)S(1)}, bf16[512,1024]{1,0:T(8,128)(2,1)S(1)}, u32[]{:S(2)}, u32[]{:S(2)}) %collective-permute-start.33) | collective-permute-done | bytes 1048608 | tf_op jit(solution)/shard_map/ppermute | solution.py:44
  93.6 1.3 first_sent.1
  94.9 1.4 collective-permute-start.34
  96.3 1.6 %second_sent.1 = (bf16[256,512]{1,0:T(8,128)(2,1)S(1)}, bf16[256,512]{1,0:T(8,128)(2,1)S(1)}, bf16[256,512]{1,0:T(8,128)(2,1)S(1)}) custom-call(s32[4]{0:T(128)S(1)} %pad_add_fusion.where, bf16[512,1024]{1,0:T(8,128)(2,1)S(1)} %copy-done, bf16[512,1024]{1,0:T(8,128)(2,1)S(1)} %collective-permute-done.32.peer_context, ...), custom_call_target="tpu_custom_call" | custom-call | tf_op jit(solution)/shard_map/second_sent/pallas_call | solution.py:503
  97.9 1.8 %collective-permute-start.36 = (bf16[256,512]{1,0:T(8,128)(2,1)S(1)}, bf16[256,512]{1,0:T(8,128)(2,1)S(1)}, u32[]{:S(2)}, u32[]{:S(2)}) collective-permute-start(bf16[256,512]{1,0:T(8,128)(2,1)S(1)} %get-tuple-element.75), channel_id=1, source_target_pairs={{0,3},{8,11},{16,19},{24,27},{32,35},{40,43},{48,51},{56,59},{64,6... | collective-permute-start | bytes 786440 | tf_op jit(solution)/shard_map/ppermute | solution.py:44
  99.8 1.4 collective-permute-start.37
  101.2 5.6 %context.3 = bf16[512,1024]{1,0:T(8,128)(2,1)} custom-call(s32[4]{0:T(128)S(1)} %pad_add_fusion.where, bf16[512,1024]{1,0:T(8,128)(2,1)S(1)} %get-tuple-element.70.own_grad.keep, bf16[512,1024]{1,0:T(8,128)(2,1)S(1)} %get-tuple-element.71.send, bf16[512,384]{1,0:T(8,128)(2,1)S(1)} %pad_maximum_fusion.refs_0_, ...), custom_call_target="tpu_custom_call" | custom-call | tf_op jit(solution)/shard_map/context/pallas_call | solution.py:493
  106.7 1.6 %kept.1 = (f32[512,512]{1,0:T(8,128)S(1)}, f32[256,512]{1,0:T(8,128)S(1)}) custom-call(s32[4]{0:T(128)S(1)} %pad_add_fusion.where, bf16[512,1024]{1,0:T(8,128)(2,1)S(1)} %copy-done, bf16[512,1024]{1,0:T(8,128)(2,1)S(1)} %collective-permute-done.32.peer_context, bf16[512,1024]{1,0:T(8,128)(2,1)S(1)} %get-tuple-element.70.own_grad.keep, ...), custom_call_target="tpu_custom_call" | custom-call | tf_op jit(solution)/shard_map/kept/pallas_call | solution.py:503
  108.3 3.9 %collective-permute-done.37 = bf16[256,512]{1,0:T(8,128)(2,1)S(1)} collective-permute-done((bf16[256,512]{1,0:T(8,128)(2,1)S(1)}, bf16[256,512]{1,0:T(8,128)(2,1)S(1)}, u32[]{:S(2)}, u32[]{:S(2)}) %collective-permute-start.37) | collective-permute-done | bytes 262176 | tf_op jit(solution)/shard_map/ppermute | solution.py:44
  112.4 1.5 %collective-permute-start.44 = (bf16[128,512]{1,0:T(8,128)(2,1)S(1)}, bf16[128,512]{1,0:T(8,128)(2,1)S(1)}, u32[]{:S(2)}, u32[]{:S(2)}) collective-permute-start(bf16[128,512]{1,0:T(8,128)(2,1)S(1)} %slice.53), channel_id=1, source_target_pairs={{0,68},{8,76},{16,84},{24,92},{32,100},{40,108},{48,116},{56,124},... | collective-permute-start | bytes 393224 | tf_op jit(solution)/shard_map/ppermute | solution.py:44
  114.4 2.1 %collective-permute-start.40 = (bf16[128,512]{1,0:T(8,128)(2,1)S(1)}, bf16[128,512]{1,0:T(8,128)(2,1)S(1)}, u32[]{:S(2)}, u32[]{:S(2)}) collective-permute-start(bf16[128,512]{1,0:T(8,128)(2,1)S(1)} %get-tuple-element.93), channel_id=1, source_target_pairs={{0,2},{8,10},{16,18},{24,26},{32,34},{40,42},{48,50},{56,58},{64,6... | collective-permute-start | bytes 393224 | tf_op jit(solution)/shard_map/ppermute | solution.py:44
  116.5 1.7 %collective-permute-start.39 = (bf16[128,512]{1,0:T(8,128)(2,1)S(1)}, bf16[128,512]{1,0:T(8,128)(2,1)S(1)}, u32[]{:S(2)}, u32[]{:S(2)}) collective-permute-start(bf16[128,512]{1,0:T(8,128)(2,1)S(1)} %get-tuple-element.94), channel_id=1, source_target_pairs={{0,3},{8,11},{16,19},{24,27},{32,35},{40,43},{48,51},{56,59},{64,6... | collective-permute-start | bytes 393224 | tf_op jit(solution)/shard_map/ppermute | solution.py:44
  118.3 0.9 collective-permute-start.45
  119.2 1.1 collective-permute-done.40
  120.3 1.4 collective-permute-done.39
  122.6 0.9 collective-permute-start.46
  123.5 2.2 %collective-permute-done.41 = bf16[128,512]{1,0:T(8,128)(2,1)S(1)} collective-permute-done((bf16[128,512]{1,0:T(8,128)(2,1)S(1)}, bf16[128,512]{1,0:T(8,128)(2,1)S(1)}, u32[]{:S(2)}, u32[]{:S(2)}) %collective-permute-start.41) | collective-permute-done | bytes 131104 | tf_op jit(solution)/shard_map/ppermute | solution.py:44
  125.7 0.9 collective-permute-start.42
  126.6 1.0 collective-permute-done.46
  127.7 0.9 collective-permute-start.47
  128.6 1.2 collective-permute-done.42
  129.9 0.9 collective-permute-start.43
  130.9 1.1 collective-permute-done.47
  132.1 3.0 %collective-permute-done.43 = bf16[128,512]{1,0:T(8,128)(2,1)S(1)} collective-permute-done((bf16[128,512]{1,0:T(8,128)(2,1)S(1)}, bf16[128,512]{1,0:T(8,128)(2,1)S(1)}, u32[]{:S(2)}, u32[]{:S(2)}) %collective-permute-start.43) | collective-permute-done | bytes 131104 | tf_op jit(solution)/shard_map/ppermute | solution.py:44
  135.2 7.5 %collective-permute-start.48 = (bf16[128,1024]{1,0:T(8,128)(2,1)S(1)}, bf16[128,1024]{1,0:T(8,128)(2,1)S(1)}, u32[]{:S(2)}, u32[]{:S(2)}) collective-permute-start(bf16[128,1024]{1,0:T(8,128)(2,1)S(1)} %pad_maximum_fusion.3), channel_id=1, source_target_pairs={{0,8},{8,0},{16,24},{24,16},{32,40},{40,32},{48,56},{56,48},{64,72... | collective-permute-start | bytes 786440 | tf_op jit(solution)/shard_map/ppermute | solution.py:44
  142.6 1.2 collective-permute-done.48
  143.8 0.9 maximum_select_fusion
  (89 shorter events, 9.5 us)
Async XLA Ops:
  0.6 36.1 %copy-start = (bf16[512,1024]{1,0:T(8,128)(2,1)S(1)}, bf16[512,1024]{1,0:T(8,128)(2,1)}, u32[]{:S(2)}) copy-start(bf16[512,1024]{1,0:T(8,128)(2,1)} %own_context.5) | copy-start | bytes 3145732
  0.6 1.1 copy-start.4
  1.8 0.8 copy-start.6
  2.5 32.9 %copy-start.7 = (s32[2]{0:T(128)S(1)}, s32[2]{0:T(128)}, u32[]{:S(2)}) copy-start(s32[2]{0:T(128)} %lengths.1) | copy-start | bytes 28
  2.5 32.9 %copy-start.8 = (s32[8]{0:T(128)S(1)}, s32[8]{0:T(128)}, u32[]{:S(2)}) copy-start(s32[8]{0:T(128)} %param.14) | copy-start | bytes 100
  2.5 32.9 %copy-start.9 = (s32[2]{0:T(128)S(1)}, s32[2]{0:T(128)}, u32[]{:S(2)}) copy-start(s32[2]{0:T(128)} %param.16) | copy-start | bytes 28
  2.5 33.0 %copy-start.10 = (s32[2]{0:T(128)S(1)}, s32[2]{0:T(128)}, u32[]{:S(2)}) copy-start(s32[2]{0:T(128)} %param.15) | copy-start | bytes 28
  2.5 34.2 %copy-start.5 = (f32[2048]{0:T(1024)S(1)}, f32[2048]{0:T(1024)}, u32[]{:S(2)}) copy-start(f32[2048]{0:T(1024)} %param.12) | copy-start | bytes 24580
  2.7 6.7 %collective-permute-start = (bf16[128,384]{1,0:T(8,128)(2,1)S(1)}, bf16[128,384]{1,0:T(8,128)(2,1)S(1)}, u32[]{:S(2)}, u32[]{:S(2)}) collective-permute-start(bf16[128,384]{1,0:T(8,128)(2,1)S(1)} %get-tuple-element.47), channel_id=1, source_target_pairs={{0,68},{8,76},{16,84},{24,92},{32,100},{40,108},{48,116},{56,124},... | collective-permute-start | bytes 294920 | tf_op jit(solution)/shard_map/ppermute | solution.py:44
  6.3 3.5 %collective-permute-start.1 = (bf16[128,384]{1,0:T(8,128)(2,1)S(1)}, bf16[128,384]{1,0:T(8,128)(2,1)S(1)}, u32[]{:S(2)}, u32[]{:S(2)}) collective-permute-start(bf16[128,384]{1,0:T(8,128)(2,1)S(1)} %get-tuple-element.48), channel_id=1, source_target_pairs={{0,1},{8,9},{16,17},{24,25},{32,33},{40,41},{48,49},{56,57},{64,65... | collective-permute-start | bytes 294920 | tf_op jit(solution)/shard_map/ppermute | solution.py:44
  7.6 4.7 %collective-permute-start.2 = (bf16[192,256]{1,0:T(8,128)(2,1)S(1)}, bf16[192,256]{1,0:T(8,128)(2,1)S(1)}, u32[]{:S(2)}, u32[]{:S(2)}) collective-permute-start(bf16[192,256]{1,0:T(8,128)(2,1)S(1)} %get-tuple-element.49), channel_id=1, source_target_pairs={{0,3},{8,11},{16,19},{24,27},{32,35},{40,43},{48,51},{56,59},{64,6... | collective-permute-start | bytes 294920 | tf_op jit(solution)/shard_map/ppermute | solution.py:44
  12.3 4.6 %collective-permute-start.3 = (bf16[256,384]{1,0:T(8,128)(2,1)S(1)}, bf16[256,384]{1,0:T(8,128)(2,1)S(1)}, u32[]{:S(2)}, u32[]{:S(2)}) collective-permute-start(bf16[256,384]{1,0:T(8,128)(2,1)S(1)} %pad_maximum_fusion.4), channel_id=1, source_target_pairs={{0,1},{8,9},{16,17},{24,25},{32,33},{40,41},{48,49},{56,57},{64,65... | collective-permute-start | bytes 589832 | tf_op jit(solution)/shard_map/ppermute | solution.py:44
  12.3 5.8 %collective-permute-start.4 = (bf16[256,384]{1,0:T(8,128)(2,1)S(1)}, bf16[256,384]{1,0:T(8,128)(2,1)S(1)}, u32[]{:S(2)}, u32[]{:S(2)}) collective-permute-start(bf16[256,384]{1,0:T(8,128)(2,1)S(1)} %pad_maximum_fusion.5), channel_id=1, source_target_pairs={{0,3},{8,11},{16,19},{24,27},{32,35},{40,43},{48,51},{56,59},{64,6... | collective-permute-start | bytes 589832 | tf_op jit(solution)/shard_map/ppermute | solution.py:44
  14.2 6.0 %collective-permute-start.5 = (bf16[384,256]{1,0:T(8,128)(2,1)S(1)}, bf16[384,256]{1,0:T(8,128)(2,1)S(1)}, u32[]{:S(2)}, u32[]{:S(2)}) collective-permute-start(bf16[384,256]{1,0:T(8,128)(2,1)S(1)} %pad_maximum_fusion.6), channel_id=1, source_target_pairs={{0,68},{8,76},{16,84},{24,92},{32,100},{40,108},{48,116},{56,124},... | collective-permute-start | bytes 589832 | tf_op jit(solution)/shard_map/ppermute | solution.py:44
  20.3 8.5 %collective-permute-start.6 = (bf16[512,384]{1,0:T(8,128)(2,1)S(1)}, bf16[512,384]{1,0:T(8,128)(2,1)}, u32[]{:S(2)}, u32[]{:S(2)}) collective-permute-start(bf16[512,384]{1,0:T(8,128)(2,1)S(1)} %pad_maximum_fusion.refs_0_), channel_id=1, source_target_pairs={{0,3},{8,11},{16,19},{24,27},{32,35},{40,43},{48,51},{56,59},{64,6... | collective-permute-start | bytes 1179656 | tf_op jit(solution)/shard_map/ppermute | solution.py:44
  21.2 12.0 %collective-permute-start.7 = (bf16[512,384]{1,0:T(8,128)(2,1)S(1)}, bf16[512,384]{1,0:T(8,128)(2,1)}, u32[]{:S(2)}, u32[]{:S(2)}) collective-permute-start(bf16[512,384]{1,0:T(8,128)(2,1)S(1)} %pad_maximum_fusion.1.refs_2_), channel_id=1, source_target_pairs={{0,68},{8,76},{16,84},{24,92},{32,100},{40,108},{48,116},{56,124},... | collective-permute-start | bytes 1179656 | tf_op jit(solution)/shard_map/ppermute | solution.py:44
  21.5 11.8 %collective-permute-start.8 = (bf16[768,256]{1,0:T(8,128)(2,1)S(1)}, bf16[768,256]{1,0:T(8,128)(2,1)S(1)}, u32[]{:S(2)}, u32[]{:S(2)}) collective-permute-start(bf16[768,256]{1,0:T(8,128)(2,1)S(1)} %pad_maximum_fusion.2.refs_4_.refs_0_), channel_id=1, source_target_pairs={{0,1},{8,9},{16,17},{24,25},{32,33},{40,41},{48,49},{56,57},{64,65... | collective-permute-start | bytes 1179656 | tf_op jit(solution)/shard_map/ppermute | solution.py:44
  21.5 12.7 %collective-permute-start.9 = (bf16[512,384]{1,0:T(8,128)(2,1)S(1)}, bf16[512,384]{1,0:T(8,128)(2,1)S(1)}, u32[]{:S(2)}, u32[]{:S(2)}) collective-permute-start(bf16[512,384]{1,0:T(8,128)(2,1)S(1)} %pad_maximum_fusion.refs_0_), channel_id=1, source_target_pairs={{0,8},{8,0},{16,24},{24,16},{32,40},{40,32},{48,56},{56,48},{64,72... | collective-permute-start | bytes 1179656 | tf_op jit(solution)/shard_map/ppermute | solution.py:44
  26.0 9.6 %collective-permute-start.11 = (bf16[512,384]{1,0:T(8,128)(2,1)S(1)}, bf16[512,384]{1,0:T(8,128)(2,1)}, u32[]{:S(2)}, u32[]{:S(2)}) collective-permute-start(bf16[512,384]{1,0:T(8,128)(2,1)S(1)} %pad_maximum_fusion.1.refs_2_), channel_id=1, source_target_pairs={{0,8},{8,0},{16,24},{24,16},{32,40},{40,32},{48,56},{56,48},{64,72... | collective-permute-start | bytes 1179656 | tf_op jit(solution)/shard_map/ppermute | solution.py:44
  28.8 6.8 %collective-permute-start.13 = (bf16[768,256]{1,0:T(8,128)(2,1)S(1)}, bf16[768,256]{1,0:T(8,128)(2,1)S(1)}, u32[]{:S(2)}, u32[]{:S(2)}) collective-permute-start(bf16[768,256]{1,0:T(8,128)(2,1)S(1)} %pad_maximum_fusion.2.refs_4_.refs_0_), channel_id=1, source_target_pairs={{0,8},{8,0},{16,24},{24,16},{32,40},{40,32},{48,56},{56,48},{64,72... | collective-permute-start | bytes 1179656 | tf_op jit(solution)/shard_map/ppermute | solution.py:44
  33.2 2.6 %collective-permute-start.10 = (bf16[512,384]{1,0:T(8,128)(2,1)}, bf16[512,384]{1,0:T(8,128)(2,1)}, u32[]{:S(2)}, u32[]{:S(2)}) collective-permute-start(bf16[512,384]{1,0:T(8,128)(2,1)} %collective-permute-done.6.refs_1_), channel_id=1, source_target_pairs={{0,8},{8,0},{16,24},{24,16},{32,40},{40,32},{48,56},{56,48},{64,72... | collective-permute-start | bytes 1179656 | tf_op jit(solution)/shard_map/ppermute | solution.py:44
  34.1 2.3 %collective-permute-start.12 = (bf16[512,384]{1,0:T(8,128)(2,1)}, bf16[512,384]{1,0:T(8,128)(2,1)}, u32[]{:S(2)}, u32[]{:S(2)}) collective-permute-start(bf16[512,384]{1,0:T(8,128)(2,1)} %collective-permute-done.7.refs_3_), channel_id=1, source_target_pairs={{0,8},{8,0},{16,24},{24,16},{32,40},{40,32},{48,56},{56,48},{64,72... | collective-permute-start | bytes 1179656 | tf_op jit(solution)/shard_map/ppermute | solution.py:44
  34.1 0.7 copy-start.2
  34.9 1.9 %collective-permute-start.14 = (bf16[768,256]{1,0:T(8,128)(2,1)S(1)}, bf16[768,256]{1,0:T(8,128)(2,1)S(1)}, u32[]{:S(2)}, u32[]{:S(2)}) collective-permute-start(bf16[768,256]{1,0:T(8,128)(2,1)S(1)} %collective-permute-done.8.refs_5_.refs_1_), channel_id=1, source_target_pairs={{0,8},{8,0},{16,24},{24,16},{32,40},{40,32},{48,56},{56,48},{64,72... | collective-permute-start | bytes 1179656 | tf_op jit(solution)/shard_map/ppermute | solution.py:44
  36.8 1.6 %copy-start.1 = (bf16[512,2048]{1,0:T(8,128)(2,1)S(1)}, bf16[512,2048]{1,0:T(8,128)(2,1)}, u32[]{:S(2)}) copy-start(bf16[512,2048]{1,0:T(8,128)(2,1)} %residual.2) | copy-start | bytes 6291460
  38.3 1.0 copy-start.3
  45.2 4.1 %collective-permute-start.17 = (bf16[2,2176]{1,0:T(2,128)(2,1)S(1)}, bf16[2,2176]{1,0:T(2,128)(2,1)S(1)}, u32[]{:S(2)}, u32[]{:S(2)}) collective-permute-start(bf16[2,2176]{1,0:T(2,128)(2,1)S(1)} %get-tuple-element.62), channel_id=1, source_target_pairs={{0,2},{8,10},{16,18},{24,26},{32,34},{40,42},{48,50},{56,58},{64,6... | collective-permute-start | bytes 26120 | tf_op jit(solution)/shard_map/ppermute | solution.py:44
  47.3 3.7 %collective-permute-start.16 = (bf16[2,2176]{1,0:T(2,128)(2,1)S(1)}, bf16[2,2176]{1,0:T(2,128)(2,1)S(1)}, u32[]{:S(2)}, u32[]{:S(2)}) collective-permute-start(bf16[2,2176]{1,0:T(2,128)(2,1)S(1)} %get-tuple-element.62), channel_id=1, source_target_pairs={{0,3},{8,11},{16,19},{24,27},{32,35},{40,43},{48,51},{56,59},{64,6... | collective-permute-start | bytes 26120 | tf_op jit(solution)/shard_map/ppermute | solution.py:44
  48.2 2.9 %collective-permute-start.15 = (bf16[2,2176]{1,0:T(2,128)(2,1)S(1)}, bf16[2,2176]{1,0:T(2,128)(2,1)S(1)}, u32[]{:S(2)}, u32[]{:S(2)}) collective-permute-start(bf16[2,2176]{1,0:T(2,128)(2,1)S(1)} %get-tuple-element.62), channel_id=1, source_target_pairs={{0,1},{8,9},{16,17},{24,25},{32,33},{40,41},{48,49},{56,57},{64,65... | collective-permute-start | bytes 26120 | tf_op jit(solution)/shard_map/ppermute | solution.py:44
  51.1 4.5 %collective-permute-start.20 = (bf16[8,2176]{1,0:T(8,128)(2,1)S(1)}, bf16[8,2176]{1,0:T(8,128)(2,1)S(1)}, u32[]{:S(2)}, u32[]{:S(2)}) collective-permute-start(bf16[8,2176]{1,0:T(8,128)(2,1)S(1)} %pad_maximum_fusion.8), channel_id=1, source_target_pairs={{0,4},{8,12},{16,20},{24,28},{32,36},{40,44},{48,52},{56,60},{64,6... | collective-permute-start | bytes 104456 | tf_op jit(solution)/shard_map/ppermute | solution.py:44
  51.2 4.5 %collective-permute-start.19 = (bf16[8,2176]{1,0:T(8,128)(2,1)S(1)}, bf16[8,2176]{1,0:T(8,128)(2,1)S(1)}, u32[]{:S(2)}, u32[]{:S(2)}) collective-permute-start(bf16[8,2176]{1,0:T(8,128)(2,1)S(1)} %pad_maximum_fusion.8), channel_id=1, source_target_pairs={{0,68},{8,76},{16,84},{24,92},{32,100},{40,108},{48,116},{56,124},... | collective-permute-start | bytes 104456 | tf_op jit(solution)/shard_map/ppermute | solution.py:44
  52.9 2.8 %collective-permute-start.18 = (bf16[8,2176]{1,0:T(8,128)(2,1)S(1)}, bf16[8,2176]{1,0:T(8,128)(2,1)S(1)}, u32[]{:S(2)}, u32[]{:S(2)}) collective-permute-start(bf16[8,2176]{1,0:T(8,128)(2,1)S(1)} %pad_maximum_fusion.8), channel_id=1, source_target_pairs={{0,64},{8,72},{16,80},{24,88},{32,96},{40,104},{48,112},{56,120},{... | collective-permute-start | bytes 104456 | tf_op jit(solution)/shard_map/ppermute | solution.py:44
  55.7 8.2 %collective-permute-start.23 = (bf16[32,2176]{1,0:T(8,128)(2,1)S(1)}, bf16[32,2176]{1,0:T(8,128)(2,1)S(1)}, u32[]{:S(2)}, u32[]{:S(2)}) collective-permute-start(bf16[32,2176]{1,0:T(8,128)(2,1)S(1)} %pad_maximum_fusion.7.refs_4_), channel_id=1, source_target_pairs={{0,32},{8,40},{16,48},{24,56},{32,0},{40,8},{48,16},{56,24},{64,96... | collective-permute-start | bytes 417800 | tf_op jit(solution)/shard_map/ppermute | solution.py:44
  59.4 7.7 %collective-permute-start.22 = (bf16[32,2176]{1,0:T(8,128)(2,1)S(1)}, bf16[32,2176]{1,0:T(8,128)(2,1)S(1)}, u32[]{:S(2)}, u32[]{:S(2)}) collective-permute-start(bf16[32,2176]{1,0:T(8,128)(2,1)S(1)} %pad_maximum_fusion.7.refs_4_), channel_id=1, source_target_pairs={{0,48},{8,56},{16,32},{24,40},{32,16},{40,24},{48,0},{56,8},{64,11... | collective-permute-start | bytes 417800 | tf_op jit(solution)/shard_map/ppermute | solution.py:44
  59.8 9.4 %collective-permute-start.21 = (bf16[32,2176]{1,0:T(8,128)(2,1)S(1)}, bf16[32,2176]{1,0:T(8,128)(2,1)S(1)}, u32[]{:S(2)}, u32[]{:S(2)}) collective-permute-start(bf16[32,2176]{1,0:T(8,128)(2,1)S(1)} %pad_maximum_fusion.7.refs_4_), channel_id=1, source_target_pairs={{0,16},{8,24},{16,0},{24,8},{32,48},{40,56},{48,32},{56,40},{64,80... | collective-permute-start | bytes 417800 | tf_op jit(solution)/shard_map/ppermute | solution.py:44
  60.1 9.1 %collective-permute-start.24 = (bf16[32,2176]{1,0:T(8,128)(2,1)S(1)}, bf16[32,2176]{1,0:T(8,128)(2,1)S(1)}, u32[]{:S(2)}, u32[]{:S(2)}) collective-permute-start(bf16[32,2176]{1,0:T(8,128)(2,1)S(1)} %pad_maximum_fusion.7.refs_4_), channel_id=1, source_target_pairs={{0,8},{8,0},{16,24},{24,16},{32,40},{40,32},{48,56},{56,48},{64,72... | collective-permute-start | bytes 417800 | tf_op jit(solution)/shard_map/ppermute | solution.py:44
  63.9 5.3 %collective-permute-start.27 = (bf16[32,2176]{1,0:T(8,128)(2,1)S(1)}, bf16[32,2176]{1,0:T(8,128)(2,1)S(1)}, u32[]{:S(2)}, u32[]{:S(2)}) collective-permute-start(bf16[32,2176]{1,0:T(8,128)(2,1)S(1)} %collective-permute-done.23.refs_7_), channel_id=1, source_target_pairs={{0,8},{8,0},{16,24},{24,16},{32,40},{40,32},{48,56},{56,48},{64,72... | collective-permute-start | bytes 417800 | tf_op jit(solution)/shard_map/ppermute | solution.py:44
  67.0 3.1 %collective-permute-start.26 = (bf16[32,2176]{1,0:T(8,128)(2,1)S(1)}, bf16[32,2176]{1,0:T(8,128)(2,1)S(1)}, u32[]{:S(2)}, u32[]{:S(2)}) collective-permute-start(bf16[32,2176]{1,0:T(8,128)(2,1)S(1)} %collective-permute-done.22.refs_6_), channel_id=1, source_target_pairs={{0,8},{8,0},{16,24},{24,16},{32,40},{40,32},{48,56},{56,48},{64,72... | collective-permute-start | bytes 417800 | tf_op jit(solution)/shard_map/ppermute | solution.py:44
  69.1 1.4 collective-permute-start.25
  75.6 3.6 %collective-permute-start.28 = (f32[8,2048]{1,0:T(8,128)S(1)}, f32[8,2048]{1,0:T(8,128)S(1)}, u32[]{:S(2)}, u32[]{:S(2)}) collective-permute-start(f32[8,2048]{1,0:T(8,128)S(1)} %get-tuple-element.64), channel_id=1, source_target_pairs={{0,16},{8,24},{16,0},{24,8},{32,48},{40,56},{48,32},{56,40},{64,80... | collective-permute-start | bytes 196616 | tf_op jit(solution)/shard_map/ppermute | solution.py:44
  75.7 4.8 %collective-permute-start.29 = (f32[8,2048]{1,0:T(8,128)S(1)}, f32[8,2048]{1,0:T(8,128)S(1)}, u32[]{:S(2)}, u32[]{:S(2)}) collective-permute-start(f32[8,2048]{1,0:T(8,128)S(1)} %get-tuple-element.65), channel_id=1, source_target_pairs={{0,48},{8,56},{16,32},{24,40},{32,16},{40,24},{48,0},{56,8},{64,11... | collective-permute-start | bytes 196616 | tf_op jit(solution)/shard_map/ppermute | solution.py:44
  77.4 4.6 %collective-permute-start.30 = (f32[8,2048]{1,0:T(8,128)S(1)}, f32[8,2048]{1,0:T(8,128)S(1)}, u32[]{:S(2)}, u32[]{:S(2)}) collective-permute-start(f32[8,2048]{1,0:T(8,128)S(1)} %get-tuple-element.66), channel_id=1, source_target_pairs={{0,32},{8,40},{16,48},{24,56},{32,0},{40,8},{48,16},{56,24},{64,96... | collective-permute-start | bytes 196616 | tf_op jit(solution)/shard_map/ppermute | solution.py:44
  82.1 3.4 %collective-permute-start.31 = (f32[8,2048]{1,0:T(8,128)S(1)}, f32[8,2048]{1,0:T(8,128)S(1)}, u32[]{:S(2)}, u32[]{:S(2)}) collective-permute-start(f32[8,2048]{1,0:T(8,128)S(1)} %add_add_fusion.refs_0_), channel_id=1, source_target_pairs={{0,64},{8,72},{16,80},{24,88},{32,96},{40,104},{48,112},{56,120},{... | collective-permute-start | bytes 196616 | tf_op jit(solution)/shard_map/ppermute | solution.py:44
  83.3 7.9 %collective-permute-start.32 = (bf16[512,1024]{1,0:T(8,128)(2,1)S(1)}, bf16[512,1024]{1,0:T(8,128)(2,1)S(1)}, u32[]{:S(2)}, u32[]{:S(2)}) collective-permute-start(bf16[512,1024]{1,0:T(8,128)(2,1)S(1)} %copy-done), channel_id=1, source_target_pairs={{0,8},{8,0},{16,24},{24,16},{32,40},{40,32},{48,56},{56,48},{64,72... | collective-permute-start | bytes 3145736 | tf_op jit(solution)/shard_map/ppermute | solution.py:44
  88.5 5.1 %collective-permute-start.33 = (bf16[512,1024]{1,0:T(8,128)(2,1)S(1)}, bf16[512,1024]{1,0:T(8,128)(2,1)S(1)}, u32[]{:S(2)}, u32[]{:S(2)}) collective-permute-start(bf16[512,1024]{1,0:T(8,128)(2,1)S(1)} %get-tuple-element.71.send), channel_id=1, source_target_pairs={{0,8},{8,0},{16,24},{24,16},{32,40},{40,32},{48,56},{56,48},{64,72... | collective-permute-start | bytes 3145736 | tf_op jit(solution)/shard_map/ppermute | solution.py:44
  94.9 17.3 %collective-permute-start.34 = (bf16[512,512]{1,0:T(8,128)(2,1)S(1)}, bf16[512,512]{1,0:T(8,128)(2,1)S(1)}, u32[]{:S(2)}, u32[]{:S(2)}) collective-permute-start(bf16[512,512]{1,0:T(8,128)(2,1)S(1)} %first_sent.1), channel_id=1, source_target_pairs={{0,68},{8,76},{16,84},{24,92},{32,100},{40,108},{48,116},{56,124},... | collective-permute-start | bytes 1572872 | tf_op jit(solution)/shard_map/ppermute | solution.py:44
  97.8 10.5 %collective-permute-start.35 = (bf16[256,512]{1,0:T(8,128)(2,1)S(1)}, bf16[256,512]{1,0:T(8,128)(2,1)S(1)}, u32[]{:S(2)}, u32[]{:S(2)}) collective-permute-start(bf16[256,512]{1,0:T(8,128)(2,1)S(1)} %get-tuple-element.74), channel_id=1, source_target_pairs={{0,1},{8,9},{16,17},{24,25},{32,33},{40,41},{48,49},{56,57},{64,65... | collective-permute-start | bytes 786440 | tf_op jit(solution)/shard_map/ppermute | solution.py:44
  97.9 10.4 %collective-permute-start.36 = (bf16[256,512]{1,0:T(8,128)(2,1)S(1)}, bf16[256,512]{1,0:T(8,128)(2,1)S(1)}, u32[]{:S(2)}, u32[]{:S(2)}) collective-permute-start(bf16[256,512]{1,0:T(8,128)(2,1)S(1)} %get-tuple-element.75), channel_id=1, source_target_pairs={{0,3},{8,11},{16,19},{24,27},{32,35},{40,43},{48,51},{56,59},{64,6... | collective-permute-start | bytes 786440 | tf_op jit(solution)/shard_map/ppermute | solution.py:44
  99.8 12.4 %collective-permute-start.37 = (bf16[256,512]{1,0:T(8,128)(2,1)S(1)}, bf16[256,512]{1,0:T(8,128)(2,1)S(1)}, u32[]{:S(2)}, u32[]{:S(2)}) collective-permute-start(bf16[256,512]{1,0:T(8,128)(2,1)S(1)} %get-tuple-element.76), channel_id=1, source_target_pairs={{0,2},{8,10},{16,18},{24,26},{32,34},{40,42},{48,50},{56,58},{64,6... | collective-permute-start | bytes 786440 | tf_op jit(solution)/shard_map/ppermute | solution.py:44
  112.4 5.9 %collective-permute-start.44 = (bf16[128,512]{1,0:T(8,128)(2,1)S(1)}, bf16[128,512]{1,0:T(8,128)(2,1)S(1)}, u32[]{:S(2)}, u32[]{:S(2)}) collective-permute-start(bf16[128,512]{1,0:T(8,128)(2,1)S(1)} %slice.53), channel_id=1, source_target_pairs={{0,68},{8,76},{16,84},{24,92},{32,100},{40,108},{48,116},{56,124},... | collective-permute-start | bytes 393224 | tf_op jit(solution)/shard_map/ppermute | solution.py:44
  114.1 5.1 %collective-permute-start.38 = (bf16[128,512]{1,0:T(8,128)(2,1)S(1)}, bf16[128,512]{1,0:T(8,128)(2,1)S(1)}, u32[]{:S(2)}, u32[]{:S(2)}) collective-permute-start(bf16[128,512]{1,0:T(8,128)(2,1)S(1)} %get-tuple-element.92), channel_id=1, source_target_pairs={{0,1},{8,9},{16,17},{24,25},{32,33},{40,41},{48,49},{56,57},{64,65... | collective-permute-start | bytes 393224 | tf_op jit(solution)/shard_map/ppermute | solution.py:44
  114.4 5.9 %collective-permute-start.40 = (bf16[128,512]{1,0:T(8,128)(2,1)S(1)}, bf16[128,512]{1,0:T(8,128)(2,1)S(1)}, u32[]{:S(2)}, u32[]{:S(2)}) collective-permute-start(bf16[128,512]{1,0:T(8,128)(2,1)S(1)} %get-tuple-element.93), channel_id=1, source_target_pairs={{0,2},{8,10},{16,18},{24,26},{32,34},{40,42},{48,50},{56,58},{64,6... | collective-permute-start | bytes 393224 | tf_op jit(solution)/shard_map/ppermute | solution.py:44
  116.5 5.2 %collective-permute-start.39 = (bf16[128,512]{1,0:T(8,128)(2,1)S(1)}, bf16[128,512]{1,0:T(8,128)(2,1)S(1)}, u32[]{:S(2)}, u32[]{:S(2)}) collective-permute-start(bf16[128,512]{1,0:T(8,128)(2,1)S(1)} %get-tuple-element.94), channel_id=1, source_target_pairs={{0,3},{8,11},{16,19},{24,27},{32,35},{40,43},{48,51},{56,59},{64,6... | collective-permute-start | bytes 393224 | tf_op jit(solution)/shard_map/ppermute | solution.py:44
  118.3 4.2 %collective-permute-start.45 = (bf16[128,512]{1,0:T(8,128)(2,1)S(1)}, bf16[128,512]{1,0:T(8,128)(2,1)S(1)}, u32[]{:S(2)}, u32[]{:S(2)}) collective-permute-start(bf16[128,512]{1,0:T(8,128)(2,1)S(1)} %fusion.8), channel_id=1, source_target_pairs={{0,16},{8,24},{16,0},{24,8},{32,48},{40,56},{48,32},{56,40},{64,80... | collective-permute-start | bytes 393224 | tf_op jit(solution)/shard_map/ppermute | solution.py:44
  121.8 3.9 %collective-permute-start.41 = (bf16[128,512]{1,0:T(8,128)(2,1)S(1)}, bf16[128,512]{1,0:T(8,128)(2,1)S(1)}, u32[]{:S(2)}, u32[]{:S(2)}) collective-permute-start(bf16[128,512]{1,0:T(8,128)(2,1)S(1)} %get-tuple-element.88), channel_id=1, source_target_pairs={{0,64},{8,72},{16,80},{24,88},{32,96},{40,104},{48,112},{56,120},{... | collective-permute-start | bytes 393224 | tf_op jit(solution)/shard_map/ppermute | solution.py:44
  122.6 5.1 %collective-permute-start.46 = (bf16[128,512]{1,0:T(8,128)(2,1)S(1)}, bf16[128,512]{1,0:T(8,128)(2,1)S(1)}, u32[]{:S(2)}, u32[]{:S(2)}) collective-permute-start(bf16[128,512]{1,0:T(8,128)(2,1)S(1)} %fusion.5), channel_id=1, source_target_pairs={{0,48},{8,56},{16,32},{24,40},{32,16},{40,24},{48,0},{56,8},{64,11... | collective-permute-start | bytes 393224 | tf_op jit(solution)/shard_map/ppermute | solution.py:44
  125.7 4.2 %collective-permute-start.42 = (bf16[128,512]{1,0:T(8,128)(2,1)S(1)}, bf16[128,512]{1,0:T(8,128)(2,1)S(1)}, u32[]{:S(2)}, u32[]{:S(2)}) collective-permute-start(bf16[128,512]{1,0:T(8,128)(2,1)S(1)} %fusion.4), channel_id=1, source_target_pairs={{0,16},{8,24},{16,0},{24,8},{32,48},{40,56},{48,32},{56,40},{64,80... | collective-permute-start | bytes 393224 | tf_op jit(solution)/shard_map/ppermute | solution.py:44
  127.7 4.2 %collective-permute-start.47 = (bf16[128,512]{1,0:T(8,128)(2,1)S(1)}, bf16[128,512]{1,0:T(8,128)(2,1)S(1)}, u32[]{:S(2)}, u32[]{:S(2)}) collective-permute-start(bf16[128,512]{1,0:T(8,128)(2,1)S(1)} %fusion.7), channel_id=1, source_target_pairs={{0,64},{8,72},{16,80},{24,88},{32,96},{40,104},{48,112},{56,120},{... | collective-permute-start | bytes 393224 | tf_op jit(solution)/shard_map/ppermute | solution.py:44
  129.9 5.1 %collective-permute-start.43 = (bf16[128,512]{1,0:T(8,128)(2,1)S(1)}, bf16[128,512]{1,0:T(8,128)(2,1)S(1)}, u32[]{:S(2)}, u32[]{:S(2)}) collective-permute-start(bf16[128,512]{1,0:T(8,128)(2,1)S(1)} %fusion.6), channel_id=1, source_target_pairs={{0,48},{8,56},{16,32},{24,40},{32,16},{40,24},{48,0},{56,8},{64,11... | collective-permute-start | bytes 393224 | tf_op jit(solution)/shard_map/ppermute | solution.py:44
  135.2 8.6 %collective-permute-start.48 = (bf16[128,1024]{1,0:T(8,128)(2,1)S(1)}, bf16[128,1024]{1,0:T(8,128)(2,1)S(1)}, u32[]{:S(2)}, u32[]{:S(2)}) collective-permute-start(bf16[128,1024]{1,0:T(8,128)(2,1)S(1)} %pad_maximum_fusion.3), channel_id=1, source_target_pairs={{0,8},{8,0},{16,24},{24,16},{32,40},{40,32},{48,56},{56,48},{64,72... | collective-permute-start | bytes 786440 | tf_op jit(solution)/shard_map/ppermute | solution.py:44

commit v9 on v8

--- a/solution.py
+++ b/solution.py
@@ -136,7 +136,7 @@
 
 
 def forward_kernel(items, ints, context, residual, gain, *refs):
-    stream, inverse, pooled, embedding, added_rows, sem = refs[12:]
+    stream, inverse, pooled, embedding = refs[12:]
     where = [ints[i] for i in range(4)]
     lengths, ids, counts = ([ints[4 + j * items + i] for i in range(items)] for j in range(3))
     positive = [ints[i] for i in range(4 + 3 * items, ints.shape[0])]
@@ -144,8 +144,6 @@
     half = width // 2
     block = context.shape[1] // 8
     length = tokens // items
-    copy = pltpu.make_async_copy(residual, added_rows, sem)
-    copy.start()
     for p, (start, columns, orders) in enumerate(parts_of(half)):
         lanes = [blocks_of(context, where, order, block) for order in orders]
         for side in range(2):
@@ -153,10 +151,9 @@
             stream[:, pl.ds(pl.multiple_of(base + start, 128), columns)] = sum(
                 dot(lanes[k], weight_rows(refs[side * 6 + p * 2 + k], block)) for k in range(2)
             )
-    copy.wait()
     for i in range(items):
         span = slice(i * length, (i + 1) * length)
-        rows = stream[span, :] + added_rows[span, :].astype(F32)
+        rows = stream[span, :] + residual[span, :].astype(F32)
         stream[span, :] = rows
         inv = lax.rsqrt(jnp.mean(rows * rows, axis=-1, keepdims=True) + EPSILON)
         inverse[i * length : (i + 1) * length, :] = inv
@@ -188,14 +185,16 @@
     return jnp.where(to == home(of), 1.0, 0.0).astype(BF16)
 
 
-def loss_kernel(users_here, items_here, block, where, gain, *refs):
-    piece_refs, emb_refs = refs[:4], refs[4:12]
-    sums, user_grad, grads, emb_grads, riders, sems = refs[12:16], *refs[16:]
-    x, y, z, core = where[0], where[1], where[2], where[3]
-    group, full = emb_refs[0].shape
-    width = full - LABELS
-    items = 8 * group
-    people = 16 * users_here
+def hold_kernel(source, out, sem):
+    copy = pltpu.make_async_copy(source, out, sem)
+    copy.start()
+    copy.wait()
+
+
+def users_kernel(users_here, block, where, *refs):
+    piece_refs, (out, riders, sems) = refs[:4], refs[4:]
+    x, y, core = where[0], where[1], where[3]
+    people, width = out.shape
     stride, part = piece_refs[0].shape[0] // 4, piece_refs[0].shape[1]
     parts = width // part
     rode = parts * users_here
@@ -211,20 +210,9 @@
             )
     for copy in copies:
         copy.start()
-
-    def item_home(s):
-        one = s // items_here
-        ax = x ^ bit(one, 0) ^ (3 * bit(one, 1))
-        ay = y ^ bit(one, 2) ^ (3 * bit(one, 3))
-        az = z ^ bit(one, 4) ^ (3 * bit(one, 5))
-        ac = core ^ bit(one, 6)
-        return (((ac * 4 + az) * 4 + ay) * 4 + ax) * items_here + s % items_here
-
-    placed = jnp.concatenate([ref[...] for ref in emb_refs], axis=0)
-    turned = dot(one_hot_turn(items, item_home), placed).astype(BF16)
-    emb, labels = turned[:, :width], turned[:, width:]
     for copy in copies:
         copy.wait()
+
     def user_home(s):
         one = s // users_here
         ac, ay = core ^ bit(one, 3), (y // 2) ^ bit(one, 1)
@@ -245,7 +233,29 @@
         ],
         axis=1,
     ).astype(BF16)
-    users = dot(one_hot_turn(people, user_home), placed).astype(BF16)
+    out[...] = dot(one_hot_turn(people, user_home), placed).astype(BF16)
+
+def loss_kernel(users_here, items_here, where, gain, users_ref, *refs):
+    emb_refs = refs[:8]
+    sums, user_grad, grads, emb_grads = refs[8:12], *refs[12:]
+    x, y, z, core = where[0], where[1], where[2], where[3]
+    group, full = emb_refs[0].shape
+    width = full - LABELS
+    items = 8 * group
+    people = users_ref.shape[0]
+
+    def item_home(s):
+        one = s // items_here
+        ax = x ^ bit(one, 0) ^ (3 * bit(one, 1))
+        ay = y ^ bit(one, 2) ^ (3 * bit(one, 3))
+        az = z ^ bit(one, 4) ^ (3 * bit(one, 5))
+        ac = core ^ bit(one, 6)
+        return (((ac * 4 + az) * 4 + ay) * 4 + ax) * items_here + s % items_here
+
+    placed = jnp.concatenate([ref[...] for ref in emb_refs], axis=0)
+    turned = dot(one_hot_turn(items, item_home), placed).astype(BF16)
+    emb, labels = turned[:, :width], turned[:, width:]
+    users = users_ref[...]
     person = lax.broadcasted_iota(jnp.int32, (people, items), 0)
     at = lax.broadcasted_iota(jnp.int32, (people, items), 1)
     g = person // users_here
@@ -425,7 +435,16 @@
         travel = [jnp.concatenate([v, swap(v, n)], axis=0) for v, (swap, n) in zip(travel, turns)]
         travel = lax.optimization_barrier(travel)
     arrived = [swap_x(travel[0], 3), swap_y(travel[1], 3), swap_x(travel[2], 1)]
-    arrived = lax.optimization_barrier(arrived)
+    held = pl.pallas_call(
+        hold_kernel,
+        out_shape=shaped((tokens, width), BF16),
+        in_specs=[HBM],
+        out_specs=VMEM,
+        scratch_shapes=[pltpu.SemaphoreType.DMA],
+        compiler_params=params(6),
+        name="hold",
+    )(residual)
+    arrived, held = lax.optimization_barrier((arrived, held))
     pieces = [piece for both in zip(travel, arrived) for piece in both]
     pieces = pieces + [swap_core(p) for p in pieces]
     ints, filled = 0, 0
@@ -443,35 +462,44 @@
             shaped((items_here, width)),
             shaped((items_here, width + LABELS), BF16),
         ),
-        in_specs=[SMEM, VMEM, HBM] + [VMEM] * 13,
+        in_specs=[SMEM] + [VMEM] * 15,
         out_specs=(VMEM,) * 4,
-        scratch_shapes=[pltpu.VMEM((tokens, width), BF16), pltpu.SemaphoreType.DMA],
         compiler_params=params(16),
         name="forward",
-    )(ints, context, residual, gain, *pieces)
+    )(ints, context, held, gain, *pieces)
 
     emb = lax.optimization_barrier(jnp.concatenate(four(emb, swap_x), axis=0))
     peer_context = swap_core(after(context, emb))
-    emb = lax.optimization_barrier(jnp.concatenate(four(emb, swap_y), axis=0))
+    riding = pieces[4:6] + pieces[10:12]
+    users = pl.pallas_call(
+        functools.partial(users_kernel, users_here, rows),
+        out_shape=shaped((16 * users_here, width), BF16),
+        in_specs=[SMEM] + [ANY] * 4,
+        out_specs=VMEM,
+        scratch_shapes=[
+            pltpu.VMEM((16 * rode, columns[2]), BF16),
+            pltpu.SemaphoreType.DMA((16,)),
+        ],
+        compiler_params=params(10),
+        name="users",
+    )(where, *riding)
+    emb, users = lax.optimization_barrier((jnp.concatenate(four(emb, swap_y), axis=0), users))
     emb_pieces = four(emb, swap_z)
     emb_pieces = emb_pieces + [swap_core(p) for p in emb_pieces]
 
     items, people = 128 * items_here, 16 * users_here
-    riding = pieces[4:6] + pieces[10:12]
     *sums, user_grad = pl.pallas_call(
-        functools.partial(loss_kernel, users_here, items_here, rows),
+        functools.partial(loss_kernel, users_here, items_here),
         out_shape=(shaped((8, width)),) * 4 + (shaped((users_here, width), BF16),),
-        in_specs=[SMEM, VMEM] + [ANY] * 4 + [VMEM] * 8,
+        in_specs=[SMEM] + [VMEM] * 10,
         out_specs=(VMEM,) * 5,
         scratch_shapes=[
             pltpu.VMEM((people, items), F32),
             pltpu.VMEM((items, width), F32),
-            pltpu.VMEM((16 * rode, columns[2]), BF16),
-            pltpu.SemaphoreType.DMA((16,)),
         ],
         compiler_params=params(18),
         name="loss",
-    )(where, gain, *riding, *emb_pieces)
+    )(where, gain, users, *emb_pieces)
     sums = [sums[0]] + [swap_z(sums[q], OFFSETS[q]) for q in (1, 2, 3)]
     sums = (sums[0] + sums[1]) + (sums[2] + sums[3])
 

time: 145 us -> 144 us (level)
  waiting for transfers between devices: 40.5 us -> 36.1 us
  Pallas kernels: 24.1 us -> 25.7 us
    ppermute x49, waiting for transfers between devices: 40.5 us -> 36.1 us  [move(): return lax.ppermute(value, AXES, perm)]
    pallas_call x1 -> x3, Pallas kernels: 5.06 us -> 6.16 us  [the longest x1 3.94 us: on_device(): pl.pallas_call(functools.partial(loss_kernel, users_here, items_here), ou...]
    unnamed x22 -> x26, local copies, waits for them, and re-layouts: 5.23 us -> 4.72 us
  transfers between devices with their start and end apart: 49 -> 49, of which waited for: 30 -> 26; matrix products, arithmetic and copies ran while one was open for 1% -> 2% of each run, Pallas kernels for 8% -> 10%
where the time goes in v9:
time: 144 us; the launch traced here: 143 us
  starting transfers between devices  72 us (50%)
  waiting for transfers between devices  36.1 us (25%)
  Pallas kernels  25.7 us (18%)
  local copies, waits for them, and re-layouts  4.77 us (3%)
  other arithmetic  3.59 us (2%)
    ppermute x49, starting transfers between devices, move(): return lax.ppermute(value, AXES, perm)  72 us
    ppermute x49, waiting for transfers between devices, move(): return lax.ppermute(value, AXES, perm)  36.1 us
    pallas_call x1, Pallas kernels, on_device(): pl.pallas_call(context_kernel, out_shape=shaped((tokens, head), BF16), in...  6.03 us
    pallas_call x1, Pallas kernels, on_device(): pl.pallas_call(functools.partial(forward_kernel, items_here), out_shape=(...  5.95 us
    unnamed x26, local copies, waits for them, and re-layouts  4.72 us
    pallas_call x3, Pallas kernels, blocks(): pl.pallas_call(functools.partial(blocks_kernel, first_blocks, second_bloc...  4.48 us
    pallas_call x1, Pallas kernels, on_device(): pl.pallas_call(functools.partial(loss_kernel, users_here, items_here), ou...  3.94 us
    pallas_call x1, Pallas kernels, on_device(): pl.pallas_call(functools.partial(residual_kernel, 8 * people), out_shape=...  2.95 us
  transfers between devices with their start and end apart: 49, of which 26 were waited for; matrix products, arithmetic and copies ran while one was open for 2% of the time, Pallas kernels for 10%

profile of v9, /device:TPU:1, one launch (start us, length us, event | category | flops | bytes accessed | tf_op | source)
XLA Modules:
  0.0 143.1 jit_solution(6302451302248075627)
XLA Ops:
  0.7 1.2 copy-done.8
  2.7 3.6 %collective-permute-start = (bf16[128,384]{1,0:T(8,128)(2,1)S(1)}, bf16[128,384]{1,0:T(8,128)(2,1)S(1)}, u32[]{:S(2)}, u32[]{:S(2)}) collective-permute-start(bf16[128,384]{1,0:T(8,128)(2,1)S(1)} %get-tuple-element.50), channel_id=1, source_target_pairs={{0,68},{8,76},{16,84},{24,92},{32,100},{40,108},{48,116},{56,124},... | collective-permute-start | bytes 294920 | tf_op jit(solution)/shard_map/ppermute | solution.py:44
  6.3 1.2 collective-permute-start.1
  7.5 1.8 %collective-permute-start.2 = (bf16[192,256]{1,0:T(8,128)(2,1)S(1)}, bf16[192,256]{1,0:T(8,128)(2,1)S(1)}, u32[]{:S(2)}, u32[]{:S(2)}) collective-permute-start(bf16[192,256]{1,0:T(8,128)(2,1)S(1)} %get-tuple-element.52), channel_id=1, source_target_pairs={{0,3},{8,11},{16,19},{24,27},{32,35},{40,43},{48,51},{56,59},{64,6... | collective-permute-start | bytes 294920 | tf_op jit(solution)/shard_map/ppermute | solution.py:44
  9.8 2.4 %collective-permute-done.2 = bf16[192,256]{1,0:T(8,128)(2,1)S(1)} collective-permute-done((bf16[192,256]{1,0:T(8,128)(2,1)S(1)}, bf16[192,256]{1,0:T(8,128)(2,1)S(1)}, u32[]{:S(2)}, u32[]{:S(2)}) %collective-permute-start.2) | collective-permute-done | bytes 98336 | tf_op jit(solution)/shard_map/ppermute | solution.py:44
  12.3 1.9 %collective-permute-start.4 = (bf16[256,384]{1,0:T(8,128)(2,1)S(1)}, bf16[256,384]{1,0:T(8,128)(2,1)S(1)}, u32[]{:S(2)}, u32[]{:S(2)}) collective-permute-start(bf16[256,384]{1,0:T(8,128)(2,1)S(1)} %pad_maximum_fusion.5), channel_id=1, source_target_pairs={{0,3},{8,11},{16,19},{24,27},{32,35},{40,43},{48,51},{56,59},{64,6... | collective-permute-start | bytes 589832 | tf_op jit(solution)/shard_map/ppermute | solution.py:44
  14.6 2.2 %collective-permute-done.3 = bf16[256,384]{1,0:T(8,128)(2,1)S(1)} collective-permute-done((bf16[256,384]{1,0:T(8,128)(2,1)S(1)}, bf16[256,384]{1,0:T(8,128)(2,1)S(1)}, u32[]{:S(2)}, u32[]{:S(2)}) %collective-permute-start.3) | collective-permute-done | bytes 196640 | tf_op jit(solution)/shard_map/ppermute | solution.py:44
  16.9 1.2 collective-permute-done.4
  18.9 1.3 collective-permute-done.5
  20.3 0.9 collective-permute-start.6
  21.5 4.5 %collective-permute-start.9 = (bf16[512,384]{1,0:T(8,128)(2,1)S(1)}, bf16[512,384]{1,0:T(8,128)(2,1)S(1)}, u32[]{:S(2)}, u32[]{:S(2)}) collective-permute-start(bf16[512,384]{1,0:T(8,128)(2,1)S(1)} %pad_maximum_fusion.refs_0_), channel_id=1, source_target_pairs={{0,8},{8,0},{16,24},{24,16},{32,40},{40,32},{48,56},{56,48},{64,72... | collective-permute-start | bytes 1179656 | tf_op jit(solution)/shard_map/ppermute | solution.py:44
  26.3 2.5 %collective-permute-done.6.refs_1_ = bf16[512,384]{1,0:T(8,128)(2,1)} collective-permute-done((bf16[512,384]{1,0:T(8,128)(2,1)S(1)}, bf16[512,384]{1,0:T(8,128)(2,1)}, u32[]{:S(2)}, u32[]{:S(2)}) %collective-permute-start.6) | collective-permute-done | bytes 393248 | tf_op jit(solution)/shard_map/ppermute | solution.py:44
  28.8 4.4 %collective-permute-start.13 = (bf16[768,256]{1,0:T(8,128)(2,1)S(1)}, bf16[768,256]{1,0:T(8,128)(2,1)}, u32[]{:S(2)}, u32[]{:S(2)}) collective-permute-start(bf16[768,256]{1,0:T(8,128)(2,1)S(1)} %pad_maximum_fusion.2.refs_4_.refs_0_), channel_id=1, source_target_pairs={{0,8},{8,0},{16,24},{24,16},{32,40},{40,32},{48,56},{56,48},{64,72... | collective-permute-start | bytes 1179656 | tf_op jit(solution)/shard_map/ppermute | solution.py:44
  33.3 1.1 collective-permute-start.10
  37.3 1.0 copy-done.2
  38.3 1.0 copy-done.6
  39.3 5.9 %forward.1 = (f32[512,2048]{1,0:T(8,128)S(1)}, f32[512,1]{1,0:T(8,128)S(1)}, f32[2,2048]{1,0:T(2,128)S(1)}, bf16[2,2176]{1,0:T(2,128)(2,1)S(1)}) custom-call(s32[18]{0:T(128)S(1)} %pad_add_fusion.1.ints, bf16[512,1024]{1,0:T(8,128)(2,1)S(1)} %copy-done, bf16[512,2048]{1,0:T(8,128)(2,1)S(1)} %hold.1.residual, f32[1,2048]{1,0:T(1,128)S(1)} %bitcast.7, ...), custom_call_target="tpu_custom_call" | custom-call | tf_op jit(solution)/shard_map/forward/pallas_call | solution.py:457
  45.3 2.1 %collective-permute-start.17 = (bf16[2,2176]{1,0:T(2,128)(2,1)S(1)}, bf16[2,2176]{1,0:T(2,128)(2,1)S(1)}, u32[]{:S(2)}, u32[]{:S(2)}) collective-permute-start(bf16[2,2176]{1,0:T(2,128)(2,1)S(1)} %get-tuple-element.66), channel_id=1, source_target_pairs={{0,2},{8,10},{16,18},{24,26},{32,34},{40,42},{48,50},{56,58},{64,6... | collective-permute-start | bytes 26120 | tf_op jit(solution)/shard_map/ppermute | solution.py:44
  47.4 0.9 collective-permute-start.16
  48.2 1.2 collective-permute-done.17
  49.4 1.7 %collective-permute-done.16 = bf16[2,2176]{1,0:T(2,128)(2,1)S(1)} collective-permute-done((bf16[2,2176]{1,0:T(2,128)(2,1)S(1)}, bf16[2,2176]{1,0:T(2,128)(2,1)S(1)}, u32[]{:S(2)}, u32[]{:S(2)}) %collective-permute-start.16) | collective-permute-done | bytes 8736 | tf_op jit(solution)/shard_map/ppermute | solution.py:44
  51.2 1.6 %collective-permute-start.19 = (bf16[8,2176]{1,0:T(8,128)(2,1)S(1)}, bf16[8,2176]{1,0:T(8,128)(2,1)S(1)}, u32[]{:S(2)}, u32[]{:S(2)}) collective-permute-start(bf16[8,2176]{1,0:T(8,128)(2,1)S(1)} %pad_maximum_fusion.8), channel_id=1, source_target_pairs={{0,68},{8,76},{16,84},{24,92},{32,100},{40,108},{48,116},{56,124},... | collective-permute-start | bytes 104456 | tf_op jit(solution)/shard_map/ppermute | solution.py:44
  52.8 1.0 collective-permute-start.18
  53.9 2.1 %users.3.users_ref = bf16[128,2048]{1,0:T(8,128)(2,1)S(1)} custom-call(s32[4]{0:T(128)S(1)} %pad_add_fusion.where, bf16[768,256]{1,0:T(8,128)(2,1)S(1)} %pad_maximum_fusion.2.refs_4_.refs_0_, bf16[768,256]{1,0:T(8,128)(2,1)} %collective-permute-done.8.refs_5_.refs_1_, bf16[768,256]{1,0:T(8,128)(2,1)} %collective-permute-done.13.refs_10_.refs_2_, ...), custom_call_target="tpu_custom_call" | custom-call | tf_op jit(solution)/shard_map/users/pallas_call | solution.py:474
  56.0 3.7 %collective-permute-start.23 = (bf16[32,2176]{1,0:T(8,128)(2,1)S(1)}, bf16[32,2176]{1,0:T(8,128)(2,1)S(1)}, u32[]{:S(2)}, u32[]{:S(2)}) collective-permute-start(bf16[32,2176]{1,0:T(8,128)(2,1)S(1)} %pad_maximum_fusion.7.refs_0_), channel_id=1, source_target_pairs={{0,32},{8,40},{16,48},{24,56},{32,0},{40,8},{48,16},{56,24},{64,96... | collective-permute-start | bytes 417800 | tf_op jit(solution)/shard_map/ppermute | solution.py:44
  60.4 3.4 %collective-permute-start.24 = (bf16[32,2176]{1,0:T(8,128)(2,1)S(1)}, bf16[32,2176]{1,0:T(8,128)(2,1)S(1)}, u32[]{:S(2)}, u32[]{:S(2)}) collective-permute-start(bf16[32,2176]{1,0:T(8,128)(2,1)S(1)} %pad_maximum_fusion.7.refs_0_), channel_id=1, source_target_pairs={{0,8},{8,0},{16,24},{24,16},{32,40},{40,32},{48,56},{56,48},{64,72... | collective-permute-start | bytes 417800 | tf_op jit(solution)/shard_map/ppermute | solution.py:44
  63.8 2.7 %collective-permute-start.27 = (bf16[32,2176]{1,0:T(8,128)(2,1)S(1)}, bf16[32,2176]{1,0:T(8,128)(2,1)S(1)}, u32[]{:S(2)}, u32[]{:S(2)}) collective-permute-start(bf16[32,2176]{1,0:T(8,128)(2,1)S(1)} %collective-permute-done.23.refs_3_), channel_id=1, source_target_pairs={{0,8},{8,0},{16,24},{24,16},{32,40},{40,32},{48,56},{56,48},{64,72... | collective-permute-start | bytes 417800 | tf_op jit(solution)/shard_map/ppermute | solution.py:44
  66.6 2.5 %collective-permute-start.26 = (bf16[32,2176]{1,0:T(8,128)(2,1)S(1)}, bf16[32,2176]{1,0:T(8,128)(2,1)S(1)}, u32[]{:S(2)}, u32[]{:S(2)}) collective-permute-start(bf16[32,2176]{1,0:T(8,128)(2,1)S(1)} %collective-permute-done.22.refs_2_), channel_id=1, source_target_pairs={{0,8},{8,0},{16,24},{24,16},{32,40},{40,32},{48,56},{56,48},{64,72... | collective-permute-start | bytes 417800 | tf_op jit(solution)/shard_map/ppermute | solution.py:44
  69.1 1.0 collective-permute-done.26.refs_6_
  70.5 3.9 %loss.1 = (f32[8,2048]{1,0:T(8,128)S(1)}, f32[8,2048]{1,0:T(8,128)S(1)}, f32[8,2048]{1,0:T(8,128)S(1)}, f32[8,2048]{1,0:T(8,128)S(1)}, bf16[8,2048]{1,0:T(8,128)(2,1)}) custom-call(s32[4]{0:T(128)S(1)} %pad_add_fusion.where, f32[1,2048]{1,0:T(1,128)S(1)} %bitcast.8, bf16[128,2048]{1,0:T(8,128)(2,1)S(1)} %users.3.users_ref, ...), custom_call_target="tpu_custom_call" | custom-call | tf_op jit(solution)/shard_map/loss/pallas_call | solution.py:491
  74.5 1.6 %collective-permute-start.29 = (f32[8,2048]{1,0:T(8,128)S(1)}, f32[8,2048]{1,0:T(8,128)S(1)}, u32[]{:S(2)}, u32[]{:S(2)}) collective-permute-start(f32[8,2048]{1,0:T(8,128)S(1)} %get-tuple-element.71), channel_id=1, source_target_pairs={{0,48},{8,56},{16,32},{24,40},{32,16},{40,24},{48,0},{56,8},{64,11... | collective-permute-start | bytes 196616 | tf_op jit(solution)/shard_map/ppermute | solution.py:44
  76.1 1.6 %collective-permute-start.30 = (f32[8,2048]{1,0:T(8,128)S(1)}, f32[8,2048]{1,0:T(8,128)S(1)}, u32[]{:S(2)}, u32[]{:S(2)}) collective-permute-start(f32[8,2048]{1,0:T(8,128)S(1)} %get-tuple-element.72), channel_id=1, source_target_pairs={{0,32},{8,40},{16,48},{24,56},{32,0},{40,8},{48,16},{56,24},{64,96... | collective-permute-start | bytes 196616 | tf_op jit(solution)/shard_map/ppermute | solution.py:44
  77.9 0.9 collective-permute-done.29
  78.8 1.9 %collective-permute-done.30 = f32[8,2048]{1,0:T(8,128)S(1)} collective-permute-done((f32[8,2048]{1,0:T(8,128)S(1)}, f32[8,2048]{1,0:T(8,128)S(1)}, u32[]{:S(2)}, u32[]{:S(2)}) %collective-permute-start.30) | collective-permute-done | bytes 65568 | tf_op jit(solution)/shard_map/ppermute | solution.py:44
  80.7 1.4 collective-permute-start.31
  82.1 2.2 %collective-permute-start.32 = (bf16[512,1024]{1,0:T(8,128)(2,1)S(1)}, bf16[512,1024]{1,0:T(8,128)(2,1)S(1)}, u32[]{:S(2)}, u32[]{:S(2)}) collective-permute-start(bf16[512,1024]{1,0:T(8,128)(2,1)S(1)} %copy-done), channel_id=1, source_target_pairs={{0,8},{8,0},{16,24},{24,16},{32,40},{40,32},{48,56},{56,48},{64,72... | collective-permute-start | bytes 3145736 | tf_op jit(solution)/shard_map/ppermute | solution.py:44
  84.3 2.9 %residual.1 = (bf16[512,2048]{1,0:T(8,128)(2,1)}, bf16[512,1024]{1,0:T(8,128)(2,1)S(1)}, bf16[512,1024]{1,0:T(8,128)(2,1)S(1)}, f32[1,2048]{1,0:T(1,128)}, f32[1,1]{1,0:T(1,128)}) custom-call(s32[4]{0:T(128)S(1)} %pad_add_fusion.where, s32[2]{0:T(128)S(1)} %copy-done.11, f32[512,2048]{1,0:T(8,128)S(1)} %get-tuple-element.63.stream, ...), custom_call_target="tpu_custom_call" | custom-call | tf_op jit(solution)/shard_map/residual/pallas_call | solution.py:506
  87.2 2.7 %collective-permute-start.33 = (bf16[512,1024]{1,0:T(8,128)(2,1)S(1)}, bf16[512,1024]{1,0:T(8,128)(2,1)S(1)}, u32[]{:S(2)}, u32[]{:S(2)}) collective-permute-start(bf16[512,1024]{1,0:T(8,128)(2,1)S(1)} %get-tuple-element.77.send), channel_id=1, source_target_pairs={{0,8},{8,0},{16,24},{24,16},{32,40},{40,32},{48,56},{56,48},{64,72... | collective-permute-start | bytes 3145736 | tf_op jit(solution)/shard_map/ppermute | solution.py:44
  89.9 2.3 %collective-permute-done.33.peer_grad = bf16[512,1024]{1,0:T(8,128)(2,1)S(1)} collective-permute-done((bf16[512,1024]{1,0:T(8,128)(2,1)S(1)}, bf16[512,1024]{1,0:T(8,128)(2,1)S(1)}, u32[]{:S(2)}, u32[]{:S(2)}) %collective-permute-start.33) | collective-permute-done | bytes 1048608 | tf_op jit(solution)/shard_map/ppermute | solution.py:44
  92.2 1.3 first_sent.1
  93.5 1.4 collective-permute-start.34
  94.9 1.6 %second_sent.1 = (bf16[256,512]{1,0:T(8,128)(2,1)S(1)}, bf16[256,512]{1,0:T(8,128)(2,1)S(1)}, bf16[256,512]{1,0:T(8,128)(2,1)S(1)}) custom-call(s32[4]{0:T(128)S(1)} %pad_add_fusion.where, bf16[512,1024]{1,0:T(8,128)(2,1)S(1)} %copy-done, bf16[512,1024]{1,0:T(8,128)(2,1)S(1)} %collective-permute-done.32.peer_context, ...), custom_call_target="tpu_custom_call" | custom-call | tf_op jit(solution)/shard_map/second_sent/pallas_call | solution.py:531
  96.6 1.8 %collective-permute-start.36 = (bf16[256,512]{1,0:T(8,128)(2,1)S(1)}, bf16[256,512]{1,0:T(8,128)(2,1)S(1)}, u32[]{:S(2)}, u32[]{:S(2)}) collective-permute-start(bf16[256,512]{1,0:T(8,128)(2,1)S(1)} %get-tuple-element.81), channel_id=1, source_target_pairs={{0,3},{8,11},{16,19},{24,27},{32,35},{40,43},{48,51},{56,59},{64,6... | collective-permute-start | bytes 786440 | tf_op jit(solution)/shard_map/ppermute | solution.py:44
  98.4 1.4 %collective-permute-start.37 = (bf16[256,512]{1,0:T(8,128)(2,1)S(1)}, bf16[256,512]{1,0:T(8,128)(2,1)S(1)}, u32[]{:S(2)}, u32[]{:S(2)}) collective-permute-start(bf16[256,512]{1,0:T(8,128)(2,1)S(1)} %get-tuple-element.82), channel_id=1, source_target_pairs={{0,2},{8,10},{16,18},{24,26},{32,34},{40,42},{48,50},{56,58},{64,6... | collective-permute-start | bytes 786440 | tf_op jit(solution)/shard_map/ppermute | solution.py:44
  99.9 6.0 %context.3 = bf16[512,1024]{1,0:T(8,128)(2,1)} custom-call(s32[4]{0:T(128)S(1)} %pad_add_fusion.where, bf16[512,1024]{1,0:T(8,128)(2,1)S(1)} %get-tuple-element.76.own_grad.keep, bf16[512,1024]{1,0:T(8,128)(2,1)S(1)} %get-tuple-element.77.send, bf16[512,384]{1,0:T(8,128)(2,1)S(1)} %copy-done.3, bf16[512,384]{1,0:T(8,128)(2,1)} %collective-permute-done.6.refs_1_, ...), custom_call_target="tpu_custom_call" | custom-call | tf_op jit(solution)/shard_map/context/pallas_call | solution.py:521
  105.9 1.6 %kept.1 = (f32[512,512]{1,0:T(8,128)S(1)}, f32[256,512]{1,0:T(8,128)S(1)}) custom-call(s32[4]{0:T(128)S(1)} %pad_add_fusion.where, bf16[512,1024]{1,0:T(8,128)(2,1)S(1)} %copy-done, bf16[512,1024]{1,0:T(8,128)(2,1)S(1)} %collective-permute-done.32.peer_context, bf16[512,1024]{1,0:T(8,128)(2,1)S(1)} %get-tuple-element.76.own_grad.keep, ...), custom_call_target="tpu_custom_call" | custom-call | tf_op jit(solution)/shard_map/kept/pallas_call | solution.py:531
  107.5 3.3 %collective-permute-done.37 = bf16[256,512]{1,0:T(8,128)(2,1)S(1)} collective-permute-done((bf16[256,512]{1,0:T(8,128)(2,1)S(1)}, bf16[256,512]{1,0:T(8,128)(2,1)S(1)}, u32[]{:S(2)}, u32[]{:S(2)}) %collective-permute-start.37) | collective-permute-done | bytes 262176 | tf_op jit(solution)/shard_map/ppermute | solution.py:44
  111.0 1.4 collective-permute-start.44
  112.8 2.2 %collective-permute-start.40 = (bf16[128,512]{1,0:T(8,128)(2,1)S(1)}, bf16[128,512]{1,0:T(8,128)(2,1)S(1)}, u32[]{:S(2)}, u32[]{:S(2)}) collective-permute-start(bf16[128,512]{1,0:T(8,128)(2,1)S(1)} %get-tuple-element.99), channel_id=1, source_target_pairs={{0,2},{8,10},{16,18},{24,26},{32,34},{40,42},{48,50},{56,58},{64,6... | collective-permute-start | bytes 393224 | tf_op jit(solution)/shard_map/ppermute | solution.py:44
  115.0 1.7 %collective-permute-start.39 = (bf16[128,512]{1,0:T(8,128)(2,1)S(1)}, bf16[128,512]{1,0:T(8,128)(2,1)S(1)}, u32[]{:S(2)}, u32[]{:S(2)}) collective-permute-start(bf16[128,512]{1,0:T(8,128)(2,1)S(1)} %get-tuple-element.100), channel_id=1, source_target_pairs={{0,3},{8,11},{16,19},{24,27},{32,35},{40,43},{48,51},{56,59},{64,6... | collective-permute-start | bytes 393224 | tf_op jit(solution)/shard_map/ppermute | solution.py:44
  116.7 0.9 collective-permute-start.45
  117.6 1.1 collective-permute-done.40
  118.7 1.4 collective-permute-done.39
  120.9 1.2 collective-permute-start.46
  122.1 2.0 %collective-permute-done.41 = bf16[128,512]{1,0:T(8,128)(2,1)S(1)} collective-permute-done((bf16[128,512]{1,0:T(8,128)(2,1)S(1)}, bf16[128,512]{1,0:T(8,128)(2,1)S(1)}, u32[]{:S(2)}, u32[]{:S(2)}) %collective-permute-start.41) | collective-permute-done | bytes 131104 | tf_op jit(solution)/shard_map/ppermute | solution.py:44
  124.2 0.9 collective-permute-start.42
  125.1 1.0 collective-permute-done.46
  126.1 1.0 collective-permute-start.47
  127.1 1.2 collective-permute-done.42
  128.4 1.2 collective-permute-start.43
  130.4 3.1 %collective-permute-done.43 = bf16[128,512]{1,0:T(8,128)(2,1)S(1)} collective-permute-done((bf16[128,512]{1,0:T(8,128)(2,1)S(1)}, bf16[128,512]{1,0:T(8,128)(2,1)S(1)}, u32[]{:S(2)}, u32[]{:S(2)}) %collective-permute-start.43) | collective-permute-done | bytes 131104 | tf_op jit(solution)/shard_map/ppermute | solution.py:44
  133.6 7.4 %collective-permute-start.48 = (bf16[128,1024]{1,0:T(8,128)(2,1)S(1)}, bf16[128,1024]{1,0:T(8,128)(2,1)S(1)}, u32[]{:S(2)}, u32[]{:S(2)}) collective-permute-start(bf16[128,1024]{1,0:T(8,128)(2,1)S(1)} %pad_maximum_fusion.3), channel_id=1, source_target_pairs={{0,8},{8,0},{16,24},{24,16},{32,40},{40,32},{48,56},{56,48},{64,72... | collective-permute-start | bytes 786440 | tf_op jit(solution)/shard_map/ppermute | solution.py:44
  141.1 1.2 collective-permute-done.48
  142.2 0.9 maximum_select_fusion
  (95 shorter events, 10.2 us)
Async XLA Ops:
  0.6 25.4 %copy-start.4 = (bf16[512,2048]{1,0:T(8,128)(2,1)S(1)}, bf16[512,2048]{1,0:T(8,128)(2,1)}, u32[]{:S(2)}) copy-start(bf16[512,2048]{1,0:T(8,128)(2,1)} %source.1) | copy-start | bytes 6291460
  0.6 1.2 copy-start.8
  1.8 0.8 copy-start.10
  2.7 6.7 %collective-permute-start = (bf16[128,384]{1,0:T(8,128)(2,1)S(1)}, bf16[128,384]{1,0:T(8,128)(2,1)S(1)}, u32[]{:S(2)}, u32[]{:S(2)}) collective-permute-start(bf16[128,384]{1,0:T(8,128)(2,1)S(1)} %get-tuple-element.50), channel_id=1, source_target_pairs={{0,68},{8,76},{16,84},{24,92},{32,100},{40,108},{48,116},{56,124},... | collective-permute-start | bytes 294920 | tf_op jit(solution)/shard_map/ppermute | solution.py:44
  6.3 3.5 %collective-permute-start.1 = (bf16[128,384]{1,0:T(8,128)(2,1)S(1)}, bf16[128,384]{1,0:T(8,128)(2,1)S(1)}, u32[]{:S(2)}, u32[]{:S(2)}) collective-permute-start(bf16[128,384]{1,0:T(8,128)(2,1)S(1)} %get-tuple-element.51), channel_id=1, source_target_pairs={{0,1},{8,9},{16,17},{24,25},{32,33},{40,41},{48,49},{56,57},{64,65... | collective-permute-start | bytes 294920 | tf_op jit(solution)/shard_map/ppermute | solution.py:44
  7.5 4.7 %collective-permute-start.2 = (bf16[192,256]{1,0:T(8,128)(2,1)S(1)}, bf16[192,256]{1,0:T(8,128)(2,1)S(1)}, u32[]{:S(2)}, u32[]{:S(2)}) collective-permute-start(bf16[192,256]{1,0:T(8,128)(2,1)S(1)} %get-tuple-element.52), channel_id=1, source_target_pairs={{0,3},{8,11},{16,19},{24,27},{32,35},{40,43},{48,51},{56,59},{64,6... | collective-permute-start | bytes 294920 | tf_op jit(solution)/shard_map/ppermute | solution.py:44
  12.2 4.6 %collective-permute-start.3 = (bf16[256,384]{1,0:T(8,128)(2,1)S(1)}, bf16[256,384]{1,0:T(8,128)(2,1)S(1)}, u32[]{:S(2)}, u32[]{:S(2)}) collective-permute-start(bf16[256,384]{1,0:T(8,128)(2,1)S(1)} %pad_maximum_fusion.4), channel_id=1, source_target_pairs={{0,1},{8,9},{16,17},{24,25},{32,33},{40,41},{48,49},{56,57},{64,65... | collective-permute-start | bytes 589832 | tf_op jit(solution)/shard_map/ppermute | solution.py:44
  12.3 5.8 %collective-permute-start.4 = (bf16[256,384]{1,0:T(8,128)(2,1)S(1)}, bf16[256,384]{1,0:T(8,128)(2,1)S(1)}, u32[]{:S(2)}, u32[]{:S(2)}) collective-permute-start(bf16[256,384]{1,0:T(8,128)(2,1)S(1)} %pad_maximum_fusion.5), channel_id=1, source_target_pairs={{0,3},{8,11},{16,19},{24,27},{32,35},{40,43},{48,51},{56,59},{64,6... | collective-permute-start | bytes 589832 | tf_op jit(solution)/shard_map/ppermute | solution.py:44
  14.2 6.0 %collective-permute-start.5 = (bf16[384,256]{1,0:T(8,128)(2,1)S(1)}, bf16[384,256]{1,0:T(8,128)(2,1)S(1)}, u32[]{:S(2)}, u32[]{:S(2)}) collective-permute-start(bf16[384,256]{1,0:T(8,128)(2,1)S(1)} %pad_maximum_fusion.6), channel_id=1, source_target_pairs={{0,68},{8,76},{16,84},{24,92},{32,100},{40,108},{48,116},{56,124},... | collective-permute-start | bytes 589832 | tf_op jit(solution)/shard_map/ppermute | solution.py:44
  16.9 9.3 %copy-start.1 = (bf16[512,384]{1,0:T(8,128)(2,1)}, bf16[512,384]{1,0:T(8,128)(2,1)S(1)}, u32[]{:S(2)}) copy-start(bf16[512,384]{1,0:T(8,128)(2,1)S(1)} %pad_maximum_fusion.refs_0_) | copy-start | bytes 1179652
  20.3 15.4 %copy-start.11 = (s32[2]{0:T(128)S(1)}, s32[2]{0:T(128)}, u32[]{:S(2)}) copy-start(s32[2]{0:T(128)} %lengths.1) | copy-start | bytes 28
  20.3 15.4 %copy-start.12 = (s32[8]{0:T(128)S(1)}, s32[8]{0:T(128)}, u32[]{:S(2)}) copy-start(s32[8]{0:T(128)} %param.14) | copy-start | bytes 100
  20.3 17.0 %copy-start = (bf16[512,1024]{1,0:T(8,128)(2,1)S(1)}, bf16[512,1024]{1,0:T(8,128)(2,1)}, u32[]{:S(2)}) copy-start(bf16[512,1024]{1,0:T(8,128)(2,1)} %own_context.5) | copy-start | bytes 3145732
  20.3 17.0 %copy-start.9 = (f32[2048]{0:T(1024)S(1)}, f32[2048]{0:T(1024)}, u32[]{:S(2)}) copy-start(f32[2048]{0:T(1024)} %param.12) | copy-start | bytes 24580
  20.3 8.5 %collective-permute-start.6 = (bf16[512,384]{1,0:T(8,128)(2,1)S(1)}, bf16[512,384]{1,0:T(8,128)(2,1)}, u32[]{:S(2)}, u32[]{:S(2)}) collective-permute-start(bf16[512,384]{1,0:T(8,128)(2,1)S(1)} %pad_maximum_fusion.refs_0_), channel_id=1, source_target_pairs={{0,3},{8,11},{16,19},{24,27},{32,35},{40,43},{48,51},{56,59},{64,6... | collective-permute-start | bytes 1179656 | tf_op jit(solution)/shard_map/ppermute | solution.py:44
  21.3 12.0 %collective-permute-start.7 = (bf16[512,384]{1,0:T(8,128)(2,1)}, bf16[512,384]{1,0:T(8,128)(2,1)}, u32[]{:S(2)}, u32[]{:S(2)}) collective-permute-start(bf16[512,384]{1,0:T(8,128)(2,1)} %pad_maximum_fusion.1.refs_2_), channel_id=1, source_target_pairs={{0,68},{8,76},{16,84},{24,92},{32,100},{40,108},{48,116},{56,124},... | collective-permute-start | bytes 1179656 | tf_op jit(solution)/shard_map/ppermute | solution.py:44
  21.5 11.8 %collective-permute-start.8 = (bf16[768,256]{1,0:T(8,128)(2,1)S(1)}, bf16[768,256]{1,0:T(8,128)(2,1)}, u32[]{:S(2)}, u32[]{:S(2)}) collective-permute-start(bf16[768,256]{1,0:T(8,128)(2,1)S(1)} %pad_maximum_fusion.2.refs_4_.refs_0_), channel_id=1, source_target_pairs={{0,1},{8,9},{16,17},{24,25},{32,33},{40,41},{48,49},{56,57},{64,65... | collective-permute-start | bytes 1179656 | tf_op jit(solution)/shard_map/ppermute | solution.py:44
  21.5 12.9 %collective-permute-start.9 = (bf16[512,384]{1,0:T(8,128)(2,1)S(1)}, bf16[512,384]{1,0:T(8,128)(2,1)S(1)}, u32[]{:S(2)}, u32[]{:S(2)}) collective-permute-start(bf16[512,384]{1,0:T(8,128)(2,1)S(1)} %pad_maximum_fusion.refs_0_), channel_id=1, source_target_pairs={{0,8},{8,0},{16,24},{24,16},{32,40},{40,32},{48,56},{56,48},{64,72... | collective-permute-start | bytes 1179656 | tf_op jit(solution)/shard_map/ppermute | solution.py:44
  26.2 10.3 %collective-permute-start.11 = (bf16[512,384]{1,0:T(8,128)(2,1)}, bf16[512,384]{1,0:T(8,128)(2,1)}, u32[]{:S(2)}, u32[]{:S(2)}) collective-permute-start(bf16[512,384]{1,0:T(8,128)(2,1)} %pad_maximum_fusion.1.refs_2_), channel_id=1, source_target_pairs={{0,8},{8,0},{16,24},{24,16},{32,40},{40,32},{48,56},{56,48},{64,72... | collective-permute-start | bytes 1179656 | tf_op jit(solution)/shard_map/ppermute | solution.py:44
  28.8 7.7 %collective-permute-start.13 = (bf16[768,256]{1,0:T(8,128)(2,1)S(1)}, bf16[768,256]{1,0:T(8,128)(2,1)}, u32[]{:S(2)}, u32[]{:S(2)}) collective-permute-start(bf16[768,256]{1,0:T(8,128)(2,1)S(1)} %pad_maximum_fusion.2.refs_4_.refs_0_), channel_id=1, source_target_pairs={{0,8},{8,0},{16,24},{24,16},{32,40},{40,32},{48,56},{56,48},{64,72... | collective-permute-start | bytes 1179656 | tf_op jit(solution)/shard_map/ppermute | solution.py:44
  33.3 3.2 %collective-permute-start.10 = (bf16[512,384]{1,0:T(8,128)(2,1)}, bf16[512,384]{1,0:T(8,128)(2,1)}, u32[]{:S(2)}, u32[]{:S(2)}) collective-permute-start(bf16[512,384]{1,0:T(8,128)(2,1)} %collective-permute-done.6.refs_1_), channel_id=1, source_target_pairs={{0,8},{8,0},{16,24},{24,16},{32,40},{40,32},{48,56},{56,48},{64,72... | collective-permute-start | bytes 1179656 | tf_op jit(solution)/shard_map/ppermute | solution.py:44
  34.4 2.3 %collective-permute-start.12 = (bf16[512,384]{1,0:T(8,128)(2,1)}, bf16[512,384]{1,0:T(8,128)(2,1)}, u32[]{:S(2)}, u32[]{:S(2)}) collective-permute-start(bf16[512,384]{1,0:T(8,128)(2,1)} %collective-permute-done.7.refs_3_), channel_id=1, source_target_pairs={{0,8},{8,0},{16,24},{24,16},{32,40},{40,32},{48,56},{56,48},{64,72... | collective-permute-start | bytes 1179656 | tf_op jit(solution)/shard_map/ppermute | solution.py:44
  34.4 0.7 copy-start.5
  35.1 2.2 %collective-permute-start.14 = (bf16[768,256]{1,0:T(8,128)(2,1)}, bf16[768,256]{1,0:T(8,128)(2,1)}, u32[]{:S(2)}, u32[]{:S(2)}) collective-permute-start(bf16[768,256]{1,0:T(8,128)(2,1)} %collective-permute-done.8.refs_5_.refs_1_), channel_id=1, source_target_pairs={{0,8},{8,0},{16,24},{24,16},{32,40},{40,32},{48,56},{56,48},{64,72... | collective-permute-start | bytes 1179656 | tf_op jit(solution)/shard_map/ppermute | solution.py:44
  37.3 1.0 copy-start.2
  38.3 1.0 copy-start.6
  45.3 4.1 %collective-permute-start.17 = (bf16[2,2176]{1,0:T(2,128)(2,1)S(1)}, bf16[2,2176]{1,0:T(2,128)(2,1)S(1)}, u32[]{:S(2)}, u32[]{:S(2)}) collective-permute-start(bf16[2,2176]{1,0:T(2,128)(2,1)S(1)} %get-tuple-element.66), channel_id=1, source_target_pairs={{0,2},{8,10},{16,18},{24,26},{32,34},{40,42},{48,50},{56,58},{64,6... | collective-permute-start | bytes 26120 | tf_op jit(solution)/shard_map/ppermute | solution.py:44
  47.4 3.7 %collective-permute-start.16 = (bf16[2,2176]{1,0:T(2,128)(2,1)S(1)}, bf16[2,2176]{1,0:T(2,128)(2,1)S(1)}, u32[]{:S(2)}, u32[]{:S(2)}) collective-permute-start(bf16[2,2176]{1,0:T(2,128)(2,1)S(1)} %get-tuple-element.66), channel_id=1, source_target_pairs={{0,3},{8,11},{16,19},{24,27},{32,35},{40,43},{48,51},{56,59},{64,6... | collective-permute-start | bytes 26120 | tf_op jit(solution)/shard_map/ppermute | solution.py:44
  48.2 2.9 %collective-permute-start.15 = (bf16[2,2176]{1,0:T(2,128)(2,1)S(1)}, bf16[2,2176]{1,0:T(2,128)(2,1)S(1)}, u32[]{:S(2)}, u32[]{:S(2)}) collective-permute-start(bf16[2,2176]{1,0:T(2,128)(2,1)S(1)} %get-tuple-element.66), channel_id=1, source_target_pairs={{0,1},{8,9},{16,17},{24,25},{32,33},{40,41},{48,49},{56,57},{64,65... | collective-permute-start | bytes 26120 | tf_op jit(solution)/shard_map/ppermute | solution.py:44
  51.1 4.8 %collective-permute-start.20 = (bf16[8,2176]{1,0:T(8,128)(2,1)S(1)}, bf16[8,2176]{1,0:T(8,128)(2,1)S(1)}, u32[]{:S(2)}, u32[]{:S(2)}) collective-permute-start(bf16[8,2176]{1,0:T(8,128)(2,1)S(1)} %pad_maximum_fusion.8), channel_id=1, source_target_pairs={{0,4},{8,12},{16,20},{24,28},{32,36},{40,44},{48,52},{56,60},{64,6... | collective-permute-start | bytes 104456 | tf_op jit(solution)/shard_map/ppermute | solution.py:44
  51.2 4.7 %collective-permute-start.19 = (bf16[8,2176]{1,0:T(8,128)(2,1)S(1)}, bf16[8,2176]{1,0:T(8,128)(2,1)S(1)}, u32[]{:S(2)}, u32[]{:S(2)}) collective-permute-start(bf16[8,2176]{1,0:T(8,128)(2,1)S(1)} %pad_maximum_fusion.8), channel_id=1, source_target_pairs={{0,68},{8,76},{16,84},{24,92},{32,100},{40,108},{48,116},{56,124},... | collective-permute-start | bytes 104456 | tf_op jit(solution)/shard_map/ppermute | solution.py:44
  52.8 3.1 %collective-permute-start.18 = (bf16[8,2176]{1,0:T(8,128)(2,1)S(1)}, bf16[8,2176]{1,0:T(8,128)(2,1)S(1)}, u32[]{:S(2)}, u32[]{:S(2)}) collective-permute-start(bf16[8,2176]{1,0:T(8,128)(2,1)S(1)} %pad_maximum_fusion.8), channel_id=1, source_target_pairs={{0,64},{8,72},{16,80},{24,88},{32,96},{40,104},{48,112},{56,120},{... | collective-permute-start | bytes 104456 | tf_op jit(solution)/shard_map/ppermute | solution.py:44
  56.0 7.9 %collective-permute-start.23 = (bf16[32,2176]{1,0:T(8,128)(2,1)S(1)}, bf16[32,2176]{1,0:T(8,128)(2,1)S(1)}, u32[]{:S(2)}, u32[]{:S(2)}) collective-permute-start(bf16[32,2176]{1,0:T(8,128)(2,1)S(1)} %pad_maximum_fusion.7.refs_0_), channel_id=1, source_target_pairs={{0,32},{8,40},{16,48},{24,56},{32,0},{40,8},{48,16},{56,24},{64,96... | collective-permute-start | bytes 417800 | tf_op jit(solution)/shard_map/ppermute | solution.py:44
  59.7 6.9 %collective-permute-start.22 = (bf16[32,2176]{1,0:T(8,128)(2,1)S(1)}, bf16[32,2176]{1,0:T(8,128)(2,1)S(1)}, u32[]{:S(2)}, u32[]{:S(2)}) collective-permute-start(bf16[32,2176]{1,0:T(8,128)(2,1)S(1)} %pad_maximum_fusion.7.refs_0_), channel_id=1, source_target_pairs={{0,48},{8,56},{16,32},{24,40},{32,16},{40,24},{48,0},{56,8},{64,11... | collective-permute-start | bytes 417800 | tf_op jit(solution)/shard_map/ppermute | solution.py:44
  60.1 9.0 %collective-permute-start.21 = (bf16[32,2176]{1,0:T(8,128)(2,1)S(1)}, bf16[32,2176]{1,0:T(8,128)(2,1)S(1)}, u32[]{:S(2)}, u32[]{:S(2)}) collective-permute-start(bf16[32,2176]{1,0:T(8,128)(2,1)S(1)} %pad_maximum_fusion.7.refs_0_), channel_id=1, source_target_pairs={{0,16},{8,24},{16,0},{24,8},{32,48},{40,56},{48,32},{56,40},{64,80... | collective-permute-start | bytes 417800 | tf_op jit(solution)/shard_map/ppermute | solution.py:44
  60.4 8.7 %collective-permute-start.24 = (bf16[32,2176]{1,0:T(8,128)(2,1)S(1)}, bf16[32,2176]{1,0:T(8,128)(2,1)S(1)}, u32[]{:S(2)}, u32[]{:S(2)}) collective-permute-start(bf16[32,2176]{1,0:T(8,128)(2,1)S(1)} %pad_maximum_fusion.7.refs_0_), channel_id=1, source_target_pairs={{0,8},{8,0},{16,24},{24,16},{32,40},{40,32},{48,56},{56,48},{64,72... | collective-permute-start | bytes 417800 | tf_op jit(solution)/shard_map/ppermute | solution.py:44
  63.8 5.3 %collective-permute-start.27 = (bf16[32,2176]{1,0:T(8,128)(2,1)S(1)}, bf16[32,2176]{1,0:T(8,128)(2,1)S(1)}, u32[]{:S(2)}, u32[]{:S(2)}) collective-permute-start(bf16[32,2176]{1,0:T(8,128)(2,1)S(1)} %collective-permute-done.23.refs_3_), channel_id=1, source_target_pairs={{0,8},{8,0},{16,24},{24,16},{32,40},{40,32},{48,56},{56,48},{64,72... | collective-permute-start | bytes 417800 | tf_op jit(solution)/shard_map/ppermute | solution.py:44
  66.6 3.5 %collective-permute-start.26 = (bf16[32,2176]{1,0:T(8,128)(2,1)S(1)}, bf16[32,2176]{1,0:T(8,128)(2,1)S(1)}, u32[]{:S(2)}, u32[]{:S(2)}) collective-permute-start(bf16[32,2176]{1,0:T(8,128)(2,1)S(1)} %collective-permute-done.22.refs_2_), channel_id=1, source_target_pairs={{0,8},{8,0},{16,24},{24,16},{32,40},{40,32},{48,56},{56,48},{64,72... | collective-permute-start | bytes 417800 | tf_op jit(solution)/shard_map/ppermute | solution.py:44
  69.1 1.4 collective-permute-start.25
  74.4 3.5 %collective-permute-start.28 = (f32[8,2048]{1,0:T(8,128)S(1)}, f32[8,2048]{1,0:T(8,128)S(1)}, u32[]{:S(2)}, u32[]{:S(2)}) collective-permute-start(f32[8,2048]{1,0:T(8,128)S(1)} %get-tuple-element.70), channel_id=1, source_target_pairs={{0,16},{8,24},{16,0},{24,8},{32,48},{40,56},{48,32},{56,40},{64,80... | collective-permute-start | bytes 196616 | tf_op jit(solution)/shard_map/ppermute | solution.py:44
  74.5 4.3 %collective-permute-start.29 = (f32[8,2048]{1,0:T(8,128)S(1)}, f32[8,2048]{1,0:T(8,128)S(1)}, u32[]{:S(2)}, u32[]{:S(2)}) collective-permute-start(f32[8,2048]{1,0:T(8,128)S(1)} %get-tuple-element.71), channel_id=1, source_target_pairs={{0,48},{8,56},{16,32},{24,40},{32,16},{40,24},{48,0},{56,8},{64,11... | collective-permute-start | bytes 196616 | tf_op jit(solution)/shard_map/ppermute | solution.py:44
  76.1 4.6 %collective-permute-start.30 = (f32[8,2048]{1,0:T(8,128)S(1)}, f32[8,2048]{1,0:T(8,128)S(1)}, u32[]{:S(2)}, u32[]{:S(2)}) collective-permute-start(f32[8,2048]{1,0:T(8,128)S(1)} %get-tuple-element.72), channel_id=1, source_target_pairs={{0,32},{8,40},{16,48},{24,56},{32,0},{40,8},{48,16},{56,24},{64,96... | collective-permute-start | bytes 196616 | tf_op jit(solution)/shard_map/ppermute | solution.py:44
  80.7 3.6 %collective-permute-start.31 = (f32[8,2048]{1,0:T(8,128)S(1)}, f32[8,2048]{1,0:T(8,128)S(1)}, u32[]{:S(2)}, u32[]{:S(2)}) collective-permute-start(f32[8,2048]{1,0:T(8,128)S(1)} %add_add_fusion.refs_0_), channel_id=1, source_target_pairs={{0,64},{8,72},{16,80},{24,88},{32,96},{40,104},{48,112},{56,120},{... | collective-permute-start | bytes 196616 | tf_op jit(solution)/shard_map/ppermute | solution.py:44
  82.1 7.8 %collective-permute-start.32 = (bf16[512,1024]{1,0:T(8,128)(2,1)S(1)}, bf16[512,1024]{1,0:T(8,128)(2,1)S(1)}, u32[]{:S(2)}, u32[]{:S(2)}) collective-permute-start(bf16[512,1024]{1,0:T(8,128)(2,1)S(1)} %copy-done), channel_id=1, source_target_pairs={{0,8},{8,0},{16,24},{24,16},{32,40},{40,32},{48,56},{56,48},{64,72... | collective-permute-start | bytes 3145736 | tf_op jit(solution)/shard_map/ppermute | solution.py:44
  87.2 5.0 %collective-permute-start.33 = (bf16[512,1024]{1,0:T(8,128)(2,1)S(1)}, bf16[512,1024]{1,0:T(8,128)(2,1)S(1)}, u32[]{:S(2)}, u32[]{:S(2)}) collective-permute-start(bf16[512,1024]{1,0:T(8,128)(2,1)S(1)} %get-tuple-element.77.send), channel_id=1, source_target_pairs={{0,8},{8,0},{16,24},{24,16},{32,40},{40,32},{48,56},{56,48},{64,72... | collective-permute-start | bytes 3145736 | tf_op jit(solution)/shard_map/ppermute | solution.py:44
  93.5 6.4 %copy-start.3 = (bf16[512,384]{1,0:T(8,128)(2,1)S(1)}, bf16[512,384]{1,0:T(8,128)(2,1)}, u32[]{:S(2)}) copy-start(bf16[512,384]{1,0:T(8,128)(2,1)} %copy-done.1) | copy-start | bytes 1179652
  93.5 6.3 %copy-start.7 = (bf16[512,384]{1,0:T(8,128)(2,1)S(1)}, bf16[512,384]{1,0:T(8,128)(2,1)}, u32[]{:S(2)}) copy-start(bf16[512,384]{1,0:T(8,128)(2,1)} %copy-done.5) | copy-start | bytes 1179652
  93.5 17.3 %collective-permute-start.34 = (bf16[512,512]{1,0:T(8,128)(2,1)S(1)}, bf16[512,512]{1,0:T(8,128)(2,1)S(1)}, u32[]{:S(2)}, u32[]{:S(2)}) collective-permute-start(bf16[512,512]{1,0:T(8,128)(2,1)S(1)} %first_sent.1), channel_id=1, source_target_pairs={{0,68},{8,76},{16,84},{24,92},{32,100},{40,108},{48,116},{56,124},... | collective-permute-start | bytes 1572872 | tf_op jit(solution)/shard_map/ppermute | solution.py:44
  96.5 11.0 %collective-permute-start.35 = (bf16[256,512]{1,0:T(8,128)(2,1)S(1)}, bf16[256,512]{1,0:T(8,128)(2,1)S(1)}, u32[]{:S(2)}, u32[]{:S(2)}) collective-permute-start(bf16[256,512]{1,0:T(8,128)(2,1)S(1)} %get-tuple-element.80), channel_id=1, source_target_pairs={{0,1},{8,9},{16,17},{24,25},{32,33},{40,41},{48,49},{56,57},{64,65... | collective-permute-start | bytes 786440 | tf_op jit(solution)/shard_map/ppermute | solution.py:44
  96.6 10.9 %collective-permute-start.36 = (bf16[256,512]{1,0:T(8,128)(2,1)S(1)}, bf16[256,512]{1,0:T(8,128)(2,1)S(1)}, u32[]{:S(2)}, u32[]{:S(2)}) collective-permute-start(bf16[256,512]{1,0:T(8,128)(2,1)S(1)} %get-tuple-element.81), channel_id=1, source_target_pairs={{0,3},{8,11},{16,19},{24,27},{32,35},{40,43},{48,51},{56,59},{64,6... | collective-permute-start | bytes 786440 | tf_op jit(solution)/shard_map/ppermute | solution.py:44
  98.4 12.5 %collective-permute-start.37 = (bf16[256,512]{1,0:T(8,128)(2,1)S(1)}, bf16[256,512]{1,0:T(8,128)(2,1)S(1)}, u32[]{:S(2)}, u32[]{:S(2)}) collective-permute-start(bf16[256,512]{1,0:T(8,128)(2,1)S(1)} %get-tuple-element.82), channel_id=1, source_target_pairs={{0,2},{8,10},{16,18},{24,26},{32,34},{40,42},{48,50},{56,58},{64,6... | collective-permute-start | bytes 786440 | tf_op jit(solution)/shard_map/ppermute | solution.py:44
  111.0 5.6 %collective-permute-start.44 = (bf16[128,512]{1,0:T(8,128)(2,1)S(1)}, bf16[128,512]{1,0:T(8,128)(2,1)S(1)}, u32[]{:S(2)}, u32[]{:S(2)}) collective-permute-start(bf16[128,512]{1,0:T(8,128)(2,1)S(1)} %slice.53), channel_id=1, source_target_pairs={{0,68},{8,76},{16,84},{24,92},{32,100},{40,108},{48,116},{56,124},... | collective-permute-start | bytes 393224 | tf_op jit(solution)/shard_map/ppermute | solution.py:44
  112.7 4.9 %collective-permute-start.38 = (bf16[128,512]{1,0:T(8,128)(2,1)S(1)}, bf16[128,512]{1,0:T(8,128)(2,1)S(1)}, u32[]{:S(2)}, u32[]{:S(2)}) collective-permute-start(bf16[128,512]{1,0:T(8,128)(2,1)S(1)} %get-tuple-element.98), channel_id=1, source_target_pairs={{0,1},{8,9},{16,17},{24,25},{32,33},{40,41},{48,49},{56,57},{64,65... | collective-permute-start | bytes 393224 | tf_op jit(solution)/shard_map/ppermute | solution.py:44
  112.8 6.0 %collective-permute-start.40 = (bf16[128,512]{1,0:T(8,128)(2,1)S(1)}, bf16[128,512]{1,0:T(8,128)(2,1)S(1)}, u32[]{:S(2)}, u32[]{:S(2)}) collective-permute-start(bf16[128,512]{1,0:T(8,128)(2,1)S(1)} %get-tuple-element.99), channel_id=1, source_target_pairs={{0,2},{8,10},{16,18},{24,26},{32,34},{40,42},{48,50},{56,58},{64,6... | collective-permute-start | bytes 393224 | tf_op jit(solution)/shard_map/ppermute | solution.py:44
  115.0 5.2 %collective-permute-start.39 = (bf16[128,512]{1,0:T(8,128)(2,1)S(1)}, bf16[128,512]{1,0:T(8,128)(2,1)S(1)}, u32[]{:S(2)}, u32[]{:S(2)}) collective-permute-start(bf16[128,512]{1,0:T(8,128)(2,1)S(1)} %get-tuple-element.100), channel_id=1, source_target_pairs={{0,3},{8,11},{16,19},{24,27},{32,35},{40,43},{48,51},{56,59},{64,6... | collective-permute-start | bytes 393224 | tf_op jit(solution)/shard_map/ppermute | solution.py:44
  116.7 4.2 %collective-permute-start.45 = (bf16[128,512]{1,0:T(8,128)(2,1)S(1)}, bf16[128,512]{1,0:T(8,128)(2,1)S(1)}, u32[]{:S(2)}, u32[]{:S(2)}) collective-permute-start(bf16[128,512]{1,0:T(8,128)(2,1)S(1)} %fusion.8), channel_id=1, source_target_pairs={{0,16},{8,24},{16,0},{24,8},{32,48},{40,56},{48,32},{56,40},{64,80... | collective-permute-start | bytes 393224 | tf_op jit(solution)/shard_map/ppermute | solution.py:44
  120.2 3.9 %collective-permute-start.41 = (bf16[128,512]{1,0:T(8,128)(2,1)S(1)}, bf16[128,512]{1,0:T(8,128)(2,1)S(1)}, u32[]{:S(2)}, u32[]{:S(2)}) collective-permute-start(bf16[128,512]{1,0:T(8,128)(2,1)S(1)} %get-tuple-element.94), channel_id=1, source_target_pairs={{0,64},{8,72},{16,80},{24,88},{32,96},{40,104},{48,112},{56,120},{... | collective-permute-start | bytes 393224 | tf_op jit(solution)/shard_map/ppermute | solution.py:44
  120.9 5.1 %collective-permute-start.46 = (bf16[128,512]{1,0:T(8,128)(2,1)S(1)}, bf16[128,512]{1,0:T(8,128)(2,1)S(1)}, u32[]{:S(2)}, u32[]{:S(2)}) collective-permute-start(bf16[128,512]{1,0:T(8,128)(2,1)S(1)} %fusion.5), channel_id=1, source_target_pairs={{0,48},{8,56},{16,32},{24,40},{32,16},{40,24},{48,0},{56,8},{64,11... | collective-permute-start | bytes 393224 | tf_op jit(solution)/shard_map/ppermute | solution.py:44
  124.2 4.2 %collective-permute-start.42 = (bf16[128,512]{1,0:T(8,128)(2,1)S(1)}, bf16[128,512]{1,0:T(8,128)(2,1)S(1)}, u32[]{:S(2)}, u32[]{:S(2)}) collective-permute-start(bf16[128,512]{1,0:T(8,128)(2,1)S(1)} %fusion.4), channel_id=1, source_target_pairs={{0,16},{8,24},{16,0},{24,8},{32,48},{40,56},{48,32},{56,40},{64,80... | collective-permute-start | bytes 393224 | tf_op jit(solution)/shard_map/ppermute | solution.py:44
  126.1 4.2 %collective-permute-start.47 = (bf16[128,512]{1,0:T(8,128)(2,1)S(1)}, bf16[128,512]{1,0:T(8,128)(2,1)S(1)}, u32[]{:S(2)}, u32[]{:S(2)}) collective-permute-start(bf16[128,512]{1,0:T(8,128)(2,1)S(1)} %fusion.7), channel_id=1, source_target_pairs={{0,64},{8,72},{16,80},{24,88},{32,96},{40,104},{48,112},{56,120},{... | collective-permute-start | bytes 393224 | tf_op jit(solution)/shard_map/ppermute | solution.py:44
  128.4 5.1 %collective-permute-start.43 = (bf16[128,512]{1,0:T(8,128)(2,1)S(1)}, bf16[128,512]{1,0:T(8,128)(2,1)S(1)}, u32[]{:S(2)}, u32[]{:S(2)}) collective-permute-start(bf16[128,512]{1,0:T(8,128)(2,1)S(1)} %fusion.6), channel_id=1, source_target_pairs={{0,48},{8,56},{16,32},{24,40},{32,16},{40,24},{48,0},{56,8},{64,11... | collective-permute-start | bytes 393224 | tf_op jit(solution)/shard_map/ppermute | solution.py:44
  133.6 8.6 %collective-permute-start.48 = (bf16[128,1024]{1,0:T(8,128)(2,1)S(1)}, bf16[128,1024]{1,0:T(8,128)(2,1)S(1)}, u32[]{:S(2)}, u32[]{:S(2)}) collective-permute-start(bf16[128,1024]{1,0:T(8,128)(2,1)S(1)} %pad_maximum_fusion.3), channel_id=1, source_target_pairs={{0,8},{8,0},{16,24},{24,16},{32,40},{40,32},{48,56},{56,48},{64,72... | collective-permute-start | bytes 786440 | tf_op jit(solution)/shard_map/ppermute | solution.py:44

commit v10 on v9

--- a/solution.py
+++ b/solution.py
@@ -360,16 +360,18 @@
         context_grad[:, pl.ds(pl.multiple_of(home * block, block), block)] = value.astype(BF16)
 
 
-def blocks_kernel(first_blocks, second_blocks, where, own_context, peer_context, own_grad, peer_grad, *outs):
-    part = own_grad.shape[1] // 2
+def blocks_kernel(
+    split, first_blocks, second_blocks, where, own_context, peer_context, own_grad, peer_grad, *outs
+):
+    half = own_grad.shape[1]
     block = own_context.shape[1] // 8
     outs = list(outs)
-    for at, blocks in ((0, first_blocks), (part, second_blocks)):
+    for start, stop, blocks in ((0, split, first_blocks), (split, half, second_blocks)):
         if not blocks:
             continue
         value = contract_rows(
-            blocks_of(own_context, where, blocks, block), own_grad[:, at : at + part]
-        ) + contract_rows(blocks_of(peer_context, where, blocks, block), peer_grad[:, at : at + part])
+            blocks_of(own_context, where, blocks, block), own_grad[:, start:stop]
+        ) + contract_rows(blocks_of(peer_context, where, blocks, block), peer_grad[:, start:stop])
         done = 0
         while done < value.shape[0]:
             out = outs.pop(0)
@@ -527,12 +529,15 @@
         name="context",
     )(where, keep, send, *pieces)
 
-    def blocks(first_blocks, second_blocks, heights, dtype, operands, name):
+    split = half * 5 // 8
+    first_width, second_width = split, half - split
+
+    def blocks(first_blocks, second_blocks, sizes, dtype, operands, name):
         return pl.pallas_call(
-            functools.partial(blocks_kernel, first_blocks, second_blocks),
-            out_shape=tuple(shaped((height * rows, half // 2), dtype) for height in heights),
+            functools.partial(blocks_kernel, split, first_blocks, second_blocks),
+            out_shape=tuple(shaped((height * rows, across), dtype) for height, across in sizes),
             in_specs=[SMEM] + [VMEM] * 4,
-            out_specs=(VMEM,) * len(heights),
+            out_specs=(VMEM,) * len(sizes),
             compiler_params=params(14),
             name=name,
         )(where, *operands)
@@ -544,11 +549,15 @@
         return [(q, ry) for q in places for ry in range(2)]
 
     operands = (context, peer_context, keep, peer_grad)
-    (first_sent,) = blocks(with_ry(1), [], (4,), BF16, operands, "first_sent")
+    (first_sent,) = blocks(with_ry(1), [], [(4, first_width)], BF16, operands, "first_sent")
     first_sent, peer_grad = lax.optimization_barrier((first_sent, peer_grad))
     operands = (context, peer_context, keep, peer_grad)
-    second_sent = blocks([], with_q(1, 2, 3), (2, 2, 2), BF16, operands, "second_sent")
-    first, second = blocks(with_ry(0), with_q(0), (4, 2), F32, operands, "kept")
+    second_sent = blocks(
+        [], with_q(1, 2, 3), [(2, second_width)] * 3, BF16, operands, "second_sent"
+    )
+    first, second = blocks(
+        with_ry(0), with_q(0), [(4, first_width), (2, second_width)], F32, operands, "kept"
+    )
     arrived = [swap_y(first_sent, 3)] + [swap_x(second_sent[q - 1], OFFSETS[q]) for q in (1, 2, 3)]
     arrived, first, second, context_grad = lax.optimization_barrier(
         (arrived, first, second, context_grad)
@@ -561,6 +570,8 @@
     first = first[:rows]
     for piece in arrived:
         first = first + piece.astype(F32)
+    second = jnp.concatenate([first[:, half // 2 :], second], axis=1)
+    first = first[:, : half // 2]
     first = all_added(first, swap_y, 1)
     second = all_added(second, swap_z, 1)
     first = all_added(first, swap_z, 1)

time: 144 us -> 147 us (1.021)
  waiting for transfers between devices: 36.1 us -> 40.4 us
  starting transfers between devices: 72 us -> 70.5 us
    ppermute x49, waiting for transfers between devices: 36.1 us -> 40.4 us  [move(): return lax.ppermute(value, AXES, perm)]
    ppermute x49, starting transfers between devices: 72 us -> 70.5 us  [move(): return lax.ppermute(value, AXES, perm)]
  transfers between devices with their start and end apart: 49 -> 49, of which waited for: 26 -> 25; matrix products, arithmetic and copies ran while one was open for 2% -> 2% of each run, Pallas kernels for 10% -> 10%
where the time goes in v10:
time: 147 us; the launch traced here: 146 us
  starting transfers between devices  70.5 us (48%)
  waiting for transfers between devices  40.4 us (27%)
  Pallas kernels  26.2 us (18%)
  local copies, waits for them, and re-layouts  4.64 us (3%)
  other arithmetic  3.47 us (2%)
    ppermute x49, starting transfers between devices, move(): return lax.ppermute(value, AXES, perm)  70.5 us
    ppermute x49, waiting for transfers between devices, move(): return lax.ppermute(value, AXES, perm)  40.4 us
    pallas_call x1, Pallas kernels, on_device(): pl.pallas_call(context_kernel, out_shape=shaped((tokens, head), BF16), in...  6.03 us
    pallas_call x1, Pallas kernels, on_device(): pl.pallas_call(functools.partial(forward_kernel, items_here), out_shape=(...  5.95 us
    pallas_call x3, Pallas kernels, blocks(): pl.pallas_call(functools.partial(blocks_kernel, split, first_blocks, seco...  5.01 us
    unnamed x26, local copies, waits for them, and re-layouts  4.58 us
    pallas_call x1, Pallas kernels, on_device(): pl.pallas_call(functools.partial(loss_kernel, users_here, items_here), ou...  3.94 us
    pallas_call x1, Pallas kernels, on_device(): pl.pallas_call(functools.partial(residual_kernel, 8 * people), out_shape=...  2.95 us
  transfers between devices with their start and end apart: 49, of which 25 were waited for; matrix products, arithmetic and copies ran while one was open for 2% of the time, Pallas kernels for 10%

profile of v10, /device:TPU:1, one launch (start us, length us, event | category | flops | bytes accessed | tf_op | source)
XLA Modules:
  0.0 146.2 jit_solution(18407701763994637045)
XLA Ops:
  0.6 1.0 copy-done.8
  2.5 3.6 %collective-permute-start = (bf16[128,384]{1,0:T(8,128)(2,1)S(1)}, bf16[128,384]{1,0:T(8,128)(2,1)S(1)}, u32[]{:S(2)}, u32[]{:S(2)}) collective-permute-start(bf16[128,384]{1,0:T(8,128)(2,1)S(1)} %get-tuple-element.50), channel_id=1, source_target_pairs={{0,68},{8,76},{16,84},{24,92},{32,100},{40,108},{48,116},{56,124},... | collective-permute-start | bytes 294920 | tf_op jit(solution)/shard_map/ppermute | solution.py:44
  6.2 1.2 collective-permute-start.1
  7.4 1.8 %collective-permute-start.2 = (bf16[192,256]{1,0:T(8,128)(2,1)S(1)}, bf16[192,256]{1,0:T(8,128)(2,1)S(1)}, u32[]{:S(2)}, u32[]{:S(2)}) collective-permute-start(bf16[192,256]{1,0:T(8,128)(2,1)S(1)} %get-tuple-element.52), channel_id=1, source_target_pairs={{0,3},{8,11},{16,19},{24,27},{32,35},{40,43},{48,51},{56,59},{64,6... | collective-permute-start | bytes 294920 | tf_op jit(solution)/shard_map/ppermute | solution.py:44
  9.7 2.4 %collective-permute-done.2 = bf16[192,256]{1,0:T(8,128)(2,1)S(1)} collective-permute-done((bf16[192,256]{1,0:T(8,128)(2,1)S(1)}, bf16[192,256]{1,0:T(8,128)(2,1)S(1)}, u32[]{:S(2)}, u32[]{:S(2)}) %collective-permute-start.2) | collective-permute-done | bytes 98336 | tf_op jit(solution)/shard_map/ppermute | solution.py:44
  12.2 1.9 %collective-permute-start.4 = (bf16[256,384]{1,0:T(8,128)(2,1)S(1)}, bf16[256,384]{1,0:T(8,128)(2,1)S(1)}, u32[]{:S(2)}, u32[]{:S(2)}) collective-permute-start(bf16[256,384]{1,0:T(8,128)(2,1)S(1)} %pad_maximum_fusion.5), channel_id=1, source_target_pairs={{0,3},{8,11},{16,19},{24,27},{32,35},{40,43},{48,51},{56,59},{64,6... | collective-permute-start | bytes 589832 | tf_op jit(solution)/shard_map/ppermute | solution.py:44
  14.5 2.2 %collective-permute-done.3 = bf16[256,384]{1,0:T(8,128)(2,1)S(1)} collective-permute-done((bf16[256,384]{1,0:T(8,128)(2,1)S(1)}, bf16[256,384]{1,0:T(8,128)(2,1)S(1)}, u32[]{:S(2)}, u32[]{:S(2)}) %collective-permute-start.3) | collective-permute-done | bytes 196640 | tf_op jit(solution)/shard_map/ppermute | solution.py:44
  16.7 1.2 collective-permute-done.4
  18.8 1.3 collective-permute-done.5
  20.2 0.9 collective-permute-start.6
  21.3 4.5 %collective-permute-start.9 = (bf16[512,384]{1,0:T(8,128)(2,1)S(1)}, bf16[512,384]{1,0:T(8,128)(2,1)S(1)}, u32[]{:S(2)}, u32[]{:S(2)}) collective-permute-start(bf16[512,384]{1,0:T(8,128)(2,1)S(1)} %pad_maximum_fusion.refs_0_), channel_id=1, source_target_pairs={{0,8},{8,0},{16,24},{24,16},{32,40},{40,32},{48,56},{56,48},{64,72... | collective-permute-start | bytes 1179656 | tf_op jit(solution)/shard_map/ppermute | solution.py:44
  26.1 2.5 %collective-permute-done.6.refs_1_ = bf16[512,384]{1,0:T(8,128)(2,1)} collective-permute-done((bf16[512,384]{1,0:T(8,128)(2,1)S(1)}, bf16[512,384]{1,0:T(8,128)(2,1)}, u32[]{:S(2)}, u32[]{:S(2)}) %collective-permute-start.6) | collective-permute-done | bytes 393248 | tf_op jit(solution)/shard_map/ppermute | solution.py:44
  28.7 4.4 %collective-permute-start.13 = (bf16[768,256]{1,0:T(8,128)(2,1)S(1)}, bf16[768,256]{1,0:T(8,128)(2,1)}, u32[]{:S(2)}, u32[]{:S(2)}) collective-permute-start(bf16[768,256]{1,0:T(8,128)(2,1)S(1)} %pad_maximum_fusion.2.refs_4_.refs_0_), channel_id=1, source_target_pairs={{0,8},{8,0},{16,24},{24,16},{32,40},{40,32},{48,56},{56,48},{64,72... | collective-permute-start | bytes 1179656 | tf_op jit(solution)/shard_map/ppermute | solution.py:44
  33.1 1.1 collective-permute-start.10
  37.2 1.0 copy-done.2
  38.2 1.0 copy-done.6
  39.2 5.9 %forward.1 = (f32[512,2048]{1,0:T(8,128)S(1)}, f32[512,1]{1,0:T(8,128)S(1)}, f32[2,2048]{1,0:T(2,128)S(1)}, bf16[2,2176]{1,0:T(2,128)(2,1)S(1)}) custom-call(s32[18]{0:T(128)S(1)} %pad_add_fusion.1.ints, bf16[512,1024]{1,0:T(8,128)(2,1)S(1)} %copy-done, bf16[512,2048]{1,0:T(8,128)(2,1)S(1)} %hold.1.residual, f32[1,2048]{1,0:T(1,128)S(1)} %bitcast.7, ...), custom_call_target="tpu_custom_call" | custom-call | tf_op jit(solution)/shard_map/forward/pallas_call | solution.py:459
  45.1 2.1 %collective-permute-start.17 = (bf16[2,2176]{1,0:T(2,128)(2,1)S(1)}, bf16[2,2176]{1,0:T(2,128)(2,1)S(1)}, u32[]{:S(2)}, u32[]{:S(2)}) collective-permute-start(bf16[2,2176]{1,0:T(2,128)(2,1)S(1)} %get-tuple-element.66), channel_id=1, source_target_pairs={{0,2},{8,10},{16,18},{24,26},{32,34},{40,42},{48,50},{56,58},{64,6... | collective-permute-start | bytes 26120 | tf_op jit(solution)/shard_map/ppermute | solution.py:44
  47.2 0.9 collective-permute-start.16
  48.0 1.2 collective-permute-done.17
  49.2 1.7 %collective-permute-done.16 = bf16[2,2176]{1,0:T(2,128)(2,1)S(1)} collective-permute-done((bf16[2,2176]{1,0:T(2,128)(2,1)S(1)}, bf16[2,2176]{1,0:T(2,128)(2,1)S(1)}, u32[]{:S(2)}, u32[]{:S(2)}) %collective-permute-start.16) | collective-permute-done | bytes 8736 | tf_op jit(solution)/shard_map/ppermute | solution.py:44
  51.1 1.6 %collective-permute-start.19 = (bf16[8,2176]{1,0:T(8,128)(2,1)S(1)}, bf16[8,2176]{1,0:T(8,128)(2,1)S(1)}, u32[]{:S(2)}, u32[]{:S(2)}) collective-permute-start(bf16[8,2176]{1,0:T(8,128)(2,1)S(1)} %pad_maximum_fusion.8), channel_id=1, source_target_pairs={{0,68},{8,76},{16,84},{24,92},{32,100},{40,108},{48,116},{56,124},... | collective-permute-start | bytes 104456 | tf_op jit(solution)/shard_map/ppermute | solution.py:44
  52.7 1.0 collective-permute-start.18
  53.7 2.1 %users.3.users_ref = bf16[128,2048]{1,0:T(8,128)(2,1)S(1)} custom-call(s32[4]{0:T(128)S(1)} %pad_add_fusion.where, bf16[768,256]{1,0:T(8,128)(2,1)S(1)} %pad_maximum_fusion.2.refs_4_.refs_0_, bf16[768,256]{1,0:T(8,128)(2,1)} %collective-permute-done.8.refs_5_.refs_1_, bf16[768,256]{1,0:T(8,128)(2,1)} %collective-permute-done.13.refs_10_.refs_2_, ...), custom_call_target="tpu_custom_call" | custom-call | tf_op jit(solution)/shard_map/users/pallas_call | solution.py:476
  55.8 3.7 %collective-permute-start.23 = (bf16[32,2176]{1,0:T(8,128)(2,1)S(1)}, bf16[32,2176]{1,0:T(8,128)(2,1)S(1)}, u32[]{:S(2)}, u32[]{:S(2)}) collective-permute-start(bf16[32,2176]{1,0:T(8,128)(2,1)S(1)} %pad_maximum_fusion.7.refs_0_), channel_id=1, source_target_pairs={{0,32},{8,40},{16,48},{24,56},{32,0},{40,8},{48,16},{56,24},{64,96... | collective-permute-start | bytes 417800 | tf_op jit(solution)/shard_map/ppermute | solution.py:44
  60.2 3.4 %collective-permute-start.24 = (bf16[32,2176]{1,0:T(8,128)(2,1)S(1)}, bf16[32,2176]{1,0:T(8,128)(2,1)S(1)}, u32[]{:S(2)}, u32[]{:S(2)}) collective-permute-start(bf16[32,2176]{1,0:T(8,128)(2,1)S(1)} %pad_maximum_fusion.7.refs_0_), channel_id=1, source_target_pairs={{0,8},{8,0},{16,24},{24,16},{32,40},{40,32},{48,56},{56,48},{64,72... | collective-permute-start | bytes 417800 | tf_op jit(solution)/shard_map/ppermute | solution.py:44
  63.7 2.7 %collective-permute-start.27 = (bf16[32,2176]{1,0:T(8,128)(2,1)S(1)}, bf16[32,2176]{1,0:T(8,128)(2,1)S(1)}, u32[]{:S(2)}, u32[]{:S(2)}) collective-permute-start(bf16[32,2176]{1,0:T(8,128)(2,1)S(1)} %collective-permute-done.23.refs_3_), channel_id=1, source_target_pairs={{0,8},{8,0},{16,24},{24,16},{32,40},{40,32},{48,56},{56,48},{64,72... | collective-permute-start | bytes 417800 | tf_op jit(solution)/shard_map/ppermute | solution.py:44
  66.4 2.5 %collective-permute-start.26 = (bf16[32,2176]{1,0:T(8,128)(2,1)S(1)}, bf16[32,2176]{1,0:T(8,128)(2,1)S(1)}, u32[]{:S(2)}, u32[]{:S(2)}) collective-permute-start(bf16[32,2176]{1,0:T(8,128)(2,1)S(1)} %collective-permute-done.22.refs_2_), channel_id=1, source_target_pairs={{0,8},{8,0},{16,24},{24,16},{32,40},{40,32},{48,56},{56,48},{64,72... | collective-permute-start | bytes 417800 | tf_op jit(solution)/shard_map/ppermute | solution.py:44
  69.0 1.0 collective-permute-done.26.refs_6_
  70.3 3.9 %loss.1 = (f32[8,2048]{1,0:T(8,128)S(1)}, f32[8,2048]{1,0:T(8,128)S(1)}, f32[8,2048]{1,0:T(8,128)S(1)}, f32[8,2048]{1,0:T(8,128)S(1)}, bf16[8,2048]{1,0:T(8,128)(2,1)}) custom-call(s32[4]{0:T(128)S(1)} %pad_add_fusion.where, f32[1,2048]{1,0:T(1,128)S(1)} %bitcast.8, bf16[128,2048]{1,0:T(8,128)(2,1)S(1)} %users.3.users_ref, ...), custom_call_target="tpu_custom_call" | custom-call | tf_op jit(solution)/shard_map/loss/pallas_call | solution.py:493
  74.3 1.6 %collective-permute-start.29 = (f32[8,2048]{1,0:T(8,128)S(1)}, f32[8,2048]{1,0:T(8,128)S(1)}, u32[]{:S(2)}, u32[]{:S(2)}) collective-permute-start(f32[8,2048]{1,0:T(8,128)S(1)} %get-tuple-element.71), channel_id=1, source_target_pairs={{0,48},{8,56},{16,32},{24,40},{32,16},{40,24},{48,0},{56,8},{64,11... | collective-permute-start | bytes 196616 | tf_op jit(solution)/shard_map/ppermute | solution.py:44
  75.9 1.6 %collective-permute-start.30 = (f32[8,2048]{1,0:T(8,128)S(1)}, f32[8,2048]{1,0:T(8,128)S(1)}, u32[]{:S(2)}, u32[]{:S(2)}) collective-permute-start(f32[8,2048]{1,0:T(8,128)S(1)} %get-tuple-element.72), channel_id=1, source_target_pairs={{0,32},{8,40},{16,48},{24,56},{32,0},{40,8},{48,16},{56,24},{64,96... | collective-permute-start | bytes 196616 | tf_op jit(solution)/shard_map/ppermute | solution.py:44
  77.7 0.9 collective-permute-done.29
  78.6 1.9 %collective-permute-done.30 = f32[8,2048]{1,0:T(8,128)S(1)} collective-permute-done((f32[8,2048]{1,0:T(8,128)S(1)}, f32[8,2048]{1,0:T(8,128)S(1)}, u32[]{:S(2)}, u32[]{:S(2)}) %collective-permute-start.30) | collective-permute-done | bytes 65568 | tf_op jit(solution)/shard_map/ppermute | solution.py:44
  80.5 1.4 collective-permute-start.31
  81.9 2.2 %collective-permute-start.32 = (bf16[512,1024]{1,0:T(8,128)(2,1)S(1)}, bf16[512,1024]{1,0:T(8,128)(2,1)S(1)}, u32[]{:S(2)}, u32[]{:S(2)}) collective-permute-start(bf16[512,1024]{1,0:T(8,128)(2,1)S(1)} %copy-done), channel_id=1, source_target_pairs={{0,8},{8,0},{16,24},{24,16},{32,40},{40,32},{48,56},{56,48},{64,72... | collective-permute-start | bytes 3145736 | tf_op jit(solution)/shard_map/ppermute | solution.py:44
  84.1 2.9 %residual.1 = (bf16[512,2048]{1,0:T(8,128)(2,1)}, bf16[512,1024]{1,0:T(8,128)(2,1)S(1)}, bf16[512,1024]{1,0:T(8,128)(2,1)S(1)}, f32[1,2048]{1,0:T(1,128)}, f32[1,1]{1,0:T(1,128)}) custom-call(s32[4]{0:T(128)S(1)} %pad_add_fusion.where, s32[2]{0:T(128)S(1)} %copy-done.11, f32[512,2048]{1,0:T(8,128)S(1)} %get-tuple-element.63.stream, ...), custom_call_target="tpu_custom_call" | custom-call | tf_op jit(solution)/shard_map/residual/pallas_call | solution.py:508
  87.1 2.7 %collective-permute-start.33 = (bf16[512,1024]{1,0:T(8,128)(2,1)S(1)}, bf16[512,1024]{1,0:T(8,128)(2,1)S(1)}, u32[]{:S(2)}, u32[]{:S(2)}) collective-permute-start(bf16[512,1024]{1,0:T(8,128)(2,1)S(1)} %get-tuple-element.77.send), channel_id=1, source_target_pairs={{0,8},{8,0},{16,24},{24,16},{32,40},{40,32},{48,56},{56,48},{64,72... | collective-permute-start | bytes 3145736 | tf_op jit(solution)/shard_map/ppermute | solution.py:44
  89.7 2.3 %collective-permute-done.33.peer_grad = bf16[512,1024]{1,0:T(8,128)(2,1)S(1)} collective-permute-done((bf16[512,1024]{1,0:T(8,128)(2,1)S(1)}, bf16[512,1024]{1,0:T(8,128)(2,1)S(1)}, u32[]{:S(2)}, u32[]{:S(2)}) %collective-permute-start.33) | collective-permute-done | bytes 1048608 | tf_op jit(solution)/shard_map/ppermute | solution.py:44
  92.0 1.6 %first_sent.1 = bf16[512,640]{1,0:T(8,128)(2,1)S(1)} custom-call(s32[4]{0:T(128)S(1)} %pad_add_fusion.where, bf16[512,1024]{1,0:T(8,128)(2,1)S(1)} %copy-done, bf16[512,1024]{1,0:T(8,128)(2,1)S(1)} %collective-permute-done.32.peer_context, bf16[512,1024]{1,0:T(8,128)(2,1)S(1)} %get-tuple-element.76.own_grad.keep, ...), custom_call_target="tpu_custom_call" | custom-call | tf_op jit(solution)/shard_map/first_sent/pallas_call | solution.py:536
  93.6 1.4 collective-permute-start.34
  95.0 1.6 %second_sent.1 = (bf16[256,384]{1,0:T(8,128)(2,1)S(1)}, bf16[256,384]{1,0:T(8,128)(2,1)S(1)}, bf16[256,384]{1,0:T(8,128)(2,1)S(1)}) custom-call(s32[4]{0:T(128)S(1)} %pad_add_fusion.where, bf16[512,1024]{1,0:T(8,128)(2,1)S(1)} %copy-done, bf16[512,1024]{1,0:T(8,128)(2,1)S(1)} %collective-permute-done.32.peer_context, ...), custom_call_target="tpu_custom_call" | custom-call | tf_op jit(solution)/shard_map/second_sent/pallas_call | solution.py:536
  96.7 1.8 %collective-permute-start.36 = (bf16[256,384]{1,0:T(8,128)(2,1)S(1)}, bf16[256,384]{1,0:T(8,128)(2,1)S(1)}, u32[]{:S(2)}, u32[]{:S(2)}) collective-permute-start(bf16[256,384]{1,0:T(8,128)(2,1)S(1)} %get-tuple-element.81), channel_id=1, source_target_pairs={{0,3},{8,11},{16,19},{24,27},{32,35},{40,43},{48,51},{56,59},{64,6... | collective-permute-start | bytes 589832 | tf_op jit(solution)/shard_map/ppermute | solution.py:44
  98.5 1.4 collective-permute-start.37
  100.0 6.0 %context.3 = bf16[512,1024]{1,0:T(8,128)(2,1)} custom-call(s32[4]{0:T(128)S(1)} %pad_add_fusion.where, bf16[512,1024]{1,0:T(8,128)(2,1)S(1)} %get-tuple-element.76.own_grad.keep, bf16[512,1024]{1,0:T(8,128)(2,1)S(1)} %get-tuple-element.77.send, bf16[512,384]{1,0:T(8,128)(2,1)S(1)} %copy-done.3, bf16[512,384]{1,0:T(8,128)(2,1)} %collective-permute-done.6.refs_1_, ...), custom_call_target="tpu_custom_call" | custom-call | tf_op jit(solution)/shard_map/context/pallas_call | solution.py:523
  106.0 1.8 %kept.1 = (f32[512,640]{1,0:T(8,128)S(1)}, f32[256,384]{1,0:T(8,128)S(1)}) custom-call(s32[4]{0:T(128)S(1)} %pad_add_fusion.where, bf16[512,1024]{1,0:T(8,128)(2,1)S(1)} %copy-done, bf16[512,1024]{1,0:T(8,128)(2,1)S(1)} %collective-permute-done.32.peer_context, bf16[512,1024]{1,0:T(8,128)(2,1)S(1)} %get-tuple-element.76.own_grad.keep, ...), custom_call_target="tpu_custom_call" | custom-call | tf_op jit(solution)/shard_map/kept/pallas_call | solution.py:536
  108.2 2.7 %collective-permute-done.34 = bf16[512,640]{1,0:T(8,128)(2,1)S(1)} collective-permute-done((bf16[512,640]{1,0:T(8,128)(2,1)S(1)}, bf16[512,640]{1,0:T(8,128)(2,1)S(1)}, u32[]{:S(2)}, u32[]{:S(2)}) %collective-permute-start.34) | collective-permute-done | bytes 655392 | tf_op jit(solution)/shard_map/ppermute | solution.py:44
  111.4 2.9 %collective-permute-start.40 = (bf16[128,640]{1,0:T(8,128)(2,1)S(1)}, bf16[128,640]{1,0:T(8,128)(2,1)S(1)}, u32[]{:S(2)}, u32[]{:S(2)}) collective-permute-start(bf16[128,640]{1,0:T(8,128)(2,1)S(1)} %get-tuple-element.97), channel_id=1, source_target_pairs={{0,2},{8,10},{16,18},{24,26},{32,34},{40,42},{48,50},{56,58},{64,6... | collective-permute-start | bytes 491528 | tf_op jit(solution)/shard_map/ppermute | solution.py:44
  114.3 0.9 collective-permute-start.39
  115.4 1.4 collective-permute-start.44
  116.7 4.1 %collective-permute-done.40 = bf16[128,640]{1,0:T(8,128)(2,1)S(1)} collective-permute-done((bf16[128,640]{1,0:T(8,128)(2,1)S(1)}, bf16[128,640]{1,0:T(8,128)(2,1)S(1)}, u32[]{:S(2)}, u32[]{:S(2)}) %collective-permute-start.40) | collective-permute-done | bytes 163872 | tf_op jit(solution)/shard_map/ppermute | solution.py:44
  120.8 2.8 %collective-permute-done.39 = bf16[128,640]{1,0:T(8,128)(2,1)S(1)} collective-permute-done((bf16[128,640]{1,0:T(8,128)(2,1)S(1)}, bf16[128,640]{1,0:T(8,128)(2,1)S(1)}, u32[]{:S(2)}, u32[]{:S(2)}) %collective-permute-start.39) | collective-permute-done | bytes 163872 | tf_op jit(solution)/shard_map/ppermute | solution.py:44
  124.0 0.9 collective-permute-start.45
  124.9 2.7 %collective-permute-done.41 = bf16[128,512]{1,0:T(8,128)(2,1)S(1)} collective-permute-done((bf16[128,512]{1,0:T(8,128)(2,1)S(1)}, bf16[128,512]{1,0:T(8,128)(2,1)S(1)}, u32[]{:S(2)}, u32[]{:S(2)}) %collective-permute-start.41) | collective-permute-done | bytes 131104 | tf_op jit(solution)/shard_map/ppermute | solution.py:44
  127.7 0.9 collective-permute-start.42
  128.6 1.1 collective-permute-start.46
  129.7 1.9 %collective-permute-done.42 = bf16[128,512]{1,0:T(8,128)(2,1)S(1)} collective-permute-done((bf16[128,512]{1,0:T(8,128)(2,1)S(1)}, bf16[128,512]{1,0:T(8,128)(2,1)S(1)}, u32[]{:S(2)}, u32[]{:S(2)}) %collective-permute-start.42) | collective-permute-done | bytes 131104 | tf_op jit(solution)/shard_map/ppermute | solution.py:44
  131.7 1.2 collective-permute-start.43
  132.8 0.9 collective-permute-done.46
  133.8 1.0 collective-permute-start.47
  134.8 3.3 %collective-permute-done.43 = bf16[128,512]{1,0:T(8,128)(2,1)S(1)} collective-permute-done((bf16[128,512]{1,0:T(8,128)(2,1)S(1)}, bf16[128,512]{1,0:T(8,128)(2,1)S(1)}, u32[]{:S(2)}, u32[]{:S(2)}) %collective-permute-start.43) | collective-permute-done | bytes 131104 | tf_op jit(solution)/shard_map/ppermute | solution.py:44
  138.3 5.8 %collective-permute-start.48 = (bf16[128,1024]{1,0:T(8,128)(2,1)S(1)}, bf16[128,1024]{1,0:T(8,128)(2,1)S(1)}, u32[]{:S(2)}, u32[]{:S(2)}) collective-permute-start(bf16[128,1024]{1,0:T(8,128)(2,1)S(1)} %pad_maximum_fusion.3), channel_id=1, source_target_pairs={{0,8},{8,0},{16,24},{24,16},{32,40},{40,32},{48,56},{56,48},{64,72... | collective-permute-start | bytes 786440 | tf_op jit(solution)/shard_map/ppermute | solution.py:44
  144.2 1.2 collective-permute-done.48
  145.3 0.9 maximum_select_fusion
  (98 shorter events, 9.4 us)
Async XLA Ops:
  0.6 1.0 copy-start.8
  1.7 0.8 copy-start.10
  2.5 6.7 %collective-permute-start = (bf16[128,384]{1,0:T(8,128)(2,1)S(1)}, bf16[128,384]{1,0:T(8,128)(2,1)S(1)}, u32[]{:S(2)}, u32[]{:S(2)}) collective-permute-start(bf16[128,384]{1,0:T(8,128)(2,1)S(1)} %get-tuple-element.50), channel_id=1, source_target_pairs={{0,68},{8,76},{16,84},{24,92},{32,100},{40,108},{48,116},{56,124},... | collective-permute-start | bytes 294920 | tf_op jit(solution)/shard_map/ppermute | solution.py:44
  6.2 3.5 %collective-permute-start.1 = (bf16[128,384]{1,0:T(8,128)(2,1)S(1)}, bf16[128,384]{1,0:T(8,128)(2,1)S(1)}, u32[]{:S(2)}, u32[]{:S(2)}) collective-permute-start(bf16[128,384]{1,0:T(8,128)(2,1)S(1)} %get-tuple-element.51), channel_id=1, source_target_pairs={{0,1},{8,9},{16,17},{24,25},{32,33},{40,41},{48,49},{56,57},{64,65... | collective-permute-start | bytes 294920 | tf_op jit(solution)/shard_map/ppermute | solution.py:44
  7.4 4.7 %collective-permute-start.2 = (bf16[192,256]{1,0:T(8,128)(2,1)S(1)}, bf16[192,256]{1,0:T(8,128)(2,1)S(1)}, u32[]{:S(2)}, u32[]{:S(2)}) collective-permute-start(bf16[192,256]{1,0:T(8,128)(2,1)S(1)} %get-tuple-element.52), channel_id=1, source_target_pairs={{0,3},{8,11},{16,19},{24,27},{32,35},{40,43},{48,51},{56,59},{64,6... | collective-permute-start | bytes 294920 | tf_op jit(solution)/shard_map/ppermute | solution.py:44
  9.7 16.2 %copy-start.4 = (bf16[512,2048]{1,0:T(8,128)(2,1)S(1)}, bf16[512,2048]{1,0:T(8,128)(2,1)}, u32[]{:S(2)}) copy-start(bf16[512,2048]{1,0:T(8,128)(2,1)} %source.1) | copy-start | bytes 6291460
  12.1 4.6 %collective-permute-start.3 = (bf16[256,384]{1,0:T(8,128)(2,1)S(1)}, bf16[256,384]{1,0:T(8,128)(2,1)S(1)}, u32[]{:S(2)}, u32[]{:S(2)}) collective-permute-start(bf16[256,384]{1,0:T(8,128)(2,1)S(1)} %pad_maximum_fusion.4), channel_id=1, source_target_pairs={{0,1},{8,9},{16,17},{24,25},{32,33},{40,41},{48,49},{56,57},{64,65... | collective-permute-start | bytes 589832 | tf_op jit(solution)/shard_map/ppermute | solution.py:44
  12.2 5.8 %collective-permute-start.4 = (bf16[256,384]{1,0:T(8,128)(2,1)S(1)}, bf16[256,384]{1,0:T(8,128)(2,1)S(1)}, u32[]{:S(2)}, u32[]{:S(2)}) collective-permute-start(bf16[256,384]{1,0:T(8,128)(2,1)S(1)} %pad_maximum_fusion.5), channel_id=1, source_target_pairs={{0,3},{8,11},{16,19},{24,27},{32,35},{40,43},{48,51},{56,59},{64,6... | collective-permute-start | bytes 589832 | tf_op jit(solution)/shard_map/ppermute | solution.py:44
  14.1 6.0 %collective-permute-start.5 = (bf16[384,256]{1,0:T(8,128)(2,1)S(1)}, bf16[384,256]{1,0:T(8,128)(2,1)S(1)}, u32[]{:S(2)}, u32[]{:S(2)}) collective-permute-start(bf16[384,256]{1,0:T(8,128)(2,1)S(1)} %pad_maximum_fusion.6), channel_id=1, source_target_pairs={{0,68},{8,76},{16,84},{24,92},{32,100},{40,108},{48,116},{56,124},... | collective-permute-start | bytes 589832 | tf_op jit(solution)/shard_map/ppermute | solution.py:44
  16.7 9.3 %copy-start.1 = (bf16[512,384]{1,0:T(8,128)(2,1)}, bf16[512,384]{1,0:T(8,128)(2,1)S(1)}, u32[]{:S(2)}) copy-start(bf16[512,384]{1,0:T(8,128)(2,1)S(1)} %pad_maximum_fusion.refs_0_) | copy-start | bytes 1179652
  20.1 15.4 %copy-start.11 = (s32[2]{0:T(128)S(1)}, s32[2]{0:T(128)}, u32[]{:S(2)}) copy-start(s32[2]{0:T(128)} %lengths.1) | copy-start | bytes 28
  20.1 15.4 %copy-start.12 = (s32[8]{0:T(128)S(1)}, s32[8]{0:T(128)}, u32[]{:S(2)}) copy-start(s32[8]{0:T(128)} %param.14) | copy-start | bytes 100
  20.2 17.0 %copy-start = (bf16[512,1024]{1,0:T(8,128)(2,1)S(1)}, bf16[512,1024]{1,0:T(8,128)(2,1)}, u32[]{:S(2)}) copy-start(bf16[512,1024]{1,0:T(8,128)(2,1)} %own_context.5) | copy-start | bytes 3145732
  20.2 17.0 %copy-start.9 = (f32[2048]{0:T(1024)S(1)}, f32[2048]{0:T(1024)}, u32[]{:S(2)}) copy-start(f32[2048]{0:T(1024)} %param.12) | copy-start | bytes 24580
  20.2 8.5 %collective-permute-start.6 = (bf16[512,384]{1,0:T(8,128)(2,1)S(1)}, bf16[512,384]{1,0:T(8,128)(2,1)}, u32[]{:S(2)}, u32[]{:S(2)}) collective-permute-start(bf16[512,384]{1,0:T(8,128)(2,1)S(1)} %pad_maximum_fusion.refs_0_), channel_id=1, source_target_pairs={{0,3},{8,11},{16,19},{24,27},{32,35},{40,43},{48,51},{56,59},{64,6... | collective-permute-start | bytes 1179656 | tf_op jit(solution)/shard_map/ppermute | solution.py:44
  21.1 12.0 %collective-permute-start.7 = (bf16[512,384]{1,0:T(8,128)(2,1)}, bf16[512,384]{1,0:T(8,128)(2,1)}, u32[]{:S(2)}, u32[]{:S(2)}) collective-permute-start(bf16[512,384]{1,0:T(8,128)(2,1)} %pad_maximum_fusion.1.refs_2_), channel_id=1, source_target_pairs={{0,68},{8,76},{16,84},{24,92},{32,100},{40,108},{48,116},{56,124},... | collective-permute-start | bytes 1179656 | tf_op jit(solution)/shard_map/ppermute | solution.py:44
  21.3 11.8 %collective-permute-start.8 = (bf16[768,256]{1,0:T(8,128)(2,1)S(1)}, bf16[768,256]{1,0:T(8,128)(2,1)}, u32[]{:S(2)}, u32[]{:S(2)}) collective-permute-start(bf16[768,256]{1,0:T(8,128)(2,1)S(1)} %pad_maximum_fusion.2.refs_4_.refs_0_), channel_id=1, source_target_pairs={{0,1},{8,9},{16,17},{24,25},{32,33},{40,41},{48,49},{56,57},{64,65... | collective-permute-start | bytes 1179656 | tf_op jit(solution)/shard_map/ppermute | solution.py:44
  21.3 12.9 %collective-permute-start.9 = (bf16[512,384]{1,0:T(8,128)(2,1)S(1)}, bf16[512,384]{1,0:T(8,128)(2,1)S(1)}, u32[]{:S(2)}, u32[]{:S(2)}) collective-permute-start(bf16[512,384]{1,0:T(8,128)(2,1)S(1)} %pad_maximum_fusion.refs_0_), channel_id=1, source_target_pairs={{0,8},{8,0},{16,24},{24,16},{32,40},{40,32},{48,56},{56,48},{64,72... | collective-permute-start | bytes 1179656 | tf_op jit(solution)/shard_map/ppermute | solution.py:44
  26.0 10.3 %collective-permute-start.11 = (bf16[512,384]{1,0:T(8,128)(2,1)}, bf16[512,384]{1,0:T(8,128)(2,1)}, u32[]{:S(2)}, u32[]{:S(2)}) collective-permute-start(bf16[512,384]{1,0:T(8,128)(2,1)} %pad_maximum_fusion.1.refs_2_), channel_id=1, source_target_pairs={{0,8},{8,0},{16,24},{24,16},{32,40},{40,32},{48,56},{56,48},{64,72... | collective-permute-start | bytes 1179656 | tf_op jit(solution)/shard_map/ppermute | solution.py:44
  28.7 7.7 %collective-permute-start.13 = (bf16[768,256]{1,0:T(8,128)(2,1)S(1)}, bf16[768,256]{1,0:T(8,128)(2,1)}, u32[]{:S(2)}, u32[]{:S(2)}) collective-permute-start(bf16[768,256]{1,0:T(8,128)(2,1)S(1)} %pad_maximum_fusion.2.refs_4_.refs_0_), channel_id=1, source_target_pairs={{0,8},{8,0},{16,24},{24,16},{32,40},{40,32},{48,56},{56,48},{64,72... | collective-permute-start | bytes 1179656 | tf_op jit(solution)/shard_map/ppermute | solution.py:44
  33.1 3.2 %collective-permute-start.10 = (bf16[512,384]{1,0:T(8,128)(2,1)}, bf16[512,384]{1,0:T(8,128)(2,1)}, u32[]{:S(2)}, u32[]{:S(2)}) collective-permute-start(bf16[512,384]{1,0:T(8,128)(2,1)} %collective-permute-done.6.refs_1_), channel_id=1, source_target_pairs={{0,8},{8,0},{16,24},{24,16},{32,40},{40,32},{48,56},{56,48},{64,72... | collective-permute-start | bytes 1179656 | tf_op jit(solution)/shard_map/ppermute | solution.py:44
  34.2 2.3 %collective-permute-start.12 = (bf16[512,384]{1,0:T(8,128)(2,1)}, bf16[512,384]{1,0:T(8,128)(2,1)}, u32[]{:S(2)}, u32[]{:S(2)}) collective-permute-start(bf16[512,384]{1,0:T(8,128)(2,1)} %collective-permute-done.7.refs_3_), channel_id=1, source_target_pairs={{0,8},{8,0},{16,24},{24,16},{32,40},{40,32},{48,56},{56,48},{64,72... | collective-permute-start | bytes 1179656 | tf_op jit(solution)/shard_map/ppermute | solution.py:44
  34.2 0.7 copy-start.5
  35.0 2.2 %collective-permute-start.14 = (bf16[768,256]{1,0:T(8,128)(2,1)}, bf16[768,256]{1,0:T(8,128)(2,1)}, u32[]{:S(2)}, u32[]{:S(2)}) collective-permute-start(bf16[768,256]{1,0:T(8,128)(2,1)} %collective-permute-done.8.refs_5_.refs_1_), channel_id=1, source_target_pairs={{0,8},{8,0},{16,24},{24,16},{32,40},{40,32},{48,56},{56,48},{64,72... | collective-permute-start | bytes 1179656 | tf_op jit(solution)/shard_map/ppermute | solution.py:44
  37.2 1.0 copy-start.2
  38.2 1.0 copy-start.6
  45.1 4.1 %collective-permute-start.17 = (bf16[2,2176]{1,0:T(2,128)(2,1)S(1)}, bf16[2,2176]{1,0:T(2,128)(2,1)S(1)}, u32[]{:S(2)}, u32[]{:S(2)}) collective-permute-start(bf16[2,2176]{1,0:T(2,128)(2,1)S(1)} %get-tuple-element.66), channel_id=1, source_target_pairs={{0,2},{8,10},{16,18},{24,26},{32,34},{40,42},{48,50},{56,58},{64,6... | collective-permute-start | bytes 26120 | tf_op jit(solution)/shard_map/ppermute | solution.py:44
  47.2 3.7 %collective-permute-start.16 = (bf16[2,2176]{1,0:T(2,128)(2,1)S(1)}, bf16[2,2176]{1,0:T(2,128)(2,1)S(1)}, u32[]{:S(2)}, u32[]{:S(2)}) collective-permute-start(bf16[2,2176]{1,0:T(2,128)(2,1)S(1)} %get-tuple-element.66), channel_id=1, source_target_pairs={{0,3},{8,11},{16,19},{24,27},{32,35},{40,43},{48,51},{56,59},{64,6... | collective-permute-start | bytes 26120 | tf_op jit(solution)/shard_map/ppermute | solution.py:44
  48.0 2.9 %collective-permute-start.15 = (bf16[2,2176]{1,0:T(2,128)(2,1)S(1)}, bf16[2,2176]{1,0:T(2,128)(2,1)S(1)}, u32[]{:S(2)}, u32[]{:S(2)}) collective-permute-start(bf16[2,2176]{1,0:T(2,128)(2,1)S(1)} %get-tuple-element.66), channel_id=1, source_target_pairs={{0,1},{8,9},{16,17},{24,25},{32,33},{40,41},{48,49},{56,57},{64,65... | collective-permute-start | bytes 26120 | tf_op jit(solution)/shard_map/ppermute | solution.py:44
  51.0 4.8 %collective-permute-start.20 = (bf16[8,2176]{1,0:T(8,128)(2,1)S(1)}, bf16[8,2176]{1,0:T(8,128)(2,1)S(1)}, u32[]{:S(2)}, u32[]{:S(2)}) collective-permute-start(bf16[8,2176]{1,0:T(8,128)(2,1)S(1)} %pad_maximum_fusion.8), channel_id=1, source_target_pairs={{0,4},{8,12},{16,20},{24,28},{32,36},{40,44},{48,52},{56,60},{64,6... | collective-permute-start | bytes 104456 | tf_op jit(solution)/shard_map/ppermute | solution.py:44
  51.1 4.7 %collective-permute-start.19 = (bf16[8,2176]{1,0:T(8,128)(2,1)S(1)}, bf16[8,2176]{1,0:T(8,128)(2,1)S(1)}, u32[]{:S(2)}, u32[]{:S(2)}) collective-permute-start(bf16[8,2176]{1,0:T(8,128)(2,1)S(1)} %pad_maximum_fusion.8), channel_id=1, source_target_pairs={{0,68},{8,76},{16,84},{24,92},{32,100},{40,108},{48,116},{56,124},... | collective-permute-start | bytes 104456 | tf_op jit(solution)/shard_map/ppermute | solution.py:44
  52.7 3.1 %collective-permute-start.18 = (bf16[8,2176]{1,0:T(8,128)(2,1)S(1)}, bf16[8,2176]{1,0:T(8,128)(2,1)S(1)}, u32[]{:S(2)}, u32[]{:S(2)}) collective-permute-start(bf16[8,2176]{1,0:T(8,128)(2,1)S(1)} %pad_maximum_fusion.8), channel_id=1, source_target_pairs={{0,64},{8,72},{16,80},{24,88},{32,96},{40,104},{48,112},{56,120},{... | collective-permute-start | bytes 104456 | tf_op jit(solution)/shard_map/ppermute | solution.py:44
  55.8 7.9 %collective-permute-start.23 = (bf16[32,2176]{1,0:T(8,128)(2,1)S(1)}, bf16[32,2176]{1,0:T(8,128)(2,1)S(1)}, u32[]{:S(2)}, u32[]{:S(2)}) collective-permute-start(bf16[32,2176]{1,0:T(8,128)(2,1)S(1)} %pad_maximum_fusion.7.refs_0_), channel_id=1, source_target_pairs={{0,32},{8,40},{16,48},{24,56},{32,0},{40,8},{48,16},{56,24},{64,96... | collective-permute-start | bytes 417800 | tf_op jit(solution)/shard_map/ppermute | solution.py:44
  59.5 6.9 %collective-permute-start.22 = (bf16[32,2176]{1,0:T(8,128)(2,1)S(1)}, bf16[32,2176]{1,0:T(8,128)(2,1)S(1)}, u32[]{:S(2)}, u32[]{:S(2)}) collective-permute-start(bf16[32,2176]{1,0:T(8,128)(2,1)S(1)} %pad_maximum_fusion.7.refs_0_), channel_id=1, source_target_pairs={{0,48},{8,56},{16,32},{24,40},{32,16},{40,24},{48,0},{56,8},{64,11... | collective-permute-start | bytes 417800 | tf_op jit(solution)/shard_map/ppermute | solution.py:44
  59.9 9.0 %collective-permute-start.21 = (bf16[32,2176]{1,0:T(8,128)(2,1)S(1)}, bf16[32,2176]{1,0:T(8,128)(2,1)S(1)}, u32[]{:S(2)}, u32[]{:S(2)}) collective-permute-start(bf16[32,2176]{1,0:T(8,128)(2,1)S(1)} %pad_maximum_fusion.7.refs_0_), channel_id=1, source_target_pairs={{0,16},{8,24},{16,0},{24,8},{32,48},{40,56},{48,32},{56,40},{64,80... | collective-permute-start | bytes 417800 | tf_op jit(solution)/shard_map/ppermute | solution.py:44
  60.2 8.7 %collective-permute-start.24 = (bf16[32,2176]{1,0:T(8,128)(2,1)S(1)}, bf16[32,2176]{1,0:T(8,128)(2,1)S(1)}, u32[]{:S(2)}, u32[]{:S(2)}) collective-permute-start(bf16[32,2176]{1,0:T(8,128)(2,1)S(1)} %pad_maximum_fusion.7.refs_0_), channel_id=1, source_target_pairs={{0,8},{8,0},{16,24},{24,16},{32,40},{40,32},{48,56},{56,48},{64,72... | collective-permute-start | bytes 417800 | tf_op jit(solution)/shard_map/ppermute | solution.py:44
  63.7 5.3 %collective-permute-start.27 = (bf16[32,2176]{1,0:T(8,128)(2,1)S(1)}, bf16[32,2176]{1,0:T(8,128)(2,1)S(1)}, u32[]{:S(2)}, u32[]{:S(2)}) collective-permute-start(bf16[32,2176]{1,0:T(8,128)(2,1)S(1)} %collective-permute-done.23.refs_3_), channel_id=1, source_target_pairs={{0,8},{8,0},{16,24},{24,16},{32,40},{40,32},{48,56},{56,48},{64,72... | collective-permute-start | bytes 417800 | tf_op jit(solution)/shard_map/ppermute | solution.py:44
  66.4 3.5 %collective-permute-start.26 = (bf16[32,2176]{1,0:T(8,128)(2,1)S(1)}, bf16[32,2176]{1,0:T(8,128)(2,1)S(1)}, u32[]{:S(2)}, u32[]{:S(2)}) collective-permute-start(bf16[32,2176]{1,0:T(8,128)(2,1)S(1)} %collective-permute-done.22.refs_2_), channel_id=1, source_target_pairs={{0,8},{8,0},{16,24},{24,16},{32,40},{40,32},{48,56},{56,48},{64,72... | collective-permute-start | bytes 417800 | tf_op jit(solution)/shard_map/ppermute | solution.py:44
  68.9 1.4 collective-permute-start.25
  74.2 3.5 %collective-permute-start.28 = (f32[8,2048]{1,0:T(8,128)S(1)}, f32[8,2048]{1,0:T(8,128)S(1)}, u32[]{:S(2)}, u32[]{:S(2)}) collective-permute-start(f32[8,2048]{1,0:T(8,128)S(1)} %get-tuple-element.70), channel_id=1, source_target_pairs={{0,16},{8,24},{16,0},{24,8},{32,48},{40,56},{48,32},{56,40},{64,80... | collective-permute-start | bytes 196616 | tf_op jit(solution)/shard_map/ppermute | solution.py:44
  74.3 4.3 %collective-permute-start.29 = (f32[8,2048]{1,0:T(8,128)S(1)}, f32[8,2048]{1,0:T(8,128)S(1)}, u32[]{:S(2)}, u32[]{:S(2)}) collective-permute-start(f32[8,2048]{1,0:T(8,128)S(1)} %get-tuple-element.71), channel_id=1, source_target_pairs={{0,48},{8,56},{16,32},{24,40},{32,16},{40,24},{48,0},{56,8},{64,11... | collective-permute-start | bytes 196616 | tf_op jit(solution)/shard_map/ppermute | solution.py:44
  75.9 4.6 %collective-permute-start.30 = (f32[8,2048]{1,0:T(8,128)S(1)}, f32[8,2048]{1,0:T(8,128)S(1)}, u32[]{:S(2)}, u32[]{:S(2)}) collective-permute-start(f32[8,2048]{1,0:T(8,128)S(1)} %get-tuple-element.72), channel_id=1, source_target_pairs={{0,32},{8,40},{16,48},{24,56},{32,0},{40,8},{48,16},{56,24},{64,96... | collective-permute-start | bytes 196616 | tf_op jit(solution)/shard_map/ppermute | solution.py:44
  80.5 3.6 %collective-permute-start.31 = (f32[8,2048]{1,0:T(8,128)S(1)}, f32[8,2048]{1,0:T(8,128)S(1)}, u32[]{:S(2)}, u32[]{:S(2)}) collective-permute-start(f32[8,2048]{1,0:T(8,128)S(1)} %add_add_fusion.refs_0_), channel_id=1, source_target_pairs={{0,64},{8,72},{16,80},{24,88},{32,96},{40,104},{48,112},{56,120},{... | collective-permute-start | bytes 196616 | tf_op jit(solution)/shard_map/ppermute | solution.py:44
  81.9 7.8 %collective-permute-start.32 = (bf16[512,1024]{1,0:T(8,128)(2,1)S(1)}, bf16[512,1024]{1,0:T(8,128)(2,1)S(1)}, u32[]{:S(2)}, u32[]{:S(2)}) collective-permute-start(bf16[512,1024]{1,0:T(8,128)(2,1)S(1)} %copy-done), channel_id=1, source_target_pairs={{0,8},{8,0},{16,24},{24,16},{32,40},{40,32},{48,56},{56,48},{64,72... | collective-permute-start | bytes 3145736 | tf_op jit(solution)/shard_map/ppermute | solution.py:44
  87.1 5.0 %collective-permute-start.33 = (bf16[512,1024]{1,0:T(8,128)(2,1)S(1)}, bf16[512,1024]{1,0:T(8,128)(2,1)S(1)}, u32[]{:S(2)}, u32[]{:S(2)}) collective-permute-start(bf16[512,1024]{1,0:T(8,128)(2,1)S(1)} %get-tuple-element.77.send), channel_id=1, source_target_pairs={{0,8},{8,0},{16,24},{24,16},{32,40},{40,32},{48,56},{56,48},{64,72... | collective-permute-start | bytes 3145736 | tf_op jit(solution)/shard_map/ppermute | solution.py:44
  93.6 6.3 %copy-start.3 = (bf16[512,384]{1,0:T(8,128)(2,1)S(1)}, bf16[512,384]{1,0:T(8,128)(2,1)}, u32[]{:S(2)}) copy-start(bf16[512,384]{1,0:T(8,128)(2,1)} %copy-done.1) | copy-start | bytes 1179652
  93.6 6.3 %copy-start.7 = (bf16[512,384]{1,0:T(8,128)(2,1)S(1)}, bf16[512,384]{1,0:T(8,128)(2,1)}, u32[]{:S(2)}) copy-start(bf16[512,384]{1,0:T(8,128)(2,1)} %copy-done.5) | copy-start | bytes 1179652
  93.6 17.2 %collective-permute-start.34 = (bf16[512,640]{1,0:T(8,128)(2,1)S(1)}, bf16[512,640]{1,0:T(8,128)(2,1)S(1)}, u32[]{:S(2)}, u32[]{:S(2)}) collective-permute-start(bf16[512,640]{1,0:T(8,128)(2,1)S(1)} %first_sent.1), channel_id=1, source_target_pairs={{0,68},{8,76},{16,84},{24,92},{32,100},{40,108},{48,116},{56,124},... | collective-permute-start | bytes 1966088 | tf_op jit(solution)/shard_map/ppermute | solution.py:44
  96.6 11.2 %collective-permute-start.35 = (bf16[256,384]{1,0:T(8,128)(2,1)S(1)}, bf16[256,384]{1,0:T(8,128)(2,1)S(1)}, u32[]{:S(2)}, u32[]{:S(2)}) collective-permute-start(bf16[256,384]{1,0:T(8,128)(2,1)S(1)} %get-tuple-element.80), channel_id=1, source_target_pairs={{0,1},{8,9},{16,17},{24,25},{32,33},{40,41},{48,49},{56,57},{64,65... | collective-permute-start | bytes 589832 | tf_op jit(solution)/shard_map/ppermute | solution.py:44
  96.7 11.1 %collective-permute-start.36 = (bf16[256,384]{1,0:T(8,128)(2,1)S(1)}, bf16[256,384]{1,0:T(8,128)(2,1)S(1)}, u32[]{:S(2)}, u32[]{:S(2)}) collective-permute-start(bf16[256,384]{1,0:T(8,128)(2,1)S(1)} %get-tuple-element.81), channel_id=1, source_target_pairs={{0,3},{8,11},{16,19},{24,27},{32,35},{40,43},{48,51},{56,59},{64,6... | collective-permute-start | bytes 589832 | tf_op jit(solution)/shard_map/ppermute | solution.py:44
  98.5 9.6 %collective-permute-start.37 = (bf16[256,384]{1,0:T(8,128)(2,1)S(1)}, bf16[256,384]{1,0:T(8,128)(2,1)S(1)}, u32[]{:S(2)}, u32[]{:S(2)}) collective-permute-start(bf16[256,384]{1,0:T(8,128)(2,1)S(1)} %get-tuple-element.82), channel_id=1, source_target_pairs={{0,2},{8,10},{16,18},{24,26},{32,34},{40,42},{48,50},{56,58},{64,6... | collective-permute-start | bytes 589832 | tf_op jit(solution)/shard_map/ppermute | solution.py:44
  111.1 5.6 %collective-permute-start.38 = (bf16[128,640]{1,0:T(8,128)(2,1)S(1)}, bf16[128,640]{1,0:T(8,128)(2,1)S(1)}, u32[]{:S(2)}, u32[]{:S(2)}) collective-permute-start(bf16[128,640]{1,0:T(8,128)(2,1)S(1)} %get-tuple-element.96), channel_id=1, source_target_pairs={{0,1},{8,9},{16,17},{24,25},{32,33},{40,41},{48,49},{56,57},{64,65... | collective-permute-start | bytes 491528 | tf_op jit(solution)/shard_map/ppermute | solution.py:44
  111.4 9.4 %collective-permute-start.40 = (bf16[128,640]{1,0:T(8,128)(2,1)S(1)}, bf16[128,640]{1,0:T(8,128)(2,1)S(1)}, u32[]{:S(2)}, u32[]{:S(2)}) collective-permute-start(bf16[128,640]{1,0:T(8,128)(2,1)S(1)} %get-tuple-element.97), channel_id=1, source_target_pairs={{0,2},{8,10},{16,18},{24,26},{32,34},{40,42},{48,50},{56,58},{64,6... | collective-permute-start | bytes 491528 | tf_op jit(solution)/shard_map/ppermute | solution.py:44
  114.3 9.3 %collective-permute-start.39 = (bf16[128,640]{1,0:T(8,128)(2,1)S(1)}, bf16[128,640]{1,0:T(8,128)(2,1)S(1)}, u32[]{:S(2)}, u32[]{:S(2)}) collective-permute-start(bf16[128,640]{1,0:T(8,128)(2,1)S(1)} %get-tuple-element.98), channel_id=1, source_target_pairs={{0,3},{8,11},{16,19},{24,27},{32,35},{40,43},{48,51},{56,59},{64,6... | collective-permute-start | bytes 491528 | tf_op jit(solution)/shard_map/ppermute | solution.py:44
  115.4 8.6 %collective-permute-start.44 = (bf16[128,384]{1,0:T(8,128)(2,1)S(1)}, bf16[128,384]{1,0:T(8,128)(2,1)S(1)}, u32[]{:S(2)}, u32[]{:S(2)}) collective-permute-start(bf16[128,384]{1,0:T(8,128)(2,1)S(1)} %slice.62), channel_id=1, source_target_pairs={{0,68},{8,76},{16,84},{24,92},{32,100},{40,108},{48,116},{56,124},... | collective-permute-start | bytes 294920 | tf_op jit(solution)/shard_map/ppermute | solution.py:44
  123.7 3.9 %collective-permute-start.41 = (bf16[128,512]{1,0:T(8,128)(2,1)S(1)}, bf16[128,512]{1,0:T(8,128)(2,1)S(1)}, u32[]{:S(2)}, u32[]{:S(2)}) collective-permute-start(bf16[128,512]{1,0:T(8,128)(2,1)S(1)} %fusion.2), channel_id=1, source_target_pairs={{0,64},{8,72},{16,80},{24,88},{32,96},{40,104},{48,112},{56,120},{... | collective-permute-start | bytes 393224 | tf_op jit(solution)/shard_map/ppermute | solution.py:44
  124.0 4.6 %collective-permute-start.45 = (bf16[128,512]{1,0:T(8,128)(2,1)S(1)}, bf16[128,512]{1,0:T(8,128)(2,1)S(1)}, u32[]{:S(2)}, u32[]{:S(2)}) collective-permute-start(bf16[128,512]{1,0:T(8,128)(2,1)S(1)} %fusion.3), channel_id=1, source_target_pairs={{0,16},{8,24},{16,0},{24,8},{32,48},{40,56},{48,32},{56,40},{64,80... | collective-permute-start | bytes 393224 | tf_op jit(solution)/shard_map/ppermute | solution.py:44
  127.7 3.9 %collective-permute-start.42 = (bf16[128,512]{1,0:T(8,128)(2,1)S(1)}, bf16[128,512]{1,0:T(8,128)(2,1)S(1)}, u32[]{:S(2)}, u32[]{:S(2)}) collective-permute-start(bf16[128,512]{1,0:T(8,128)(2,1)S(1)} %fusion.6), channel_id=1, source_target_pairs={{0,16},{8,24},{16,0},{24,8},{32,48},{40,56},{48,32},{56,40},{64,80... | collective-permute-start | bytes 393224 | tf_op jit(solution)/shard_map/ppermute | solution.py:44
  128.6 5.1 %collective-permute-start.46 = (bf16[128,512]{1,0:T(8,128)(2,1)S(1)}, bf16[128,512]{1,0:T(8,128)(2,1)S(1)}, u32[]{:S(2)}, u32[]{:S(2)}) collective-permute-start(bf16[128,512]{1,0:T(8,128)(2,1)S(1)} %fusion.7), channel_id=1, source_target_pairs={{0,48},{8,56},{16,32},{24,40},{32,16},{40,24},{48,0},{56,8},{64,11... | collective-permute-start | bytes 393224 | tf_op jit(solution)/shard_map/ppermute | solution.py:44
  131.7 6.4 %collective-permute-start.43 = (bf16[128,512]{1,0:T(8,128)(2,1)S(1)}, bf16[128,512]{1,0:T(8,128)(2,1)S(1)}, u32[]{:S(2)}, u32[]{:S(2)}) collective-permute-start(bf16[128,512]{1,0:T(8,128)(2,1)S(1)} %fusion.4), channel_id=1, source_target_pairs={{0,48},{8,56},{16,32},{24,40},{32,16},{40,24},{48,0},{56,8},{64,11... | collective-permute-start | bytes 393224 | tf_op jit(solution)/shard_map/ppermute | solution.py:44
  133.8 4.4 %collective-permute-start.47 = (bf16[128,512]{1,0:T(8,128)(2,1)S(1)}, bf16[128,512]{1,0:T(8,128)(2,1)S(1)}, u32[]{:S(2)}, u32[]{:S(2)}) collective-permute-start(bf16[128,512]{1,0:T(8,128)(2,1)S(1)} %fusion.5), channel_id=1, source_target_pairs={{0,64},{8,72},{16,80},{24,88},{32,96},{40,104},{48,112},{56,120},{... | collective-permute-start | bytes 393224 | tf_op jit(solution)/shard_map/ppermute | solution.py:44
  138.3 7.0 %collective-permute-start.48 = (bf16[128,1024]{1,0:T(8,128)(2,1)S(1)}, bf16[128,1024]{1,0:T(8,128)(2,1)S(1)}, u32[]{:S(2)}, u32[]{:S(2)}) collective-permute-start(bf16[128,1024]{1,0:T(8,128)(2,1)S(1)} %pad_maximum_fusion.3), channel_id=1, source_target_pairs={{0,8},{8,0},{16,24},{24,16},{32,40},{40,32},{48,56},{56,48},{64,72... | collective-permute-start | bytes 786440 | tf_op jit(solution)/shard_map/ppermute | solution.py:44

commit v11 on v9

--- a/solution.py
+++ b/solution.py
@@ -483,8 +483,10 @@
         compiler_params=params(10),
         name="users",
     )(where, *riding)
-    emb, users = lax.optimization_barrier((jnp.concatenate(four(emb, swap_y), axis=0), users))
+    emb = lax.optimization_barrier(jnp.concatenate(four(emb, swap_y), axis=0))
     emb_pieces = four(emb, swap_z)
+    arrived, users = lax.optimization_barrier((emb_pieces[1:], users))
+    emb_pieces = emb_pieces[:1] + arrived
     emb_pieces = emb_pieces + [swap_core(p) for p in emb_pieces]
 
     items, people = 128 * items_here, 16 * users_here

time: 144 us -> 144 us (level)
  waiting for transfers between devices: 36.1 us -> 38.5 us
  starting transfers between devices: 72 us -> 70 us
    ppermute x49, waiting for transfers between devices: 36.1 us -> 38.5 us  [move(): return lax.ppermute(value, AXES, perm)]
    ppermute x49, starting transfers between devices: 72 us -> 70 us  [move(): return lax.ppermute(value, AXES, perm)]
  transfers between devices with their start and end apart: 49 -> 49, of which waited for: 26 -> 28; matrix products, arithmetic and copies ran while one was open for 2% -> 2% of each run, Pallas kernels for 10% -> 10%
where the time goes in v11:
time: 144 us
  starting transfers between devices  70 us (49%)
  waiting for transfers between devices  38.5 us (27%)
  Pallas kernels  25.7 us (18%)
  local copies, waits for them, and re-layouts  4.77 us (3%)
  other arithmetic  3.59 us (2%)
    ppermute x49, starting transfers between devices, move(): return lax.ppermute(value, AXES, perm)  70 us
    ppermute x49, waiting for transfers between devices, move(): return lax.ppermute(value, AXES, perm)  38.5 us
    pallas_call x1, Pallas kernels, on_device(): pl.pallas_call(context_kernel, out_shape=shaped((tokens, head), BF16), in...  6.03 us
    pallas_call x1, Pallas kernels, on_device(): pl.pallas_call(functools.partial(forward_kernel, items_here), out_shape=(...  5.95 us
    unnamed x26, local copies, waits for them, and re-layouts  4.72 us
    pallas_call x3, Pallas kernels, blocks(): pl.pallas_call(functools.partial(blocks_kernel, first_blocks, second_bloc...  4.47 us
    pallas_call x1, Pallas kernels, on_device(): pl.pallas_call(functools.partial(loss_kernel, users_here, items_here), ou...  3.94 us
    pallas_call x1, Pallas kernels, on_device(): pl.pallas_call(functools.partial(residual_kernel, 8 * people), out_shape=...  2.95 us
  transfers between devices with their start and end apart: 49, of which 28 were waited for; matrix products, arithmetic and copies ran while one was open for 2% of the time, Pallas kernels for 10%

profile of v11, /device:TPU:1, one launch (start us, length us, event | category | flops | bytes accessed | tf_op | source)
XLA Modules:
  0.0 143.6 jit_solution(9741931114563719627)
XLA Ops:
  0.7 1.2 copy-done.8
  2.7 3.6 %collective-permute-start = (bf16[128,384]{1,0:T(8,128)(2,1)S(1)}, bf16[128,384]{1,0:T(8,128)(2,1)S(1)}, u32[]{:S(2)}, u32[]{:S(2)}) collective-permute-start(bf16[128,384]{1,0:T(8,128)(2,1)S(1)} %get-tuple-element.52), channel_id=1, source_target_pairs={{0,68},{8,76},{16,84},{24,92},{32,100},{40,108},{48,116},{56,124},... | collective-permute-start | bytes 294920 | tf_op jit(solution)/shard_map/ppermute | solution.py:44
  6.3 1.2 collective-permute-start.1
  7.5 1.8 %collective-permute-start.2 = (bf16[192,256]{1,0:T(8,128)(2,1)S(1)}, bf16[192,256]{1,0:T(8,128)(2,1)S(1)}, u32[]{:S(2)}, u32[]{:S(2)}) collective-permute-start(bf16[192,256]{1,0:T(8,128)(2,1)S(1)} %get-tuple-element.54), channel_id=1, source_target_pairs={{0,3},{8,11},{16,19},{24,27},{32,35},{40,43},{48,51},{56,59},{64,6... | collective-permute-start | bytes 294920 | tf_op jit(solution)/shard_map/ppermute | solution.py:44
  9.8 2.4 %collective-permute-done.2 = bf16[192,256]{1,0:T(8,128)(2,1)S(1)} collective-permute-done((bf16[192,256]{1,0:T(8,128)(2,1)S(1)}, bf16[192,256]{1,0:T(8,128)(2,1)S(1)}, u32[]{:S(2)}, u32[]{:S(2)}) %collective-permute-start.2) | collective-permute-done | bytes 98336 | tf_op jit(solution)/shard_map/ppermute | solution.py:44
  12.3 1.9 %collective-permute-start.4 = (bf16[256,384]{1,0:T(8,128)(2,1)S(1)}, bf16[256,384]{1,0:T(8,128)(2,1)S(1)}, u32[]{:S(2)}, u32[]{:S(2)}) collective-permute-start(bf16[256,384]{1,0:T(8,128)(2,1)S(1)} %pad_maximum_fusion.5), channel_id=1, source_target_pairs={{0,3},{8,11},{16,19},{24,27},{32,35},{40,43},{48,51},{56,59},{64,6... | collective-permute-start | bytes 589832 | tf_op jit(solution)/shard_map/ppermute | solution.py:44
  14.6 2.2 %collective-permute-done.3 = bf16[256,384]{1,0:T(8,128)(2,1)S(1)} collective-permute-done((bf16[256,384]{1,0:T(8,128)(2,1)S(1)}, bf16[256,384]{1,0:T(8,128)(2,1)S(1)}, u32[]{:S(2)}, u32[]{:S(2)}) %collective-permute-start.3) | collective-permute-done | bytes 196640 | tf_op jit(solution)/shard_map/ppermute | solution.py:44
  16.9 1.2 collective-permute-done.4
  18.9 1.3 collective-permute-done.5
  20.3 0.9 collective-permute-start.6
  21.5 4.5 %collective-permute-start.9 = (bf16[512,384]{1,0:T(8,128)(2,1)S(1)}, bf16[512,384]{1,0:T(8,128)(2,1)S(1)}, u32[]{:S(2)}, u32[]{:S(2)}) collective-permute-start(bf16[512,384]{1,0:T(8,128)(2,1)S(1)} %pad_maximum_fusion.refs_0_), channel_id=1, source_target_pairs={{0,8},{8,0},{16,24},{24,16},{32,40},{40,32},{48,56},{56,48},{64,72... | collective-permute-start | bytes 1179656 | tf_op jit(solution)/shard_map/ppermute | solution.py:44
  26.3 2.5 %collective-permute-done.6.refs_1_ = bf16[512,384]{1,0:T(8,128)(2,1)} collective-permute-done((bf16[512,384]{1,0:T(8,128)(2,1)S(1)}, bf16[512,384]{1,0:T(8,128)(2,1)}, u32[]{:S(2)}, u32[]{:S(2)}) %collective-permute-start.6) | collective-permute-done | bytes 393248 | tf_op jit(solution)/shard_map/ppermute | solution.py:44
  28.8 4.4 %collective-permute-start.13 = (bf16[768,256]{1,0:T(8,128)(2,1)S(1)}, bf16[768,256]{1,0:T(8,128)(2,1)}, u32[]{:S(2)}, u32[]{:S(2)}) collective-permute-start(bf16[768,256]{1,0:T(8,128)(2,1)S(1)} %pad_maximum_fusion.2.refs_4_.refs_0_), channel_id=1, source_target_pairs={{0,8},{8,0},{16,24},{24,16},{32,40},{40,32},{48,56},{56,48},{64,72... | collective-permute-start | bytes 1179656 | tf_op jit(solution)/shard_map/ppermute | solution.py:44
  33.3 1.1 collective-permute-start.10
  37.3 1.0 copy-done.2
  38.3 1.0 copy-done.6
  39.3 5.9 %forward.1 = (f32[512,2048]{1,0:T(8,128)S(1)}, f32[512,1]{1,0:T(8,128)S(1)}, f32[2,2048]{1,0:T(2,128)S(1)}, bf16[2,2176]{1,0:T(2,128)(2,1)S(1)}) custom-call(s32[18]{0:T(128)S(1)} %pad_add_fusion.1.ints, bf16[512,1024]{1,0:T(8,128)(2,1)S(1)} %copy-done, bf16[512,2048]{1,0:T(8,128)(2,1)S(1)} %hold.1.residual, f32[1,2048]{1,0:T(1,128)S(1)} %bitcast.7, ...), custom_call_target="tpu_custom_call" | custom-call | tf_op jit(solution)/shard_map/forward/pallas_call | solution.py:457
  45.3 2.1 %collective-permute-start.17 = (bf16[2,2176]{1,0:T(2,128)(2,1)S(1)}, bf16[2,2176]{1,0:T(2,128)(2,1)S(1)}, u32[]{:S(2)}, u32[]{:S(2)}) collective-permute-start(bf16[2,2176]{1,0:T(2,128)(2,1)S(1)} %get-tuple-element.68), channel_id=1, source_target_pairs={{0,2},{8,10},{16,18},{24,26},{32,34},{40,42},{48,50},{56,58},{64,6... | collective-permute-start | bytes 26120 | tf_op jit(solution)/shard_map/ppermute | solution.py:44
  47.4 0.9 collective-permute-start.16
  48.2 1.2 collective-permute-done.17
  49.4 1.7 %collective-permute-done.16 = bf16[2,2176]{1,0:T(2,128)(2,1)S(1)} collective-permute-done((bf16[2,2176]{1,0:T(2,128)(2,1)S(1)}, bf16[2,2176]{1,0:T(2,128)(2,1)S(1)}, u32[]{:S(2)}, u32[]{:S(2)}) %collective-permute-start.16) | collective-permute-done | bytes 8736 | tf_op jit(solution)/shard_map/ppermute | solution.py:44
  51.2 1.6 %collective-permute-start.19 = (bf16[8,2176]{1,0:T(8,128)(2,1)S(1)}, bf16[8,2176]{1,0:T(8,128)(2,1)S(1)}, u32[]{:S(2)}, u32[]{:S(2)}) collective-permute-start(bf16[8,2176]{1,0:T(8,128)(2,1)S(1)} %pad_maximum_fusion.8), channel_id=1, source_target_pairs={{0,68},{8,76},{16,84},{24,92},{32,100},{40,108},{48,116},{56,124},... | collective-permute-start | bytes 104456 | tf_op jit(solution)/shard_map/ppermute | solution.py:44
  52.8 1.0 collective-permute-start.18
  53.9 1.7 %collective-permute-done.20 = bf16[8,2176]{1,0:T(8,128)(2,1)S(1)} collective-permute-done((bf16[8,2176]{1,0:T(8,128)(2,1)S(1)}, bf16[8,2176]{1,0:T(8,128)(2,1)S(1)}, u32[]{:S(2)}, u32[]{:S(2)}) %collective-permute-start.20) | collective-permute-done | bytes 34848 | tf_op jit(solution)/shard_map/ppermute | solution.py:44
  55.7 3.7 %collective-permute-start.23 = (bf16[32,2176]{1,0:T(8,128)(2,1)S(1)}, bf16[32,2176]{1,0:T(8,128)(2,1)S(1)}, u32[]{:S(2)}, u32[]{:S(2)}) collective-permute-start(bf16[32,2176]{1,0:T(8,128)(2,1)S(1)} %pad_maximum_fusion.7.refs_0_), channel_id=1, source_target_pairs={{0,32},{8,40},{16,48},{24,56},{32,0},{40,8},{48,16},{56,24},{64,96... | collective-permute-start | bytes 417800 | tf_op jit(solution)/shard_map/ppermute | solution.py:44
  60.1 2.1 %users.3.users_ref = bf16[128,2048]{1,0:T(8,128)(2,1)S(1)} custom-call(s32[4]{0:T(128)S(1)} %pad_add_fusion.where, bf16[768,256]{1,0:T(8,128)(2,1)S(1)} %pad_maximum_fusion.2.refs_4_.refs_0_, bf16[768,256]{1,0:T(8,128)(2,1)} %collective-permute-done.8.refs_5_.refs_1_, bf16[768,256]{1,0:T(8,128)(2,1)} %collective-permute-done.13.refs_10_.refs_2_, ...), custom_call_target="tpu_custom_call" | custom-call | tf_op jit(solution)/shard_map/users/pallas_call | solution.py:474
  62.2 3.8 %collective-permute-start.24 = (bf16[32,2176]{1,0:T(8,128)(2,1)S(1)}, bf16[32,2176]{1,0:T(8,128)(2,1)S(1)}, u32[]{:S(2)}, u32[]{:S(2)}) collective-permute-start(bf16[32,2176]{1,0:T(8,128)(2,1)S(1)} %pad_maximum_fusion.7.refs_0_), channel_id=1, source_target_pairs={{0,8},{8,0},{16,24},{24,16},{32,40},{40,32},{48,56},{56,48},{64,72... | collective-permute-start | bytes 417800 | tf_op jit(solution)/shard_map/ppermute | solution.py:44
  66.0 3.1 %collective-permute-start.25 = (bf16[32,2176]{1,0:T(8,128)(2,1)S(1)}, bf16[32,2176]{1,0:T(8,128)(2,1)S(1)}, u32[]{:S(2)}, u32[]{:S(2)}) collective-permute-start(bf16[32,2176]{1,0:T(8,128)(2,1)S(1)} %collective-permute-done.21.refs_1_), channel_id=1, source_target_pairs={{0,8},{8,0},{16,24},{24,16},{32,40},{40,32},{48,56},{56,48},{64,72... | collective-permute-start | bytes 417800 | tf_op jit(solution)/shard_map/ppermute | solution.py:44
  70.7 3.9 %loss.1 = (f32[8,2048]{1,0:T(8,128)S(1)}, f32[8,2048]{1,0:T(8,128)S(1)}, f32[8,2048]{1,0:T(8,128)S(1)}, f32[8,2048]{1,0:T(8,128)S(1)}, bf16[8,2048]{1,0:T(8,128)(2,1)}) custom-call(s32[4]{0:T(128)S(1)} %pad_add_fusion.where, f32[1,2048]{1,0:T(1,128)S(1)} %bitcast.8, bf16[128,2048]{1,0:T(8,128)(2,1)S(1)} %users.3.users_ref, ...), custom_call_target="tpu_custom_call" | custom-call | tf_op jit(solution)/shard_map/loss/pallas_call | solution.py:493
  74.6 1.8 %collective-permute-start.29 = (f32[8,2048]{1,0:T(8,128)S(1)}, f32[8,2048]{1,0:T(8,128)S(1)}, u32[]{:S(2)}, u32[]{:S(2)}) collective-permute-start(f32[8,2048]{1,0:T(8,128)S(1)} %get-tuple-element.75), channel_id=1, source_target_pairs={{0,48},{8,56},{16,32},{24,40},{32,16},{40,24},{48,0},{56,8},{64,11... | collective-permute-start | bytes 196616 | tf_op jit(solution)/shard_map/ppermute | solution.py:44
  76.5 1.4 collective-permute-start.30
  77.8 1.1 collective-permute-done.29
  79.0 2.1 %collective-permute-done.30 = f32[8,2048]{1,0:T(8,128)S(1)} collective-permute-done((f32[8,2048]{1,0:T(8,128)S(1)}, f32[8,2048]{1,0:T(8,128)S(1)}, u32[]{:S(2)}, u32[]{:S(2)}) %collective-permute-start.30) | collective-permute-done | bytes 65568 | tf_op jit(solution)/shard_map/ppermute | solution.py:44
  81.1 1.4 collective-permute-start.31
  82.5 2.3 %collective-permute-start.32 = (bf16[512,1024]{1,0:T(8,128)(2,1)S(1)}, bf16[512,1024]{1,0:T(8,128)(2,1)S(1)}, u32[]{:S(2)}, u32[]{:S(2)}) collective-permute-start(bf16[512,1024]{1,0:T(8,128)(2,1)S(1)} %copy-done), channel_id=1, source_target_pairs={{0,8},{8,0},{16,24},{24,16},{32,40},{40,32},{48,56},{56,48},{64,72... | collective-permute-start | bytes 3145736 | tf_op jit(solution)/shard_map/ppermute | solution.py:44
  84.8 2.9 %residual.1 = (bf16[512,2048]{1,0:T(8,128)(2,1)}, bf16[512,1024]{1,0:T(8,128)(2,1)S(1)}, bf16[512,1024]{1,0:T(8,128)(2,1)S(1)}, f32[1,2048]{1,0:T(1,128)}, f32[1,1]{1,0:T(1,128)}) custom-call(s32[4]{0:T(128)S(1)} %pad_add_fusion.where, s32[2]{0:T(128)S(1)} %copy-done.11, f32[512,2048]{1,0:T(8,128)S(1)} %get-tuple-element.65.stream, ...), custom_call_target="tpu_custom_call" | custom-call | tf_op jit(solution)/shard_map/residual/pallas_call | solution.py:508
  87.7 2.7 %collective-permute-start.33 = (bf16[512,1024]{1,0:T(8,128)(2,1)S(1)}, bf16[512,1024]{1,0:T(8,128)(2,1)S(1)}, u32[]{:S(2)}, u32[]{:S(2)}) collective-permute-start(bf16[512,1024]{1,0:T(8,128)(2,1)S(1)} %get-tuple-element.81.send), channel_id=1, source_target_pairs={{0,8},{8,0},{16,24},{24,16},{32,40},{40,32},{48,56},{56,48},{64,72... | collective-permute-start | bytes 3145736 | tf_op jit(solution)/shard_map/ppermute | solution.py:44
  90.4 2.3 %collective-permute-done.33.peer_grad = bf16[512,1024]{1,0:T(8,128)(2,1)S(1)} collective-permute-done((bf16[512,1024]{1,0:T(8,128)(2,1)S(1)}, bf16[512,1024]{1,0:T(8,128)(2,1)S(1)}, u32[]{:S(2)}, u32[]{:S(2)}) %collective-permute-start.33) | collective-permute-done | bytes 1048608 | tf_op jit(solution)/shard_map/ppermute | solution.py:44
  92.7 1.3 first_sent.1
  94.0 1.4 collective-permute-start.34
  95.4 1.6 %second_sent.1 = (bf16[256,512]{1,0:T(8,128)(2,1)S(1)}, bf16[256,512]{1,0:T(8,128)(2,1)S(1)}, bf16[256,512]{1,0:T(8,128)(2,1)S(1)}) custom-call(s32[4]{0:T(128)S(1)} %pad_add_fusion.where, bf16[512,1024]{1,0:T(8,128)(2,1)S(1)} %copy-done, bf16[512,1024]{1,0:T(8,128)(2,1)S(1)} %collective-permute-done.32.peer_context, ...), custom_call_target="tpu_custom_call" | custom-call | tf_op jit(solution)/shard_map/second_sent/pallas_call | solution.py:533
  97.1 1.8 %collective-permute-start.36 = (bf16[256,512]{1,0:T(8,128)(2,1)S(1)}, bf16[256,512]{1,0:T(8,128)(2,1)S(1)}, u32[]{:S(2)}, u32[]{:S(2)}) collective-permute-start(bf16[256,512]{1,0:T(8,128)(2,1)S(1)} %get-tuple-element.85), channel_id=1, source_target_pairs={{0,3},{8,11},{16,19},{24,27},{32,35},{40,43},{48,51},{56,59},{64,6... | collective-permute-start | bytes 786440 | tf_op jit(solution)/shard_map/ppermute | solution.py:44
  98.9 1.4 %collective-permute-start.37 = (bf16[256,512]{1,0:T(8,128)(2,1)S(1)}, bf16[256,512]{1,0:T(8,128)(2,1)S(1)}, u32[]{:S(2)}, u32[]{:S(2)}) collective-permute-start(bf16[256,512]{1,0:T(8,128)(2,1)S(1)} %get-tuple-element.86), channel_id=1, source_target_pairs={{0,2},{8,10},{16,18},{24,26},{32,34},{40,42},{48,50},{56,58},{64,6... | collective-permute-start | bytes 786440 | tf_op jit(solution)/shard_map/ppermute | solution.py:44
  100.4 6.0 %context.3 = bf16[512,1024]{1,0:T(8,128)(2,1)} custom-call(s32[4]{0:T(128)S(1)} %pad_add_fusion.where, bf16[512,1024]{1,0:T(8,128)(2,1)S(1)} %get-tuple-element.80.own_grad.keep, bf16[512,1024]{1,0:T(8,128)(2,1)S(1)} %get-tuple-element.81.send, bf16[512,384]{1,0:T(8,128)(2,1)S(1)} %copy-done.3, bf16[512,384]{1,0:T(8,128)(2,1)} %collective-permute-done.6.refs_1_, ...), custom_call_target="tpu_custom_call" | custom-call | tf_op jit(solution)/shard_map/context/pallas_call | solution.py:523
  106.4 1.6 %kept.1 = (f32[512,512]{1,0:T(8,128)S(1)}, f32[256,512]{1,0:T(8,128)S(1)}) custom-call(s32[4]{0:T(128)S(1)} %pad_add_fusion.where, bf16[512,1024]{1,0:T(8,128)(2,1)S(1)} %copy-done, bf16[512,1024]{1,0:T(8,128)(2,1)S(1)} %collective-permute-done.32.peer_context, bf16[512,1024]{1,0:T(8,128)(2,1)S(1)} %get-tuple-element.80.own_grad.keep, ...), custom_call_target="tpu_custom_call" | custom-call | tf_op jit(solution)/shard_map/kept/pallas_call | solution.py:533
  108.0 3.3 %collective-permute-done.37 = bf16[256,512]{1,0:T(8,128)(2,1)S(1)} collective-permute-done((bf16[256,512]{1,0:T(8,128)(2,1)S(1)}, bf16[256,512]{1,0:T(8,128)(2,1)S(1)}, u32[]{:S(2)}, u32[]{:S(2)}) %collective-permute-start.37) | collective-permute-done | bytes 262176 | tf_op jit(solution)/shard_map/ppermute | solution.py:44
  111.5 1.5 %collective-permute-start.44 = (bf16[128,512]{1,0:T(8,128)(2,1)S(1)}, bf16[128,512]{1,0:T(8,128)(2,1)S(1)}, u32[]{:S(2)}, u32[]{:S(2)}) collective-permute-start(bf16[128,512]{1,0:T(8,128)(2,1)S(1)} %slice.53), channel_id=1, source_target_pairs={{0,68},{8,76},{16,84},{24,92},{32,100},{40,108},{48,116},{56,124},... | collective-permute-start | bytes 393224 | tf_op jit(solution)/shard_map/ppermute | solution.py:44
  113.3 2.1 %collective-permute-start.40 = (bf16[128,512]{1,0:T(8,128)(2,1)S(1)}, bf16[128,512]{1,0:T(8,128)(2,1)S(1)}, u32[]{:S(2)}, u32[]{:S(2)}) collective-permute-start(bf16[128,512]{1,0:T(8,128)(2,1)S(1)} %get-tuple-element.103), channel_id=1, source_target_pairs={{0,2},{8,10},{16,18},{24,26},{32,34},{40,42},{48,50},{56,58},{64,6... | collective-permute-start | bytes 393224 | tf_op jit(solution)/shard_map/ppermute | solution.py:44
  115.5 1.7 %collective-permute-start.39 = (bf16[128,512]{1,0:T(8,128)(2,1)S(1)}, bf16[128,512]{1,0:T(8,128)(2,1)S(1)}, u32[]{:S(2)}, u32[]{:S(2)}) collective-permute-start(bf16[128,512]{1,0:T(8,128)(2,1)S(1)} %get-tuple-element.104), channel_id=1, source_target_pairs={{0,3},{8,11},{16,19},{24,27},{32,35},{40,43},{48,51},{56,59},{64,6... | collective-permute-start | bytes 393224 | tf_op jit(solution)/shard_map/ppermute | solution.py:44
  117.2 0.8 collective-permute-start.45
  118.0 1.2 collective-permute-done.40
  119.2 1.4 collective-permute-done.39
  121.5 0.9 collective-permute-start.46
  122.4 2.2 %collective-permute-done.41 = bf16[128,512]{1,0:T(8,128)(2,1)S(1)} collective-permute-done((bf16[128,512]{1,0:T(8,128)(2,1)S(1)}, bf16[128,512]{1,0:T(8,128)(2,1)S(1)}, u32[]{:S(2)}, u32[]{:S(2)}) %collective-permute-start.41) | collective-permute-done | bytes 131104 | tf_op jit(solution)/shard_map/ppermute | solution.py:44
  124.6 0.8 collective-permute-start.42
  125.4 1.1 collective-permute-done.46
  126.7 0.9 collective-permute-start.47
  127.6 1.2 collective-permute-done.42
  128.9 0.9 collective-permute-start.43
  129.8 1.0 collective-permute-done.47
  131.0 3.0 %collective-permute-done.43 = bf16[128,512]{1,0:T(8,128)(2,1)S(1)} collective-permute-done((bf16[128,512]{1,0:T(8,128)(2,1)S(1)}, bf16[128,512]{1,0:T(8,128)(2,1)S(1)}, u32[]{:S(2)}, u32[]{:S(2)}) %collective-permute-start.43) | collective-permute-done | bytes 131104 | tf_op jit(solution)/shard_map/ppermute | solution.py:44
  134.1 7.4 %collective-permute-start.48 = (bf16[128,1024]{1,0:T(8,128)(2,1)S(1)}, bf16[128,1024]{1,0:T(8,128)(2,1)S(1)}, u32[]{:S(2)}, u32[]{:S(2)}) collective-permute-start(bf16[128,1024]{1,0:T(8,128)(2,1)S(1)} %pad_maximum_fusion.3), channel_id=1, source_target_pairs={{0,8},{8,0},{16,24},{24,16},{32,40},{40,32},{48,56},{56,48},{64,72... | collective-permute-start | bytes 786440 | tf_op jit(solution)/shard_map/ppermute | solution.py:44
  141.5 1.2 collective-permute-done.48
  142.6 0.9 maximum_select_fusion
  (95 shorter events, 10.5 us)
Async XLA Ops:
  0.6 25.4 %copy-start.4 = (bf16[512,2048]{1,0:T(8,128)(2,1)S(1)}, bf16[512,2048]{1,0:T(8,128)(2,1)}, u32[]{:S(2)}) copy-start(bf16[512,2048]{1,0:T(8,128)(2,1)} %source.1) | copy-start | bytes 6291460
  0.6 1.2 copy-start.8
  1.8 0.8 copy-start.10
  2.7 6.7 %collective-permute-start = (bf16[128,384]{1,0:T(8,128)(2,1)S(1)}, bf16[128,384]{1,0:T(8,128)(2,1)S(1)}, u32[]{:S(2)}, u32[]{:S(2)}) collective-permute-start(bf16[128,384]{1,0:T(8,128)(2,1)S(1)} %get-tuple-element.52), channel_id=1, source_target_pairs={{0,68},{8,76},{16,84},{24,92},{32,100},{40,108},{48,116},{56,124},... | collective-permute-start | bytes 294920 | tf_op jit(solution)/shard_map/ppermute | solution.py:44
  6.3 3.5 %collective-permute-start.1 = (bf16[128,384]{1,0:T(8,128)(2,1)S(1)}, bf16[128,384]{1,0:T(8,128)(2,1)S(1)}, u32[]{:S(2)}, u32[]{:S(2)}) collective-permute-start(bf16[128,384]{1,0:T(8,128)(2,1)S(1)} %get-tuple-element.53), channel_id=1, source_target_pairs={{0,1},{8,9},{16,17},{24,25},{32,33},{40,41},{48,49},{56,57},{64,65... | collective-permute-start | bytes 294920 | tf_op jit(solution)/shard_map/ppermute | solution.py:44
  7.5 4.7 %collective-permute-start.2 = (bf16[192,256]{1,0:T(8,128)(2,1)S(1)}, bf16[192,256]{1,0:T(8,128)(2,1)S(1)}, u32[]{:S(2)}, u32[]{:S(2)}) collective-permute-start(bf16[192,256]{1,0:T(8,128)(2,1)S(1)} %get-tuple-element.54), channel_id=1, source_target_pairs={{0,3},{8,11},{16,19},{24,27},{32,35},{40,43},{48,51},{56,59},{64,6... | collective-permute-start | bytes 294920 | tf_op jit(solution)/shard_map/ppermute | solution.py:44
  12.2 4.6 %collective-permute-start.3 = (bf16[256,384]{1,0:T(8,128)(2,1)S(1)}, bf16[256,384]{1,0:T(8,128)(2,1)S(1)}, u32[]{:S(2)}, u32[]{:S(2)}) collective-permute-start(bf16[256,384]{1,0:T(8,128)(2,1)S(1)} %pad_maximum_fusion.4), channel_id=1, source_target_pairs={{0,1},{8,9},{16,17},{24,25},{32,33},{40,41},{48,49},{56,57},{64,65... | collective-permute-start | bytes 589832 | tf_op jit(solution)/shard_map/ppermute | solution.py:44
  12.3 5.8 %collective-permute-start.4 = (bf16[256,384]{1,0:T(8,128)(2,1)S(1)}, bf16[256,384]{1,0:T(8,128)(2,1)S(1)}, u32[]{:S(2)}, u32[]{:S(2)}) collective-permute-start(bf16[256,384]{1,0:T(8,128)(2,1)S(1)} %pad_maximum_fusion.5), channel_id=1, source_target_pairs={{0,3},{8,11},{16,19},{24,27},{32,35},{40,43},{48,51},{56,59},{64,6... | collective-permute-start | bytes 589832 | tf_op jit(solution)/shard_map/ppermute | solution.py:44
  14.2 6.0 %collective-permute-start.5 = (bf16[384,256]{1,0:T(8,128)(2,1)S(1)}, bf16[384,256]{1,0:T(8,128)(2,1)S(1)}, u32[]{:S(2)}, u32[]{:S(2)}) collective-permute-start(bf16[384,256]{1,0:T(8,128)(2,1)S(1)} %pad_maximum_fusion.6), channel_id=1, source_target_pairs={{0,68},{8,76},{16,84},{24,92},{32,100},{40,108},{48,116},{56,124},... | collective-permute-start | bytes 589832 | tf_op jit(solution)/shard_map/ppermute | solution.py:44
  16.9 9.3 %copy-start.1 = (bf16[512,384]{1,0:T(8,128)(2,1)}, bf16[512,384]{1,0:T(8,128)(2,1)S(1)}, u32[]{:S(2)}) copy-start(bf16[512,384]{1,0:T(8,128)(2,1)S(1)} %pad_maximum_fusion.refs_0_) | copy-start | bytes 1179652
  20.3 15.4 %copy-start.11 = (s32[2]{0:T(128)S(1)}, s32[2]{0:T(128)}, u32[]{:S(2)}) copy-start(s32[2]{0:T(128)} %lengths.1) | copy-start | bytes 28
  20.3 15.4 %copy-start.12 = (s32[8]{0:T(128)S(1)}, s32[8]{0:T(128)}, u32[]{:S(2)}) copy-start(s32[8]{0:T(128)} %param.14) | copy-start | bytes 100
  20.3 17.0 %copy-start = (bf16[512,1024]{1,0:T(8,128)(2,1)S(1)}, bf16[512,1024]{1,0:T(8,128)(2,1)}, u32[]{:S(2)}) copy-start(bf16[512,1024]{1,0:T(8,128)(2,1)} %own_context.5) | copy-start | bytes 3145732
  20.3 17.0 %copy-start.9 = (f32[2048]{0:T(1024)S(1)}, f32[2048]{0:T(1024)}, u32[]{:S(2)}) copy-start(f32[2048]{0:T(1024)} %param.12) | copy-start | bytes 24580
  20.3 8.5 %collective-permute-start.6 = (bf16[512,384]{1,0:T(8,128)(2,1)S(1)}, bf16[512,384]{1,0:T(8,128)(2,1)}, u32[]{:S(2)}, u32[]{:S(2)}) collective-permute-start(bf16[512,384]{1,0:T(8,128)(2,1)S(1)} %pad_maximum_fusion.refs_0_), channel_id=1, source_target_pairs={{0,3},{8,11},{16,19},{24,27},{32,35},{40,43},{48,51},{56,59},{64,6... | collective-permute-start | bytes 1179656 | tf_op jit(solution)/shard_map/ppermute | solution.py:44
  21.3 12.0 %collective-permute-start.7 = (bf16[512,384]{1,0:T(8,128)(2,1)}, bf16[512,384]{1,0:T(8,128)(2,1)}, u32[]{:S(2)}, u32[]{:S(2)}) collective-permute-start(bf16[512,384]{1,0:T(8,128)(2,1)} %pad_maximum_fusion.1.refs_2_), channel_id=1, source_target_pairs={{0,68},{8,76},{16,84},{24,92},{32,100},{40,108},{48,116},{56,124},... | collective-permute-start | bytes 1179656 | tf_op jit(solution)/shard_map/ppermute | solution.py:44
  21.5 11.8 %collective-permute-start.8 = (bf16[768,256]{1,0:T(8,128)(2,1)S(1)}, bf16[768,256]{1,0:T(8,128)(2,1)}, u32[]{:S(2)}, u32[]{:S(2)}) collective-permute-start(bf16[768,256]{1,0:T(8,128)(2,1)S(1)} %pad_maximum_fusion.2.refs_4_.refs_0_), channel_id=1, source_target_pairs={{0,1},{8,9},{16,17},{24,25},{32,33},{40,41},{48,49},{56,57},{64,65... | collective-permute-start | bytes 1179656 | tf_op jit(solution)/shard_map/ppermute | solution.py:44
  21.5 12.9 %collective-permute-start.9 = (bf16[512,384]{1,0:T(8,128)(2,1)S(1)}, bf16[512,384]{1,0:T(8,128)(2,1)S(1)}, u32[]{:S(2)}, u32[]{:S(2)}) collective-permute-start(bf16[512,384]{1,0:T(8,128)(2,1)S(1)} %pad_maximum_fusion.refs_0_), channel_id=1, source_target_pairs={{0,8},{8,0},{16,24},{24,16},{32,40},{40,32},{48,56},{56,48},{64,72... | collective-permute-start | bytes 1179656 | tf_op jit(solution)/shard_map/ppermute | solution.py:44
  26.2 10.3 %collective-permute-start.11 = (bf16[512,384]{1,0:T(8,128)(2,1)}, bf16[512,384]{1,0:T(8,128)(2,1)}, u32[]{:S(2)}, u32[]{:S(2)}) collective-permute-start(bf16[512,384]{1,0:T(8,128)(2,1)} %pad_maximum_fusion.1.refs_2_), channel_id=1, source_target_pairs={{0,8},{8,0},{16,24},{24,16},{32,40},{40,32},{48,56},{56,48},{64,72... | collective-permute-start | bytes 1179656 | tf_op jit(solution)/shard_map/ppermute | solution.py:44
  28.8 7.7 %collective-permute-start.13 = (bf16[768,256]{1,0:T(8,128)(2,1)S(1)}, bf16[768,256]{1,0:T(8,128)(2,1)}, u32[]{:S(2)}, u32[]{:S(2)}) collective-permute-start(bf16[768,256]{1,0:T(8,128)(2,1)S(1)} %pad_maximum_fusion.2.refs_4_.refs_0_), channel_id=1, source_target_pairs={{0,8},{8,0},{16,24},{24,16},{32,40},{40,32},{48,56},{56,48},{64,72... | collective-permute-start | bytes 1179656 | tf_op jit(solution)/shard_map/ppermute | solution.py:44
  33.3 3.2 %collective-permute-start.10 = (bf16[512,384]{1,0:T(8,128)(2,1)}, bf16[512,384]{1,0:T(8,128)(2,1)}, u32[]{:S(2)}, u32[]{:S(2)}) collective-permute-start(bf16[512,384]{1,0:T(8,128)(2,1)} %collective-permute-done.6.refs_1_), channel_id=1, source_target_pairs={{0,8},{8,0},{16,24},{24,16},{32,40},{40,32},{48,56},{56,48},{64,72... | collective-permute-start | bytes 1179656 | tf_op jit(solution)/shard_map/ppermute | solution.py:44
  34.4 2.3 %collective-permute-start.12 = (bf16[512,384]{1,0:T(8,128)(2,1)}, bf16[512,384]{1,0:T(8,128)(2,1)}, u32[]{:S(2)}, u32[]{:S(2)}) collective-permute-start(bf16[512,384]{1,0:T(8,128)(2,1)} %collective-permute-done.7.refs_3_), channel_id=1, source_target_pairs={{0,8},{8,0},{16,24},{24,16},{32,40},{40,32},{48,56},{56,48},{64,72... | collective-permute-start | bytes 1179656 | tf_op jit(solution)/shard_map/ppermute | solution.py:44
  34.4 0.7 copy-start.5
  35.1 2.2 %collective-permute-start.14 = (bf16[768,256]{1,0:T(8,128)(2,1)}, bf16[768,256]{1,0:T(8,128)(2,1)}, u32[]{:S(2)}, u32[]{:S(2)}) collective-permute-start(bf16[768,256]{1,0:T(8,128)(2,1)} %collective-permute-done.8.refs_5_.refs_1_), channel_id=1, source_target_pairs={{0,8},{8,0},{16,24},{24,16},{32,40},{40,32},{48,56},{56,48},{64,72... | collective-permute-start | bytes 1179656 | tf_op jit(solution)/shard_map/ppermute | solution.py:44
  37.3 1.0 copy-start.2
  38.3 1.0 copy-start.6
  45.3 4.1 %collective-permute-start.17 = (bf16[2,2176]{1,0:T(2,128)(2,1)S(1)}, bf16[2,2176]{1,0:T(2,128)(2,1)S(1)}, u32[]{:S(2)}, u32[]{:S(2)}) collective-permute-start(bf16[2,2176]{1,0:T(2,128)(2,1)S(1)} %get-tuple-element.68), channel_id=1, source_target_pairs={{0,2},{8,10},{16,18},{24,26},{32,34},{40,42},{48,50},{56,58},{64,6... | collective-permute-start | bytes 26120 | tf_op jit(solution)/shard_map/ppermute | solution.py:44
  47.4 3.7 %collective-permute-start.16 = (bf16[2,2176]{1,0:T(2,128)(2,1)S(1)}, bf16[2,2176]{1,0:T(2,128)(2,1)S(1)}, u32[]{:S(2)}, u32[]{:S(2)}) collective-permute-start(bf16[2,2176]{1,0:T(2,128)(2,1)S(1)} %get-tuple-element.68), channel_id=1, source_target_pairs={{0,3},{8,11},{16,19},{24,27},{32,35},{40,43},{48,51},{56,59},{64,6... | collective-permute-start | bytes 26120 | tf_op jit(solution)/shard_map/ppermute | solution.py:44
  48.2 2.9 %collective-permute-start.15 = (bf16[2,2176]{1,0:T(2,128)(2,1)S(1)}, bf16[2,2176]{1,0:T(2,128)(2,1)S(1)}, u32[]{:S(2)}, u32[]{:S(2)}) collective-permute-start(bf16[2,2176]{1,0:T(2,128)(2,1)S(1)} %get-tuple-element.68), channel_id=1, source_target_pairs={{0,1},{8,9},{16,17},{24,25},{32,33},{40,41},{48,49},{56,57},{64,65... | collective-permute-start | bytes 26120 | tf_op jit(solution)/shard_map/ppermute | solution.py:44
  51.1 4.5 %collective-permute-start.20 = (bf16[8,2176]{1,0:T(8,128)(2,1)S(1)}, bf16[8,2176]{1,0:T(8,128)(2,1)S(1)}, u32[]{:S(2)}, u32[]{:S(2)}) collective-permute-start(bf16[8,2176]{1,0:T(8,128)(2,1)S(1)} %pad_maximum_fusion.8), channel_id=1, source_target_pairs={{0,4},{8,12},{16,20},{24,28},{32,36},{40,44},{48,52},{56,60},{64,6... | collective-permute-start | bytes 104456 | tf_op jit(solution)/shard_map/ppermute | solution.py:44
  51.2 4.5 %collective-permute-start.19 = (bf16[8,2176]{1,0:T(8,128)(2,1)S(1)}, bf16[8,2176]{1,0:T(8,128)(2,1)S(1)}, u32[]{:S(2)}, u32[]{:S(2)}) collective-permute-start(bf16[8,2176]{1,0:T(8,128)(2,1)S(1)} %pad_maximum_fusion.8), channel_id=1, source_target_pairs={{0,68},{8,76},{16,84},{24,92},{32,100},{40,108},{48,116},{56,124},... | collective-permute-start | bytes 104456 | tf_op jit(solution)/shard_map/ppermute | solution.py:44
  52.8 2.8 %collective-permute-start.18 = (bf16[8,2176]{1,0:T(8,128)(2,1)S(1)}, bf16[8,2176]{1,0:T(8,128)(2,1)S(1)}, u32[]{:S(2)}, u32[]{:S(2)}) collective-permute-start(bf16[8,2176]{1,0:T(8,128)(2,1)S(1)} %pad_maximum_fusion.8), channel_id=1, source_target_pairs={{0,64},{8,72},{16,80},{24,88},{32,96},{40,104},{48,112},{56,120},{... | collective-permute-start | bytes 104456 | tf_op jit(solution)/shard_map/ppermute | solution.py:44
  55.7 10.3 %collective-permute-start.23 = (bf16[32,2176]{1,0:T(8,128)(2,1)S(1)}, bf16[32,2176]{1,0:T(8,128)(2,1)S(1)}, u32[]{:S(2)}, u32[]{:S(2)}) collective-permute-start(bf16[32,2176]{1,0:T(8,128)(2,1)S(1)} %pad_maximum_fusion.7.refs_0_), channel_id=1, source_target_pairs={{0,32},{8,40},{16,48},{24,56},{32,0},{40,8},{48,16},{56,24},{64,96... | collective-permute-start | bytes 417800 | tf_op jit(solution)/shard_map/ppermute | solution.py:44
  59.4 6.6 %collective-permute-start.22 = (bf16[32,2176]{1,0:T(8,128)(2,1)S(1)}, bf16[32,2176]{1,0:T(8,128)(2,1)S(1)}, u32[]{:S(2)}, u32[]{:S(2)}) collective-permute-start(bf16[32,2176]{1,0:T(8,128)(2,1)S(1)} %pad_maximum_fusion.7.refs_0_), channel_id=1, source_target_pairs={{0,48},{8,56},{16,32},{24,40},{32,16},{40,24},{48,0},{56,8},{64,11... | collective-permute-start | bytes 417800 | tf_op jit(solution)/shard_map/ppermute | solution.py:44
  59.8 6.2 %collective-permute-start.21 = (bf16[32,2176]{1,0:T(8,128)(2,1)S(1)}, bf16[32,2176]{1,0:T(8,128)(2,1)S(1)}, u32[]{:S(2)}, u32[]{:S(2)}) collective-permute-start(bf16[32,2176]{1,0:T(8,128)(2,1)S(1)} %pad_maximum_fusion.7.refs_0_), channel_id=1, source_target_pairs={{0,16},{8,24},{16,0},{24,8},{32,48},{40,56},{48,32},{56,40},{64,80... | collective-permute-start | bytes 417800 | tf_op jit(solution)/shard_map/ppermute | solution.py:44
  62.2 7.4 %collective-permute-start.24 = (bf16[32,2176]{1,0:T(8,128)(2,1)S(1)}, bf16[32,2176]{1,0:T(8,128)(2,1)S(1)}, u32[]{:S(2)}, u32[]{:S(2)}) collective-permute-start(bf16[32,2176]{1,0:T(8,128)(2,1)S(1)} %pad_maximum_fusion.7.refs_0_), channel_id=1, source_target_pairs={{0,8},{8,0},{16,24},{24,16},{32,40},{40,32},{48,56},{56,48},{64,72... | collective-permute-start | bytes 417800 | tf_op jit(solution)/shard_map/ppermute | solution.py:44
  66.0 4.1 %collective-permute-start.25 = (bf16[32,2176]{1,0:T(8,128)(2,1)S(1)}, bf16[32,2176]{1,0:T(8,128)(2,1)S(1)}, u32[]{:S(2)}, u32[]{:S(2)}) collective-permute-start(bf16[32,2176]{1,0:T(8,128)(2,1)S(1)} %collective-permute-done.21.refs_1_), channel_id=1, source_target_pairs={{0,8},{8,0},{16,24},{24,16},{32,40},{40,32},{48,56},{56,48},{64,72... | collective-permute-start | bytes 417800 | tf_op jit(solution)/shard_map/ppermute | solution.py:44
  69.1 1.4 collective-permute-start.26
  69.1 1.6 %collective-permute-start.27 = (bf16[32,2176]{1,0:T(8,128)(2,1)S(1)}, bf16[32,2176]{1,0:T(8,128)(2,1)S(1)}, u32[]{:S(2)}, u32[]{:S(2)}) collective-permute-start(bf16[32,2176]{1,0:T(8,128)(2,1)S(1)} %collective-permute-done.23.refs_3_), channel_id=1, source_target_pairs={{0,8},{8,0},{16,24},{24,16},{32,40},{40,32},{48,56},{56,48},{64,72... | collective-permute-start | bytes 417800 | tf_op jit(solution)/shard_map/ppermute | solution.py:44
  74.6 3.3 %collective-permute-start.28 = (f32[8,2048]{1,0:T(8,128)S(1)}, f32[8,2048]{1,0:T(8,128)S(1)}, u32[]{:S(2)}, u32[]{:S(2)}) collective-permute-start(f32[8,2048]{1,0:T(8,128)S(1)} %get-tuple-element.74), channel_id=1, source_target_pairs={{0,16},{8,24},{16,0},{24,8},{32,48},{40,56},{48,32},{56,40},{64,80... | collective-permute-start | bytes 196616 | tf_op jit(solution)/shard_map/ppermute | solution.py:44
  74.6 4.3 %collective-permute-start.29 = (f32[8,2048]{1,0:T(8,128)S(1)}, f32[8,2048]{1,0:T(8,128)S(1)}, u32[]{:S(2)}, u32[]{:S(2)}) collective-permute-start(f32[8,2048]{1,0:T(8,128)S(1)} %get-tuple-element.75), channel_id=1, source_target_pairs={{0,48},{8,56},{16,32},{24,40},{32,16},{40,24},{48,0},{56,8},{64,11... | collective-permute-start | bytes 196616 | tf_op jit(solution)/shard_map/ppermute | solution.py:44
  76.5 4.6 %collective-permute-start.30 = (f32[8,2048]{1,0:T(8,128)S(1)}, f32[8,2048]{1,0:T(8,128)S(1)}, u32[]{:S(2)}, u32[]{:S(2)}) collective-permute-start(f32[8,2048]{1,0:T(8,128)S(1)} %get-tuple-element.76), channel_id=1, source_target_pairs={{0,32},{8,40},{16,48},{24,56},{32,0},{40,8},{48,16},{56,24},{64,96... | collective-permute-start | bytes 196616 | tf_op jit(solution)/shard_map/ppermute | solution.py:44
  81.1 3.7 %collective-permute-start.31 = (f32[8,2048]{1,0:T(8,128)S(1)}, f32[8,2048]{1,0:T(8,128)S(1)}, u32[]{:S(2)}, u32[]{:S(2)}) collective-permute-start(f32[8,2048]{1,0:T(8,128)S(1)} %add_add_fusion.refs_0_), channel_id=1, source_target_pairs={{0,64},{8,72},{16,80},{24,88},{32,96},{40,104},{48,112},{56,120},{... | collective-permute-start | bytes 196616 | tf_op jit(solution)/shard_map/ppermute | solution.py:44
  82.5 7.9 %collective-permute-start.32 = (bf16[512,1024]{1,0:T(8,128)(2,1)S(1)}, bf16[512,1024]{1,0:T(8,128)(2,1)S(1)}, u32[]{:S(2)}, u32[]{:S(2)}) collective-permute-start(bf16[512,1024]{1,0:T(8,128)(2,1)S(1)} %copy-done), channel_id=1, source_target_pairs={{0,8},{8,0},{16,24},{24,16},{32,40},{40,32},{48,56},{56,48},{64,72... | collective-permute-start | bytes 3145736 | tf_op jit(solution)/shard_map/ppermute | solution.py:44
  87.7 5.0 %collective-permute-start.33 = (bf16[512,1024]{1,0:T(8,128)(2,1)S(1)}, bf16[512,1024]{1,0:T(8,128)(2,1)S(1)}, u32[]{:S(2)}, u32[]{:S(2)}) collective-permute-start(bf16[512,1024]{1,0:T(8,128)(2,1)S(1)} %get-tuple-element.81.send), channel_id=1, source_target_pairs={{0,8},{8,0},{16,24},{24,16},{32,40},{40,32},{48,56},{56,48},{64,72... | collective-permute-start | bytes 3145736 | tf_op jit(solution)/shard_map/ppermute | solution.py:44
  94.0 6.4 %copy-start.3 = (bf16[512,384]{1,0:T(8,128)(2,1)S(1)}, bf16[512,384]{1,0:T(8,128)(2,1)}, u32[]{:S(2)}) copy-start(bf16[512,384]{1,0:T(8,128)(2,1)} %copy-done.1) | copy-start | bytes 1179652
  94.0 6.4 %copy-start.7 = (bf16[512,384]{1,0:T(8,128)(2,1)S(1)}, bf16[512,384]{1,0:T(8,128)(2,1)}, u32[]{:S(2)}) copy-start(bf16[512,384]{1,0:T(8,128)(2,1)} %copy-done.5) | copy-start | bytes 1179652
  94.0 17.3 %collective-permute-start.34 = (bf16[512,512]{1,0:T(8,128)(2,1)S(1)}, bf16[512,512]{1,0:T(8,128)(2,1)S(1)}, u32[]{:S(2)}, u32[]{:S(2)}) collective-permute-start(bf16[512,512]{1,0:T(8,128)(2,1)S(1)} %first_sent.1), channel_id=1, source_target_pairs={{0,68},{8,76},{16,84},{24,92},{32,100},{40,108},{48,116},{56,124},... | collective-permute-start | bytes 1572872 | tf_op jit(solution)/shard_map/ppermute | solution.py:44
  97.0 11.0 %collective-permute-start.35 = (bf16[256,512]{1,0:T(8,128)(2,1)S(1)}, bf16[256,512]{1,0:T(8,128)(2,1)S(1)}, u32[]{:S(2)}, u32[]{:S(2)}) collective-permute-start(bf16[256,512]{1,0:T(8,128)(2,1)S(1)} %get-tuple-element.84), channel_id=1, source_target_pairs={{0,1},{8,9},{16,17},{24,25},{32,33},{40,41},{48,49},{56,57},{64,65... | collective-permute-start | bytes 786440 | tf_op jit(solution)/shard_map/ppermute | solution.py:44
  97.1 10.9 %collective-permute-start.36 = (bf16[256,512]{1,0:T(8,128)(2,1)S(1)}, bf16[256,512]{1,0:T(8,128)(2,1)S(1)}, u32[]{:S(2)}, u32[]{:S(2)}) collective-permute-start(bf16[256,512]{1,0:T(8,128)(2,1)S(1)} %get-tuple-element.85), channel_id=1, source_target_pairs={{0,3},{8,11},{16,19},{24,27},{32,35},{40,43},{48,51},{56,59},{64,6... | collective-permute-start | bytes 786440 | tf_op jit(solution)/shard_map/ppermute | solution.py:44
  98.9 12.4 %collective-permute-start.37 = (bf16[256,512]{1,0:T(8,128)(2,1)S(1)}, bf16[256,512]{1,0:T(8,128)(2,1)S(1)}, u32[]{:S(2)}, u32[]{:S(2)}) collective-permute-start(bf16[256,512]{1,0:T(8,128)(2,1)S(1)} %get-tuple-element.86), channel_id=1, source_target_pairs={{0,2},{8,10},{16,18},{24,26},{32,34},{40,42},{48,50},{56,58},{64,6... | collective-permute-start | bytes 786440 | tf_op jit(solution)/shard_map/ppermute | solution.py:44
  111.5 5.7 %collective-permute-start.44 = (bf16[128,512]{1,0:T(8,128)(2,1)S(1)}, bf16[128,512]{1,0:T(8,128)(2,1)S(1)}, u32[]{:S(2)}, u32[]{:S(2)}) collective-permute-start(bf16[128,512]{1,0:T(8,128)(2,1)S(1)} %slice.53), channel_id=1, source_target_pairs={{0,68},{8,76},{16,84},{24,92},{32,100},{40,108},{48,116},{56,124},... | collective-permute-start | bytes 393224 | tf_op jit(solution)/shard_map/ppermute | solution.py:44
  113.2 4.8 %collective-permute-start.38 = (bf16[128,512]{1,0:T(8,128)(2,1)S(1)}, bf16[128,512]{1,0:T(8,128)(2,1)S(1)}, u32[]{:S(2)}, u32[]{:S(2)}) collective-permute-start(bf16[128,512]{1,0:T(8,128)(2,1)S(1)} %get-tuple-element.102), channel_id=1, source_target_pairs={{0,1},{8,9},{16,17},{24,25},{32,33},{40,41},{48,49},{56,57},{64,65... | collective-permute-start | bytes 393224 | tf_op jit(solution)/shard_map/ppermute | solution.py:44
  113.3 5.9 %collective-permute-start.40 = (bf16[128,512]{1,0:T(8,128)(2,1)S(1)}, bf16[128,512]{1,0:T(8,128)(2,1)S(1)}, u32[]{:S(2)}, u32[]{:S(2)}) collective-permute-start(bf16[128,512]{1,0:T(8,128)(2,1)S(1)} %get-tuple-element.103), channel_id=1, source_target_pairs={{0,2},{8,10},{16,18},{24,26},{32,34},{40,42},{48,50},{56,58},{64,6... | collective-permute-start | bytes 393224 | tf_op jit(solution)/shard_map/ppermute | solution.py:44
  115.5 5.2 %collective-permute-start.39 = (bf16[128,512]{1,0:T(8,128)(2,1)S(1)}, bf16[128,512]{1,0:T(8,128)(2,1)S(1)}, u32[]{:S(2)}, u32[]{:S(2)}) collective-permute-start(bf16[128,512]{1,0:T(8,128)(2,1)S(1)} %get-tuple-element.104), channel_id=1, source_target_pairs={{0,3},{8,11},{16,19},{24,27},{32,35},{40,43},{48,51},{56,59},{64,6... | collective-permute-start | bytes 393224 | tf_op jit(solution)/shard_map/ppermute | solution.py:44
  117.2 4.2 %collective-permute-start.45 = (bf16[128,512]{1,0:T(8,128)(2,1)S(1)}, bf16[128,512]{1,0:T(8,128)(2,1)S(1)}, u32[]{:S(2)}, u32[]{:S(2)}) collective-permute-start(bf16[128,512]{1,0:T(8,128)(2,1)S(1)} %fusion.8), channel_id=1, source_target_pairs={{0,16},{8,24},{16,0},{24,8},{32,48},{40,56},{48,32},{56,40},{64,80... | collective-permute-start | bytes 393224 | tf_op jit(solution)/shard_map/ppermute | solution.py:44
  120.7 3.9 %collective-permute-start.41 = (bf16[128,512]{1,0:T(8,128)(2,1)S(1)}, bf16[128,512]{1,0:T(8,128)(2,1)S(1)}, u32[]{:S(2)}, u32[]{:S(2)}) collective-permute-start(bf16[128,512]{1,0:T(8,128)(2,1)S(1)} %get-tuple-element.98), channel_id=1, source_target_pairs={{0,64},{8,72},{16,80},{24,88},{32,96},{40,104},{48,112},{56,120},{... | collective-permute-start | bytes 393224 | tf_op jit(solution)/shard_map/ppermute | solution.py:44
  121.5 5.1 %collective-permute-start.46 = (bf16[128,512]{1,0:T(8,128)(2,1)S(1)}, bf16[128,512]{1,0:T(8,128)(2,1)S(1)}, u32[]{:S(2)}, u32[]{:S(2)}) collective-permute-start(bf16[128,512]{1,0:T(8,128)(2,1)S(1)} %fusion.5), channel_id=1, source_target_pairs={{0,48},{8,56},{16,32},{24,40},{32,16},{40,24},{48,0},{56,8},{64,11... | collective-permute-start | bytes 393224 | tf_op jit(solution)/shard_map/ppermute | solution.py:44
  124.6 4.2 %collective-permute-start.42 = (bf16[128,512]{1,0:T(8,128)(2,1)S(1)}, bf16[128,512]{1,0:T(8,128)(2,1)S(1)}, u32[]{:S(2)}, u32[]{:S(2)}) collective-permute-start(bf16[128,512]{1,0:T(8,128)(2,1)S(1)} %fusion.4), channel_id=1, source_target_pairs={{0,16},{8,24},{16,0},{24,8},{32,48},{40,56},{48,32},{56,40},{64,80... | collective-permute-start | bytes 393224 | tf_op jit(solution)/shard_map/ppermute | solution.py:44
  126.7 4.2 %collective-permute-start.47 = (bf16[128,512]{1,0:T(8,128)(2,1)S(1)}, bf16[128,512]{1,0:T(8,128)(2,1)S(1)}, u32[]{:S(2)}, u32[]{:S(2)}) collective-permute-start(bf16[128,512]{1,0:T(8,128)(2,1)S(1)} %fusion.7), channel_id=1, source_target_pairs={{0,64},{8,72},{16,80},{24,88},{32,96},{40,104},{48,112},{56,120},{... | collective-permute-start | bytes 393224 | tf_op jit(solution)/shard_map/ppermute | solution.py:44
  128.9 5.1 %collective-permute-start.43 = (bf16[128,512]{1,0:T(8,128)(2,1)S(1)}, bf16[128,512]{1,0:T(8,128)(2,1)S(1)}, u32[]{:S(2)}, u32[]{:S(2)}) collective-permute-start(bf16[128,512]{1,0:T(8,128)(2,1)S(1)} %fusion.6), channel_id=1, source_target_pairs={{0,48},{8,56},{16,32},{24,40},{32,16},{40,24},{48,0},{56,8},{64,11... | collective-permute-start | bytes 393224 | tf_op jit(solution)/shard_map/ppermute | solution.py:44
  134.1 8.5 %collective-permute-start.48 = (bf16[128,1024]{1,0:T(8,128)(2,1)S(1)}, bf16[128,1024]{1,0:T(8,128)(2,1)S(1)}, u32[]{:S(2)}, u32[]{:S(2)}) collective-permute-start(bf16[128,1024]{1,0:T(8,128)(2,1)S(1)} %pad_maximum_fusion.3), channel_id=1, source_target_pairs={{0,8},{8,0},{16,24},{24,16},{32,40},{40,32},{48,56},{56,48},{64,72... | collective-permute-start | bytes 786440 | tf_op jit(solution)/shard_map/ppermute | solution.py:44

commit v12 on v9

--- a/solution.py
+++ b/solution.py
@@ -567,10 +567,12 @@
     second = all_added(second, swap_z, 3)
     first = all_added(first, swap_z, 3)
     second = all_added(second, swap_y, 1)
-    own = jnp.concatenate([first, second], axis=1).astype(BF16)
-    other = swap_core(own)
+    halves = [first.astype(BF16), second.astype(BF16)]
+    others = [swap_core(v) for v in halves]
     weight_grad = jnp.where(
-        core == 0, jnp.concatenate([own, other], axis=1), jnp.concatenate([other, own], axis=1)
+        core == 0,
+        jnp.concatenate(halves + others, axis=1),
+        jnp.concatenate(others + halves, axis=1),
     )
     return (loss[0, 0], residual_grad, context_grad, weight_grad, gain_grad[0], user_grad)
 

time: 144 us -> 143 us (level)
  waiting for transfers between devices: 36.1 us -> 32.8 us
  starting transfers between devices: 72 us -> 75.1 us
    ppermute x49 -> x50, waiting for transfers between devices: 36.1 us -> 32.8 us  [move(): return lax.ppermute(value, AXES, perm)]
    ppermute x49 -> x50, starting transfers between devices: 72 us -> 75.1 us  [move(): return lax.ppermute(value, AXES, perm)]
  transfers between devices with their start and end apart: 49 -> 50, of which waited for: 26 -> 25; matrix products, arithmetic and copies ran while one was open for 2% -> 2% of each run, Pallas kernels for 10% -> 10%
where the time goes in v12:
time: 143 us
  starting transfers between devices  75.1 us (53%)
  waiting for transfers between devices  32.8 us (23%)
  Pallas kernels  25.7 us (18%)
  local copies, waits for them, and re-layouts  4.77 us (3%)
  other arithmetic  3.57 us (2%)
    ppermute x50, starting transfers between devices, move(): return lax.ppermute(value, AXES, perm)  75.1 us
    ppermute x50, waiting for transfers between devices, move(): return lax.ppermute(value, AXES, perm)  32.8 us
    pallas_call x1, Pallas kernels, on_device(): pl.pallas_call(context_kernel, out_shape=shaped((tokens, head), BF16), in...  6.03 us
    pallas_call x1, Pallas kernels, on_device(): pl.pallas_call(functools.partial(forward_kernel, items_here), out_shape=(...  5.95 us
    unnamed x26, local copies, waits for them, and re-layouts  4.72 us
    pallas_call x3, Pallas kernels, blocks(): pl.pallas_call(functools.partial(blocks_kernel, first_blocks, second_bloc...  4.48 us
    pallas_call x1, Pallas kernels, on_device(): pl.pallas_call(functools.partial(loss_kernel, users_here, items_here), ou...  3.94 us
    pallas_call x1, Pallas kernels, on_device(): pl.pallas_call(functools.partial(residual_kernel, 8 * people), out_shape=...  2.95 us
  transfers between devices with their start and end apart: 50, of which 25 were waited for; matrix products, arithmetic and copies ran while one was open for 2% of the time, Pallas kernels for 10%

profile of v12, /device:TPU:1, one launch (start us, length us, event | category | flops | bytes accessed | tf_op | source)
XLA Modules:
  0.0 142.9 jit_solution(5764925076482018433)
XLA Ops:
  0.7 1.2 copy-done.8
  2.7 3.6 %collective-permute-start = (bf16[128,384]{1,0:T(8,128)(2,1)S(1)}, bf16[128,384]{1,0:T(8,128)(2,1)S(1)}, u32[]{:S(2)}, u32[]{:S(2)}) collective-permute-start(bf16[128,384]{1,0:T(8,128)(2,1)S(1)} %get-tuple-element.50), channel_id=1, source_target_pairs={{0,68},{8,76},{16,84},{24,92},{32,100},{40,108},{48,116},{56,124},... | collective-permute-start | bytes 294920 | tf_op jit(solution)/shard_map/ppermute | solution.py:44
  6.3 1.2 collective-permute-start.1
  7.5 1.8 %collective-permute-start.2 = (bf16[192,256]{1,0:T(8,128)(2,1)S(1)}, bf16[192,256]{1,0:T(8,128)(2,1)S(1)}, u32[]{:S(2)}, u32[]{:S(2)}) collective-permute-start(bf16[192,256]{1,0:T(8,128)(2,1)S(1)} %get-tuple-element.52), channel_id=1, source_target_pairs={{0,3},{8,11},{16,19},{24,27},{32,35},{40,43},{48,51},{56,59},{64,6... | collective-permute-start | bytes 294920 | tf_op jit(solution)/shard_map/ppermute | solution.py:44
  9.8 2.4 %collective-permute-done.2 = bf16[192,256]{1,0:T(8,128)(2,1)S(1)} collective-permute-done((bf16[192,256]{1,0:T(8,128)(2,1)S(1)}, bf16[192,256]{1,0:T(8,128)(2,1)S(1)}, u32[]{:S(2)}, u32[]{:S(2)}) %collective-permute-start.2) | collective-permute-done | bytes 98336 | tf_op jit(solution)/shard_map/ppermute | solution.py:44
  12.3 1.9 %collective-permute-start.4 = (bf16[256,384]{1,0:T(8,128)(2,1)S(1)}, bf16[256,384]{1,0:T(8,128)(2,1)S(1)}, u32[]{:S(2)}, u32[]{:S(2)}) collective-permute-start(bf16[256,384]{1,0:T(8,128)(2,1)S(1)} %pad_maximum_fusion.4), channel_id=1, source_target_pairs={{0,3},{8,11},{16,19},{24,27},{32,35},{40,43},{48,51},{56,59},{64,6... | collective-permute-start | bytes 589832 | tf_op jit(solution)/shard_map/ppermute | solution.py:44
  14.6 2.2 %collective-permute-done.3 = bf16[256,384]{1,0:T(8,128)(2,1)S(1)} collective-permute-done((bf16[256,384]{1,0:T(8,128)(2,1)S(1)}, bf16[256,384]{1,0:T(8,128)(2,1)S(1)}, u32[]{:S(2)}, u32[]{:S(2)}) %collective-permute-start.3) | collective-permute-done | bytes 196640 | tf_op jit(solution)/shard_map/ppermute | solution.py:44
  16.9 1.2 collective-permute-done.4
  18.9 1.3 collective-permute-done.5
  20.3 0.9 collective-permute-start.6
  21.5 4.5 %collective-permute-start.9 = (bf16[512,384]{1,0:T(8,128)(2,1)S(1)}, bf16[512,384]{1,0:T(8,128)(2,1)S(1)}, u32[]{:S(2)}, u32[]{:S(2)}) collective-permute-start(bf16[512,384]{1,0:T(8,128)(2,1)S(1)} %pad_maximum_fusion.refs_0_), channel_id=1, source_target_pairs={{0,8},{8,0},{16,24},{24,16},{32,40},{40,32},{48,56},{56,48},{64,72... | collective-permute-start | bytes 1179656 | tf_op jit(solution)/shard_map/ppermute | solution.py:44
  26.3 2.5 %collective-permute-done.6.refs_1_ = bf16[512,384]{1,0:T(8,128)(2,1)} collective-permute-done((bf16[512,384]{1,0:T(8,128)(2,1)S(1)}, bf16[512,384]{1,0:T(8,128)(2,1)}, u32[]{:S(2)}, u32[]{:S(2)}) %collective-permute-start.6) | collective-permute-done | bytes 393248 | tf_op jit(solution)/shard_map/ppermute | solution.py:44
  28.8 4.4 %collective-permute-start.13 = (bf16[768,256]{1,0:T(8,128)(2,1)S(1)}, bf16[768,256]{1,0:T(8,128)(2,1)}, u32[]{:S(2)}, u32[]{:S(2)}) collective-permute-start(bf16[768,256]{1,0:T(8,128)(2,1)S(1)} %pad_maximum_fusion.2.refs_4_.refs_0_), channel_id=1, source_target_pairs={{0,8},{8,0},{16,24},{24,16},{32,40},{40,32},{48,56},{56,48},{64,72... | collective-permute-start | bytes 1179656 | tf_op jit(solution)/shard_map/ppermute | solution.py:44
  33.3 1.1 collective-permute-start.10
  37.3 1.0 copy-done.2
  38.3 1.0 copy-done.6
  39.3 5.9 %forward.1 = (f32[512,2048]{1,0:T(8,128)S(1)}, f32[512,1]{1,0:T(8,128)S(1)}, f32[2,2048]{1,0:T(2,128)S(1)}, bf16[2,2176]{1,0:T(2,128)(2,1)S(1)}) custom-call(s32[18]{0:T(128)S(1)} %pad_add_fusion.1.ints, bf16[512,1024]{1,0:T(8,128)(2,1)S(1)} %copy-done, bf16[512,2048]{1,0:T(8,128)(2,1)S(1)} %hold.1.residual, f32[1,2048]{1,0:T(1,128)S(1)} %bitcast.7, ...), custom_call_target="tpu_custom_call" | custom-call | tf_op jit(solution)/shard_map/forward/pallas_call | solution.py:457
  45.3 2.1 %collective-permute-start.17 = (bf16[2,2176]{1,0:T(2,128)(2,1)S(1)}, bf16[2,2176]{1,0:T(2,128)(2,1)S(1)}, u32[]{:S(2)}, u32[]{:S(2)}) collective-permute-start(bf16[2,2176]{1,0:T(2,128)(2,1)S(1)} %get-tuple-element.66), channel_id=1, source_target_pairs={{0,2},{8,10},{16,18},{24,26},{32,34},{40,42},{48,50},{56,58},{64,6... | collective-permute-start | bytes 26120 | tf_op jit(solution)/shard_map/ppermute | solution.py:44
  47.4 0.9 collective-permute-start.16
  48.2 1.2 collective-permute-done.17
  49.4 1.7 %collective-permute-done.16 = bf16[2,2176]{1,0:T(2,128)(2,1)S(1)} collective-permute-done((bf16[2,2176]{1,0:T(2,128)(2,1)S(1)}, bf16[2,2176]{1,0:T(2,128)(2,1)S(1)}, u32[]{:S(2)}, u32[]{:S(2)}) %collective-permute-start.16) | collective-permute-done | bytes 8736 | tf_op jit(solution)/shard_map/ppermute | solution.py:44
  51.2 1.6 %collective-permute-start.19 = (bf16[8,2176]{1,0:T(8,128)(2,1)S(1)}, bf16[8,2176]{1,0:T(8,128)(2,1)S(1)}, u32[]{:S(2)}, u32[]{:S(2)}) collective-permute-start(bf16[8,2176]{1,0:T(8,128)(2,1)S(1)} %pad_maximum_fusion.7), channel_id=1, source_target_pairs={{0,68},{8,76},{16,84},{24,92},{32,100},{40,108},{48,116},{56,124},... | collective-permute-start | bytes 104456 | tf_op jit(solution)/shard_map/ppermute | solution.py:44
  52.8 1.0 collective-permute-start.18
  53.9 2.1 %users.3.users_ref = bf16[128,2048]{1,0:T(8,128)(2,1)S(1)} custom-call(s32[4]{0:T(128)S(1)} %pad_add_fusion.where, bf16[768,256]{1,0:T(8,128)(2,1)S(1)} %pad_maximum_fusion.2.refs_4_.refs_0_, bf16[768,256]{1,0:T(8,128)(2,1)} %collective-permute-done.8.refs_5_.refs_1_, bf16[768,256]{1,0:T(8,128)(2,1)} %collective-permute-done.13.refs_10_.refs_2_, ...), custom_call_target="tpu_custom_call" | custom-call | tf_op jit(solution)/shard_map/users/pallas_call | solution.py:474
  56.0 3.7 %collective-permute-start.23 = (bf16[32,2176]{1,0:T(8,128)(2,1)S(1)}, bf16[32,2176]{1,0:T(8,128)(2,1)S(1)}, u32[]{:S(2)}, u32[]{:S(2)}) collective-permute-start(bf16[32,2176]{1,0:T(8,128)(2,1)S(1)} %pad_maximum_fusion.6.refs_0_), channel_id=1, source_target_pairs={{0,32},{8,40},{16,48},{24,56},{32,0},{40,8},{48,16},{56,24},{64,96... | collective-permute-start | bytes 417800 | tf_op jit(solution)/shard_map/ppermute | solution.py:44
  60.4 3.4 %collective-permute-start.24 = (bf16[32,2176]{1,0:T(8,128)(2,1)S(1)}, bf16[32,2176]{1,0:T(8,128)(2,1)S(1)}, u32[]{:S(2)}, u32[]{:S(2)}) collective-permute-start(bf16[32,2176]{1,0:T(8,128)(2,1)S(1)} %pad_maximum_fusion.6.refs_0_), channel_id=1, source_target_pairs={{0,8},{8,0},{16,24},{24,16},{32,40},{40,32},{48,56},{56,48},{64,72... | collective-permute-start | bytes 417800 | tf_op jit(solution)/shard_map/ppermute | solution.py:44
  63.8 2.7 %collective-permute-start.27 = (bf16[32,2176]{1,0:T(8,128)(2,1)S(1)}, bf16[32,2176]{1,0:T(8,128)(2,1)S(1)}, u32[]{:S(2)}, u32[]{:S(2)}) collective-permute-start(bf16[32,2176]{1,0:T(8,128)(2,1)S(1)} %collective-permute-done.23.refs_3_), channel_id=1, source_target_pairs={{0,8},{8,0},{16,24},{24,16},{32,40},{40,32},{48,56},{56,48},{64,72... | collective-permute-start | bytes 417800 | tf_op jit(solution)/shard_map/ppermute | solution.py:44
  66.6 2.5 %collective-permute-start.26 = (bf16[32,2176]{1,0:T(8,128)(2,1)S(1)}, bf16[32,2176]{1,0:T(8,128)(2,1)S(1)}, u32[]{:S(2)}, u32[]{:S(2)}) collective-permute-start(bf16[32,2176]{1,0:T(8,128)(2,1)S(1)} %collective-permute-done.22.refs_2_), channel_id=1, source_target_pairs={{0,8},{8,0},{16,24},{24,16},{32,40},{40,32},{48,56},{56,48},{64,72... | collective-permute-start | bytes 417800 | tf_op jit(solution)/shard_map/ppermute | solution.py:44
  69.1 1.0 collective-permute-done.26.refs_6_
  70.5 3.9 %loss.1 = (f32[8,2048]{1,0:T(8,128)S(1)}, f32[8,2048]{1,0:T(8,128)S(1)}, f32[8,2048]{1,0:T(8,128)S(1)}, f32[8,2048]{1,0:T(8,128)S(1)}, bf16[8,2048]{1,0:T(8,128)(2,1)}) custom-call(s32[4]{0:T(128)S(1)} %pad_add_fusion.where, f32[1,2048]{1,0:T(1,128)S(1)} %bitcast.8, bf16[128,2048]{1,0:T(8,128)(2,1)S(1)} %users.3.users_ref, ...), custom_call_target="tpu_custom_call" | custom-call | tf_op jit(solution)/shard_map/loss/pallas_call | solution.py:491
  74.5 1.6 %collective-permute-start.29 = (f32[8,2048]{1,0:T(8,128)S(1)}, f32[8,2048]{1,0:T(8,128)S(1)}, u32[]{:S(2)}, u32[]{:S(2)}) collective-permute-start(f32[8,2048]{1,0:T(8,128)S(1)} %get-tuple-element.71), channel_id=1, source_target_pairs={{0,48},{8,56},{16,32},{24,40},{32,16},{40,24},{48,0},{56,8},{64,11... | collective-permute-start | bytes 196616 | tf_op jit(solution)/shard_map/ppermute | solution.py:44
  76.1 1.6 %collective-permute-start.30 = (f32[8,2048]{1,0:T(8,128)S(1)}, f32[8,2048]{1,0:T(8,128)S(1)}, u32[]{:S(2)}, u32[]{:S(2)}) collective-permute-start(f32[8,2048]{1,0:T(8,128)S(1)} %get-tuple-element.72), channel_id=1, source_target_pairs={{0,32},{8,40},{16,48},{24,56},{32,0},{40,8},{48,16},{56,24},{64,96... | collective-permute-start | bytes 196616 | tf_op jit(solution)/shard_map/ppermute | solution.py:44
  77.9 0.9 collective-permute-done.29
  78.8 1.9 %collective-permute-done.30 = f32[8,2048]{1,0:T(8,128)S(1)} collective-permute-done((f32[8,2048]{1,0:T(8,128)S(1)}, f32[8,2048]{1,0:T(8,128)S(1)}, u32[]{:S(2)}, u32[]{:S(2)}) %collective-permute-start.30) | collective-permute-done | bytes 65568 | tf_op jit(solution)/shard_map/ppermute | solution.py:44
  80.7 1.4 collective-permute-start.31
  82.1 2.2 %collective-permute-start.32 = (bf16[512,1024]{1,0:T(8,128)(2,1)S(1)}, bf16[512,1024]{1,0:T(8,128)(2,1)S(1)}, u32[]{:S(2)}, u32[]{:S(2)}) collective-permute-start(bf16[512,1024]{1,0:T(8,128)(2,1)S(1)} %copy-done), channel_id=1, source_target_pairs={{0,8},{8,0},{16,24},{24,16},{32,40},{40,32},{48,56},{56,48},{64,72... | collective-permute-start | bytes 3145736 | tf_op jit(solution)/shard_map/ppermute | solution.py:44
  84.3 2.9 %residual.1 = (bf16[512,2048]{1,0:T(8,128)(2,1)}, bf16[512,1024]{1,0:T(8,128)(2,1)S(1)}, bf16[512,1024]{1,0:T(8,128)(2,1)S(1)}, f32[1,2048]{1,0:T(1,128)}, f32[1,1]{1,0:T(1,128)}) custom-call(s32[4]{0:T(128)S(1)} %pad_add_fusion.where, s32[2]{0:T(128)S(1)} %copy-done.11, f32[512,2048]{1,0:T(8,128)S(1)} %get-tuple-element.63.stream, ...), custom_call_target="tpu_custom_call" | custom-call | tf_op jit(solution)/shard_map/residual/pallas_call | solution.py:506
  87.2 2.7 %collective-permute-start.33 = (bf16[512,1024]{1,0:T(8,128)(2,1)S(1)}, bf16[512,1024]{1,0:T(8,128)(2,1)S(1)}, u32[]{:S(2)}, u32[]{:S(2)}) collective-permute-start(bf16[512,1024]{1,0:T(8,128)(2,1)S(1)} %get-tuple-element.77.send), channel_id=1, source_target_pairs={{0,8},{8,0},{16,24},{24,16},{32,40},{40,32},{48,56},{56,48},{64,72... | collective-permute-start | bytes 3145736 | tf_op jit(solution)/shard_map/ppermute | solution.py:44
  89.9 2.3 %collective-permute-done.33.peer_grad = bf16[512,1024]{1,0:T(8,128)(2,1)S(1)} collective-permute-done((bf16[512,1024]{1,0:T(8,128)(2,1)S(1)}, bf16[512,1024]{1,0:T(8,128)(2,1)S(1)}, u32[]{:S(2)}, u32[]{:S(2)}) %collective-permute-start.33) | collective-permute-done | bytes 1048608 | tf_op jit(solution)/shard_map/ppermute | solution.py:44
  92.2 1.3 first_sent.1
  93.5 1.4 collective-permute-start.34
  94.9 1.6 %second_sent.1 = (bf16[256,512]{1,0:T(8,128)(2,1)S(1)}, bf16[256,512]{1,0:T(8,128)(2,1)S(1)}, bf16[256,512]{1,0:T(8,128)(2,1)S(1)}) custom-call(s32[4]{0:T(128)S(1)} %pad_add_fusion.where, bf16[512,1024]{1,0:T(8,128)(2,1)S(1)} %copy-done, bf16[512,1024]{1,0:T(8,128)(2,1)S(1)} %collective-permute-done.32.peer_context, ...), custom_call_target="tpu_custom_call" | custom-call | tf_op jit(solution)/shard_map/second_sent/pallas_call | solution.py:531
  96.6 1.8 %collective-permute-start.36 = (bf16[256,512]{1,0:T(8,128)(2,1)S(1)}, bf16[256,512]{1,0:T(8,128)(2,1)S(1)}, u32[]{:S(2)}, u32[]{:S(2)}) collective-permute-start(bf16[256,512]{1,0:T(8,128)(2,1)S(1)} %get-tuple-element.81), channel_id=1, source_target_pairs={{0,3},{8,11},{16,19},{24,27},{32,35},{40,43},{48,51},{56,59},{64,6... | collective-permute-start | bytes 786440 | tf_op jit(solution)/shard_map/ppermute | solution.py:44
  98.4 1.4 %collective-permute-start.37 = (bf16[256,512]{1,0:T(8,128)(2,1)S(1)}, bf16[256,512]{1,0:T(8,128)(2,1)S(1)}, u32[]{:S(2)}, u32[]{:S(2)}) collective-permute-start(bf16[256,512]{1,0:T(8,128)(2,1)S(1)} %get-tuple-element.82), channel_id=1, source_target_pairs={{0,2},{8,10},{16,18},{24,26},{32,34},{40,42},{48,50},{56,58},{64,6... | collective-permute-start | bytes 786440 | tf_op jit(solution)/shard_map/ppermute | solution.py:44
  99.9 6.0 %context.3 = bf16[512,1024]{1,0:T(8,128)(2,1)} custom-call(s32[4]{0:T(128)S(1)} %pad_add_fusion.where, bf16[512,1024]{1,0:T(8,128)(2,1)S(1)} %get-tuple-element.76.own_grad.keep, bf16[512,1024]{1,0:T(8,128)(2,1)S(1)} %get-tuple-element.77.send, bf16[512,384]{1,0:T(8,128)(2,1)S(1)} %copy-done.3, bf16[512,384]{1,0:T(8,128)(2,1)} %collective-permute-done.6.refs_1_, ...), custom_call_target="tpu_custom_call" | custom-call | tf_op jit(solution)/shard_map/context/pallas_call | solution.py:521
  105.9 1.6 %kept.1 = (f32[512,512]{1,0:T(8,128)S(1)}, f32[256,512]{1,0:T(8,128)S(1)}) custom-call(s32[4]{0:T(128)S(1)} %pad_add_fusion.where, bf16[512,1024]{1,0:T(8,128)(2,1)S(1)} %copy-done, bf16[512,1024]{1,0:T(8,128)(2,1)S(1)} %collective-permute-done.32.peer_context, bf16[512,1024]{1,0:T(8,128)(2,1)S(1)} %get-tuple-element.76.own_grad.keep, ...), custom_call_target="tpu_custom_call" | custom-call | tf_op jit(solution)/shard_map/kept/pallas_call | solution.py:531
  107.5 3.3 %collective-permute-done.37 = bf16[256,512]{1,0:T(8,128)(2,1)S(1)} collective-permute-done((bf16[256,512]{1,0:T(8,128)(2,1)S(1)}, bf16[256,512]{1,0:T(8,128)(2,1)S(1)}, u32[]{:S(2)}, u32[]{:S(2)}) %collective-permute-start.37) | collective-permute-done | bytes 262176 | tf_op jit(solution)/shard_map/ppermute | solution.py:44
  111.0 1.4 collective-permute-start.44
  112.8 2.2 %collective-permute-start.40 = (bf16[128,512]{1,0:T(8,128)(2,1)S(1)}, bf16[128,512]{1,0:T(8,128)(2,1)S(1)}, u32[]{:S(2)}, u32[]{:S(2)}) collective-permute-start(bf16[128,512]{1,0:T(8,128)(2,1)S(1)} %get-tuple-element.99), channel_id=1, source_target_pairs={{0,2},{8,10},{16,18},{24,26},{32,34},{40,42},{48,50},{56,58},{64,6... | collective-permute-start | bytes 393224 | tf_op jit(solution)/shard_map/ppermute | solution.py:44
  115.0 1.7 %collective-permute-start.39 = (bf16[128,512]{1,0:T(8,128)(2,1)S(1)}, bf16[128,512]{1,0:T(8,128)(2,1)S(1)}, u32[]{:S(2)}, u32[]{:S(2)}) collective-permute-start(bf16[128,512]{1,0:T(8,128)(2,1)S(1)} %get-tuple-element.100), channel_id=1, source_target_pairs={{0,3},{8,11},{16,19},{24,27},{32,35},{40,43},{48,51},{56,59},{64,6... | collective-permute-start | bytes 393224 | tf_op jit(solution)/shard_map/ppermute | solution.py:44
  116.7 0.9 collective-permute-start.45
  117.6 1.1 collective-permute-done.40
  118.7 1.4 collective-permute-done.39
  120.9 1.2 collective-permute-start.46
  122.1 2.0 %collective-permute-done.41 = bf16[128,512]{1,0:T(8,128)(2,1)S(1)} collective-permute-done((bf16[128,512]{1,0:T(8,128)(2,1)S(1)}, bf16[128,512]{1,0:T(8,128)(2,1)S(1)}, u32[]{:S(2)}, u32[]{:S(2)}) %collective-permute-start.41) | collective-permute-done | bytes 131104 | tf_op jit(solution)/shard_map/ppermute | solution.py:44
  124.2 0.9 collective-permute-start.42
  125.1 1.0 collective-permute-done.46
  126.1 1.0 collective-permute-start.47
  127.1 1.2 collective-permute-done.42
  128.4 1.2 collective-permute-start.43
  130.4 6.5 %collective-permute-start.49 = (bf16[128,512]{1,0:T(8,128)(2,1)S(1)}, bf16[128,512]{1,0:T(8,128)(2,1)S(1)}, u32[]{:S(2)}, u32[]{:S(2)}) collective-permute-start(bf16[128,512]{1,0:T(8,128)(2,1)S(1)} %add_convert_fusion), channel_id=1, source_target_pairs={{0,8},{8,0},{16,24},{24,16},{32,40},{40,32},{48,56},{56,48},{64,72... | collective-permute-start | bytes 393224 | tf_op jit(solution)/shard_map/ppermute | solution.py:44
  137.0 4.0 %collective-permute-start.48 = (bf16[128,512]{1,0:T(8,128)(2,1)S(1)}, bf16[128,512]{1,0:T(8,128)(2,1)S(1)}, u32[]{:S(2)}, u32[]{:S(2)}) collective-permute-start(bf16[128,512]{1,0:T(8,128)(2,1)S(1)} %add_convert_fusion.1), channel_id=1, source_target_pairs={{0,8},{8,0},{16,24},{24,16},{32,40},{40,32},{48,56},{56,48},{64,72... | collective-permute-start | bytes 393224 | tf_op jit(solution)/shard_map/ppermute | solution.py:44
  141.0 1.0 collective-permute-done.48
  142.0 0.9 maximum_select_fusion
  (96 shorter events, 10.2 us)
Async XLA Ops:
  0.6 25.4 %copy-start.4 = (bf16[512,2048]{1,0:T(8,128)(2,1)S(1)}, bf16[512,2048]{1,0:T(8,128)(2,1)}, u32[]{:S(2)}) copy-start(bf16[512,2048]{1,0:T(8,128)(2,1)} %source.1) | copy-start | bytes 6291460
  0.6 1.2 copy-start.8
  1.8 0.8 copy-start.10
  2.7 6.7 %collective-permute-start = (bf16[128,384]{1,0:T(8,128)(2,1)S(1)}, bf16[128,384]{1,0:T(8,128)(2,1)S(1)}, u32[]{:S(2)}, u32[]{:S(2)}) collective-permute-start(bf16[128,384]{1,0:T(8,128)(2,1)S(1)} %get-tuple-element.50), channel_id=1, source_target_pairs={{0,68},{8,76},{16,84},{24,92},{32,100},{40,108},{48,116},{56,124},... | collective-permute-start | bytes 294920 | tf_op jit(solution)/shard_map/ppermute | solution.py:44
  6.3 3.5 %collective-permute-start.1 = (bf16[128,384]{1,0:T(8,128)(2,1)S(1)}, bf16[128,384]{1,0:T(8,128)(2,1)S(1)}, u32[]{:S(2)}, u32[]{:S(2)}) collective-permute-start(bf16[128,384]{1,0:T(8,128)(2,1)S(1)} %get-tuple-element.51), channel_id=1, source_target_pairs={{0,1},{8,9},{16,17},{24,25},{32,33},{40,41},{48,49},{56,57},{64,65... | collective-permute-start | bytes 294920 | tf_op jit(solution)/shard_map/ppermute | solution.py:44
  7.5 4.7 %collective-permute-start.2 = (bf16[192,256]{1,0:T(8,128)(2,1)S(1)}, bf16[192,256]{1,0:T(8,128)(2,1)S(1)}, u32[]{:S(2)}, u32[]{:S(2)}) collective-permute-start(bf16[192,256]{1,0:T(8,128)(2,1)S(1)} %get-tuple-element.52), channel_id=1, source_target_pairs={{0,3},{8,11},{16,19},{24,27},{32,35},{40,43},{48,51},{56,59},{64,6... | collective-permute-start | bytes 294920 | tf_op jit(solution)/shard_map/ppermute | solution.py:44
  12.2 4.6 %collective-permute-start.3 = (bf16[256,384]{1,0:T(8,128)(2,1)S(1)}, bf16[256,384]{1,0:T(8,128)(2,1)S(1)}, u32[]{:S(2)}, u32[]{:S(2)}) collective-permute-start(bf16[256,384]{1,0:T(8,128)(2,1)S(1)} %pad_maximum_fusion.3), channel_id=1, source_target_pairs={{0,1},{8,9},{16,17},{24,25},{32,33},{40,41},{48,49},{56,57},{64,65... | collective-permute-start | bytes 589832 | tf_op jit(solution)/shard_map/ppermute | solution.py:44
  12.3 5.8 %collective-permute-start.4 = (bf16[256,384]{1,0:T(8,128)(2,1)S(1)}, bf16[256,384]{1,0:T(8,128)(2,1)S(1)}, u32[]{:S(2)}, u32[]{:S(2)}) collective-permute-start(bf16[256,384]{1,0:T(8,128)(2,1)S(1)} %pad_maximum_fusion.4), channel_id=1, source_target_pairs={{0,3},{8,11},{16,19},{24,27},{32,35},{40,43},{48,51},{56,59},{64,6... | collective-permute-start | bytes 589832 | tf_op jit(solution)/shard_map/ppermute | solution.py:44
  14.2 6.0 %collective-permute-start.5 = (bf16[384,256]{1,0:T(8,128)(2,1)S(1)}, bf16[384,256]{1,0:T(8,128)(2,1)S(1)}, u32[]{:S(2)}, u32[]{:S(2)}) collective-permute-start(bf16[384,256]{1,0:T(8,128)(2,1)S(1)} %pad_maximum_fusion.5), channel_id=1, source_target_pairs={{0,68},{8,76},{16,84},{24,92},{32,100},{40,108},{48,116},{56,124},... | collective-permute-start | bytes 589832 | tf_op jit(solution)/shard_map/ppermute | solution.py:44
  16.9 9.3 %copy-start.1 = (bf16[512,384]{1,0:T(8,128)(2,1)}, bf16[512,384]{1,0:T(8,128)(2,1)S(1)}, u32[]{:S(2)}) copy-start(bf16[512,384]{1,0:T(8,128)(2,1)S(1)} %pad_maximum_fusion.refs_0_) | copy-start | bytes 1179652
  20.3 15.4 %copy-start.11 = (s32[2]{0:T(128)S(1)}, s32[2]{0:T(128)}, u32[]{:S(2)}) copy-start(s32[2]{0:T(128)} %lengths.1) | copy-start | bytes 28
  20.3 15.4 %copy-start.12 = (s32[8]{0:T(128)S(1)}, s32[8]{0:T(128)}, u32[]{:S(2)}) copy-start(s32[8]{0:T(128)} %param.14) | copy-start | bytes 100
  20.3 17.0 %copy-start = (bf16[512,1024]{1,0:T(8,128)(2,1)S(1)}, bf16[512,1024]{1,0:T(8,128)(2,1)}, u32[]{:S(2)}) copy-start(bf16[512,1024]{1,0:T(8,128)(2,1)} %own_context.5) | copy-start | bytes 3145732
  20.3 17.0 %copy-start.9 = (f32[2048]{0:T(1024)S(1)}, f32[2048]{0:T(1024)}, u32[]{:S(2)}) copy-start(f32[2048]{0:T(1024)} %param.12) | copy-start | bytes 24580
  20.3 8.5 %collective-permute-start.6 = (bf16[512,384]{1,0:T(8,128)(2,1)S(1)}, bf16[512,384]{1,0:T(8,128)(2,1)}, u32[]{:S(2)}, u32[]{:S(2)}) collective-permute-start(bf16[512,384]{1,0:T(8,128)(2,1)S(1)} %pad_maximum_fusion.refs_0_), channel_id=1, source_target_pairs={{0,3},{8,11},{16,19},{24,27},{32,35},{40,43},{48,51},{56,59},{64,6... | collective-permute-start | bytes 1179656 | tf_op jit(solution)/shard_map/ppermute | solution.py:44
  21.3 12.0 %collective-permute-start.7 = (bf16[512,384]{1,0:T(8,128)(2,1)}, bf16[512,384]{1,0:T(8,128)(2,1)}, u32[]{:S(2)}, u32[]{:S(2)}) collective-permute-start(bf16[512,384]{1,0:T(8,128)(2,1)} %pad_maximum_fusion.1.refs_2_), channel_id=1, source_target_pairs={{0,68},{8,76},{16,84},{24,92},{32,100},{40,108},{48,116},{56,124},... | collective-permute-start | bytes 1179656 | tf_op jit(solution)/shard_map/ppermute | solution.py:44
  21.5 11.8 %collective-permute-start.8 = (bf16[768,256]{1,0:T(8,128)(2,1)S(1)}, bf16[768,256]{1,0:T(8,128)(2,1)}, u32[]{:S(2)}, u32[]{:S(2)}) collective-permute-start(bf16[768,256]{1,0:T(8,128)(2,1)S(1)} %pad_maximum_fusion.2.refs_4_.refs_0_), channel_id=1, source_target_pairs={{0,1},{8,9},{16,17},{24,25},{32,33},{40,41},{48,49},{56,57},{64,65... | collective-permute-start | bytes 1179656 | tf_op jit(solution)/shard_map/ppermute | solution.py:44
  21.5 12.9 %collective-permute-start.9 = (bf16[512,384]{1,0:T(8,128)(2,1)S(1)}, bf16[512,384]{1,0:T(8,128)(2,1)S(1)}, u32[]{:S(2)}, u32[]{:S(2)}) collective-permute-start(bf16[512,384]{1,0:T(8,128)(2,1)S(1)} %pad_maximum_fusion.refs_0_), channel_id=1, source_target_pairs={{0,8},{8,0},{16,24},{24,16},{32,40},{40,32},{48,56},{56,48},{64,72... | collective-permute-start | bytes 1179656 | tf_op jit(solution)/shard_map/ppermute | solution.py:44
  26.2 10.3 %collective-permute-start.11 = (bf16[512,384]{1,0:T(8,128)(2,1)}, bf16[512,384]{1,0:T(8,128)(2,1)}, u32[]{:S(2)}, u32[]{:S(2)}) collective-permute-start(bf16[512,384]{1,0:T(8,128)(2,1)} %pad_maximum_fusion.1.refs_2_), channel_id=1, source_target_pairs={{0,8},{8,0},{16,24},{24,16},{32,40},{40,32},{48,56},{56,48},{64,72... | collective-permute-start | bytes 1179656 | tf_op jit(solution)/shard_map/ppermute | solution.py:44
  28.8 7.7 %collective-permute-start.13 = (bf16[768,256]{1,0:T(8,128)(2,1)S(1)}, bf16[768,256]{1,0:T(8,128)(2,1)}, u32[]{:S(2)}, u32[]{:S(2)}) collective-permute-start(bf16[768,256]{1,0:T(8,128)(2,1)S(1)} %pad_maximum_fusion.2.refs_4_.refs_0_), channel_id=1, source_target_pairs={{0,8},{8,0},{16,24},{24,16},{32,40},{40,32},{48,56},{56,48},{64,72... | collective-permute-start | bytes 1179656 | tf_op jit(solution)/shard_map/ppermute | solution.py:44
  33.3 3.2 %collective-permute-start.10 = (bf16[512,384]{1,0:T(8,128)(2,1)}, bf16[512,384]{1,0:T(8,128)(2,1)}, u32[]{:S(2)}, u32[]{:S(2)}) collective-permute-start(bf16[512,384]{1,0:T(8,128)(2,1)} %collective-permute-done.6.refs_1_), channel_id=1, source_target_pairs={{0,8},{8,0},{16,24},{24,16},{32,40},{40,32},{48,56},{56,48},{64,72... | collective-permute-start | bytes 1179656 | tf_op jit(solution)/shard_map/ppermute | solution.py:44
  34.4 2.3 %collective-permute-start.12 = (bf16[512,384]{1,0:T(8,128)(2,1)}, bf16[512,384]{1,0:T(8,128)(2,1)}, u32[]{:S(2)}, u32[]{:S(2)}) collective-permute-start(bf16[512,384]{1,0:T(8,128)(2,1)} %collective-permute-done.7.refs_3_), channel_id=1, source_target_pairs={{0,8},{8,0},{16,24},{24,16},{32,40},{40,32},{48,56},{56,48},{64,72... | collective-permute-start | bytes 1179656 | tf_op jit(solution)/shard_map/ppermute | solution.py:44
  34.4 0.7 copy-start.5
  35.1 2.2 %collective-permute-start.14 = (bf16[768,256]{1,0:T(8,128)(2,1)}, bf16[768,256]{1,0:T(8,128)(2,1)}, u32[]{:S(2)}, u32[]{:S(2)}) collective-permute-start(bf16[768,256]{1,0:T(8,128)(2,1)} %collective-permute-done.8.refs_5_.refs_1_), channel_id=1, source_target_pairs={{0,8},{8,0},{16,24},{24,16},{32,40},{40,32},{48,56},{56,48},{64,72... | collective-permute-start | bytes 1179656 | tf_op jit(solution)/shard_map/ppermute | solution.py:44
  37.3 1.0 copy-start.2
  38.3 1.0 copy-start.6
  45.3 4.1 %collective-permute-start.17 = (bf16[2,2176]{1,0:T(2,128)(2,1)S(1)}, bf16[2,2176]{1,0:T(2,128)(2,1)S(1)}, u32[]{:S(2)}, u32[]{:S(2)}) collective-permute-start(bf16[2,2176]{1,0:T(2,128)(2,1)S(1)} %get-tuple-element.66), channel_id=1, source_target_pairs={{0,2},{8,10},{16,18},{24,26},{32,34},{40,42},{48,50},{56,58},{64,6... | collective-permute-start | bytes 26120 | tf_op jit(solution)/shard_map/ppermute | solution.py:44
  47.4 3.7 %collective-permute-start.16 = (bf16[2,2176]{1,0:T(2,128)(2,1)S(1)}, bf16[2,2176]{1,0:T(2,128)(2,1)S(1)}, u32[]{:S(2)}, u32[]{:S(2)}) collective-permute-start(bf16[2,2176]{1,0:T(2,128)(2,1)S(1)} %get-tuple-element.66), channel_id=1, source_target_pairs={{0,3},{8,11},{16,19},{24,27},{32,35},{40,43},{48,51},{56,59},{64,6... | collective-permute-start | bytes 26120 | tf_op jit(solution)/shard_map/ppermute | solution.py:44
  48.2 2.9 %collective-permute-start.15 = (bf16[2,2176]{1,0:T(2,128)(2,1)S(1)}, bf16[2,2176]{1,0:T(2,128)(2,1)S(1)}, u32[]{:S(2)}, u32[]{:S(2)}) collective-permute-start(bf16[2,2176]{1,0:T(2,128)(2,1)S(1)} %get-tuple-element.66), channel_id=1, source_target_pairs={{0,1},{8,9},{16,17},{24,25},{32,33},{40,41},{48,49},{56,57},{64,65... | collective-permute-start | bytes 26120 | tf_op jit(solution)/shard_map/ppermute | solution.py:44
  51.1 4.8 %collective-permute-start.20 = (bf16[8,2176]{1,0:T(8,128)(2,1)S(1)}, bf16[8,2176]{1,0:T(8,128)(2,1)S(1)}, u32[]{:S(2)}, u32[]{:S(2)}) collective-permute-start(bf16[8,2176]{1,0:T(8,128)(2,1)S(1)} %pad_maximum_fusion.7), channel_id=1, source_target_pairs={{0,4},{8,12},{16,20},{24,28},{32,36},{40,44},{48,52},{56,60},{64,6... | collective-permute-start | bytes 104456 | tf_op jit(solution)/shard_map/ppermute | solution.py:44
  51.2 4.7 %collective-permute-start.19 = (bf16[8,2176]{1,0:T(8,128)(2,1)S(1)}, bf16[8,2176]{1,0:T(8,128)(2,1)S(1)}, u32[]{:S(2)}, u32[]{:S(2)}) collective-permute-start(bf16[8,2176]{1,0:T(8,128)(2,1)S(1)} %pad_maximum_fusion.7), channel_id=1, source_target_pairs={{0,68},{8,76},{16,84},{24,92},{32,100},{40,108},{48,116},{56,124},... | collective-permute-start | bytes 104456 | tf_op jit(solution)/shard_map/ppermute | solution.py:44
  52.8 3.1 %collective-permute-start.18 = (bf16[8,2176]{1,0:T(8,128)(2,1)S(1)}, bf16[8,2176]{1,0:T(8,128)(2,1)S(1)}, u32[]{:S(2)}, u32[]{:S(2)}) collective-permute-start(bf16[8,2176]{1,0:T(8,128)(2,1)S(1)} %pad_maximum_fusion.7), channel_id=1, source_target_pairs={{0,64},{8,72},{16,80},{24,88},{32,96},{40,104},{48,112},{56,120},{... | collective-permute-start | bytes 104456 | tf_op jit(solution)/shard_map/ppermute | solution.py:44
  56.0 7.9 %collective-permute-start.23 = (bf16[32,2176]{1,0:T(8,128)(2,1)S(1)}, bf16[32,2176]{1,0:T(8,128)(2,1)S(1)}, u32[]{:S(2)}, u32[]{:S(2)}) collective-permute-start(bf16[32,2176]{1,0:T(8,128)(2,1)S(1)} %pad_maximum_fusion.6.refs_0_), channel_id=1, source_target_pairs={{0,32},{8,40},{16,48},{24,56},{32,0},{40,8},{48,16},{56,24},{64,96... | collective-permute-start | bytes 417800 | tf_op jit(solution)/shard_map/ppermute | solution.py:44
  59.7 6.9 %collective-permute-start.22 = (bf16[32,2176]{1,0:T(8,128)(2,1)S(1)}, bf16[32,2176]{1,0:T(8,128)(2,1)S(1)}, u32[]{:S(2)}, u32[]{:S(2)}) collective-permute-start(bf16[32,2176]{1,0:T(8,128)(2,1)S(1)} %pad_maximum_fusion.6.refs_0_), channel_id=1, source_target_pairs={{0,48},{8,56},{16,32},{24,40},{32,16},{40,24},{48,0},{56,8},{64,11... | collective-permute-start | bytes 417800 | tf_op jit(solution)/shard_map/ppermute | solution.py:44
  60.1 9.0 %collective-permute-start.21 = (bf16[32,2176]{1,0:T(8,128)(2,1)S(1)}, bf16[32,2176]{1,0:T(8,128)(2,1)S(1)}, u32[]{:S(2)}, u32[]{:S(2)}) collective-permute-start(bf16[32,2176]{1,0:T(8,128)(2,1)S(1)} %pad_maximum_fusion.6.refs_0_), channel_id=1, source_target_pairs={{0,16},{8,24},{16,0},{24,8},{32,48},{40,56},{48,32},{56,40},{64,80... | collective-permute-start | bytes 417800 | tf_op jit(solution)/shard_map/ppermute | solution.py:44
  60.4 8.7 %collective-permute-start.24 = (bf16[32,2176]{1,0:T(8,128)(2,1)S(1)}, bf16[32,2176]{1,0:T(8,128)(2,1)S(1)}, u32[]{:S(2)}, u32[]{:S(2)}) collective-permute-start(bf16[32,2176]{1,0:T(8,128)(2,1)S(1)} %pad_maximum_fusion.6.refs_0_), channel_id=1, source_target_pairs={{0,8},{8,0},{16,24},{24,16},{32,40},{40,32},{48,56},{56,48},{64,72... | collective-permute-start | bytes 417800 | tf_op jit(solution)/shard_map/ppermute | solution.py:44
  63.8 5.3 %collective-permute-start.27 = (bf16[32,2176]{1,0:T(8,128)(2,1)S(1)}, bf16[32,2176]{1,0:T(8,128)(2,1)S(1)}, u32[]{:S(2)}, u32[]{:S(2)}) collective-permute-start(bf16[32,2176]{1,0:T(8,128)(2,1)S(1)} %collective-permute-done.23.refs_3_), channel_id=1, source_target_pairs={{0,8},{8,0},{16,24},{24,16},{32,40},{40,32},{48,56},{56,48},{64,72... | collective-permute-start | bytes 417800 | tf_op jit(solution)/shard_map/ppermute | solution.py:44
  66.6 3.5 %collective-permute-start.26 = (bf16[32,2176]{1,0:T(8,128)(2,1)S(1)}, bf16[32,2176]{1,0:T(8,128)(2,1)S(1)}, u32[]{:S(2)}, u32[]{:S(2)}) collective-permute-start(bf16[32,2176]{1,0:T(8,128)(2,1)S(1)} %collective-permute-done.22.refs_2_), channel_id=1, source_target_pairs={{0,8},{8,0},{16,24},{24,16},{32,40},{40,32},{48,56},{56,48},{64,72... | collective-permute-start | bytes 417800 | tf_op jit(solution)/shard_map/ppermute | solution.py:44
  69.1 1.4 collective-permute-start.25
  74.4 3.5 %collective-permute-start.28 = (f32[8,2048]{1,0:T(8,128)S(1)}, f32[8,2048]{1,0:T(8,128)S(1)}, u32[]{:S(2)}, u32[]{:S(2)}) collective-permute-start(f32[8,2048]{1,0:T(8,128)S(1)} %get-tuple-element.70), channel_id=1, source_target_pairs={{0,16},{8,24},{16,0},{24,8},{32,48},{40,56},{48,32},{56,40},{64,80... | collective-permute-start | bytes 196616 | tf_op jit(solution)/shard_map/ppermute | solution.py:44
  74.5 4.3 %collective-permute-start.29 = (f32[8,2048]{1,0:T(8,128)S(1)}, f32[8,2048]{1,0:T(8,128)S(1)}, u32[]{:S(2)}, u32[]{:S(2)}) collective-permute-start(f32[8,2048]{1,0:T(8,128)S(1)} %get-tuple-element.71), channel_id=1, source_target_pairs={{0,48},{8,56},{16,32},{24,40},{32,16},{40,24},{48,0},{56,8},{64,11... | collective-permute-start | bytes 196616 | tf_op jit(solution)/shard_map/ppermute | solution.py:44
  76.1 4.6 %collective-permute-start.30 = (f32[8,2048]{1,0:T(8,128)S(1)}, f32[8,2048]{1,0:T(8,128)S(1)}, u32[]{:S(2)}, u32[]{:S(2)}) collective-permute-start(f32[8,2048]{1,0:T(8,128)S(1)} %get-tuple-element.72), channel_id=1, source_target_pairs={{0,32},{8,40},{16,48},{24,56},{32,0},{40,8},{48,16},{56,24},{64,96... | collective-permute-start | bytes 196616 | tf_op jit(solution)/shard_map/ppermute | solution.py:44
  80.7 3.6 %collective-permute-start.31 = (f32[8,2048]{1,0:T(8,128)S(1)}, f32[8,2048]{1,0:T(8,128)S(1)}, u32[]{:S(2)}, u32[]{:S(2)}) collective-permute-start(f32[8,2048]{1,0:T(8,128)S(1)} %add_add_fusion.refs_0_), channel_id=1, source_target_pairs={{0,64},{8,72},{16,80},{24,88},{32,96},{40,104},{48,112},{56,120},{... | collective-permute-start | bytes 196616 | tf_op jit(solution)/shard_map/ppermute | solution.py:44
  82.1 7.8 %collective-permute-start.32 = (bf16[512,1024]{1,0:T(8,128)(2,1)S(1)}, bf16[512,1024]{1,0:T(8,128)(2,1)S(1)}, u32[]{:S(2)}, u32[]{:S(2)}) collective-permute-start(bf16[512,1024]{1,0:T(8,128)(2,1)S(1)} %copy-done), channel_id=1, source_target_pairs={{0,8},{8,0},{16,24},{24,16},{32,40},{40,32},{48,56},{56,48},{64,72... | collective-permute-start | bytes 3145736 | tf_op jit(solution)/shard_map/ppermute | solution.py:44
  87.2 5.0 %collective-permute-start.33 = (bf16[512,1024]{1,0:T(8,128)(2,1)S(1)}, bf16[512,1024]{1,0:T(8,128)(2,1)S(1)}, u32[]{:S(2)}, u32[]{:S(2)}) collective-permute-start(bf16[512,1024]{1,0:T(8,128)(2,1)S(1)} %get-tuple-element.77.send), channel_id=1, source_target_pairs={{0,8},{8,0},{16,24},{24,16},{32,40},{40,32},{48,56},{56,48},{64,72... | collective-permute-start | bytes 3145736 | tf_op jit(solution)/shard_map/ppermute | solution.py:44
  93.5 6.4 %copy-start.3 = (bf16[512,384]{1,0:T(8,128)(2,1)S(1)}, bf16[512,384]{1,0:T(8,128)(2,1)}, u32[]{:S(2)}) copy-start(bf16[512,384]{1,0:T(8,128)(2,1)} %copy-done.1) | copy-start | bytes 1179652
  93.5 6.3 %copy-start.7 = (bf16[512,384]{1,0:T(8,128)(2,1)S(1)}, bf16[512,384]{1,0:T(8,128)(2,1)}, u32[]{:S(2)}) copy-start(bf16[512,384]{1,0:T(8,128)(2,1)} %copy-done.5) | copy-start | bytes 1179652
  93.5 17.3 %collective-permute-start.34 = (bf16[512,512]{1,0:T(8,128)(2,1)S(1)}, bf16[512,512]{1,0:T(8,128)(2,1)S(1)}, u32[]{:S(2)}, u32[]{:S(2)}) collective-permute-start(bf16[512,512]{1,0:T(8,128)(2,1)S(1)} %first_sent.1), channel_id=1, source_target_pairs={{0,68},{8,76},{16,84},{24,92},{32,100},{40,108},{48,116},{56,124},... | collective-permute-start | bytes 1572872 | tf_op jit(solution)/shard_map/ppermute | solution.py:44
  96.5 11.0 %collective-permute-start.35 = (bf16[256,512]{1,0:T(8,128)(2,1)S(1)}, bf16[256,512]{1,0:T(8,128)(2,1)S(1)}, u32[]{:S(2)}, u32[]{:S(2)}) collective-permute-start(bf16[256,512]{1,0:T(8,128)(2,1)S(1)} %get-tuple-element.80), channel_id=1, source_target_pairs={{0,1},{8,9},{16,17},{24,25},{32,33},{40,41},{48,49},{56,57},{64,65... | collective-permute-start | bytes 786440 | tf_op jit(solution)/shard_map/ppermute | solution.py:44
  96.6 10.9 %collective-permute-start.36 = (bf16[256,512]{1,0:T(8,128)(2,1)S(1)}, bf16[256,512]{1,0:T(8,128)(2,1)S(1)}, u32[]{:S(2)}, u32[]{:S(2)}) collective-permute-start(bf16[256,512]{1,0:T(8,128)(2,1)S(1)} %get-tuple-element.81), channel_id=1, source_target_pairs={{0,3},{8,11},{16,19},{24,27},{32,35},{40,43},{48,51},{56,59},{64,6... | collective-permute-start | bytes 786440 | tf_op jit(solution)/shard_map/ppermute | solution.py:44
  98.4 12.5 %collective-permute-start.37 = (bf16[256,512]{1,0:T(8,128)(2,1)S(1)}, bf16[256,512]{1,0:T(8,128)(2,1)S(1)}, u32[]{:S(2)}, u32[]{:S(2)}) collective-permute-start(bf16[256,512]{1,0:T(8,128)(2,1)S(1)} %get-tuple-element.82), channel_id=1, source_target_pairs={{0,2},{8,10},{16,18},{24,26},{32,34},{40,42},{48,50},{56,58},{64,6... | collective-permute-start | bytes 786440 | tf_op jit(solution)/shard_map/ppermute | solution.py:44
  111.0 5.6 %collective-permute-start.44 = (bf16[128,512]{1,0:T(8,128)(2,1)S(1)}, bf16[128,512]{1,0:T(8,128)(2,1)S(1)}, u32[]{:S(2)}, u32[]{:S(2)}) collective-permute-start(bf16[128,512]{1,0:T(8,128)(2,1)S(1)} %slice.53), channel_id=1, source_target_pairs={{0,68},{8,76},{16,84},{24,92},{32,100},{40,108},{48,116},{56,124},... | collective-permute-start | bytes 393224 | tf_op jit(solution)/shard_map/ppermute | solution.py:44
  112.7 4.9 %collective-permute-start.38 = (bf16[128,512]{1,0:T(8,128)(2,1)S(1)}, bf16[128,512]{1,0:T(8,128)(2,1)S(1)}, u32[]{:S(2)}, u32[]{:S(2)}) collective-permute-start(bf16[128,512]{1,0:T(8,128)(2,1)S(1)} %get-tuple-element.98), channel_id=1, source_target_pairs={{0,1},{8,9},{16,17},{24,25},{32,33},{40,41},{48,49},{56,57},{64,65... | collective-permute-start | bytes 393224 | tf_op jit(solution)/shard_map/ppermute | solution.py:44
  112.8 6.0 %collective-permute-start.40 = (bf16[128,512]{1,0:T(8,128)(2,1)S(1)}, bf16[128,512]{1,0:T(8,128)(2,1)S(1)}, u32[]{:S(2)}, u32[]{:S(2)}) collective-permute-start(bf16[128,512]{1,0:T(8,128)(2,1)S(1)} %get-tuple-element.99), channel_id=1, source_target_pairs={{0,2},{8,10},{16,18},{24,26},{32,34},{40,42},{48,50},{56,58},{64,6... | collective-permute-start | bytes 393224 | tf_op jit(solution)/shard_map/ppermute | solution.py:44
  115.0 5.2 %collective-permute-start.39 = (bf16[128,512]{1,0:T(8,128)(2,1)S(1)}, bf16[128,512]{1,0:T(8,128)(2,1)S(1)}, u32[]{:S(2)}, u32[]{:S(2)}) collective-permute-start(bf16[128,512]{1,0:T(8,128)(2,1)S(1)} %get-tuple-element.100), channel_id=1, source_target_pairs={{0,3},{8,11},{16,19},{24,27},{32,35},{40,43},{48,51},{56,59},{64,6... | collective-permute-start | bytes 393224 | tf_op jit(solution)/shard_map/ppermute | solution.py:44
  116.7 4.2 %collective-permute-start.45 = (bf16[128,512]{1,0:T(8,128)(2,1)S(1)}, bf16[128,512]{1,0:T(8,128)(2,1)S(1)}, u32[]{:S(2)}, u32[]{:S(2)}) collective-permute-start(bf16[128,512]{1,0:T(8,128)(2,1)S(1)} %fusion.8), channel_id=1, source_target_pairs={{0,16},{8,24},{16,0},{24,8},{32,48},{40,56},{48,32},{56,40},{64,80... | collective-permute-start | bytes 393224 | tf_op jit(solution)/shard_map/ppermute | solution.py:44
  120.2 3.9 %collective-permute-start.41 = (bf16[128,512]{1,0:T(8,128)(2,1)S(1)}, bf16[128,512]{1,0:T(8,128)(2,1)S(1)}, u32[]{:S(2)}, u32[]{:S(2)}) collective-permute-start(bf16[128,512]{1,0:T(8,128)(2,1)S(1)} %get-tuple-element.94), channel_id=1, source_target_pairs={{0,64},{8,72},{16,80},{24,88},{32,96},{40,104},{48,112},{56,120},{... | collective-permute-start | bytes 393224 | tf_op jit(solution)/shard_map/ppermute | solution.py:44
  120.9 5.1 %collective-permute-start.46 = (bf16[128,512]{1,0:T(8,128)(2,1)S(1)}, bf16[128,512]{1,0:T(8,128)(2,1)S(1)}, u32[]{:S(2)}, u32[]{:S(2)}) collective-permute-start(bf16[128,512]{1,0:T(8,128)(2,1)S(1)} %fusion.5), channel_id=1, source_target_pairs={{0,48},{8,56},{16,32},{24,40},{32,16},{40,24},{48,0},{56,8},{64,11... | collective-permute-start | bytes 393224 | tf_op jit(solution)/shard_map/ppermute | solution.py:44
  124.2 4.2 %collective-permute-start.42 = (bf16[128,512]{1,0:T(8,128)(2,1)S(1)}, bf16[128,512]{1,0:T(8,128)(2,1)S(1)}, u32[]{:S(2)}, u32[]{:S(2)}) collective-permute-start(bf16[128,512]{1,0:T(8,128)(2,1)S(1)} %fusion.4), channel_id=1, source_target_pairs={{0,16},{8,24},{16,0},{24,8},{32,48},{40,56},{48,32},{56,40},{64,80... | collective-permute-start | bytes 393224 | tf_op jit(solution)/shard_map/ppermute | solution.py:44
  126.1 4.2 %collective-permute-start.47 = (bf16[128,512]{1,0:T(8,128)(2,1)S(1)}, bf16[128,512]{1,0:T(8,128)(2,1)S(1)}, u32[]{:S(2)}, u32[]{:S(2)}) collective-permute-start(bf16[128,512]{1,0:T(8,128)(2,1)S(1)} %fusion.7), channel_id=1, source_target_pairs={{0,64},{8,72},{16,80},{24,88},{32,96},{40,104},{48,112},{56,120},{... | collective-permute-start | bytes 393224 | tf_op jit(solution)/shard_map/ppermute | solution.py:44
  128.4 8.5 %collective-permute-start.43 = (bf16[128,512]{1,0:T(8,128)(2,1)S(1)}, bf16[128,512]{1,0:T(8,128)(2,1)S(1)}, u32[]{:S(2)}, u32[]{:S(2)}) collective-permute-start(bf16[128,512]{1,0:T(8,128)(2,1)S(1)} %fusion.6), channel_id=1, source_target_pairs={{0,48},{8,56},{16,32},{24,40},{32,16},{40,24},{48,0},{56,8},{64,11... | collective-permute-start | bytes 393224 | tf_op jit(solution)/shard_map/ppermute | solution.py:44
  130.4 10.6 %collective-permute-start.49 = (bf16[128,512]{1,0:T(8,128)(2,1)S(1)}, bf16[128,512]{1,0:T(8,128)(2,1)S(1)}, u32[]{:S(2)}, u32[]{:S(2)}) collective-permute-start(bf16[128,512]{1,0:T(8,128)(2,1)S(1)} %add_convert_fusion), channel_id=1, source_target_pairs={{0,8},{8,0},{16,24},{24,16},{32,40},{40,32},{48,56},{56,48},{64,72... | collective-permute-start | bytes 393224 | tf_op jit(solution)/shard_map/ppermute | solution.py:44
  137.0 5.0 %collective-permute-start.48 = (bf16[128,512]{1,0:T(8,128)(2,1)S(1)}, bf16[128,512]{1,0:T(8,128)(2,1)S(1)}, u32[]{:S(2)}, u32[]{:S(2)}) collective-permute-start(bf16[128,512]{1,0:T(8,128)(2,1)S(1)} %add_convert_fusion.1), channel_id=1, source_target_pairs={{0,8},{8,0},{16,24},{24,16},{32,40},{40,32},{48,56},{56,48},{64,72... | collective-permute-start | bytes 393224 | tf_op jit(solution)/shard_map/ppermute | solution.py:44
